TPU v7x, 32 devices: a whole 2x2x4 slice. The times are simulated.
32 devices in a mesh: pipe: 16 (over z, y, core), tensor: 2 (over x).
Axes of the slice: x: 2, y: 2, z: 4, core: 2. Of those that a mesh axis runs over, the one named last changes fastest.
Arguments:
- query: bfloat16 [4096, 2048], P(('pipe', 'tensor')), may hold values from -20 to 20
- key: bfloat16 [4096, 1024], P(('pipe', 'tensor')), may hold values from -20 to 20
- value: bfloat16 [4096, 1024], P(('pipe', 'tensor')), may hold values from -6 to 6
- grad_out: bfloat16 [4096, 2048], P(('pipe', 'tensor')), may hold values from -6 to 6
- segment_ids: int32 [4096], replicated, may hold values from 0 to 3, never falling along the last dimension, each value on 1 to 2048 neighbouring positions
Outputs:
- attn_out: bfloat16 [4096, 2048], P(('pipe', 'tensor'))
- grad_query: bfloat16 [4096, 2048], P(('pipe', 'tensor'))
- grad_key: bfloat16 [4096, 1024], P(('pipe', 'tensor'))
- grad_value: bfloat16 [4096, 1024], P(('pipe', 'tensor'))
Inputs may be any that keep to these rules, and one draw needn't show every extreme that they name: `segment_ids`: segment ids never fall along the tokens; each of the 4 documents holds 1 to 2048 tokens and one holds exactly 2048.
All inputs are finite; a program needn't handle non-finite values.
Results may differ from a plain program's by a relative error of at most 0.029.
Values may be sent and summed in bfloat16 or wider, within the bound.
No kernel may reach another device: no remote copies, remote signals or barrier semaphores. Data moves between devices by JAX's collectives and lax.ppermute only.
A program may use at most 64 MiB of HBM per device.

v0:
```python
import jax
import jax.numpy as jnp
from jax import lax
from jax.sharding import PartitionSpec as P

HEAD_DIM = 128
WINDOW = 1024


logit_scale = 168.0 ** (-0.5)


def shifted(value, axis, steps):
    count = lax.axis_size(axis)
    initial, last = (max(0, -steps), min(count, count - steps))
    return lax.ppermute(value, axis, [(source, source + steps) for source in range(initial, last)])


def tile_allowed(segment_ids, index, lag, tok):
    q_start = index * tok
    k_start = (index - lag) * tok
    q_seg = lax.dynamic_slice_in_dim(segment_ids, q_start, tok, 0)
    k_seg = lax.dynamic_slice_in_dim(segment_ids, jnp.maximum(k_start, 0), tok, 0)
    offsets = jnp.arange(tok, dtype=jnp.int32)
    k_pos = k_start + offsets
    distance = (q_start + offsets)[:, None] - k_pos[None, :]
    return (
        (k_pos[None, :] >= 0)
        & (distance >= 0)
        & (distance < WINDOW)
        & (q_seg[:, None] == k_seg[None, :])
    )


def body(query, key, value, grad_out, segment_ids):
    q_rows, k_rows, v_rows, g_rows = (
        lax.all_to_all(query, "tensor", split_axis=1, concat_axis=0, tiled=True),
        lax.all_to_all(key, "tensor", split_axis=1, concat_axis=0, tiled=True),
        lax.all_to_all(value, "tensor", split_axis=1, concat_axis=0, tiled=True),
        lax.all_to_all(grad_out, "tensor", split_axis=1, concat_axis=0, tiled=True),
    )
    tok = q_rows.shape[0]
    kv_local = k_rows.shape[1] // HEAD_DIM
    group = q_rows.shape[1] // k_rows.shape[1]
    reach = WINDOW // tok
    index = lax.axis_index("pipe")
    grouped_queries = jnp.transpose(q_rows.reshape(tok, kv_local, group, HEAD_DIM), (1, 2, 0, 3))
    grouped_output_gradient = jnp.transpose(
        g_rows.reshape(tok, kv_local, group, HEAD_DIM), (1, 2, 0, 3)
    )
    kv_pair = jnp.stack((k_rows, v_rows))
    tiles = [kv_pair]
    for lag in range(1, reach + 1):
        tiles.append(shifted(kv_pair, "pipe", lag))
    masks = [tile_allowed(segment_ids, index, lag, tok) for lag in range(reach + 1)]
    scores = []
    for lag in range(reach + 1):
        raw_key_tensor = tiles[lag][0].reshape(tok, kv_local, HEAD_DIM)
        part = (
            jnp.einsum(
                "pmcz,fpz->pmcf",
                grouped_queries,
                raw_key_tensor,
                preferred_element_type=jnp.float32,
            )
            * logit_scale
        )
        scores.append(jnp.where(masks[lag], part, -jnp.inf))
    top = jnp.max(scores[0], axis=-1, keepdims=True)
    for part in scores[1:]:
        top = jnp.maximum(top, jnp.max(part, axis=-1, keepdims=True))
    expos = [jnp.exp(part - top) for part in scores]
    denominator_sum = jnp.sum(expos[0], axis=-1, keepdims=True)
    for part in expos[1:]:
        denominator_sum = denominator_sum + jnp.sum(part, axis=-1, keepdims=True)
    out_shape = (kv_local, group, tok, HEAD_DIM)
    summed = jnp.zeros(out_shape, jnp.float32)
    for lag in range(reach + 1):
        weighted_value_tensor = tiles[lag][1].reshape(tok, kv_local, HEAD_DIM)
        summed = summed + jnp.einsum(
            "xypq,qxa->xypa",
            expos[lag].astype(jnp.bfloat16),
            weighted_value_tensor,
            preferred_element_type=jnp.float32,
        )
    out_half = (summed / denominator_sum).astype(jnp.bfloat16)
    delta = jnp.sum(
        grouped_output_gradient.astype(jnp.float32) * out_half.astype(jnp.float32),
        axis=-1,
        keepdims=True,
    )
    dq_sum = jnp.zeros(out_shape, jnp.float32)
    kv_terms = []
    for lag in range(reach + 1):
        key_tensor = tiles[lag][0].reshape(tok, kv_local, HEAD_DIM)
        value_tensor = tiles[lag][1].reshape(tok, kv_local, HEAD_DIM)
        probabilities = expos[lag] / denominator_sum
        probability_gradient = jnp.einsum(
            "pmcz,fpz->pmcf",
            grouped_output_gradient,
            value_tensor,
            preferred_element_type=jnp.float32,
        )
        score_gradient = (probabilities * (probability_gradient - delta)).astype(jnp.bfloat16)
        query_gradient_term = jnp.einsum(
            "xypq,qxa->xypa", score_gradient, key_tensor, preferred_element_type=jnp.float32
        )
        dk_term = (
            jnp.einsum(
                "ihjm,ihjx->mix",
                score_gradient,
                grouped_queries,
                preferred_element_type=jnp.float32,
            )
            * logit_scale
        )
        dv_term = jnp.einsum(
            "ihjm,ihjx->mix",
            probabilities.astype(jnp.bfloat16),
            grouped_output_gradient,
            preferred_element_type=jnp.float32,
        )
        query_gradient_term, kv_term = (
            query_gradient_term,
            jnp.stack(
                (
                    dk_term.reshape(tok, kv_local * HEAD_DIM),
                    dv_term.reshape(tok, kv_local * HEAD_DIM),
                )
            ),
        )
        dq_sum = dq_sum + query_gradient_term
        kv_terms.append(kv_term)
    kv_grad = kv_terms[0]
    for lag in range(1, reach + 1):
        kv_grad = kv_grad + shifted(kv_terms[lag].astype(jnp.bfloat16), "pipe", -lag).astype(
            jnp.float32
        )
    out_rows = jnp.transpose(out_half, (2, 0, 1, 3)).reshape(tok, kv_local * group * HEAD_DIM)
    grad_q_rows = (
        jnp.transpose(dq_sum * logit_scale, (2, 0, 1, 3))
        .reshape(tok, kv_local * group * HEAD_DIM)
        .astype(jnp.bfloat16)
    )
    grad_k_rows = kv_grad[0].astype(jnp.bfloat16)
    grad_v_rows = kv_grad[1].astype(jnp.bfloat16)
    attn_out, grad_query, grad_key, grad_value = (
        lax.all_to_all(out_rows, "tensor", split_axis=0, concat_axis=1, tiled=True),
        lax.all_to_all(grad_q_rows, "tensor", split_axis=0, concat_axis=1, tiled=True),
        lax.all_to_all(grad_k_rows, "tensor", split_axis=0, concat_axis=1, tiled=True),
        lax.all_to_all(grad_v_rows, "tensor", split_axis=0, concat_axis=1, tiled=True),
    )
    return (attn_out, grad_query, grad_key, grad_value)


def solution(mesh):
    placed = (
        P(("pipe", "tensor"), None),
        P(("pipe", "tensor"), None),
        P(("pipe", "tensor"), None),
        P(("pipe", "tensor"), None),
        P(),
    )
    return jax.shard_map(
        body,
        mesh=mesh,
        in_specs=placed,
        out_specs=(
            P(("pipe", "tensor"), None),
            P(("pipe", "tensor"), None),
            P(("pipe", "tensor"), None),
            P(("pipe", "tensor"), None),
        ),
        check_vma=False,
    )
```

profile of v0, /device:TPU:0, one launch (start us, length us, event | category | flops | bytes accessed | tf_op | source)
XLA Modules:
  0.0 161.7 jit_solution(15386340668958333050)
XLA Ops:
  0.7 1.9 %copy.232 = bf16[128,1024]{0,1:T(8,128)(2,1)} copy(bf16[128,1024]{1,0:T(8,128)(2,1)} %param.7) | data formatting | bytes 524288 | tf_op args[2]
  2.5 4.2 %all-to-all-start.2 = ((bf16[128,2,512]{0,2,1:T(8,128)(2,1)}), bf16[128,2,512]{0,2,1:T(8,128)(2,1)S(1)}, u32[]{:S(2)}, u32[]{:S(2)}) async-start(bf16[128,2,512]{0,2,1:T(8,128)(2,1)} %bitcast.5), calls=%async_computation.2 | async-start | bytes 524288 | tf_op jit(solution)/shard_map/all_to_all | solution.py:39
  6.7 1.7 %copy.456 = bf16[16,2,8,512]{3,2,0,1:T(8,128)(2,1)} copy(bf16[16,2,8,512]{3,2,1,0:T(8,128)(2,1)} %bitcast.435) | data formatting | bytes 524288 | tf_op jit(solution)/shard_map/all_to_all | solution.py:38
  8.4 4.2 %all-to-all-done.2 = bf16[128,2,512]{0,2,1:T(8,128)(2,1)S(1)} async-done(((bf16[128,2,512]{0,2,1:T(8,128)(2,1)}), bf16[128,2,512]{0,2,1:T(8,128)(2,1)S(1)}, u32[]{:S(2)}, u32[]{:S(2)}) %all-to-all-start.2) | async-done | bytes 262176 | tf_op jit(solution)/shard_map/all_to_all | solution.py:39
  12.6 3.4 %all-to-all-start.1 = ((bf16[128,2,512]{2,0,1:T(8,128)(2,1)}), bf16[128,2,512]{2,0,1:T(8,128)(2,1)S(1)}, u32[]{:S(2)}, u32[]{:S(2)}) async-start(bf16[128,2,512]{2,0,1:T(8,128)(2,1)} %bitcast.378), calls=%async_computation.1 | async-start | bytes 524288 | tf_op jit(solution)/shard_map/all_to_all | solution.py:38
  16.9 4.3 %all-to-all-done.1 = bf16[128,2,512]{2,0,1:T(8,128)(2,1)S(1)} async-done(((bf16[128,2,512]{2,0,1:T(8,128)(2,1)}), bf16[128,2,512]{2,0,1:T(8,128)(2,1)S(1)}, u32[]{:S(2)}, u32[]{:S(2)}) %all-to-all-start.1) | async-done | bytes 262176 | tf_op jit(solution)/shard_map/all_to_all | solution.py:38
  21.2 3.5 %all-to-all-start = ((bf16[128,2,1024]{2,0,1:T(8,128)(2,1)}), bf16[128,2,1024]{2,0,1:T(8,128)(2,1)S(1)}, u32[]{:S(2)}, u32[]{:S(2)}) async-start(bf16[128,2,1024]{2,0,1:T(8,128)(2,1)} %bitcast.377), calls=%async_computation | async-start | bytes 1048576 | tf_op jit(solution)/shard_map/all_to_all | solution.py:37
  27.4 3.9 %all-to-all-done = bf16[128,2,1024]{2,0,1:T(8,128)(2,1)S(1)} async-done(((bf16[128,2,1024]{2,0,1:T(8,128)(2,1)}), bf16[128,2,1024]{2,0,1:T(8,128)(2,1)S(1)}, u32[]{:S(2)}, u32[]{:S(2)}) %all-to-all-start) | async-done | bytes 524320 | tf_op jit(solution)/shard_map/all_to_all | solution.py:37
  31.3 3.5 %all-to-all-start.4 = ((bf16[128,2,1024]{0,2,1:T(8,128)(2,1)}), bf16[128,2,1024]{0,2,1:T(8,128)(2,1)S(1)}, u32[]{:S(2)}, u32[]{:S(2)}) async-start(bf16[128,2,1024]{0,2,1:T(8,128)(2,1)} %bitcast.36), calls=%async_computation.4 | async-start | bytes 1048576 | tf_op jit(solution)/shard_map/all_to_all | solution.py:40
  35.6 4.5 %collective-permute-start.3 = (bf16[2,256,512]{1,2,0:T(8,128)(2,1)}, bf16[2,256,512]{1,2,0:T(8,128)(2,1)}, u32[]{:S(2)}, u32[]{:S(2)}) collective-permute-start(bf16[2,256,512]{1,2,0:T(8,128)(2,1)} %pad_maximum_fusion), channel_id=1, source_target_pairs={{0,8},{2,10},{4,12},{6,14},{8,16},{10,18},{12,20},{14,22},{16,24},... | collective-permute-start | bytes 1572872 | tf_op jit(solution)/shard_map/ppermute | solution.py:16
  40.9 2.1 %collective-permute-start.2 = (bf16[2,256,512]{1,2,0:T(8,128)(2,1)}, bf16[2,256,512]{1,2,0:T(8,128)(2,1)}, u32[]{:S(2)}, u32[]{:S(2)}) collective-permute-start(bf16[2,256,512]{1,2,0:T(8,128)(2,1)} %pad_maximum_fusion), channel_id=1, source_target_pairs={{0,6},{2,8},{4,10},{6,12},{8,14},{10,16},{12,18},{14,20},{16,22},{... | collective-permute-start | bytes 1572872 | tf_op jit(solution)/shard_map/ppermute | solution.py:16
  43.0 4.2 %collective-permute-start.1 = (bf16[2,256,512]{1,2,0:T(8,128)(2,1)}, bf16[2,256,512]{1,2,0:T(8,128)(2,1)}, u32[]{:S(2)}, u32[]{:S(2)}) collective-permute-start(bf16[2,256,512]{1,2,0:T(8,128)(2,1)} %pad_maximum_fusion), channel_id=1, source_target_pairs={{0,4},{2,6},{4,8},{6,10},{8,12},{10,14},{12,16},{14,18},{16,20},{1... | collective-permute-start | bytes 1572872 | tf_op jit(solution)/shard_map/ppermute | solution.py:16
  47.3 3.2 %collective-permute-start = (bf16[2,256,512]{1,2,0:T(8,128)(2,1)}, bf16[2,256,512]{1,2,0:T(8,128)(2,1)}, u32[]{:S(2)}, u32[]{:S(2)}) collective-permute-start(bf16[2,256,512]{1,2,0:T(8,128)(2,1)} %pad_maximum_fusion), channel_id=1, source_target_pairs={{0,2},{2,4},{4,6},{6,8},{8,10},{10,12},{12,14},{14,16},{16,18},{18... | collective-permute-start | bytes 1572872 | tf_op jit(solution)/shard_map/ppermute | solution.py:16
  54.2 1.5 fusion.4
  59.0 3.0 %collective-permute-done.1 = bf16[2,256,512]{1,2,0:T(8,128)(2,1)} collective-permute-done((bf16[2,256,512]{1,2,0:T(8,128)(2,1)}, bf16[2,256,512]{1,2,0:T(8,128)(2,1)}, u32[]{:S(2)}, u32[]{:S(2)}) %collective-permute-start.1) | collective-permute-done | bytes 524320 | tf_op jit(solution)/shard_map/ppermute | solution.py:16
  65.3 2.5 %fusion.33 = (f32[4,2,256]{2,1,0:T(2,128)S(1)}, f32[4,2,256]{2,1,0:T(2,128)S(1)}, f32[4,2,256]{2,1,0:T(2,128)S(1)}, f32[4,2,256]{2,1,0:T(2,128)S(1)}, f32[4,2,256]{2,1,0:T(2,128)S(1)}) fusion(f32[4,256,2,256]{3,1,2,0:T(8,128)S(1)} %get-tuple-element.51, f32[4,2,256]{2,1,0:T(2,128)S(1)} %bitcast.419, pred[256,256]{0,1:T(8,128)(4,1)S(1)} %get-tuple-element.37, ...), kind=kLoop, calls=%fused_computation.61 | loop fusion | flops 10475520 | bytes 10862592 | tf_op jit(solution)/shard_map/reduce_sum | solution.py:75
  72.1 1.5 fusion.56
  82.0 1.4 collective-permute-start.4
  84.8 1.5 collective-permute-start.5
  95.5 2.2 %convert_element_type.105 = bf16[2,128,1024]{2,1,0:T(8,128)(2,1)} reshape(bf16[256,4,2,128]{3,2,1,0:T(2,128)(2,1)} %copy.268) | data formatting | bytes 1048576 | tf_op jit(solution)/shard_map/convert_element_type | solution.py:143
  97.7 4.2 %all-to-all-start.5 = ((bf16[2,128,1024]{2,1,0:T(8,128)(2,1)}), bf16[2,128,1024]{2,1,0:T(8,128)(2,1)}, u32[]{:S(2)}, u32[]{:S(2)}) async-start(bf16[2,128,1024]{2,1,0:T(8,128)(2,1)} %convert_element_type.105), calls=%async_computation.5 | async-start | bytes 1048576 | tf_op jit(solution)/shard_map/all_to_all | solution.py:149
  102.0 2.0 %all_to_all.107 = bf16[2,128,1024]{1,0,2:T(2,128)(2,1)} reshape(bf16[256,4,2,128]{0,3,2,1:T(8,128)(2,1)} %get-tuple-element.52) | data formatting | bytes 1048576 | tf_op jit(solution)/shard_map/all_to_all | solution.py:148
  103.9 1.9 %copy.244 = bf16[2,128,1024]{1,2,0:T(8,128)(2,1)} copy(bf16[2,128,1024]{1,0,2:T(2,128)(2,1)} %all_to_all.107) | data formatting | bytes 1048576 | tf_op jit(solution)/shard_map/all_to_all | solution.py:148
  105.8 1.5 fusion.61
  108.9 3.5 %all-to-all-start.3 = ((bf16[2,128,1024]{1,2,0:T(8,128)(2,1)}), bf16[2,128,1024]{1,2,0:T(8,128)(2,1)S(1)}, u32[]{:S(2)}, u32[]{:S(2)}) async-start(bf16[2,128,1024]{1,2,0:T(8,128)(2,1)} %copy.244), calls=%async_computation.3 | async-start | bytes 1048576 | tf_op jit(solution)/shard_map/all_to_all | solution.py:148
  112.4 5.1 %collective-permute-done.5 = bf16[2,256,512]{1,2,0:T(8,128)(2,1)} collective-permute-done((bf16[2,256,512]{1,2,0:T(8,128)(2,1)}, bf16[2,256,512]{1,2,0:T(8,128)(2,1)}, u32[]{:S(2)}, u32[]{:S(2)}) %collective-permute-start.5) | collective-permute-done | bytes 524320 | tf_op jit(solution)/shard_map/ppermute | solution.py:16
  117.5 3.6 %collective-permute-done.6 = bf16[2,256,512]{1,2,0:T(8,128)(2,1)} collective-permute-done((bf16[2,256,512]{1,2,0:T(8,128)(2,1)}, bf16[2,256,512]{1,2,0:T(8,128)(2,1)}, u32[]{:S(2)}, u32[]{:S(2)}) %collective-permute-start.6) | collective-permute-done | bytes 524320 | tf_op jit(solution)/shard_map/ppermute | solution.py:16
  121.1 19.6 %collective-permute-done.7 = bf16[2,256,512]{1,2,0:T(8,128)(2,1)} collective-permute-done((bf16[2,256,512]{1,2,0:T(8,128)(2,1)}, bf16[2,256,512]{1,2,0:T(8,128)(2,1)}, u32[]{:S(2)}, u32[]{:S(2)}) %collective-permute-start.7) | collective-permute-done | bytes 524320 | tf_op jit(solution)/shard_map/ppermute | solution.py:16
  140.8 1.8 %fusion.55 = bf16[2,256,512]{1,2,0:T(8,128)(2,1)S(1)} fusion(f32[1,256,512]{1,2,0:T(8,128)S(1)} %bitcast.417, f32[1,256,512]{1,2,0:T(8,128)S(1)} %bitcast.404, bf16[2,256,512]{1,2,0:T(8,128)(2,1)} %collective-permute-done.7, bf16[2,256,512]{1,2,0:T(8,128)(2,1)} %collective-permute-done.6, bf16[2,256,512]{1,2,0:T(8,128)(2,1)} %collective-permute-done.5, ...), kind=kLoop, calls=%fused_computation.79 | loop fusion | flops 2621440 | bytes 3670016 | tf_op jit(solution)/shard_map/convert.1
  143.5 3.4 %all-to-all-start.6 = ((bf16[2,128,512]{2,1,0:T(8,128)(2,1)}), bf16[2,128,512]{2,1,0:T(8,128)(2,1)S(1)}, u32[]{:S(2)}, u32[]{:S(2)}) async-start(bf16[2,128,512]{2,1,0:T(8,128)(2,1)} %bitcast.106), calls=%async_computation.6 | async-start | bytes 524288 | tf_op jit(solution)/shard_map/all_to_all | solution.py:150
  147.8 4.3 %all-to-all-done.6 = bf16[2,128,512]{2,1,0:T(8,128)(2,1)S(1)} async-done(((bf16[2,128,512]{2,1,0:T(8,128)(2,1)}), bf16[2,128,512]{2,1,0:T(8,128)(2,1)S(1)}, u32[]{:S(2)}, u32[]{:S(2)}) %all-to-all-start.6) | async-done | bytes 262176 | tf_op jit(solution)/shard_map/all_to_all | solution.py:150
  152.1 3.4 %all-to-all-start.7 = ((bf16[2,128,512]{2,1,0:T(8,128)(2,1)}), bf16[2,128,512]{2,1,0:T(8,128)(2,1)S(1)}, u32[]{:S(2)}, u32[]{:S(2)}) async-start(bf16[2,128,512]{2,1,0:T(8,128)(2,1)} %bitcast.109), calls=%async_computation.7 | async-start | bytes 524288 | tf_op jit(solution)/shard_map/all_to_all | solution.py:151
  (94 shorter events, 47.9 us)
Async XLA Ops:
  0.6 15.4 %copy-start.5 = (bf16[128,2048]{1,0:T(8,128)(2,1)S(1)}, bf16[128,2048]{1,0:T(8,128)(2,1)}, u32[]{:S(2)}) copy-start(bf16[128,2048]{1,0:T(8,128)(2,1)} %param.5) | copy-start | bytes 1572868
  0.6 24.1 %copy-start.6 = (bf16[128,2048]{1,0:T(8,128)(2,1)S(1)}, bf16[128,2048]{1,0:T(8,128)(2,1)}, u32[]{:S(2)}) copy-start(bf16[128,2048]{1,0:T(8,128)(2,1)} %param.8) | copy-start | bytes 1572868
  2.5 10.1 %all-to-all-start.2 = ((bf16[128,2,512]{0,2,1:T(8,128)(2,1)}), bf16[128,2,512]{0,2,1:T(8,128)(2,1)S(1)}, u32[]{:S(2)}, u32[]{:S(2)}) async-start(bf16[128,2,512]{0,2,1:T(8,128)(2,1)} %bitcast.5), calls=%async_computation.2 | async-start | bytes 524288 | tf_op jit(solution)/shard_map/all_to_all | solution.py:39
  12.6 8.6 %all-to-all-start.1 = ((bf16[128,2,512]{2,0,1:T(8,128)(2,1)}), bf16[128,2,512]{2,0,1:T(8,128)(2,1)S(1)}, u32[]{:S(2)}, u32[]{:S(2)}) async-start(bf16[128,2,512]{2,0,1:T(8,128)(2,1)} %bitcast.378), calls=%async_computation.1 | async-start | bytes 524288 | tf_op jit(solution)/shard_map/all_to_all | solution.py:38
  21.2 10.1 %all-to-all-start = ((bf16[128,2,1024]{2,0,1:T(8,128)(2,1)}), bf16[128,2,1024]{2,0,1:T(8,128)(2,1)S(1)}, u32[]{:S(2)}, u32[]{:S(2)}) async-start(bf16[128,2,1024]{2,0,1:T(8,128)(2,1)} %bitcast.377), calls=%async_computation | async-start | bytes 1048576 | tf_op jit(solution)/shard_map/all_to_all | solution.py:37
  31.3 22.0 %all-to-all-start.4 = ((bf16[128,2,1024]{0,2,1:T(8,128)(2,1)}), bf16[128,2,1024]{0,2,1:T(8,128)(2,1)S(1)}, u32[]{:S(2)}, u32[]{:S(2)}) async-start(bf16[128,2,1024]{0,2,1:T(8,128)(2,1)} %bitcast.36), calls=%async_computation.4 | async-start | bytes 1048576 | tf_op jit(solution)/shard_map/all_to_all | solution.py:40
  35.6 20.1 %collective-permute-start.3 = (bf16[2,256,512]{1,2,0:T(8,128)(2,1)}, bf16[2,256,512]{1,2,0:T(8,128)(2,1)}, u32[]{:S(2)}, u32[]{:S(2)}) collective-permute-start(bf16[2,256,512]{1,2,0:T(8,128)(2,1)} %pad_maximum_fusion), channel_id=1, source_target_pairs={{0,8},{2,10},{4,12},{6,14},{8,16},{10,18},{12,20},{14,22},{16,24},... | collective-permute-start | bytes 1572872 | tf_op jit(solution)/shard_map/ppermute | solution.py:16
  40.9 16.4 %collective-permute-start.2 = (bf16[2,256,512]{1,2,0:T(8,128)(2,1)}, bf16[2,256,512]{1,2,0:T(8,128)(2,1)}, u32[]{:S(2)}, u32[]{:S(2)}) collective-permute-start(bf16[2,256,512]{1,2,0:T(8,128)(2,1)} %pad_maximum_fusion), channel_id=1, source_target_pairs={{0,6},{2,8},{4,10},{6,12},{8,14},{10,16},{12,18},{14,20},{16,22},{... | collective-permute-start | bytes 1572872 | tf_op jit(solution)/shard_map/ppermute | solution.py:16
  43.0 18.9 %collective-permute-start.1 = (bf16[2,256,512]{1,2,0:T(8,128)(2,1)}, bf16[2,256,512]{1,2,0:T(8,128)(2,1)}, u32[]{:S(2)}, u32[]{:S(2)}) collective-permute-start(bf16[2,256,512]{1,2,0:T(8,128)(2,1)} %pad_maximum_fusion), channel_id=1, source_target_pairs={{0,4},{2,6},{4,8},{6,10},{8,12},{10,14},{12,16},{14,18},{16,20},{1... | collective-permute-start | bytes 1572872 | tf_op jit(solution)/shard_map/ppermute | solution.py:16
  47.3 16.3 %collective-permute-start = (bf16[2,256,512]{1,2,0:T(8,128)(2,1)}, bf16[2,256,512]{1,2,0:T(8,128)(2,1)}, u32[]{:S(2)}, u32[]{:S(2)}) collective-permute-start(bf16[2,256,512]{1,2,0:T(8,128)(2,1)} %pad_maximum_fusion), channel_id=1, source_target_pairs={{0,2},{2,4},{4,6},{6,8},{8,10},{10,12},{12,14},{14,16},{16,18},{18... | collective-permute-start | bytes 1572872 | tf_op jit(solution)/shard_map/ppermute | solution.py:16
  68.5 1.0 copy-start.3
  82.0 8.7 %copy-start.7 = (bf16[256,4,128]{0,2,1:T(8,128)(2,1)S(1)}, bf16[256,4,128]{0,2,1:T(8,128)(2,1)}, u32[]{:S(2)}) copy-start(bf16[256,4,128]{0,2,1:T(8,128)(2,1)} %reshape_squeeze_stack.9) | copy-start | bytes 786436
  82.0 30.4 %collective-permute-start.4 = (bf16[2,256,512]{1,2,0:T(8,128)(2,1)}, bf16[2,256,512]{1,2,0:T(8,128)(2,1)}, u32[]{:S(2)}, u32[]{:S(2)}) collective-permute-start(bf16[2,256,512]{1,2,0:T(8,128)(2,1)} %pad_maximum_fusion.1), channel_id=1, source_target_pairs={{2,0},{4,2},{6,4},{8,6},{10,8},{12,10},{14,12},{16,14},{18,16},{20... | collective-permute-start | bytes 1572872 | tf_op jit(solution)/shard_map/ppermute | solution.py:16
  84.8 32.8 %collective-permute-start.5 = (bf16[2,256,512]{1,2,0:T(8,128)(2,1)}, bf16[2,256,512]{1,2,0:T(8,128)(2,1)}, u32[]{:S(2)}, u32[]{:S(2)}) collective-permute-start(bf16[2,256,512]{1,2,0:T(8,128)(2,1)} %pad_maximum_fusion.2), channel_id=1, source_target_pairs={{4,0},{6,2},{8,4},{10,6},{12,8},{14,10},{16,12},{18,14},{20,16},{2... | collective-permute-start | bytes 1572872 | tf_op jit(solution)/shard_map/ppermute | solution.py:16
  87.1 34.0 %collective-permute-start.6 = (bf16[2,256,512]{1,2,0:T(8,128)(2,1)}, bf16[2,256,512]{1,2,0:T(8,128)(2,1)}, u32[]{:S(2)}, u32[]{:S(2)}) collective-permute-start(bf16[2,256,512]{1,2,0:T(8,128)(2,1)} %pad_maximum_fusion.3), channel_id=1, source_target_pairs={{6,0},{8,2},{10,4},{12,6},{14,8},{16,10},{18,12},{20,14},{22,16},{... | collective-permute-start | bytes 1572872 | tf_op jit(solution)/shard_map/ppermute | solution.py:16
  89.3 3.2 %copy-start.2 = (bf16[256,4,128]{2,1,0:T(4,128)(2,1)S(1)}, bf16[256,4,128]{2,1,0:T(4,128)(2,1)}, u32[]{:S(2)}) copy-start(bf16[256,4,128]{2,1,0:T(4,128)(2,1)} %reshape_squeeze_stack.8) | copy-start | bytes 786436
  89.3 51.5 %collective-permute-start.7 = (bf16[2,256,512]{1,2,0:T(8,128)(2,1)}, bf16[2,256,512]{1,2,0:T(8,128)(2,1)}, u32[]{:S(2)}, u32[]{:S(2)}) collective-permute-start(bf16[2,256,512]{1,2,0:T(8,128)(2,1)} %pad_maximum_fusion.4), channel_id=1, source_target_pairs={{8,0},{10,2},{12,4},{14,6},{16,8},{18,10},{20,12},{22,14},{24,16},... | collective-permute-start | bytes 1572872 | tf_op jit(solution)/shard_map/ppermute | solution.py:16
  91.5 1.0 copy-start
  97.7 11.2 %all-to-all-start.5 = ((bf16[2,128,1024]{2,1,0:T(8,128)(2,1)}), bf16[2,128,1024]{2,1,0:T(8,128)(2,1)}, u32[]{:S(2)}, u32[]{:S(2)}) async-start(bf16[2,128,1024]{2,1,0:T(8,128)(2,1)} %convert_element_type.105), calls=%async_computation.5 | async-start | bytes 1048576 | tf_op jit(solution)/shard_map/all_to_all | solution.py:149
  105.8 1.5 copy-start.1
  107.3 33.4 %copy-start.4 = (f32[4,256,128,1]{1,2,3,0:T(8,128)S(1)}, f32[4,256,128,1]{1,2,3,0:T(8,128)}, u32[]{:S(2)}) copy-start(f32[4,256,128,1]{1,2,3,0:T(8,128)} %fusion.61) | copy-start | bytes 1572868
  108.9 34.6 %all-to-all-start.3 = ((bf16[2,128,1024]{1,2,0:T(8,128)(2,1)}), bf16[2,128,1024]{1,2,0:T(8,128)(2,1)S(1)}, u32[]{:S(2)}, u32[]{:S(2)}) async-start(bf16[2,128,1024]{1,2,0:T(8,128)(2,1)} %copy.244), calls=%async_computation.3 | async-start | bytes 1048576 | tf_op jit(solution)/shard_map/all_to_all | solution.py:148
  143.5 8.6 %all-to-all-start.6 = ((bf16[2,128,512]{2,1,0:T(8,128)(2,1)}), bf16[2,128,512]{2,1,0:T(8,128)(2,1)S(1)}, u32[]{:S(2)}, u32[]{:S(2)}) async-start(bf16[2,128,512]{2,1,0:T(8,128)(2,1)} %bitcast.106), calls=%async_computation.6 | async-start | bytes 524288 | tf_op jit(solution)/shard_map/all_to_all | solution.py:150
  152.1 8.6 %all-to-all-start.7 = ((bf16[2,128,512]{2,1,0:T(8,128)(2,1)}), bf16[2,128,512]{2,1,0:T(8,128)(2,1)S(1)}, u32[]{:S(2)}, u32[]{:S(2)}) async-start(bf16[2,128,512]{2,1,0:T(8,128)(2,1)} %bitcast.109), calls=%async_computation.7 | async-start | bytes 524288 | tf_op jit(solution)/shard_map/all_to_all | solution.py:151
where the time goes:
time: 163 us; the launch traced here: 162 us
  waiting for transfers between devices  50 us (31%)
  starting transfers between devices  48.9 us (30%)
  local copies, waits for them, and re-layouts  29.7 us (18%)
  matrix products  21.5 us (13%)
  other arithmetic  10.5 us (6%)
    ppermute x8, waiting for transfers between devices, shifted(): lax.ppermute(value, axis, [(source, source + steps) for source in range(i...  31.4 us
    ppermute x8, starting transfers between devices, shifted(): lax.ppermute(value, axis, [(source, source + steps) for source in range(i...  19.7 us
    unnamed x22, local copies, waits for them, and re-layouts  7.82 us
    dot_general x5, matrix products, body(): jnp.einsum('ihjm,ihjx->mix', probabilities.astype(jnp.bfloat16), grouped_...  4.4 us
    all_to_all x1, waiting for transfers between devices, body(): lax.all_to_all(grad_k_rows, 'tensor', split_axis=0, concat_axis=1, tiled=...  4.33 us
    all_to_all x1, waiting for transfers between devices, body(): lax.all_to_all(key, 'tensor', split_axis=1, concat_axis=0, tiled=True)  4.3 us
    all_to_all x1, starting transfers between devices, body(): lax.all_to_all(grad_q_rows, 'tensor', split_axis=0, concat_axis=1, tiled=...  4.21 us
    all_to_all x1, starting transfers between devices, body(): lax.all_to_all(value, 'tensor', split_axis=1, concat_axis=0, tiled=True)  4.21 us
  transfers between devices with their start and end apart: 16, of which 10 were waited for; matrix products, arithmetic and copies ran while one was open for 23% of the time, Pallas kernels for 0%

commit v1 on v0

v1 whole, which is shorter than its diff:
```python
import functools

import jax
import jax.numpy as jnp
from jax import lax
from jax.experimental import pallas as pl
from jax.experimental.pallas import tpu as pltpu
from jax.sharding import PartitionSpec as P

HEAD_DIM = 128
WINDOW = 1024
CORES = 2
TILE = 128

logit_scale = 168.0 ** (-0.5)
exp2_scale = logit_scale * 1.4426950408889634

ANY = pl.BlockSpec(memory_space=pl.ANY)
VMEM = pl.BlockSpec(memory_space=pltpu.VMEM)
F32 = jnp.float32
BF16 = jnp.bfloat16


def member():
    return lax.rem(lax.axis_index("pipe"), CORES) * lax.axis_size("tensor") + lax.axis_index(
        "tensor"
    )


def swap(value, mask):
    count = lax.axis_size("pipe") * lax.axis_size("tensor")
    return lax.ppermute(value, ("pipe", "tensor"), [(i, i ^ mask) for i in range(count)])


def shifted(value, groups, size):
    count = lax.axis_size("pipe") * lax.axis_size("tensor")
    step = groups * size
    pairs = [(i, i + step) for i in range(count) if 0 <= i + step < count]
    return lax.ppermute(value, ("pipe", "tensor"), pairs)


def place(index, width):
    return pl.ds(pl.multiple_of(index * width, width), width)


def run_copies(copies, sems):
    started = []
    for at, (source, target) in enumerate(copies):
        copy = pltpu.make_async_copy(source, target, sems.at[at])
        copy.start()
        started.append(copy)
    for copy in started:
        copy.wait()


def pack_body(size, first, widths, *refs):
    arrays, pieces, sems = refs[: len(widths)], refs[len(widths) : -1], refs[-1]
    me = member()
    copies = []
    for at, piece in enumerate(pieces):
        other = lax.bitwise_xor(me, first + at)
        start = 0
        for array, width in zip(arrays, widths):
            copies.append((array.at[:, place(other, width)], piece.at[:, start : start + width]))
            start += width
    run_copies(copies, sems)


def pack(arrays, size, first):
    rows = arrays[0].shape[0]
    widths = [array.shape[1] // size for array in arrays]
    count = size - first
    return pl.pallas_call(
        functools.partial(pack_body, size, first, widths),
        out_shape=[jax.ShapeDtypeStruct((rows, sum(widths)), BF16)] * count,
        in_specs=[ANY] * len(arrays),
        out_specs=[ANY] * count,
        scratch_shapes=[pltpu.SemaphoreType.DMA((count * len(arrays),))],
        name="pack",
    )(*arrays)


def join_body(size, rows, *refs):
    pieces, out, sems = refs[:size], refs[size], refs[size + 1]
    me = member()
    run_copies(
        [(pieces[j], out.at[place(lax.bitwise_xor(me, j), rows), :]) for j in range(size)], sems
    )


def join(pieces):
    size, (rows, cols) = len(pieces), pieces[0].shape
    return pl.pallas_call(
        functools.partial(join_body, size, rows),
        out_shape=jax.ShapeDtypeStruct((size * rows, cols), BF16),
        in_specs=[ANY] * size,
        out_specs=ANY,
        scratch_shapes=[pltpu.SemaphoreType.DMA((size,))],
        name="join",
    )(*pieces)


def combine_body(size, rows, own, one, two, *refs):
    pieces, total, sems = refs[:size], refs[size], refs[size + 1]
    total[...] = (own[...] + one[...].astype(F32) + two[...].astype(F32)).astype(BF16)
    me = member()
    run_copies(
        [(total.at[place(lax.bitwise_xor(me, j), rows), :], pieces[j]) for j in range(size)], sems
    )


def combine(own, one, two, size):
    tok, cols = own.shape
    rows = tok // size
    return pl.pallas_call(
        functools.partial(combine_body, size, rows),
        out_shape=[jax.ShapeDtypeStruct((rows, cols), BF16)] * size,
        in_specs=[VMEM] * 3,
        out_specs=[ANY] * size,
        scratch_shapes=[pltpu.VMEM((tok, cols), BF16), pltpu.SemaphoreType.DMA((size,))],
        name="combine",
    )(own, one, two)


def spread_body(size, widths, *refs):
    pieces, outs, sems = refs[:size], refs[size:-1], refs[-1]
    me = member()
    copies = []
    for j in range(size):
        other = lax.bitwise_xor(me, j)
        start = 0
        for out, width in zip(outs, widths):
            copies.append((pieces[j].at[:, start : start + width], out.at[:, place(other, width)]))
            start += width
    run_copies(copies, sems)


def spread(pieces, widths):
    size, rows = len(pieces), pieces[0].shape[0]
    return pl.pallas_call(
        functools.partial(spread_body, size, widths),
        out_shape=[jax.ShapeDtypeStruct((rows, width * size), BF16) for width in widths],
        in_specs=[ANY] * size,
        out_specs=[ANY] * len(widths),
        scratch_shapes=[pltpu.SemaphoreType.DMA((size * len(widths),))],
        name="spread",
    )(*pieces)


def dot(a, b):
    return lax.dot_general(a, b, (((1,), (0,)), ((), ())), preferred_element_type=F32)


def dot_t(a, b):
    return lax.dot_general(a, b, (((1,), (1,)), ((), ())), preferred_element_type=F32)


def fold(x, op):
    parts = [x[at : at + 8] for at in range(0, x.shape[0], 8)]
    while len(parts) > 1:
        parts = [op(*parts[at : at + 2]) if at + 1 < len(parts) else parts[at] for at in range(0, len(parts), 2)]
    return parts[0]


def attend_body(size, kv_heads, group, rows, *refs):
    refs = list(refs)
    low, q_own, g_own = refs[:3]
    received = refs[3 : 2 + size]
    kv0, kv1, kv2 = refs[2 + size : 5 + size]
    og = refs[5 + size : 5 + 2 * size]
    dkv0, dkv1, dkv2 = refs[5 + 2 * size : 8 + 2 * size]
    qs, gs, ks, vs, kt, vt, os, dqs, dk, dv, s_scr, e_scr, ds_scr, half1, half2, sems = refs[
        8 + 2 * size :
    ]
    tok = size * rows
    kw = kv_heads * HEAD_DIM
    qw = group * kw
    span = WINDOW + TILE
    me = member()
    copies = [
        (q_own.at[:, place(me, qw)], qs.at[place(me, rows), :]),
        (g_own.at[:, place(me, qw)], gs.at[place(me, rows), :]),
    ]
    for j in range(1, size):
        to = place(lax.bitwise_xor(me, j), rows)
        copies.append((received[j - 1].at[:, :qw], qs.at[to, :]))
        copies.append((received[j - 1].at[:, qw:], gs.at[to, :]))
    for at, kv in enumerate((kv2, kv1, kv0)):
        copies.append((kv.at[:, :kw], ks.at[at * tok : (at + 1) * tok, :]))
        copies.append((kv.at[:, kw:], vs.at[at * tok : (at + 1) * tok, :]))
    run_copies(copies, sems)

    dk[...] = jnp.zeros_like(dk)
    dv[...] = jnp.zeros_like(dv)
    lane = lax.broadcasted_iota(jnp.int32, (TILE, HEAD_DIM), 1)
    ones = jnp.where(lane < 2, 1.0, 0.0).astype(BF16)
    wide_lane = lax.broadcasted_iota(jnp.int32, (group * TILE, HEAD_DIM), 1)
    row_of = lax.broadcasted_iota(jnp.int32, (TILE, group * TILE), 0)
    col_of = lax.broadcasted_iota(jnp.int32, (TILE, TILE), 1)
    causal = lax.broadcasted_iota(jnp.int32, (TILE, TILE), 0) <= col_of
    causal = jnp.concatenate([causal] * group, axis=1)

    for head in range(kv_heads):
        cols = slice(head * HEAD_DIM, (head + 1) * HEAD_DIM)
        kt[...] = ks[:, cols].T
        vt[...] = vs[:, cols].T
        q_cols = [
            slice((head * group + at) * HEAD_DIM, (head * group + at + 1) * HEAD_DIM)
            for at in range(group)
        ]
        for tile in range(tok // TILE):
            base = tile * TILE
            here = slice(base, base + TILE)
            q2 = jnp.concatenate([qs[here, c] for c in q_cols], axis=0)
            g2 = jnp.concatenate([gs[here, c] for c in q_cols], axis=0)
            low_row = jnp.concatenate([low[:, here]] * group, axis=1) - base
            top = None
            for at in range(0, span, TILE):
                s = dot_t(ks[base + at : base + at + TILE, cols], q2)
                keep = row_of >= low_row - at
                if at == span - TILE:
                    keep = keep & causal
                s = jnp.where(keep, s, -1e30)
                s_scr[at : at + TILE, :] = s
                part = fold(s, jnp.maximum)
                top = part if top is None else jnp.maximum(top, part)
            top = jnp.max(top, axis=0, keepdims=True) * exp2_scale
            total = None
            for at in range(0, span, TILE):
                e = jnp.exp2(s_scr[at : at + TILE, :] * exp2_scale - top)
                e_scr[at : at + TILE, :] = e.astype(BF16)
                part = fold(e, jnp.add)
                total = part if total is None else total + part
            inv = 1.0 / jnp.sum(total, axis=0, keepdims=True)
            inv = jnp.broadcast_to(inv, (HEAD_DIM, group * TILE)).T
            out = dot(vt[:, base : base + span], e_scr[...]).T * inv
            out = out.astype(BF16)
            g2 = (g2.astype(F32) * inv).astype(BF16)
            delta = jnp.sum(g2.astype(F32) * out.astype(F32), axis=1, keepdims=True)
            high = delta.astype(BF16).astype(F32)
            extra = jnp.where(wide_lane == 0, -high, jnp.where(wide_lane == 1, high - delta, 0.0))
            g_wide = jnp.concatenate([g2, extra.astype(BF16)], axis=1)
            for at in range(0, span, TILE):
                there = slice(base + at, base + at + TILE)
                dp = dot_t(jnp.concatenate([vs[there, cols], ones], axis=1), g_wide)
                e = e_scr[at : at + TILE, :]
                ds = (e.astype(F32) * dp).astype(BF16)
                ds_scr[at : at + TILE, :] = ds
                dv[there, cols] += dot(e, g2)
                dk[there, cols] += dot(ds, q2)
            dq = (dot(kt[:, base : base + span], ds_scr[...]) * logit_scale).T.astype(BF16)
            for at, c in enumerate(q_cols):
                os[here, c] = out[at * TILE : (at + 1) * TILE]
                dqs[here, c] = dq[at * TILE : (at + 1) * TILE]

    dkv0[:, :kw] = dk[2 * tok :, :] * logit_scale
    dkv0[:, kw:] = dv[2 * tok :, :]
    for half, at in ((half1, 1), (half2, 0)):
        half[:, :kw] = (dk[at * tok : (at + 1) * tok, :] * logit_scale).astype(BF16)
        half[:, kw:] = dv[at * tok : (at + 1) * tok, :].astype(BF16)
    copies = [(half1, dkv1), (half2, dkv2)]
    for j in range(size):
        of = place(lax.bitwise_xor(me, j), rows)
        copies.append((os.at[of, :], og[j].at[:, :qw]))
        copies.append((dqs.at[of, :], og[j].at[:, qw:]))
    run_copies(copies, sems)


def attend(low, query, grad_out, received, kv0, kv1, kv2, size):
    rows = query.shape[0]
    tok = size * rows
    qw = query.shape[1] // size
    kw = kv0.shape[1] // 2
    kv_heads, group = kw // HEAD_DIM, qw // kw
    span = WINDOW + TILE
    wide = group * TILE
    half = jax.ShapeDtypeStruct((tok, 2 * kw), BF16)
    n_copies = max(2 * size + 6, 2 * size + 2)
    flops = 6 * 2 * tok * group * kv_heads * span * HEAD_DIM
    results = pl.pallas_call(
        functools.partial(attend_body, size, kv_heads, group, rows),
        out_shape=[jax.ShapeDtypeStruct((rows, 2 * qw), BF16)] * size
        + [jax.ShapeDtypeStruct((tok, 2 * kw), F32), half, half],
        in_specs=[VMEM] + [ANY] * (size + 4),
        out_specs=[ANY] * size + [VMEM, ANY, ANY],
        scratch_shapes=[
            pltpu.VMEM((tok, qw), BF16),
            pltpu.VMEM((tok, qw), BF16),
            pltpu.VMEM((3 * tok, kw), BF16),
            pltpu.VMEM((3 * tok, kw), BF16),
            pltpu.VMEM((HEAD_DIM, 3 * tok), BF16),
            pltpu.VMEM((HEAD_DIM, 3 * tok), BF16),
            pltpu.VMEM((tok, qw), BF16),
            pltpu.VMEM((tok, qw), BF16),
            pltpu.VMEM((3 * tok, kw), F32),
            pltpu.VMEM((3 * tok, kw), F32),
            pltpu.VMEM((span, wide), F32),
            pltpu.VMEM((span, wide), BF16),
            pltpu.VMEM((span, wide), BF16),
            pltpu.VMEM((tok, 2 * kw), BF16),
            pltpu.VMEM((tok, 2 * kw), BF16),
            pltpu.SemaphoreType.DMA((n_copies,)),
        ],
        compiler_params=pltpu.CompilerParams(vmem_limit_bytes=40 * 1024 * 1024),
        cost_estimate=pl.CostEstimate(
            flops=flops, bytes_accessed=8 * 1024 * 1024, transcendentals=flops // 1536
        ),
        name="attend",
    )(low, query, grad_out, *received, kv0, kv1, kv2)
    return results[:size], results[size:]


def lowest_key(segment_ids, tok):
    start = (lax.axis_index("pipe") // CORES) * tok
    padded = jnp.concatenate([jnp.full((WINDOW,), -1, jnp.int32), segment_ids])
    keys = lax.dynamic_slice_in_dim(padded, start, WINDOW + tok, 0)
    queries = lax.dynamic_slice_in_dim(segment_ids, start, tok, 0)
    before = jnp.sum((keys[:, None] < queries[None, :]).astype(jnp.int32), axis=0)
    return jnp.maximum(before, jnp.arange(1, tok + 1, dtype=jnp.int32))[None, :]


def body(query, key, value, grad_out, segment_ids):
    size = CORES * lax.axis_size("tensor")
    rows = query.shape[0]
    tok = size * rows
    assert WINDOW == 2 * tok
    q_width, k_width = query.shape[1] // size, key.shape[1] // size
    low = lowest_key(segment_ids, tok)

    kv_pieces = pack((key, value), size, 0)
    kv_pieces = [kv_pieces[0]] + [swap(kv_pieces[j], j) for j in range(1, size)]
    kv0 = join(kv_pieces)
    qg_pieces = pack((query, grad_out), size, 1)
    kv0, qg_pieces = lax.optimization_barrier((kv0, qg_pieces))
    kv1 = shifted(kv0, 1, size)
    kv2 = shifted(kv0, 2, size)
    qg_pieces = [swap(qg_pieces[j - 1], j) for j in range(1, size)]

    og, (dkv0, dkv1, dkv2) = attend(low, query, grad_out, qg_pieces, kv0, kv1, kv2, size)

    back1 = shifted(dkv1, -1, size)
    back2 = shifted(dkv2, -2, size)
    og = [og[0]] + [swap(og[j], j) for j in range(1, size)]
    grads = combine(dkv0, back1, back2, size)
    grads = [grads[0]] + [swap(grads[j], j) for j in range(1, size)]
    attn_out, grad_query = spread(og, (q_width, q_width))
    grad_key, grad_value = spread(grads, (k_width, k_width))
    return (attn_out, grad_query, grad_key, grad_value)


def solution(mesh):
    placed = P(("pipe", "tensor"), None)
    return jax.shard_map(
        body,
        mesh=mesh,
        in_specs=(placed, placed, placed, placed, P()),
        out_specs=(placed, placed, placed, placed),
        check_vma=False,
    )
```

time: 163 us -> 195 us (1.20)
  Pallas kernels: 0 us -> 128 us
  starting transfers between devices: 48.9 us -> 19.8 us
  local copies, waits for them, and re-layouts: 29.7 us -> 5.87 us
  matrix products: 21.5 us -> 0 us
  waiting for transfers between devices: 50 us -> 39.7 us
  other arithmetic: 10.5 us -> 0.39 us
    pallas_call x0 -> x7, Pallas kernels: none -> 128 us  [the longest x2 50 us: spread(): pl.pallas_call(functools.partial(spread_body, size, widths), out_shape=[j...]
    all_to_all x8 -> x0, starting transfers between devices: 29.2 us -> none  [the longest x1 4.21 us: body(): lax.all_to_all(grad_q_rows, 'tensor', split_axis=0, concat_axis=1, tiled=...]
    dot_general x30 -> x0, matrix products: 21.5 us -> none  [the longest x5 4.4 us: body(): jnp.einsum('ihjm,ihjx->mix', probabilities.astype(jnp.bfloat16), grouped_...]
    all_to_all x8 -> x0, waiting for transfers between devices: 18.6 us -> none  [the longest x1 4.33 us: body(): lax.all_to_all(grad_k_rows, 'tensor', split_axis=0, concat_axis=1, tiled=...]
    all_to_all x9 -> x0, local copies, waits for them, and re-layouts: 8.82 us -> none  [the longest x2 3.86 us: body(): lax.all_to_all(out_rows, 'tensor', split_axis=0, concat_axis=1, tiled=True)]
    ppermute x8 -> x16, waiting for transfers between devices: 31.4 us -> 39.7 us  [the longest x4 29.8 us: shifted(): return lax.ppermute(value, ('pipe', 'tensor'), pairs)]
    another operation x6 -> x0, other arithmetic: 6.08 us -> none  [the longest x4 3.43 us: body(): jnp.stack((dk_term.reshape(tok, kv_local * HEAD_DIM), dv_term.reshape(tok...]
    slice x7 -> x0, local copies, waits for them, and re-layouts: 5.97 us -> none  [the longest x3 3.19 us: body(): weighted_value_tensor = tiles[lag][1].reshape(tok, kv_local, HEAD_DIM)]
  transfers between devices with their start and end apart: 16 -> 16, of which waited for: 10 -> 4; matrix products, arithmetic and copies ran while one was open for 23% -> 0% of each run, Pallas kernels for 0% -> 31%
where the time goes in v1:
time: 195 us; the launch traced here: 194 us
  Pallas kernels  128 us (66%)
  waiting for transfers between devices  39.7 us (20%)
  starting transfers between devices  19.8 us (10%)
  local copies, waits for them, and re-layouts  5.87 us (3%)
    pallas_call x2, Pallas kernels, spread(): pl.pallas_call(functools.partial(spread_body, size, widths), out_shape=[j...  50 us
    pallas_call x2, Pallas kernels, pack(): pl.pallas_call(functools.partial(pack_body, size, first, widths), out_sha...  42 us
    ppermute x4, waiting for transfers between devices, shifted(): return lax.ppermute(value, ('pipe', 'tensor'), pairs)  29.8 us
    pallas_call x1, Pallas kernels, join(): pl.pallas_call(functools.partial(join_body, size, rows), out_shape=jax.Sh...  17 us
    pallas_call x1, Pallas kernels, attend(): pl.pallas_call(functools.partial(attend_body, size, kv_heads, group, rows...  16.1 us
    ppermute x4, starting transfers between devices, shifted(): return lax.ppermute(value, ('pipe', 'tensor'), pairs)  9.97 us
    ppermute x12, waiting for transfers between devices, swap(): lax.ppermute(value, ('pipe', 'tensor'), [(i, i ^ mask) for i in range(cou...  9.83 us
    ppermute x12, starting transfers between devices, swap(): lax.ppermute(value, ('pipe', 'tensor'), [(i, i ^ mask) for i in range(cou...  9.81 us
  transfers between devices with their start and end apart: 16, of which 4 were waited for; matrix products, arithmetic and copies ran while one was open for 0% of the time, Pallas kernels for 31%

profile of v1, /device:TPU:0, one launch (start us, length us, event | category | flops | bytes accessed | tf_op | source)
XLA Modules:
  0.0 194.2 jit_solution(18313602176425569000)
XLA Ops:
  0.6 17.1 %pack.2 = (bf16[128,512]{1,0:T(8,128)(2,1)}, bf16[128,512]{1,0:T(8,128)(2,1)}, bf16[128,512]{1,0:T(8,128)(2,1)}, bf16[128,512]{1,0:T(8,128)(2,1)}) custom-call(bf16[128,1024]{1,0:T(8,128)(2,1)} %refs_0_.2, bf16[128,1024]{1,0:T(8,128)(2,1)} %refs_1_.3), custom_call_target="tpu_custom_call" | custom-call | tf_op jit(solution)/shard_map/pack/pallas_call | solution.py:73
  17.7 3.0 %collective-permute-start = (bf16[128,512]{1,0:T(8,128)(2,1)}, bf16[128,512]{1,0:T(8,128)(2,1)S(1)}, u32[]{:S(2)}, u32[]{:S(2)}) collective-permute-start(bf16[128,512]{1,0:T(8,128)(2,1)} %get-tuple-element.31), channel_id=1, source_target_pairs={{0,1},{1,0},{2,3},{3,2},{4,5},{5,4},{6,7},{7,6},{8,9},{9,8},{10,11... | collective-permute-start | bytes 393224 | tf_op jit(solution)/shard_map/ppermute | solution.py:32
  20.7 0.2 collective-permute-start.2
  20.9 25.0 %pack.3 = (bf16[128,1024]{1,0:T(8,128)(2,1)}, bf16[128,1024]{1,0:T(8,128)(2,1)}, bf16[128,1024]{1,0:T(8,128)(2,1)}) custom-call(bf16[128,2048]{1,0:T(8,128)(2,1)} %refs_1_.5, bf16[128,2048]{1,0:T(8,128)(2,1)} %refs_2_.1), custom_call_target="tpu_custom_call" | custom-call | tf_op jit(solution)/shard_map/pack/pallas_call | solution.py:73
  46.0 0.6 copy-done.13
  46.7 17.0 %join.1.refs_6_ = bf16[512,512]{1,0:T(8,128)(2,1)} custom-call(bf16[128,512]{1,0:T(8,128)(2,1)} %get-tuple-element.30.refs_0_, bf16[128,512]{1,0:T(8,128)(2,1)} %copy-done.13, bf16[128,512]{1,0:T(8,128)(2,1)} %copy-done.14, bf16[128,512]{1,0:T(8,128)(2,1)} %copy-done.15), custom_call_target="tpu_custom_call" | custom-call | tf_op jit(solution)/shard_map/join/pallas_call | solution.py:93
  63.7 3.9 %collective-permute-start.7 = (bf16[512,512]{1,0:T(8,128)(2,1)}, bf16[512,512]{1,0:T(8,128)(2,1)S(1)}, u32[]{:S(2)}, u32[]{:S(2)}) collective-permute-start(bf16[512,512]{1,0:T(8,128)(2,1)} %join.1.refs_6_), channel_id=1, source_target_pairs={{0,8},{1,9},{2,10},{3,11},{4,12},{5,13},{6,14},{7,15},{8,16},{9,17... | collective-permute-start | bytes 1572872 | tf_op jit(solution)/shard_map/ppermute | solution.py:39
  67.7 3.5 %collective-permute-start.6 = (bf16[512,512]{1,0:T(8,128)(2,1)}, bf16[512,512]{1,0:T(8,128)(2,1)S(1)}, u32[]{:S(2)}, u32[]{:S(2)}) collective-permute-start(bf16[512,512]{1,0:T(8,128)(2,1)} %join.1.refs_6_), channel_id=1, source_target_pairs={{0,4},{1,5},{2,6},{3,7},{4,8},{5,9},{6,10},{7,11},{8,12},{9,13},{1... | collective-permute-start | bytes 1572872 | tf_op jit(solution)/shard_map/ppermute | solution.py:39
  71.3 1.5 collective-permute-start.3
  72.9 0.6 collective-permute-start.5
  73.5 0.4 convert_reduce_fusion
  73.9 6.7 %collective-permute-done.3.refs_3_ = bf16[128,1024]{1,0:T(8,128)(2,1)S(1)} collective-permute-done((bf16[128,1024]{1,0:T(8,128)(2,1)S(1)}, bf16[128,1024]{1,0:T(8,128)(2,1)S(1)}, u32[]{:S(2)}, u32[]{:S(2)}) %collective-permute-start.3) | collective-permute-done | bytes 262176 | tf_op jit(solution)/shard_map/ppermute | solution.py:32
  80.6 3.1 %collective-permute-done.5.refs_5_ = bf16[128,1024]{1,0:T(8,128)(2,1)S(1)} collective-permute-done((bf16[128,1024]{1,0:T(8,128)(2,1)S(1)}, bf16[128,1024]{1,0:T(8,128)(2,1)S(1)}, u32[]{:S(2)}, u32[]{:S(2)}) %collective-permute-start.5) | collective-permute-done | bytes 262176 | tf_op jit(solution)/shard_map/ppermute | solution.py:32
  83.7 1.0 copy-done.3
  84.8 16.1 %attend.1 = (bf16[128,1024]{1,0:T(8,128)(2,1)S(1)}, bf16[128,1024]{1,0:T(8,128)(2,1)S(1)}, bf16[128,1024]{1,0:T(8,128)(2,1)S(1)}, bf16[128,1024]{1,0:T(8,128)(2,...) custom-call(s32[1,512]{1,0:T(1,128)S(1)} %add_maximum_fusion.refs_0_, ...), custom_call_target="tpu_custom_call" | custom-call | flops 3623878656 | bytes 8388608 | tf_op jit(solution)/shard_map/attend/pallas_call | solution.py:280
  100.8 1.0 copy-done
  101.8 0.7 copy-done.4
  102.5 1.3 collective-permute-start.11
  103.8 1.3 collective-permute-start.12
  105.1 1.0 collective-permute-start.8
  106.1 1.1 collective-permute-start.9
  107.2 0.2 collective-permute-start.10
  107.4 16.8 %collective-permute-done.11.one = bf16[512,512]{1,0:T(8,128)(2,1)S(1)} collective-permute-done((bf16[512,512]{1,0:T(8,128)(2,1)S(1)}, bf16[512,512]{1,0:T(8,128)(2,1)S(1)}, u32[]{:S(2)}, u32[]{:S(2)}) %collective-permute-start.11) | collective-permute-done | bytes 524320 | tf_op jit(solution)/shard_map/ppermute | solution.py:39
  124.1 13.0 %collective-permute-done.12.two = bf16[512,512]{1,0:T(8,128)(2,1)S(1)} collective-permute-done((bf16[512,512]{1,0:T(8,128)(2,1)S(1)}, bf16[512,512]{1,0:T(8,128)(2,1)S(1)}, u32[]{:S(2)}, u32[]{:S(2)}) %collective-permute-start.12) | collective-permute-done | bytes 524320 | tf_op jit(solution)/shard_map/ppermute | solution.py:39
  137.2 0.8 copy-done.6
  138.0 2.5 %combine.1 = (bf16[128,512]{1,0:T(8,128)(2,1)}, bf16[128,512]{1,0:T(8,128)(2,1)}, bf16[128,512]{1,0:T(8,128)(2,1)}, bf16[128,512]{1,0:T(8,128)(2,1)}) custom-call(f32[512,512]{1,0:T(8,128)} %copy-done, bf16[512,512]{1,0:T(8,128)(2,1)} %copy-done.5, bf16[512,512]{1,0:T(8,128)(2,1)} %copy-done.6), custom_call_target="tpu_custom_call" | custom-call | tf_op jit(solution)/shard_map/combine/pallas_call | solution.py:115
  140.5 1.6 collective-permute-start.13
  142.1 0.6 collective-permute-start.15
  142.8 0.6 copy-done.8
  143.5 32.9 %spread.2 = (bf16[128,2048]{1,0:T(8,128)(2,1)}, bf16[128,2048]{1,0:T(8,128)(2,1)}) custom-call(bf16[128,1024]{1,0:T(8,128)(2,1)} %copy-done.4, bf16[128,1024]{1,0:T(8,128)(2,1)} %copy-done.7, bf16[128,1024]{1,0:T(8,128)(2,1)} %copy-done.8, bf16[128,1024]{1,0:T(8,128)(2,1)} %copy-done.9), custom_call_target="tpu_custom_call" | custom-call | tf_op jit(solution)/shard_map/spread/pallas_call | solution.py:140
  176.5 0.6 copy-done.10
  177.2 17.1 %spread.3 = (bf16[128,1024]{1,0:T(8,128)(2,1)}, bf16[128,1024]{1,0:T(8,128)(2,1)}) custom-call(bf16[128,512]{1,0:T(8,128)(2,1)} %get-tuple-element.50.refs_0_, bf16[128,512]{1,0:T(8,128)(2,1)} %copy-done.10, bf16[128,512]{1,0:T(8,128)(2,1)} %copy-done.11, bf16[128,512]{1,0:T(8,128)(2,1)} %copy-done.12), custom_call_target="tpu_custom_call" | custom-call | tf_op jit(solution)/shard_map/spread/pallas_call | solution.py:140
  (51 shorter events, 0.6 us)
Async XLA Ops:
  17.7 28.3 %collective-permute-start = (bf16[128,512]{1,0:T(8,128)(2,1)}, bf16[128,512]{1,0:T(8,128)(2,1)S(1)}, u32[]{:S(2)}, u32[]{:S(2)}) collective-permute-start(bf16[128,512]{1,0:T(8,128)(2,1)} %get-tuple-element.31), channel_id=1, source_target_pairs={{0,1},{1,0},{2,3},{3,2},{4,5},{5,4},{6,7},{7,6},{8,9},{9,8},{10,11... | collective-permute-start | bytes 393224 | tf_op jit(solution)/shard_map/ppermute | solution.py:32
  20.7 25.3 %collective-permute-start.1 = (bf16[128,512]{1,0:T(8,128)(2,1)}, bf16[128,512]{1,0:T(8,128)(2,1)S(1)}, u32[]{:S(2)}, u32[]{:S(2)}) collective-permute-start(bf16[128,512]{1,0:T(8,128)(2,1)} %get-tuple-element.32), channel_id=1, source_target_pairs={{0,2},{1,3},{2,0},{3,1},{4,6},{5,7},{6,4},{7,5},{8,10},{9,11},{10,... | collective-permute-start | bytes 393224 | tf_op jit(solution)/shard_map/ppermute | solution.py:32
  20.7 50.5 %copy-start.16 = (s32[4096]{0:T(1024)S(1)}, s32[4096]{0:T(1024)}, u32[]{:S(2)}) copy-start(s32[4096]{0:T(1024)} %param.9) | copy-start | bytes 49156
  20.7 63.0 %copy-start.1 = (bf16[128,2048]{1,0:T(8,128)(2,1)S(1)}, bf16[128,2048]{1,0:T(8,128)(2,1)}, u32[]{:S(2)}) copy-start(bf16[128,2048]{1,0:T(8,128)(2,1)} %refs_1_.5) | copy-start | bytes 1572868
  20.7 63.0 %copy-start.2 = (bf16[128,2048]{1,0:T(8,128)(2,1)S(1)}, bf16[128,2048]{1,0:T(8,128)(2,1)}, u32[]{:S(2)}) copy-start(bf16[128,2048]{1,0:T(8,128)(2,1)} %refs_2_.1) | copy-start | bytes 1572868
  20.7 25.3 %collective-permute-start.2 = (bf16[128,512]{1,0:T(8,128)(2,1)}, bf16[128,512]{1,0:T(8,128)(2,1)S(1)}, u32[]{:S(2)}, u32[]{:S(2)}) collective-permute-start(bf16[128,512]{1,0:T(8,128)(2,1)} %get-tuple-element.33), channel_id=1, source_target_pairs={{0,3},{1,2},{2,1},{3,0},{4,7},{5,6},{6,5},{7,4},{8,11},{9,10},{10,... | collective-permute-start | bytes 393224 | tf_op jit(solution)/shard_map/ppermute | solution.py:32
  45.9 25.4 %copy-start.19 = (bf16[128,1024]{1,0:T(8,128)(2,1)S(1)}, bf16[128,1024]{1,0:T(8,128)(2,1)}, u32[]{:S(2)}) copy-start(bf16[128,1024]{1,0:T(8,128)(2,1)} %get-tuple-element.37) | copy-start | bytes 786436
  45.9 26.9 %copy-start.18 = (bf16[128,1024]{1,0:T(8,128)(2,1)S(1)}, bf16[128,1024]{1,0:T(8,128)(2,1)}, u32[]{:S(2)}) copy-start(bf16[128,1024]{1,0:T(8,128)(2,1)} %get-tuple-element.38) | copy-start | bytes 786436
  45.9 26.9 %copy-start.17 = (bf16[128,1024]{1,0:T(8,128)(2,1)S(1)}, bf16[128,1024]{1,0:T(8,128)(2,1)}, u32[]{:S(2)}) copy-start(bf16[128,1024]{1,0:T(8,128)(2,1)} %get-tuple-element.39) | copy-start | bytes 786436
  46.0 0.7 copy-start.15
  63.7 20.0 %collective-permute-start.7 = (bf16[512,512]{1,0:T(8,128)(2,1)}, bf16[512,512]{1,0:T(8,128)(2,1)S(1)}, u32[]{:S(2)}, u32[]{:S(2)}) collective-permute-start(bf16[512,512]{1,0:T(8,128)(2,1)} %join.1.refs_6_), channel_id=1, source_target_pairs={{0,8},{1,9},{2,10},{3,11},{4,12},{5,13},{6,14},{7,15},{8,16},{9,17... | collective-permute-start | bytes 1572872 | tf_op jit(solution)/shard_map/ppermute | solution.py:39
  67.7 16.0 %collective-permute-start.6 = (bf16[512,512]{1,0:T(8,128)(2,1)}, bf16[512,512]{1,0:T(8,128)(2,1)S(1)}, u32[]{:S(2)}, u32[]{:S(2)}) collective-permute-start(bf16[512,512]{1,0:T(8,128)(2,1)} %join.1.refs_6_), channel_id=1, source_target_pairs={{0,4},{1,5},{2,6},{3,7},{4,8},{5,9},{6,10},{7,11},{8,12},{9,13},{1... | collective-permute-start | bytes 1572872 | tf_op jit(solution)/shard_map/ppermute | solution.py:39
  71.3 9.2 %collective-permute-start.3 = (bf16[128,1024]{1,0:T(8,128)(2,1)S(1)}, bf16[128,1024]{1,0:T(8,128)(2,1)S(1)}, u32[]{:S(2)}, u32[]{:S(2)}) collective-permute-start(bf16[128,1024]{1,0:T(8,128)(2,1)S(1)} %copy-done.19), channel_id=1, source_target_pairs={{0,1},{1,0},{2,3},{3,2},{4,5},{5,4},{6,7},{7,6},{8,9},{9,8},{10,11... | collective-permute-start | bytes 786440 | tf_op jit(solution)/shard_map/ppermute | solution.py:32
  72.8 7.7 %collective-permute-start.4 = (bf16[128,1024]{1,0:T(8,128)(2,1)S(1)}, bf16[128,1024]{1,0:T(8,128)(2,1)S(1)}, u32[]{:S(2)}, u32[]{:S(2)}) collective-permute-start(bf16[128,1024]{1,0:T(8,128)(2,1)S(1)} %copy-done.18), channel_id=1, source_target_pairs={{0,2},{1,3},{2,0},{3,1},{4,6},{5,7},{6,4},{7,5},{8,10},{9,11},{10,... | collective-permute-start | bytes 786440 | tf_op jit(solution)/shard_map/ppermute | solution.py:32
  72.9 10.8 %collective-permute-start.5 = (bf16[128,1024]{1,0:T(8,128)(2,1)S(1)}, bf16[128,1024]{1,0:T(8,128)(2,1)S(1)}, u32[]{:S(2)}, u32[]{:S(2)}) collective-permute-start(bf16[128,1024]{1,0:T(8,128)(2,1)S(1)} %copy-done.17), channel_id=1, source_target_pairs={{0,3},{1,2},{2,1},{3,0},{4,7},{5,6},{6,5},{7,4},{8,11},{9,10},{10,... | collective-permute-start | bytes 786440 | tf_op jit(solution)/shard_map/ppermute | solution.py:32
  83.7 1.0 copy-start.3
  100.8 1.0 copy-start
  101.8 0.7 copy-start.4
  102.5 21.6 %collective-permute-start.11 = (bf16[512,512]{1,0:T(8,128)(2,1)S(1)}, bf16[512,512]{1,0:T(8,128)(2,1)S(1)}, u32[]{:S(2)}, u32[]{:S(2)}) collective-permute-start(bf16[512,512]{1,0:T(8,128)(2,1)S(1)} %get-tuple-element.48), channel_id=1, source_target_pairs={{4,0},{5,1},{6,2},{7,3},{8,4},{9,5},{10,6},{11,7},{12,8},{13,9},{1... | collective-permute-start | bytes 1572872 | tf_op jit(solution)/shard_map/ppermute | solution.py:39
  103.8 33.4 %collective-permute-start.12 = (bf16[512,512]{1,0:T(8,128)(2,1)S(1)}, bf16[512,512]{1,0:T(8,128)(2,1)S(1)}, u32[]{:S(2)}, u32[]{:S(2)}) collective-permute-start(bf16[512,512]{1,0:T(8,128)(2,1)S(1)} %get-tuple-element.49), channel_id=1, source_target_pairs={{8,0},{9,1},{10,2},{11,3},{12,4},{13,5},{14,6},{15,7},{16,8},{17,9... | collective-permute-start | bytes 1572872 | tf_op jit(solution)/shard_map/ppermute | solution.py:39
  105.1 36.9 %collective-permute-start.8 = (bf16[128,1024]{1,0:T(8,128)(2,1)S(1)}, bf16[128,1024]{1,0:T(8,128)(2,1)S(1)}, u32[]{:S(2)}, u32[]{:S(2)}) collective-permute-start(bf16[128,1024]{1,0:T(8,128)(2,1)S(1)} %get-tuple-element.42), channel_id=1, source_target_pairs={{0,1},{1,0},{2,3},{3,2},{4,5},{5,4},{6,7},{7,6},{8,9},{9,8},{10,11... | collective-permute-start | bytes 786440 | tf_op jit(solution)/shard_map/ppermute | solution.py:32
  106.1 36.6 %collective-permute-start.9 = (bf16[128,1024]{1,0:T(8,128)(2,1)S(1)}, bf16[128,1024]{1,0:T(8,128)(2,1)S(1)}, u32[]{:S(2)}, u32[]{:S(2)}) collective-permute-start(bf16[128,1024]{1,0:T(8,128)(2,1)S(1)} %get-tuple-element.43), channel_id=1, source_target_pairs={{0,2},{1,3},{2,0},{3,1},{4,6},{5,7},{6,4},{7,5},{8,10},{9,11},{10,... | collective-permute-start | bytes 786440 | tf_op jit(solution)/shard_map/ppermute | solution.py:32
  107.2 35.5 %collective-permute-start.10 = (bf16[128,1024]{1,0:T(8,128)(2,1)S(1)}, bf16[128,1024]{1,0:T(8,128)(2,1)S(1)}, u32[]{:S(2)}, u32[]{:S(2)}) collective-permute-start(bf16[128,1024]{1,0:T(8,128)(2,1)S(1)} %get-tuple-element.44), channel_id=1, source_target_pairs={{0,3},{1,2},{2,1},{3,0},{4,7},{5,6},{6,5},{7,4},{8,11},{9,10},{10,... | collective-permute-start | bytes 786440 | tf_op jit(solution)/shard_map/ppermute | solution.py:32
  124.1 13.1 %copy-start.5 = (bf16[512,512]{1,0:T(8,128)(2,1)}, bf16[512,512]{1,0:T(8,128)(2,1)S(1)}, u32[]{:S(2)}) copy-start(bf16[512,512]{1,0:T(8,128)(2,1)S(1)} %collective-permute-done.11.one) | copy-start | bytes 1572868
  137.2 0.8 copy-start.6
  140.5 35.9 %collective-permute-start.13 = (bf16[128,512]{1,0:T(8,128)(2,1)}, bf16[128,512]{1,0:T(8,128)(2,1)S(1)}, u32[]{:S(2)}, u32[]{:S(2)}) collective-permute-start(bf16[128,512]{1,0:T(8,128)(2,1)} %get-tuple-element.51), channel_id=1, source_target_pairs={{0,1},{1,0},{2,3},{3,2},{4,5},{5,4},{6,7},{7,6},{8,9},{9,8},{10,11... | collective-permute-start | bytes 393224 | tf_op jit(solution)/shard_map/ppermute | solution.py:32
  142.0 34.4 %collective-permute-start.14 = (bf16[128,512]{1,0:T(8,128)(2,1)}, bf16[128,512]{1,0:T(8,128)(2,1)S(1)}, u32[]{:S(2)}, u32[]{:S(2)}) collective-permute-start(bf16[128,512]{1,0:T(8,128)(2,1)} %get-tuple-element.52), channel_id=1, source_target_pairs={{0,2},{1,3},{2,0},{3,1},{4,6},{5,7},{6,4},{7,5},{8,10},{9,11},{10,... | collective-permute-start | bytes 393224 | tf_op jit(solution)/shard_map/ppermute | solution.py:32
  142.1 0.7 copy-start.7
  142.1 34.4 %collective-permute-start.15 = (bf16[128,512]{1,0:T(8,128)(2,1)}, bf16[128,512]{1,0:T(8,128)(2,1)S(1)}, u32[]{:S(2)}, u32[]{:S(2)}) collective-permute-start(bf16[128,512]{1,0:T(8,128)(2,1)} %get-tuple-element.53), channel_id=1, source_target_pairs={{0,3},{1,2},{2,1},{3,0},{4,7},{5,6},{6,5},{7,4},{8,11},{9,10},{10,... | collective-permute-start | bytes 393224 | tf_op jit(solution)/shard_map/ppermute | solution.py:32
  142.7 0.7 copy-start.8
  142.7 0.8 copy-start.9
  176.5 0.7 copy-start.12
  (4 other events, 2.7 us)

commit v2 on v1

--- a/solution.py
+++ b/solution.py
@@ -15,6 +15,7 @@
 logit_scale = 168.0 ** (-0.5)
 exp2_scale = logit_scale * 1.4426950408889634
 
+SMALL = pltpu.CompilerParams(vmem_limit_bytes=4 * 1024 * 1024)
 ANY = pl.BlockSpec(memory_space=pl.ANY)
 VMEM = pl.BlockSpec(memory_space=pltpu.VMEM)
 F32 = jnp.float32
@@ -76,6 +77,7 @@
         in_specs=[ANY] * len(arrays),
         out_specs=[ANY] * count,
         scratch_shapes=[pltpu.SemaphoreType.DMA((count * len(arrays),))],
+        compiler_params=SMALL,
         name="pack",
     )(*arrays)
 
@@ -96,6 +98,7 @@
         in_specs=[ANY] * size,
         out_specs=ANY,
         scratch_shapes=[pltpu.SemaphoreType.DMA((size,))],
+        compiler_params=SMALL,
         name="join",
     )(*pieces)
 
@@ -118,6 +121,7 @@
         in_specs=[VMEM] * 3,
         out_specs=[ANY] * size,
         scratch_shapes=[pltpu.VMEM((tok, cols), BF16), pltpu.SemaphoreType.DMA((size,))],
+        compiler_params=SMALL,
         name="combine",
     )(own, one, two)
 
@@ -143,6 +147,7 @@
         in_specs=[ANY] * size,
         out_specs=[ANY] * len(widths),
         scratch_shapes=[pltpu.SemaphoreType.DMA((size * len(widths),))],
+        compiler_params=SMALL,
         name="spread",
     )(*pieces)
 

time: 195 us -> 93.1 us (0.48)
  Pallas kernels: 128 us -> 19.9 us
  waiting for transfers between devices: 39.7 us -> 48.3 us
    pallas_call x2, Pallas kernels: 50 us -> 1.87 us  [spread(): pl.pallas_call(functools.partial(spread_body, size, widths), out_shape=[j...]
    pallas_call x2, Pallas kernels: 42 us -> 0.35 us  [pack(): pl.pallas_call(functools.partial(pack_body, size, first, widths), out_sha...]
    pallas_call x1, Pallas kernels: 17 us -> 0.69 us  [join(): pl.pallas_call(functools.partial(join_body, size, rows), out_shape=jax.Sh...]
    ppermute x12, waiting for transfers between devices: 9.83 us -> 18.1 us  [swap(): lax.ppermute(value, ('pipe', 'tensor'), [(i, i ^ mask) for i in range(cou...]
    unnamed x40 -> x14, local copies, waits for them, and re-layouts: 5.71 us -> 3.99 us
  transfers between devices with their start and end apart: 16 -> 16, of which waited for: 4 -> 8; matrix products, arithmetic and copies ran while one was open for 0% -> 1% of each run, Pallas kernels for 31% -> 2%
where the time goes in v2:
time: 93.1 us; the launch traced here: 92.7 us
  waiting for transfers between devices  48.3 us (52%)
  Pallas kernels  19.9 us (21%)
  starting transfers between devices  19.3 us (21%)
  local copies, waits for them, and re-layouts  4.14 us (4%)
    ppermute x4, waiting for transfers between devices, shifted(): return lax.ppermute(value, ('pipe', 'tensor'), pairs)  30.2 us
    ppermute x12, waiting for transfers between devices, swap(): lax.ppermute(value, ('pipe', 'tensor'), [(i, i ^ mask) for i in range(cou...  18.1 us
    pallas_call x1, Pallas kernels, attend(): pl.pallas_call(functools.partial(attend_body, size, kv_heads, group, rows...  16.1 us
    ppermute x12, starting transfers between devices, swap(): lax.ppermute(value, ('pipe', 'tensor'), [(i, i ^ mask) for i in range(cou...  9.78 us
    ppermute x4, starting transfers between devices, shifted(): return lax.ppermute(value, ('pipe', 'tensor'), pairs)  9.48 us
    unnamed x14, local copies, waits for them, and re-layouts  3.99 us
    pallas_call x2, Pallas kernels, spread(): pl.pallas_call(functools.partial(spread_body, size, widths), out_shape=[j...  1.87 us
  transfers between devices with their start and end apart: 16, of which 8 were waited for; matrix products, arithmetic and copies ran while one was open for 1% of the time, Pallas kernels for 2%

profile of v2, /device:TPU:0, one launch (start us, length us, event | category | flops | bytes accessed | tf_op | source)
XLA Modules:
  0.0 92.7 jit_solution(15243490687463806390)
XLA Ops:
  0.6 0.9 %copy-done.4 = bf16[128,1024]{1,0:T(8,128)(2,1)S(1)} copy-done((bf16[128,1024]{1,0:T(8,128)(2,1)S(1)}, bf16[128,1024]{1,0:T(8,128)(2,1)}, u32[]{:S(2)}) %copy-start.4) | copy-done | bytes 262168
  1.6 0.9 %copy-done.5 = bf16[128,1024]{1,0:T(8,128)(2,1)S(1)} copy-done((bf16[128,1024]{1,0:T(8,128)(2,1)S(1)}, bf16[128,1024]{1,0:T(8,128)(2,1)}, u32[]{:S(2)}) %copy-start.5) | copy-done | bytes 262168
  2.5 0.2 pack.2
  2.7 3.0 %collective-permute-start = (bf16[128,512]{1,0:T(8,128)(2,1)S(1)}, bf16[128,512]{1,0:T(8,128)(2,1)S(1)}, u32[]{:S(2)}, u32[]{:S(2)}) collective-permute-start(bf16[128,512]{1,0:T(8,128)(2,1)S(1)} %get-tuple-element.31), channel_id=1, source_target_pairs={{0,1},{1,0},{2,3},{3,2},{4,5},{5,4},{6,7},{7,6},{8,9},{9,8},{10,11... | collective-permute-start | bytes 393224 | tf_op jit(solution)/shard_map/ppermute | solution.py:33
  5.7 0.2 collective-permute-start.2
  5.9 1.0 %copy-done = bf16[128,2048]{1,0:T(8,128)(2,1)S(1)} copy-done((bf16[128,2048]{1,0:T(8,128)(2,1)S(1)}, bf16[128,2048]{1,0:T(8,128)(2,1)}, u32[]{:S(2)}) %copy-start) | copy-done | bytes 524312
  7.0 1.0 %copy-done.2 = bf16[128,2048]{1,0:T(8,128)(2,1)S(1)} copy-done((bf16[128,2048]{1,0:T(8,128)(2,1)S(1)}, bf16[128,2048]{1,0:T(8,128)(2,1)}, u32[]{:S(2)}) %copy-start.2) | copy-done | bytes 524312
  8.0 0.2 pack.3
  8.2 1.4 %collective-permute-done.refs_1_ = bf16[128,512]{1,0:T(8,128)(2,1)S(1)} collective-permute-done((bf16[128,512]{1,0:T(8,128)(2,1)S(1)}, bf16[128,512]{1,0:T(8,128)(2,1)S(1)}, u32[]{:S(2)}, u32[]{:S(2)}) %collective-permute-start) | collective-permute-done | bytes 131104 | tf_op jit(solution)/shard_map/ppermute | solution.py:33
  9.6 1.9 %collective-permute-done.2.refs_3_ = bf16[128,512]{1,0:T(8,128)(2,1)S(1)} collective-permute-done((bf16[128,512]{1,0:T(8,128)(2,1)S(1)}, bf16[128,512]{1,0:T(8,128)(2,1)S(1)}, u32[]{:S(2)}, u32[]{:S(2)}) %collective-permute-start.2) | collective-permute-done | bytes 131104 | tf_op jit(solution)/shard_map/ppermute | solution.py:33
  11.6 0.7 join.1.refs_6_
  12.3 3.4 %collective-permute-start.7 = (bf16[512,512]{1,0:T(8,128)(2,1)S(1)}, bf16[512,512]{1,0:T(8,128)(2,1)S(1)}, u32[]{:S(2)}, u32[]{:S(2)}) collective-permute-start(bf16[512,512]{1,0:T(8,128)(2,1)S(1)} %join.1.refs_6_), channel_id=1, source_target_pairs={{0,8},{1,9},{2,10},{3,11},{4,12},{5,13},{6,14},{7,15},{8,16},{9,17... | collective-permute-start | bytes 1572872 | tf_op jit(solution)/shard_map/ppermute | solution.py:40
  15.7 3.5 %collective-permute-start.6 = (bf16[512,512]{1,0:T(8,128)(2,1)S(1)}, bf16[512,512]{1,0:T(8,128)(2,1)S(1)}, u32[]{:S(2)}, u32[]{:S(2)}) collective-permute-start(bf16[512,512]{1,0:T(8,128)(2,1)S(1)} %join.1.refs_6_), channel_id=1, source_target_pairs={{0,4},{1,5},{2,6},{3,7},{4,8},{5,9},{6,10},{7,11},{8,12},{9,13},{1... | collective-permute-start | bytes 1572872 | tf_op jit(solution)/shard_map/ppermute | solution.py:40
  19.4 1.1 %collective-permute-start.3 = (bf16[128,1024]{1,0:T(8,128)(2,1)S(1)}, bf16[128,1024]{1,0:T(8,128)(2,1)S(1)}, u32[]{:S(2)}, u32[]{:S(2)}) collective-permute-start(bf16[128,1024]{1,0:T(8,128)(2,1)S(1)} %get-tuple-element.37), channel_id=1, source_target_pairs={{0,1},{1,0},{2,3},{3,2},{4,5},{5,4},{6,7},{7,6},{8,9},{9,8},{10,11... | collective-permute-start | bytes 786440 | tf_op jit(solution)/shard_map/ppermute | solution.py:33
  20.6 0.9 collective-permute-start.5
  21.5 0.4 convert_reduce_fusion
  21.9 6.6 %collective-permute-done.3.refs_3_ = bf16[128,1024]{1,0:T(8,128)(2,1)S(1)} collective-permute-done((bf16[128,1024]{1,0:T(8,128)(2,1)S(1)}, bf16[128,1024]{1,0:T(8,128)(2,1)S(1)}, u32[]{:S(2)}, u32[]{:S(2)}) %collective-permute-start.3) | collective-permute-done | bytes 262176 | tf_op jit(solution)/shard_map/ppermute | solution.py:33
  28.5 3.8 %collective-permute-done.5.refs_5_ = bf16[128,1024]{1,0:T(8,128)(2,1)S(1)} collective-permute-done((bf16[128,1024]{1,0:T(8,128)(2,1)S(1)}, bf16[128,1024]{1,0:T(8,128)(2,1)S(1)}, u32[]{:S(2)}, u32[]{:S(2)}) %collective-permute-start.5) | collective-permute-done | bytes 262176 | tf_op jit(solution)/shard_map/ppermute | solution.py:33
  32.3 16.1 %attend.1 = (bf16[128,1024]{1,0:T(8,128)(2,1)S(1)}, bf16[128,1024]{1,0:T(8,128)(2,1)S(1)}, bf16[128,1024]{1,0:T(8,128)(2,1)S(1)}, bf16[128,1024]{1,0:T(8,128)(2,...) custom-call(s32[1,512]{1,0:T(1,128)S(1)} %add_maximum_fusion.refs_0_, ...), custom_call_target="tpu_custom_call" | custom-call | flops 3623878656 | bytes 8388608 | tf_op jit(solution)/shard_map/attend/pallas_call | solution.py:285
  48.4 1.3 %collective-permute-start.11 = (bf16[512,512]{1,0:T(8,128)(2,1)S(1)}, bf16[512,512]{1,0:T(8,128)(2,1)S(1)}, u32[]{:S(2)}, u32[]{:S(2)}) collective-permute-start(bf16[512,512]{1,0:T(8,128)(2,1)S(1)} %get-tuple-element.48), channel_id=1, source_target_pairs={{4,0},{5,1},{6,2},{7,3},{8,4},{9,5},{10,6},{11,7},{12,8},{13,9},{1... | collective-permute-start | bytes 1572872 | tf_op jit(solution)/shard_map/ppermute | solution.py:40
  49.7 1.3 %collective-permute-start.12 = (bf16[512,512]{1,0:T(8,128)(2,1)S(1)}, bf16[512,512]{1,0:T(8,128)(2,1)S(1)}, u32[]{:S(2)}, u32[]{:S(2)}) collective-permute-start(bf16[512,512]{1,0:T(8,128)(2,1)S(1)} %get-tuple-element.49), channel_id=1, source_target_pairs={{8,0},{9,1},{10,2},{11,3},{12,4},{13,5},{14,6},{15,7},{16,8},{17,9... | collective-permute-start | bytes 1572872 | tf_op jit(solution)/shard_map/ppermute | solution.py:40
  51.0 2.0 %collective-permute-start.8 = (bf16[128,1024]{1,0:T(8,128)(2,1)S(1)}, bf16[128,1024]{1,0:T(8,128)(2,1)S(1)}, u32[]{:S(2)}, u32[]{:S(2)}) collective-permute-start(bf16[128,1024]{1,0:T(8,128)(2,1)S(1)} %get-tuple-element.42), channel_id=1, source_target_pairs={{0,1},{1,0},{2,3},{3,2},{4,5},{5,4},{6,7},{7,6},{8,9},{9,8},{10,11... | collective-permute-start | bytes 786440 | tf_op jit(solution)/shard_map/ppermute | solution.py:33
  53.1 0.2 collective-permute-start.10
  53.2 17.0 %collective-permute-done.11.one = bf16[512,512]{1,0:T(8,128)(2,1)S(1)} collective-permute-done((bf16[512,512]{1,0:T(8,128)(2,1)S(1)}, bf16[512,512]{1,0:T(8,128)(2,1)S(1)}, u32[]{:S(2)}, u32[]{:S(2)}) %collective-permute-start.11) | collective-permute-done | bytes 524320 | tf_op jit(solution)/shard_map/ppermute | solution.py:40
  70.2 13.2 %collective-permute-done.12.two = bf16[512,512]{1,0:T(8,128)(2,1)S(1)} collective-permute-done((bf16[512,512]{1,0:T(8,128)(2,1)S(1)}, bf16[512,512]{1,0:T(8,128)(2,1)S(1)}, u32[]{:S(2)}, u32[]{:S(2)}) %collective-permute-start.12) | collective-permute-done | bytes 524320 | tf_op jit(solution)/shard_map/ppermute | solution.py:40
  83.4 0.9 combine.1
  84.3 1.9 %collective-permute-start.13 = (bf16[128,512]{1,0:T(8,128)(2,1)S(1)}, bf16[128,512]{1,0:T(8,128)(2,1)S(1)}, u32[]{:S(2)}, u32[]{:S(2)}) collective-permute-start(bf16[128,512]{1,0:T(8,128)(2,1)S(1)} %get-tuple-element.51), channel_id=1, source_target_pairs={{0,1},{1,0},{2,3},{3,2},{4,5},{5,4},{6,7},{7,6},{8,9},{9,8},{10,11... | collective-permute-start | bytes 393224 | tf_op jit(solution)/shard_map/ppermute | solution.py:33
  86.1 0.3 collective-permute-start.15
  86.5 1.0 %spread.2 = (bf16[128,2048]{1,0:T(8,128)(2,1)}, bf16[128,2048]{1,0:T(8,128)(2,1)}) custom-call(bf16[128,1024]{1,0:T(8,128)(2,1)S(1)} %get-tuple-element.41.refs_0_, bf16[128,1024]{1,0:T(8,128)(2,1)S(1)} %collective-permute-done.8.refs_1_, bf16[128,1024]{1,0:T(8,128)(2,1)S(1)} %collective-permute-done.9.refs_2_, ...), custom_call_target="tpu_custom_call" | custom-call | tf_op jit(solution)/shard_map/spread/pallas_call | solution.py:144
  87.5 2.5 %collective-permute-done.13.refs_1_ = bf16[128,512]{1,0:T(8,128)(2,1)S(1)} collective-permute-done((bf16[128,512]{1,0:T(8,128)(2,1)S(1)}, bf16[128,512]{1,0:T(8,128)(2,1)S(1)}, u32[]{:S(2)}, u32[]{:S(2)}) %collective-permute-start.13) | collective-permute-done | bytes 131104 | tf_op jit(solution)/shard_map/ppermute | solution.py:33
  90.1 1.8 %collective-permute-done.15.refs_3_ = bf16[128,512]{1,0:T(8,128)(2,1)S(1)} collective-permute-done((bf16[128,512]{1,0:T(8,128)(2,1)S(1)}, bf16[128,512]{1,0:T(8,128)(2,1)S(1)}, u32[]{:S(2)}, u32[]{:S(2)}) %collective-permute-start.15) | collective-permute-done | bytes 131104 | tf_op jit(solution)/shard_map/ppermute | solution.py:33
  91.9 0.8 spread.3
  (25 shorter events, 0.4 us)
Async XLA Ops:
  0.6 1.0 %copy-start.4 = (bf16[128,1024]{1,0:T(8,128)(2,1)S(1)}, bf16[128,1024]{1,0:T(8,128)(2,1)}, u32[]{:S(2)}) copy-start(bf16[128,1024]{1,0:T(8,128)(2,1)} %refs_0_.2) | copy-start | bytes 786436
  1.6 0.9 %copy-start.5 = (bf16[128,1024]{1,0:T(8,128)(2,1)S(1)}, bf16[128,1024]{1,0:T(8,128)(2,1)}, u32[]{:S(2)}) copy-start(bf16[128,1024]{1,0:T(8,128)(2,1)} %refs_1_.3) | copy-start | bytes 786436
  2.7 6.9 %collective-permute-start = (bf16[128,512]{1,0:T(8,128)(2,1)S(1)}, bf16[128,512]{1,0:T(8,128)(2,1)S(1)}, u32[]{:S(2)}, u32[]{:S(2)}) collective-permute-start(bf16[128,512]{1,0:T(8,128)(2,1)S(1)} %get-tuple-element.31), channel_id=1, source_target_pairs={{0,1},{1,0},{2,3},{3,2},{4,5},{5,4},{6,7},{7,6},{8,9},{9,8},{10,11... | collective-permute-start | bytes 393224 | tf_op jit(solution)/shard_map/ppermute | solution.py:33
  5.7 3.9 %collective-permute-start.1 = (bf16[128,512]{1,0:T(8,128)(2,1)S(1)}, bf16[128,512]{1,0:T(8,128)(2,1)S(1)}, u32[]{:S(2)}, u32[]{:S(2)}) collective-permute-start(bf16[128,512]{1,0:T(8,128)(2,1)S(1)} %get-tuple-element.32), channel_id=1, source_target_pairs={{0,2},{1,3},{2,0},{3,1},{4,6},{5,7},{6,4},{7,5},{8,10},{9,11},{10,... | collective-permute-start | bytes 393224 | tf_op jit(solution)/shard_map/ppermute | solution.py:33
  5.7 5.9 %collective-permute-start.2 = (bf16[128,512]{1,0:T(8,128)(2,1)S(1)}, bf16[128,512]{1,0:T(8,128)(2,1)S(1)}, u32[]{:S(2)}, u32[]{:S(2)}) collective-permute-start(bf16[128,512]{1,0:T(8,128)(2,1)S(1)} %get-tuple-element.33), channel_id=1, source_target_pairs={{0,3},{1,2},{2,1},{3,0},{4,7},{5,6},{6,5},{7,4},{8,11},{9,10},{10,... | collective-permute-start | bytes 393224 | tf_op jit(solution)/shard_map/ppermute | solution.py:33
  5.9 1.0 %copy-start = (bf16[128,2048]{1,0:T(8,128)(2,1)S(1)}, bf16[128,2048]{1,0:T(8,128)(2,1)}, u32[]{:S(2)}) copy-start(bf16[128,2048]{1,0:T(8,128)(2,1)} %refs_1_.5) | copy-start | bytes 1572868
  7.0 1.0 %copy-start.2 = (bf16[128,2048]{1,0:T(8,128)(2,1)S(1)}, bf16[128,2048]{1,0:T(8,128)(2,1)}, u32[]{:S(2)}) copy-start(bf16[128,2048]{1,0:T(8,128)(2,1)} %refs_2_.1) | copy-start | bytes 1572868
  8.0 11.2 %copy-start.6 = (s32[4096]{0:T(1024)S(1)}, s32[4096]{0:T(1024)}, u32[]{:S(2)}) copy-start(s32[4096]{0:T(1024)} %param.9) | copy-start | bytes 49156
  8.0 24.3 %copy-start.1 = (bf16[128,2048]{1,0:T(8,128)(2,1)S(1)}, bf16[128,2048]{1,0:T(8,128)(2,1)}, u32[]{:S(2)}) copy-start(bf16[128,2048]{1,0:T(8,128)(2,1)} %refs_1_.5) | copy-start | bytes 1572868
  8.0 24.3 %copy-start.3 = (bf16[128,2048]{1,0:T(8,128)(2,1)S(1)}, bf16[128,2048]{1,0:T(8,128)(2,1)}, u32[]{:S(2)}) copy-start(bf16[128,2048]{1,0:T(8,128)(2,1)} %refs_2_.1) | copy-start | bytes 1572868
  12.3 20.0 %collective-permute-start.7 = (bf16[512,512]{1,0:T(8,128)(2,1)S(1)}, bf16[512,512]{1,0:T(8,128)(2,1)S(1)}, u32[]{:S(2)}, u32[]{:S(2)}) collective-permute-start(bf16[512,512]{1,0:T(8,128)(2,1)S(1)} %join.1.refs_6_), channel_id=1, source_target_pairs={{0,8},{1,9},{2,10},{3,11},{4,12},{5,13},{6,14},{7,15},{8,16},{9,17... | collective-permute-start | bytes 1572872 | tf_op jit(solution)/shard_map/ppermute | solution.py:40
  15.7 16.6 %collective-permute-start.6 = (bf16[512,512]{1,0:T(8,128)(2,1)S(1)}, bf16[512,512]{1,0:T(8,128)(2,1)S(1)}, u32[]{:S(2)}, u32[]{:S(2)}) collective-permute-start(bf16[512,512]{1,0:T(8,128)(2,1)S(1)} %join.1.refs_6_), channel_id=1, source_target_pairs={{0,4},{1,5},{2,6},{3,7},{4,8},{5,9},{6,10},{7,11},{8,12},{9,13},{1... | collective-permute-start | bytes 1572872 | tf_op jit(solution)/shard_map/ppermute | solution.py:40
  19.4 9.2 %collective-permute-start.3 = (bf16[128,1024]{1,0:T(8,128)(2,1)S(1)}, bf16[128,1024]{1,0:T(8,128)(2,1)S(1)}, u32[]{:S(2)}, u32[]{:S(2)}) collective-permute-start(bf16[128,1024]{1,0:T(8,128)(2,1)S(1)} %get-tuple-element.37), channel_id=1, source_target_pairs={{0,1},{1,0},{2,3},{3,2},{4,5},{5,4},{6,7},{7,6},{8,9},{9,8},{10,11... | collective-permute-start | bytes 786440 | tf_op jit(solution)/shard_map/ppermute | solution.py:33
  20.5 8.1 %collective-permute-start.4 = (bf16[128,1024]{1,0:T(8,128)(2,1)S(1)}, bf16[128,1024]{1,0:T(8,128)(2,1)S(1)}, u32[]{:S(2)}, u32[]{:S(2)}) collective-permute-start(bf16[128,1024]{1,0:T(8,128)(2,1)S(1)} %get-tuple-element.38), channel_id=1, source_target_pairs={{0,2},{1,3},{2,0},{3,1},{4,6},{5,7},{6,4},{7,5},{8,10},{9,11},{10,... | collective-permute-start | bytes 786440 | tf_op jit(solution)/shard_map/ppermute | solution.py:33
  20.6 11.7 %collective-permute-start.5 = (bf16[128,1024]{1,0:T(8,128)(2,1)S(1)}, bf16[128,1024]{1,0:T(8,128)(2,1)S(1)}, u32[]{:S(2)}, u32[]{:S(2)}) collective-permute-start(bf16[128,1024]{1,0:T(8,128)(2,1)S(1)} %get-tuple-element.39), channel_id=1, source_target_pairs={{0,3},{1,2},{2,1},{3,0},{4,7},{5,6},{6,5},{7,4},{8,11},{9,10},{10,... | collective-permute-start | bytes 786440 | tf_op jit(solution)/shard_map/ppermute | solution.py:33
  48.4 21.8 %collective-permute-start.11 = (bf16[512,512]{1,0:T(8,128)(2,1)S(1)}, bf16[512,512]{1,0:T(8,128)(2,1)S(1)}, u32[]{:S(2)}, u32[]{:S(2)}) collective-permute-start(bf16[512,512]{1,0:T(8,128)(2,1)S(1)} %get-tuple-element.48), channel_id=1, source_target_pairs={{4,0},{5,1},{6,2},{7,3},{8,4},{9,5},{10,6},{11,7},{12,8},{13,9},{1... | collective-permute-start | bytes 1572872 | tf_op jit(solution)/shard_map/ppermute | solution.py:40
  49.7 33.7 %collective-permute-start.12 = (bf16[512,512]{1,0:T(8,128)(2,1)S(1)}, bf16[512,512]{1,0:T(8,128)(2,1)S(1)}, u32[]{:S(2)}, u32[]{:S(2)}) collective-permute-start(bf16[512,512]{1,0:T(8,128)(2,1)S(1)} %get-tuple-element.49), channel_id=1, source_target_pairs={{8,0},{9,1},{10,2},{11,3},{12,4},{13,5},{14,6},{15,7},{16,8},{17,9... | collective-permute-start | bytes 1572872 | tf_op jit(solution)/shard_map/ppermute | solution.py:40
  51.0 35.1 %collective-permute-start.8 = (bf16[128,1024]{1,0:T(8,128)(2,1)S(1)}, bf16[128,1024]{1,0:T(8,128)(2,1)S(1)}, u32[]{:S(2)}, u32[]{:S(2)}) collective-permute-start(bf16[128,1024]{1,0:T(8,128)(2,1)S(1)} %get-tuple-element.42), channel_id=1, source_target_pairs={{0,1},{1,0},{2,3},{3,2},{4,5},{5,4},{6,7},{7,6},{8,9},{9,8},{10,11... | collective-permute-start | bytes 786440 | tf_op jit(solution)/shard_map/ppermute | solution.py:33
  53.0 33.5 %collective-permute-start.9 = (bf16[128,1024]{1,0:T(8,128)(2,1)S(1)}, bf16[128,1024]{1,0:T(8,128)(2,1)S(1)}, u32[]{:S(2)}, u32[]{:S(2)}) collective-permute-start(bf16[128,1024]{1,0:T(8,128)(2,1)S(1)} %get-tuple-element.43), channel_id=1, source_target_pairs={{0,2},{1,3},{2,0},{3,1},{4,6},{5,7},{6,4},{7,5},{8,10},{9,11},{10,... | collective-permute-start | bytes 786440 | tf_op jit(solution)/shard_map/ppermute | solution.py:33
  53.1 33.4 %collective-permute-start.10 = (bf16[128,1024]{1,0:T(8,128)(2,1)S(1)}, bf16[128,1024]{1,0:T(8,128)(2,1)S(1)}, u32[]{:S(2)}, u32[]{:S(2)}) collective-permute-start(bf16[128,1024]{1,0:T(8,128)(2,1)S(1)} %get-tuple-element.44), channel_id=1, source_target_pairs={{0,3},{1,2},{2,1},{3,0},{4,7},{5,6},{6,5},{7,4},{8,11},{9,10},{10,... | collective-permute-start | bytes 786440 | tf_op jit(solution)/shard_map/ppermute | solution.py:33
  84.3 5.8 %collective-permute-start.13 = (bf16[128,512]{1,0:T(8,128)(2,1)S(1)}, bf16[128,512]{1,0:T(8,128)(2,1)S(1)}, u32[]{:S(2)}, u32[]{:S(2)}) collective-permute-start(bf16[128,512]{1,0:T(8,128)(2,1)S(1)} %get-tuple-element.51), channel_id=1, source_target_pairs={{0,1},{1,0},{2,3},{3,2},{4,5},{5,4},{6,7},{7,6},{8,9},{9,8},{10,11... | collective-permute-start | bytes 393224 | tf_op jit(solution)/shard_map/ppermute | solution.py:33
  86.1 3.9 %collective-permute-start.14 = (bf16[128,512]{1,0:T(8,128)(2,1)S(1)}, bf16[128,512]{1,0:T(8,128)(2,1)S(1)}, u32[]{:S(2)}, u32[]{:S(2)}) collective-permute-start(bf16[128,512]{1,0:T(8,128)(2,1)S(1)} %get-tuple-element.52), channel_id=1, source_target_pairs={{0,2},{1,3},{2,0},{3,1},{4,6},{5,7},{6,4},{7,5},{8,10},{9,11},{10,... | collective-permute-start | bytes 393224 | tf_op jit(solution)/shard_map/ppermute | solution.py:33
  86.1 5.7 %collective-permute-start.15 = (bf16[128,512]{1,0:T(8,128)(2,1)S(1)}, bf16[128,512]{1,0:T(8,128)(2,1)S(1)}, u32[]{:S(2)}, u32[]{:S(2)}) collective-permute-start(bf16[128,512]{1,0:T(8,128)(2,1)S(1)} %get-tuple-element.53), channel_id=1, source_target_pairs={{0,3},{1,2},{2,1},{3,0},{4,7},{5,6},{6,5},{7,4},{8,11},{9,10},{10,... | collective-permute-start | bytes 393224 | tf_op jit(solution)/shard_map/ppermute | solution.py:33

commit v3 on v2

v3 whole, which is shorter than its diff:
```python
import functools

import jax
import jax.numpy as jnp
from jax import lax
from jax.experimental import pallas as pl
from jax.experimental.pallas import tpu as pltpu
from jax.sharding import PartitionSpec as P

HEAD_DIM = 128
WINDOW = 1024
CORES = 2
TILE = 128

logit_scale = 168.0 ** (-0.5)
exp2_scale = logit_scale * 1.4426950408889634

SMALL = pltpu.CompilerParams(vmem_limit_bytes=4 * 1024 * 1024)
ANY = pl.BlockSpec(memory_space=pl.ANY)
VMEM = pl.BlockSpec(memory_space=pltpu.VMEM)
F32 = jnp.float32
BF16 = jnp.bfloat16


def member():
    return lax.rem(lax.axis_index("pipe"), CORES) * lax.axis_size("tensor") + lax.axis_index(
        "tensor"
    )


def swap(value, mask):
    count = lax.axis_size("pipe") * lax.axis_size("tensor")
    return lax.ppermute(value, ("pipe", "tensor"), [(i, i ^ mask) for i in range(count)])


def hop(value, size, back):
    count = lax.axis_size("pipe") * lax.axis_size("tensor")
    step = 2 * size
    results = []
    for odd in (0, 1):
        low = [i for i in range(count - step) if (i // step) % 2 == odd]
        pairs = [(i + step, i) if back else (i, i + step) for i in low]
        results.append(lax.ppermute(value, ("pipe", "tensor"), pairs))
    return results


def after(value, *others):
    return lax.optimization_barrier((value, *others))


def place(index, width):
    return pl.ds(pl.multiple_of(index * width, width), width)


def run_copies(copies, sems):
    started = []
    for at, (source, target) in enumerate(copies):
        copy = pltpu.make_async_copy(source, target, sems.at[at])
        copy.start()
        started.append(copy)
    for copy in started:
        copy.wait()


def pack_body(widths, *refs):
    arrays, pieces, sems = refs[: len(widths)], refs[len(widths) : -1], refs[-1]
    me = member()
    copies = []
    for at, piece in enumerate(pieces):
        other = lax.bitwise_xor(me, at)
        start = 0
        for array, width in zip(arrays, widths):
            copies.append((array.at[:, place(other, width)], piece.at[:, start : start + width]))
            start += width
    run_copies(copies, sems)


def pack(arrays, size):
    rows = arrays[0].shape[0]
    widths = [array.shape[1] // size for array in arrays]
    return pl.pallas_call(
        functools.partial(pack_body, widths),
        out_shape=[jax.ShapeDtypeStruct((rows, sum(widths)), BF16)] * size,
        in_specs=[pl.BlockSpec(memory_space=pltpu.HBM)] * len(arrays),
        out_specs=[ANY] * size,
        scratch_shapes=[pltpu.SemaphoreType.DMA((size * len(arrays),))],
        compiler_params=SMALL,
        name="pack",
    )(*arrays)


def join_body(size, rows, heads, *refs):
    pieces, outs, sems = refs[:size], refs[size:-1], refs[-1]
    me = member()
    copies = []
    for head, out in enumerate(outs):
        for j in range(size):
            to = place(lax.bitwise_xor(me, j), rows)
            for at in range(2):
                start = (at * heads + head) * HEAD_DIM
                copies.append(
                    (
                        pieces[j].at[:, start : start + HEAD_DIM],
                        out.at[to, at * HEAD_DIM : (at + 1) * HEAD_DIM],
                    )
                )
    run_copies(copies, sems)


def join(pieces):
    size, (rows, cols) = len(pieces), pieces[0].shape
    heads = cols // (2 * HEAD_DIM)
    return pl.pallas_call(
        functools.partial(join_body, size, rows, heads),
        out_shape=[jax.ShapeDtypeStruct((size * rows, 2 * HEAD_DIM), BF16)] * heads,
        in_specs=[ANY] * size,
        out_specs=[ANY] * heads,
        scratch_shapes=[pltpu.SemaphoreType.DMA((2 * heads * size,))],
        compiler_params=SMALL,
        name="join",
    )(*pieces)


def combine_body(size, rows, heads, *refs):
    terms, pieces, total, sems = refs[: 3 * heads], refs[3 * heads : -2], refs[-2], refs[-1]
    for head in range(heads):
        own, one, two = terms[3 * head : 3 * head + 3]
        added = (own[...] + one[...].astype(F32) + two[...].astype(F32)).astype(BF16)
        for at in range(2):
            start = (at * heads + head) * HEAD_DIM
            total[:, start : start + HEAD_DIM] = added[:, at * HEAD_DIM : (at + 1) * HEAD_DIM]
    me = member()
    run_copies(
        [(total.at[place(lax.bitwise_xor(me, j), rows), :], pieces[j]) for j in range(size)], sems
    )


def combine(terms, size):
    heads = len(terms) // 3
    tok = terms[0].shape[0]
    rows, cols = tok // size, 2 * heads * HEAD_DIM
    return pl.pallas_call(
        functools.partial(combine_body, size, rows, heads),
        out_shape=[jax.ShapeDtypeStruct((rows, cols), BF16)] * size,
        in_specs=[VMEM] * len(terms),
        out_specs=[ANY] * size,
        scratch_shapes=[pltpu.VMEM((tok, cols), BF16), pltpu.SemaphoreType.DMA((size,))],
        compiler_params=SMALL,
        name="combine",
    )(*terms)


def spread_body(size, chunks, count, *refs):
    pieces, outs, sems = refs[: size * chunks], refs[size * chunks : -1], refs[-1]
    me = member()
    copies = []
    for j in range(size):
        other = lax.bitwise_xor(me, j)
        for chunk in range(chunks):
            piece = pieces[chunk * size + j]
            width = piece.shape[1] // count
            for at, out in enumerate(outs):
                start = pl.multiple_of((other * chunks + chunk) * width, width)
                copies.append(
                    (piece.at[:, at * width : (at + 1) * width], out.at[:, pl.ds(start, width)])
                )
    run_copies(copies, sems)


def spread(chunks, count):
    size, (rows, cols) = len(chunks[0]), chunks[0][0].shape
    pieces = [piece for chunk in chunks for piece in chunk]
    return pl.pallas_call(
        functools.partial(spread_body, size, len(chunks), count),
        out_shape=[jax.ShapeDtypeStruct((rows, cols // count * len(pieces)), BF16)] * count,
        in_specs=[ANY] * len(pieces),
        out_specs=[ANY] * count,
        scratch_shapes=[pltpu.SemaphoreType.DMA((len(pieces) * count,))],
        compiler_params=SMALL,
        name="spread",
    )(*pieces)


def dot(a, b):
    return lax.dot_general(a, b, (((1,), (0,)), ((), ())), preferred_element_type=F32)


def dot_t(a, b):
    return lax.dot_general(a, b, (((1,), (1,)), ((), ())), preferred_element_type=F32)


def fold(x, op):
    parts = [x[at : at + 8] for at in range(0, x.shape[0], 8)]
    while len(parts) > 1:
        parts = [op(*parts[at : at + 2]) if at + 1 < len(parts) else parts[at] for at in range(0, len(parts), 2)]
    return parts[0]


def attend_body(size, head, heads, group, rows, *refs):
    low, pieces = refs[0], refs[1 : 1 + size]
    kv0, kv1, kv2 = refs[1 + size : 4 + size]
    og = refs[4 + size : 4 + 2 * size]
    dkv0, dkv1, dkv2 = refs[4 + 2 * size : 7 + 2 * size]
    qs, gs, ks, vs, kt, vt, os, dqs, dk, dv, s_scr, e_scr, ds_scr, half1, half2, sems = refs[
        7 + 2 * size :
    ]
    tok = size * rows
    width = group * HEAD_DIM
    span = WINDOW + TILE
    me = member()
    copies = []
    for j in range(size):
        to = place(lax.bitwise_xor(me, j), rows)
        for at, target in enumerate((qs, gs)):
            start = (at * heads + head) * width
            copies.append((pieces[j].at[:, start : start + width], target.at[to, :]))
    for at, kv in enumerate((kv2, kv1, kv0)):
        copies.append((kv.at[:, :HEAD_DIM], ks.at[at * tok : (at + 1) * tok, :]))
        copies.append((kv.at[:, HEAD_DIM:], vs.at[at * tok : (at + 1) * tok, :]))
    run_copies(copies, sems)

    dk[...] = jnp.zeros_like(dk)
    dv[...] = jnp.zeros_like(dv)
    lane = lax.broadcasted_iota(jnp.int32, (TILE, HEAD_DIM), 1)
    ones = jnp.where(lane < 2, 1.0, 0.0).astype(BF16)
    wide_lane = lax.broadcasted_iota(jnp.int32, (group * TILE, HEAD_DIM), 1)
    row_of = lax.broadcasted_iota(jnp.int32, (TILE, group * TILE), 0)
    col_of = lax.broadcasted_iota(jnp.int32, (TILE, TILE), 1)
    causal = lax.broadcasted_iota(jnp.int32, (TILE, TILE), 0) <= col_of
    causal = jnp.concatenate([causal] * group, axis=1)

    kt[...] = ks[...].T
    vt[...] = vs[...].T
    q_cols = [slice(at * HEAD_DIM, (at + 1) * HEAD_DIM) for at in range(group)]
    for tile in range(tok // TILE):
        base = tile * TILE
        here = slice(base, base + TILE)
        q2 = jnp.concatenate([qs[here, c] for c in q_cols], axis=0)
        g2 = jnp.concatenate([gs[here, c] for c in q_cols], axis=0)
        low_row = jnp.concatenate([low[:, here]] * group, axis=1) - base
        top = None
        for at in range(0, span, TILE):
            s = dot_t(ks[base + at : base + at + TILE, :], q2)
            keep = row_of >= low_row - at
            if at == span - TILE:
                keep = keep & causal
            s = jnp.where(keep, s, -1e30)
            s_scr[at : at + TILE, :] = s
            part = fold(s, jnp.maximum)
            top = part if top is None else jnp.maximum(top, part)
        top = jnp.max(top, axis=0, keepdims=True) * exp2_scale
        total = None
        for at in range(0, span, TILE):
            e = jnp.exp2(s_scr[at : at + TILE, :] * exp2_scale - top)
            e_scr[at : at + TILE, :] = e.astype(BF16)
            part = fold(e, jnp.add)
            total = part if total is None else total + part
        inv = 1.0 / jnp.sum(total, axis=0, keepdims=True)
        inv = jnp.broadcast_to(inv, (HEAD_DIM, group * TILE)).T
        out = dot(vt[:, base : base + span], e_scr[...]).T * inv
        out = out.astype(BF16)
        g2 = (g2.astype(F32) * inv).astype(BF16)
        delta = jnp.sum(g2.astype(F32) * out.astype(F32), axis=1, keepdims=True)
        high = delta.astype(BF16).astype(F32)
        extra = jnp.where(wide_lane == 0, -high, jnp.where(wide_lane == 1, high - delta, 0.0))
        g_wide = jnp.concatenate([g2, extra.astype(BF16)], axis=1)
        for at in range(0, span, TILE):
            there = slice(base + at, base + at + TILE)
            dp = dot_t(jnp.concatenate([vs[there, :], ones], axis=1), g_wide)
            e = e_scr[at : at + TILE, :]
            ds = (e.astype(F32) * dp).astype(BF16)
            ds_scr[at : at + TILE, :] = ds
            dv[there, :] += dot(e, g2)
            dk[there, :] += dot(ds, q2)
        dq = (dot(kt[:, base : base + span], ds_scr[...]) * logit_scale).T.astype(BF16)
        for at, c in enumerate(q_cols):
            os[here, c] = out[at * TILE : (at + 1) * TILE]
            dqs[here, c] = dq[at * TILE : (at + 1) * TILE]

    dkv0[:, :HEAD_DIM] = dk[2 * tok :, :] * logit_scale
    dkv0[:, HEAD_DIM:] = dv[2 * tok :, :]
    for half, at in ((half1, 1), (half2, 0)):
        half[:, :HEAD_DIM] = (dk[at * tok : (at + 1) * tok, :] * logit_scale).astype(BF16)
        half[:, HEAD_DIM:] = dv[at * tok : (at + 1) * tok, :].astype(BF16)
    copies = [(half1, dkv1), (half2, dkv2)]
    for j in range(size):
        of = place(lax.bitwise_xor(me, j), rows)
        copies.append((os.at[of, :], og[j].at[:, :width]))
        copies.append((dqs.at[of, :], og[j].at[:, width:]))
    run_copies(copies, sems)


def attend(low, pieces, kv0, kv1, kv2, head, heads):
    size, (rows, cols) = len(pieces), pieces[0].shape
    tok = size * rows
    width = cols // (2 * heads)
    group = width // HEAD_DIM
    span = WINDOW + TILE
    wide = group * TILE
    half = jax.ShapeDtypeStruct((tok, 2 * HEAD_DIM), BF16)
    flops = 6 * 2 * tok * group * span * HEAD_DIM
    results = pl.pallas_call(
        functools.partial(attend_body, size, head, heads, group, rows),
        out_shape=[jax.ShapeDtypeStruct((rows, 2 * width), BF16)] * size
        + [jax.ShapeDtypeStruct((tok, 2 * HEAD_DIM), F32), half, half],
        in_specs=[VMEM] + [ANY] * (size + 3),
        out_specs=[ANY] * size + [VMEM, ANY, ANY],
        scratch_shapes=[
            pltpu.VMEM((tok, width), BF16),
            pltpu.VMEM((tok, width), BF16),
            pltpu.VMEM((3 * tok, HEAD_DIM), BF16),
            pltpu.VMEM((3 * tok, HEAD_DIM), BF16),
            pltpu.VMEM((HEAD_DIM, 3 * tok), BF16),
            pltpu.VMEM((HEAD_DIM, 3 * tok), BF16),
            pltpu.VMEM((tok, width), BF16),
            pltpu.VMEM((tok, width), BF16),
            pltpu.VMEM((3 * tok, HEAD_DIM), F32),
            pltpu.VMEM((3 * tok, HEAD_DIM), F32),
            pltpu.VMEM((span, wide), F32),
            pltpu.VMEM((span, wide), BF16),
            pltpu.VMEM((span, wide), BF16),
            pltpu.VMEM((tok, 2 * HEAD_DIM), BF16),
            pltpu.VMEM((tok, 2 * HEAD_DIM), BF16),
            pltpu.SemaphoreType.DMA((2 * size + 6,)),
        ],
        compiler_params=pltpu.CompilerParams(vmem_limit_bytes=32 * 1024 * 1024),
        cost_estimate=pl.CostEstimate(
            flops=flops, bytes_accessed=8 * 1024 * 1024, transcendentals=flops // 1536
        ),
        name="attend",
    )(low, *pieces, kv0, kv1, kv2)
    return results[:size], results[size:]


def lowest_key(segment_ids, tok):
    start = (lax.axis_index("pipe") // CORES) * tok
    padded = jnp.concatenate([jnp.full((WINDOW,), -1, jnp.int32), segment_ids])
    keys = lax.dynamic_slice_in_dim(padded, start, WINDOW + tok, 0)
    queries = lax.dynamic_slice_in_dim(segment_ids, start, tok, 0)
    before = jnp.sum((keys[:, None] < queries[None, :]).astype(jnp.int32), axis=0)
    return jnp.maximum(before, jnp.arange(1, tok + 1, dtype=jnp.int32))[None, :]


def body(query, key, value, grad_out, segment_ids):
    size = CORES * lax.axis_size("tensor")
    rows = query.shape[0]
    tok = size * rows
    assert WINDOW == 2 * tok
    heads = key.shape[1] // (size * HEAD_DIM)
    low = lowest_key(segment_ids, tok)
    group_at = lax.axis_index("pipe") // CORES
    odd = group_at % 2 == 1
    odd_pair = (group_at // 2) % 2 == 1

    kv = pack((key, value), size)
    kv = [kv[0]] + [swap(kv[j], j) for j in range(1, size)]
    kv0 = list(join(kv))
    qg = pack((query, grad_out), size)
    kv1, kv2 = [None] * heads, [None] * heads
    for head in range(heads):
        if head:
            kv0[head], kv2[head - 1] = after(kv0[head], kv2[head - 1])
        hops = hop(kv0[head], size, False)
        if head == 0:
            kv0[0], *qg = after(kv0[0], *qg)
            qg = [qg[0]] + [swap(qg[j], j) for j in range(1, size)]
        kv2[head] = jnp.where(odd_pair, hops[0], hops[1])
        kv1[head] = swap(jnp.where(odd, kv2[head], kv0[head]), size)

    og, dkv0, sent, backs, turns = [], [], [], [], []
    for head in range(heads):
        og_head, (dkv0_head, dkv1_head, dkv2_head) = attend(
            low, qg, kv0[head], kv1[head], kv2[head], head, heads
        )
        turns.append((dkv0_head, swap(dkv1_head, size), dkv2_head))
        og.append([og_head[0]] + [swap(og_head[j], j) for j in range(1, size)])
    terms = []
    for dkv0_head, turned, dkv2_head in turns:
        turned = turned.astype(F32)
        own = dkv0_head + jnp.where(odd, 0.0, turned)
        give = (dkv2_head.astype(F32) + jnp.where(odd, turned, 0.0)).astype(BF16)
        terms += [own] + hop(give, size, True)
    grads = combine(terms, size)
    grads = [grads[0]] + [swap(grads[j], j) for j in range(1, size)]
    attn_out, grad_query = spread(og, 2)
    grad_key, grad_value = spread([grads], 2)
    return (attn_out, grad_query, grad_key, grad_value)


def solution(mesh):
    placed = P(("pipe", "tensor"), None)
    return jax.shard_map(
        body,
        mesh=mesh,
        in_specs=(placed, placed, placed, placed, P()),
        out_specs=(placed, placed, placed, placed),
        check_vma=False,
    )
```

time: 93.1 us -> 94.7 us (1.017)
  starting transfers between devices: 19.3 us -> 34.5 us
  waiting for transfers between devices: 48.3 us -> 35.7 us
  local copies, waits for them, and re-layouts: 4.14 us -> 2.12 us
    ppermute x4 -> x8, waiting for transfers between devices: 30.2 us -> 12 us  [hop(): results.append(lax.ppermute(value, ('pipe', 'tensor'), pairs))]
    ppermute x12 -> x19, starting transfers between devices: 9.78 us -> 18 us  [swap(): lax.ppermute(value, ('pipe', 'tensor'), [(i, i ^ mask) for i in range(cou...]
    ppermute x4 -> x8, starting transfers between devices: 9.48 us -> 16.6 us  [hop(): results.append(lax.ppermute(value, ('pipe', 'tensor'), pairs))]
    ppermute x12 -> x19, waiting for transfers between devices: 18.1 us -> 23.7 us  [swap(): lax.ppermute(value, ('pipe', 'tensor'), [(i, i ^ mask) for i in range(cou...]
    unnamed x14 -> x10, local copies, waits for them, and re-layouts: 3.99 us -> 1.96 us
    pallas_call x7 -> x8, Pallas kernels: 19.9 us -> 20.3 us  [the longest x2 16.8 us: attend(): pl.pallas_call(functools.partial(attend_body, size, head, heads, group, r...]
  transfers between devices with their start and end apart: 16 -> 27, of which waited for: 8 -> 11; matrix products, arithmetic and copies ran while one was open for 1% -> 1% of each run, Pallas kernels for 2% -> 20%
where the time goes in v3:
time: 94.7 us; the launch traced here: 94.5 us
  waiting for transfers between devices  35.7 us (38%)
  starting transfers between devices  34.5 us (36%)
  Pallas kernels  20.3 us (21%)
  local copies, waits for them, and re-layouts  2.12 us (2%)
  between operations  1.06 us (1%)
    ppermute x19, waiting for transfers between devices, swap(): lax.ppermute(value, ('pipe', 'tensor'), [(i, i ^ mask) for i in range(cou...  23.7 us
    ppermute x19, starting transfers between devices, swap(): lax.ppermute(value, ('pipe', 'tensor'), [(i, i ^ mask) for i in range(cou...  18 us
    pallas_call x2, Pallas kernels, attend(): pl.pallas_call(functools.partial(attend_body, size, head, heads, group, r...  16.8 us
    ppermute x8, starting transfers between devices, hop(): results.append(lax.ppermute(value, ('pipe', 'tensor'), pairs))  16.6 us
    ppermute x8, waiting for transfers between devices, hop(): results.append(lax.ppermute(value, ('pipe', 'tensor'), pairs))  12 us
    unnamed x10, local copies, waits for them, and re-layouts  1.96 us
    pallas_call x2, Pallas kernels, spread(): pl.pallas_call(functools.partial(spread_body, size, len(chunks), count),...  1.93 us
  transfers between devices with their start and end apart: 27, of which 11 were waited for; matrix products, arithmetic and copies ran while one was open for 1% of the time, Pallas kernels for 20%

profile of v3, /device:TPU:0, one launch (start us, length us, event | category | flops | bytes accessed | tf_op | source)
XLA Modules:
  0.0 94.5 jit_solution(15900463123554925168)
XLA Ops:
  0.7 1.0 %copy-done.2 = bf16[128,1024]{1,0:T(8,128)(2,1)S(1)} copy-done((bf16[128,1024]{1,0:T(8,128)(2,1)S(1)}, bf16[128,1024]{1,0:T(8,128)(2,1)}, u32[]{:S(2)}) %copy-start.2) | copy-done | bytes 262168
  1.7 0.9 %copy-done.3 = bf16[128,1024]{1,0:T(8,128)(2,1)S(1)} copy-done((bf16[128,1024]{1,0:T(8,128)(2,1)S(1)}, bf16[128,1024]{1,0:T(8,128)(2,1)}, u32[]{:S(2)}) %copy-start.3) | copy-done | bytes 262168
  2.8 3.0 %collective-permute-start = (bf16[128,512]{1,0:T(8,128)(2,1)S(1)}, bf16[128,512]{1,0:T(8,128)(2,1)S(1)}, u32[]{:S(2)}, u32[]{:S(2)}) collective-permute-start(bf16[128,512]{1,0:T(8,128)(2,1)S(1)} %get-tuple-element.44), channel_id=1, source_target_pairs={{0,1},{1,0},{2,3},{3,2},{4,5},{5,4},{6,7},{7,6},{8,9},{9,8},{10,11... | collective-permute-start | bytes 393224 | tf_op jit(solution)/shard_map/ppermute | solution.py:33
  6.0 3.7 %collective-permute-done.refs_1_ = bf16[128,512]{1,0:T(8,128)(2,1)S(1)} collective-permute-done((bf16[128,512]{1,0:T(8,128)(2,1)S(1)}, bf16[128,512]{1,0:T(8,128)(2,1)S(1)}, u32[]{:S(2)}, u32[]{:S(2)}) %collective-permute-start) | collective-permute-done | bytes 131104 | tf_op jit(solution)/shard_map/ppermute | solution.py:33
  9.7 1.9 %collective-permute-done.2.refs_3_ = bf16[128,512]{1,0:T(8,128)(2,1)S(1)} collective-permute-done((bf16[128,512]{1,0:T(8,128)(2,1)S(1)}, bf16[128,512]{1,0:T(8,128)(2,1)S(1)}, u32[]{:S(2)}, u32[]{:S(2)}) %collective-permute-start.2) | collective-permute-done | bytes 131104 | tf_op jit(solution)/shard_map/ppermute | solution.py:33
  12.6 6.2 %collective-permute-start.6 = (bf16[512,256]{1,0:T(8,128)(2,1)S(1)}, bf16[512,256]{1,0:T(8,128)(2,1)S(1)}, u32[]{:S(2)}, u32[]{:S(2)}) collective-permute-start(bf16[512,256]{1,0:T(8,128)(2,1)S(1)} %get-tuple-element.56.refs_5_), channel_id=1, source_target_pairs={{0,8},{1,9},{2,10},{3,11},{4,12},{5,13},{6,14},{7,15},{16,24},{17,... | collective-permute-start | bytes 786440 | tf_op jit(solution)/shard_map/ppermute | solution.py:43
  19.3 5.6 %collective-permute-done.6 = bf16[512,256]{1,0:T(8,128)(2,1)S(1)} collective-permute-done((bf16[512,256]{1,0:T(8,128)(2,1)S(1)}, bf16[512,256]{1,0:T(8,128)(2,1)S(1)}, u32[]{:S(2)}, u32[]{:S(2)}) %collective-permute-start.6) | collective-permute-done | bytes 262176 | tf_op jit(solution)/shard_map/ppermute | solution.py:43
  25.7 5.0 %collective-permute-start.12 = (bf16[512,256]{1,0:T(8,128)(2,1)S(1)}, bf16[512,256]{1,0:T(8,128)(2,1)S(1)}, u32[]{:S(2)}, u32[]{:S(2)}) collective-permute-start(bf16[512,256]{1,0:T(8,128)(2,1)S(1)} %get-tuple-element.63.refs_5_), channel_id=1, source_target_pairs={{0,8},{1,9},{2,10},{3,11},{4,12},{5,13},{6,14},{7,15},{16,24},{17,... | collective-permute-start | bytes 786440 | tf_op jit(solution)/shard_map/ppermute | solution.py:43
  31.1 1.6 %collective-permute-start.3 = (bf16[128,1024]{1,0:T(8,128)(2,1)S(1)}, bf16[128,1024]{1,0:T(8,128)(2,1)S(1)}, u32[]{:S(2)}, u32[]{:S(2)}) collective-permute-start(bf16[128,1024]{1,0:T(8,128)(2,1)S(1)} %get-tuple-element.53), channel_id=1, source_target_pairs={{0,1},{1,0},{2,3},{3,2},{4,5},{5,4},{6,7},{7,6},{8,9},{9,8},{10,11... | collective-permute-start | bytes 786440 | tf_op jit(solution)/shard_map/ppermute | solution.py:33
  33.3 1.5 %collective-permute-start.8 = (bf16[512,256]{1,0:T(8,128)(2,1)S(1)}, bf16[512,256]{1,0:T(8,128)(2,1)S(1)}, u32[]{:S(2)}, u32[]{:S(2)}) collective-permute-start(bf16[512,256]{1,0:T(8,128)(2,1)S(1)} %get-tuple-element.84), channel_id=1, source_target_pairs={{0,4},{1,5},{2,6},{3,7},{4,0},{5,1},{6,2},{7,3},{8,12},{9,13},{10,... | collective-permute-start | bytes 786440 | tf_op jit(solution)/shard_map/ppermute | solution.py:33
  34.8 1.1 %collective-permute-done.12 = bf16[512,256]{1,0:T(8,128)(2,1)S(1)} collective-permute-done((bf16[512,256]{1,0:T(8,128)(2,1)S(1)}, bf16[512,256]{1,0:T(8,128)(2,1)S(1)}, u32[]{:S(2)}, u32[]{:S(2)}) %collective-permute-start.12) | collective-permute-done | bytes 262176 | tf_op jit(solution)/shard_map/ppermute | solution.py:43
  36.0 1.6 %collective-permute-start.14 = (bf16[512,256]{1,0:T(8,128)(2,1)S(1)}, bf16[512,256]{1,0:T(8,128)(2,1)S(1)}, u32[]{:S(2)}, u32[]{:S(2)}) collective-permute-start(bf16[512,256]{1,0:T(8,128)(2,1)S(1)} %get-tuple-element.82), channel_id=1, source_target_pairs={{0,4},{1,5},{2,6},{3,7},{4,0},{5,1},{6,2},{7,3},{8,12},{9,13},{10,... | collective-permute-start | bytes 786440 | tf_op jit(solution)/shard_map/ppermute | solution.py:33
  37.5 2.9 %collective-permute-done.3.refs_2_ = bf16[128,1024]{1,0:T(8,128)(2,1)S(1)} collective-permute-done((bf16[128,1024]{1,0:T(8,128)(2,1)S(1)}, bf16[128,1024]{1,0:T(8,128)(2,1)S(1)}, u32[]{:S(2)}, u32[]{:S(2)}) %collective-permute-start.3) | collective-permute-done | bytes 262176 | tf_op jit(solution)/shard_map/ppermute | solution.py:33
  40.4 3.1 %collective-permute-done.5.refs_4_ = bf16[128,1024]{1,0:T(8,128)(2,1)S(1)} collective-permute-done((bf16[128,1024]{1,0:T(8,128)(2,1)S(1)}, bf16[128,1024]{1,0:T(8,128)(2,1)S(1)}, u32[]{:S(2)}, u32[]{:S(2)}) %collective-permute-start.5) | collective-permute-done | bytes 262176 | tf_op jit(solution)/shard_map/ppermute | solution.py:33
  43.6 8.3 %attend.2 = (bf16[128,512]{1,0:T(8,128)(2,1)S(1)}, bf16[128,512]{1,0:T(8,128)(2,1)S(1)}, bf16[128,512]{1,0:T(8,128)(2,1)S(1)}, bf16[128,512]{1,0:T(8,128)(2,1)S(...) custom-call(s32[1,512]{1,0:T(1,128)S(1)} %add_maximum_fusion.refs_0_, ...), custom_call_target="tpu_custom_call" | custom-call | flops 1811939328 | bytes 8388608 | tf_op jit(solution)/shard_map/attend/pallas_call | solution.py:302
  51.9 1.6 %collective-permute-start.18 = (bf16[512,256]{1,0:T(8,128)(2,1)S(1)}, bf16[512,256]{1,0:T(8,128)(2,1)S(1)}, u32[]{:S(2)}, u32[]{:S(2)}) collective-permute-start(bf16[512,256]{1,0:T(8,128)(2,1)S(1)} %get-tuple-element.71), channel_id=1, source_target_pairs={{0,4},{1,5},{2,6},{3,7},{4,0},{5,1},{6,2},{7,3},{8,12},{9,13},{10,... | collective-permute-start | bytes 786440 | tf_op jit(solution)/shard_map/ppermute | solution.py:33
  53.5 8.5 %attend.3 = (bf16[128,512]{1,0:T(8,128)(2,1)S(1)}, bf16[128,512]{1,0:T(8,128)(2,1)S(1)}, bf16[128,512]{1,0:T(8,128)(2,1)S(1)}, bf16[128,512]{1,0:T(8,128)(2,1)S(...) custom-call(s32[1,512]{1,0:T(1,128)S(1)} %add_maximum_fusion.refs_0_, ...), custom_call_target="tpu_custom_call" | custom-call | flops 1811939328 | bytes 8388608 | tf_op jit(solution)/shard_map/attend/pallas_call | solution.py:302
  63.3 1.3 %collective-permute-start.19 = (bf16[512,256]{1,0:T(8,128)(2,1)S(1)}, bf16[512,256]{1,0:T(8,128)(2,1)S(1)}, u32[]{:S(2)}, u32[]{:S(2)}) collective-permute-start(bf16[512,256]{1,0:T(8,128)(2,1)S(1)} %get-tuple-element.88), channel_id=1, source_target_pairs={{8,0},{9,1},{10,2},{11,3},{12,4},{13,5},{14,6},{15,7},{24,16},{25,... | collective-permute-start | bytes 786440 | tf_op jit(solution)/shard_map/ppermute | solution.py:43
  64.6 6.2 %collective-permute-done.21 = bf16[512,256]{1,0:T(8,128)(2,1)S(1)} collective-permute-done((bf16[512,256]{1,0:T(8,128)(2,1)S(1)}, bf16[512,256]{1,0:T(8,128)(2,1)S(1)}, u32[]{:S(2)}, u32[]{:S(2)}) %collective-permute-start.21) | collective-permute-done | bytes 262176 | tf_op jit(solution)/shard_map/ppermute | solution.py:33
  71.6 1.3 %collective-permute-start.22 = (bf16[512,256]{1,0:T(8,128)(2,1)S(1)}, bf16[512,256]{1,0:T(8,128)(2,1)S(1)}, u32[]{:S(2)}, u32[]{:S(2)}) collective-permute-start(bf16[512,256]{1,0:T(8,128)(2,1)S(1)} %get-tuple-element.86), channel_id=1, source_target_pairs={{8,0},{9,1},{10,2},{11,3},{12,4},{13,5},{14,6},{15,7},{24,16},{25,... | collective-permute-start | bytes 786440 | tf_op jit(solution)/shard_map/ppermute | solution.py:43
  72.9 1.1 %collective-permute-start.9 = (bf16[128,512]{1,0:T(8,128)(2,1)S(1)}, bf16[128,512]{1,0:T(8,128)(2,1)S(1)}, u32[]{:S(2)}, u32[]{:S(2)}) collective-permute-start(bf16[128,512]{1,0:T(8,128)(2,1)S(1)} %get-tuple-element.60), channel_id=1, source_target_pairs={{0,1},{1,0},{2,3},{3,2},{4,5},{5,4},{6,7},{7,6},{8,9},{9,8},{10,11... | collective-permute-start | bytes 393224 | tf_op jit(solution)/shard_map/ppermute | solution.py:33
  74.2 0.9 collective-permute-start.11
  75.1 1.1 %collective-permute-start.15 = (bf16[128,512]{1,0:T(8,128)(2,1)S(1)}, bf16[128,512]{1,0:T(8,128)(2,1)S(1)}, u32[]{:S(2)}, u32[]{:S(2)}) collective-permute-start(bf16[128,512]{1,0:T(8,128)(2,1)S(1)} %get-tuple-element.65), channel_id=1, source_target_pairs={{0,1},{1,0},{2,3},{3,2},{4,5},{5,4},{6,7},{7,6},{8,9},{9,8},{10,11... | collective-permute-start | bytes 393224 | tf_op jit(solution)/shard_map/ppermute | solution.py:33
  76.2 5.3 %collective-permute-done.22.refs_4_ = bf16[512,256]{1,0:T(8,128)(2,1)S(1)} collective-permute-done((bf16[512,256]{1,0:T(8,128)(2,1)S(1)}, bf16[512,256]{1,0:T(8,128)(2,1)S(1)}, u32[]{:S(2)}, u32[]{:S(2)}) %collective-permute-start.22) | collective-permute-done | bytes 262176 | tf_op jit(solution)/shard_map/ppermute | solution.py:43
  81.5 0.9 combine.1
  82.4 1.9 %collective-permute-start.17 = (bf16[128,512]{1,0:T(8,128)(2,1)S(1)}, bf16[128,512]{1,0:T(8,128)(2,1)S(1)}, u32[]{:S(2)}, u32[]{:S(2)}) collective-permute-start(bf16[128,512]{1,0:T(8,128)(2,1)S(1)} %get-tuple-element.67), channel_id=1, source_target_pairs={{0,3},{1,2},{2,1},{3,0},{4,7},{5,6},{6,5},{7,4},{8,11},{9,10},{10,... | collective-permute-start | bytes 393224 | tf_op jit(solution)/shard_map/ppermute | solution.py:33
  84.7 1.8 %collective-permute-start.26 = (bf16[128,512]{1,0:T(8,128)(2,1)S(1)}, bf16[128,512]{1,0:T(8,128)(2,1)S(1)}, u32[]{:S(2)}, u32[]{:S(2)}) collective-permute-start(bf16[128,512]{1,0:T(8,128)(2,1)S(1)} %get-tuple-element.79), channel_id=1, source_target_pairs={{0,3},{1,2},{2,1},{3,0},{4,7},{5,6},{6,5},{7,4},{8,11},{9,10},{10,... | collective-permute-start | bytes 393224 | tf_op jit(solution)/shard_map/ppermute | solution.py:33
  86.5 1.7 %collective-permute-done.17.refs_7_ = bf16[128,512]{1,0:T(8,128)(2,1)S(1)} collective-permute-done((bf16[128,512]{1,0:T(8,128)(2,1)S(1)}, bf16[128,512]{1,0:T(8,128)(2,1)S(1)}, u32[]{:S(2)}, u32[]{:S(2)}) %collective-permute-start.17) | collective-permute-done | bytes 131104 | tf_op jit(solution)/shard_map/ppermute | solution.py:33
  88.2 1.1 %spread.2 = (bf16[128,2048]{1,0:T(8,128)(2,1)}, bf16[128,2048]{1,0:T(8,128)(2,1)}) custom-call(bf16[128,512]{1,0:T(8,128)(2,1)S(1)} %get-tuple-element.59.refs_0_, bf16[128,512]{1,0:T(8,128)(2,1)S(1)} %collective-permute-done.9.refs_1_, bf16[128,512]{1,0:T(8,128)(2,1)S(1)} %collective-permute-done.10.refs_2_, ...), custom_call_target="tpu_custom_call" | custom-call | tf_op jit(solution)/shard_map/spread/pallas_call | solution.py:173
  89.3 2.5 %collective-permute-done.24.refs_1_ = bf16[128,512]{1,0:T(8,128)(2,1)S(1)} collective-permute-done((bf16[128,512]{1,0:T(8,128)(2,1)S(1)}, bf16[128,512]{1,0:T(8,128)(2,1)S(1)}, u32[]{:S(2)}, u32[]{:S(2)}) %collective-permute-start.24) | collective-permute-done | bytes 131104 | tf_op jit(solution)/shard_map/ppermute | solution.py:33
  91.7 1.7 %collective-permute-done.26.refs_3_ = bf16[128,512]{1,0:T(8,128)(2,1)S(1)} collective-permute-done((bf16[128,512]{1,0:T(8,128)(2,1)S(1)}, bf16[128,512]{1,0:T(8,128)(2,1)S(1)}, u32[]{:S(2)}, u32[]{:S(2)}) %collective-permute-start.26) | collective-permute-done | bytes 131104 | tf_op jit(solution)/shard_map/ppermute | solution.py:33
  93.5 0.8 spread.3
  (48 shorter events, 6.2 us)
Async XLA Ops:
  0.6 18.4 %copy-start.1 = (bf16[128,2048]{1,0:T(8,128)(2,1)S(1)}, bf16[128,2048]{1,0:T(8,128)(2,1)}, u32[]{:S(2)}) copy-start(bf16[128,2048]{1,0:T(8,128)(2,1)} %refs_1_.3) | copy-start | bytes 1572868
  0.6 1.0 %copy-start.2 = (bf16[128,1024]{1,0:T(8,128)(2,1)S(1)}, bf16[128,1024]{1,0:T(8,128)(2,1)}, u32[]{:S(2)}) copy-start(bf16[128,1024]{1,0:T(8,128)(2,1)} %refs_0_.2) | copy-start | bytes 786436
  1.6 0.9 %copy-start.3 = (bf16[128,1024]{1,0:T(8,128)(2,1)S(1)}, bf16[128,1024]{1,0:T(8,128)(2,1)}, u32[]{:S(2)}) copy-start(bf16[128,1024]{1,0:T(8,128)(2,1)} %refs_1_.2) | copy-start | bytes 786436
  2.6 16.3 %copy-start.4 = (s32[4096]{0:T(1024)S(1)}, s32[4096]{0:T(1024)}, u32[]{:S(2)}) copy-start(s32[4096]{0:T(1024)} %param.9) | copy-start | bytes 49156
  2.6 16.4 %copy-start = (bf16[128,2048]{1,0:T(8,128)(2,1)S(1)}, bf16[128,2048]{1,0:T(8,128)(2,1)}, u32[]{:S(2)}) copy-start(bf16[128,2048]{1,0:T(8,128)(2,1)} %refs_0_.3) | copy-start | bytes 1572868
  2.8 6.9 %collective-permute-start = (bf16[128,512]{1,0:T(8,128)(2,1)S(1)}, bf16[128,512]{1,0:T(8,128)(2,1)S(1)}, u32[]{:S(2)}, u32[]{:S(2)}) collective-permute-start(bf16[128,512]{1,0:T(8,128)(2,1)S(1)} %get-tuple-element.44), channel_id=1, source_target_pairs={{0,1},{1,0},{2,3},{3,2},{4,5},{5,4},{6,7},{7,6},{8,9},{9,8},{10,11... | collective-permute-start | bytes 393224 | tf_op jit(solution)/shard_map/ppermute | solution.py:33
  5.8 3.9 %collective-permute-start.1 = (bf16[128,512]{1,0:T(8,128)(2,1)S(1)}, bf16[128,512]{1,0:T(8,128)(2,1)S(1)}, u32[]{:S(2)}, u32[]{:S(2)}) collective-permute-start(bf16[128,512]{1,0:T(8,128)(2,1)S(1)} %get-tuple-element.45), channel_id=1, source_target_pairs={{0,2},{1,3},{2,0},{3,1},{4,6},{5,7},{6,4},{7,5},{8,10},{9,11},{10,... | collective-permute-start | bytes 393224 | tf_op jit(solution)/shard_map/ppermute | solution.py:33
  5.8 5.9 %collective-permute-start.2 = (bf16[128,512]{1,0:T(8,128)(2,1)S(1)}, bf16[128,512]{1,0:T(8,128)(2,1)S(1)}, u32[]{:S(2)}, u32[]{:S(2)}) collective-permute-start(bf16[128,512]{1,0:T(8,128)(2,1)S(1)} %get-tuple-element.46), channel_id=1, source_target_pairs={{0,3},{1,2},{2,1},{3,0},{4,7},{5,6},{6,5},{7,4},{8,11},{9,10},{10,... | collective-permute-start | bytes 393224 | tf_op jit(solution)/shard_map/ppermute | solution.py:33
  11.9 7.3 %collective-permute-start.7 = (bf16[512,256]{1,0:T(8,128)(2,1)S(1)}, bf16[512,256]{1,0:T(8,128)(2,1)S(1)}, u32[]{:S(2)}, u32[]{:S(2)}) collective-permute-start(bf16[512,256]{1,0:T(8,128)(2,1)S(1)} %get-tuple-element.56.refs_5_), channel_id=1, source_target_pairs={{8,16},{9,17},{10,18},{11,19},{12,20},{13,21},{14,22},{15,23}} | collective-permute-start | bytes 786440 | tf_op jit(solution)/shard_map/ppermute | solution.py:43
  12.6 12.3 %collective-permute-start.6 = (bf16[512,256]{1,0:T(8,128)(2,1)S(1)}, bf16[512,256]{1,0:T(8,128)(2,1)S(1)}, u32[]{:S(2)}, u32[]{:S(2)}) collective-permute-start(bf16[512,256]{1,0:T(8,128)(2,1)S(1)} %get-tuple-element.56.refs_5_), channel_id=1, source_target_pairs={{0,8},{1,9},{2,10},{3,11},{4,12},{5,13},{6,14},{7,15},{16,24},{17,... | collective-permute-start | bytes 786440 | tf_op jit(solution)/shard_map/ppermute | solution.py:43
  24.9 8.4 %collective-permute-start.13 = (bf16[512,256]{1,0:T(8,128)(2,1)S(1)}, bf16[512,256]{1,0:T(8,128)(2,1)S(1)}, u32[]{:S(2)}, u32[]{:S(2)}) collective-permute-start(bf16[512,256]{1,0:T(8,128)(2,1)S(1)} %get-tuple-element.63.refs_5_), channel_id=1, source_target_pairs={{8,16},{9,17},{10,18},{11,19},{12,20},{13,21},{14,22},{15,23}} | collective-permute-start | bytes 786440 | tf_op jit(solution)/shard_map/ppermute | solution.py:43
  25.7 10.2 %collective-permute-start.12 = (bf16[512,256]{1,0:T(8,128)(2,1)S(1)}, bf16[512,256]{1,0:T(8,128)(2,1)S(1)}, u32[]{:S(2)}, u32[]{:S(2)}) collective-permute-start(bf16[512,256]{1,0:T(8,128)(2,1)S(1)} %get-tuple-element.63.refs_5_), channel_id=1, source_target_pairs={{0,8},{1,9},{2,10},{3,11},{4,12},{5,13},{6,14},{7,15},{16,24},{17,... | collective-permute-start | bytes 786440 | tf_op jit(solution)/shard_map/ppermute | solution.py:43
  31.1 9.3 %collective-permute-start.3 = (bf16[128,1024]{1,0:T(8,128)(2,1)S(1)}, bf16[128,1024]{1,0:T(8,128)(2,1)S(1)}, u32[]{:S(2)}, u32[]{:S(2)}) collective-permute-start(bf16[128,1024]{1,0:T(8,128)(2,1)S(1)} %get-tuple-element.53), channel_id=1, source_target_pairs={{0,1},{1,0},{2,3},{3,2},{4,5},{5,4},{6,7},{7,6},{8,9},{9,8},{10,11... | collective-permute-start | bytes 786440 | tf_op jit(solution)/shard_map/ppermute | solution.py:33
  32.6 7.8 %collective-permute-start.4 = (bf16[128,1024]{1,0:T(8,128)(2,1)S(1)}, bf16[128,1024]{1,0:T(8,128)(2,1)S(1)}, u32[]{:S(2)}, u32[]{:S(2)}) collective-permute-start(bf16[128,1024]{1,0:T(8,128)(2,1)S(1)} %get-tuple-element.54), channel_id=1, source_target_pairs={{0,2},{1,3},{2,0},{3,1},{4,6},{5,7},{6,4},{7,5},{8,10},{9,11},{10,... | collective-permute-start | bytes 786440 | tf_op jit(solution)/shard_map/ppermute | solution.py:33
  32.6 10.9 %collective-permute-start.5 = (bf16[128,1024]{1,0:T(8,128)(2,1)S(1)}, bf16[128,1024]{1,0:T(8,128)(2,1)S(1)}, u32[]{:S(2)}, u32[]{:S(2)}) collective-permute-start(bf16[128,1024]{1,0:T(8,128)(2,1)S(1)} %get-tuple-element.55), channel_id=1, source_target_pairs={{0,3},{1,2},{2,1},{3,0},{4,7},{5,6},{6,5},{7,4},{8,11},{9,10},{10,... | collective-permute-start | bytes 786440 | tf_op jit(solution)/shard_map/ppermute | solution.py:33
  33.3 10.3 %collective-permute-start.8 = (bf16[512,256]{1,0:T(8,128)(2,1)S(1)}, bf16[512,256]{1,0:T(8,128)(2,1)S(1)}, u32[]{:S(2)}, u32[]{:S(2)}) collective-permute-start(bf16[512,256]{1,0:T(8,128)(2,1)S(1)} %get-tuple-element.84), channel_id=1, source_target_pairs={{0,4},{1,5},{2,6},{3,7},{4,0},{5,1},{6,2},{7,3},{8,12},{9,13},{10,... | collective-permute-start | bytes 786440 | tf_op jit(solution)/shard_map/ppermute | solution.py:33
  36.0 17.5 %collective-permute-start.14 = (bf16[512,256]{1,0:T(8,128)(2,1)S(1)}, bf16[512,256]{1,0:T(8,128)(2,1)S(1)}, u32[]{:S(2)}, u32[]{:S(2)}) collective-permute-start(bf16[512,256]{1,0:T(8,128)(2,1)S(1)} %get-tuple-element.82), channel_id=1, source_target_pairs={{0,4},{1,5},{2,6},{3,7},{4,0},{5,1},{6,2},{7,3},{8,12},{9,13},{10,... | collective-permute-start | bytes 786440 | tf_op jit(solution)/shard_map/ppermute | solution.py:33
  51.9 10.7 %collective-permute-start.18 = (bf16[512,256]{1,0:T(8,128)(2,1)S(1)}, bf16[512,256]{1,0:T(8,128)(2,1)S(1)}, u32[]{:S(2)}, u32[]{:S(2)}) collective-permute-start(bf16[512,256]{1,0:T(8,128)(2,1)S(1)} %get-tuple-element.71), channel_id=1, source_target_pairs={{0,4},{1,5},{2,6},{3,7},{4,0},{5,1},{6,2},{7,3},{8,12},{9,13},{10,... | collective-permute-start | bytes 786440 | tf_op jit(solution)/shard_map/ppermute | solution.py:33
  62.0 8.9 %collective-permute-start.21 = (bf16[512,256]{1,0:T(8,128)(2,1)S(1)}, bf16[512,256]{1,0:T(8,128)(2,1)S(1)}, u32[]{:S(2)}, u32[]{:S(2)}) collective-permute-start(bf16[512,256]{1,0:T(8,128)(2,1)S(1)} %get-tuple-element.74), channel_id=1, source_target_pairs={{0,4},{1,5},{2,6},{3,7},{4,0},{5,1},{6,2},{7,3},{8,12},{9,13},{10,... | collective-permute-start | bytes 786440 | tf_op jit(solution)/shard_map/ppermute | solution.py:33
  62.6 11.4 %collective-permute-start.20 = (bf16[512,256]{1,0:T(8,128)(2,1)S(1)}, bf16[512,256]{1,0:T(8,128)(2,1)S(1)}, u32[]{:S(2)}, u32[]{:S(2)}) collective-permute-start(bf16[512,256]{1,0:T(8,128)(2,1)S(1)} %get-tuple-element.88), channel_id=1, source_target_pairs={{16,8},{17,9},{18,10},{19,11},{20,12},{21,13},{22,14},{23,15}} | collective-permute-start | bytes 786440 | tf_op jit(solution)/shard_map/ppermute | solution.py:43
  63.3 10.9 %collective-permute-start.19 = (bf16[512,256]{1,0:T(8,128)(2,1)S(1)}, bf16[512,256]{1,0:T(8,128)(2,1)S(1)}, u32[]{:S(2)}, u32[]{:S(2)}) collective-permute-start(bf16[512,256]{1,0:T(8,128)(2,1)S(1)} %get-tuple-element.88), channel_id=1, source_target_pairs={{8,0},{9,1},{10,2},{11,3},{12,4},{13,5},{14,6},{15,7},{24,16},{25,... | collective-permute-start | bytes 786440 | tf_op jit(solution)/shard_map/ppermute | solution.py:43
  70.9 4.2 %collective-permute-start.23 = (bf16[512,256]{1,0:T(8,128)(2,1)S(1)}, bf16[512,256]{1,0:T(8,128)(2,1)S(1)}, u32[]{:S(2)}, u32[]{:S(2)}) collective-permute-start(bf16[512,256]{1,0:T(8,128)(2,1)S(1)} %get-tuple-element.86), channel_id=1, source_target_pairs={{16,8},{17,9},{18,10},{19,11},{20,12},{21,13},{22,14},{23,15}} | collective-permute-start | bytes 786440 | tf_op jit(solution)/shard_map/ppermute | solution.py:43
  71.6 9.9 %collective-permute-start.22 = (bf16[512,256]{1,0:T(8,128)(2,1)S(1)}, bf16[512,256]{1,0:T(8,128)(2,1)S(1)}, u32[]{:S(2)}, u32[]{:S(2)}) collective-permute-start(bf16[512,256]{1,0:T(8,128)(2,1)S(1)} %get-tuple-element.86), channel_id=1, source_target_pairs={{8,0},{9,1},{10,2},{11,3},{12,4},{13,5},{14,6},{15,7},{24,16},{25,... | collective-permute-start | bytes 786440 | tf_op jit(solution)/shard_map/ppermute | solution.py:43
  72.9 9.5 %collective-permute-start.9 = (bf16[128,512]{1,0:T(8,128)(2,1)S(1)}, bf16[128,512]{1,0:T(8,128)(2,1)S(1)}, u32[]{:S(2)}, u32[]{:S(2)}) collective-permute-start(bf16[128,512]{1,0:T(8,128)(2,1)S(1)} %get-tuple-element.60), channel_id=1, source_target_pairs={{0,1},{1,0},{2,3},{3,2},{4,5},{5,4},{6,7},{7,6},{8,9},{9,8},{10,11... | collective-permute-start | bytes 393224 | tf_op jit(solution)/shard_map/ppermute | solution.py:33
  74.1 10.3 %collective-permute-start.10 = (bf16[128,512]{1,0:T(8,128)(2,1)S(1)}, bf16[128,512]{1,0:T(8,128)(2,1)S(1)}, u32[]{:S(2)}, u32[]{:S(2)}) collective-permute-start(bf16[128,512]{1,0:T(8,128)(2,1)S(1)} %get-tuple-element.61), channel_id=1, source_target_pairs={{0,2},{1,3},{2,0},{3,1},{4,6},{5,7},{6,4},{7,5},{8,10},{9,11},{10,... | collective-permute-start | bytes 393224 | tf_op jit(solution)/shard_map/ppermute | solution.py:33
  74.2 10.4 %collective-permute-start.11 = (bf16[128,512]{1,0:T(8,128)(2,1)S(1)}, bf16[128,512]{1,0:T(8,128)(2,1)S(1)}, u32[]{:S(2)}, u32[]{:S(2)}) collective-permute-start(bf16[128,512]{1,0:T(8,128)(2,1)S(1)} %get-tuple-element.62), channel_id=1, source_target_pairs={{0,3},{1,2},{2,1},{3,0},{4,7},{5,6},{6,5},{7,4},{8,11},{9,10},{10,... | collective-permute-start | bytes 393224 | tf_op jit(solution)/shard_map/ppermute | solution.py:33
  75.1 9.5 %collective-permute-start.15 = (bf16[128,512]{1,0:T(8,128)(2,1)S(1)}, bf16[128,512]{1,0:T(8,128)(2,1)S(1)}, u32[]{:S(2)}, u32[]{:S(2)}) collective-permute-start(bf16[128,512]{1,0:T(8,128)(2,1)S(1)} %get-tuple-element.65), channel_id=1, source_target_pairs={{0,1},{1,0},{2,3},{3,2},{4,5},{5,4},{6,7},{7,6},{8,9},{9,8},{10,11... | collective-permute-start | bytes 393224 | tf_op jit(solution)/shard_map/ppermute | solution.py:33
  81.5 5.0 %collective-permute-start.16 = (bf16[128,512]{1,0:T(8,128)(2,1)S(1)}, bf16[128,512]{1,0:T(8,128)(2,1)S(1)}, u32[]{:S(2)}, u32[]{:S(2)}) collective-permute-start(bf16[128,512]{1,0:T(8,128)(2,1)S(1)} %get-tuple-element.66), channel_id=1, source_target_pairs={{0,2},{1,3},{2,0},{3,1},{4,6},{5,7},{6,4},{7,5},{8,10},{9,11},{10,... | collective-permute-start | bytes 393224 | tf_op jit(solution)/shard_map/ppermute | solution.py:33
  82.4 5.7 %collective-permute-start.17 = (bf16[128,512]{1,0:T(8,128)(2,1)S(1)}, bf16[128,512]{1,0:T(8,128)(2,1)S(1)}, u32[]{:S(2)}, u32[]{:S(2)}) collective-permute-start(bf16[128,512]{1,0:T(8,128)(2,1)S(1)} %get-tuple-element.67), channel_id=1, source_target_pairs={{0,3},{1,2},{2,1},{3,0},{4,7},{5,6},{6,5},{7,4},{8,11},{9,10},{10,... | collective-permute-start | bytes 393224 | tf_op jit(solution)/shard_map/ppermute | solution.py:33
  84.3 7.4 %collective-permute-start.24 = (bf16[128,512]{1,0:T(8,128)(2,1)S(1)}, bf16[128,512]{1,0:T(8,128)(2,1)S(1)}, u32[]{:S(2)}, u32[]{:S(2)}) collective-permute-start(bf16[128,512]{1,0:T(8,128)(2,1)S(1)} %get-tuple-element.77), channel_id=1, source_target_pairs={{0,1},{1,0},{2,3},{3,2},{4,5},{5,4},{6,7},{7,6},{8,9},{9,8},{10,11... | collective-permute-start | bytes 393224 | tf_op jit(solution)/shard_map/ppermute | solution.py:33
  84.7 7.1 %collective-permute-start.25 = (bf16[128,512]{1,0:T(8,128)(2,1)S(1)}, bf16[128,512]{1,0:T(8,128)(2,1)S(1)}, u32[]{:S(2)}, u32[]{:S(2)}) collective-permute-start(bf16[128,512]{1,0:T(8,128)(2,1)S(1)} %get-tuple-element.78), channel_id=1, source_target_pairs={{0,2},{1,3},{2,0},{3,1},{4,6},{5,7},{6,4},{7,5},{8,10},{9,11},{10,... | collective-permute-start | bytes 393224 | tf_op jit(solution)/shard_map/ppermute | solution.py:33
  84.7 8.8 %collective-permute-start.26 = (bf16[128,512]{1,0:T(8,128)(2,1)S(1)}, bf16[128,512]{1,0:T(8,128)(2,1)S(1)}, u32[]{:S(2)}, u32[]{:S(2)}) collective-permute-start(bf16[128,512]{1,0:T(8,128)(2,1)S(1)} %get-tuple-element.79), channel_id=1, source_target_pairs={{0,3},{1,2},{2,1},{3,0},{4,7},{5,6},{6,5},{7,4},{8,11},{9,10},{10,... | collective-permute-start | bytes 393224 | tf_op jit(solution)/shard_map/ppermute | solution.py:33

commit v4 on v3

v4 whole, which is shorter than its diff:
```python
import functools

import jax
import jax.numpy as jnp
from jax import lax
from jax.experimental import pallas as pl
from jax.experimental.pallas import tpu as pltpu
from jax.sharding import PartitionSpec as P

HEAD_DIM = 128
WINDOW = 1024
TILE = 128

logit_scale = 168.0 ** (-0.5)
exp2_scale = logit_scale * 1.4426950408889634

SMALL = pltpu.CompilerParams(vmem_limit_bytes=4 * 1024 * 1024)
ANY = pl.BlockSpec(memory_space=pl.ANY)
VMEM = pl.BlockSpec(memory_space=pltpu.VMEM)
F32 = jnp.float32
BF16 = jnp.bfloat16
BOTH = ("pipe", "tensor")


def flat_index():
    return lax.axis_index("pipe") * lax.axis_size("tensor") + lax.axis_index("tensor")


def device_count():
    return lax.axis_size("pipe") * lax.axis_size("tensor")


def exchange(value):
    size = value.shape[0]
    groups = [[at + i for i in range(size)] for at in range(0, device_count(), size)]
    return lax.all_to_all(
        value, BOTH, split_axis=0, concat_axis=0, axis_index_groups=groups, tiled=True
    )


def shifted(value, step):
    count = device_count()
    pairs = [(i, i + step) for i in range(count) if 0 <= i + step < count]
    return lax.ppermute(value, BOTH, pairs)


def after(value, *others):
    return lax.optimization_barrier((value, *others))


def run_copies(copies, sems):
    started = []
    for at, (source, target) in enumerate(copies):
        copy = pltpu.make_async_copy(source, target, sems.at[at])
        copy.start()
        started.append(copy)
    for copy in started:
        copy.wait()


def pack_body(size, widths, *refs):
    arrays, out, sems = refs[: len(widths)], refs[-2], refs[-1]
    copies = []
    for j in range(size):
        start = 0
        for array, width in zip(arrays, widths):
            copies.append(
                (
                    array.at[:, j * width : (j + 1) * width],
                    out.at[j, :, start : start + width],
                )
            )
            start += width
    run_copies(copies, sems)


def pack(arrays, size):
    rows = arrays[0].shape[0]
    widths = [array.shape[1] // size for array in arrays]
    return pl.pallas_call(
        functools.partial(pack_body, size, widths),
        out_shape=jax.ShapeDtypeStruct((size, rows, sum(widths)), BF16),
        in_specs=[ANY] * len(arrays),
        out_specs=ANY,
        scratch_shapes=[pltpu.SemaphoreType.DMA((size * len(arrays),))],
        compiler_params=SMALL,
        name="pack",
    )(*arrays)


def spread_body(size, width, shares, *refs):
    outs, sems = refs[:-1], refs[-1]
    copies = []
    for j in range(size):
        for at, out in enumerate(outs):
            copies.append(
                (
                    shares.at[j, :, at * width : (at + 1) * width],
                    out.at[:, j * width : (j + 1) * width],
                )
            )
    run_copies(copies, sems)


def spread(shares, count):
    size, rows, cols = shares.shape
    width = cols // count
    return pl.pallas_call(
        functools.partial(spread_body, size, width),
        out_shape=[jax.ShapeDtypeStruct((rows, width * size), BF16)] * count,
        in_specs=[ANY],
        out_specs=[ANY] * count,
        scratch_shapes=[pltpu.SemaphoreType.DMA((size * count,))],
        compiler_params=SMALL,
        name="spread",
    )(shares)


def dot(a, b):
    return lax.dot_general(a, b, (((1,), (0,)), ((), ())), preferred_element_type=F32)


def dot_t(a, b):
    return lax.dot_general(a, b, (((1,), (1,)), ((), ())), preferred_element_type=F32)


def fold(x, op):
    parts = [x[at : at + 8] for at in range(0, x.shape[0], 8)]
    while len(parts) > 1:
        parts = [
            op(*parts[at : at + 2]) if at + 1 < len(parts) else parts[at]
            for at in range(0, len(parts), 2)
        ]
    return parts[0]


def attend_body(reach, tok, group, *refs):
    low, qg, kvs = refs[0], refs[1], refs[2 : 3 + reach]
    og, dkv0, sent = refs[3 + reach], refs[4 + reach], refs[5 + reach : 5 + 2 * reach]
    kt, vt, dk, dv, s_scr, e_scr, ds_scr = refs[5 + 2 * reach :]
    width = group * HEAD_DIM
    span = WINDOW + TILE
    dk[...] = jnp.zeros_like(dk)
    dv[...] = jnp.zeros_like(dv)
    lane = lax.broadcasted_iota(jnp.int32, (TILE, HEAD_DIM), 1)
    ones = jnp.where(lane < 2, 1.0, 0.0).astype(BF16)
    wide_lane = lax.broadcasted_iota(jnp.int32, (group * TILE, HEAD_DIM), 1)
    row_of = lax.broadcasted_iota(jnp.int32, (TILE, group * TILE), 0)
    col_of = lax.broadcasted_iota(jnp.int32, (TILE, TILE), 1)
    causal = lax.broadcasted_iota(jnp.int32, (TILE, TILE), 0) <= col_of
    causal = jnp.concatenate([causal] * group, axis=1)

    def rows(start, first):
        lag = reach - start // tok
        at = start % tok
        return kvs[lag][at : at + TILE, first * HEAD_DIM : (first + 1) * HEAD_DIM]

    for lag in range(reach + 1):
        there = slice((reach - lag) * tok, (reach - lag + 1) * tok)
        kt[:, there] = kvs[lag][:, :HEAD_DIM].T
        vt[:, there] = kvs[lag][:, HEAD_DIM:].T
    for tile in range(tok // TILE):
        base = tile * TILE
        here = slice(base, base + TILE)
        q2 = jnp.concatenate(
            [qg[here, at * HEAD_DIM : (at + 1) * HEAD_DIM] for at in range(group)], axis=0
        )
        g2 = jnp.concatenate(
            [qg[here, width + at * HEAD_DIM : width + (at + 1) * HEAD_DIM] for at in range(group)],
            axis=0,
        )
        low_row = jnp.concatenate([low[:, here]] * group, axis=1) - base
        top = None
        for at in range(0, span, TILE):
            s = dot_t(rows(base + at, 0), q2)
            keep = row_of >= low_row - at
            if at == span - TILE:
                keep = keep & causal
            s = jnp.where(keep, s, -1e30)
            s_scr[at : at + TILE, :] = s
            part = fold(s, jnp.maximum)
            top = part if top is None else jnp.maximum(top, part)
        top = jnp.max(top, axis=0, keepdims=True) * exp2_scale
        total = None
        for at in range(0, span, TILE):
            e = jnp.exp2(s_scr[at : at + TILE, :] * exp2_scale - top)
            e_scr[at : at + TILE, :] = e.astype(BF16)
            part = fold(e, jnp.add)
            total = part if total is None else total + part
        inv = 1.0 / jnp.sum(total, axis=0, keepdims=True)
        inv = jnp.broadcast_to(inv, (HEAD_DIM, group * TILE)).T
        out = dot(vt[:, base : base + span], e_scr[...]).T * inv
        out = out.astype(BF16)
        g2 = (g2.astype(F32) * inv).astype(BF16)
        delta = jnp.sum(g2.astype(F32) * out.astype(F32), axis=1, keepdims=True)
        high = delta.astype(BF16).astype(F32)
        extra = jnp.where(wide_lane == 0, -high, jnp.where(wide_lane == 1, high - delta, 0.0))
        g_wide = jnp.concatenate([g2, extra.astype(BF16)], axis=1)
        for at in range(0, span, TILE):
            there = slice(base + at, base + at + TILE)
            dp = dot_t(jnp.concatenate([rows(base + at, 1), ones], axis=1), g_wide)
            e = e_scr[at : at + TILE, :]
            ds = (e.astype(F32) * dp).astype(BF16)
            ds_scr[at : at + TILE, :] = ds
            dv[there, :] += dot(e, g2)
            dk[there, :] += dot(ds, q2)
        dq = (dot(kt[:, base : base + span], ds_scr[...]) * logit_scale).T.astype(BF16)
        for at in range(group):
            part = slice(at * TILE, (at + 1) * TILE)
            og[here, at * HEAD_DIM : (at + 1) * HEAD_DIM] = out[part]
            og[here, width + at * HEAD_DIM : width + (at + 1) * HEAD_DIM] = dq[part]

    dkv0[:, :HEAD_DIM] = dk[reach * tok :, :] * logit_scale
    dkv0[:, HEAD_DIM:] = dv[reach * tok :, :]
    for lag in range(1, reach + 1):
        there = slice((reach - lag) * tok, (reach - lag + 1) * tok)
        sent[lag - 1][:, :HEAD_DIM] = (dk[there, :] * logit_scale).astype(BF16)
        sent[lag - 1][:, HEAD_DIM:] = dv[there, :].astype(BF16)


def attend(low, qg, kvs):
    tok, cols = qg.shape
    width = cols // 2
    group = width // HEAD_DIM
    reach = len(kvs) - 1
    span = WINDOW + TILE
    wide = group * TILE
    keys = (reach + 1) * tok
    half = jax.ShapeDtypeStruct((tok, 2 * HEAD_DIM), BF16)
    flops = 6 * 2 * tok * group * span * HEAD_DIM
    og, dkv0, *sent = pl.pallas_call(
        functools.partial(attend_body, reach, tok, group),
        out_shape=[
            jax.ShapeDtypeStruct((tok, cols), BF16),
            jax.ShapeDtypeStruct((tok, 2 * HEAD_DIM), F32),
        ]
        + [half] * reach,
        in_specs=[VMEM] * (3 + reach),
        out_specs=[VMEM] * (2 + reach),
        scratch_shapes=[
            pltpu.VMEM((HEAD_DIM, keys), BF16),
            pltpu.VMEM((HEAD_DIM, keys), BF16),
            pltpu.VMEM((keys, HEAD_DIM), F32),
            pltpu.VMEM((keys, HEAD_DIM), F32),
            pltpu.VMEM((span, wide), F32),
            pltpu.VMEM((span, wide), BF16),
            pltpu.VMEM((span, wide), BF16),
        ],
        compiler_params=pltpu.CompilerParams(vmem_limit_bytes=32 * 1024 * 1024),
        cost_estimate=pl.CostEstimate(
            flops=flops, bytes_accessed=8 * 1024 * 1024, transcendentals=flops // 1536
        ),
        name="attend",
    )(low, qg, *kvs)
    return og, dkv0, sent


def lowest_key(segment_ids, tok, size):
    start = (flat_index() // size) * tok
    padded = jnp.concatenate([jnp.full((WINDOW,), -1, jnp.int32), segment_ids])
    keys = lax.dynamic_slice_in_dim(padded, start, WINDOW + tok, 0)
    queries = lax.dynamic_slice_in_dim(segment_ids, start, tok, 0)
    before = jnp.sum((keys[:, None] < queries[None, :]).astype(jnp.int32), axis=0)
    return jnp.maximum(before, jnp.arange(1, tok + 1, dtype=jnp.int32))[None, :]


def body(query, key, value, grad_out, segment_ids):
    size = key.shape[1] // HEAD_DIM
    rows = query.shape[0]
    tok = size * rows
    reach = WINDOW // tok
    assert reach * tok == WINDOW and device_count() % size == 0
    low = lowest_key(segment_ids, tok, size)

    kv = exchange(pack((key, value), size)).reshape(tok, -1)
    kv, qg = after(kv, pack((query, grad_out), size))
    kvs = [kv] + [shifted(kv, lag * size) for lag in range(1, reach + 1)]
    qg = exchange(qg).reshape(tok, -1)

    og, total, sent = attend(low, qg, kvs)

    for lag in range(1, reach + 1):
        total = total + shifted(sent[lag - 1], -lag * size).astype(F32)
    og = exchange(og.reshape(size, rows, -1))
    grads = exchange(total.astype(BF16).reshape(size, rows, -1))
    attn_out, grad_query = spread(og, 2)
    grad_key, grad_value = spread(grads, 2)
    return (attn_out, grad_query, grad_key, grad_value)


def solution(mesh):
    placed = P(("pipe", "tensor"), None)
    return jax.shard_map(
        body,
        mesh=mesh,
        in_specs=(placed, placed, placed, placed, P()),
        out_specs=(placed, placed, placed, placed),
        check_vma=False,
    )
```

time: 94.7 us -> 90.6 us (0.957)
  starting transfers between devices: 34.5 us -> 21.5 us
  waiting for transfers between devices: 35.7 us -> 42.6 us
  other arithmetic: 0.73 us -> 1.93 us
    ppermute x27 -> x2, starting transfers between devices: 34.5 us -> 4.82 us  [shifted(): return lax.ppermute(value, BOTH, pairs)]
    all_to_all x0 -> x4, starting transfers between devices: none -> 16.7 us  [exchange(): lax.all_to_all(value, BOTH, split_axis=0, concat_axis=0, axis_index_group...]
    all_to_all x0 -> x4, waiting for transfers between devices: none -> 16.3 us  [exchange(): lax.all_to_all(value, BOTH, split_axis=0, concat_axis=0, axis_index_group...]
    ppermute x27 -> x2, waiting for transfers between devices: 35.7 us -> 26.3 us  [shifted(): return lax.ppermute(value, BOTH, pairs)]
    unnamed x10 -> x14, local copies, waits for them, and re-layouts: 1.96 us -> 2.79 us
    pallas_call x8 -> x5, Pallas kernels: 20.3 us -> 20.5 us  [the longest x1 16.4 us: attend(): pl.pallas_call(functools.partial(attend_body, reach, tok, group), out_sha...]
  transfers between devices with their start and end apart: 27 -> 6, of which waited for: 11 -> 4; matrix products, arithmetic and copies ran while one was open for 1% -> 2% of each run, Pallas kernels for 20% -> 2%
where the time goes in v4:
time: 90.6 us; the launch traced here: 90.1 us
  waiting for transfers between devices  42.6 us (47%)
  starting transfers between devices  21.5 us (24%)
  Pallas kernels  20.5 us (23%)
  local copies, waits for them, and re-layouts  2.81 us (3%)
  other arithmetic  1.93 us (2%)
    ppermute x2, waiting for transfers between devices, shifted(): return lax.ppermute(value, BOTH, pairs)  26.3 us
    all_to_all x4, starting transfers between devices, exchange(): lax.all_to_all(value, BOTH, split_axis=0, concat_axis=0, axis_index_group...  16.7 us
    pallas_call x1, Pallas kernels, attend(): pl.pallas_call(functools.partial(attend_body, reach, tok, group), out_sha...  16.4 us
    all_to_all x4, waiting for transfers between devices, exchange(): lax.all_to_all(value, BOTH, split_axis=0, concat_axis=0, axis_index_group...  16.3 us
    ppermute x2, starting transfers between devices, shifted(): return lax.ppermute(value, BOTH, pairs)  4.82 us
    unnamed x14, local copies, waits for them, and re-layouts  2.79 us
    pallas_call x2, Pallas kernels, pack(): pl.pallas_call(functools.partial(pack_body, size, widths), out_shape=jax....  2.05 us
    pallas_call x2, Pallas kernels, spread(): pl.pallas_call(functools.partial(spread_body, size, width), out_shape=[ja...  2 us
  transfers between devices with their start and end apart: 6, of which 4 were waited for; matrix products, arithmetic and copies ran while one was open for 2% of the time, Pallas kernels for 2%

profile of v4, /device:TPU:0, one launch (start us, length us, event | category | flops | bytes accessed | tf_op | source)
XLA Modules:
  0.0 90.1 jit_solution(15817225909113340539)
XLA Ops:
  0.6 0.0 copy-start.1
  0.6 0.0 copy-start
  0.7 0.0 copy-start.2
  0.7 1.0 %copy-done.2 = bf16[128,1024]{1,0:T(8,128)(2,1)S(1)} copy-done((bf16[128,1024]{1,0:T(8,128)(2,1)S(1)}, bf16[128,1024]{1,0:T(8,128)(2,1)}, u32[]{:S(2)}) %copy-start.2) | copy-done | bytes 262168
  1.7 0.0 copy-start.3
  1.7 0.9 %copy-done.3 = bf16[128,1024]{1,0:T(8,128)(2,1)S(1)} copy-done((bf16[128,1024]{1,0:T(8,128)(2,1)S(1)}, bf16[128,1024]{1,0:T(8,128)(2,1)}, u32[]{:S(2)}) %copy-start.3) | copy-done | bytes 262168
  2.6 0.9 %pack.2 = bf16[8,128,256]{2,1,0:T(8,128)(2,1)} custom-call(bf16[128,1024]{1,0:T(8,128)(2,1)S(1)} %copy-done.2, bf16[128,1024]{1,0:T(8,128)(2,1)S(1)} %copy-done.3), custom_call_target="tpu_custom_call" | custom-call | tf_op jit(solution)/shard_map/pack/pallas_call | solution.py:80
  3.6 5.2 %all-to-all-start = ((bf16[8,128,256]{2,1,0:T(8,128)(2,1)}), bf16[8,128,256]{2,1,0:T(8,128)(2,1)S(1)}, u32[]{:S(2)}, u32[]{:S(2)}) async-start(bf16[8,128,256]{2,1,0:T(8,128)(2,1)} %pack.2), calls=%async_computation | async-start | bytes 1048576 | tf_op jit(solution)/shard_map/all_to_all | solution.py:36
  8.7 0.0 copy-done.1
  8.7 0.0 copy-done
  8.8 1.1 %pack.3 = bf16[8,128,512]{2,1,0:T(8,128)(2,1)} custom-call(bf16[128,2048]{1,0:T(8,128)(2,1)S(1)} %copy-done, bf16[128,2048]{1,0:T(8,128)(2,1)S(1)} %copy-done.1), custom_call_target="tpu_custom_call" | custom-call | tf_op jit(solution)/shard_map/pack/pallas_call | solution.py:80
  9.9 8.1 %all-to-all-done = bf16[8,128,256]{2,1,0:T(8,128)(2,1)S(1)} async-done(((bf16[8,128,256]{2,1,0:T(8,128)(2,1)}), bf16[8,128,256]{2,1,0:T(8,128)(2,1)S(1)}, u32[]{:S(2)}, u32[]{:S(2)}) %all-to-all-start) | async-done | bytes 524320 | tf_op jit(solution)/shard_map/all_to_all | solution.py:36
  18.0 0.0 copy-start.6
  18.0 3.7 %all-to-all-start.1 = ((bf16[8,128,512]{2,1,0:T(8,128)(2,1)}), bf16[8,128,512]{2,1,0:T(8,128)(2,1)S(1)}, u32[]{:S(2)}, u32[]{:S(2)}) async-start(bf16[8,128,512]{2,1,0:T(8,128)(2,1)} %pack.3), calls=%async_computation.1 | async-start | bytes 2097152 | tf_op jit(solution)/shard_map/all_to_all | solution.py:36
  21.7 0.0 copy-done.6
  21.8 3.5 %collective-permute-start = (bf16[1024,256]{1,0:T(8,128)(2,1)S(1)}, bf16[1024,256]{1,0:T(8,128)(2,1)S(1)}, u32[]{:S(2)}, u32[]{:S(2)}) collective-permute-start(bf16[1024,256]{1,0:T(8,128)(2,1)S(1)} %bitcast.6), channel_id=1, source_target_pairs={{0,8},{1,9},{2,10},{3,11},{4,12},{5,13},{6,14},{7,15},{8,16},{9,17... | collective-permute-start | bytes 1572872 | tf_op jit(solution)/shard_map/ppermute | solution.py:44
  25.3 1.0 %convert_reduce_fusion = s32[1024]{0:T(1024)S(1)} fusion(s32[1024]{0:T(1024)S(1)} %dynamic_slice.7, s32[2048]{0:T(1024)S(1)} %pad_dynamic-slice_fusion), kind=kLoop, calls=%fused_computation | loop fusion | flops 6290432 | bytes 16384 | tf_op jit(solution)/shard_map/reduce_sum | solution.py:263
  26.3 10.6 %collective-permute-done.refs_3_ = bf16[1024,256]{1,0:T(8,128)(2,1)S(1)} collective-permute-done((bf16[1024,256]{1,0:T(8,128)(2,1)S(1)}, bf16[1024,256]{1,0:T(8,128)(2,1)S(1)}, u32[]{:S(2)}, u32[]{:S(2)}) %collective-permute-start) | collective-permute-done | bytes 524320 | tf_op jit(solution)/shard_map/ppermute | solution.py:44
  36.9 0.0 all-to-all-done.1
  36.9 16.4 %attend.1 = (bf16[1024,512]{1,0:T(8,128)(2,1)}, f32[1024,256]{1,0:T(8,128)S(1)}, bf16[1024,256]{1,0:T(8,128)(2,1)S(1)}) custom-call(s32[1,1024]{1,0:T(1,128)S(1)} %add_maximum_fusion.refs_0_, bf16[1024,512]{1,0:T(8,128)(2,1)S(1)} %bitcast.5, bf16[1024,256]{1,0:T(8,128)(2,1)S(1)} %bitcast.7, bf16[1024,256]{1,0:T(8,128)(2,1)S(1)} %collective-permute-done.refs_3_), custom_call_target="tpu_custom_call" | custom-call | flops 3623878656 | bytes 8388608 | tf_op jit(solution)/shard_map/attend/pallas_call | solution.py:231
  53.4 0.0 copy-start.4
  53.4 0.8 copy-done.4
  54.2 4.0 %all-to-all-start.2 = ((bf16[8,128,512]{2,1,0:T(8,128)(2,1)}), bf16[8,128,512]{2,1,0:T(8,128)(2,1)S(1)}, u32[]{:S(2)}, u32[]{:S(2)}) async-start(bf16[8,128,512]{2,1,0:T(8,128)(2,1)} %bitcast.3), calls=%async_computation.2 | async-start | bytes 2097152 | tf_op jit(solution)/shard_map/all_to_all | solution.py:36
  58.2 0.0 copy-done.5
  58.2 1.3 %collective-permute-start.1 = (bf16[1024,256]{1,0:T(8,128)(2,1)S(1)}, bf16[1024,256]{1,0:T(8,128)(2,1)S(1)}, u32[]{:S(2)}, u32[]{:S(2)}) collective-permute-start(bf16[1024,256]{1,0:T(8,128)(2,1)S(1)} %copy-done.5), channel_id=1, source_target_pairs={{8,0},{9,1},{10,2},{11,3},{12,4},{13,5},{14,6},{15,7},{16,8},{17,9... | collective-permute-start | bytes 1572872 | tf_op jit(solution)/shard_map/ppermute | solution.py:44
  59.5 15.7 %collective-permute-done.1 = bf16[1024,256]{1,0:T(8,128)(2,1)S(1)} collective-permute-done((bf16[1024,256]{1,0:T(8,128)(2,1)S(1)}, bf16[1024,256]{1,0:T(8,128)(2,1)S(1)}, u32[]{:S(2)}, u32[]{:S(2)}) %collective-permute-start.1) | collective-permute-done | bytes 524320 | tf_op jit(solution)/shard_map/ppermute | solution.py:44
  75.1 0.9 %add_convert_fusion = bf16[1024,256]{1,0:T(8,128)(2,1)} fusion(f32[1024,256]{1,0:T(8,128)S(1)} %get-tuple-element.18, bf16[1024,256]{1,0:T(8,128)(2,1)S(1)} %collective-permute-done.1), kind=kLoop, calls=%fused_computation.1 | loop fusion | flops 786432 | bytes 2097152 | tf_op jit(solution)/shard_map/convert_element_type | solution.py:285
  76.1 0.0 all-to-all-done.2.shares
  76.1 3.8 %all-to-all-start.3 = ((bf16[8,128,256]{2,1,0:T(8,128)(2,1)}), bf16[8,128,256]{2,1,0:T(8,128)(2,1)S(1)}, u32[]{:S(2)}, u32[]{:S(2)}) async-start(bf16[8,128,256]{2,1,0:T(8,128)(2,1)} %bitcast.4), calls=%async_computation.3 | async-start | bytes 1048576 | tf_op jit(solution)/shard_map/all_to_all | solution.py:36
  79.9 1.1 %spread.2 = (bf16[128,2048]{1,0:T(8,128)(2,1)}, bf16[128,2048]{1,0:T(8,128)(2,1)}) custom-call(bf16[8,128,512]{2,1,0:T(8,128)(2,1)S(1)} %all-to-all-done.2.shares), custom_call_target="tpu_custom_call" | custom-call | tf_op jit(solution)/shard_map/spread/pallas_call | solution.py:108
  81.0 8.2 %all-to-all-done.3.shares = bf16[8,128,256]{2,1,0:T(8,128)(2,1)S(1)} async-done(((bf16[8,128,256]{2,1,0:T(8,128)(2,1)}), bf16[8,128,256]{2,1,0:T(8,128)(2,1)S(1)}, u32[]{:S(2)}, u32[]{:S(2)}) %all-to-all-start.3) | async-done | bytes 524320 | tf_op jit(solution)/shard_map/all_to_all | solution.py:36
  89.2 0.9 %spread.3 = (bf16[128,1024]{1,0:T(8,128)(2,1)}, bf16[128,1024]{1,0:T(8,128)(2,1)}) custom-call(bf16[8,128,256]{2,1,0:T(8,128)(2,1)S(1)} %all-to-all-done.3.shares), custom_call_target="tpu_custom_call" | custom-call | tf_op jit(solution)/shard_map/spread/pallas_call | solution.py:108
  (4 shorter events, 0.0 us)
Async XLA Ops:
  0.6 8.1 %copy-start.1 = (bf16[128,2048]{1,0:T(8,128)(2,1)S(1)}, bf16[128,2048]{1,0:T(8,128)(2,1)}, u32[]{:S(2)}) copy-start(bf16[128,2048]{1,0:T(8,128)(2,1)} %refs_1_.3) | copy-start | bytes 1572868
  0.6 8.1 %copy-start = (bf16[128,2048]{1,0:T(8,128)(2,1)S(1)}, bf16[128,2048]{1,0:T(8,128)(2,1)}, u32[]{:S(2)}) copy-start(bf16[128,2048]{1,0:T(8,128)(2,1)} %refs_0_.3) | copy-start | bytes 1572868
  0.7 1.0 %copy-start.2 = (bf16[128,1024]{1,0:T(8,128)(2,1)S(1)}, bf16[128,1024]{1,0:T(8,128)(2,1)}, u32[]{:S(2)}) copy-start(bf16[128,1024]{1,0:T(8,128)(2,1)} %refs_0_.2) | copy-start | bytes 786436
  1.7 0.9 %copy-start.3 = (bf16[128,1024]{1,0:T(8,128)(2,1)S(1)}, bf16[128,1024]{1,0:T(8,128)(2,1)}, u32[]{:S(2)}) copy-start(bf16[128,1024]{1,0:T(8,128)(2,1)} %refs_1_.2) | copy-start | bytes 786436
  3.6 14.4 %all-to-all-start = ((bf16[8,128,256]{2,1,0:T(8,128)(2,1)}), bf16[8,128,256]{2,1,0:T(8,128)(2,1)S(1)}, u32[]{:S(2)}, u32[]{:S(2)}) async-start(bf16[8,128,256]{2,1,0:T(8,128)(2,1)} %pack.2), calls=%async_computation | async-start | bytes 1048576 | tf_op jit(solution)/shard_map/all_to_all | solution.py:36
  18.0 3.7 %copy-start.6 = (s32[4096]{0:T(1024)S(1)}, s32[4096]{0:T(1024)}, u32[]{:S(2)}) copy-start(s32[4096]{0:T(1024)} %param.9) | copy-start | bytes 49156
  18.0 18.9 %all-to-all-start.1 = ((bf16[8,128,512]{2,1,0:T(8,128)(2,1)}), bf16[8,128,512]{2,1,0:T(8,128)(2,1)S(1)}, u32[]{:S(2)}, u32[]{:S(2)}) async-start(bf16[8,128,512]{2,1,0:T(8,128)(2,1)} %pack.3), calls=%async_computation.1 | async-start | bytes 2097152 | tf_op jit(solution)/shard_map/all_to_all | solution.py:36
  21.8 15.2 %collective-permute-start = (bf16[1024,256]{1,0:T(8,128)(2,1)S(1)}, bf16[1024,256]{1,0:T(8,128)(2,1)S(1)}, u32[]{:S(2)}, u32[]{:S(2)}) collective-permute-start(bf16[1024,256]{1,0:T(8,128)(2,1)S(1)} %bitcast.6), channel_id=1, source_target_pairs={{0,8},{1,9},{2,10},{3,11},{4,12},{5,13},{6,14},{7,15},{8,16},{9,17... | collective-permute-start | bytes 1572872 | tf_op jit(solution)/shard_map/ppermute | solution.py:44
  53.4 0.8 copy-start.4
  54.2 4.0 %copy-start.5 = (bf16[1024,256]{1,0:T(8,128)(2,1)S(1)}, bf16[1024,256]{1,0:T(8,128)(2,1)}, u32[]{:S(2)}) copy-start(bf16[1024,256]{1,0:T(8,128)(2,1)} %copy-done.4) | copy-start | bytes 1572868
  54.2 21.9 %all-to-all-start.2 = ((bf16[8,128,512]{2,1,0:T(8,128)(2,1)}), bf16[8,128,512]{2,1,0:T(8,128)(2,1)S(1)}, u32[]{:S(2)}, u32[]{:S(2)}) async-start(bf16[8,128,512]{2,1,0:T(8,128)(2,1)} %bitcast.3), calls=%async_computation.2 | async-start | bytes 2097152 | tf_op jit(solution)/shard_map/all_to_all | solution.py:36
  58.2 17.0 %collective-permute-start.1 = (bf16[1024,256]{1,0:T(8,128)(2,1)S(1)}, bf16[1024,256]{1,0:T(8,128)(2,1)S(1)}, u32[]{:S(2)}, u32[]{:S(2)}) collective-permute-start(bf16[1024,256]{1,0:T(8,128)(2,1)S(1)} %copy-done.5), channel_id=1, source_target_pairs={{8,0},{9,1},{10,2},{11,3},{12,4},{13,5},{14,6},{15,7},{16,8},{17,9... | collective-permute-start | bytes 1572872 | tf_op jit(solution)/shard_map/ppermute | solution.py:44
  76.1 13.1 %all-to-all-start.3 = ((bf16[8,128,256]{2,1,0:T(8,128)(2,1)}), bf16[8,128,256]{2,1,0:T(8,128)(2,1)S(1)}, u32[]{:S(2)}, u32[]{:S(2)}) async-start(bf16[8,128,256]{2,1,0:T(8,128)(2,1)} %bitcast.4), calls=%async_computation.3 | async-start | bytes 1048576 | tf_op jit(solution)/shard_map/all_to_all | solution.py:36

commit v5 on v4

--- a/solution.py
+++ b/solution.py
@@ -30,12 +30,20 @@
     return lax.axis_size("pipe") * lax.axis_size("tensor")
 
 
-def exchange(value):
-    size = value.shape[0]
-    groups = [[at + i for i in range(size)] for at in range(0, device_count(), size)]
-    return lax.all_to_all(
-        value, BOTH, split_axis=0, concat_axis=0, axis_index_groups=groups, tiled=True
-    )
+def exchange(pieces):
+    count = device_count()
+    return [pieces[0]] + [
+        lax.ppermute(pieces[j], BOTH, [(i, i ^ j) for i in range(count)])
+        for j in range(1, len(pieces))
+    ]
+
+
+def partner(size, j):
+    return lax.bitwise_xor(lax.rem(flat_index(), size), j)
+
+
+def place(index, width):
+    return pl.ds(pl.multiple_of(index * width, width), width)
 
 
 def shifted(value, step):
@@ -59,19 +67,12 @@
 
 
 def pack_body(size, widths, *refs):
-    arrays, out, sems = refs[: len(widths)], refs[-2], refs[-1]
-    copies = []
-    for j in range(size):
+    arrays, pieces = refs[: len(widths)], refs[len(widths) :]
+    for j, piece in enumerate(pieces):
         start = 0
         for array, width in zip(arrays, widths):
-            copies.append(
-                (
-                    array.at[:, j * width : (j + 1) * width],
-                    out.at[j, :, start : start + width],
-                )
-            )
+            piece[:, start : start + width] = array[:, place(partner(size, j), width)]
             start += width
-    run_copies(copies, sems)
 
 
 def pack(arrays, size):
@@ -79,41 +80,80 @@
     widths = [array.shape[1] // size for array in arrays]
     return pl.pallas_call(
         functools.partial(pack_body, size, widths),
-        out_shape=jax.ShapeDtypeStruct((size, rows, sum(widths)), BF16),
-        in_specs=[ANY] * len(arrays),
-        out_specs=ANY,
-        scratch_shapes=[pltpu.SemaphoreType.DMA((size * len(arrays),))],
+        out_shape=[jax.ShapeDtypeStruct((rows, sum(widths)), BF16)] * size,
+        in_specs=[VMEM] * len(arrays),
+        out_specs=[VMEM] * size,
         compiler_params=SMALL,
         name="pack",
     )(*arrays)
 
 
-def spread_body(size, width, shares, *refs):
-    outs, sems = refs[:-1], refs[-1]
+def join_body(size, *refs):
+    pieces, out = refs[:size], refs[size]
+    for j, piece in enumerate(pieces):
+        out[place(partner(size, j), piece.shape[0]), :] = piece[...]
+
+
+def join(pieces):
+    size, (rows, cols) = len(pieces), pieces[0].shape
+    return pl.pallas_call(
+        functools.partial(join_body, size),
+        out_shape=jax.ShapeDtypeStruct((size * rows, cols), BF16),
+        in_specs=[VMEM] * size,
+        out_specs=VMEM,
+        compiler_params=SMALL,
+        name="join",
+    )(*pieces)
+
+
+def combine_body(terms, *refs):
+    added, pieces = refs[:terms], refs[terms:]
+    for j, piece in enumerate(pieces):
+        there = place(partner(len(pieces), j), piece.shape[0])
+        total = added[0][there, :]
+        for term in added[1:]:
+            total = total + term[there, :].astype(F32)
+        piece[...] = total.astype(BF16)
+
+
+def combine(terms, size):
+    tok, cols = terms[0].shape
+    return pl.pallas_call(
+        functools.partial(combine_body, len(terms)),
+        out_shape=[jax.ShapeDtypeStruct((tok // size, cols), BF16)] * size,
+        in_specs=[VMEM] * len(terms),
+        out_specs=[VMEM] * size,
+        compiler_params=SMALL,
+        name="combine",
+    )(*terms)
+
+
+def spread_body(size, width, *refs):
+    pieces, outs, sems = refs[:size], refs[size:-1], refs[-1]
     copies = []
-    for j in range(size):
+    for j, piece in enumerate(pieces):
         for at, out in enumerate(outs):
             copies.append(
                 (
-                    shares.at[j, :, at * width : (at + 1) * width],
-                    out.at[:, j * width : (j + 1) * width],
+                    piece.at[:, at * width : (at + 1) * width],
+                    out.at[:, place(partner(size, j), width)],
                 )
             )
     run_copies(copies, sems)
 
 
-def spread(shares, count):
-    size, rows, cols = shares.shape
+def spread(pieces, count):
+    size, (rows, cols) = len(pieces), pieces[0].shape
     width = cols // count
     return pl.pallas_call(
         functools.partial(spread_body, size, width),
         out_shape=[jax.ShapeDtypeStruct((rows, width * size), BF16)] * count,
-        in_specs=[ANY],
+        in_specs=[ANY] * size,
         out_specs=[ANY] * count,
         scratch_shapes=[pltpu.SemaphoreType.DMA((size * count,))],
         compiler_params=SMALL,
         name="spread",
-    )(shares)
+    )(*pieces)
 
 
 def dot(a, b):
@@ -134,10 +174,14 @@
     return parts[0]
 
 
-def attend_body(reach, tok, group, *refs):
-    low, qg, kvs = refs[0], refs[1], refs[2 : 3 + reach]
-    og, dkv0, sent = refs[3 + reach], refs[4 + reach], refs[5 + reach : 5 + 2 * reach]
-    kt, vt, dk, dv, s_scr, e_scr, ds_scr = refs[5 + 2 * reach :]
+def attend_body(size, reach, tok, group, *refs):
+    refs = list(refs)
+    take = lambda count: [refs.pop(0) for _ in range(count)]
+    (low,), qg_pieces, kvs = take(1), take(size), take(1 + reach)
+    og_pieces, (dkv0,), sent = take(size), take(1), take(reach)
+    qg, og, kt, vt, dk, dv, s_scr, e_scr, ds_scr = refs
+    for j, piece in enumerate(qg_pieces):
+        qg[place(partner(size, j), piece.shape[0]), :] = piece[...]
     width = group * HEAD_DIM
     span = WINDOW + TILE
     dk[...] = jnp.zeros_like(dk)
@@ -216,10 +260,13 @@
         there = slice((reach - lag) * tok, (reach - lag + 1) * tok)
         sent[lag - 1][:, :HEAD_DIM] = (dk[there, :] * logit_scale).astype(BF16)
         sent[lag - 1][:, HEAD_DIM:] = dv[there, :].astype(BF16)
+    for j, piece in enumerate(og_pieces):
+        piece[...] = og[place(partner(size, j), piece.shape[0]), :]
 
 
 def attend(low, qg, kvs):
-    tok, cols = qg.shape
+    size, (rows, cols) = len(qg), qg[0].shape
+    tok = size * rows
     width = cols // 2
     group = width // HEAD_DIM
     reach = len(kvs) - 1
@@ -228,16 +275,16 @@
     keys = (reach + 1) * tok
     half = jax.ShapeDtypeStruct((tok, 2 * HEAD_DIM), BF16)
     flops = 6 * 2 * tok * group * span * HEAD_DIM
-    og, dkv0, *sent = pl.pallas_call(
-        functools.partial(attend_body, reach, tok, group),
-        out_shape=[
-            jax.ShapeDtypeStruct((tok, cols), BF16),
-            jax.ShapeDtypeStruct((tok, 2 * HEAD_DIM), F32),
-        ]
+    results = pl.pallas_call(
+        functools.partial(attend_body, size, reach, tok, group),
+        out_shape=[jax.ShapeDtypeStruct((rows, cols), BF16)] * size
+        + [jax.ShapeDtypeStruct((tok, 2 * HEAD_DIM), F32)]
         + [half] * reach,
-        in_specs=[VMEM] * (3 + reach),
-        out_specs=[VMEM] * (2 + reach),
+        in_specs=[VMEM] * (size + 2 + reach),
+        out_specs=[VMEM] * (size + 1 + reach),
         scratch_shapes=[
+            pltpu.VMEM((tok, cols), BF16),
+            pltpu.VMEM((tok, cols), BF16),
             pltpu.VMEM((HEAD_DIM, keys), BF16),
             pltpu.VMEM((HEAD_DIM, keys), BF16),
             pltpu.VMEM((keys, HEAD_DIM), F32),
@@ -251,8 +298,8 @@
             flops=flops, bytes_accessed=8 * 1024 * 1024, transcendentals=flops // 1536
         ),
         name="attend",
-    )(low, qg, *kvs)
-    return og, dkv0, sent
+    )(low, *qg, *kvs)
+    return results[:size], results[size], results[size + 1 :]
 
 
 def lowest_key(segment_ids, tok, size):
@@ -272,17 +319,16 @@
     assert reach * tok == WINDOW and device_count() % size == 0
     low = lowest_key(segment_ids, tok, size)
 
-    kv = exchange(pack((key, value), size)).reshape(tok, -1)
-    kv, qg = after(kv, pack((query, grad_out), size))
+    kv = join(exchange(pack((key, value), size)))
+    kv, *qg = after(kv, *pack((query, grad_out), size))
     kvs = [kv] + [shifted(kv, lag * size) for lag in range(1, reach + 1)]
-    qg = exchange(qg).reshape(tok, -1)
-
-    og, total, sent = attend(low, qg, kvs)
-
-    for lag in range(1, reach + 1):
-        total = total + shifted(sent[lag - 1], -lag * size).astype(F32)
-    og = exchange(og.reshape(size, rows, -1))
-    grads = exchange(total.astype(BF16).reshape(size, rows, -1))
+    qg = exchange(qg)
+
+    og, dkv, sent = attend(low, qg, kvs)
+
+    back = [shifted(sent[lag - 1], -lag * size) for lag in range(1, reach + 1)]
+    og = exchange(og)
+    grads = exchange(combine([dkv] + back, size))
     attn_out, grad_query = spread(og, 2)
     grad_key, grad_value = spread(grads, 2)
     return (attn_out, grad_query, grad_key, grad_value)

time: 90.6 us -> 83.4 us (0.921)
  waiting for transfers between devices: 42.6 us -> 25.9 us
  starting transfers between devices: 21.5 us -> 33.1 us
  Pallas kernels: 20.5 us -> 18.1 us
  local copies, waits for them, and re-layouts: 2.81 us -> 3.99 us
  other arithmetic: 1.93 us -> 0.98 us
    ppermute x0 -> x28, starting transfers between devices: none -> 28.3 us  [exchange(): lax.ppermute(pieces[j], BOTH, [(i, i ^ j) for i in range(count)])]
    ppermute x2, waiting for transfers between devices: 26.3 us -> 6.01 us  [shifted(): return lax.ppermute(value, BOTH, pairs)]
    ppermute x0 -> x28, waiting for transfers between devices: none -> 19.8 us  [exchange(): lax.ppermute(pieces[j], BOTH, [(i, i ^ j) for i in range(count)])]
    all_to_all x4 -> x0, starting transfers between devices: 16.7 us -> none  [exchange(): lax.all_to_all(value, BOTH, split_axis=0, concat_axis=0, axis_index_group...]
    all_to_all x4 -> x0, waiting for transfers between devices: 16.3 us -> none  [exchange(): lax.all_to_all(value, BOTH, split_axis=0, concat_axis=0, axis_index_group...]
    pallas_call x3 -> x5, Pallas kernels: 18.5 us -> 16.1 us  [the longest x1 15.7 us: attend(): pl.pallas_call(functools.partial(attend_body, size, reach, tok, group), o...]
    unnamed x14 -> x10, local copies, waits for them, and re-layouts: 2.79 us -> 3.98 us
    convert_element_type x1 -> x0, other arithmetic: 0.94 us -> none  [body(): grads = exchange(total.astype(BF16).reshape(size, rows, -1))]
  transfers between devices with their start and end apart: 6 -> 30, of which waited for: 4 -> 10; matrix products, arithmetic and copies ran while one was open for 2% -> 1% of each run, Pallas kernels for 2% -> 2%
where the time goes in v5:
time: 83.4 us; the launch traced here: 83.1 us
  starting transfers between devices  33.1 us (40%)
  waiting for transfers between devices  25.9 us (31%)
  Pallas kernels  18.1 us (22%)
  local copies, waits for them, and re-layouts  3.99 us (5%)
  other arithmetic  0.98 us (1%)
  between operations  0.96 us (1%)
    ppermute x28, starting transfers between devices, exchange(): lax.ppermute(pieces[j], BOTH, [(i, i ^ j) for i in range(count)])  28.3 us
    ppermute x28, waiting for transfers between devices, exchange(): lax.ppermute(pieces[j], BOTH, [(i, i ^ j) for i in range(count)])  19.8 us
    pallas_call x1, Pallas kernels, attend(): pl.pallas_call(functools.partial(attend_body, size, reach, tok, group), o...  15.7 us
    ppermute x2, waiting for transfers between devices, shifted(): return lax.ppermute(value, BOTH, pairs)  6.01 us
    ppermute x2, starting transfers between devices, shifted(): return lax.ppermute(value, BOTH, pairs)  4.84 us
    unnamed x10, local copies, waits for them, and re-layouts  3.98 us
    pallas_call x2, Pallas kernels, spread(): pl.pallas_call(functools.partial(spread_body, size, width), out_shape=[ja...  2 us
  transfers between devices with their start and end apart: 30, of which 10 were waited for; matrix products, arithmetic and copies ran while one was open for 1% of the time, Pallas kernels for 2%

profile of v5, /device:TPU:0, one launch (start us, length us, event | category | flops | bytes accessed | tf_op | source)
XLA Modules:
  0.0 83.1 jit_solution(13219366710976636067)
XLA Ops:
  1.6 0.9 %copy-done.3 = bf16[128,1024]{1,0:T(8,128)(2,1)S(1)} copy-done((bf16[128,1024]{1,0:T(8,128)(2,1)S(1)}, bf16[128,1024]{1,0:T(8,128)(2,1)}, u32[]{:S(2)}) %copy-start.3) | copy-done | bytes 262168
  2.7 3.0 %collective-permute-start = (bf16[128,256]{1,0:T(8,128)(2,1)S(1)}, bf16[128,256]{1,0:T(8,128)(2,1)S(1)}, u32[]{:S(2)}, u32[]{:S(2)}) collective-permute-start(bf16[128,256]{1,0:T(8,128)(2,1)S(1)} %get-tuple-element.52), channel_id=1, source_target_pairs={{0,1},{1,0},{2,3},{3,2},{4,5},{5,4},{6,7},{7,6},{8,9},{9,8},{10,11... | collective-permute-start | bytes 196616 | tf_op jit(solution)/shard_map/ppermute | solution.py:36
  5.9 2.0 %collective-permute-start.3 = (bf16[128,256]{1,0:T(8,128)(2,1)S(1)}, bf16[128,256]{1,0:T(8,128)(2,1)S(1)}, u32[]{:S(2)}, u32[]{:S(2)}) collective-permute-start(bf16[128,256]{1,0:T(8,128)(2,1)S(1)} %get-tuple-element.55), channel_id=1, source_target_pairs={{0,4},{1,5},{2,6},{3,7},{4,0},{5,1},{6,2},{7,3},{8,12},{9,13},{10,... | collective-permute-start | bytes 196616 | tf_op jit(solution)/shard_map/ppermute | solution.py:36
  7.8 1.4 %collective-permute-start.4 = (bf16[128,256]{1,0:T(8,128)(2,1)S(1)}, bf16[128,256]{1,0:T(8,128)(2,1)S(1)}, u32[]{:S(2)}, u32[]{:S(2)}) collective-permute-start(bf16[128,256]{1,0:T(8,128)(2,1)S(1)} %get-tuple-element.56), channel_id=1, source_target_pairs={{0,5},{1,4},{2,7},{3,6},{4,1},{5,0},{6,3},{7,2},{8,13},{9,12},{10,... | collective-permute-start | bytes 196616 | tf_op jit(solution)/shard_map/ppermute | solution.py:36
  9.9 1.8 %collective-permute-start.6 = (bf16[128,256]{1,0:T(8,128)(2,1)S(1)}, bf16[128,256]{1,0:T(8,128)(2,1)S(1)}, u32[]{:S(2)}, u32[]{:S(2)}) collective-permute-start(bf16[128,256]{1,0:T(8,128)(2,1)S(1)} %get-tuple-element.58), channel_id=1, source_target_pairs={{0,7},{1,6},{2,5},{3,4},{4,3},{5,2},{6,1},{7,0},{8,15},{9,14},{10,... | collective-permute-start | bytes 196616 | tf_op jit(solution)/shard_map/ppermute | solution.py:36
  11.7 1.0 %copy-done = bf16[128,2048]{1,0:T(8,128)(2,1)S(1)} copy-done((bf16[128,2048]{1,0:T(8,128)(2,1)S(1)}, bf16[128,2048]{1,0:T(8,128)(2,1)}, u32[]{:S(2)}) %copy-start) | copy-done | bytes 524312
  12.7 1.0 %copy-done.1 = bf16[128,2048]{1,0:T(8,128)(2,1)S(1)} copy-done((bf16[128,2048]{1,0:T(8,128)(2,1)S(1)}, bf16[128,2048]{1,0:T(8,128)(2,1)}, u32[]{:S(2)}) %copy-start.1) | copy-done | bytes 524312
  13.9 1.3 %collective-permute-done.5.refs_6_ = bf16[128,256]{1,0:T(8,128)(2,1)S(1)} collective-permute-done((bf16[128,256]{1,0:T(8,128)(2,1)S(1)}, bf16[128,256]{1,0:T(8,128)(2,1)S(1)}, u32[]{:S(2)}, u32[]{:S(2)}) %collective-permute-start.5) | collective-permute-done | bytes 65568 | tf_op jit(solution)/shard_map/ppermute | solution.py:36
  15.3 3.5 %collective-permute-start.14 = (bf16[1024,256]{1,0:T(8,128)(2,1)S(1)}, bf16[1024,256]{1,0:T(8,128)(2,1)S(1)}, u32[]{:S(2)}, u32[]{:S(2)}) collective-permute-start(bf16[1024,256]{1,0:T(8,128)(2,1)S(1)} %join.1.refs_9_), channel_id=1, source_target_pairs={{0,8},{1,9},{2,10},{3,11},{4,12},{5,13},{6,14},{7,15},{8,16},{9,17... | collective-permute-start | bytes 1572872 | tf_op jit(solution)/shard_map/ppermute | solution.py:52
  18.9 1.2 %collective-permute-start.7 = (bf16[128,512]{1,0:T(8,128)(2,1)S(1)}, bf16[128,512]{1,0:T(8,128)(2,1)S(1)}, u32[]{:S(2)}, u32[]{:S(2)}) collective-permute-start(bf16[128,512]{1,0:T(8,128)(2,1)S(1)} %get-tuple-element.68), channel_id=1, source_target_pairs={{0,1},{1,0},{2,3},{3,2},{4,5},{5,4},{6,7},{7,6},{8,9},{9,8},{10,11... | collective-permute-start | bytes 393224 | tf_op jit(solution)/shard_map/ppermute | solution.py:36
  20.0 1.0 %collective-permute-start.9 = (bf16[128,512]{1,0:T(8,128)(2,1)S(1)}, bf16[128,512]{1,0:T(8,128)(2,1)S(1)}, u32[]{:S(2)}, u32[]{:S(2)}) collective-permute-start(bf16[128,512]{1,0:T(8,128)(2,1)S(1)} %get-tuple-element.70), channel_id=1, source_target_pairs={{0,3},{1,2},{2,1},{3,0},{4,7},{5,6},{6,5},{7,4},{8,11},{9,10},{10,... | collective-permute-start | bytes 393224 | tf_op jit(solution)/shard_map/ppermute | solution.py:36
  21.1 1.0 %convert_reduce_fusion = s32[1024]{0:T(1024)S(1)} fusion(s32[1024]{0:T(1024)S(1)} %dynamic-slice-done, s32[2048]{0:T(1024)S(1)} %pad_dynamic-slice_fusion), kind=kLoop, calls=%fused_computation | loop fusion | flops 6290432 | bytes 16384 | tf_op jit(solution)/shard_map/reduce_sum | solution.py:310
  22.0 1.1 %collective-permute-start.10 = (bf16[128,512]{1,0:T(8,128)(2,1)S(1)}, bf16[128,512]{1,0:T(8,128)(2,1)S(1)}, u32[]{:S(2)}, u32[]{:S(2)}) collective-permute-start(bf16[128,512]{1,0:T(8,128)(2,1)S(1)} %get-tuple-element.71), channel_id=1, source_target_pairs={{0,4},{1,5},{2,6},{3,7},{4,0},{5,1},{6,2},{7,3},{8,12},{9,13},{10,... | collective-permute-start | bytes 393224 | tf_op jit(solution)/shard_map/ppermute | solution.py:36
  23.2 2.1 %collective-permute-done.7.refs_2_ = bf16[128,512]{1,0:T(8,128)(2,1)S(1)} collective-permute-done((bf16[128,512]{1,0:T(8,128)(2,1)S(1)}, bf16[128,512]{1,0:T(8,128)(2,1)S(1)}, u32[]{:S(2)}, u32[]{:S(2)}) %collective-permute-start.7) | collective-permute-done | bytes 131104 | tf_op jit(solution)/shard_map/ppermute | solution.py:36
  25.3 2.1 %collective-permute-start.11 = (bf16[128,512]{1,0:T(8,128)(2,1)S(1)}, bf16[128,512]{1,0:T(8,128)(2,1)S(1)}, u32[]{:S(2)}, u32[]{:S(2)}) collective-permute-start(bf16[128,512]{1,0:T(8,128)(2,1)S(1)} %get-tuple-element.72), channel_id=1, source_target_pairs={{0,5},{1,4},{2,7},{3,6},{4,1},{5,0},{6,3},{7,2},{8,13},{9,12},{10,... | collective-permute-start | bytes 393224 | tf_op jit(solution)/shard_map/ppermute | solution.py:36
  27.4 1.2 %collective-permute-start.13 = (bf16[128,512]{1,0:T(8,128)(2,1)S(1)}, bf16[128,512]{1,0:T(8,128)(2,1)S(1)}, u32[]{:S(2)}, u32[]{:S(2)}) collective-permute-start(bf16[128,512]{1,0:T(8,128)(2,1)S(1)} %get-tuple-element.74), channel_id=1, source_target_pairs={{0,7},{1,6},{2,5},{3,4},{4,3},{5,2},{6,1},{7,0},{8,15},{9,14},{10,... | collective-permute-start | bytes 393224 | tf_op jit(solution)/shard_map/ppermute | solution.py:36
  28.9 2.3 %collective-permute-done.11.refs_6_ = bf16[128,512]{1,0:T(8,128)(2,1)S(1)} collective-permute-done((bf16[128,512]{1,0:T(8,128)(2,1)S(1)}, bf16[128,512]{1,0:T(8,128)(2,1)S(1)}, u32[]{:S(2)}, u32[]{:S(2)}) %collective-permute-start.11) | collective-permute-done | bytes 131104 | tf_op jit(solution)/shard_map/ppermute | solution.py:36
  31.2 5.1 %collective-permute-done.12.refs_7_ = bf16[128,512]{1,0:T(8,128)(2,1)S(1)} collective-permute-done((bf16[128,512]{1,0:T(8,128)(2,1)S(1)}, bf16[128,512]{1,0:T(8,128)(2,1)S(1)}, u32[]{:S(2)}, u32[]{:S(2)}) %collective-permute-start.12) | collective-permute-done | bytes 131104 | tf_op jit(solution)/shard_map/ppermute | solution.py:36
  36.4 15.7 %attend.1 = (bf16[128,512]{1,0:T(8,128)(2,1)S(1)}, bf16[128,512]{1,0:T(8,128)(2,1)S(1)}, bf16[128,512]{1,0:T(8,128)(2,1)S(1)}, bf16[128,512]{1,0:T(8,128)(2,1)S(...) custom-call(s32[1,1024]{1,0:T(1,128)S(1)} %add_maximum_fusion.refs_0, ...), custom_call_target="tpu_custom_call" | custom-call | flops 3623878656 | bytes 8388608 | tf_op jit(solution)/shard_map/attend/pallas_call | solution.py:278
  52.0 1.3 %collective-permute-start.22 = (bf16[1024,256]{1,0:T(8,128)(2,1)S(1)}, bf16[1024,256]{1,0:T(8,128)(2,1)S(1)}, u32[]{:S(2)}, u32[]{:S(2)}) collective-permute-start(bf16[1024,256]{1,0:T(8,128)(2,1)S(1)} %get-tuple-element.87), channel_id=1, source_target_pairs={{8,0},{9,1},{10,2},{11,3},{12,4},{13,5},{14,6},{15,7},{16,8},{17,9... | collective-permute-start | bytes 1572872 | tf_op jit(solution)/shard_map/ppermute | solution.py:52
  54.2 1.4 %collective-permute-start.17 = (bf16[128,512]{1,0:T(8,128)(2,1)S(1)}, bf16[128,512]{1,0:T(8,128)(2,1)S(1)}, u32[]{:S(2)}, u32[]{:S(2)}) collective-permute-start(bf16[128,512]{1,0:T(8,128)(2,1)S(1)} %get-tuple-element.79), channel_id=1, source_target_pairs={{0,3},{1,2},{2,1},{3,0},{4,7},{5,6},{6,5},{7,4},{8,11},{9,10},{10,... | collective-permute-start | bytes 393224 | tf_op jit(solution)/shard_map/ppermute | solution.py:36
  56.3 3.5 %collective-permute-done.15.refs_1_ = bf16[128,512]{1,0:T(8,128)(2,1)S(1)} collective-permute-done((bf16[128,512]{1,0:T(8,128)(2,1)S(1)}, bf16[128,512]{1,0:T(8,128)(2,1)S(1)}, u32[]{:S(2)}, u32[]{:S(2)}) %collective-permute-start.15) | collective-permute-done | bytes 131104 | tf_op jit(solution)/shard_map/ppermute | solution.py:36
  59.7 1.7 %collective-permute-start.19 = (bf16[128,512]{1,0:T(8,128)(2,1)S(1)}, bf16[128,512]{1,0:T(8,128)(2,1)S(1)}, u32[]{:S(2)}, u32[]{:S(2)}) collective-permute-start(bf16[128,512]{1,0:T(8,128)(2,1)S(1)} %get-tuple-element.81), channel_id=1, source_target_pairs={{0,5},{1,4},{2,7},{3,6},{4,1},{5,0},{6,3},{7,2},{8,13},{9,12},{10,... | collective-permute-start | bytes 393224 | tf_op jit(solution)/shard_map/ppermute | solution.py:36
  61.4 6.0 %collective-permute-done.22.refs_1_ = bf16[1024,256]{1,0:T(8,128)(2,1)S(1)} collective-permute-done((bf16[1024,256]{1,0:T(8,128)(2,1)S(1)}, bf16[1024,256]{1,0:T(8,128)(2,1)S(1)}, u32[]{:S(2)}, u32[]{:S(2)}) %collective-permute-start.22) | collective-permute-done | bytes 524320 | tf_op jit(solution)/shard_map/ppermute | solution.py:52
  67.8 1.4 %collective-permute-start.23 = (bf16[128,256]{1,0:T(8,128)(2,1)S(1)}, bf16[128,256]{1,0:T(8,128)(2,1)S(1)}, u32[]{:S(2)}, u32[]{:S(2)}) collective-permute-start(bf16[128,256]{1,0:T(8,128)(2,1)S(1)} %get-tuple-element.89), channel_id=1, source_target_pairs={{0,1},{1,0},{2,3},{3,2},{4,5},{5,4},{6,7},{7,6},{8,9},{9,8},{10,11... | collective-permute-start | bytes 196616 | tf_op jit(solution)/shard_map/ppermute | solution.py:36
  69.2 0.9 %collective-permute-start.24 = (bf16[128,256]{1,0:T(8,128)(2,1)S(1)}, bf16[128,256]{1,0:T(8,128)(2,1)S(1)}, u32[]{:S(2)}, u32[]{:S(2)}) collective-permute-start(bf16[128,256]{1,0:T(8,128)(2,1)S(1)} %get-tuple-element.90), channel_id=1, source_target_pairs={{0,2},{1,3},{2,0},{3,1},{4,6},{5,7},{6,4},{7,5},{8,10},{9,11},{10,... | collective-permute-start | bytes 196616 | tf_op jit(solution)/shard_map/ppermute | solution.py:36
  70.9 1.0 %collective-permute-start.26 = (bf16[128,256]{1,0:T(8,128)(2,1)S(1)}, bf16[128,256]{1,0:T(8,128)(2,1)S(1)}, u32[]{:S(2)}, u32[]{:S(2)}) collective-permute-start(bf16[128,256]{1,0:T(8,128)(2,1)S(1)} %get-tuple-element.92), channel_id=1, source_target_pairs={{0,4},{1,5},{2,6},{3,7},{4,0},{5,1},{6,2},{7,3},{8,12},{9,13},{10,... | collective-permute-start | bytes 196616 | tf_op jit(solution)/shard_map/ppermute | solution.py:36
  71.9 2.2 %collective-permute-done.21.refs_7_ = bf16[128,512]{1,0:T(8,128)(2,1)S(1)} collective-permute-done((bf16[128,512]{1,0:T(8,128)(2,1)S(1)}, bf16[128,512]{1,0:T(8,128)(2,1)S(1)}, u32[]{:S(2)}, u32[]{:S(2)}) %collective-permute-start.21) | collective-permute-done | bytes 131104 | tf_op jit(solution)/shard_map/ppermute | solution.py:36
  74.0 1.8 %collective-permute-start.27 = (bf16[128,256]{1,0:T(8,128)(2,1)S(1)}, bf16[128,256]{1,0:T(8,128)(2,1)S(1)}, u32[]{:S(2)}, u32[]{:S(2)}) collective-permute-start(bf16[128,256]{1,0:T(8,128)(2,1)S(1)} %get-tuple-element.93), channel_id=1, source_target_pairs={{0,5},{1,4},{2,7},{3,6},{4,1},{5,0},{6,3},{7,2},{8,13},{9,12},{10,... | collective-permute-start | bytes 196616 | tf_op jit(solution)/shard_map/ppermute | solution.py:36
  75.8 2.1 %collective-permute-start.29 = (bf16[128,256]{1,0:T(8,128)(2,1)S(1)}, bf16[128,256]{1,0:T(8,128)(2,1)S(1)}, u32[]{:S(2)}, u32[]{:S(2)}) collective-permute-start(bf16[128,256]{1,0:T(8,128)(2,1)S(1)} %get-tuple-element.95), channel_id=1, source_target_pairs={{0,7},{1,6},{2,5},{3,4},{4,3},{5,2},{6,1},{7,0},{8,15},{9,14},{10,... | collective-permute-start | bytes 196616 | tf_op jit(solution)/shard_map/ppermute | solution.py:36
  77.9 1.1 %spread.2 = (bf16[128,2048]{1,0:T(8,128)(2,1)}, bf16[128,2048]{1,0:T(8,128)(2,1)}) custom-call(bf16[128,512]{1,0:T(8,128)(2,1)S(1)} %get-tuple-element.76.refs_0_, bf16[128,512]{1,0:T(8,128)(2,1)S(1)} %collective-permute-done.15.refs_1_, bf16[128,512]{1,0:T(8,128)(2,1)S(1)} %collective-permute-done.16.refs_2_, ...), custom_call_target="tpu_custom_call" | custom-call | tf_op jit(solution)/shard_map/spread/pallas_call | solution.py:148
  79.3 2.7 %collective-permute-done.28.refs_6_ = bf16[128,256]{1,0:T(8,128)(2,1)S(1)} collective-permute-done((bf16[128,256]{1,0:T(8,128)(2,1)S(1)}, bf16[128,256]{1,0:T(8,128)(2,1)S(1)}, u32[]{:S(2)}, u32[]{:S(2)}) %collective-permute-start.28) | collective-permute-done | bytes 65568 | tf_op jit(solution)/shard_map/ppermute | solution.py:36
  (50 shorter events, 6.4 us)
Async XLA Ops:
  2.7 6.6 %collective-permute-start = (bf16[128,256]{1,0:T(8,128)(2,1)S(1)}, bf16[128,256]{1,0:T(8,128)(2,1)S(1)}, u32[]{:S(2)}, u32[]{:S(2)}) collective-permute-start(bf16[128,256]{1,0:T(8,128)(2,1)S(1)} %get-tuple-element.52), channel_id=1, source_target_pairs={{0,1},{1,0},{2,3},{3,2},{4,5},{5,4},{6,7},{7,6},{8,9},{9,8},{10,11... | collective-permute-start | bytes 196616 | tf_op jit(solution)/shard_map/ppermute | solution.py:36
  5.7 4.2 %collective-permute-start.1 = (bf16[128,256]{1,0:T(8,128)(2,1)S(1)}, bf16[128,256]{1,0:T(8,128)(2,1)S(1)}, u32[]{:S(2)}, u32[]{:S(2)}) collective-permute-start(bf16[128,256]{1,0:T(8,128)(2,1)S(1)} %get-tuple-element.53), channel_id=1, source_target_pairs={{0,2},{1,3},{2,0},{3,1},{4,6},{5,7},{6,4},{7,5},{8,10},{9,11},{10,... | collective-permute-start | bytes 196616 | tf_op jit(solution)/shard_map/ppermute | solution.py:36
  5.7 8.2 %collective-permute-start.2 = (bf16[128,256]{1,0:T(8,128)(2,1)S(1)}, bf16[128,256]{1,0:T(8,128)(2,1)S(1)}, u32[]{:S(2)}, u32[]{:S(2)}) collective-permute-start(bf16[128,256]{1,0:T(8,128)(2,1)S(1)} %get-tuple-element.54), channel_id=1, source_target_pairs={{0,3},{1,2},{2,1},{3,0},{4,7},{5,6},{6,5},{7,4},{8,11},{9,10},{10,... | collective-permute-start | bytes 196616 | tf_op jit(solution)/shard_map/ppermute | solution.py:36
  5.9 8.0 %collective-permute-start.3 = (bf16[128,256]{1,0:T(8,128)(2,1)S(1)}, bf16[128,256]{1,0:T(8,128)(2,1)S(1)}, u32[]{:S(2)}, u32[]{:S(2)}) collective-permute-start(bf16[128,256]{1,0:T(8,128)(2,1)S(1)} %get-tuple-element.55), channel_id=1, source_target_pairs={{0,4},{1,5},{2,6},{3,7},{4,0},{5,1},{6,2},{7,3},{8,12},{9,13},{10,... | collective-permute-start | bytes 196616 | tf_op jit(solution)/shard_map/ppermute | solution.py:36
  7.8 6.1 %collective-permute-start.4 = (bf16[128,256]{1,0:T(8,128)(2,1)S(1)}, bf16[128,256]{1,0:T(8,128)(2,1)S(1)}, u32[]{:S(2)}, u32[]{:S(2)}) collective-permute-start(bf16[128,256]{1,0:T(8,128)(2,1)S(1)} %get-tuple-element.56), channel_id=1, source_target_pairs={{0,5},{1,4},{2,7},{3,6},{4,1},{5,0},{6,3},{7,2},{8,13},{9,12},{10,... | collective-permute-start | bytes 196616 | tf_op jit(solution)/shard_map/ppermute | solution.py:36
  9.3 5.9 %collective-permute-start.5 = (bf16[128,256]{1,0:T(8,128)(2,1)S(1)}, bf16[128,256]{1,0:T(8,128)(2,1)S(1)}, u32[]{:S(2)}, u32[]{:S(2)}) collective-permute-start(bf16[128,256]{1,0:T(8,128)(2,1)S(1)} %get-tuple-element.57), channel_id=1, source_target_pairs={{0,6},{1,7},{2,4},{3,5},{4,2},{5,3},{6,0},{7,1},{8,14},{9,15},{10,... | collective-permute-start | bytes 196616 | tf_op jit(solution)/shard_map/ppermute | solution.py:36
  9.9 5.4 %collective-permute-start.6 = (bf16[128,256]{1,0:T(8,128)(2,1)S(1)}, bf16[128,256]{1,0:T(8,128)(2,1)S(1)}, u32[]{:S(2)}, u32[]{:S(2)}) collective-permute-start(bf16[128,256]{1,0:T(8,128)(2,1)S(1)} %get-tuple-element.58), channel_id=1, source_target_pairs={{0,7},{1,6},{2,5},{3,4},{4,3},{5,2},{6,1},{7,0},{8,15},{9,14},{10,... | collective-permute-start | bytes 196616 | tf_op jit(solution)/shard_map/ppermute | solution.py:36
  13.7 5.1 %copy-start.4 = (s32[4096]{0:T(1024)S(1)}, s32[4096]{0:T(1024)}, u32[]{:S(2)}) copy-start(s32[4096]{0:T(1024)} %param.9) | copy-start | bytes 49156
  13.7 7.3 %dynamic-slice-start = ((s32[4096]{0:T(1024)}, s32[]{:T(128)}), s32[1024]{0:T(1024)S(1)}, s32[]{:S(2)}) async-start(s32[4096]{0:T(1024)} %param.9, s32[]{:T(128)} %select_n.13), calls=%async_computation | async-start | bytes 8704 | tf_op jit(solution)/shard_map/dynamic_slice | solution.py:309
  15.3 21.1 %collective-permute-start.14 = (bf16[1024,256]{1,0:T(8,128)(2,1)S(1)}, bf16[1024,256]{1,0:T(8,128)(2,1)S(1)}, u32[]{:S(2)}, u32[]{:S(2)}) collective-permute-start(bf16[1024,256]{1,0:T(8,128)(2,1)S(1)} %join.1.refs_9_), channel_id=1, source_target_pairs={{0,8},{1,9},{2,10},{3,11},{4,12},{5,13},{6,14},{7,15},{8,16},{9,17... | collective-permute-start | bytes 1572872 | tf_op jit(solution)/shard_map/ppermute | solution.py:52
  18.9 6.4 %collective-permute-start.7 = (bf16[128,512]{1,0:T(8,128)(2,1)S(1)}, bf16[128,512]{1,0:T(8,128)(2,1)S(1)}, u32[]{:S(2)}, u32[]{:S(2)}) collective-permute-start(bf16[128,512]{1,0:T(8,128)(2,1)S(1)} %get-tuple-element.68), channel_id=1, source_target_pairs={{0,1},{1,0},{2,3},{3,2},{4,5},{5,4},{6,7},{7,6},{8,9},{9,8},{10,11... | collective-permute-start | bytes 393224 | tf_op jit(solution)/shard_map/ppermute | solution.py:36
  20.0 7.3 %collective-permute-start.8 = (bf16[128,512]{1,0:T(8,128)(2,1)S(1)}, bf16[128,512]{1,0:T(8,128)(2,1)S(1)}, u32[]{:S(2)}, u32[]{:S(2)}) collective-permute-start(bf16[128,512]{1,0:T(8,128)(2,1)S(1)} %get-tuple-element.69), channel_id=1, source_target_pairs={{0,2},{1,3},{2,0},{3,1},{4,6},{5,7},{6,4},{7,5},{8,10},{9,11},{10,... | collective-permute-start | bytes 393224 | tf_op jit(solution)/shard_map/ppermute | solution.py:36
  20.0 7.3 %collective-permute-start.9 = (bf16[128,512]{1,0:T(8,128)(2,1)S(1)}, bf16[128,512]{1,0:T(8,128)(2,1)S(1)}, u32[]{:S(2)}, u32[]{:S(2)}) collective-permute-start(bf16[128,512]{1,0:T(8,128)(2,1)S(1)} %get-tuple-element.70), channel_id=1, source_target_pairs={{0,3},{1,2},{2,1},{3,0},{4,7},{5,6},{6,5},{7,4},{8,11},{9,10},{10,... | collective-permute-start | bytes 393224 | tf_op jit(solution)/shard_map/ppermute | solution.py:36
  22.0 6.9 %collective-permute-start.10 = (bf16[128,512]{1,0:T(8,128)(2,1)S(1)}, bf16[128,512]{1,0:T(8,128)(2,1)S(1)}, u32[]{:S(2)}, u32[]{:S(2)}) collective-permute-start(bf16[128,512]{1,0:T(8,128)(2,1)S(1)} %get-tuple-element.71), channel_id=1, source_target_pairs={{0,4},{1,5},{2,6},{3,7},{4,0},{5,1},{6,2},{7,3},{8,12},{9,13},{10,... | collective-permute-start | bytes 393224 | tf_op jit(solution)/shard_map/ppermute | solution.py:36
  25.3 6.0 %collective-permute-start.11 = (bf16[128,512]{1,0:T(8,128)(2,1)S(1)}, bf16[128,512]{1,0:T(8,128)(2,1)S(1)}, u32[]{:S(2)}, u32[]{:S(2)}) collective-permute-start(bf16[128,512]{1,0:T(8,128)(2,1)S(1)} %get-tuple-element.72), channel_id=1, source_target_pairs={{0,5},{1,4},{2,7},{3,6},{4,1},{5,0},{6,3},{7,2},{8,13},{9,12},{10,... | collective-permute-start | bytes 393224 | tf_op jit(solution)/shard_map/ppermute | solution.py:36
  27.3 9.0 %collective-permute-start.12 = (bf16[128,512]{1,0:T(8,128)(2,1)S(1)}, bf16[128,512]{1,0:T(8,128)(2,1)S(1)}, u32[]{:S(2)}, u32[]{:S(2)}) collective-permute-start(bf16[128,512]{1,0:T(8,128)(2,1)S(1)} %get-tuple-element.73), channel_id=1, source_target_pairs={{0,6},{1,7},{2,4},{3,5},{4,2},{5,3},{6,0},{7,1},{8,14},{9,15},{10,... | collective-permute-start | bytes 393224 | tf_op jit(solution)/shard_map/ppermute | solution.py:36
  27.4 9.0 %collective-permute-start.13 = (bf16[128,512]{1,0:T(8,128)(2,1)S(1)}, bf16[128,512]{1,0:T(8,128)(2,1)S(1)}, u32[]{:S(2)}, u32[]{:S(2)}) collective-permute-start(bf16[128,512]{1,0:T(8,128)(2,1)S(1)} %get-tuple-element.74), channel_id=1, source_target_pairs={{0,7},{1,6},{2,5},{3,4},{4,3},{5,2},{6,1},{7,0},{8,15},{9,14},{10,... | collective-permute-start | bytes 393224 | tf_op jit(solution)/shard_map/ppermute | solution.py:36
  52.0 15.4 %collective-permute-start.22 = (bf16[1024,256]{1,0:T(8,128)(2,1)S(1)}, bf16[1024,256]{1,0:T(8,128)(2,1)S(1)}, u32[]{:S(2)}, u32[]{:S(2)}) collective-permute-start(bf16[1024,256]{1,0:T(8,128)(2,1)S(1)} %get-tuple-element.87), channel_id=1, source_target_pairs={{8,0},{9,1},{10,2},{11,3},{12,4},{13,5},{14,6},{15,7},{16,8},{17,9... | collective-permute-start | bytes 1572872 | tf_op jit(solution)/shard_map/ppermute | solution.py:52
  53.3 6.4 %collective-permute-start.15 = (bf16[128,512]{1,0:T(8,128)(2,1)S(1)}, bf16[128,512]{1,0:T(8,128)(2,1)S(1)}, u32[]{:S(2)}, u32[]{:S(2)}) collective-permute-start(bf16[128,512]{1,0:T(8,128)(2,1)S(1)} %get-tuple-element.77), channel_id=1, source_target_pairs={{0,1},{1,0},{2,3},{3,2},{4,5},{5,4},{6,7},{7,6},{8,9},{9,8},{10,11... | collective-permute-start | bytes 393224 | tf_op jit(solution)/shard_map/ppermute | solution.py:36
  54.2 7.2 %collective-permute-start.16 = (bf16[128,512]{1,0:T(8,128)(2,1)S(1)}, bf16[128,512]{1,0:T(8,128)(2,1)S(1)}, u32[]{:S(2)}, u32[]{:S(2)}) collective-permute-start(bf16[128,512]{1,0:T(8,128)(2,1)S(1)} %get-tuple-element.78), channel_id=1, source_target_pairs={{0,2},{1,3},{2,0},{3,1},{4,6},{5,7},{6,4},{7,5},{8,10},{9,11},{10,... | collective-permute-start | bytes 393224 | tf_op jit(solution)/shard_map/ppermute | solution.py:36
  54.2 13.6 %collective-permute-start.17 = (bf16[128,512]{1,0:T(8,128)(2,1)S(1)}, bf16[128,512]{1,0:T(8,128)(2,1)S(1)}, u32[]{:S(2)}, u32[]{:S(2)}) collective-permute-start(bf16[128,512]{1,0:T(8,128)(2,1)S(1)} %get-tuple-element.79), channel_id=1, source_target_pairs={{0,3},{1,2},{2,1},{3,0},{4,7},{5,6},{6,5},{7,4},{8,11},{9,10},{10,... | collective-permute-start | bytes 393224 | tf_op jit(solution)/shard_map/ppermute | solution.py:36
  55.6 13.6 %collective-permute-start.18 = (bf16[128,512]{1,0:T(8,128)(2,1)S(1)}, bf16[128,512]{1,0:T(8,128)(2,1)S(1)}, u32[]{:S(2)}, u32[]{:S(2)}) collective-permute-start(bf16[128,512]{1,0:T(8,128)(2,1)S(1)} %get-tuple-element.80), channel_id=1, source_target_pairs={{0,4},{1,5},{2,6},{3,7},{4,0},{5,1},{6,2},{7,3},{8,12},{9,13},{10,... | collective-permute-start | bytes 393224 | tf_op jit(solution)/shard_map/ppermute | solution.py:36
  59.7 10.4 %collective-permute-start.19 = (bf16[128,512]{1,0:T(8,128)(2,1)S(1)}, bf16[128,512]{1,0:T(8,128)(2,1)S(1)}, u32[]{:S(2)}, u32[]{:S(2)}) collective-permute-start(bf16[128,512]{1,0:T(8,128)(2,1)S(1)} %get-tuple-element.81), channel_id=1, source_target_pairs={{0,5},{1,4},{2,7},{3,6},{4,1},{5,0},{6,3},{7,2},{8,13},{9,12},{10,... | collective-permute-start | bytes 393224 | tf_op jit(solution)/shard_map/ppermute | solution.py:36
  61.4 9.5 %collective-permute-start.20 = (bf16[128,512]{1,0:T(8,128)(2,1)S(1)}, bf16[128,512]{1,0:T(8,128)(2,1)S(1)}, u32[]{:S(2)}, u32[]{:S(2)}) collective-permute-start(bf16[128,512]{1,0:T(8,128)(2,1)S(1)} %get-tuple-element.82), channel_id=1, source_target_pairs={{0,6},{1,7},{2,4},{3,5},{4,2},{5,3},{6,0},{7,1},{8,14},{9,15},{10,... | collective-permute-start | bytes 393224 | tf_op jit(solution)/shard_map/ppermute | solution.py:36
  67.4 6.6 %collective-permute-start.21 = (bf16[128,512]{1,0:T(8,128)(2,1)S(1)}, bf16[128,512]{1,0:T(8,128)(2,1)S(1)}, u32[]{:S(2)}, u32[]{:S(2)}) collective-permute-start(bf16[128,512]{1,0:T(8,128)(2,1)S(1)} %get-tuple-element.83), channel_id=1, source_target_pairs={{0,7},{1,6},{2,5},{3,4},{4,3},{5,2},{6,1},{7,0},{8,15},{9,14},{10,... | collective-permute-start | bytes 393224 | tf_op jit(solution)/shard_map/ppermute | solution.py:36
  67.8 8.0 %collective-permute-start.23 = (bf16[128,256]{1,0:T(8,128)(2,1)S(1)}, bf16[128,256]{1,0:T(8,128)(2,1)S(1)}, u32[]{:S(2)}, u32[]{:S(2)}) collective-permute-start(bf16[128,256]{1,0:T(8,128)(2,1)S(1)} %get-tuple-element.89), channel_id=1, source_target_pairs={{0,1},{1,0},{2,3},{3,2},{4,5},{5,4},{6,7},{7,6},{8,9},{9,8},{10,11... | collective-permute-start | bytes 196616 | tf_op jit(solution)/shard_map/ppermute | solution.py:36
  69.2 6.7 %collective-permute-start.24 = (bf16[128,256]{1,0:T(8,128)(2,1)S(1)}, bf16[128,256]{1,0:T(8,128)(2,1)S(1)}, u32[]{:S(2)}, u32[]{:S(2)}) collective-permute-start(bf16[128,256]{1,0:T(8,128)(2,1)S(1)} %get-tuple-element.90), channel_id=1, source_target_pairs={{0,2},{1,3},{2,0},{3,1},{4,6},{5,7},{6,4},{7,5},{8,10},{9,11},{10,... | collective-permute-start | bytes 196616 | tf_op jit(solution)/shard_map/ppermute | solution.py:36
  70.1 8.9 %collective-permute-start.25 = (bf16[128,256]{1,0:T(8,128)(2,1)S(1)}, bf16[128,256]{1,0:T(8,128)(2,1)S(1)}, u32[]{:S(2)}, u32[]{:S(2)}) collective-permute-start(bf16[128,256]{1,0:T(8,128)(2,1)S(1)} %get-tuple-element.91), channel_id=1, source_target_pairs={{0,3},{1,2},{2,1},{3,0},{4,7},{5,6},{6,5},{7,4},{8,11},{9,10},{10,... | collective-permute-start | bytes 196616 | tf_op jit(solution)/shard_map/ppermute | solution.py:36
  70.9 8.1 %collective-permute-start.26 = (bf16[128,256]{1,0:T(8,128)(2,1)S(1)}, bf16[128,256]{1,0:T(8,128)(2,1)S(1)}, u32[]{:S(2)}, u32[]{:S(2)}) collective-permute-start(bf16[128,256]{1,0:T(8,128)(2,1)S(1)} %get-tuple-element.92), channel_id=1, source_target_pairs={{0,4},{1,5},{2,6},{3,7},{4,0},{5,1},{6,2},{7,3},{8,12},{9,13},{10,... | collective-permute-start | bytes 196616 | tf_op jit(solution)/shard_map/ppermute | solution.py:36
  74.0 5.3 %collective-permute-start.27 = (bf16[128,256]{1,0:T(8,128)(2,1)S(1)}, bf16[128,256]{1,0:T(8,128)(2,1)S(1)}, u32[]{:S(2)}, u32[]{:S(2)}) collective-permute-start(bf16[128,256]{1,0:T(8,128)(2,1)S(1)} %get-tuple-element.93), channel_id=1, source_target_pairs={{0,5},{1,4},{2,7},{3,6},{4,1},{5,0},{6,3},{7,2},{8,13},{9,12},{10,... | collective-permute-start | bytes 196616 | tf_op jit(solution)/shard_map/ppermute | solution.py:36
  75.8 6.2 %collective-permute-start.28 = (bf16[128,256]{1,0:T(8,128)(2,1)S(1)}, bf16[128,256]{1,0:T(8,128)(2,1)S(1)}, u32[]{:S(2)}, u32[]{:S(2)}) collective-permute-start(bf16[128,256]{1,0:T(8,128)(2,1)S(1)} %get-tuple-element.94), channel_id=1, source_target_pairs={{0,6},{1,7},{2,4},{3,5},{4,2},{5,3},{6,0},{7,1},{8,14},{9,15},{10,... | collective-permute-start | bytes 196616 | tf_op jit(solution)/shard_map/ppermute | solution.py:36
  75.8 6.1 %collective-permute-start.29 = (bf16[128,256]{1,0:T(8,128)(2,1)S(1)}, bf16[128,256]{1,0:T(8,128)(2,1)S(1)}, u32[]{:S(2)}, u32[]{:S(2)}) collective-permute-start(bf16[128,256]{1,0:T(8,128)(2,1)S(1)} %get-tuple-element.95), channel_id=1, source_target_pairs={{0,7},{1,6},{2,5},{3,4},{4,3},{5,2},{6,1},{7,0},{8,15},{9,14},{10,... | collective-permute-start | bytes 196616 | tf_op jit(solution)/shard_map/ppermute | solution.py:36
  (4 other events, 4.0 us)

commit v6 on v4

v6 whole, which is shorter than its diff:
```python
import functools

import jax
import jax.numpy as jnp
from jax import lax
from jax.experimental import pallas as pl
from jax.experimental.pallas import tpu as pltpu
from jax.sharding import PartitionSpec as P

HEAD_DIM = 128
WINDOW = 1024
TILE = 128

logit_scale = 168.0 ** (-0.5)
exp2_scale = logit_scale * 1.4426950408889634

SMALL = pltpu.CompilerParams(vmem_limit_bytes=4 * 1024 * 1024)
ANY = pl.BlockSpec(memory_space=pl.ANY)
VMEM = pl.BlockSpec(memory_space=pltpu.VMEM)
F32 = jnp.float32
BF16 = jnp.bfloat16
BOTH = ("pipe", "tensor")


def flat_index():
    return lax.axis_index("pipe") * lax.axis_size("tensor") + lax.axis_index("tensor")


def device_count():
    return lax.axis_size("pipe") * lax.axis_size("tensor")


def swap(value, mask):
    return lax.ppermute(value, BOTH, [(i, i ^ mask) for i in range(device_count())])


def core_mask():
    return lax.axis_size("tensor")


def chip_masks(size):
    return [mask for mask in range(size) if not mask & core_mask()]


def swap_chips(pieces, size):
    return [pieces[0]] + [
        swap(piece, mask) for piece, mask in zip(pieces[1:], chip_masks(size)[1:])
    ]


def partner(size, j):
    return lax.bitwise_xor(lax.rem(flat_index(), size), j)


def place(index, width):
    return pl.ds(pl.multiple_of(index * width, width), width)


def shifted(value, step):
    count = device_count()
    pairs = [(i, i + step) for i in range(count) if 0 <= i + step < count]
    return lax.ppermute(value, BOTH, pairs)


def after(value, *others):
    return lax.optimization_barrier((value, *others))


def run_copies(copies, sems):
    started = []
    for at, (source, target) in enumerate(copies):
        copy = pltpu.make_async_copy(source, target, sems.at[at])
        copy.start()
        started.append(copy)
    for copy in started:
        copy.wait()


def small_call(kernel, out_shape, name, *args):
    return pl.pallas_call(
        kernel,
        out_shape=out_shape,
        in_specs=[VMEM] * len(args),
        out_specs=jax.tree.map(lambda _: VMEM, out_shape),
        compiler_params=SMALL,
        name=name,
    )(*args)


def cut_body(size, core, masks, widths, *refs):
    arrays, outs = refs[: len(widths)], refs[len(widths) :]
    for out, flip in zip(outs, (0, core)):
        start = 0
        for mask in masks:
            for array, width in zip(arrays, widths):
                out[:, start : start + width] = array[:, place(partner(size, mask ^ flip), width)]
                start += width


def stack_body(count, keep, got, *pieces):
    rows, width = keep.shape[0], keep.shape[1] // count
    for at, piece in enumerate(pieces):
        piece[:rows, :] = keep[:, at * width : (at + 1) * width]
        piece[rows:, :] = got[:, at * width : (at + 1) * width]


def gather_cores(arrays, size):
    rows = arrays[0].shape[0]
    masks = chip_masks(size)
    widths = [array.shape[1] // size for array in arrays]
    half = jax.ShapeDtypeStruct((rows, len(masks) * sum(widths)), BF16)
    keep, give = small_call(
        functools.partial(cut_body, size, core_mask(), masks, widths), [half] * 2, "cut", *arrays
    )
    got = swap(give, core_mask())
    piece = jax.ShapeDtypeStruct((2 * rows, sum(widths)), BF16)
    return small_call(
        functools.partial(stack_body, len(masks)), [piece] * len(masks), "stack", keep, got
    )


def place_rows(size, core, masks, pieces, out):
    for mask, piece in zip(masks, pieces):
        rows = piece.shape[0] // 2
        out[place(partner(size, mask), rows), :] = piece[:rows, :]
        out[place(partner(size, mask ^ core), rows), :] = piece[rows:, :]


def take_rows(size, core, masks, source, pieces):
    for mask, piece in zip(masks, pieces):
        rows = piece.shape[0] // 2
        piece[:rows, :] = source(place(partner(size, mask), rows))
        piece[rows:, :] = source(place(partner(size, mask ^ core), rows))


def join(pieces, size):
    rows, cols = pieces[0].shape
    core, masks = core_mask(), chip_masks(size)

    def kernel(*refs):
        place_rows(size, core, masks, refs[:-1], refs[-1])

    out = jax.ShapeDtypeStruct((len(pieces) * rows, cols), BF16)
    return small_call(kernel, out, "join", *pieces)


def combine(terms, size):
    tok, cols = terms[0].shape
    core, masks = core_mask(), chip_masks(size)

    def kernel(*refs):
        added = refs[: len(terms)]

        def source(there):
            total = added[0][there, :]
            for term in added[1:]:
                total = total + term[there, :].astype(F32)
            return total.astype(BF16)

        take_rows(size, core, masks, source, refs[len(terms) :])

    piece = jax.ShapeDtypeStruct((2 * (tok // size), cols), BF16)
    return small_call(kernel, [piece] * len(masks), "combine", *terms)


def bottom_body(*refs):
    out = refs[-1]
    for at, piece in enumerate(refs[:-1]):
        rows, width = piece.shape[0] // 2, piece.shape[1]
        out[:, at * width : (at + 1) * width] = piece[rows:, :]


def spread_body(size, core, masks, count, *refs):
    pieces, got, outs, sems = refs[: len(masks)], refs[len(masks)], refs[-1 - count : -1], refs[-1]
    copies = []
    for chip, (mask, piece) in enumerate(zip(masks, pieces)):
        rows, cols = piece.shape
        rows, width = rows // 2, cols // count
        for at, out in enumerate(outs):
            copies.append(
                (
                    piece.at[:rows, at * width : (at + 1) * width],
                    out.at[:, place(partner(size, mask), width)],
                )
            )
            start = chip * cols + at * width
            copies.append(
                (
                    got.at[:, start : start + width],
                    out.at[:, place(partner(size, mask ^ core), width)],
                )
            )
    run_copies(copies, sems)


def spread_cores(pieces, size, count):
    rows, cols = pieces[0].shape
    rows = rows // 2
    give = jax.ShapeDtypeStruct((rows, cols * len(pieces)), BF16)
    got = swap(small_call(bottom_body, give, "bottom", *pieces), core_mask())
    width = cols // count
    return pl.pallas_call(
        functools.partial(spread_body, size, core_mask(), chip_masks(size), count),
        out_shape=[jax.ShapeDtypeStruct((rows, width * size), BF16)] * count,
        in_specs=[ANY] * (len(pieces) + 1),
        out_specs=[ANY] * count,
        scratch_shapes=[pltpu.SemaphoreType.DMA((size * count,))],
        compiler_params=SMALL,
        name="spread",
    )(*pieces, got)


def dot(a, b):
    return lax.dot_general(a, b, (((1,), (0,)), ((), ())), preferred_element_type=F32)


def dot_t(a, b):
    return lax.dot_general(a, b, (((1,), (1,)), ((), ())), preferred_element_type=F32)


def fold(x, op):
    parts = [x[at : at + 8] for at in range(0, x.shape[0], 8)]
    while len(parts) > 1:
        parts = [
            op(*parts[at : at + 2]) if at + 1 < len(parts) else parts[at]
            for at in range(0, len(parts), 2)
        ]
    return parts[0]


def attend_body(size, core, masks, reach, tok, group, *refs):
    refs = list(refs)
    take = lambda count: [refs.pop(0) for _ in range(count)]
    (low,), qg_pieces, kvs = take(1), take(len(masks)), take(1 + reach)
    og_pieces, (dkv0,), sent = take(len(masks)), take(1), take(reach)
    qg, og, ks, va, kt, vt, dk, dv, s_scr, e_scr, ds_scr = refs
    width = group * HEAD_DIM
    span = WINDOW + TILE
    place_rows(size, core, masks, qg_pieces, qg)
    va[:, HEAD_DIM:] = jnp.where(
        lax.broadcasted_iota(jnp.int32, (va.shape[0], HEAD_DIM), 1) < 2, 1.0, 0.0
    ).astype(BF16)
    for lag in range(reach + 1):
        there = slice((reach - lag) * tok, (reach - lag + 1) * tok)
        ks[there, :] = kvs[lag][:, :HEAD_DIM]
        va[there, :HEAD_DIM] = kvs[lag][:, HEAD_DIM:]
        kt[:, there] = kvs[lag][:, :HEAD_DIM].T
        vt[:, there] = kvs[lag][:, HEAD_DIM:].T
    dk[...] = jnp.zeros_like(dk)
    dv[...] = jnp.zeros_like(dv)
    wide_lane = lax.broadcasted_iota(jnp.int32, (group * TILE, HEAD_DIM), 1)
    row_of = lax.broadcasted_iota(jnp.int32, (TILE, group * TILE), 0)
    col_of = lax.broadcasted_iota(jnp.int32, (TILE, TILE), 1)
    causal = lax.broadcasted_iota(jnp.int32, (TILE, TILE), 0) <= col_of
    causal = jnp.concatenate([causal] * group, axis=1)

    def stacked(base, first):
        here = slice(base, base + TILE)
        return jnp.concatenate(
            [
                qg[here, first + at * HEAD_DIM : first + (at + 1) * HEAD_DIM]
                for at in range(group)
            ],
            axis=0,
        )

    def scores(tile):
        base = tile * TILE
        s_scr[tile % 2] = dot_t(ks[base : base + span, :], stacked(base, 0))

    tiles = tok // TILE
    scores(0)
    for tile in range(tiles):
        base, turn = tile * TILE, tile % 2
        here, there = slice(base, base + TILE), slice(base, base + span)
        low_row = jnp.concatenate([low[:, here]] * group, axis=1) - base
        top = None
        for at in range(0, span, TILE):
            keep = row_of >= low_row - at
            if at == span - TILE:
                keep = keep & causal
            s = jnp.where(keep, s_scr[turn, at : at + TILE, :], -1e30)
            s_scr[turn, at : at + TILE, :] = s
            part = fold(s, jnp.maximum)
            top = part if top is None else jnp.maximum(top, part)
        top = jnp.max(top, axis=0, keepdims=True) * exp2_scale
        if tile + 1 < tiles:
            scores(tile + 1)
        total = None
        for at in range(0, span, TILE):
            e = jnp.exp2(s_scr[turn, at : at + TILE, :] * exp2_scale - top)
            e_scr[turn, at : at + TILE, :] = e.astype(BF16)
            part = fold(e, jnp.add)
            total = part if total is None else total + part
        inv = 1.0 / jnp.sum(total, axis=0, keepdims=True)
        inv = jnp.broadcast_to(inv, (HEAD_DIM, group * TILE)).T
        out = dot(vt[:, there], e_scr[turn]).T * inv
        out = out.astype(BF16)
        g2 = (stacked(base, width).astype(F32) * inv).astype(BF16)
        delta = jnp.sum(g2.astype(F32) * out.astype(F32), axis=1, keepdims=True)
        high = delta.astype(BF16).astype(F32)
        extra = jnp.where(wide_lane == 0, -high, jnp.where(wide_lane == 1, high - delta, 0.0))
        dp = dot_t(va[there, :], jnp.concatenate([g2, extra.astype(BF16)], axis=1))
        dv[there, :] += dot(e_scr[turn], g2)
        for at in range(0, span, TILE):
            part = slice(at, at + TILE)
            ds_scr[turn, part, :] = (e_scr[turn, part, :].astype(F32) * dp[part]).astype(BF16)
        dk[there, :] += dot(ds_scr[turn], stacked(base, 0))
        dq = (dot(kt[:, there], ds_scr[turn]) * logit_scale).T.astype(BF16)
        for at in range(group):
            part = slice(at * TILE, (at + 1) * TILE)
            og[here, at * HEAD_DIM : (at + 1) * HEAD_DIM] = out[part]
            og[here, width + at * HEAD_DIM : width + (at + 1) * HEAD_DIM] = dq[part]

    dkv0[:, :HEAD_DIM] = dk[reach * tok :, :] * logit_scale
    dkv0[:, HEAD_DIM:] = dv[reach * tok :, :]
    for lag in range(1, reach + 1):
        there = slice((reach - lag) * tok, (reach - lag + 1) * tok)
        sent[lag - 1][:, :HEAD_DIM] = (dk[there, :] * logit_scale).astype(BF16)
        sent[lag - 1][:, HEAD_DIM:] = dv[there, :].astype(BF16)
    take_rows(size, core, masks, lambda there: og[there, :], og_pieces)


def attend(low, qg, kvs, size):
    rows, cols = qg[0].shape
    tok = len(qg) * rows
    group = cols // (2 * HEAD_DIM)
    reach = len(kvs) - 1
    span = WINDOW + TILE
    wide = group * TILE
    keys = (reach + 1) * tok
    half = jax.ShapeDtypeStruct((tok, 2 * HEAD_DIM), BF16)
    flops = 6 * 2 * tok * group * span * HEAD_DIM
    count = len(qg)
    results = pl.pallas_call(
        functools.partial(attend_body, size, core_mask(), chip_masks(size), reach, tok, group),
        out_shape=[jax.ShapeDtypeStruct((rows, cols), BF16)] * count
        + [jax.ShapeDtypeStruct((tok, 2 * HEAD_DIM), F32)]
        + [half] * reach,
        in_specs=[VMEM] * (count + 2 + reach),
        out_specs=[VMEM] * (count + 1 + reach),
        scratch_shapes=[
            pltpu.VMEM((tok, cols), BF16),
            pltpu.VMEM((tok, cols), BF16),
            pltpu.VMEM((keys, HEAD_DIM), BF16),
            pltpu.VMEM((keys, 2 * HEAD_DIM), BF16),
            pltpu.VMEM((HEAD_DIM, keys), BF16),
            pltpu.VMEM((HEAD_DIM, keys), BF16),
            pltpu.VMEM((keys, HEAD_DIM), F32),
            pltpu.VMEM((keys, HEAD_DIM), F32),
            pltpu.VMEM((2, span, wide), F32),
            pltpu.VMEM((2, span, wide), BF16),
            pltpu.VMEM((2, span, wide), BF16),
        ],
        compiler_params=pltpu.CompilerParams(vmem_limit_bytes=36 * 1024 * 1024),
        cost_estimate=pl.CostEstimate(
            flops=flops, bytes_accessed=8 * 1024 * 1024, transcendentals=flops // 1536
        ),
        name="attend",
    )(low, *qg, *kvs)
    return results[:count], results[count], results[count + 1 :]


def lowest_key(segment_ids, tok, size):
    start = (flat_index() // size) * tok
    padded = jnp.concatenate([jnp.full((WINDOW,), -1, jnp.int32), segment_ids])
    keys = lax.dynamic_slice_in_dim(padded, start, WINDOW + tok, 0)
    queries = lax.dynamic_slice_in_dim(segment_ids, start, tok, 0)
    before = jnp.sum((keys[:, None] < queries[None, :]).astype(jnp.int32), axis=0)
    return jnp.maximum(before, jnp.arange(1, tok + 1, dtype=jnp.int32))[None, :]


def body(query, key, value, grad_out, segment_ids):
    size = key.shape[1] // HEAD_DIM
    rows = query.shape[0]
    tok = size * rows
    reach = WINDOW // tok
    assert reach * tok == WINDOW and device_count() % size == 0
    low = lowest_key(segment_ids, tok, size)

    pieces = list(gather_cores((key, value), size))
    pieces[0], query, grad_out = after(pieces[0], query, grad_out)
    kv = join(swap_chips(pieces, size), size)
    kv, *qg = after(kv, *gather_cores((query, grad_out), size))
    kvs = [kv] + [shifted(kv, lag * size) for lag in range(1, reach + 1)]
    qg = swap_chips(qg, size)

    og, dkv, sent = attend(low, qg, kvs, size)

    back = [shifted(sent[lag - 1], -lag * size) for lag in range(1, reach + 1)]
    attn_out, grad_query = spread_cores(swap_chips(og, size), size, 2)
    grads = swap_chips(combine([dkv] + back, size), size)
    grad_key, grad_value = spread_cores(grads, size, 2)
    return (attn_out, grad_query, grad_key, grad_value)


def solution(mesh):
    placed = P(("pipe", "tensor"), None)
    return jax.shard_map(
        body,
        mesh=mesh,
        in_specs=(placed, placed, placed, placed, P()),
        out_specs=(placed, placed, placed, placed),
        check_vma=False,
    )
```

time: 90.6 us -> 71 us (0.78)
  waiting for transfers between devices: 42.6 us -> 33 us
  Pallas kernels: 20.5 us -> 13.3 us
  other arithmetic: 1.93 us -> 0.98 us
    ppermute x0 -> x16, waiting for transfers between devices: none -> 33 us  [swap(): lax.ppermute(value, BOTH, [(i, i ^ mask) for i in range(device_count())])]
    ppermute x2, waiting for transfers between devices: 26.3 us -> 0.06 us  [shifted(): return lax.ppermute(value, BOTH, pairs)]
    all_to_all x4 -> x0, starting transfers between devices: 16.7 us -> none  [exchange(): lax.all_to_all(value, BOTH, split_axis=0, concat_axis=0, axis_index_group...]
    all_to_all x4 -> x0, waiting for transfers between devices: 16.3 us -> none  [exchange(): lax.all_to_all(value, BOTH, split_axis=0, concat_axis=0, axis_index_group...]
    ppermute x0 -> x16, starting transfers between devices: none -> 15.9 us  [swap(): lax.ppermute(value, BOTH, [(i, i ^ mask) for i in range(device_count())])]
    pallas_call x5 -> x11, Pallas kernels: 20.5 us -> 13.3 us  [the longest x1 10.6 us: attend(): pl.pallas_call(functools.partial(attend_body, size, core_mask(), chip_mas...]
    convert_element_type x1 -> x0, other arithmetic: 0.94 us -> none  [body(): grads = exchange(total.astype(BF16).reshape(size, rows, -1))]
    unnamed x14 -> x10, local copies, waits for them, and re-layouts: 2.79 us -> 1.99 us
  transfers between devices with their start and end apart: 6 -> 18, of which waited for: 4 -> 11; matrix products, arithmetic and copies ran while one was open for 2% -> 1% of each run, Pallas kernels for 2% -> 2%
where the time goes in v6:
time: 71 us; the launch traced here: 70.8 us
  waiting for transfers between devices  33 us (46%)
  starting transfers between devices  20.7 us (29%)
  Pallas kernels  13.3 us (19%)
  local copies, waits for them, and re-layouts  2.01 us (3%)
  other arithmetic  0.98 us (1%)
  between operations  0.83 us (1%)
    ppermute x16, waiting for transfers between devices, swap(): lax.ppermute(value, BOTH, [(i, i ^ mask) for i in range(device_count())])  33 us
    ppermute x16, starting transfers between devices, swap(): lax.ppermute(value, BOTH, [(i, i ^ mask) for i in range(device_count())])  15.9 us
    pallas_call x1, Pallas kernels, attend(): pl.pallas_call(functools.partial(attend_body, size, core_mask(), chip_mas...  10.6 us
    ppermute x2, starting transfers between devices, shifted(): return lax.ppermute(value, BOTH, pairs)  4.81 us
    pallas_call x2, Pallas kernels, spread_cores(): pl.pallas_call(functools.partial(spread_body, size, core_mask(), chip_mas...  2.02 us
    unnamed x10, local copies, waits for them, and re-layouts  1.99 us
  transfers between devices with their start and end apart: 18, of which 11 were waited for; matrix products, arithmetic and copies ran while one was open for 1% of the time, Pallas kernels for 2%

profile of v6, /device:TPU:0, one launch (start us, length us, event | category | flops | bytes accessed | tf_op | source)
XLA Modules:
  0.0 70.8 jit_solution(10721802579220856813)
XLA Ops:
  0.7 1.0 %copy-done.2 = bf16[128,1024]{1,0:T(8,128)(2,1)S(1)} copy-done((bf16[128,1024]{1,0:T(8,128)(2,1)S(1)}, bf16[128,1024]{1,0:T(8,128)(2,1)}, u32[]{:S(2)}) %copy-start.2) | copy-done | bytes 262168
  1.7 0.9 %copy-done.3 = bf16[128,1024]{1,0:T(8,128)(2,1)S(1)} copy-done((bf16[128,1024]{1,0:T(8,128)(2,1)S(1)}, bf16[128,1024]{1,0:T(8,128)(2,1)}, u32[]{:S(2)}) %copy-start.3) | copy-done | bytes 262168
  2.8 0.5 collective-permute-start
  3.3 1.2 %collective-permute-done.got = bf16[128,1024]{1,0:T(8,128)(2,1)S(1)} collective-permute-done((bf16[128,1024]{1,0:T(8,128)(2,1)S(1)}, bf16[128,1024]{1,0:T(8,128)(2,1)S(1)}, u32[]{:S(2)}, u32[]{:S(2)}) %collective-permute-start) | collective-permute-done | bytes 262176 | tf_op jit(solution)/shard_map/ppermute | solution.py:34
  4.5 0.2 cut.3
  4.7 0.4 collective-permute-start.4
  5.1 2.6 %collective-permute-start.1 = (bf16[256,256]{1,0:T(8,128)(2,1)S(1)}, bf16[256,256]{1,0:T(8,128)(2,1)S(1)}, u32[]{:S(2)}, u32[]{:S(2)}) collective-permute-start(bf16[256,256]{1,0:T(8,128)(2,1)S(1)} %get-tuple-element.42), channel_id=1, source_target_pairs={{0,1},{1,0},{2,3},{3,2},{4,5},{5,4},{6,7},{7,6},{8,9},{9,8},{10,11... | collective-permute-start | bytes 393224 | tf_op jit(solution)/shard_map/ppermute | solution.py:34
  7.8 1.5 %collective-permute-start.2 = (bf16[256,256]{1,0:T(8,128)(2,1)S(1)}, bf16[256,256]{1,0:T(8,128)(2,1)S(1)}, u32[]{:S(2)}, u32[]{:S(2)}) collective-permute-start(bf16[256,256]{1,0:T(8,128)(2,1)S(1)} %get-tuple-element.43), channel_id=1, source_target_pairs={{0,4},{1,5},{2,6},{3,7},{4,0},{5,1},{6,2},{7,3},{8,12},{9,13},{10,... | collective-permute-start | bytes 393224 | tf_op jit(solution)/shard_map/ppermute | solution.py:34
  9.3 2.6 %collective-permute-done.1.refs_1_ = bf16[256,256]{1,0:T(8,128)(2,1)S(1)} collective-permute-done((bf16[256,256]{1,0:T(8,128)(2,1)S(1)}, bf16[256,256]{1,0:T(8,128)(2,1)S(1)}, u32[]{:S(2)}, u32[]{:S(2)}) %collective-permute-start.1) | collective-permute-done | bytes 131104 | tf_op jit(solution)/shard_map/ppermute | solution.py:34
  11.9 4.2 %collective-permute-done.2.refs_2_ = bf16[256,256]{1,0:T(8,128)(2,1)S(1)} collective-permute-done((bf16[256,256]{1,0:T(8,128)(2,1)S(1)}, bf16[256,256]{1,0:T(8,128)(2,1)S(1)}, u32[]{:S(2)}, u32[]{:S(2)}) %collective-permute-start.2) | collective-permute-done | bytes 131104 | tf_op jit(solution)/shard_map/ppermute | solution.py:34
  16.2 3.5 %collective-permute-start.8 = (bf16[1024,256]{1,0:T(8,128)(2,1)S(1)}, bf16[1024,256]{1,0:T(8,128)(2,1)S(1)}, u32[]{:S(2)}, u32[]{:S(2)}) collective-permute-start(bf16[1024,256]{1,0:T(8,128)(2,1)S(1)} %join.1.refs_5_), channel_id=1, source_target_pairs={{0,8},{1,9},{2,10},{3,11},{4,12},{5,13},{6,14},{7,15},{8,16},{9,17... | collective-permute-start | bytes 1572872 | tf_op jit(solution)/shard_map/ppermute | solution.py:62
  19.7 1.3 %collective-permute-start.5 = (bf16[256,512]{1,0:T(8,128)(2,1)S(1)}, bf16[256,512]{1,0:T(8,128)(2,1)S(1)}, u32[]{:S(2)}, u32[]{:S(2)}) collective-permute-start(bf16[256,512]{1,0:T(8,128)(2,1)S(1)} %get-tuple-element.54), channel_id=1, source_target_pairs={{0,1},{1,0},{2,3},{3,2},{4,5},{5,4},{6,7},{7,6},{8,9},{9,8},{10,11... | collective-permute-start | bytes 786440 | tf_op jit(solution)/shard_map/ppermute | solution.py:34
  21.1 0.8 %collective-permute-start.6 = (bf16[256,512]{1,0:T(8,128)(2,1)S(1)}, bf16[256,512]{1,0:T(8,128)(2,1)S(1)}, u32[]{:S(2)}, u32[]{:S(2)}) collective-permute-start(bf16[256,512]{1,0:T(8,128)(2,1)S(1)} %get-tuple-element.55), channel_id=1, source_target_pairs={{0,4},{1,5},{2,6},{3,7},{4,0},{5,1},{6,2},{7,3},{8,12},{9,13},{10,... | collective-permute-start | bytes 786440 | tf_op jit(solution)/shard_map/ppermute | solution.py:34
  21.9 1.4 %collective-permute-start.7 = (bf16[256,512]{1,0:T(8,128)(2,1)S(1)}, bf16[256,512]{1,0:T(8,128)(2,1)S(1)}, u32[]{:S(2)}, u32[]{:S(2)}) collective-permute-start(bf16[256,512]{1,0:T(8,128)(2,1)S(1)} %get-tuple-element.56), channel_id=1, source_target_pairs={{0,5},{1,4},{2,7},{3,6},{4,1},{5,0},{6,3},{7,2},{8,13},{9,12},{10,... | collective-permute-start | bytes 786440 | tf_op jit(solution)/shard_map/ppermute | solution.py:34
  23.3 1.0 %convert_reduce_fusion = s32[1024]{0:T(1024)S(1)} fusion(s32[1024]{0:T(1024)S(1)} %dynamic-slice-done, s32[2048]{0:T(1024)S(1)} %pad_dynamic-slice_fusion), kind=kLoop, calls=%fused_computation | loop fusion | flops 6290432 | bytes 16384 | tf_op jit(solution)/shard_map/reduce_sum | solution.py:369
  24.3 4.8 %collective-permute-done.5.refs_2_ = bf16[256,512]{1,0:T(8,128)(2,1)S(1)} collective-permute-done((bf16[256,512]{1,0:T(8,128)(2,1)S(1)}, bf16[256,512]{1,0:T(8,128)(2,1)S(1)}, u32[]{:S(2)}, u32[]{:S(2)}) %collective-permute-start.5) | collective-permute-done | bytes 262176 | tf_op jit(solution)/shard_map/ppermute | solution.py:34
  29.1 4.8 %collective-permute-done.6.refs_3_ = bf16[256,512]{1,0:T(8,128)(2,1)S(1)} collective-permute-done((bf16[256,512]{1,0:T(8,128)(2,1)S(1)}, bf16[256,512]{1,0:T(8,128)(2,1)S(1)}, u32[]{:S(2)}, u32[]{:S(2)}) %collective-permute-start.6) | collective-permute-done | bytes 262176 | tf_op jit(solution)/shard_map/ppermute | solution.py:34
  33.9 10.6 %attend.1 = (bf16[256,512]{1,0:T(8,128)(2,1)S(1)}, bf16[256,512]{1,0:T(8,128)(2,1)S(1)}, bf16[256,512]{1,0:T(8,128)(2,1)S(1)}, bf16[256,512]{1,0:T(8,128)(2,1)S(...) custom-call(s32[1,1024]{1,0:T(1,128)S(1)} %add_maximum_fusion.refs_0_, ...), custom_call_target="tpu_custom_call" | custom-call | flops 3623878656 | bytes 8388608 | tf_op jit(solution)/shard_map/attend/pallas_call | solution.py:335
  44.5 1.3 %collective-permute-start.13 = (bf16[1024,256]{1,0:T(8,128)(2,1)S(1)}, bf16[1024,256]{1,0:T(8,128)(2,1)S(1)}, u32[]{:S(2)}, u32[]{:S(2)}) collective-permute-start(bf16[1024,256]{1,0:T(8,128)(2,1)S(1)} %get-tuple-element.65), channel_id=1, source_target_pairs={{8,0},{9,1},{10,2},{11,3},{12,4},{13,5},{14,6},{15,7},{16,8},{17,9... | collective-permute-start | bytes 1572872 | tf_op jit(solution)/shard_map/ppermute | solution.py:62
  45.8 0.4 collective-permute-start.9
  46.2 1.6 %collective-permute-start.10 = (bf16[256,512]{1,0:T(8,128)(2,1)S(1)}, bf16[256,512]{1,0:T(8,128)(2,1)S(1)}, u32[]{:S(2)}, u32[]{:S(2)}) collective-permute-start(bf16[256,512]{1,0:T(8,128)(2,1)S(1)} %get-tuple-element.60), channel_id=1, source_target_pairs={{0,4},{1,5},{2,6},{3,7},{4,0},{5,1},{6,2},{7,3},{8,12},{9,13},{10,... | collective-permute-start | bytes 786440 | tf_op jit(solution)/shard_map/ppermute | solution.py:34
  47.9 1.5 %collective-permute-start.11 = (bf16[256,512]{1,0:T(8,128)(2,1)S(1)}, bf16[256,512]{1,0:T(8,128)(2,1)S(1)}, u32[]{:S(2)}, u32[]{:S(2)}) collective-permute-start(bf16[256,512]{1,0:T(8,128)(2,1)S(1)} %get-tuple-element.61), channel_id=1, source_target_pairs={{0,5},{1,4},{2,7},{3,6},{4,1},{5,0},{6,3},{7,2},{8,13},{9,12},{10,... | collective-permute-start | bytes 786440 | tf_op jit(solution)/shard_map/ppermute | solution.py:34
  49.4 5.3 %collective-permute-done.9.refs_1_ = bf16[256,512]{1,0:T(8,128)(2,1)S(1)} collective-permute-done((bf16[256,512]{1,0:T(8,128)(2,1)S(1)}, bf16[256,512]{1,0:T(8,128)(2,1)S(1)}, u32[]{:S(2)}, u32[]{:S(2)}) %collective-permute-start.9) | collective-permute-done | bytes 262176 | tf_op jit(solution)/shard_map/ppermute | solution.py:34
  54.7 3.2 %collective-permute-done.10.refs_2_ = bf16[256,512]{1,0:T(8,128)(2,1)S(1)} collective-permute-done((bf16[256,512]{1,0:T(8,128)(2,1)S(1)}, bf16[256,512]{1,0:T(8,128)(2,1)S(1)}, u32[]{:S(2)}, u32[]{:S(2)}) %collective-permute-start.10) | collective-permute-done | bytes 262176 | tf_op jit(solution)/shard_map/ppermute | solution.py:34
  58.1 1.8 %collective-permute-start.14 = (bf16[256,256]{1,0:T(8,128)(2,1)S(1)}, bf16[256,256]{1,0:T(8,128)(2,1)S(1)}, u32[]{:S(2)}, u32[]{:S(2)}) collective-permute-start(bf16[256,256]{1,0:T(8,128)(2,1)S(1)} %get-tuple-element.67), channel_id=1, source_target_pairs={{0,1},{1,0},{2,3},{3,2},{4,5},{5,4},{6,7},{7,6},{8,9},{9,8},{10,11... | collective-permute-start | bytes 393224 | tf_op jit(solution)/shard_map/ppermute | solution.py:34
  59.9 0.7 collective-permute-start.15
  60.6 1.1 %collective-permute-start.16 = (bf16[256,256]{1,0:T(8,128)(2,1)S(1)}, bf16[256,256]{1,0:T(8,128)(2,1)S(1)}, u32[]{:S(2)}, u32[]{:S(2)}) collective-permute-start(bf16[256,256]{1,0:T(8,128)(2,1)S(1)} %get-tuple-element.69), channel_id=1, source_target_pairs={{0,5},{1,4},{2,7},{3,6},{4,1},{5,0},{6,3},{7,2},{8,13},{9,12},{10,... | collective-permute-start | bytes 393224 | tf_op jit(solution)/shard_map/ppermute | solution.py:34
  61.7 2.5 %collective-permute-done.14.refs_1_ = bf16[256,256]{1,0:T(8,128)(2,1)S(1)} collective-permute-done((bf16[256,256]{1,0:T(8,128)(2,1)S(1)}, bf16[256,256]{1,0:T(8,128)(2,1)S(1)}, u32[]{:S(2)}, u32[]{:S(2)}) %collective-permute-start.14) | collective-permute-done | bytes 131104 | tf_op jit(solution)/shard_map/ppermute | solution.py:34
  64.2 4.1 %collective-permute-done.15.refs_2_ = bf16[256,256]{1,0:T(8,128)(2,1)S(1)} collective-permute-done((bf16[256,256]{1,0:T(8,128)(2,1)S(1)}, bf16[256,256]{1,0:T(8,128)(2,1)S(1)}, u32[]{:S(2)}, u32[]{:S(2)}) %collective-permute-start.15) | collective-permute-done | bytes 131104 | tf_op jit(solution)/shard_map/ppermute | solution.py:34
  68.4 1.1 %spread.2 = (bf16[128,2048]{1,0:T(8,128)(2,1)}, bf16[128,2048]{1,0:T(8,128)(2,1)}) custom-call(bf16[256,512]{1,0:T(8,128)(2,1)S(1)} %get-tuple-element.58.refs_0_, bf16[256,512]{1,0:T(8,128)(2,1)S(1)} %collective-permute-done.9.refs_1_, bf16[256,512]{1,0:T(8,128)(2,1)S(1)} %collective-permute-done.10.refs_2_, ...), custom_call_target="tpu_custom_call" | custom-call | tf_op jit(solution)/shard_map/spread/pallas_call | solution.py:202
  69.5 0.4 collective-permute-done.17.refs_4_
  69.9 0.9 %spread.3 = (bf16[128,1024]{1,0:T(8,128)(2,1)}, bf16[128,1024]{1,0:T(8,128)(2,1)}) custom-call(bf16[256,256]{1,0:T(8,128)(2,1)S(1)} %get-tuple-element.66.refs_0_, bf16[256,256]{1,0:T(8,128)(2,1)S(1)} %collective-permute-done.14.refs_1_, bf16[256,256]{1,0:T(8,128)(2,1)S(1)} %collective-permute-done.15.refs_2_, ...), custom_call_target="tpu_custom_call" | custom-call | tf_op jit(solution)/shard_map/spread/pallas_call | solution.py:202
  (30 shorter events, 0.7 us)
Async XLA Ops:
  0.6 3.9 %copy-start.1 = (bf16[128,2048]{1,0:T(8,128)(2,1)S(1)}, bf16[128,2048]{1,0:T(8,128)(2,1)}, u32[]{:S(2)}) copy-start(bf16[128,2048]{1,0:T(8,128)(2,1)} %refs_1_.2) | copy-start | bytes 1572868
  0.6 3.9 %copy-start = (bf16[128,2048]{1,0:T(8,128)(2,1)S(1)}, bf16[128,2048]{1,0:T(8,128)(2,1)}, u32[]{:S(2)}) copy-start(bf16[128,2048]{1,0:T(8,128)(2,1)} %refs_0_.2) | copy-start | bytes 1572868
  0.7 1.0 %copy-start.2 = (bf16[128,1024]{1,0:T(8,128)(2,1)S(1)}, bf16[128,1024]{1,0:T(8,128)(2,1)}, u32[]{:S(2)}) copy-start(bf16[128,1024]{1,0:T(8,128)(2,1)} %refs_0_.1) | copy-start | bytes 786436
  1.7 0.9 %copy-start.3 = (bf16[128,1024]{1,0:T(8,128)(2,1)S(1)}, bf16[128,1024]{1,0:T(8,128)(2,1)}, u32[]{:S(2)}) copy-start(bf16[128,1024]{1,0:T(8,128)(2,1)} %refs_1_.1) | copy-start | bytes 786436
  2.8 1.7 %collective-permute-start = (bf16[128,1024]{1,0:T(8,128)(2,1)S(1)}, bf16[128,1024]{1,0:T(8,128)(2,1)S(1)}, u32[]{:S(2)}, u32[]{:S(2)}) collective-permute-start(bf16[128,1024]{1,0:T(8,128)(2,1)S(1)} %get-tuple-element.39), channel_id=1, source_target_pairs={{0,2},{1,3},{2,0},{3,1},{4,6},{5,7},{6,4},{7,5},{8,10},{9,11},{10,... | collective-permute-start | bytes 786440 | tf_op jit(solution)/shard_map/ppermute | solution.py:34
  4.7 11.4 %collective-permute-start.4 = (bf16[128,2048]{1,0:T(8,128)(2,1)S(1)}, bf16[128,2048]{1,0:T(8,128)(2,1)S(1)}, u32[]{:S(2)}, u32[]{:S(2)}) collective-permute-start(bf16[128,2048]{1,0:T(8,128)(2,1)S(1)} %get-tuple-element.48), channel_id=1, source_target_pairs={{0,2},{1,3},{2,0},{3,1},{4,6},{5,7},{6,4},{7,5},{8,10},{9,11},{10,... | collective-permute-start | bytes 1572872 | tf_op jit(solution)/shard_map/ppermute | solution.py:34
  5.1 6.7 %collective-permute-start.1 = (bf16[256,256]{1,0:T(8,128)(2,1)S(1)}, bf16[256,256]{1,0:T(8,128)(2,1)S(1)}, u32[]{:S(2)}, u32[]{:S(2)}) collective-permute-start(bf16[256,256]{1,0:T(8,128)(2,1)S(1)} %get-tuple-element.42), channel_id=1, source_target_pairs={{0,1},{1,0},{2,3},{3,2},{4,5},{5,4},{6,7},{7,6},{8,9},{9,8},{10,11... | collective-permute-start | bytes 393224 | tf_op jit(solution)/shard_map/ppermute | solution.py:34
  7.8 8.3 %collective-permute-start.2 = (bf16[256,256]{1,0:T(8,128)(2,1)S(1)}, bf16[256,256]{1,0:T(8,128)(2,1)S(1)}, u32[]{:S(2)}, u32[]{:S(2)}) collective-permute-start(bf16[256,256]{1,0:T(8,128)(2,1)S(1)} %get-tuple-element.43), channel_id=1, source_target_pairs={{0,4},{1,5},{2,6},{3,7},{4,0},{5,1},{6,2},{7,3},{8,12},{9,13},{10,... | collective-permute-start | bytes 393224 | tf_op jit(solution)/shard_map/ppermute | solution.py:34
  9.3 6.8 %collective-permute-start.3 = (bf16[256,256]{1,0:T(8,128)(2,1)S(1)}, bf16[256,256]{1,0:T(8,128)(2,1)S(1)}, u32[]{:S(2)}, u32[]{:S(2)}) collective-permute-start(bf16[256,256]{1,0:T(8,128)(2,1)S(1)} %get-tuple-element.44), channel_id=1, source_target_pairs={{0,5},{1,4},{2,7},{3,6},{4,1},{5,0},{6,3},{7,2},{8,13},{9,12},{10,... | collective-permute-start | bytes 393224 | tf_op jit(solution)/shard_map/ppermute | solution.py:34
  9.3 10.4 %copy-start.4 = (s32[4096]{0:T(1024)S(1)}, s32[4096]{0:T(1024)}, u32[]{:S(2)}) copy-start(s32[4096]{0:T(1024)} %param.9) | copy-start | bytes 49156
  9.3 14.0 %dynamic-slice-start = ((s32[4096]{0:T(1024)}, s32[]{:T(128)}), s32[1024]{0:T(1024)S(1)}, s32[]{:S(2)}) async-start(s32[4096]{0:T(1024)} %param.9, s32[]{:T(128)} %select_n.13), calls=%async_computation | async-start | bytes 8704 | tf_op jit(solution)/shard_map/dynamic_slice | solution.py:368
  16.2 17.7 %collective-permute-start.8 = (bf16[1024,256]{1,0:T(8,128)(2,1)S(1)}, bf16[1024,256]{1,0:T(8,128)(2,1)S(1)}, u32[]{:S(2)}, u32[]{:S(2)}) collective-permute-start(bf16[1024,256]{1,0:T(8,128)(2,1)S(1)} %join.1.refs_5_), channel_id=1, source_target_pairs={{0,8},{1,9},{2,10},{3,11},{4,12},{5,13},{6,14},{7,15},{8,16},{9,17... | collective-permute-start | bytes 1572872 | tf_op jit(solution)/shard_map/ppermute | solution.py:62
  19.7 9.3 %collective-permute-start.5 = (bf16[256,512]{1,0:T(8,128)(2,1)S(1)}, bf16[256,512]{1,0:T(8,128)(2,1)S(1)}, u32[]{:S(2)}, u32[]{:S(2)}) collective-permute-start(bf16[256,512]{1,0:T(8,128)(2,1)S(1)} %get-tuple-element.54), channel_id=1, source_target_pairs={{0,1},{1,0},{2,3},{3,2},{4,5},{5,4},{6,7},{7,6},{8,9},{9,8},{10,11... | collective-permute-start | bytes 786440 | tf_op jit(solution)/shard_map/ppermute | solution.py:34
  21.1 12.8 %collective-permute-start.6 = (bf16[256,512]{1,0:T(8,128)(2,1)S(1)}, bf16[256,512]{1,0:T(8,128)(2,1)S(1)}, u32[]{:S(2)}, u32[]{:S(2)}) collective-permute-start(bf16[256,512]{1,0:T(8,128)(2,1)S(1)} %get-tuple-element.55), channel_id=1, source_target_pairs={{0,4},{1,5},{2,6},{3,7},{4,0},{5,1},{6,2},{7,3},{8,12},{9,13},{10,... | collective-permute-start | bytes 786440 | tf_op jit(solution)/shard_map/ppermute | solution.py:34
  21.9 12.0 %collective-permute-start.7 = (bf16[256,512]{1,0:T(8,128)(2,1)S(1)}, bf16[256,512]{1,0:T(8,128)(2,1)S(1)}, u32[]{:S(2)}, u32[]{:S(2)}) collective-permute-start(bf16[256,512]{1,0:T(8,128)(2,1)S(1)} %get-tuple-element.56), channel_id=1, source_target_pairs={{0,5},{1,4},{2,7},{3,6},{4,1},{5,0},{6,3},{7,2},{8,13},{9,12},{10,... | collective-permute-start | bytes 786440 | tf_op jit(solution)/shard_map/ppermute | solution.py:34
  44.5 13.5 %collective-permute-start.13 = (bf16[1024,256]{1,0:T(8,128)(2,1)S(1)}, bf16[1024,256]{1,0:T(8,128)(2,1)S(1)}, u32[]{:S(2)}, u32[]{:S(2)}) collective-permute-start(bf16[1024,256]{1,0:T(8,128)(2,1)S(1)} %get-tuple-element.65), channel_id=1, source_target_pairs={{8,0},{9,1},{10,2},{11,3},{12,4},{13,5},{14,6},{15,7},{16,8},{17,9... | collective-permute-start | bytes 1572872 | tf_op jit(solution)/shard_map/ppermute | solution.py:62
  45.8 8.8 %collective-permute-start.9 = (bf16[256,512]{1,0:T(8,128)(2,1)S(1)}, bf16[256,512]{1,0:T(8,128)(2,1)S(1)}, u32[]{:S(2)}, u32[]{:S(2)}) collective-permute-start(bf16[256,512]{1,0:T(8,128)(2,1)S(1)} %get-tuple-element.59), channel_id=1, source_target_pairs={{0,1},{1,0},{2,3},{3,2},{4,5},{5,4},{6,7},{7,6},{8,9},{9,8},{10,11... | collective-permute-start | bytes 786440 | tf_op jit(solution)/shard_map/ppermute | solution.py:34
  46.2 11.6 %collective-permute-start.10 = (bf16[256,512]{1,0:T(8,128)(2,1)S(1)}, bf16[256,512]{1,0:T(8,128)(2,1)S(1)}, u32[]{:S(2)}, u32[]{:S(2)}) collective-permute-start(bf16[256,512]{1,0:T(8,128)(2,1)S(1)} %get-tuple-element.60), channel_id=1, source_target_pairs={{0,4},{1,5},{2,6},{3,7},{4,0},{5,1},{6,2},{7,3},{8,12},{9,13},{10,... | collective-permute-start | bytes 786440 | tf_op jit(solution)/shard_map/ppermute | solution.py:34
  47.9 10.0 %collective-permute-start.11 = (bf16[256,512]{1,0:T(8,128)(2,1)S(1)}, bf16[256,512]{1,0:T(8,128)(2,1)S(1)}, u32[]{:S(2)}, u32[]{:S(2)}) collective-permute-start(bf16[256,512]{1,0:T(8,128)(2,1)S(1)} %get-tuple-element.61), channel_id=1, source_target_pairs={{0,5},{1,4},{2,7},{3,6},{4,1},{5,0},{6,3},{7,2},{8,13},{9,12},{10,... | collective-permute-start | bytes 786440 | tf_op jit(solution)/shard_map/ppermute | solution.py:34
  57.9 10.5 %collective-permute-start.12 = (bf16[128,2048]{1,0:T(8,128)(2,1)S(1)}, bf16[128,2048]{1,0:T(8,128)(2,1)S(1)}, u32[]{:S(2)}, u32[]{:S(2)}) collective-permute-start(bf16[128,2048]{1,0:T(8,128)(2,1)S(1)} %bottom.2), channel_id=1, source_target_pairs={{0,2},{1,3},{2,0},{3,1},{4,6},{5,7},{6,4},{7,5},{8,10},{9,11},{10,... | collective-permute-start | bytes 1572872 | tf_op jit(solution)/shard_map/ppermute | solution.py:34
  58.1 6.0 %collective-permute-start.14 = (bf16[256,256]{1,0:T(8,128)(2,1)S(1)}, bf16[256,256]{1,0:T(8,128)(2,1)S(1)}, u32[]{:S(2)}, u32[]{:S(2)}) collective-permute-start(bf16[256,256]{1,0:T(8,128)(2,1)S(1)} %get-tuple-element.67), channel_id=1, source_target_pairs={{0,1},{1,0},{2,3},{3,2},{4,5},{5,4},{6,7},{7,6},{8,9},{9,8},{10,11... | collective-permute-start | bytes 393224 | tf_op jit(solution)/shard_map/ppermute | solution.py:34
  59.9 8.4 %collective-permute-start.15 = (bf16[256,256]{1,0:T(8,128)(2,1)S(1)}, bf16[256,256]{1,0:T(8,128)(2,1)S(1)}, u32[]{:S(2)}, u32[]{:S(2)}) collective-permute-start(bf16[256,256]{1,0:T(8,128)(2,1)S(1)} %get-tuple-element.68), channel_id=1, source_target_pairs={{0,4},{1,5},{2,6},{3,7},{4,0},{5,1},{6,2},{7,3},{8,12},{9,13},{10,... | collective-permute-start | bytes 393224 | tf_op jit(solution)/shard_map/ppermute | solution.py:34
  60.6 7.7 %collective-permute-start.16 = (bf16[256,256]{1,0:T(8,128)(2,1)S(1)}, bf16[256,256]{1,0:T(8,128)(2,1)S(1)}, u32[]{:S(2)}, u32[]{:S(2)}) collective-permute-start(bf16[256,256]{1,0:T(8,128)(2,1)S(1)} %get-tuple-element.69), channel_id=1, source_target_pairs={{0,5},{1,4},{2,7},{3,6},{4,1},{5,0},{6,3},{7,2},{8,13},{9,12},{10,... | collective-permute-start | bytes 393224 | tf_op jit(solution)/shard_map/ppermute | solution.py:34
  68.3 1.6 %collective-permute-start.17 = (bf16[128,1024]{1,0:T(8,128)(2,1)S(1)}, bf16[128,1024]{1,0:T(8,128)(2,1)S(1)}, u32[]{:S(2)}, u32[]{:S(2)}) collective-permute-start(bf16[128,1024]{1,0:T(8,128)(2,1)S(1)} %bottom.3), channel_id=1, source_target_pairs={{0,2},{1,3},{2,0},{3,1},{4,6},{5,7},{6,4},{7,5},{8,10},{9,11},{10,... | collective-permute-start | bytes 786440 | tf_op jit(solution)/shard_map/ppermute | solution.py:34

commit v7 on v6

--- a/solution.py
+++ b/solution.py
@@ -87,36 +87,39 @@
     )(*args)
 
 
-def cut_body(size, core, masks, widths, *refs):
-    arrays, outs = refs[: len(widths)], refs[len(widths) :]
-    for out, flip in zip(outs, (0, core)):
+def this_core(array, size):
+    core = core_mask()
+    width = array.shape[1] // size
+    shares = [array[:, r * width : (r + 1) * width] for r in range(size)]
+    first, second = (
+        jnp.concatenate([share for r, share in enumerate(shares) if (r // core) % 2 == at], axis=1)
+        for at in range(2)
+    )
+    return jnp.where((flat_index() // core) % 2 == 0, first, second)
+
+
+def stack_body(size, core, masks, count, *refs):
+    own, got, pieces = refs[:count], refs[count : 2 * count], refs[2 * count :]
+    rows = own[0].shape[0]
+    for mask, piece in zip(masks, pieces):
+        there = partner(size, mask)
+        chip = there // (2 * core) * core + lax.rem(there, core)
         start = 0
-        for mask in masks:
-            for array, width in zip(arrays, widths):
-                out[:, start : start + width] = array[:, place(partner(size, mask ^ flip), width)]
-                start += width
-
-
-def stack_body(count, keep, got, *pieces):
-    rows, width = keep.shape[0], keep.shape[1] // count
-    for at, piece in enumerate(pieces):
-        piece[:rows, :] = keep[:, at * width : (at + 1) * width]
-        piece[rows:, :] = got[:, at * width : (at + 1) * width]
+        for mine, other in zip(own, got):
+            width = other.shape[1] // size
+            piece[:rows, start : start + width] = mine[:, place(chip, width)]
+            piece[rows:, start : start + width] = other[:, place(there, width)]
+            start += width
 
 
 def gather_cores(arrays, size):
-    rows = arrays[0].shape[0]
     masks = chip_masks(size)
-    widths = [array.shape[1] // size for array in arrays]
-    half = jax.ShapeDtypeStruct((rows, len(masks) * sum(widths)), BF16)
-    keep, give = small_call(
-        functools.partial(cut_body, size, core_mask(), masks, widths), [half] * 2, "cut", *arrays
-    )
-    got = swap(give, core_mask())
-    piece = jax.ShapeDtypeStruct((2 * rows, sum(widths)), BF16)
-    return small_call(
-        functools.partial(stack_body, len(masks)), [piece] * len(masks), "stack", keep, got
-    )
+    got = [swap(array, core_mask()) for array in arrays]
+    own = [this_core(array, size) for array in arrays]
+    cols = sum(array.shape[1] // size for array in arrays)
+    piece = jax.ShapeDtypeStruct((2 * arrays[0].shape[0], cols), BF16)
+    kernel = functools.partial(stack_body, size, core_mask(), masks, len(arrays))
+    return small_call(kernel, [piece] * len(masks), "stack", *own, *got)
 
 
 def place_rows(size, core, masks, pieces, out):
@@ -126,11 +129,12 @@
         out[place(partner(size, mask ^ core), rows), :] = piece[rows:, :]
 
 
-def take_rows(size, core, masks, source, pieces):
-    for mask, piece in zip(masks, pieces):
-        rows = piece.shape[0] // 2
-        piece[:rows, :] = source(place(partner(size, mask), rows))
-        piece[rows:, :] = source(place(partner(size, mask ^ core), rows))
+def take_rows(size, core, masks, source, own, give):
+    rows = own.shape[0] // len(masks)
+    for at, mask in enumerate(masks):
+        part = slice(at * rows, (at + 1) * rows)
+        own[part, :] = source(place(partner(size, mask), rows))
+        give[part, :] = source(place(partner(size, mask ^ core), rows))
 
 
 def join(pieces, size):
@@ -157,57 +161,56 @@
                 total = total + term[there, :].astype(F32)
             return total.astype(BF16)
 
-        take_rows(size, core, masks, source, refs[len(terms) :])
-
-    piece = jax.ShapeDtypeStruct((2 * (tok // size), cols), BF16)
-    return small_call(kernel, [piece] * len(masks), "combine", *terms)
-
-
-def bottom_body(*refs):
-    out = refs[-1]
-    for at, piece in enumerate(refs[:-1]):
-        rows, width = piece.shape[0] // 2, piece.shape[1]
-        out[:, at * width : (at + 1) * width] = piece[rows:, :]
+        take_rows(size, core, masks, source, *refs[len(terms) :])
+
+    half = jax.ShapeDtypeStruct((tok // 2, cols), BF16)
+    return small_call(kernel, [half] * 2, "combine", *terms)
+
+
+def pair_body(own, got, *pieces):
+    rows = own.shape[0] // len(pieces)
+    for at, piece in enumerate(pieces):
+        part = slice(at * rows, (at + 1) * rows)
+        piece[:rows, :] = own[part, :]
+        piece[rows:, :] = got[part, :]
+
+
+def scatter(own, give, size):
+    count = len(chip_masks(size))
+    piece = jax.ShapeDtypeStruct((2 * own.shape[0] // count, own.shape[1]), BF16)
+    pieces = small_call(pair_body, [piece] * count, "pair", own, swap(give, core_mask()))
+    return swap_chips(pieces, size)
 
 
 def spread_body(size, core, masks, count, *refs):
-    pieces, got, outs, sems = refs[: len(masks)], refs[len(masks)], refs[-1 - count : -1], refs[-1]
+    pieces, outs, sems = refs[: len(masks)], refs[len(masks) : -1], refs[-1]
     copies = []
-    for chip, (mask, piece) in enumerate(zip(masks, pieces)):
+    for mask, piece in zip(masks, pieces):
         rows, cols = piece.shape
         rows, width = rows // 2, cols // count
-        for at, out in enumerate(outs):
-            copies.append(
-                (
-                    piece.at[:rows, at * width : (at + 1) * width],
-                    out.at[:, place(partner(size, mask), width)],
+        for flip in (0, 1):
+            columns = place(partner(size, mask ^ (core * flip)), width)
+            for at, out in enumerate(outs):
+                copies.append(
+                    (
+                        piece.at[flip * rows : (flip + 1) * rows, at * width : (at + 1) * width],
+                        out.at[:, columns],
+                    )
                 )
-            )
-            start = chip * cols + at * width
-            copies.append(
-                (
-                    got.at[:, start : start + width],
-                    out.at[:, place(partner(size, mask ^ core), width)],
-                )
-            )
     run_copies(copies, sems)
 
 
-def spread_cores(pieces, size, count):
+def spread(pieces, size, count):
     rows, cols = pieces[0].shape
-    rows = rows // 2
-    give = jax.ShapeDtypeStruct((rows, cols * len(pieces)), BF16)
-    got = swap(small_call(bottom_body, give, "bottom", *pieces), core_mask())
-    width = cols // count
     return pl.pallas_call(
         functools.partial(spread_body, size, core_mask(), chip_masks(size), count),
-        out_shape=[jax.ShapeDtypeStruct((rows, width * size), BF16)] * count,
-        in_specs=[ANY] * (len(pieces) + 1),
+        out_shape=[jax.ShapeDtypeStruct((rows // 2, cols // count * size), BF16)] * count,
+        in_specs=[ANY] * len(pieces),
         out_specs=[ANY] * count,
         scratch_shapes=[pltpu.SemaphoreType.DMA((size * count,))],
         compiler_params=SMALL,
         name="spread",
-    )(*pieces, got)
+    )(*pieces)
 
 
 def dot(a, b):
@@ -232,7 +235,7 @@
     refs = list(refs)
     take = lambda count: [refs.pop(0) for _ in range(count)]
     (low,), qg_pieces, kvs = take(1), take(len(masks)), take(1 + reach)
-    og_pieces, (dkv0,), sent = take(len(masks)), take(1), take(reach)
+    og_halves, (dkv0,), sent = take(2), take(1), take(reach)
     qg, og, ks, va, kt, vt, dk, dv, s_scr, e_scr, ds_scr = refs
     width = group * HEAD_DIM
     span = WINDOW + TILE
@@ -318,7 +321,7 @@
         there = slice((reach - lag) * tok, (reach - lag + 1) * tok)
         sent[lag - 1][:, :HEAD_DIM] = (dk[there, :] * logit_scale).astype(BF16)
         sent[lag - 1][:, HEAD_DIM:] = dv[there, :].astype(BF16)
-    take_rows(size, core, masks, lambda there: og[there, :], og_pieces)
+    take_rows(size, core, masks, lambda there: og[there, :], *og_halves)
 
 
 def attend(low, qg, kvs, size):
@@ -334,11 +337,11 @@
     count = len(qg)
     results = pl.pallas_call(
         functools.partial(attend_body, size, core_mask(), chip_masks(size), reach, tok, group),
-        out_shape=[jax.ShapeDtypeStruct((rows, cols), BF16)] * count
+        out_shape=[jax.ShapeDtypeStruct((tok // 2, cols), BF16)] * 2
         + [jax.ShapeDtypeStruct((tok, 2 * HEAD_DIM), F32)]
         + [half] * reach,
         in_specs=[VMEM] * (count + 2 + reach),
-        out_specs=[VMEM] * (count + 1 + reach),
+        out_specs=[VMEM] * (3 + reach),
         scratch_shapes=[
             pltpu.VMEM((tok, cols), BF16),
             pltpu.VMEM((tok, cols), BF16),
@@ -358,7 +361,7 @@
         ),
         name="attend",
     )(low, *qg, *kvs)
-    return results[:count], results[count], results[count + 1 :]
+    return results[:2], results[2], results[3:]
 
 
 def lowest_key(segment_ids, tok, size):
@@ -378,19 +381,17 @@
     assert reach * tok == WINDOW and device_count() % size == 0
     low = lowest_key(segment_ids, tok, size)
 
-    pieces = list(gather_cores((key, value), size))
-    pieces[0], query, grad_out = after(pieces[0], query, grad_out)
-    kv = join(swap_chips(pieces, size), size)
-    kv, *qg = after(kv, *gather_cores((query, grad_out), size))
+    kv = join(swap_chips(gather_cores((key, value), size), size), size)
+    qg = swap_chips(gather_cores((query, grad_out), size), size)
     kvs = [kv] + [shifted(kv, lag * size) for lag in range(1, reach + 1)]
-    qg = swap_chips(qg, size)
 
     og, dkv, sent = attend(low, qg, kvs, size)
 
     back = [shifted(sent[lag - 1], -lag * size) for lag in range(1, reach + 1)]
-    attn_out, grad_query = spread_cores(swap_chips(og, size), size, 2)
-    grads = swap_chips(combine([dkv] + back, size), size)
-    grad_key, grad_value = spread_cores(grads, size, 2)
+    dkv, *og = after(dkv, *scatter(*og, size))
+    grads = scatter(*combine([dkv] + back, size), size)
+    attn_out, grad_query = spread(og, size, 2)
+    grad_key, grad_value = spread(grads, size, 2)
     return (attn_out, grad_query, grad_key, grad_value)
 
 

time: 71 us -> 72.3 us (1.018)
    slice x0 -> x4, local copies, waits for them, and re-layouts: none -> 2.15 us  [this_core(): shares = [array[:, r * width:(r + 1) * width] for r in range(size)]]
    unnamed x10 -> x6, local copies, waits for them, and re-layouts: 1.99 us -> 0.02 us
    ppermute x16 -> x18, starting transfers between devices: 15.9 us -> 16.4 us  [swap(): lax.ppermute(value, BOTH, [(i, i ^ mask) for i in range(device_count())])]
    ppermute x16 -> x18, waiting for transfers between devices: 33 us -> 33.2 us  [swap(): lax.ppermute(value, BOTH, [(i, i ^ mask) for i in range(device_count())])]
  transfers between devices with their start and end apart: 18 -> 20, of which waited for: 11 -> 12; matrix products, arithmetic and copies ran while one was open for 1% -> 5% of each run, Pallas kernels for 2% -> 2%
where the time goes in v7:
time: 72.3 us; the launch traced here: 72 us
  waiting for transfers between devices  33.3 us (46%)
  starting transfers between devices  21.2 us (29%)
  Pallas kernels  13.2 us (18%)
  local copies, waits for them, and re-layouts  2.19 us (3%)
  other arithmetic  1.19 us (2%)
  between operations  0.9 us (1%)
    ppermute x18, waiting for transfers between devices, swap(): lax.ppermute(value, BOTH, [(i, i ^ mask) for i in range(device_count())])  33.2 us
    ppermute x18, starting transfers between devices, swap(): lax.ppermute(value, BOTH, [(i, i ^ mask) for i in range(device_count())])  16.4 us
    pallas_call x1, Pallas kernels, attend(): pl.pallas_call(functools.partial(attend_body, size, core_mask(), chip_mas...  10.6 us
    ppermute x2, starting transfers between devices, shifted(): return lax.ppermute(value, BOTH, pairs)  4.81 us
    slice x4, local copies, waits for them, and re-layouts, this_core(): shares = [array[:, r * width:(r + 1) * width] for r in range(size)]  2.15 us
    pallas_call x2, Pallas kernels, spread(): pl.pallas_call(functools.partial(spread_body, size, core_mask(), chip_mas...  2 us
  transfers between devices with their start and end apart: 20, of which 12 were waited for; matrix products, arithmetic and copies ran while one was open for 5% of the time, Pallas kernels for 2%

profile of v7, /device:TPU:0, one launch (start us, length us, event | category | flops | bytes accessed | tf_op | source)
XLA Modules:
  0.0 72.0 jit_solution(12251061659015659489)
XLA Ops:
  0.6 0.5 collective-permute-start.5
  1.2 0.4 collective-permute-start
  1.7 1.0 %fusion.3 = (bf16[128,256]{1,0:T(8,128)(2,1)S(1)}, bf16[128,256]{1,0:T(8,128)(2,1)S(1)}, bf16[128,256]{1,0:T(8,128)(2,1)S(1)}, bf16[128,256]{1,0:T(8,128)(2,1)S(1)}) fusion(bf16[128,1024]{1,0:T(8,128)(2,1)} %param.6), kind=kLoop, calls=%fused_computation.10 | loop fusion | bytes 524288 | tf_op jit(solution)/shard_map/slice | solution.py:93
  2.7 1.1 %fusion.1 = (bf16[128,512]{1,0:T(8,128)(2,1)S(1)}, bf16[128,512]{1,0:T(8,128)(2,1)S(1)}, bf16[128,512]{1,0:T(8,128)(2,1)S(1)}, bf16[128,512]{1,0:T(8,128)(2,1)S(1)}) fusion(bf16[128,2048]{1,0:T(8,128)(2,1)} %param.5), kind=kLoop, calls=%fused_computation.8 | loop fusion | bytes 1048576 | tf_op jit(solution)/shard_map/slice | solution.py:93
  4.1 3.0 %collective-permute-start.7 = (bf16[256,256]{1,0:T(8,128)(2,1)S(1)}, bf16[256,256]{1,0:T(8,128)(2,1)S(1)}, u32[]{:S(2)}, u32[]{:S(2)}) collective-permute-start(bf16[256,256]{1,0:T(8,128)(2,1)S(1)} %get-tuple-element.40), channel_id=1, source_target_pairs={{0,1},{1,0},{2,3},{3,2},{4,5},{5,4},{6,7},{7,6},{8,9},{9,8},{10,11... | collective-permute-start | bytes 393224 | tf_op jit(solution)/shard_map/ppermute | solution.py:34
  7.1 1.5 %collective-permute-start.8 = (bf16[256,256]{1,0:T(8,128)(2,1)S(1)}, bf16[256,256]{1,0:T(8,128)(2,1)S(1)}, u32[]{:S(2)}, u32[]{:S(2)}) collective-permute-start(bf16[256,256]{1,0:T(8,128)(2,1)S(1)} %get-tuple-element.41), channel_id=1, source_target_pairs={{0,4},{1,5},{2,6},{3,7},{4,0},{5,1},{6,2},{7,3},{8,12},{9,13},{10,... | collective-permute-start | bytes 393224 | tf_op jit(solution)/shard_map/ppermute | solution.py:34
  8.9 2.1 %collective-permute-done.7.refs_1_ = bf16[256,256]{1,0:T(8,128)(2,1)S(1)} collective-permute-done((bf16[256,256]{1,0:T(8,128)(2,1)S(1)}, bf16[256,256]{1,0:T(8,128)(2,1)S(1)}, u32[]{:S(2)}, u32[]{:S(2)}) %collective-permute-start.7) | collective-permute-done | bytes 131104 | tf_op jit(solution)/shard_map/ppermute | solution.py:34
  11.0 4.1 %collective-permute-done.8.refs_2_ = bf16[256,256]{1,0:T(8,128)(2,1)S(1)} collective-permute-done((bf16[256,256]{1,0:T(8,128)(2,1)S(1)}, bf16[256,256]{1,0:T(8,128)(2,1)S(1)}, u32[]{:S(2)}, u32[]{:S(2)}) %collective-permute-start.8) | collective-permute-done | bytes 131104 | tf_op jit(solution)/shard_map/ppermute | solution.py:34
  15.2 3.5 %collective-permute-start.10 = (bf16[1024,256]{1,0:T(8,128)(2,1)S(1)}, bf16[1024,256]{1,0:T(8,128)(2,1)S(1)}, u32[]{:S(2)}, u32[]{:S(2)}) collective-permute-start(bf16[1024,256]{1,0:T(8,128)(2,1)S(1)} %join.1.refs_5_), channel_id=1, source_target_pairs={{0,8},{1,9},{2,10},{3,11},{4,12},{5,13},{6,14},{7,15},{8,16},{9,17... | collective-permute-start | bytes 1572872 | tf_op jit(solution)/shard_map/ppermute | solution.py:62
  18.8 0.2 stack.2
  19.0 1.3 %collective-permute-start.2 = (bf16[256,512]{1,0:T(8,128)(2,1)S(1)}, bf16[256,512]{1,0:T(8,128)(2,1)S(1)}, u32[]{:S(2)}, u32[]{:S(2)}) collective-permute-start(bf16[256,512]{1,0:T(8,128)(2,1)S(1)} %get-tuple-element.36), channel_id=1, source_target_pairs={{0,1},{1,0},{2,3},{3,2},{4,5},{5,4},{6,7},{7,6},{8,9},{9,8},{10,11... | collective-permute-start | bytes 786440 | tf_op jit(solution)/shard_map/ppermute | solution.py:34
  20.2 0.8 %collective-permute-start.3 = (bf16[256,512]{1,0:T(8,128)(2,1)S(1)}, bf16[256,512]{1,0:T(8,128)(2,1)S(1)}, u32[]{:S(2)}, u32[]{:S(2)}) collective-permute-start(bf16[256,512]{1,0:T(8,128)(2,1)S(1)} %get-tuple-element.37), channel_id=1, source_target_pairs={{0,4},{1,5},{2,6},{3,7},{4,0},{5,1},{6,2},{7,3},{8,12},{9,13},{10,... | collective-permute-start | bytes 786440 | tf_op jit(solution)/shard_map/ppermute | solution.py:34
  21.1 1.4 %collective-permute-start.4 = (bf16[256,512]{1,0:T(8,128)(2,1)S(1)}, bf16[256,512]{1,0:T(8,128)(2,1)S(1)}, u32[]{:S(2)}, u32[]{:S(2)}) collective-permute-start(bf16[256,512]{1,0:T(8,128)(2,1)S(1)} %get-tuple-element.38), channel_id=1, source_target_pairs={{0,5},{1,4},{2,7},{3,6},{4,1},{5,0},{6,3},{7,2},{8,13},{9,12},{10,... | collective-permute-start | bytes 786440 | tf_op jit(solution)/shard_map/ppermute | solution.py:34
  22.5 1.0 %convert_reduce_fusion = s32[1024]{0:T(1024)S(1)} fusion(s32[1024]{0:T(1024)S(1)} %dynamic-slice-done, s32[2048]{0:T(1024)S(1)} %pad_dynamic-slice_fusion), kind=kLoop, calls=%fused_computation | loop fusion | flops 6290432 | bytes 16384 | tf_op jit(solution)/shard_map/reduce_sum | solution.py:372
  23.5 4.8 %collective-permute-done.2.refs_2_ = bf16[256,512]{1,0:T(8,128)(2,1)S(1)} collective-permute-done((bf16[256,512]{1,0:T(8,128)(2,1)S(1)}, bf16[256,512]{1,0:T(8,128)(2,1)S(1)}, u32[]{:S(2)}, u32[]{:S(2)}) %collective-permute-start.2) | collective-permute-done | bytes 262176 | tf_op jit(solution)/shard_map/ppermute | solution.py:34
  28.3 4.5 %collective-permute-done.3.refs_3_ = bf16[256,512]{1,0:T(8,128)(2,1)S(1)} collective-permute-done((bf16[256,512]{1,0:T(8,128)(2,1)S(1)}, bf16[256,512]{1,0:T(8,128)(2,1)S(1)}, u32[]{:S(2)}, u32[]{:S(2)}) %collective-permute-start.3) | collective-permute-done | bytes 262176 | tf_op jit(solution)/shard_map/ppermute | solution.py:34
  32.8 10.6 %attend.1 = (bf16[512,512]{1,0:T(8,128)(2,1)S(1)}, bf16[512,512]{1,0:T(8,128)(2,1)S(1)}, f32[1024,256]{1,0:T(8,128)S(1)}, bf16[1024,256]{1,0:T(8,128)(2,1)S(1)}) custom-call(s32[1,1024]{1,0:T(1,128)S(1)} %add_maximum_fusion.refs_0_, bf16[256,512]{1,0:T(8,128)(2,1)S(1)} %get-tuple-element.35.refs_1_, bf16[256,512]{1,0:T(8,128)(2,1)S(1)} %collective-permute-done.2.refs_2_, ...), custom_call_target="tpu_custom_call" | custom-call | flops 3623878656 | bytes 8388608 | tf_op jit(solution)/shard_map/attend/pallas_call | solution.py:338
  43.5 1.3 %collective-permute-start.15 = (bf16[1024,256]{1,0:T(8,128)(2,1)S(1)}, bf16[1024,256]{1,0:T(8,128)(2,1)S(1)}, u32[]{:S(2)}, u32[]{:S(2)}) collective-permute-start(bf16[1024,256]{1,0:T(8,128)(2,1)S(1)} %get-tuple-element.57), channel_id=1, source_target_pairs={{8,0},{9,1},{10,2},{11,3},{12,4},{13,5},{14,6},{15,7},{16,8},{17,9... | collective-permute-start | bytes 1572872 | tf_op jit(solution)/shard_map/ppermute | solution.py:62
  44.8 0.6 collective-permute-done.11.got
  45.4 0.4 collective-permute-start.12
  45.9 1.4 %collective-permute-start.13 = (bf16[256,512]{1,0:T(8,128)(2,1)S(1)}, bf16[256,512]{1,0:T(8,128)(2,1)S(1)}, u32[]{:S(2)}, u32[]{:S(2)}) collective-permute-start(bf16[256,512]{1,0:T(8,128)(2,1)S(1)} %get-tuple-element.48), channel_id=1, source_target_pairs={{0,4},{1,5},{2,6},{3,7},{4,0},{5,1},{6,2},{7,3},{8,12},{9,13},{10,... | collective-permute-start | bytes 786440 | tf_op jit(solution)/shard_map/ppermute | solution.py:34
  47.3 1.7 %collective-permute-start.14 = (bf16[256,512]{1,0:T(8,128)(2,1)S(1)}, bf16[256,512]{1,0:T(8,128)(2,1)S(1)}, u32[]{:S(2)}, u32[]{:S(2)}) collective-permute-start(bf16[256,512]{1,0:T(8,128)(2,1)S(1)} %get-tuple-element.49), channel_id=1, source_target_pairs={{0,5},{1,4},{2,7},{3,6},{4,1},{5,0},{6,3},{7,2},{8,13},{9,12},{10,... | collective-permute-start | bytes 786440 | tf_op jit(solution)/shard_map/ppermute | solution.py:34
  49.0 5.7 %collective-permute-done.12.refs_1_ = bf16[256,512]{1,0:T(8,128)(2,1)S(1)} collective-permute-done((bf16[256,512]{1,0:T(8,128)(2,1)S(1)}, bf16[256,512]{1,0:T(8,128)(2,1)S(1)}, u32[]{:S(2)}, u32[]{:S(2)}) %collective-permute-start.12) | collective-permute-done | bytes 262176 | tf_op jit(solution)/shard_map/ppermute | solution.py:34
  54.7 4.8 %collective-permute-done.14.refs_3_ = bf16[256,512]{1,0:T(8,128)(2,1)S(1)} collective-permute-done((bf16[256,512]{1,0:T(8,128)(2,1)S(1)}, bf16[256,512]{1,0:T(8,128)(2,1)S(1)}, u32[]{:S(2)}, u32[]{:S(2)}) %collective-permute-start.14) | collective-permute-done | bytes 262176 | tf_op jit(solution)/shard_map/ppermute | solution.py:34
  59.9 1.5 %collective-permute-done.16.got = bf16[512,256]{1,0:T(8,128)(2,1)S(1)} collective-permute-done((bf16[512,256]{1,0:T(8,128)(2,1)S(1)}, bf16[512,256]{1,0:T(8,128)(2,1)S(1)}, u32[]{:S(2)}, u32[]{:S(2)}) %collective-permute-start.16) | collective-permute-done | bytes 262176 | tf_op jit(solution)/shard_map/ppermute | solution.py:34
  61.4 1.6 %collective-permute-start.17 = (bf16[256,256]{1,0:T(8,128)(2,1)S(1)}, bf16[256,256]{1,0:T(8,128)(2,1)S(1)}, u32[]{:S(2)}, u32[]{:S(2)}) collective-permute-start(bf16[256,256]{1,0:T(8,128)(2,1)S(1)} %get-tuple-element.61), channel_id=1, source_target_pairs={{0,1},{1,0},{2,3},{3,2},{4,5},{5,4},{6,7},{7,6},{8,9},{9,8},{10,11... | collective-permute-start | bytes 393224 | tf_op jit(solution)/shard_map/ppermute | solution.py:34
  63.1 0.6 collective-permute-start.18
  63.6 1.4 %collective-permute-start.19 = (bf16[256,256]{1,0:T(8,128)(2,1)S(1)}, bf16[256,256]{1,0:T(8,128)(2,1)S(1)}, u32[]{:S(2)}, u32[]{:S(2)}) collective-permute-start(bf16[256,256]{1,0:T(8,128)(2,1)S(1)} %get-tuple-element.63), channel_id=1, source_target_pairs={{0,5},{1,4},{2,7},{3,6},{4,1},{5,0},{6,3},{7,2},{8,13},{9,12},{10,... | collective-permute-start | bytes 393224 | tf_op jit(solution)/shard_map/ppermute | solution.py:34
  65.0 1.1 %spread.2 = (bf16[128,2048]{1,0:T(8,128)(2,1)}, bf16[128,2048]{1,0:T(8,128)(2,1)}) custom-call(bf16[256,512]{1,0:T(8,128)(2,1)S(1)} %get-tuple-element.50.refs_0_, bf16[256,512]{1,0:T(8,128)(2,1)S(1)} %collective-permute-done.12.refs_1_, bf16[256,512]{1,0:T(8,128)(2,1)S(1)} %collective-permute-done.13.refs_2_, ...), custom_call_target="tpu_custom_call" | custom-call | tf_op jit(solution)/shard_map/spread/pallas_call | solution.py:205
  66.1 1.2 %collective-permute-done.17.refs_1_ = bf16[256,256]{1,0:T(8,128)(2,1)S(1)} collective-permute-done((bf16[256,256]{1,0:T(8,128)(2,1)S(1)}, bf16[256,256]{1,0:T(8,128)(2,1)S(1)}, u32[]{:S(2)}, u32[]{:S(2)}) %collective-permute-start.17) | collective-permute-done | bytes 131104 | tf_op jit(solution)/shard_map/ppermute | solution.py:34
  67.3 3.8 %collective-permute-done.18.refs_2_ = bf16[256,256]{1,0:T(8,128)(2,1)S(1)} collective-permute-done((bf16[256,256]{1,0:T(8,128)(2,1)S(1)}, bf16[256,256]{1,0:T(8,128)(2,1)S(1)}, u32[]{:S(2)}, u32[]{:S(2)}) %collective-permute-start.18) | collective-permute-done | bytes 131104 | tf_op jit(solution)/shard_map/ppermute | solution.py:34
  71.1 0.9 %spread.3 = (bf16[128,1024]{1,0:T(8,128)(2,1)}, bf16[128,1024]{1,0:T(8,128)(2,1)}) custom-call(bf16[256,256]{1,0:T(8,128)(2,1)S(1)} %get-tuple-element.60.refs_0_, bf16[256,256]{1,0:T(8,128)(2,1)S(1)} %collective-permute-done.17.refs_1_, bf16[256,256]{1,0:T(8,128)(2,1)S(1)} %collective-permute-done.18.refs_2_, ...), custom_call_target="tpu_custom_call" | custom-call | tf_op jit(solution)/shard_map/spread/pallas_call | solution.py:205
  (34 shorter events, 1.3 us)
Async XLA Ops:
  0.6 3.2 %copy-start.1 = (bf16[128,1024]{1,0:T(8,128)(2,1)S(1)}, bf16[128,1024]{1,0:T(8,128)(2,1)}, u32[]{:S(2)}) copy-start(bf16[128,1024]{1,0:T(8,128)(2,1)} %param.7) | copy-start | bytes 786436
  0.6 3.4 %collective-permute-start.5 = (bf16[128,1024]{1,0:T(8,128)(2,1)}, bf16[128,1024]{1,0:T(8,128)(2,1)S(1)}, u32[]{:S(2)}, u32[]{:S(2)}) collective-permute-start(bf16[128,1024]{1,0:T(8,128)(2,1)} %param.6), channel_id=1, source_target_pairs={{0,2},{1,3},{2,0},{3,1},{4,6},{5,7},{6,4},{7,5},{8,10},{9,11},{10,... | collective-permute-start | bytes 786440 | tf_op jit(solution)/shard_map/ppermute | solution.py:34
  1.2 2.8 %collective-permute-start.6 = (bf16[128,1024]{1,0:T(8,128)(2,1)}, bf16[128,1024]{1,0:T(8,128)(2,1)S(1)}, u32[]{:S(2)}, u32[]{:S(2)}) collective-permute-start(bf16[128,1024]{1,0:T(8,128)(2,1)} %param.7), channel_id=1, source_target_pairs={{0,2},{1,3},{2,0},{3,1},{4,6},{5,7},{6,4},{7,5},{8,10},{9,11},{10,... | collective-permute-start | bytes 786440 | tf_op jit(solution)/shard_map/ppermute | solution.py:34
  1.2 17.5 %collective-permute-start = (bf16[128,2048]{1,0:T(8,128)(2,1)}, bf16[128,2048]{1,0:T(8,128)(2,1)S(1)}, u32[]{:S(2)}, u32[]{:S(2)}) collective-permute-start(bf16[128,2048]{1,0:T(8,128)(2,1)} %param.5), channel_id=1, source_target_pairs={{0,2},{1,3},{2,0},{3,1},{4,6},{5,7},{6,4},{7,5},{8,10},{9,11},{10,... | collective-permute-start | bytes 1572872 | tf_op jit(solution)/shard_map/ppermute | solution.py:34
  1.7 17.1 %collective-permute-start.1 = (bf16[128,2048]{1,0:T(8,128)(2,1)}, bf16[128,2048]{1,0:T(8,128)(2,1)S(1)}, u32[]{:S(2)}, u32[]{:S(2)}) collective-permute-start(bf16[128,2048]{1,0:T(8,128)(2,1)} %param.8), channel_id=1, source_target_pairs={{0,2},{1,3},{2,0},{3,1},{4,6},{5,7},{6,4},{7,5},{8,10},{9,11},{10,... | collective-permute-start | bytes 1572872 | tf_op jit(solution)/shard_map/ppermute | solution.py:34
  3.9 4.8 %copy-start = (bf16[128,2048]{1,0:T(8,128)(2,1)S(1)}, bf16[128,2048]{1,0:T(8,128)(2,1)}, u32[]{:S(2)}) copy-start(bf16[128,2048]{1,0:T(8,128)(2,1)} %param.8) | copy-start | bytes 1572868
  4.1 6.9 %collective-permute-start.7 = (bf16[256,256]{1,0:T(8,128)(2,1)S(1)}, bf16[256,256]{1,0:T(8,128)(2,1)S(1)}, u32[]{:S(2)}, u32[]{:S(2)}) collective-permute-start(bf16[256,256]{1,0:T(8,128)(2,1)S(1)} %get-tuple-element.40), channel_id=1, source_target_pairs={{0,1},{1,0},{2,3},{3,2},{4,5},{5,4},{6,7},{7,6},{8,9},{9,8},{10,11... | collective-permute-start | bytes 393224 | tf_op jit(solution)/shard_map/ppermute | solution.py:34
  7.1 8.0 %collective-permute-start.8 = (bf16[256,256]{1,0:T(8,128)(2,1)S(1)}, bf16[256,256]{1,0:T(8,128)(2,1)S(1)}, u32[]{:S(2)}, u32[]{:S(2)}) collective-permute-start(bf16[256,256]{1,0:T(8,128)(2,1)S(1)} %get-tuple-element.41), channel_id=1, source_target_pairs={{0,4},{1,5},{2,6},{3,7},{4,0},{5,1},{6,2},{7,3},{8,12},{9,13},{10,... | collective-permute-start | bytes 393224 | tf_op jit(solution)/shard_map/ppermute | solution.py:34
  8.6 6.5 %collective-permute-start.9 = (bf16[256,256]{1,0:T(8,128)(2,1)S(1)}, bf16[256,256]{1,0:T(8,128)(2,1)S(1)}, u32[]{:S(2)}, u32[]{:S(2)}) collective-permute-start(bf16[256,256]{1,0:T(8,128)(2,1)S(1)} %get-tuple-element.42), channel_id=1, source_target_pairs={{0,5},{1,4},{2,7},{3,6},{4,1},{5,0},{6,3},{7,2},{8,13},{9,12},{10,... | collective-permute-start | bytes 393224 | tf_op jit(solution)/shard_map/ppermute | solution.py:34
  8.7 10.0 %copy-start.2 = (s32[4096]{0:T(1024)S(1)}, s32[4096]{0:T(1024)}, u32[]{:S(2)}) copy-start(s32[4096]{0:T(1024)} %param.9) | copy-start | bytes 49156
  15.2 7.3 %dynamic-slice-start = ((s32[4096]{0:T(1024)}, s32[]{:T(128)}), s32[1024]{0:T(1024)S(1)}, s32[]{:S(2)}) async-start(s32[4096]{0:T(1024)} %param.9, s32[]{:T(128)} %select_n.55), calls=%async_computation | async-start | bytes 8704 | tf_op jit(solution)/shard_map/dynamic_slice | solution.py:371
  15.2 17.5 %collective-permute-start.10 = (bf16[1024,256]{1,0:T(8,128)(2,1)S(1)}, bf16[1024,256]{1,0:T(8,128)(2,1)S(1)}, u32[]{:S(2)}, u32[]{:S(2)}) collective-permute-start(bf16[1024,256]{1,0:T(8,128)(2,1)S(1)} %join.1.refs_5_), channel_id=1, source_target_pairs={{0,8},{1,9},{2,10},{3,11},{4,12},{5,13},{6,14},{7,15},{8,16},{9,17... | collective-permute-start | bytes 1572872 | tf_op jit(solution)/shard_map/ppermute | solution.py:62
  19.0 9.3 %collective-permute-start.2 = (bf16[256,512]{1,0:T(8,128)(2,1)S(1)}, bf16[256,512]{1,0:T(8,128)(2,1)S(1)}, u32[]{:S(2)}, u32[]{:S(2)}) collective-permute-start(bf16[256,512]{1,0:T(8,128)(2,1)S(1)} %get-tuple-element.36), channel_id=1, source_target_pairs={{0,1},{1,0},{2,3},{3,2},{4,5},{5,4},{6,7},{7,6},{8,9},{9,8},{10,11... | collective-permute-start | bytes 786440 | tf_op jit(solution)/shard_map/ppermute | solution.py:34
  20.2 12.5 %collective-permute-start.3 = (bf16[256,512]{1,0:T(8,128)(2,1)S(1)}, bf16[256,512]{1,0:T(8,128)(2,1)S(1)}, u32[]{:S(2)}, u32[]{:S(2)}) collective-permute-start(bf16[256,512]{1,0:T(8,128)(2,1)S(1)} %get-tuple-element.37), channel_id=1, source_target_pairs={{0,4},{1,5},{2,6},{3,7},{4,0},{5,1},{6,2},{7,3},{8,12},{9,13},{10,... | collective-permute-start | bytes 786440 | tf_op jit(solution)/shard_map/ppermute | solution.py:34
  21.1 11.7 %collective-permute-start.4 = (bf16[256,512]{1,0:T(8,128)(2,1)S(1)}, bf16[256,512]{1,0:T(8,128)(2,1)S(1)}, u32[]{:S(2)}, u32[]{:S(2)}) collective-permute-start(bf16[256,512]{1,0:T(8,128)(2,1)S(1)} %get-tuple-element.38), channel_id=1, source_target_pairs={{0,5},{1,4},{2,7},{3,6},{4,1},{5,0},{6,3},{7,2},{8,13},{9,12},{10,... | collective-permute-start | bytes 786440 | tf_op jit(solution)/shard_map/ppermute | solution.py:34
  43.4 2.0 %collective-permute-start.11 = (bf16[512,512]{1,0:T(8,128)(2,1)S(1)}, bf16[512,512]{1,0:T(8,128)(2,1)S(1)}, u32[]{:S(2)}, u32[]{:S(2)}) collective-permute-start(bf16[512,512]{1,0:T(8,128)(2,1)S(1)} %get-tuple-element.45), channel_id=1, source_target_pairs={{0,2},{1,3},{2,0},{3,1},{4,6},{5,7},{6,4},{7,5},{8,10},{9,11},{10,... | collective-permute-start | bytes 1572872 | tf_op jit(solution)/shard_map/ppermute | solution.py:34
  43.5 16.2 %collective-permute-start.15 = (bf16[1024,256]{1,0:T(8,128)(2,1)S(1)}, bf16[1024,256]{1,0:T(8,128)(2,1)S(1)}, u32[]{:S(2)}, u32[]{:S(2)}) collective-permute-start(bf16[1024,256]{1,0:T(8,128)(2,1)S(1)} %get-tuple-element.57), channel_id=1, source_target_pairs={{8,0},{9,1},{10,2},{11,3},{12,4},{13,5},{14,6},{15,7},{16,8},{17,9... | collective-permute-start | bytes 1572872 | tf_op jit(solution)/shard_map/ppermute | solution.py:62
  45.4 9.2 %collective-permute-start.12 = (bf16[256,512]{1,0:T(8,128)(2,1)S(1)}, bf16[256,512]{1,0:T(8,128)(2,1)S(1)}, u32[]{:S(2)}, u32[]{:S(2)}) collective-permute-start(bf16[256,512]{1,0:T(8,128)(2,1)S(1)} %get-tuple-element.47), channel_id=1, source_target_pairs={{0,1},{1,0},{2,3},{3,2},{4,5},{5,4},{6,7},{7,6},{8,9},{9,8},{10,11... | collective-permute-start | bytes 786440 | tf_op jit(solution)/shard_map/ppermute | solution.py:34
  45.9 8.9 %collective-permute-start.13 = (bf16[256,512]{1,0:T(8,128)(2,1)S(1)}, bf16[256,512]{1,0:T(8,128)(2,1)S(1)}, u32[]{:S(2)}, u32[]{:S(2)}) collective-permute-start(bf16[256,512]{1,0:T(8,128)(2,1)S(1)} %get-tuple-element.48), channel_id=1, source_target_pairs={{0,4},{1,5},{2,6},{3,7},{4,0},{5,1},{6,2},{7,3},{8,12},{9,13},{10,... | collective-permute-start | bytes 786440 | tf_op jit(solution)/shard_map/ppermute | solution.py:34
  47.3 12.2 %collective-permute-start.14 = (bf16[256,512]{1,0:T(8,128)(2,1)S(1)}, bf16[256,512]{1,0:T(8,128)(2,1)S(1)}, u32[]{:S(2)}, u32[]{:S(2)}) collective-permute-start(bf16[256,512]{1,0:T(8,128)(2,1)S(1)} %get-tuple-element.49), channel_id=1, source_target_pairs={{0,5},{1,4},{2,7},{3,6},{4,1},{5,0},{6,3},{7,2},{8,13},{9,12},{10,... | collective-permute-start | bytes 786440 | tf_op jit(solution)/shard_map/ppermute | solution.py:34
  59.8 1.6 %collective-permute-start.16 = (bf16[512,256]{1,0:T(8,128)(2,1)S(1)}, bf16[512,256]{1,0:T(8,128)(2,1)S(1)}, u32[]{:S(2)}, u32[]{:S(2)}) collective-permute-start(bf16[512,256]{1,0:T(8,128)(2,1)S(1)} %get-tuple-element.59), channel_id=1, source_target_pairs={{0,2},{1,3},{2,0},{3,1},{4,6},{5,7},{6,4},{7,5},{8,10},{9,11},{10,... | collective-permute-start | bytes 786440 | tf_op jit(solution)/shard_map/ppermute | solution.py:34
  61.4 5.9 %collective-permute-start.17 = (bf16[256,256]{1,0:T(8,128)(2,1)S(1)}, bf16[256,256]{1,0:T(8,128)(2,1)S(1)}, u32[]{:S(2)}, u32[]{:S(2)}) collective-permute-start(bf16[256,256]{1,0:T(8,128)(2,1)S(1)} %get-tuple-element.61), channel_id=1, source_target_pairs={{0,1},{1,0},{2,3},{3,2},{4,5},{5,4},{6,7},{7,6},{8,9},{9,8},{10,11... | collective-permute-start | bytes 393224 | tf_op jit(solution)/shard_map/ppermute | solution.py:34
  63.1 8.1 %collective-permute-start.18 = (bf16[256,256]{1,0:T(8,128)(2,1)S(1)}, bf16[256,256]{1,0:T(8,128)(2,1)S(1)}, u32[]{:S(2)}, u32[]{:S(2)}) collective-permute-start(bf16[256,256]{1,0:T(8,128)(2,1)S(1)} %get-tuple-element.62), channel_id=1, source_target_pairs={{0,4},{1,5},{2,6},{3,7},{4,0},{5,1},{6,2},{7,3},{8,12},{9,13},{10,... | collective-permute-start | bytes 393224 | tf_op jit(solution)/shard_map/ppermute | solution.py:34
  63.6 7.5 %collective-permute-start.19 = (bf16[256,256]{1,0:T(8,128)(2,1)S(1)}, bf16[256,256]{1,0:T(8,128)(2,1)S(1)}, u32[]{:S(2)}, u32[]{:S(2)}) collective-permute-start(bf16[256,256]{1,0:T(8,128)(2,1)S(1)} %get-tuple-element.63), channel_id=1, source_target_pairs={{0,5},{1,4},{2,7},{3,6},{4,1},{5,0},{6,3},{7,2},{8,13},{9,12},{10,... | collective-permute-start | bytes 393224 | tf_op jit(solution)/shard_map/ppermute | solution.py:34

commit v8 on v7

--- a/solution.py
+++ b/solution.py
@@ -39,7 +39,8 @@
 
 
 def chip_masks(size):
-    return [mask for mask in range(size) if not mask & core_mask()]
+    masks = [mask for mask in range(size) if not mask & core_mask()]
+    return masks[:1] + sorted(masks[1:], key=lambda mask: -mask.bit_count())
 
 
 def swap_chips(pieces, size):
@@ -48,18 +49,26 @@
     ]
 
 
+def hop(value, step):
+    count = device_count()
+    results = []
+    for odd in (0, 1):
+        low = [i for i in range(count - step) if (i // step) % 2 == odd]
+        pairs = [(i, i + step) for i in low] + [(i + step, i) for i in low]
+        results.append(lax.ppermute(value, BOTH, pairs))
+    return results
+
+
+def from_odd(step):
+    return lax.rem(lax.div(flat_index(), step), 2) == 1
+
+
 def partner(size, j):
     return lax.bitwise_xor(lax.rem(flat_index(), size), j)
 
 
 def place(index, width):
     return pl.ds(pl.multiple_of(index * width, width), width)
-
-
-def shifted(value, step):
-    count = device_count()
-    pairs = [(i, i + step) for i in range(count) if 0 <= i + step < count]
-    return lax.ppermute(value, BOTH, pairs)
 
 
 def after(value, *others):
@@ -112,9 +121,8 @@
             start += width
 
 
-def gather_cores(arrays, size):
+def gather_cores(arrays, got, size):
     masks = chip_masks(size)
-    got = [swap(array, core_mask()) for array in arrays]
     own = [this_core(array, size) for array in arrays]
     cols = sum(array.shape[1] // size for array in arrays)
     piece = jax.ShapeDtypeStruct((2 * arrays[0].shape[0], cols), BF16)
@@ -148,23 +156,23 @@
     return small_call(kernel, out, "join", *pieces)
 
 
-def combine(terms, size):
-    tok, cols = terms[0].shape
+def combine(own, backs, size):
+    tok, cols = own.shape
     core, masks = core_mask(), chip_masks(size)
 
     def kernel(*refs):
-        added = refs[: len(terms)]
-
         def source(there):
-            total = added[0][there, :]
-            for term in added[1:]:
-                total = total + term[there, :].astype(F32)
+            total = refs[0][there, :]
+            for lag in range(1, len(backs) + 1):
+                first, second = refs[2 * lag - 1], refs[2 * lag]
+                odd = from_odd(lag * size)
+                total = total + jnp.where(odd, second[there, :], first[there, :]).astype(F32)
             return total.astype(BF16)
 
-        take_rows(size, core, masks, source, *refs[len(terms) :])
+        take_rows(size, core, masks, source, *refs[-2:])
 
     half = jax.ShapeDtypeStruct((tok // 2, cols), BF16)
-    return small_call(kernel, [half] * 2, "combine", *terms)
+    return small_call(kernel, [half] * 2, "combine", own, *sum(backs, []))
 
 
 def pair_body(own, got, *pieces):
@@ -234,7 +242,7 @@
 def attend_body(size, core, masks, reach, tok, group, *refs):
     refs = list(refs)
     take = lambda count: [refs.pop(0) for _ in range(count)]
-    (low,), qg_pieces, kvs = take(1), take(len(masks)), take(1 + reach)
+    (low,), qg_pieces, kvs = take(1), take(len(masks)), take(1 + 2 * reach)
     og_halves, (dkv0,), sent = take(2), take(1), take(reach)
     qg, og, ks, va, kt, vt, dk, dv, s_scr, e_scr, ds_scr = refs
     width = group * HEAD_DIM
@@ -245,10 +253,15 @@
     ).astype(BF16)
     for lag in range(reach + 1):
         there = slice((reach - lag) * tok, (reach - lag + 1) * tok)
-        ks[there, :] = kvs[lag][:, :HEAD_DIM]
-        va[there, :HEAD_DIM] = kvs[lag][:, HEAD_DIM:]
-        kt[:, there] = kvs[lag][:, :HEAD_DIM].T
-        vt[:, there] = kvs[lag][:, HEAD_DIM:].T
+        if lag:
+            odd = from_odd(lag * size)
+            kv = jnp.where(odd, kvs[2 * lag - 1][...], kvs[2 * lag][...])
+        else:
+            kv = kvs[0][...]
+        ks[there, :] = kv[:, :HEAD_DIM]
+        va[there, :HEAD_DIM] = kv[:, HEAD_DIM:]
+        kt[:, there] = kv[:, :HEAD_DIM].T
+        vt[:, there] = kv[:, HEAD_DIM:].T
     dk[...] = jnp.zeros_like(dk)
     dv[...] = jnp.zeros_like(dv)
     wide_lane = lax.broadcasted_iota(jnp.int32, (group * TILE, HEAD_DIM), 1)
@@ -324,11 +337,11 @@
     take_rows(size, core, masks, lambda there: og[there, :], *og_halves)
 
 
-def attend(low, qg, kvs, size):
+def attend(low, qg, kv, lags, size):
     rows, cols = qg[0].shape
     tok = len(qg) * rows
     group = cols // (2 * HEAD_DIM)
-    reach = len(kvs) - 1
+    reach = len(lags)
     span = WINDOW + TILE
     wide = group * TILE
     keys = (reach + 1) * tok
@@ -340,7 +353,7 @@
         out_shape=[jax.ShapeDtypeStruct((tok // 2, cols), BF16)] * 2
         + [jax.ShapeDtypeStruct((tok, 2 * HEAD_DIM), F32)]
         + [half] * reach,
-        in_specs=[VMEM] * (count + 2 + reach),
+        in_specs=[VMEM] * (count + 2 + 2 * reach),
         out_specs=[VMEM] * (3 + reach),
         scratch_shapes=[
             pltpu.VMEM((tok, cols), BF16),
@@ -360,7 +373,7 @@
             flops=flops, bytes_accessed=8 * 1024 * 1024, transcendentals=flops // 1536
         ),
         name="attend",
-    )(low, *qg, *kvs)
+    )(low, *qg, kv, *sum(lags, []))
     return results[:2], results[2], results[3:]
 
 
@@ -381,15 +394,18 @@
     assert reach * tok == WINDOW and device_count() % size == 0
     low = lowest_key(segment_ids, tok, size)
 
-    kv = join(swap_chips(gather_cores((key, value), size), size), size)
-    qg = swap_chips(gather_cores((query, grad_out), size), size)
-    kvs = [kv] + [shifted(kv, lag * size) for lag in range(1, reach + 1)]
-
-    og, dkv, sent = attend(low, qg, kvs, size)
-
-    back = [shifted(sent[lag - 1], -lag * size) for lag in range(1, reach + 1)]
+    got = [swap(array, core_mask()) for array in (key, value, query, grad_out)]
+    pieces = list(gather_cores((key, value), got[:2], size))
+    pieces[0], query, grad_out = after(pieces[0], query, grad_out)
+    kv = join(swap_chips(pieces, size), size)
+    lags = [hop(kv, lag * size) for lag in range(1, reach + 1)]
+    qg = swap_chips(gather_cores((query, grad_out), got[2:], size), size)
+
+    og, dkv, sent = attend(low, qg, kv, lags, size)
+
+    backs = [hop(sent[lag - 1], lag * size) for lag in range(1, reach + 1)]
     dkv, *og = after(dkv, *scatter(*og, size))
-    grads = scatter(*combine([dkv] + back, size), size)
+    grads = scatter(*combine(dkv, backs, size), size)
     attn_out, grad_query = spread(og, size, 2)
     grad_key, grad_value = spread(grads, size, 2)
     return (attn_out, grad_query, grad_key, grad_value)

time: 72.3 us -> 75.1 us (1.039)
  starting transfers between devices: 21.2 us -> 24.3 us
    ppermute x2 -> x4, starting transfers between devices: 4.81 us -> 7.84 us  [hop(): results.append(lax.ppermute(value, BOTH, pairs))]
  transfers between devices with their start and end apart: 20 -> 22, of which waited for: 12 -> 10; matrix products, arithmetic and copies ran while one was open for 5% -> 4% of each run, Pallas kernels for 2% -> 2%
where the time goes in v8:
time: 75.1 us; the launch traced here: 74.9 us
  waiting for transfers between devices  33.2 us (44%)
  starting transfers between devices  24.3 us (32%)
  Pallas kernels  13.2 us (18%)
  local copies, waits for them, and re-layouts  2.09 us (3%)
  other arithmetic  1.18 us (2%)
  between operations  0.94 us (1%)
    ppermute x18, waiting for transfers between devices, swap(): lax.ppermute(value, BOTH, [(i, i ^ mask) for i in range(device_count())])  33.1 us
    ppermute x18, starting transfers between devices, swap(): lax.ppermute(value, BOTH, [(i, i ^ mask) for i in range(device_count())])  16.5 us
    pallas_call x1, Pallas kernels, attend(): pl.pallas_call(functools.partial(attend_body, size, core_mask(), chip_mas...  10.6 us
    ppermute x4, starting transfers between devices, hop(): results.append(lax.ppermute(value, BOTH, pairs))  7.84 us
    slice x4, local copies, waits for them, and re-layouts, this_core(): shares = [array[:, r * width:(r + 1) * width] for r in range(size)]  2.05 us
    pallas_call x2, Pallas kernels, spread(): pl.pallas_call(functools.partial(spread_body, size, core_mask(), chip_mas...  2 us
  transfers between devices with their start and end apart: 22, of which 10 were waited for; matrix products, arithmetic and copies ran while one was open for 4% of the time, Pallas kernels for 2%

profile of v8, /device:TPU:0, one launch (start us, length us, event | category | flops | bytes accessed | tf_op | source)
XLA Modules:
  0.0 74.9 jit_solution(1104731516979969238)
XLA Ops:
  0.6 0.5 collective-permute-start
  1.2 0.4 collective-permute-start.2
  1.8 1.0 %fusion.3 = (bf16[128,256]{1,0:T(8,128)(2,1)S(1)}, bf16[128,256]{1,0:T(8,128)(2,1)S(1)}, bf16[128,256]{1,0:T(8,128)(2,1)S(1)}, bf16[128,256]{1,0:T(8,128)(2,1)S(1)}) fusion(bf16[128,1024]{1,0:T(8,128)(2,1)} %param.6), kind=kLoop, calls=%fused_computation.10 | loop fusion | bytes 524288 | tf_op jit(solution)/shard_map/slice | solution.py:102
  2.7 1.0 %fusion.2 = (bf16[128,256]{1,0:T(8,128)(2,1)S(1)}, bf16[128,256]{1,0:T(8,128)(2,1)S(1)}, bf16[128,256]{1,0:T(8,128)(2,1)S(1)}, bf16[128,256]{1,0:T(8,128)(2,1)S(1)}) fusion(bf16[128,1024]{1,0:T(8,128)(2,1)} %param.7), kind=kLoop, calls=%fused_computation.9 | loop fusion | bytes 524288 | tf_op jit(solution)/shard_map/slice | solution.py:102
  4.1 3.9 %collective-permute-start.7 = (bf16[256,256]{1,0:T(8,128)(2,1)S(1)}, bf16[256,256]{1,0:T(8,128)(2,1)S(1)}, u32[]{:S(2)}, u32[]{:S(2)}) collective-permute-start(bf16[256,256]{1,0:T(8,128)(2,1)S(1)} %get-tuple-element.46), channel_id=1, source_target_pairs={{0,5},{1,4},{2,7},{3,6},{4,1},{5,0},{6,3},{7,2},{8,13},{9,12},{10,... | collective-permute-start | bytes 393224 | tf_op jit(solution)/shard_map/ppermute | solution.py:34
  8.0 0.5 collective-permute-start.8
  8.8 3.5 %collective-permute-done.7.refs_1_ = bf16[256,256]{1,0:T(8,128)(2,1)S(1)} collective-permute-done((bf16[256,256]{1,0:T(8,128)(2,1)S(1)}, bf16[256,256]{1,0:T(8,128)(2,1)S(1)}, u32[]{:S(2)}, u32[]{:S(2)}) %collective-permute-start.7) | collective-permute-done | bytes 131104 | tf_op jit(solution)/shard_map/ppermute | solution.py:34
  12.3 2.5 %collective-permute-done.8.refs_2_ = bf16[256,256]{1,0:T(8,128)(2,1)S(1)} collective-permute-done((bf16[256,256]{1,0:T(8,128)(2,1)S(1)}, bf16[256,256]{1,0:T(8,128)(2,1)S(1)}, u32[]{:S(2)}, u32[]{:S(2)}) %collective-permute-start.8) | collective-permute-done | bytes 131104 | tf_op jit(solution)/shard_map/ppermute | solution.py:34
  14.9 0.7 collective-permute-start.11
  15.6 4.4 %collective-permute-start.10 = (bf16[1024,256]{1,0:T(8,128)(2,1)S(1)}, bf16[1024,256]{1,0:T(8,128)(2,1)S(1)}, u32[]{:S(2)}, u32[]{:S(2)}) collective-permute-start(bf16[1024,256]{1,0:T(8,128)(2,1)S(1)} %join.1.refs_5_), channel_id=1, source_target_pairs={{0,8},{1,9},{2,10},{3,11},{4,12},{5,13},{6,14},{7,15},{16,24},{17,... | collective-permute-start | bytes 1572872 | tf_op jit(solution)/shard_map/ppermute | solution.py:58
  20.4 2.5 %collective-permute-start.4 = (bf16[256,512]{1,0:T(8,128)(2,1)S(1)}, bf16[256,512]{1,0:T(8,128)(2,1)S(1)}, u32[]{:S(2)}, u32[]{:S(2)}) collective-permute-start(bf16[256,512]{1,0:T(8,128)(2,1)S(1)} %get-tuple-element.42), channel_id=1, source_target_pairs={{0,5},{1,4},{2,7},{3,6},{4,1},{5,0},{6,3},{7,2},{8,13},{9,12},{10,... | collective-permute-start | bytes 786440 | tf_op jit(solution)/shard_map/ppermute | solution.py:34
  22.8 0.5 collective-permute-start.5
  23.3 0.6 collective-permute-start.6
  23.9 1.0 %convert_reduce_fusion = s32[1024]{0:T(1024)S(1)} fusion(s32[1024]{0:T(1024)S(1)} %dynamic-slice-done, s32[2048]{0:T(1024)S(1)} %pad_dynamic-slice_fusion), kind=kLoop, calls=%fused_computation | loop fusion | flops 6290432 | bytes 16384 | tf_op jit(solution)/shard_map/reduce_sum | solution.py:385
  24.9 5.7 %collective-permute-done.4.refs_2_ = bf16[256,512]{1,0:T(8,128)(2,1)S(1)} collective-permute-done((bf16[256,512]{1,0:T(8,128)(2,1)S(1)}, bf16[256,512]{1,0:T(8,128)(2,1)S(1)}, u32[]{:S(2)}, u32[]{:S(2)}) %collective-permute-start.4) | collective-permute-done | bytes 262176 | tf_op jit(solution)/shard_map/ppermute | solution.py:34
  30.6 4.0 %collective-permute-done.5.refs_3_ = bf16[256,512]{1,0:T(8,128)(2,1)S(1)} collective-permute-done((bf16[256,512]{1,0:T(8,128)(2,1)S(1)}, bf16[256,512]{1,0:T(8,128)(2,1)S(1)}, u32[]{:S(2)}, u32[]{:S(2)}) %collective-permute-start.5) | collective-permute-done | bytes 262176 | tf_op jit(solution)/shard_map/ppermute | solution.py:34
  34.7 10.6 %attend.1 = (bf16[512,512]{1,0:T(8,128)(2,1)S(1)}, bf16[512,512]{1,0:T(8,128)(2,1)S(1)}, f32[1024,256]{1,0:T(8,128)S(1)}, bf16[1024,256]{1,0:T(8,128)(2,1)S(1)}) custom-call(s32[1,1024]{1,0:T(1,128)S(1)} %add_maximum_fusion.refs_0_, bf16[256,512]{1,0:T(8,128)(2,1)S(1)} %get-tuple-element.41.refs_1_, bf16[256,512]{1,0:T(8,128)(2,1)S(1)} %collective-permute-done.4.refs_2_, ...), custom_call_target="tpu_custom_call" | custom-call | flops 3623878656 | bytes 8388608 | tf_op jit(solution)/shard_map/attend/pallas_call | solution.py:351
  45.3 0.7 collective-permute-start.17
  46.0 2.0 %collective-permute-start.16 = (bf16[1024,256]{1,0:T(8,128)(2,1)S(1)}, bf16[1024,256]{1,0:T(8,128)(2,1)S(1)}, u32[]{:S(2)}, u32[]{:S(2)}) collective-permute-start(bf16[1024,256]{1,0:T(8,128)(2,1)S(1)} %get-tuple-element.63), channel_id=1, source_target_pairs={{0,8},{1,9},{2,10},{3,11},{4,12},{5,13},{6,14},{7,15},{16,24},{17,... | collective-permute-start | bytes 1572872 | tf_op jit(solution)/shard_map/ppermute | solution.py:58
  48.1 2.4 %collective-permute-start.13 = (bf16[256,512]{1,0:T(8,128)(2,1)S(1)}, bf16[256,512]{1,0:T(8,128)(2,1)S(1)}, u32[]{:S(2)}, u32[]{:S(2)}) collective-permute-start(bf16[256,512]{1,0:T(8,128)(2,1)S(1)} %get-tuple-element.53), channel_id=1, source_target_pairs={{0,5},{1,4},{2,7},{3,6},{4,1},{5,0},{6,3},{7,2},{8,13},{9,12},{10,... | collective-permute-start | bytes 786440 | tf_op jit(solution)/shard_map/ppermute | solution.py:34
  50.5 0.5 collective-permute-start.14
  51.1 0.6 collective-permute-start.15
  51.7 6.6 %collective-permute-done.13.refs_1_ = bf16[256,512]{1,0:T(8,128)(2,1)S(1)} collective-permute-done((bf16[256,512]{1,0:T(8,128)(2,1)S(1)}, bf16[256,512]{1,0:T(8,128)(2,1)S(1)}, u32[]{:S(2)}, u32[]{:S(2)}) %collective-permute-start.13) | collective-permute-done | bytes 262176 | tf_op jit(solution)/shard_map/ppermute | solution.py:34
  58.3 4.5 %collective-permute-done.14.refs_2_ = bf16[256,512]{1,0:T(8,128)(2,1)S(1)} collective-permute-done((bf16[256,512]{1,0:T(8,128)(2,1)S(1)}, bf16[256,512]{1,0:T(8,128)(2,1)S(1)}, u32[]{:S(2)}, u32[]{:S(2)}) %collective-permute-start.14) | collective-permute-done | bytes 262176 | tf_op jit(solution)/shard_map/ppermute | solution.py:34
  63.1 1.5 %collective-permute-done.18.got = bf16[512,256]{1,0:T(8,128)(2,1)S(1)} collective-permute-done((bf16[512,256]{1,0:T(8,128)(2,1)S(1)}, bf16[512,256]{1,0:T(8,128)(2,1)S(1)}, u32[]{:S(2)}, u32[]{:S(2)}) %collective-permute-start.18) | collective-permute-done | bytes 262176 | tf_op jit(solution)/shard_map/ppermute | solution.py:34
  64.7 2.4 %collective-permute-start.19 = (bf16[256,256]{1,0:T(8,128)(2,1)S(1)}, bf16[256,256]{1,0:T(8,128)(2,1)S(1)}, u32[]{:S(2)}, u32[]{:S(2)}) collective-permute-start(bf16[256,256]{1,0:T(8,128)(2,1)S(1)} %get-tuple-element.67), channel_id=1, source_target_pairs={{0,5},{1,4},{2,7},{3,6},{4,1},{5,0},{6,3},{7,2},{8,13},{9,12},{10,... | collective-permute-start | bytes 393224 | tf_op jit(solution)/shard_map/ppermute | solution.py:34
  67.1 0.5 collective-permute-start.20
  67.6 0.6 collective-permute-start.21
  68.2 1.1 %spread.2 = (bf16[128,2048]{1,0:T(8,128)(2,1)}, bf16[128,2048]{1,0:T(8,128)(2,1)}) custom-call(bf16[256,512]{1,0:T(8,128)(2,1)S(1)} %get-tuple-element.56.refs_0_, bf16[256,512]{1,0:T(8,128)(2,1)S(1)} %collective-permute-done.13.refs_1_, bf16[256,512]{1,0:T(8,128)(2,1)S(1)} %collective-permute-done.14.refs_2_, ...), custom_call_target="tpu_custom_call" | custom-call | tf_op jit(solution)/shard_map/spread/pallas_call | solution.py:213
  69.3 2.7 %collective-permute-done.19.refs_1_ = bf16[256,256]{1,0:T(8,128)(2,1)S(1)} collective-permute-done((bf16[256,256]{1,0:T(8,128)(2,1)S(1)}, bf16[256,256]{1,0:T(8,128)(2,1)S(1)}, u32[]{:S(2)}, u32[]{:S(2)}) %collective-permute-start.19) | collective-permute-done | bytes 131104 | tf_op jit(solution)/shard_map/ppermute | solution.py:34
  72.0 1.9 %collective-permute-done.20.refs_2_ = bf16[256,256]{1,0:T(8,128)(2,1)S(1)} collective-permute-done((bf16[256,256]{1,0:T(8,128)(2,1)S(1)}, bf16[256,256]{1,0:T(8,128)(2,1)S(1)}, u32[]{:S(2)}, u32[]{:S(2)}) %collective-permute-start.20) | collective-permute-done | bytes 131104 | tf_op jit(solution)/shard_map/ppermute | solution.py:34
  74.0 0.9 %spread.3 = (bf16[128,1024]{1,0:T(8,128)(2,1)}, bf16[128,1024]{1,0:T(8,128)(2,1)}) custom-call(bf16[256,256]{1,0:T(8,128)(2,1)S(1)} %get-tuple-element.66.refs_0_, bf16[256,256]{1,0:T(8,128)(2,1)S(1)} %collective-permute-done.19.refs_1_, bf16[256,256]{1,0:T(8,128)(2,1)S(1)} %collective-permute-done.20.refs_2_, ...), custom_call_target="tpu_custom_call" | custom-call | tf_op jit(solution)/shard_map/spread/pallas_call | solution.py:213
  (39 shorter events, 1.4 us)
Async XLA Ops:
  0.6 3.1 %copy-start.2 = (s32[4096]{0:T(1024)S(1)}, s32[4096]{0:T(1024)}, u32[]{:S(2)}) copy-start(s32[4096]{0:T(1024)} %param.9) | copy-start | bytes 49156
  0.6 3.3 %collective-permute-start = (bf16[128,1024]{1,0:T(8,128)(2,1)}, bf16[128,1024]{1,0:T(8,128)(2,1)S(1)}, u32[]{:S(2)}, u32[]{:S(2)}) collective-permute-start(bf16[128,1024]{1,0:T(8,128)(2,1)} %param.6), channel_id=1, source_target_pairs={{0,2},{1,3},{2,0},{3,1},{4,6},{5,7},{6,4},{7,5},{8,10},{9,11},{10,... | collective-permute-start | bytes 786440 | tf_op jit(solution)/shard_map/ppermute | solution.py:34
  1.2 2.8 %collective-permute-start.1 = (bf16[128,1024]{1,0:T(8,128)(2,1)}, bf16[128,1024]{1,0:T(8,128)(2,1)S(1)}, u32[]{:S(2)}, u32[]{:S(2)}) collective-permute-start(bf16[128,1024]{1,0:T(8,128)(2,1)} %param.7), channel_id=1, source_target_pairs={{0,2},{1,3},{2,0},{3,1},{4,6},{5,7},{6,4},{7,5},{8,10},{9,11},{10,... | collective-permute-start | bytes 786440 | tf_op jit(solution)/shard_map/ppermute | solution.py:34
  1.2 18.9 %collective-permute-start.2 = (bf16[128,2048]{1,0:T(8,128)(2,1)}, bf16[128,2048]{1,0:T(8,128)(2,1)S(1)}, u32[]{:S(2)}, u32[]{:S(2)}) collective-permute-start(bf16[128,2048]{1,0:T(8,128)(2,1)} %param.5), channel_id=1, source_target_pairs={{0,2},{1,3},{2,0},{3,1},{4,6},{5,7},{6,4},{7,5},{8,10},{9,11},{10,... | collective-permute-start | bytes 1572872 | tf_op jit(solution)/shard_map/ppermute | solution.py:34
  1.7 18.5 %collective-permute-start.3 = (bf16[128,2048]{1,0:T(8,128)(2,1)}, bf16[128,2048]{1,0:T(8,128)(2,1)S(1)}, u32[]{:S(2)}, u32[]{:S(2)}) collective-permute-start(bf16[128,2048]{1,0:T(8,128)(2,1)} %param.8), channel_id=1, source_target_pairs={{0,2},{1,3},{2,0},{3,1},{4,6},{5,7},{6,4},{7,5},{8,10},{9,11},{10,... | collective-permute-start | bytes 1572872 | tf_op jit(solution)/shard_map/ppermute | solution.py:34
  2.7 6.0 %copy-start = (bf16[128,2048]{1,0:T(8,128)(2,1)S(1)}, bf16[128,2048]{1,0:T(8,128)(2,1)}, u32[]{:S(2)}) copy-start(bf16[128,2048]{1,0:T(8,128)(2,1)} %param.5) | copy-start | bytes 1572868
  3.9 4.8 %copy-start.1 = (bf16[128,2048]{1,0:T(8,128)(2,1)S(1)}, bf16[128,2048]{1,0:T(8,128)(2,1)}, u32[]{:S(2)}) copy-start(bf16[128,2048]{1,0:T(8,128)(2,1)} %param.8) | copy-start | bytes 1572868
  4.1 8.2 %collective-permute-start.7 = (bf16[256,256]{1,0:T(8,128)(2,1)S(1)}, bf16[256,256]{1,0:T(8,128)(2,1)S(1)}, u32[]{:S(2)}, u32[]{:S(2)}) collective-permute-start(bf16[256,256]{1,0:T(8,128)(2,1)S(1)} %get-tuple-element.46), channel_id=1, source_target_pairs={{0,5},{1,4},{2,7},{3,6},{4,1},{5,0},{6,3},{7,2},{8,13},{9,12},{10,... | collective-permute-start | bytes 393224 | tf_op jit(solution)/shard_map/ppermute | solution.py:34
  8.0 6.8 %collective-permute-start.8 = (bf16[256,256]{1,0:T(8,128)(2,1)S(1)}, bf16[256,256]{1,0:T(8,128)(2,1)S(1)}, u32[]{:S(2)}, u32[]{:S(2)}) collective-permute-start(bf16[256,256]{1,0:T(8,128)(2,1)S(1)} %get-tuple-element.47), channel_id=1, source_target_pairs={{0,1},{1,0},{2,3},{3,2},{4,5},{5,4},{6,7},{7,6},{8,9},{9,8},{10,11... | collective-permute-start | bytes 393224 | tf_op jit(solution)/shard_map/ppermute | solution.py:34
  8.6 6.3 %collective-permute-start.9 = (bf16[256,256]{1,0:T(8,128)(2,1)S(1)}, bf16[256,256]{1,0:T(8,128)(2,1)S(1)}, u32[]{:S(2)}, u32[]{:S(2)}) collective-permute-start(bf16[256,256]{1,0:T(8,128)(2,1)S(1)} %get-tuple-element.48), channel_id=1, source_target_pairs={{0,4},{1,5},{2,6},{3,7},{4,0},{5,1},{6,2},{7,3},{8,12},{9,13},{10,... | collective-permute-start | bytes 393224 | tf_op jit(solution)/shard_map/ppermute | solution.py:34
  14.9 19.8 %collective-permute-start.11 = (bf16[1024,256]{1,0:T(8,128)(2,1)S(1)}, bf16[1024,256]{1,0:T(8,128)(2,1)S(1)}, u32[]{:S(2)}, u32[]{:S(2)}) collective-permute-start(bf16[1024,256]{1,0:T(8,128)(2,1)S(1)} %join.1.refs_5_), channel_id=1, source_target_pairs={{8,16},{9,17},{10,18},{11,19},{12,20},{13,21},{14,22},{15,23},{16,... | collective-permute-start | bytes 1572872 | tf_op jit(solution)/shard_map/ppermute | solution.py:58
  15.6 19.1 %collective-permute-start.10 = (bf16[1024,256]{1,0:T(8,128)(2,1)S(1)}, bf16[1024,256]{1,0:T(8,128)(2,1)S(1)}, u32[]{:S(2)}, u32[]{:S(2)}) collective-permute-start(bf16[1024,256]{1,0:T(8,128)(2,1)S(1)} %join.1.refs_5_), channel_id=1, source_target_pairs={{0,8},{1,9},{2,10},{3,11},{4,12},{5,13},{6,14},{7,15},{16,24},{17,... | collective-permute-start | bytes 1572872 | tf_op jit(solution)/shard_map/ppermute | solution.py:58
  20.2 3.8 %dynamic-slice-start = ((s32[4096]{0:T(1024)}, s32[]{:T(128)}), s32[1024]{0:T(1024)S(1)}, s32[]{:S(2)}) async-start(s32[4096]{0:T(1024)} %param.9, s32[]{:T(128)} %select_n.55), calls=%async_computation | async-start | bytes 8704 | tf_op jit(solution)/shard_map/dynamic_slice | solution.py:384
  20.4 10.3 %collective-permute-start.4 = (bf16[256,512]{1,0:T(8,128)(2,1)S(1)}, bf16[256,512]{1,0:T(8,128)(2,1)S(1)}, u32[]{:S(2)}, u32[]{:S(2)}) collective-permute-start(bf16[256,512]{1,0:T(8,128)(2,1)S(1)} %get-tuple-element.42), channel_id=1, source_target_pairs={{0,5},{1,4},{2,7},{3,6},{4,1},{5,0},{6,3},{7,2},{8,13},{9,12},{10,... | collective-permute-start | bytes 786440 | tf_op jit(solution)/shard_map/ppermute | solution.py:34
  22.8 11.8 %collective-permute-start.5 = (bf16[256,512]{1,0:T(8,128)(2,1)S(1)}, bf16[256,512]{1,0:T(8,128)(2,1)S(1)}, u32[]{:S(2)}, u32[]{:S(2)}) collective-permute-start(bf16[256,512]{1,0:T(8,128)(2,1)S(1)} %get-tuple-element.43), channel_id=1, source_target_pairs={{0,1},{1,0},{2,3},{3,2},{4,5},{5,4},{6,7},{7,6},{8,9},{9,8},{10,11... | collective-permute-start | bytes 786440 | tf_op jit(solution)/shard_map/ppermute | solution.py:34
  23.3 11.3 %collective-permute-start.6 = (bf16[256,512]{1,0:T(8,128)(2,1)S(1)}, bf16[256,512]{1,0:T(8,128)(2,1)S(1)}, u32[]{:S(2)}, u32[]{:S(2)}) collective-permute-start(bf16[256,512]{1,0:T(8,128)(2,1)S(1)} %get-tuple-element.44), channel_id=1, source_target_pairs={{0,4},{1,5},{2,6},{3,7},{4,0},{5,1},{6,2},{7,3},{8,12},{9,13},{10,... | collective-permute-start | bytes 786440 | tf_op jit(solution)/shard_map/ppermute | solution.py:34
  45.3 2.8 %collective-permute-start.12 = (bf16[512,512]{1,0:T(8,128)(2,1)S(1)}, bf16[512,512]{1,0:T(8,128)(2,1)S(1)}, u32[]{:S(2)}, u32[]{:S(2)}) collective-permute-start(bf16[512,512]{1,0:T(8,128)(2,1)S(1)} %get-tuple-element.51), channel_id=1, source_target_pairs={{0,2},{1,3},{2,0},{3,1},{4,6},{5,7},{6,4},{7,5},{8,10},{9,11},{10,... | collective-permute-start | bytes 1572872 | tf_op jit(solution)/shard_map/ppermute | solution.py:34
  45.3 17.5 %collective-permute-start.17 = (bf16[1024,256]{1,0:T(8,128)(2,1)S(1)}, bf16[1024,256]{1,0:T(8,128)(2,1)S(1)}, u32[]{:S(2)}, u32[]{:S(2)}) collective-permute-start(bf16[1024,256]{1,0:T(8,128)(2,1)S(1)} %get-tuple-element.63), channel_id=1, source_target_pairs={{8,16},{9,17},{10,18},{11,19},{12,20},{13,21},{14,22},{15,23},{16,... | collective-permute-start | bytes 1572872 | tf_op jit(solution)/shard_map/ppermute | solution.py:58
  46.0 16.8 %collective-permute-start.16 = (bf16[1024,256]{1,0:T(8,128)(2,1)S(1)}, bf16[1024,256]{1,0:T(8,128)(2,1)S(1)}, u32[]{:S(2)}, u32[]{:S(2)}) collective-permute-start(bf16[1024,256]{1,0:T(8,128)(2,1)S(1)} %get-tuple-element.63), channel_id=1, source_target_pairs={{0,8},{1,9},{2,10},{3,11},{4,12},{5,13},{6,14},{7,15},{16,24},{17,... | collective-permute-start | bytes 1572872 | tf_op jit(solution)/shard_map/ppermute | solution.py:58
  48.1 10.2 %collective-permute-start.13 = (bf16[256,512]{1,0:T(8,128)(2,1)S(1)}, bf16[256,512]{1,0:T(8,128)(2,1)S(1)}, u32[]{:S(2)}, u32[]{:S(2)}) collective-permute-start(bf16[256,512]{1,0:T(8,128)(2,1)S(1)} %get-tuple-element.53), channel_id=1, source_target_pairs={{0,5},{1,4},{2,7},{3,6},{4,1},{5,0},{6,3},{7,2},{8,13},{9,12},{10,... | collective-permute-start | bytes 786440 | tf_op jit(solution)/shard_map/ppermute | solution.py:34
  50.5 12.3 %collective-permute-start.14 = (bf16[256,512]{1,0:T(8,128)(2,1)S(1)}, bf16[256,512]{1,0:T(8,128)(2,1)S(1)}, u32[]{:S(2)}, u32[]{:S(2)}) collective-permute-start(bf16[256,512]{1,0:T(8,128)(2,1)S(1)} %get-tuple-element.54), channel_id=1, source_target_pairs={{0,1},{1,0},{2,3},{3,2},{4,5},{5,4},{6,7},{7,6},{8,9},{9,8},{10,11... | collective-permute-start | bytes 786440 | tf_op jit(solution)/shard_map/ppermute | solution.py:34
  51.1 11.8 %collective-permute-start.15 = (bf16[256,512]{1,0:T(8,128)(2,1)S(1)}, bf16[256,512]{1,0:T(8,128)(2,1)S(1)}, u32[]{:S(2)}, u32[]{:S(2)}) collective-permute-start(bf16[256,512]{1,0:T(8,128)(2,1)S(1)} %get-tuple-element.55), channel_id=1, source_target_pairs={{0,4},{1,5},{2,6},{3,7},{4,0},{5,1},{6,2},{7,3},{8,12},{9,13},{10,... | collective-permute-start | bytes 786440 | tf_op jit(solution)/shard_map/ppermute | solution.py:34
  63.0 1.6 %collective-permute-start.18 = (bf16[512,256]{1,0:T(8,128)(2,1)S(1)}, bf16[512,256]{1,0:T(8,128)(2,1)S(1)}, u32[]{:S(2)}, u32[]{:S(2)}) collective-permute-start(bf16[512,256]{1,0:T(8,128)(2,1)S(1)} %get-tuple-element.65), channel_id=1, source_target_pairs={{0,2},{1,3},{2,0},{3,1},{4,6},{5,7},{6,4},{7,5},{8,10},{9,11},{10,... | collective-permute-start | bytes 786440 | tf_op jit(solution)/shard_map/ppermute | solution.py:34
  64.7 7.3 %collective-permute-start.19 = (bf16[256,256]{1,0:T(8,128)(2,1)S(1)}, bf16[256,256]{1,0:T(8,128)(2,1)S(1)}, u32[]{:S(2)}, u32[]{:S(2)}) collective-permute-start(bf16[256,256]{1,0:T(8,128)(2,1)S(1)} %get-tuple-element.67), channel_id=1, source_target_pairs={{0,5},{1,4},{2,7},{3,6},{4,1},{5,0},{6,3},{7,2},{8,13},{9,12},{10,... | collective-permute-start | bytes 393224 | tf_op jit(solution)/shard_map/ppermute | solution.py:34
  67.1 6.9 %collective-permute-start.20 = (bf16[256,256]{1,0:T(8,128)(2,1)S(1)}, bf16[256,256]{1,0:T(8,128)(2,1)S(1)}, u32[]{:S(2)}, u32[]{:S(2)}) collective-permute-start(bf16[256,256]{1,0:T(8,128)(2,1)S(1)} %get-tuple-element.68), channel_id=1, source_target_pairs={{0,1},{1,0},{2,3},{3,2},{4,5},{5,4},{6,7},{7,6},{8,9},{9,8},{10,11... | collective-permute-start | bytes 393224 | tf_op jit(solution)/shard_map/ppermute | solution.py:34
  67.6 6.4 %collective-permute-start.21 = (bf16[256,256]{1,0:T(8,128)(2,1)S(1)}, bf16[256,256]{1,0:T(8,128)(2,1)S(1)}, u32[]{:S(2)}, u32[]{:S(2)}) collective-permute-start(bf16[256,256]{1,0:T(8,128)(2,1)S(1)} %get-tuple-element.69), channel_id=1, source_target_pairs={{0,4},{1,5},{2,6},{3,7},{4,0},{5,1},{6,2},{7,3},{8,12},{9,13},{10,... | collective-permute-start | bytes 393224 | tf_op jit(solution)/shard_map/ppermute | solution.py:34

commit v9 on v7

--- a/solution.py
+++ b/solution.py
@@ -14,6 +14,7 @@
 logit_scale = 168.0 ** (-0.5)
 exp2_scale = logit_scale * 1.4426950408889634
 
+FAR = -(2.0**30)
 SMALL = pltpu.CompilerParams(vmem_limit_bytes=4 * 1024 * 1024)
 ANY = pl.BlockSpec(memory_space=pl.ANY)
 VMEM = pl.BlockSpec(memory_space=pltpu.VMEM)
@@ -39,7 +40,8 @@
 
 
 def chip_masks(size):
-    return [mask for mask in range(size) if not mask & core_mask()]
+    masks = [mask for mask in range(size) if not mask & core_mask()]
+    return masks[:1] + sorted(masks[1:], key=lambda mask: -mask.bit_count())
 
 
 def swap_chips(pieces, size):
@@ -48,18 +50,18 @@
     ]
 
 
-def partner(size, j):
-    return lax.bitwise_xor(lax.rem(flat_index(), size), j)
-
-
-def place(index, width):
-    return pl.ds(pl.multiple_of(index * width, width), width)
-
-
 def shifted(value, step):
     count = device_count()
     pairs = [(i, i + step) for i in range(count) if 0 <= i + step < count]
     return lax.ppermute(value, BOTH, pairs)
+
+
+def partner(size, j):
+    return lax.bitwise_xor(lax.rem(flat_index(), size), j)
+
+
+def place(index, width):
+    return pl.ds(pl.multiple_of(index * width, width), width)
 
 
 def after(value, *others):
@@ -112,9 +114,8 @@
             start += width
 
 
-def gather_cores(arrays, size):
+def gather_cores(arrays, got, size):
     masks = chip_masks(size)
-    got = [swap(array, core_mask()) for array in arrays]
     own = [this_core(array, size) for array in arrays]
     cols = sum(array.shape[1] // size for array in arrays)
     piece = jax.ShapeDtypeStruct((2 * arrays[0].shape[0], cols), BF16)
@@ -129,12 +130,11 @@
         out[place(partner(size, mask ^ core), rows), :] = piece[rows:, :]
 
 
-def take_rows(size, core, masks, source, own, give):
-    rows = own.shape[0] // len(masks)
-    for at, mask in enumerate(masks):
-        part = slice(at * rows, (at + 1) * rows)
-        own[part, :] = source(place(partner(size, mask), rows))
-        give[part, :] = source(place(partner(size, mask ^ core), rows))
+def take_rows(size, core, masks, source, pieces):
+    for mask, piece in zip(masks, pieces):
+        rows = piece.shape[0] // 2
+        piece[:rows, :] = source(place(partner(size, mask), rows))
+        piece[rows:, :] = source(place(partner(size, mask ^ core), rows))
 
 
 def join(pieces, size):
@@ -161,56 +161,52 @@
                 total = total + term[there, :].astype(F32)
             return total.astype(BF16)
 
-        take_rows(size, core, masks, source, *refs[len(terms) :])
-
-    half = jax.ShapeDtypeStruct((tok // 2, cols), BF16)
-    return small_call(kernel, [half] * 2, "combine", *terms)
-
-
-def pair_body(own, got, *pieces):
-    rows = own.shape[0] // len(pieces)
-    for at, piece in enumerate(pieces):
-        part = slice(at * rows, (at + 1) * rows)
-        piece[:rows, :] = own[part, :]
-        piece[rows:, :] = got[part, :]
-
-
-def scatter(own, give, size):
-    count = len(chip_masks(size))
-    piece = jax.ShapeDtypeStruct((2 * own.shape[0] // count, own.shape[1]), BF16)
-    pieces = small_call(pair_body, [piece] * count, "pair", own, swap(give, core_mask()))
-    return swap_chips(pieces, size)
-
-
-def spread_body(size, core, masks, count, *refs):
-    pieces, outs, sems = refs[: len(masks)], refs[len(masks) : -1], refs[-1]
-    copies = []
-    for mask, piece in zip(masks, pieces):
-        rows, cols = piece.shape
-        rows, width = rows // 2, cols // count
-        for flip in (0, 1):
-            columns = place(partner(size, mask ^ (core * flip)), width)
-            for at, out in enumerate(outs):
-                copies.append(
-                    (
-                        piece.at[flip * rows : (flip + 1) * rows, at * width : (at + 1) * width],
-                        out.at[:, columns],
-                    )
-                )
+        take_rows(size, core, masks, source, refs[len(terms) :])
+
+    piece = jax.ShapeDtypeStruct((2 * (tok // size), cols), BF16)
+    return small_call(kernel, [piece] * len(masks), "combine", *terms)
+
+
+def bottom_body(*refs):
+    out, start = refs[-1], 0
+    for piece in refs[:-1]:
+        rows, width = piece.shape[0] // 2, piece.shape[1]
+        out[:, start : start + width] = piece[rows:, :]
+        start += width
+
+
+def spread_body(size, core, masks, *refs):
+    count = len(masks)
+    sets, got, outs, sems = (refs[:count], refs[count : 2 * count]), refs[2 * count], refs[-5:-1], refs[-1]
+    copies, start = [], 0
+    for which, pieces in enumerate(sets):
+        for mask, piece in zip(masks, pieces):
+            rows, width = piece.shape[0] // 2, piece.shape[1] // 2
+            for at, out in enumerate(outs[2 * which : 2 * which + 2]):
+                mine = out.at[:, place(partner(size, mask), width)]
+                other = out.at[:, place(partner(size, mask ^ core), width)]
+                copies.append((piece.at[:rows, at * width : (at + 1) * width], mine))
+                copies.append((got.at[:, start : start + width], other))
+                start += width
     run_copies(copies, sems)
 
 
-def spread(pieces, size, count):
-    rows, cols = pieces[0].shape
+def spread_cores(og, grads, size):
+    rows = og[0].shape[0] // 2
+    widths = [og[0].shape[1] // 2, grads[0].shape[1] // 2]
+    give = jax.ShapeDtypeStruct((rows, size * sum(widths)), BF16)
+    got = swap(small_call(bottom_body, give, "bottom", *og, *grads), core_mask())
     return pl.pallas_call(
-        functools.partial(spread_body, size, core_mask(), chip_masks(size), count),
-        out_shape=[jax.ShapeDtypeStruct((rows // 2, cols // count * size), BF16)] * count,
-        in_specs=[ANY] * len(pieces),
-        out_specs=[ANY] * count,
-        scratch_shapes=[pltpu.SemaphoreType.DMA((size * count,))],
+        functools.partial(spread_body, size, core_mask(), chip_masks(size)),
+        out_shape=[
+            jax.ShapeDtypeStruct((rows, width * size), BF16) for width in widths for _ in range(2)
+        ],
+        in_specs=[ANY] * (2 * len(og) + 1),
+        out_specs=[ANY] * 4,
+        scratch_shapes=[pltpu.SemaphoreType.DMA((4 * size,))],
         compiler_params=SMALL,
         name="spread",
-    )(*pieces)
+    )(*og, *grads, got)
 
 
 def dot(a, b):
@@ -234,28 +230,27 @@
 def attend_body(size, core, masks, reach, tok, group, *refs):
     refs = list(refs)
     take = lambda count: [refs.pop(0) for _ in range(count)]
-    (low,), qg_pieces, kvs = take(1), take(len(masks)), take(1 + reach)
-    og_halves, (dkv0,), sent = take(2), take(1), take(reach)
-    qg, og, ks, va, kt, vt, dk, dv, s_scr, e_scr, ds_scr = refs
+    (seg_k, seg_q), qg_pieces, kvs = take(2), take(len(masks)), take(1 + reach)
+    og_pieces, (dkv0,), sent = take(len(masks)), take(1), take(reach)
+    qg, og, ka, va, kt, vt, dk, dv, s_scr, e_scr, ds_scr = refs
     width = group * HEAD_DIM
     span = WINDOW + TILE
     place_rows(size, core, masks, qg_pieces, qg)
     va[:, HEAD_DIM:] = jnp.where(
         lax.broadcasted_iota(jnp.int32, (va.shape[0], HEAD_DIM), 1) < 2, 1.0, 0.0
     ).astype(BF16)
+    ka[:, HEAD_DIM:] = seg_k[...]
     for lag in range(reach + 1):
         there = slice((reach - lag) * tok, (reach - lag + 1) * tok)
-        ks[there, :] = kvs[lag][:, :HEAD_DIM]
-        va[there, :HEAD_DIM] = kvs[lag][:, HEAD_DIM:]
-        kt[:, there] = kvs[lag][:, :HEAD_DIM].T
-        vt[:, there] = kvs[lag][:, HEAD_DIM:].T
-    dk[...] = jnp.zeros_like(dk)
-    dv[...] = jnp.zeros_like(dv)
+        kv = kvs[lag][...]
+        ka[there, :HEAD_DIM] = kv[:, :HEAD_DIM]
+        va[there, :HEAD_DIM] = kv[:, HEAD_DIM:]
+        kt[:, there] = kv[:, :HEAD_DIM].T
+        vt[:, there] = kv[:, HEAD_DIM:].T
     wide_lane = lax.broadcasted_iota(jnp.int32, (group * TILE, HEAD_DIM), 1)
-    row_of = lax.broadcasted_iota(jnp.int32, (TILE, group * TILE), 0)
+    row_of = lax.broadcasted_iota(jnp.int32, (TILE, TILE), 0)
     col_of = lax.broadcasted_iota(jnp.int32, (TILE, TILE), 1)
-    causal = lax.broadcasted_iota(jnp.int32, (TILE, TILE), 0) <= col_of
-    causal = jnp.concatenate([causal] * group, axis=1)
+    causal = jnp.concatenate([row_of <= col_of] * group, axis=1)
 
     def stacked(base, first):
         here = slice(base, base + TILE)
@@ -269,22 +264,27 @@
 
     def scores(tile):
         base = tile * TILE
-        s_scr[tile % 2] = dot_t(ks[base : base + span, :], stacked(base, 0))
+        mine = jnp.concatenate([seg_q[base : base + TILE, :]] * group, axis=0)
+        wide = jnp.concatenate([stacked(base, 0), mine], axis=1)
+        s_scr[tile % 2] = dot_t(ka[base : base + span, :], wide)
+
+    def add(target, base, value):
+        fresh = base + (WINDOW if base else 0)
+        if base:
+            target[base:fresh, :] += value[:WINDOW]
+        target[fresh : base + span, :] = value[fresh - base :]
 
     tiles = tok // TILE
     scores(0)
     for tile in range(tiles):
         base, turn = tile * TILE, tile % 2
         here, there = slice(base, base + TILE), slice(base, base + span)
-        low_row = jnp.concatenate([low[:, here]] * group, axis=1) - base
+        for at, keep in ((0, ~causal), (WINDOW, causal)):
+            part = slice(at, at + TILE)
+            s_scr[turn, part, :] = jnp.where(keep, s_scr[turn, part, :], FAR)
         top = None
         for at in range(0, span, TILE):
-            keep = row_of >= low_row - at
-            if at == span - TILE:
-                keep = keep & causal
-            s = jnp.where(keep, s_scr[turn, at : at + TILE, :], -1e30)
-            s_scr[turn, at : at + TILE, :] = s
-            part = fold(s, jnp.maximum)
+            part = fold(s_scr[turn, at : at + TILE, :], jnp.maximum)
             top = part if top is None else jnp.maximum(top, part)
         top = jnp.max(top, axis=0, keepdims=True) * exp2_scale
         if tile + 1 < tiles:
@@ -304,11 +304,11 @@
         high = delta.astype(BF16).astype(F32)
         extra = jnp.where(wide_lane == 0, -high, jnp.where(wide_lane == 1, high - delta, 0.0))
         dp = dot_t(va[there, :], jnp.concatenate([g2, extra.astype(BF16)], axis=1))
-        dv[there, :] += dot(e_scr[turn], g2)
+        add(dv, base, dot(e_scr[turn], g2))
         for at in range(0, span, TILE):
             part = slice(at, at + TILE)
             ds_scr[turn, part, :] = (e_scr[turn, part, :].astype(F32) * dp[part]).astype(BF16)
-        dk[there, :] += dot(ds_scr[turn], stacked(base, 0))
+        add(dk, base, dot(ds_scr[turn], stacked(base, 0)))
         dq = (dot(kt[:, there], ds_scr[turn]) * logit_scale).T.astype(BF16)
         for at in range(group):
             part = slice(at * TILE, (at + 1) * TILE)
@@ -321,14 +321,14 @@
         there = slice((reach - lag) * tok, (reach - lag + 1) * tok)
         sent[lag - 1][:, :HEAD_DIM] = (dk[there, :] * logit_scale).astype(BF16)
         sent[lag - 1][:, HEAD_DIM:] = dv[there, :].astype(BF16)
-    take_rows(size, core, masks, lambda there: og[there, :], *og_halves)
-
-
-def attend(low, qg, kvs, size):
+    take_rows(size, core, masks, lambda there: og[there, :], og_pieces)
+
+
+def attend(documents, qg, kv, lags, size):
     rows, cols = qg[0].shape
     tok = len(qg) * rows
     group = cols // (2 * HEAD_DIM)
-    reach = len(kvs) - 1
+    reach = len(lags)
     span = WINDOW + TILE
     wide = group * TILE
     keys = (reach + 1) * tok
@@ -337,15 +337,15 @@
     count = len(qg)
     results = pl.pallas_call(
         functools.partial(attend_body, size, core_mask(), chip_masks(size), reach, tok, group),
-        out_shape=[jax.ShapeDtypeStruct((tok // 2, cols), BF16)] * 2
+        out_shape=[jax.ShapeDtypeStruct((rows, cols), BF16)] * count
         + [jax.ShapeDtypeStruct((tok, 2 * HEAD_DIM), F32)]
         + [half] * reach,
-        in_specs=[VMEM] * (count + 2 + reach),
-        out_specs=[VMEM] * (3 + reach),
+        in_specs=[VMEM] * (count + 3 + reach),
+        out_specs=[VMEM] * (count + 1 + reach),
         scratch_shapes=[
             pltpu.VMEM((tok, cols), BF16),
             pltpu.VMEM((tok, cols), BF16),
-            pltpu.VMEM((keys, HEAD_DIM), BF16),
+            pltpu.VMEM((keys, 2 * HEAD_DIM), BF16),
             pltpu.VMEM((keys, 2 * HEAD_DIM), BF16),
             pltpu.VMEM((HEAD_DIM, keys), BF16),
             pltpu.VMEM((HEAD_DIM, keys), BF16),
@@ -360,17 +360,20 @@
             flops=flops, bytes_accessed=8 * 1024 * 1024, transcendentals=flops // 1536
         ),
         name="attend",
-    )(low, *qg, *kvs)
-    return results[:2], results[2], results[3:]
-
-
-def lowest_key(segment_ids, tok, size):
+    )(*documents, *qg, kv, *lags)
+    return results[:count], results[count], results[count + 1 :]
+
+
+def document_columns(segment_ids, tok, size):
     start = (flat_index() // size) * tok
     padded = jnp.concatenate([jnp.full((WINDOW,), -1, jnp.int32), segment_ids])
     keys = lax.dynamic_slice_in_dim(padded, start, WINDOW + tok, 0)
     queries = lax.dynamic_slice_in_dim(segment_ids, start, tok, 0)
-    before = jnp.sum((keys[:, None] < queries[None, :]).astype(jnp.int32), axis=0)
-    return jnp.maximum(before, jnp.arange(1, tok + 1, dtype=jnp.int32))[None, :]
+    number = jnp.arange(HEAD_DIM, dtype=jnp.int32)[None, :]
+    return (
+        jnp.where(keys[:, None] == number, 0.0, FAR).astype(BF16),
+        jnp.where(queries[:, None] == number, 1.0, 0.0).astype(BF16),
+    )
 
 
 def body(query, key, value, grad_out, segment_ids):
@@ -379,20 +382,21 @@
     tok = size * rows
     reach = WINDOW // tok
     assert reach * tok == WINDOW and device_count() % size == 0
-    low = lowest_key(segment_ids, tok, size)
-
-    kv = join(swap_chips(gather_cores((key, value), size), size), size)
-    qg = swap_chips(gather_cores((query, grad_out), size), size)
-    kvs = [kv] + [shifted(kv, lag * size) for lag in range(1, reach + 1)]
-
-    og, dkv, sent = attend(low, qg, kvs, size)
-
-    back = [shifted(sent[lag - 1], -lag * size) for lag in range(1, reach + 1)]
-    dkv, *og = after(dkv, *scatter(*og, size))
-    grads = scatter(*combine([dkv] + back, size), size)
-    attn_out, grad_query = spread(og, size, 2)
-    grad_key, grad_value = spread(grads, size, 2)
-    return (attn_out, grad_query, grad_key, grad_value)
+    documents = document_columns(segment_ids, tok, size)
+
+    got = [swap(array, core_mask()) for array in (key, value, query, grad_out)]
+    pieces = list(gather_cores((key, value), got[:2], size))
+    pieces[0], query, grad_out = after(pieces[0], query, grad_out)
+    kv = join(swap_chips(pieces, size), size)
+    lags = [shifted(kv, lag * size) for lag in range(1, reach + 1)]
+    qg = swap_chips(gather_cores((query, grad_out), got[2:], size), size)
+
+    og, dkv, sent = attend(documents, qg, kv, lags, size)
+
+    backs = [shifted(sent[lag - 1], -lag * size) for lag in range(1, reach + 1)]
+    og = swap_chips(og, size)
+    grads = swap_chips(combine([dkv, *backs], size), size)
+    return tuple(spread_cores(og, grads, size))
 
 
 def solution(mesh):

time: 72.3 us -> 73 us (level)
  local copies, waits for them, and re-layouts: 2.19 us -> 3.44 us
    ppermute x18 -> x17, waiting for transfers between devices: 33.2 us -> 22.4 us  [swap(): lax.ppermute(value, BOTH, [(i, i ^ mask) for i in range(device_count())])]
    ppermute x2, waiting for transfers between devices: 0.13 us -> 10.6 us  [shifted(): return lax.ppermute(value, BOTH, pairs)]
    unnamed x6 -> x8, local copies, waits for them, and re-layouts: 0.02 us -> 1.66 us
    slice x4, local copies, waits for them, and re-layouts: 2.15 us -> 1.09 us  [this_core(): shares = [array[:, r * width:(r + 1) * width] for r in range(size)]]
    reduce_sum x1 -> x0, other arithmetic: 0.97 us -> none  [lowest_key(): jnp.sum((keys[:, None] < queries[None, :]).astype(jnp.int32), axis=0)]
    pallas_call x2 -> x1, Pallas kernels: 2 us -> 1.39 us  [spread_cores(): pl.pallas_call(functools.partial(spread_body, size, core_mask(), chip_mas...]
    ppermute x18 -> x17, starting transfers between devices: 16.4 us -> 16.4 us  [swap(): lax.ppermute(value, BOTH, [(i, i ^ mask) for i in range(device_count())])]
  transfers between devices with their start and end apart: 20 -> 19, of which waited for: 12 -> 9; matrix products, arithmetic and copies ran while one was open for 5% -> 3% of each run, Pallas kernels for 2% -> 2%
where the time goes in v9:
time: 73 us; the launch traced here: 72.7 us
  waiting for transfers between devices  33 us (45%)
  starting transfers between devices  21.2 us (29%)
  Pallas kernels  13.5 us (18%)
  local copies, waits for them, and re-layouts  3.44 us (5%)
  between operations  0.85 us (1%)
  other arithmetic  0.74 us (1%)
    ppermute x17, waiting for transfers between devices, swap(): lax.ppermute(value, BOTH, [(i, i ^ mask) for i in range(device_count())])  22.4 us
    ppermute x17, starting transfers between devices, swap(): lax.ppermute(value, BOTH, [(i, i ^ mask) for i in range(device_count())])  16.4 us
    pallas_call x1, Pallas kernels, attend(): pl.pallas_call(functools.partial(attend_body, size, core_mask(), chip_mas...  10.9 us
    ppermute x2, waiting for transfers between devices, shifted(): return lax.ppermute(value, BOTH, pairs)  10.6 us
    ppermute x2, starting transfers between devices, shifted(): return lax.ppermute(value, BOTH, pairs)  4.8 us
    unnamed x8, local copies, waits for them, and re-layouts  1.66 us
  transfers between devices with their start and end apart: 19, of which 9 were waited for; matrix products, arithmetic and copies ran while one was open for 3% of the time, Pallas kernels for 2%

profile of v9, /device:TPU:0, one launch (start us, length us, event | category | flops | bytes accessed | tf_op | source)
XLA Modules:
  0.0 72.7 jit_solution(16317144795810396193)
XLA Ops:
  0.6 0.5 collective-permute-start
  1.2 0.4 collective-permute-start.2
  1.7 1.0 %fusion.3 = (bf16[128,256]{1,0:T(8,128)(2,1)S(1)}, bf16[128,256]{1,0:T(8,128)(2,1)S(1)}, bf16[128,256]{1,0:T(8,128)(2,1)S(1)}, bf16[128,256]{1,0:T(8,128)(2,1)S(1)}) fusion(bf16[128,1024]{1,0:T(8,128)(2,1)} %param.6), kind=kLoop, calls=%fused_computation.12 | loop fusion | bytes 524288 | tf_op jit(solution)/shard_map/slice | solution.py:95
  2.9 0.7 copy-done.3
  3.8 3.9 %collective-permute-start.7 = (bf16[256,256]{1,0:T(8,128)(2,1)S(1)}, bf16[256,256]{1,0:T(8,128)(2,1)S(1)}, u32[]{:S(2)}, u32[]{:S(2)}) collective-permute-start(bf16[256,256]{1,0:T(8,128)(2,1)S(1)} %get-tuple-element.33), channel_id=1, source_target_pairs={{0,5},{1,4},{2,7},{3,6},{4,1},{5,0},{6,3},{7,2},{8,13},{9,12},{10,... | collective-permute-start | bytes 393224 | tf_op jit(solution)/shard_map/ppermute | solution.py:35
  7.8 0.5 collective-permute-start.8
  8.4 0.9 %copy-done.1 = bf16[128,2048]{1,0:T(8,128)(2,1)S(1)} copy-done((bf16[128,2048]{1,0:T(8,128)(2,1)S(1)}, bf16[128,2048]{1,0:T(8,128)(2,1)}, u32[]{:S(2)}) %copy-start.1) | copy-done | bytes 524312
  9.5 2.5 %collective-permute-done.7.refs_1_ = bf16[256,256]{1,0:T(8,128)(2,1)S(1)} collective-permute-done((bf16[256,256]{1,0:T(8,128)(2,1)S(1)}, bf16[256,256]{1,0:T(8,128)(2,1)S(1)}, u32[]{:S(2)}, u32[]{:S(2)}) %collective-permute-start.7) | collective-permute-done | bytes 131104 | tf_op jit(solution)/shard_map/ppermute | solution.py:35
  12.0 2.5 %collective-permute-done.8.refs_2_ = bf16[256,256]{1,0:T(8,128)(2,1)S(1)} collective-permute-done((bf16[256,256]{1,0:T(8,128)(2,1)S(1)}, bf16[256,256]{1,0:T(8,128)(2,1)S(1)}, u32[]{:S(2)}, u32[]{:S(2)}) %collective-permute-start.8) | collective-permute-done | bytes 131104 | tf_op jit(solution)/shard_map/ppermute | solution.py:35
  14.6 3.5 %collective-permute-start.10 = (bf16[1024,256]{1,0:T(8,128)(2,1)S(1)}, bf16[1024,256]{1,0:T(8,128)(2,1)S(1)}, u32[]{:S(2)}, u32[]{:S(2)}) collective-permute-start(bf16[1024,256]{1,0:T(8,128)(2,1)S(1)} %join.1.refs_6_), channel_id=1, source_target_pairs={{0,8},{1,9},{2,10},{3,11},{4,12},{5,13},{6,14},{7,15},{8,16},{9,17... | collective-permute-start | bytes 1572872 | tf_op jit(solution)/shard_map/ppermute | solution.py:56
  18.2 0.9 %stack.3 = (bf16[256,512]{1,0:T(8,128)(2,1)S(1)}, bf16[256,512]{1,0:T(8,128)(2,1)}, bf16[256,512]{1,0:T(8,128)(2,1)}, bf16[256,512]{1,0:T(8,128)(2,1)S(1)}) custom-call(bf16[128,1024]{1,0:T(8,128)(2,1)S(1)} %get-tuple-element.62.refs_0_, bf16[128,1024]{1,0:T(8,128)(2,1)S(1)} %get-tuple-element.63.refs_1_, ...), custom_call_target="tpu_custom_call" | custom-call | tf_op jit(solution)/shard_map/stack/pallas_call | solution.py:82
  19.1 2.4 %collective-permute-start.4 = (bf16[256,512]{1,0:T(8,128)(2,1)}, bf16[256,512]{1,0:T(8,128)(2,1)S(1)}, u32[]{:S(2)}, u32[]{:S(2)}) collective-permute-start(bf16[256,512]{1,0:T(8,128)(2,1)} %get-tuple-element.29), channel_id=1, source_target_pairs={{0,5},{1,4},{2,7},{3,6},{4,1},{5,0},{6,3},{7,2},{8,13},{9,12},{10,... | collective-permute-start | bytes 786440 | tf_op jit(solution)/shard_map/ppermute | solution.py:35
  21.5 0.5 collective-permute-start.5
  22.0 0.6 collective-permute-start.6
  22.6 0.3 select_convert_fusion.refs_0_
  23.0 0.7 dynamic-slice-done
  23.6 0.2 select_convert_fusion.1.refs_1_
  23.8 5.7 %collective-permute-done.4.refs_3_ = bf16[256,512]{1,0:T(8,128)(2,1)S(1)} collective-permute-done((bf16[256,512]{1,0:T(8,128)(2,1)}, bf16[256,512]{1,0:T(8,128)(2,1)S(1)}, u32[]{:S(2)}, u32[]{:S(2)}) %collective-permute-start.4) | collective-permute-done | bytes 262176 | tf_op jit(solution)/shard_map/ppermute | solution.py:35
  29.5 4.3 %collective-permute-done.5.refs_4_ = bf16[256,512]{1,0:T(8,128)(2,1)S(1)} collective-permute-done((bf16[256,512]{1,0:T(8,128)(2,1)}, bf16[256,512]{1,0:T(8,128)(2,1)S(1)}, u32[]{:S(2)}, u32[]{:S(2)}) %collective-permute-start.5) | collective-permute-done | bytes 262176 | tf_op jit(solution)/shard_map/ppermute | solution.py:35
  33.8 10.9 %attend.1 = (bf16[256,512]{1,0:T(8,128)(2,1)S(1)}, bf16[256,512]{1,0:T(8,128)(2,1)S(1)}, bf16[256,512]{1,0:T(8,128)(2,1)S(1)}, bf16[256,512]{1,0:T(8,128)(2,1)S(...) custom-call(bf16[2048,128]{1,0:T(8,128)(2,1)S(1)} %select_convert_fusion.refs_0_, ...), custom_call_target="tpu_custom_call" | custom-call | flops 3623878656 | bytes 8388608 | tf_op jit(solution)/shard_map/attend/pallas_call | solution.py:338
  44.7 1.3 %collective-permute-start.14 = (bf16[1024,256]{1,0:T(8,128)(2,1)S(1)}, bf16[1024,256]{1,0:T(8,128)(2,1)S(1)}, u32[]{:S(2)}, u32[]{:S(2)}) collective-permute-start(bf16[1024,256]{1,0:T(8,128)(2,1)S(1)} %get-tuple-element.41), channel_id=1, source_target_pairs={{8,0},{9,1},{10,2},{11,3},{12,4},{13,5},{14,6},{15,7},{16,8},{17,9... | collective-permute-start | bytes 1572872 | tf_op jit(solution)/shard_map/ppermute | solution.py:56
  46.0 2.4 %collective-permute-start.11 = (bf16[256,512]{1,0:T(8,128)(2,1)S(1)}, bf16[256,512]{1,0:T(8,128)(2,1)S(1)}, u32[]{:S(2)}, u32[]{:S(2)}) collective-permute-start(bf16[256,512]{1,0:T(8,128)(2,1)S(1)} %get-tuple-element.37), channel_id=1, source_target_pairs={{0,5},{1,4},{2,7},{3,6},{4,1},{5,0},{6,3},{7,2},{8,13},{9,12},{10,... | collective-permute-start | bytes 786440 | tf_op jit(solution)/shard_map/ppermute | solution.py:35
  48.4 0.5 collective-permute-start.12
  48.9 0.6 collective-permute-start.13
  49.5 10.6 %collective-permute-done.14.refs_1_ = bf16[1024,256]{1,0:T(8,128)(2,1)S(1)} collective-permute-done((bf16[1024,256]{1,0:T(8,128)(2,1)S(1)}, bf16[1024,256]{1,0:T(8,128)(2,1)S(1)}, u32[]{:S(2)}, u32[]{:S(2)}) %collective-permute-start.14) | collective-permute-done | bytes 524320 | tf_op jit(solution)/shard_map/ppermute | solution.py:56
  60.2 2.7 %collective-permute-start.15 = (bf16[256,256]{1,0:T(8,128)(2,1)S(1)}, bf16[256,256]{1,0:T(8,128)(2,1)S(1)}, u32[]{:S(2)}, u32[]{:S(2)}) collective-permute-start(bf16[256,256]{1,0:T(8,128)(2,1)S(1)} %get-tuple-element.43), channel_id=1, source_target_pairs={{0,5},{1,4},{2,7},{3,6},{4,1},{5,0},{6,3},{7,2},{8,13},{9,12},{10,... | collective-permute-start | bytes 393224 | tf_op jit(solution)/shard_map/ppermute | solution.py:35
  62.9 0.5 collective-permute-start.16
  63.5 0.3 collective-permute-start.17
  63.8 3.5 %collective-permute-done.15.refs_5_ = bf16[256,256]{1,0:T(8,128)(2,1)S(1)} collective-permute-done((bf16[256,256]{1,0:T(8,128)(2,1)S(1)}, bf16[256,256]{1,0:T(8,128)(2,1)S(1)}, u32[]{:S(2)}, u32[]{:S(2)}) %collective-permute-start.15) | collective-permute-done | bytes 131104 | tf_op jit(solution)/shard_map/ppermute | solution.py:35
  67.3 1.5 %collective-permute-done.16.refs_6_ = bf16[256,256]{1,0:T(8,128)(2,1)S(1)} collective-permute-done((bf16[256,256]{1,0:T(8,128)(2,1)S(1)}, bf16[256,256]{1,0:T(8,128)(2,1)S(1)}, u32[]{:S(2)}, u32[]{:S(2)}) %collective-permute-start.16) | collective-permute-done | bytes 131104 | tf_op jit(solution)/shard_map/ppermute | solution.py:35
  69.1 2.3 %collective-permute-done.18.refs_8_ = bf16[128,3072]{1,0:T(8,128)(2,1)S(1)} collective-permute-done((bf16[128,3072]{1,0:T(8,128)(2,1)S(1)}, bf16[128,3072]{1,0:T(8,128)(2,1)S(1)}, u32[]{:S(2)}, u32[]{:S(2)}) %collective-permute-start.18) | collective-permute-done | bytes 786464 | tf_op jit(solution)/shard_map/ppermute | solution.py:35
  71.3 1.4 %spread.1 = (bf16[128,2048]{1,0:T(8,128)(2,1)}, bf16[128,2048]{1,0:T(8,128)(2,1)}, bf16[128,1024]{1,0:T(8,128)(2,1)}, bf16[128,1024]{1,0:T(8,128)(2,1)}) custom-call(bf16[256,512]{1,0:T(8,128)(2,1)S(1)} %get-tuple-element.36.refs_0_, bf16[256,512]{1,0:T(8,128)(2,1)S(1)} %collective-permute-done.11.refs_1_, ...), custom_call_target="tpu_custom_call" | custom-call | tf_op jit(solution)/shard_map/spread/pallas_call | solution.py:199
  (33 shorter events, 1.1 us)
Async XLA Ops:
  0.6 3.0 %collective-permute-start = (bf16[128,1024]{1,0:T(8,128)(2,1)}, bf16[128,1024]{1,0:T(8,128)(2,1)S(1)}, u32[]{:S(2)}, u32[]{:S(2)}) collective-permute-start(bf16[128,1024]{1,0:T(8,128)(2,1)} %param.6), channel_id=1, source_target_pairs={{0,2},{1,3},{2,0},{3,1},{4,6},{5,7},{6,4},{7,5},{8,10},{9,11},{10,... | collective-permute-start | bytes 786440 | tf_op jit(solution)/shard_map/ppermute | solution.py:35
  1.1 2.5 %collective-permute-start.1 = (bf16[128,1024]{1,0:T(8,128)(2,1)}, bf16[128,1024]{1,0:T(8,128)(2,1)S(1)}, u32[]{:S(2)}, u32[]{:S(2)}) collective-permute-start(bf16[128,1024]{1,0:T(8,128)(2,1)} %param.7), channel_id=1, source_target_pairs={{0,2},{1,3},{2,0},{3,1},{4,6},{5,7},{6,4},{7,5},{8,10},{9,11},{10,... | collective-permute-start | bytes 786440 | tf_op jit(solution)/shard_map/ppermute | solution.py:35
  1.2 16.9 %collective-permute-start.2 = (bf16[128,2048]{1,0:T(8,128)(2,1)}, bf16[128,2048]{1,0:T(8,128)(2,1)S(1)}, u32[]{:S(2)}, u32[]{:S(2)}) collective-permute-start(bf16[128,2048]{1,0:T(8,128)(2,1)} %param.5), channel_id=1, source_target_pairs={{0,2},{1,3},{2,0},{3,1},{4,6},{5,7},{6,4},{7,5},{8,10},{9,11},{10,... | collective-permute-start | bytes 1572872 | tf_op jit(solution)/shard_map/ppermute | solution.py:35
  1.7 16.5 %collective-permute-start.3 = (bf16[128,2048]{1,0:T(8,128)(2,1)}, bf16[128,2048]{1,0:T(8,128)(2,1)S(1)}, u32[]{:S(2)}, u32[]{:S(2)}) collective-permute-start(bf16[128,2048]{1,0:T(8,128)(2,1)} %param.8), channel_id=1, source_target_pairs={{0,2},{1,3},{2,0},{3,1},{4,6},{5,7},{6,4},{7,5},{8,10},{9,11},{10,... | collective-permute-start | bytes 1572872 | tf_op jit(solution)/shard_map/ppermute | solution.py:35
  1.7 1.1 %copy-start.2 = (bf16[128,1024]{1,0:T(8,128)(2,1)S(1)}, bf16[128,1024]{1,0:T(8,128)(2,1)}, u32[]{:S(2)}) copy-start(bf16[128,1024]{1,0:T(8,128)(2,1)} %param.7) | copy-start | bytes 786436
  2.8 0.7 copy-start.3
  3.6 4.8 %copy-start = (bf16[128,2048]{1,0:T(8,128)(2,1)S(1)}, bf16[128,2048]{1,0:T(8,128)(2,1)}, u32[]{:S(2)}) copy-start(bf16[128,2048]{1,0:T(8,128)(2,1)} %param.5) | copy-start | bytes 1572868
  3.8 8.2 %collective-permute-start.7 = (bf16[256,256]{1,0:T(8,128)(2,1)S(1)}, bf16[256,256]{1,0:T(8,128)(2,1)S(1)}, u32[]{:S(2)}, u32[]{:S(2)}) collective-permute-start(bf16[256,256]{1,0:T(8,128)(2,1)S(1)} %get-tuple-element.33), channel_id=1, source_target_pairs={{0,5},{1,4},{2,7},{3,6},{4,1},{5,0},{6,3},{7,2},{8,13},{9,12},{10,... | collective-permute-start | bytes 393224 | tf_op jit(solution)/shard_map/ppermute | solution.py:35
  7.8 6.8 %collective-permute-start.8 = (bf16[256,256]{1,0:T(8,128)(2,1)S(1)}, bf16[256,256]{1,0:T(8,128)(2,1)S(1)}, u32[]{:S(2)}, u32[]{:S(2)}) collective-permute-start(bf16[256,256]{1,0:T(8,128)(2,1)S(1)} %get-tuple-element.34), channel_id=1, source_target_pairs={{0,1},{1,0},{2,3},{3,2},{4,5},{5,4},{6,7},{7,6},{8,9},{9,8},{10,11... | collective-permute-start | bytes 393224 | tf_op jit(solution)/shard_map/ppermute | solution.py:35
  8.3 1.0 %copy-start.1 = (bf16[128,2048]{1,0:T(8,128)(2,1)S(1)}, bf16[128,2048]{1,0:T(8,128)(2,1)}, u32[]{:S(2)}) copy-start(bf16[128,2048]{1,0:T(8,128)(2,1)} %param.8) | copy-start | bytes 1572868
  8.3 6.3 %collective-permute-start.9 = (bf16[256,256]{1,0:T(8,128)(2,1)S(1)}, bf16[256,256]{1,0:T(8,128)(2,1)S(1)}, u32[]{:S(2)}, u32[]{:S(2)}) collective-permute-start(bf16[256,256]{1,0:T(8,128)(2,1)S(1)} %get-tuple-element.35), channel_id=1, source_target_pairs={{0,4},{1,5},{2,6},{3,7},{4,0},{5,1},{6,2},{7,3},{8,12},{9,13},{10,... | collective-permute-start | bytes 393224 | tf_op jit(solution)/shard_map/ppermute | solution.py:35
  14.6 19.2 %collective-permute-start.10 = (bf16[1024,256]{1,0:T(8,128)(2,1)S(1)}, bf16[1024,256]{1,0:T(8,128)(2,1)S(1)}, u32[]{:S(2)}, u32[]{:S(2)}) collective-permute-start(bf16[1024,256]{1,0:T(8,128)(2,1)S(1)} %join.1.refs_6_), channel_id=1, source_target_pairs={{0,8},{1,9},{2,10},{3,11},{4,12},{5,13},{6,14},{7,15},{8,16},{9,17... | collective-permute-start | bytes 1572872 | tf_op jit(solution)/shard_map/ppermute | solution.py:56
  19.1 10.4 %collective-permute-start.4 = (bf16[256,512]{1,0:T(8,128)(2,1)}, bf16[256,512]{1,0:T(8,128)(2,1)S(1)}, u32[]{:S(2)}, u32[]{:S(2)}) collective-permute-start(bf16[256,512]{1,0:T(8,128)(2,1)} %get-tuple-element.29), channel_id=1, source_target_pairs={{0,5},{1,4},{2,7},{3,6},{4,1},{5,0},{6,3},{7,2},{8,13},{9,12},{10,... | collective-permute-start | bytes 786440 | tf_op jit(solution)/shard_map/ppermute | solution.py:35
  21.5 12.3 %collective-permute-start.5 = (bf16[256,512]{1,0:T(8,128)(2,1)}, bf16[256,512]{1,0:T(8,128)(2,1)S(1)}, u32[]{:S(2)}, u32[]{:S(2)}) collective-permute-start(bf16[256,512]{1,0:T(8,128)(2,1)} %get-tuple-element.30), channel_id=1, source_target_pairs={{0,1},{1,0},{2,3},{3,2},{4,5},{5,4},{6,7},{7,6},{8,9},{9,8},{10,11... | collective-permute-start | bytes 786440 | tf_op jit(solution)/shard_map/ppermute | solution.py:35
  22.0 11.8 %collective-permute-start.6 = (bf16[256,512]{1,0:T(8,128)(2,1)S(1)}, bf16[256,512]{1,0:T(8,128)(2,1)S(1)}, u32[]{:S(2)}, u32[]{:S(2)}) collective-permute-start(bf16[256,512]{1,0:T(8,128)(2,1)S(1)} %get-tuple-element.31), channel_id=1, source_target_pairs={{0,4},{1,5},{2,6},{3,7},{4,0},{5,1},{6,2},{7,3},{8,12},{9,13},{10,... | collective-permute-start | bytes 786440 | tf_op jit(solution)/shard_map/ppermute | solution.py:35
  22.9 0.7 dynamic-slice-start
  44.7 15.4 %collective-permute-start.14 = (bf16[1024,256]{1,0:T(8,128)(2,1)S(1)}, bf16[1024,256]{1,0:T(8,128)(2,1)S(1)}, u32[]{:S(2)}, u32[]{:S(2)}) collective-permute-start(bf16[1024,256]{1,0:T(8,128)(2,1)S(1)} %get-tuple-element.41), channel_id=1, source_target_pairs={{8,0},{9,1},{10,2},{11,3},{12,4},{13,5},{14,6},{15,7},{16,8},{17,9... | collective-permute-start | bytes 1572872 | tf_op jit(solution)/shard_map/ppermute | solution.py:56
  46.0 17.5 %collective-permute-start.11 = (bf16[256,512]{1,0:T(8,128)(2,1)S(1)}, bf16[256,512]{1,0:T(8,128)(2,1)S(1)}, u32[]{:S(2)}, u32[]{:S(2)}) collective-permute-start(bf16[256,512]{1,0:T(8,128)(2,1)S(1)} %get-tuple-element.37), channel_id=1, source_target_pairs={{0,5},{1,4},{2,7},{3,6},{4,1},{5,0},{6,3},{7,2},{8,13},{9,12},{10,... | collective-permute-start | bytes 786440 | tf_op jit(solution)/shard_map/ppermute | solution.py:35
  48.4 15.4 %collective-permute-start.12 = (bf16[256,512]{1,0:T(8,128)(2,1)S(1)}, bf16[256,512]{1,0:T(8,128)(2,1)S(1)}, u32[]{:S(2)}, u32[]{:S(2)}) collective-permute-start(bf16[256,512]{1,0:T(8,128)(2,1)S(1)} %get-tuple-element.38), channel_id=1, source_target_pairs={{0,1},{1,0},{2,3},{3,2},{4,5},{5,4},{6,7},{7,6},{8,9},{9,8},{10,11... | collective-permute-start | bytes 786440 | tf_op jit(solution)/shard_map/ppermute | solution.py:35
  48.9 14.8 %collective-permute-start.13 = (bf16[256,512]{1,0:T(8,128)(2,1)S(1)}, bf16[256,512]{1,0:T(8,128)(2,1)S(1)}, u32[]{:S(2)}, u32[]{:S(2)}) collective-permute-start(bf16[256,512]{1,0:T(8,128)(2,1)S(1)} %get-tuple-element.39), channel_id=1, source_target_pairs={{0,4},{1,5},{2,6},{3,7},{4,0},{5,1},{6,2},{7,3},{8,12},{9,13},{10,... | collective-permute-start | bytes 786440 | tf_op jit(solution)/shard_map/ppermute | solution.py:35
  60.2 7.1 %collective-permute-start.15 = (bf16[256,256]{1,0:T(8,128)(2,1)S(1)}, bf16[256,256]{1,0:T(8,128)(2,1)S(1)}, u32[]{:S(2)}, u32[]{:S(2)}) collective-permute-start(bf16[256,256]{1,0:T(8,128)(2,1)S(1)} %get-tuple-element.43), channel_id=1, source_target_pairs={{0,5},{1,4},{2,7},{3,6},{4,1},{5,0},{6,3},{7,2},{8,13},{9,12},{10,... | collective-permute-start | bytes 393224 | tf_op jit(solution)/shard_map/ppermute | solution.py:35
  62.9 5.9 %collective-permute-start.16 = (bf16[256,256]{1,0:T(8,128)(2,1)S(1)}, bf16[256,256]{1,0:T(8,128)(2,1)S(1)}, u32[]{:S(2)}, u32[]{:S(2)}) collective-permute-start(bf16[256,256]{1,0:T(8,128)(2,1)S(1)} %get-tuple-element.44), channel_id=1, source_target_pairs={{0,1},{1,0},{2,3},{3,2},{4,5},{5,4},{6,7},{7,6},{8,9},{9,8},{10,11... | collective-permute-start | bytes 393224 | tf_op jit(solution)/shard_map/ppermute | solution.py:35
  63.5 5.4 %collective-permute-start.17 = (bf16[256,256]{1,0:T(8,128)(2,1)S(1)}, bf16[256,256]{1,0:T(8,128)(2,1)S(1)}, u32[]{:S(2)}, u32[]{:S(2)}) collective-permute-start(bf16[256,256]{1,0:T(8,128)(2,1)S(1)} %get-tuple-element.45), channel_id=1, source_target_pairs={{0,4},{1,5},{2,6},{3,7},{4,0},{5,1},{6,2},{7,3},{8,12},{9,13},{10,... | collective-permute-start | bytes 393224 | tf_op jit(solution)/shard_map/ppermute | solution.py:35
  69.0 2.4 %collective-permute-start.18 = (bf16[128,3072]{1,0:T(8,128)(2,1)S(1)}, bf16[128,3072]{1,0:T(8,128)(2,1)S(1)}, u32[]{:S(2)}, u32[]{:S(2)}) collective-permute-start(bf16[128,3072]{1,0:T(8,128)(2,1)S(1)} %bottom.1), channel_id=1, source_target_pairs={{0,2},{1,3},{2,0},{3,1},{4,6},{5,7},{6,4},{7,5},{8,10},{9,11},{10,... | collective-permute-start | bytes 2359304 | tf_op jit(solution)/shard_map/ppermute | solution.py:35

commit v10 on v9

--- a/solution.py
+++ b/solution.py
@@ -40,8 +40,7 @@
 
 
 def chip_masks(size):
-    masks = [mask for mask in range(size) if not mask & core_mask()]
-    return masks[:1] + sorted(masks[1:], key=lambda mask: -mask.bit_count())
+    return [mask for mask in range(size) if not mask & core_mask()]
 
 
 def swap_chips(pieces, size):
@@ -175,14 +174,16 @@
         start += width
 
 
-def spread_body(size, core, masks, *refs):
-    count = len(masks)
-    sets, got, outs, sems = (refs[:count], refs[count : 2 * count]), refs[2 * count], refs[-5:-1], refs[-1]
+def spread_body(size, core, masks, counts, *refs):
+    refs = list(refs)
+    take = lambda count: [refs.pop(0) for _ in range(count)]
+    sets = [take(len(masks)) for _ in counts]
+    (got,), sets_out, (sems,) = take(1), [take(count) for count in counts], take(1)
     copies, start = [], 0
-    for which, pieces in enumerate(sets):
+    for pieces, outs in zip(sets, sets_out):
         for mask, piece in zip(masks, pieces):
-            rows, width = piece.shape[0] // 2, piece.shape[1] // 2
-            for at, out in enumerate(outs[2 * which : 2 * which + 2]):
+            rows, width = piece.shape[0] // 2, piece.shape[1] // len(outs)
+            for at, out in enumerate(outs):
                 mine = out.at[:, place(partner(size, mask), width)]
                 other = out.at[:, place(partner(size, mask ^ core), width)]
                 copies.append((piece.at[:rows, at * width : (at + 1) * width], mine))
@@ -191,22 +192,21 @@
     run_copies(copies, sems)
 
 
-def spread_cores(og, grads, size):
-    rows = og[0].shape[0] // 2
-    widths = [og[0].shape[1] // 2, grads[0].shape[1] // 2]
-    give = jax.ShapeDtypeStruct((rows, size * sum(widths)), BF16)
-    got = swap(small_call(bottom_body, give, "bottom", *og, *grads), core_mask())
+def spread_cores(sets, counts, size):
+    pieces = [piece for part in sets for piece in part]
+    rows = pieces[0].shape[0] // 2
+    give = jax.ShapeDtypeStruct((rows, sum(piece.shape[1] for piece in pieces)), BF16)
+    got = swap(small_call(bottom_body, give, "bottom", *pieces), core_mask())
+    widths = [part[0].shape[1] // count for part, count in zip(sets, counts) for _ in range(count)]
     return pl.pallas_call(
-        functools.partial(spread_body, size, core_mask(), chip_masks(size)),
-        out_shape=[
-            jax.ShapeDtypeStruct((rows, width * size), BF16) for width in widths for _ in range(2)
-        ],
-        in_specs=[ANY] * (2 * len(og) + 1),
-        out_specs=[ANY] * 4,
-        scratch_shapes=[pltpu.SemaphoreType.DMA((4 * size,))],
+        functools.partial(spread_body, size, core_mask(), chip_masks(size), counts),
+        out_shape=[jax.ShapeDtypeStruct((rows, width * size), BF16) for width in widths],
+        in_specs=[ANY] * (len(pieces) + 1),
+        out_specs=[ANY] * len(widths),
+        scratch_shapes=[pltpu.SemaphoreType.DMA((len(widths) * size,))],
         compiler_params=SMALL,
         name="spread",
-    )(*og, *grads, got)
+    )(*pieces, got)
 
 
 def dot(a, b):
@@ -227,58 +227,79 @@
     return parts[0]
 
 
-def attend_body(size, core, masks, reach, tok, group, *refs):
+def taker(refs):
     refs = list(refs)
-    take = lambda count: [refs.pop(0) for _ in range(count)]
+    return lambda count: [refs.pop(0) for _ in range(count)]
+
+
+def stacked(rows, base, group, first=0):
+    parts = [slice(first + at * HEAD_DIM, first + (at + 1) * HEAD_DIM) for at in range(group)]
+    return jnp.concatenate([rows[base : base + TILE, part] for part in parts], axis=0)
+
+
+def unstacked(rows, base, group, value):
+    for at in range(group):
+        part = slice(at * TILE, (at + 1) * TILE)
+        rows[base : base + TILE, at * HEAD_DIM : (at + 1) * HEAD_DIM] = value[part]
+
+
+def set_values(va, values):
+    lane = lax.broadcasted_iota(jnp.int32, values.shape, 1)
+    va[:, :HEAD_DIM] = values
+    va[:, HEAD_DIM:] = jnp.where(lane < 2, 1.0, 0.0).astype(BF16)
+
+
+def add_rows(target, start, old, value):
+    if old:
+        target[start : start + old, :] += value[:old]
+    if old < value.shape[0]:
+        target[start + old : start + value.shape[0], :] = value[old:]
+
+
+def score_gradients(ds_scr, e, dp):
+    for at in range(0, e.shape[0], TILE):
+        part = slice(at, at + TILE)
+        ds_scr[part, :] = (e[part, :].astype(F32) * dp[part]).astype(BF16)
+
+
+def own_rows(tile):
+    start = tile * (tile + 1) // 2 * TILE
+    return slice(start, start + (tile + 1) * TILE)
+
+
+def forward_body(size, core, masks, reach, tok, group, *refs):
+    take = taker(refs)
     (seg_k, seg_q), qg_pieces, kvs = take(2), take(len(masks)), take(1 + reach)
-    og_pieces, (dkv0,), sent = take(len(masks)), take(1), take(reach)
-    qg, og, ka, va, kt, vt, dk, dv, s_scr, e_scr, ds_scr = refs
+    out_pieces, sent, (e_own, g_own, dq_part) = take(len(masks)), take(reach), take(3)
+    qg, outs, ka, va, kt, vt, dk, dv, s_scr, e_scr, ds_scr = take(11)
     width = group * HEAD_DIM
-    span = WINDOW + TILE
+    span, wide = WINDOW + TILE, group * TILE
     place_rows(size, core, masks, qg_pieces, qg)
-    va[:, HEAD_DIM:] = jnp.where(
-        lax.broadcasted_iota(jnp.int32, (va.shape[0], HEAD_DIM), 1) < 2, 1.0, 0.0
-    ).astype(BF16)
     ka[:, HEAD_DIM:] = seg_k[...]
     for lag in range(reach + 1):
         there = slice((reach - lag) * tok, (reach - lag + 1) * tok)
         kv = kvs[lag][...]
         ka[there, :HEAD_DIM] = kv[:, :HEAD_DIM]
-        va[there, :HEAD_DIM] = kv[:, HEAD_DIM:]
-        kt[:, there] = kv[:, :HEAD_DIM].T
         vt[:, there] = kv[:, HEAD_DIM:].T
-    wide_lane = lax.broadcasted_iota(jnp.int32, (group * TILE, HEAD_DIM), 1)
+        if lag:
+            kt[:, there] = kv[:, :HEAD_DIM].T
+            set_values(va.at[there, :], kv[:, HEAD_DIM:])
+    wide_lane = lax.broadcasted_iota(jnp.int32, (wide, HEAD_DIM), 1)
     row_of = lax.broadcasted_iota(jnp.int32, (TILE, TILE), 0)
     col_of = lax.broadcasted_iota(jnp.int32, (TILE, TILE), 1)
     causal = jnp.concatenate([row_of <= col_of] * group, axis=1)
 
-    def stacked(base, first):
-        here = slice(base, base + TILE)
-        return jnp.concatenate(
-            [
-                qg[here, first + at * HEAD_DIM : first + (at + 1) * HEAD_DIM]
-                for at in range(group)
-            ],
-            axis=0,
-        )
-
     def scores(tile):
         base = tile * TILE
         mine = jnp.concatenate([seg_q[base : base + TILE, :]] * group, axis=0)
-        wide = jnp.concatenate([stacked(base, 0), mine], axis=1)
-        s_scr[tile % 2] = dot_t(ka[base : base + span, :], wide)
-
-    def add(target, base, value):
-        fresh = base + (WINDOW if base else 0)
-        if base:
-            target[base:fresh, :] += value[:WINDOW]
-        target[fresh : base + span, :] = value[fresh - base :]
+        queries = jnp.concatenate([stacked(qg, base, group), mine], axis=1)
+        s_scr[tile % 2] = dot_t(ka[base : base + span, :], queries)
 
     tiles = tok // TILE
     scores(0)
     for tile in range(tiles):
         base, turn = tile * TILE, tile % 2
-        here, there = slice(base, base + TILE), slice(base, base + span)
+        early = WINDOW - base
         for at, keep in ((0, ~causal), (WINDOW, causal)):
             part = slice(at, at + TILE)
             s_scr[turn, part, :] = jnp.where(keep, s_scr[turn, part, :], FAR)
@@ -289,79 +310,151 @@
         top = jnp.max(top, axis=0, keepdims=True) * exp2_scale
         if tile + 1 < tiles:
             scores(tile + 1)
+        e_mine = e_own.at[own_rows(tile), :]
         total = None
         for at in range(0, span, TILE):
             e = jnp.exp2(s_scr[turn, at : at + TILE, :] * exp2_scale - top)
-            e_scr[turn, at : at + TILE, :] = e.astype(BF16)
+            if at < early:
+                e_scr[turn, at : at + TILE, :] = e.astype(BF16)
+            else:
+                e_mine[at - early : at - early + TILE, :] = e.astype(BF16)
             part = fold(e, jnp.add)
             total = part if total is None else total + part
         inv = 1.0 / jnp.sum(total, axis=0, keepdims=True)
-        inv = jnp.broadcast_to(inv, (HEAD_DIM, group * TILE)).T
-        out = dot(vt[:, there], e_scr[turn]).T * inv
-        out = out.astype(BF16)
-        g2 = (stacked(base, width).astype(F32) * inv).astype(BF16)
+        inv = jnp.broadcast_to(inv, (HEAD_DIM, wide)).T
+        e_early = e_scr[turn, :early, :]
+        out = dot(vt[:, base:WINDOW], e_early)
+        out = out + dot(vt[:, WINDOW : base + span], e_mine[...])
+        out = (out.T * inv).astype(BF16)
+        unstacked(outs, base, group, out)
+        g2 = (stacked(qg, base, group, width).astype(F32) * inv).astype(BF16)
         delta = jnp.sum(g2.astype(F32) * out.astype(F32), axis=1, keepdims=True)
         high = delta.astype(BF16).astype(F32)
         extra = jnp.where(wide_lane == 0, -high, jnp.where(wide_lane == 1, high - delta, 0.0))
-        dp = dot_t(va[there, :], jnp.concatenate([g2, extra.astype(BF16)], axis=1))
-        add(dv, base, dot(e_scr[turn], g2))
-        for at in range(0, span, TILE):
-            part = slice(at, at + TILE)
-            ds_scr[turn, part, :] = (e_scr[turn, part, :].astype(F32) * dp[part]).astype(BF16)
-        add(dk, base, dot(ds_scr[turn], stacked(base, 0)))
-        dq = (dot(kt[:, there], ds_scr[turn]) * logit_scale).T.astype(BF16)
-        for at in range(group):
-            part = slice(at * TILE, (at + 1) * TILE)
-            og[here, at * HEAD_DIM : (at + 1) * HEAD_DIM] = out[part]
-            og[here, width + at * HEAD_DIM : width + (at + 1) * HEAD_DIM] = dq[part]
-
-    dkv0[:, :HEAD_DIM] = dk[reach * tok :, :] * logit_scale
-    dkv0[:, HEAD_DIM:] = dv[reach * tok :, :]
+        g_wide = jnp.concatenate([g2, extra.astype(BF16)], axis=1)
+        g_own[tile * wide : (tile + 1) * wide, :] = g_wide
+        dp = dot_t(va[base:WINDOW, :], g_wide)
+        old = early if tile else 0
+        add_rows(dv, base, old, dot(e_early, g2))
+        score_gradients(ds_scr.at[turn, :early, :], e_early, dp)
+        ds = ds_scr[turn, :early, :]
+        add_rows(dk, base, old, dot(ds, stacked(qg, base, group)))
+        dq_part[:, tile * wide : (tile + 1) * wide] = dot(kt[:, base:WINDOW], ds)
+
     for lag in range(1, reach + 1):
         there = slice((reach - lag) * tok, (reach - lag + 1) * tok)
         sent[lag - 1][:, :HEAD_DIM] = (dk[there, :] * logit_scale).astype(BF16)
         sent[lag - 1][:, HEAD_DIM:] = dv[there, :].astype(BF16)
-    take_rows(size, core, masks, lambda there: og[there, :], og_pieces)
-
-
-def attend(documents, qg, kv, lags, size):
+    take_rows(size, core, masks, lambda there: outs[there, :], out_pieces)
+
+
+def backward_body(size, core, masks, tok, group, *refs):
+    take = taker(refs)
+    qg_pieces, (kv, e_own, g_own, dq_part) = take(len(masks)), take(4)
+    dq_pieces, (dkv,) = take(len(masks)), take(1)
+    qg, dqs, va, kt, dk, dv, ds_scr = take(7)
+    wide = group * TILE
+    place_rows(size, core, masks, qg_pieces, qg)
+    kt[...] = kv[:, :HEAD_DIM].T
+    set_values(va, kv[:, HEAD_DIM:])
+    for tile in range(tok // TILE):
+        base, turn = tile * TILE, tile % 2
+        count = base + TILE
+        columns = slice(tile * wide, (tile + 1) * wide)
+        e = e_own[own_rows(tile), :]
+        dp = dot_t(va[:count, :], g_own[columns, :])
+        add_rows(dv, 0, base, dot(e, g_own[columns, :HEAD_DIM]))
+        score_gradients(ds_scr.at[turn, :count, :], e, dp)
+        ds = ds_scr[turn, :count, :]
+        add_rows(dk, 0, base, dot(ds, stacked(qg, base, group)))
+        dq = (dq_part[:, columns] + dot(kt[:, :count], ds)) * logit_scale
+        unstacked(dqs, base, group, dq.T.astype(BF16))
+    dkv[:, :HEAD_DIM] = dk[...] * logit_scale
+    dkv[:, HEAD_DIM:] = dv[...]
+    take_rows(size, core, masks, lambda there: dqs[there, :], dq_pieces)
+
+
+def attend_call(kernel, out_shape, scratch_shapes, flops, name, *args):
+    return pl.pallas_call(
+        kernel,
+        out_shape=out_shape,
+        in_specs=[VMEM] * len(args),
+        out_specs=[VMEM] * len(out_shape),
+        scratch_shapes=scratch_shapes,
+        compiler_params=pltpu.CompilerParams(vmem_limit_bytes=24 * 1024 * 1024),
+        cost_estimate=pl.CostEstimate(
+            flops=flops, bytes_accessed=8 * 1024 * 1024, transcendentals=0
+        ),
+        name=name,
+    )(*args)
+
+
+def forward(documents, qg, kv, lags, size):
     rows, cols = qg[0].shape
-    tok = len(qg) * rows
+    tok, count, reach = len(qg) * rows, len(qg), len(lags)
     group = cols // (2 * HEAD_DIM)
-    reach = len(lags)
-    span = WINDOW + TILE
+    span, wide, keys, tiles = WINDOW + TILE, group * TILE, (reach + 1) * tok, tok // TILE
+    half = jax.ShapeDtypeStruct((tok, 2 * HEAD_DIM), BF16)
+    out_shape = [jax.ShapeDtypeStruct((rows, cols // 2), BF16)] * count + [half] * reach
+    out_shape += [
+        jax.ShapeDtypeStruct((own_rows(tiles - 1).stop, wide), BF16),
+        jax.ShapeDtypeStruct((tiles * wide, 2 * HEAD_DIM), BF16),
+        jax.ShapeDtypeStruct((HEAD_DIM, tiles * wide), F32),
+    ]
+    scratch = [
+        pltpu.VMEM((tok, cols), BF16),
+        pltpu.VMEM((tok, cols // 2), BF16),
+        pltpu.VMEM((keys, 2 * HEAD_DIM), BF16),
+        pltpu.VMEM((WINDOW, 2 * HEAD_DIM), BF16),
+        pltpu.VMEM((HEAD_DIM, WINDOW), BF16),
+        pltpu.VMEM((HEAD_DIM, keys), BF16),
+        pltpu.VMEM((WINDOW, HEAD_DIM), F32),
+        pltpu.VMEM((WINDOW, HEAD_DIM), F32),
+        pltpu.VMEM((2, span, wide), F32),
+        pltpu.VMEM((2, WINDOW, wide), BF16),
+        pltpu.VMEM((2, WINDOW, wide), BF16),
+    ]
+    results = attend_call(
+        functools.partial(
+            forward_body, size, core_mask(), chip_masks(size), reach, tok, group
+        ),
+        out_shape,
+        scratch,
+        8 * tok * group * span * HEAD_DIM,
+        "forward",
+        *documents,
+        *qg,
+        kv,
+        *lags,
+    )
+    return results[:count], results[count : count + reach], results[count + reach :]
+
+
+def backward(qg, kv, carried, size):
+    rows, cols = qg[0].shape
+    tok, count = len(qg) * rows, len(qg)
+    group = cols // (2 * HEAD_DIM)
     wide = group * TILE
-    keys = (reach + 1) * tok
-    half = jax.ShapeDtypeStruct((tok, 2 * HEAD_DIM), BF16)
-    flops = 6 * 2 * tok * group * span * HEAD_DIM
-    count = len(qg)
-    results = pl.pallas_call(
-        functools.partial(attend_body, size, core_mask(), chip_masks(size), reach, tok, group),
-        out_shape=[jax.ShapeDtypeStruct((rows, cols), BF16)] * count
-        + [jax.ShapeDtypeStruct((tok, 2 * HEAD_DIM), F32)]
-        + [half] * reach,
-        in_specs=[VMEM] * (count + 3 + reach),
-        out_specs=[VMEM] * (count + 1 + reach),
-        scratch_shapes=[
+    results = attend_call(
+        functools.partial(backward_body, size, core_mask(), chip_masks(size), tok, group),
+        [jax.ShapeDtypeStruct((rows, cols // 2), BF16)] * count
+        + [jax.ShapeDtypeStruct((tok, 2 * HEAD_DIM), F32)],
+        [
             pltpu.VMEM((tok, cols), BF16),
-            pltpu.VMEM((tok, cols), BF16),
-            pltpu.VMEM((keys, 2 * HEAD_DIM), BF16),
-            pltpu.VMEM((keys, 2 * HEAD_DIM), BF16),
-            pltpu.VMEM((HEAD_DIM, keys), BF16),
-            pltpu.VMEM((HEAD_DIM, keys), BF16),
-            pltpu.VMEM((keys, HEAD_DIM), F32),
-            pltpu.VMEM((keys, HEAD_DIM), F32),
-            pltpu.VMEM((2, span, wide), F32),
-            pltpu.VMEM((2, span, wide), BF16),
-            pltpu.VMEM((2, span, wide), BF16),
+            pltpu.VMEM((tok, cols // 2), BF16),
+            pltpu.VMEM((tok, 2 * HEAD_DIM), BF16),
+            pltpu.VMEM((HEAD_DIM, tok), BF16),
+            pltpu.VMEM((tok, HEAD_DIM), F32),
+            pltpu.VMEM((tok, HEAD_DIM), F32),
+            pltpu.VMEM((2, tok, wide), BF16),
         ],
-        compiler_params=pltpu.CompilerParams(vmem_limit_bytes=36 * 1024 * 1024),
-        cost_estimate=pl.CostEstimate(
-            flops=flops, bytes_accessed=8 * 1024 * 1024, transcendentals=flops // 1536
-        ),
-        name="attend",
-    )(*documents, *qg, kv, *lags)
-    return results[:count], results[count], results[count + 1 :]
+        4 * tok * group * (WINDOW + TILE) * HEAD_DIM,
+        "backward",
+        *qg,
+        kv,
+        *carried,
+    )
+    return results[:count], results[count]
 
 
 def document_columns(segment_ids, tok, size):
@@ -391,12 +484,15 @@
     lags = [shifted(kv, lag * size) for lag in range(1, reach + 1)]
     qg = swap_chips(gather_cores((query, grad_out), got[2:], size), size)
 
-    og, dkv, sent = attend(documents, qg, kv, lags, size)
-
+    out, sent, carried = forward(documents, qg, kv, lags, size)
     backs = [shifted(sent[lag - 1], -lag * size) for lag in range(1, reach + 1)]
-    og = swap_chips(og, size)
+    out = swap_chips(out, size)
+    grad_q, dkv = backward(qg, kv, carried, size)
+    both = after(*out, *grad_q)
+    out, grad_q = both[: len(out)], both[len(out) :]
+    grad_q = swap_chips(grad_q, size)
     grads = swap_chips(combine([dkv, *backs], size), size)
-    return tuple(spread_cores(og, grads, size))
+    return tuple(spread_cores([out, grad_q, grads], (1, 1, 2), size))
 
 
 def solution(mesh):

time: 73 us -> 68.6 us (0.940)
  waiting for transfers between devices: 33 us -> 23 us
  starting transfers between devices: 21.2 us -> 26.2 us
    ppermute x2, waiting for transfers between devices: 10.6 us -> 0.01 us  [shifted(): return lax.ppermute(value, BOTH, pairs)]
    ppermute x17 -> x20, starting transfers between devices: 16.4 us -> 21.2 us  [swap(): lax.ppermute(value, BOTH, [(i, i ^ mask) for i in range(device_count())])]
    unnamed x8 -> x4, local copies, waits for them, and re-layouts: 1.66 us -> 0.01 us
    pallas_call x1 -> x2, Pallas kernels: 10.9 us -> 11.9 us  [attend_call(): pl.pallas_call(kernel, out_shape=out_shape, in_specs=[VMEM] * len(args),...]
    slice x4, local copies, waits for them, and re-layouts: 1.09 us -> 1.99 us  [this_core(): shares = [array[:, r * width:(r + 1) * width] for r in range(size)]]
    pallas_call x5, Pallas kernels: 1.27 us -> 0.5 us  [small_call(): pl.pallas_call(kernel, out_shape=out_shape, in_specs=[VMEM] * len(args),...]
    ppermute x17 -> x20, waiting for transfers between devices: 22.4 us -> 23 us  [swap(): lax.ppermute(value, BOTH, [(i, i ^ mask) for i in range(device_count())])]
  transfers between devices with their start and end apart: 19 -> 22, of which waited for: 9 -> 10; matrix products, arithmetic and copies ran while one was open for 3% -> 6% of each run, Pallas kernels for 2% -> 5%
where the time goes in v10:
time: 68.6 us; the launch traced here: 68.1 us
  starting transfers between devices  26.2 us (38%)
  waiting for transfers between devices  23 us (34%)
  Pallas kernels  13.8 us (20%)
  local copies, waits for them, and re-layouts  3.39 us (5%)
  between operations  1.04 us (2%)
  other arithmetic  0.74 us (1%)
    ppermute x20, waiting for transfers between devices, swap(): lax.ppermute(value, BOTH, [(i, i ^ mask) for i in range(device_count())])  23 us
    ppermute x20, starting transfers between devices, swap(): lax.ppermute(value, BOTH, [(i, i ^ mask) for i in range(device_count())])  21.2 us
    pallas_call x2, Pallas kernels, attend_call(): pl.pallas_call(kernel, out_shape=out_shape, in_specs=[VMEM] * len(args),...  11.9 us
    ppermute x2, starting transfers between devices, shifted(): return lax.ppermute(value, BOTH, pairs)  5 us
    slice x4, local copies, waits for them, and re-layouts, this_core(): shares = [array[:, r * width:(r + 1) * width] for r in range(size)]  1.99 us
    pallas_call x1, Pallas kernels, spread_cores(): pl.pallas_call(functools.partial(spread_body, size, core_mask(), chip_mas...  1.39 us
  transfers between devices with their start and end apart: 22, of which 10 were waited for; matrix products, arithmetic and copies ran while one was open for 6% of the time, Pallas kernels for 5%

profile of v10, /device:TPU:0, one launch (start us, length us, event | category | flops | bytes accessed | tf_op | source)
XLA Modules:
  0.0 68.1 jit_solution(6762068373274585855)
XLA Ops:
  0.7 0.5 collective-permute-start
  1.8 1.0 %fusion.3 = (bf16[128,256]{1,0:T(8,128)(2,1)S(1)}, bf16[128,256]{1,0:T(8,128)(2,1)S(1)}, bf16[128,256]{1,0:T(8,128)(2,1)S(1)}, bf16[128,256]{1,0:T(8,128)(2,1)S(1)}) fusion(bf16[128,1024]{1,0:T(8,128)(2,1)} %param.6), kind=kLoop, calls=%fused_computation.12 | loop fusion | bytes 524288 | tf_op jit(solution)/shard_map/slice | solution.py:94
  2.7 1.0 %fusion.2 = (bf16[128,256]{1,0:T(8,128)(2,1)S(1)}, bf16[128,256]{1,0:T(8,128)(2,1)S(1)}, bf16[128,256]{1,0:T(8,128)(2,1)S(1)}, bf16[128,256]{1,0:T(8,128)(2,1)S(1)}) fusion(bf16[128,1024]{1,0:T(8,128)(2,1)} %param.7), kind=kLoop, calls=%fused_computation.11 | loop fusion | bytes 524288 | tf_op jit(solution)/shard_map/slice | solution.py:94
  3.7 0.7 %pad_dynamic-slice_fusion = s32[2048]{0:T(1024)S(1)} fusion(s32[]{:T(128)S(6)} %select_n.62, s32[4096]{0:T(1024)} %param.9), kind=kLoop, calls=%fused_computation.8 | loop fusion | bytes 24580 | tf_op jit(solution)/shard_map/dynamic_slice | solution.py:463
  4.6 3.0 %collective-permute-start.7 = (bf16[256,256]{1,0:T(8,128)(2,1)S(1)}, bf16[256,256]{1,0:T(8,128)(2,1)S(1)}, u32[]{:S(2)}, u32[]{:S(2)}) collective-permute-start(bf16[256,256]{1,0:T(8,128)(2,1)S(1)} %get-tuple-element.48), channel_id=1, source_target_pairs={{0,1},{1,0},{2,3},{3,2},{4,5},{5,4},{6,7},{7,6},{8,9},{9,8},{10,11... | collective-permute-start | bytes 393224 | tf_op jit(solution)/shard_map/ppermute | solution.py:35
  7.6 1.5 %collective-permute-start.8 = (bf16[256,256]{1,0:T(8,128)(2,1)S(1)}, bf16[256,256]{1,0:T(8,128)(2,1)S(1)}, u32[]{:S(2)}, u32[]{:S(2)}) collective-permute-start(bf16[256,256]{1,0:T(8,128)(2,1)S(1)} %get-tuple-element.49), channel_id=1, source_target_pairs={{0,4},{1,5},{2,6},{3,7},{4,0},{5,1},{6,2},{7,3},{8,12},{9,13},{10,... | collective-permute-start | bytes 393224 | tf_op jit(solution)/shard_map/ppermute | solution.py:35
  9.4 2.1 %collective-permute-done.7.refs_1_ = bf16[256,256]{1,0:T(8,128)(2,1)S(1)} collective-permute-done((bf16[256,256]{1,0:T(8,128)(2,1)S(1)}, bf16[256,256]{1,0:T(8,128)(2,1)S(1)}, u32[]{:S(2)}, u32[]{:S(2)}) %collective-permute-start.7) | collective-permute-done | bytes 131104 | tf_op jit(solution)/shard_map/ppermute | solution.py:35
  11.5 4.1 %collective-permute-done.8.refs_2_ = bf16[256,256]{1,0:T(8,128)(2,1)S(1)} collective-permute-done((bf16[256,256]{1,0:T(8,128)(2,1)S(1)}, bf16[256,256]{1,0:T(8,128)(2,1)S(1)}, u32[]{:S(2)}, u32[]{:S(2)}) %collective-permute-start.8) | collective-permute-done | bytes 131104 | tf_op jit(solution)/shard_map/ppermute | solution.py:35
  15.7 3.5 %collective-permute-start.10 = (bf16[1024,256]{1,0:T(8,128)(2,1)S(1)}, bf16[1024,256]{1,0:T(8,128)(2,1)S(1)}, u32[]{:S(2)}, u32[]{:S(2)}) collective-permute-start(bf16[1024,256]{1,0:T(8,128)(2,1)S(1)} %join.1.refs_6_.refs_4_), channel_id=1, source_target_pairs={{0,8},{1,9},{2,10},{3,11},{4,12},{5,13},{6,14},{7,15},{8,16},{9,17... | collective-permute-start | bytes 1572872 | tf_op jit(solution)/shard_map/ppermute | solution.py:55
  19.4 1.3 %collective-permute-start.4 = (bf16[256,512]{1,0:T(8,128)(2,1)S(1)}, bf16[256,512]{1,0:T(8,128)(2,1)S(1)}, u32[]{:S(2)}, u32[]{:S(2)}) collective-permute-start(bf16[256,512]{1,0:T(8,128)(2,1)S(1)} %get-tuple-element.44), channel_id=1, source_target_pairs={{0,1},{1,0},{2,3},{3,2},{4,5},{5,4},{6,7},{7,6},{8,9},{9,8},{10,11... | collective-permute-start | bytes 786440 | tf_op jit(solution)/shard_map/ppermute | solution.py:35
  20.7 0.8 %collective-permute-start.5 = (bf16[256,512]{1,0:T(8,128)(2,1)S(1)}, bf16[256,512]{1,0:T(8,128)(2,1)S(1)}, u32[]{:S(2)}, u32[]{:S(2)}) collective-permute-start(bf16[256,512]{1,0:T(8,128)(2,1)S(1)} %get-tuple-element.45), channel_id=1, source_target_pairs={{0,4},{1,5},{2,6},{3,7},{4,0},{5,1},{6,2},{7,3},{8,12},{9,13},{10,... | collective-permute-start | bytes 786440 | tf_op jit(solution)/shard_map/ppermute | solution.py:35
  21.5 1.4 %collective-permute-start.6 = (bf16[256,512]{1,0:T(8,128)(2,1)S(1)}, bf16[256,512]{1,0:T(8,128)(2,1)S(1)}, u32[]{:S(2)}, u32[]{:S(2)}) collective-permute-start(bf16[256,512]{1,0:T(8,128)(2,1)S(1)} %get-tuple-element.46), channel_id=1, source_target_pairs={{0,5},{1,4},{2,7},{3,6},{4,1},{5,0},{6,3},{7,2},{8,13},{9,12},{10,... | collective-permute-start | bytes 786440 | tf_op jit(solution)/shard_map/ppermute | solution.py:35
  23.3 0.7 %dynamic_slice.7 = s32[1024]{0:T(1024)S(1)} dynamic-slice(s32[4096]{0:T(1024)} %param.9, s32[]{:T(128)S(6)} %select_n.64), dynamic_slice_sizes={1024} | dynamic-slice | bytes 8196 | tf_op jit(solution)/shard_map/dynamic_slice | solution.py:464
  24.2 4.5 %collective-permute-done.4.refs_3_.refs_1_ = bf16[256,512]{1,0:T(8,128)(2,1)S(1)} collective-permute-done((bf16[256,512]{1,0:T(8,128)(2,1)S(1)}, bf16[256,512]{1,0:T(8,128)(2,1)S(1)}, u32[]{:S(2)}, u32[]{:S(2)}) %collective-permute-start.4) | collective-permute-done | bytes 262176 | tf_op jit(solution)/shard_map/ppermute | solution.py:35
  28.7 4.5 %collective-permute-done.5.refs_4_.refs_2_ = bf16[256,512]{1,0:T(8,128)(2,1)S(1)} collective-permute-done((bf16[256,512]{1,0:T(8,128)(2,1)S(1)}, bf16[256,512]{1,0:T(8,128)(2,1)S(1)}, u32[]{:S(2)}, u32[]{:S(2)}) %collective-permute-start.5) | collective-permute-done | bytes 262176 | tf_op jit(solution)/shard_map/ppermute | solution.py:35
  33.2 8.9 %forward.1 = (bf16[256,256]{1,0:T(8,128)(2,1)S(1)}, bf16[256,256]{1,0:T(8,128)(2,1)S(1)}, bf16[256,256]{1,0:T(8,128)(2,1)S(1)}, bf16[256,256]{1,0:T(8,128)(2,1)S...) custom-call(bf16[2048,128]{1,0:T(8,128)(2,1)S(1)} %select_convert_fu, ...), custom_call_target="tpu_custom_call" | custom-call | flops 2415919104 | bytes 8388608 | tf_op jit(solution)/shard_map/forward/pallas_call | solution.py:378
  42.1 1.5 %collective-permute-start.17 = (bf16[1024,256]{1,0:T(8,128)(2,1)S(1)}, bf16[1024,256]{1,0:T(8,128)(2,1)S(1)}, u32[]{:S(2)}, u32[]{:S(2)}) collective-permute-start(bf16[1024,256]{1,0:T(8,128)(2,1)S(1)} %get-tuple-element.71), channel_id=1, source_target_pairs={{8,0},{9,1},{10,2},{11,3},{12,4},{13,5},{14,6},{15,7},{16,8},{17,9... | collective-permute-start | bytes 1572872 | tf_op jit(solution)/shard_map/ppermute | solution.py:55
  44.0 1.4 %collective-permute-start.12 = (bf16[256,256]{1,0:T(8,128)(2,1)S(1)}, bf16[256,256]{1,0:T(8,128)(2,1)S(1)}, u32[]{:S(2)}, u32[]{:S(2)}) collective-permute-start(bf16[256,256]{1,0:T(8,128)(2,1)S(1)} %get-tuple-element.53), channel_id=1, source_target_pairs={{0,4},{1,5},{2,6},{3,7},{4,0},{5,1},{6,2},{7,3},{8,12},{9,13},{10,... | collective-permute-start | bytes 393224 | tf_op jit(solution)/shard_map/ppermute | solution.py:35
  45.4 1.7 %collective-permute-start.13 = (bf16[256,256]{1,0:T(8,128)(2,1)S(1)}, bf16[256,256]{1,0:T(8,128)(2,1)S(1)}, u32[]{:S(2)}, u32[]{:S(2)}) collective-permute-start(bf16[256,256]{1,0:T(8,128)(2,1)S(1)} %get-tuple-element.54), channel_id=1, source_target_pairs={{0,5},{1,4},{2,7},{3,6},{4,1},{5,0},{6,3},{7,2},{8,13},{9,12},{10,... | collective-permute-start | bytes 393224 | tf_op jit(solution)/shard_map/ppermute | solution.py:35
  47.1 3.1 %backward.1 = (bf16[256,256]{1,0:T(8,128)(2,1)S(1)}, bf16[256,256]{1,0:T(8,128)(2,1)S(1)}, bf16[256,256]{1,0:T(8,128)(2,1)S(1)}, bf16[256,256]{1,0:T(8,128)(2,1)S(1)}, f32[1024,256]{1,0:T(8,128)S(1)}) custom-call(bf16[256,512]{1,0:T(8,128)(2,1)S(1)} %get-tuple-element.43.refs_2_.refs_0_, bf16[256,512]{1,0:T(8,128)(2,1)S(1)} %collective-permute-done.4.refs_3_.refs_1_, ...), custom_call_target="tpu_custom_call" | custom-call | flops 1207959552 | bytes 8388608 | tf_op jit(solution)/shard_map/backward/pallas_call | solution.py:378
  50.2 1.8 %collective-permute-done.13.refs_3_ = bf16[256,256]{1,0:T(8,128)(2,1)S(1)} collective-permute-done((bf16[256,256]{1,0:T(8,128)(2,1)S(1)}, bf16[256,256]{1,0:T(8,128)(2,1)S(1)}, u32[]{:S(2)}, u32[]{:S(2)}) %collective-permute-start.13) | collective-permute-done | bytes 131104 | tf_op jit(solution)/shard_map/ppermute | solution.py:35
  52.0 1.0 %collective-permute-start.14 = (bf16[256,256]{1,0:T(8,128)(2,1)S(1)}, bf16[256,256]{1,0:T(8,128)(2,1)S(1)}, u32[]{:S(2)}, u32[]{:S(2)}) collective-permute-start(bf16[256,256]{1,0:T(8,128)(2,1)S(1)} %get-tuple-element.67), channel_id=1, source_target_pairs={{0,1},{1,0},{2,3},{3,2},{4,5},{5,4},{6,7},{7,6},{8,9},{9,8},{10,11... | collective-permute-start | bytes 393224 | tf_op jit(solution)/shard_map/ppermute | solution.py:35
  53.0 1.7 %collective-permute-start.15 = (bf16[256,256]{1,0:T(8,128)(2,1)S(1)}, bf16[256,256]{1,0:T(8,128)(2,1)S(1)}, u32[]{:S(2)}, u32[]{:S(2)}) collective-permute-start(bf16[256,256]{1,0:T(8,128)(2,1)S(1)} %get-tuple-element.68), channel_id=1, source_target_pairs={{0,4},{1,5},{2,6},{3,7},{4,0},{5,1},{6,2},{7,3},{8,12},{9,13},{10,... | collective-permute-start | bytes 393224 | tf_op jit(solution)/shard_map/ppermute | solution.py:35
  54.6 0.8 %collective-permute-start.16 = (bf16[256,256]{1,0:T(8,128)(2,1)S(1)}, bf16[256,256]{1,0:T(8,128)(2,1)S(1)}, u32[]{:S(2)}, u32[]{:S(2)}) collective-permute-start(bf16[256,256]{1,0:T(8,128)(2,1)S(1)} %get-tuple-element.69), channel_id=1, source_target_pairs={{0,5},{1,4},{2,7},{3,6},{4,1},{5,0},{6,3},{7,2},{8,13},{9,12},{10,... | collective-permute-start | bytes 393224 | tf_op jit(solution)/shard_map/ppermute | solution.py:35
  55.5 1.1 %collective-permute-start.18 = (bf16[256,256]{1,0:T(8,128)(2,1)S(1)}, bf16[256,256]{1,0:T(8,128)(2,1)S(1)}, u32[]{:S(2)}, u32[]{:S(2)}) collective-permute-start(bf16[256,256]{1,0:T(8,128)(2,1)S(1)} %get-tuple-element.73), channel_id=1, source_target_pairs={{0,1},{1,0},{2,3},{3,2},{4,5},{5,4},{6,7},{7,6},{8,9},{9,8},{10,11... | collective-permute-start | bytes 393224 | tf_op jit(solution)/shard_map/ppermute | solution.py:35
  56.6 1.7 %collective-permute-start.19 = (bf16[256,256]{1,0:T(8,128)(2,1)S(1)}, bf16[256,256]{1,0:T(8,128)(2,1)S(1)}, u32[]{:S(2)}, u32[]{:S(2)}) collective-permute-start(bf16[256,256]{1,0:T(8,128)(2,1)S(1)} %get-tuple-element.74), channel_id=1, source_target_pairs={{0,4},{1,5},{2,6},{3,7},{4,0},{5,1},{6,2},{7,3},{8,12},{9,13},{10,... | collective-permute-start | bytes 393224 | tf_op jit(solution)/shard_map/ppermute | solution.py:35
  58.3 2.1 %collective-permute-start.20 = (bf16[256,256]{1,0:T(8,128)(2,1)S(1)}, bf16[256,256]{1,0:T(8,128)(2,1)S(1)}, u32[]{:S(2)}, u32[]{:S(2)}) collective-permute-start(bf16[256,256]{1,0:T(8,128)(2,1)S(1)} %get-tuple-element.75), channel_id=1, source_target_pairs={{0,5},{1,4},{2,7},{3,6},{4,1},{5,0},{6,3},{7,2},{8,13},{9,12},{10,... | collective-permute-start | bytes 393224 | tf_op jit(solution)/shard_map/ppermute | solution.py:35
  60.4 0.6 collective-permute-done.15.refs_6_
  61.2 1.9 %collective-permute-done.19.refs_10_ = bf16[256,256]{1,0:T(8,128)(2,1)S(1)} collective-permute-done((bf16[256,256]{1,0:T(8,128)(2,1)S(1)}, bf16[256,256]{1,0:T(8,128)(2,1)S(1)}, u32[]{:S(2)}, u32[]{:S(2)}) %collective-permute-start.19) | collective-permute-done | bytes 131104 | tf_op jit(solution)/shard_map/ppermute | solution.py:35
  63.1 1.1 %collective-permute-done.20.refs_11_ = bf16[256,256]{1,0:T(8,128)(2,1)S(1)} collective-permute-done((bf16[256,256]{1,0:T(8,128)(2,1)S(1)}, bf16[256,256]{1,0:T(8,128)(2,1)S(1)}, u32[]{:S(2)}, u32[]{:S(2)}) %collective-permute-start.20) | collective-permute-done | bytes 131104 | tf_op jit(solution)/shard_map/ppermute | solution.py:35
  64.3 2.3 %collective-permute-done.21.refs_12_ = bf16[128,3072]{1,0:T(8,128)(2,1)S(1)} collective-permute-done((bf16[128,3072]{1,0:T(8,128)(2,1)S(1)}, bf16[128,3072]{1,0:T(8,128)(2,1)S(1)}, u32[]{:S(2)}, u32[]{:S(2)}) %collective-permute-start.21) | collective-permute-done | bytes 786464 | tf_op jit(solution)/shard_map/ppermute | solution.py:35
  66.6 1.4 %spread.1 = (bf16[128,2048]{1,0:T(8,128)(2,1)}, bf16[128,2048]{1,0:T(8,128)(2,1)}, bf16[128,1024]{1,0:T(8,128)(2,1)}, bf16[128,1024]{1,0:T(8,128)(2,1)}) custom-call(bf16[256,256]{1,0:T(8,128)(2,1)S(1)} %get-tuple-element.62.refs_0_, bf16[256,256]{1,0:T(8,128)(2,1)S(1)} %collective-permute-done.11.refs_1_, ...), custom_call_target="tpu_custom_call" | custom-call | tf_op jit(solution)/shard_map/spread/pallas_call | solution.py:201
  (35 shorter events, 2.7 us)
Async XLA Ops:
  0.6 8.5 %copy-start = (bf16[128,2048]{1,0:T(8,128)(2,1)S(1)}, bf16[128,2048]{1,0:T(8,128)(2,1)}, u32[]{:S(2)}) copy-start(bf16[128,2048]{1,0:T(8,128)(2,1)} %param.5) | copy-start | bytes 1572868
  0.6 8.6 %copy-start.1 = (bf16[128,2048]{1,0:T(8,128)(2,1)S(1)}, bf16[128,2048]{1,0:T(8,128)(2,1)}, u32[]{:S(2)}) copy-start(bf16[128,2048]{1,0:T(8,128)(2,1)} %param.8) | copy-start | bytes 1572868
  0.7 3.8 %collective-permute-start = (bf16[128,1024]{1,0:T(8,128)(2,1)}, bf16[128,1024]{1,0:T(8,128)(2,1)S(1)}, u32[]{:S(2)}, u32[]{:S(2)}) collective-permute-start(bf16[128,1024]{1,0:T(8,128)(2,1)} %param.6), channel_id=1, source_target_pairs={{0,2},{1,3},{2,0},{3,1},{4,6},{5,7},{6,4},{7,5},{8,10},{9,11},{10,... | collective-permute-start | bytes 786440 | tf_op jit(solution)/shard_map/ppermute | solution.py:35
  1.2 3.3 %collective-permute-start.1 = (bf16[128,1024]{1,0:T(8,128)(2,1)}, bf16[128,1024]{1,0:T(8,128)(2,1)S(1)}, u32[]{:S(2)}, u32[]{:S(2)}) collective-permute-start(bf16[128,1024]{1,0:T(8,128)(2,1)} %param.7), channel_id=1, source_target_pairs={{0,2},{1,3},{2,0},{3,1},{4,6},{5,7},{6,4},{7,5},{8,10},{9,11},{10,... | collective-permute-start | bytes 786440 | tf_op jit(solution)/shard_map/ppermute | solution.py:35
  1.2 18.0 %collective-permute-start.2 = (bf16[128,2048]{1,0:T(8,128)(2,1)}, bf16[128,2048]{1,0:T(8,128)(2,1)S(1)}, u32[]{:S(2)}, u32[]{:S(2)}) collective-permute-start(bf16[128,2048]{1,0:T(8,128)(2,1)} %param.5), channel_id=1, source_target_pairs={{0,2},{1,3},{2,0},{3,1},{4,6},{5,7},{6,4},{7,5},{8,10},{9,11},{10,... | collective-permute-start | bytes 1572872 | tf_op jit(solution)/shard_map/ppermute | solution.py:35
  1.7 17.6 %collective-permute-start.3 = (bf16[128,2048]{1,0:T(8,128)(2,1)}, bf16[128,2048]{1,0:T(8,128)(2,1)S(1)}, u32[]{:S(2)}, u32[]{:S(2)}) collective-permute-start(bf16[128,2048]{1,0:T(8,128)(2,1)} %param.8), channel_id=1, source_target_pairs={{0,2},{1,3},{2,0},{3,1},{4,6},{5,7},{6,4},{7,5},{8,10},{9,11},{10,... | collective-permute-start | bytes 1572872 | tf_op jit(solution)/shard_map/ppermute | solution.py:35
  4.6 6.9 %collective-permute-start.7 = (bf16[256,256]{1,0:T(8,128)(2,1)S(1)}, bf16[256,256]{1,0:T(8,128)(2,1)S(1)}, u32[]{:S(2)}, u32[]{:S(2)}) collective-permute-start(bf16[256,256]{1,0:T(8,128)(2,1)S(1)} %get-tuple-element.48), channel_id=1, source_target_pairs={{0,1},{1,0},{2,3},{3,2},{4,5},{5,4},{6,7},{7,6},{8,9},{9,8},{10,11... | collective-permute-start | bytes 393224 | tf_op jit(solution)/shard_map/ppermute | solution.py:35
  7.6 8.0 %collective-permute-start.8 = (bf16[256,256]{1,0:T(8,128)(2,1)S(1)}, bf16[256,256]{1,0:T(8,128)(2,1)S(1)}, u32[]{:S(2)}, u32[]{:S(2)}) collective-permute-start(bf16[256,256]{1,0:T(8,128)(2,1)S(1)} %get-tuple-element.49), channel_id=1, source_target_pairs={{0,4},{1,5},{2,6},{3,7},{4,0},{5,1},{6,2},{7,3},{8,12},{9,13},{10,... | collective-permute-start | bytes 393224 | tf_op jit(solution)/shard_map/ppermute | solution.py:35
  9.1 6.5 %collective-permute-start.9 = (bf16[256,256]{1,0:T(8,128)(2,1)S(1)}, bf16[256,256]{1,0:T(8,128)(2,1)S(1)}, u32[]{:S(2)}, u32[]{:S(2)}) collective-permute-start(bf16[256,256]{1,0:T(8,128)(2,1)S(1)} %get-tuple-element.50), channel_id=1, source_target_pairs={{0,5},{1,4},{2,7},{3,6},{4,1},{5,0},{6,3},{7,2},{8,13},{9,12},{10,... | collective-permute-start | bytes 393224 | tf_op jit(solution)/shard_map/ppermute | solution.py:35
  15.7 17.5 %collective-permute-start.10 = (bf16[1024,256]{1,0:T(8,128)(2,1)S(1)}, bf16[1024,256]{1,0:T(8,128)(2,1)S(1)}, u32[]{:S(2)}, u32[]{:S(2)}) collective-permute-start(bf16[1024,256]{1,0:T(8,128)(2,1)S(1)} %join.1.refs_6_.refs_4_), channel_id=1, source_target_pairs={{0,8},{1,9},{2,10},{3,11},{4,12},{5,13},{6,14},{7,15},{8,16},{9,17... | collective-permute-start | bytes 1572872 | tf_op jit(solution)/shard_map/ppermute | solution.py:55
  19.4 9.3 %collective-permute-start.4 = (bf16[256,512]{1,0:T(8,128)(2,1)S(1)}, bf16[256,512]{1,0:T(8,128)(2,1)S(1)}, u32[]{:S(2)}, u32[]{:S(2)}) collective-permute-start(bf16[256,512]{1,0:T(8,128)(2,1)S(1)} %get-tuple-element.44), channel_id=1, source_target_pairs={{0,1},{1,0},{2,3},{3,2},{4,5},{5,4},{6,7},{7,6},{8,9},{9,8},{10,11... | collective-permute-start | bytes 786440 | tf_op jit(solution)/shard_map/ppermute | solution.py:35
  20.7 12.5 %collective-permute-start.5 = (bf16[256,512]{1,0:T(8,128)(2,1)S(1)}, bf16[256,512]{1,0:T(8,128)(2,1)S(1)}, u32[]{:S(2)}, u32[]{:S(2)}) collective-permute-start(bf16[256,512]{1,0:T(8,128)(2,1)S(1)} %get-tuple-element.45), channel_id=1, source_target_pairs={{0,4},{1,5},{2,6},{3,7},{4,0},{5,1},{6,2},{7,3},{8,12},{9,13},{10,... | collective-permute-start | bytes 786440 | tf_op jit(solution)/shard_map/ppermute | solution.py:35
  21.5 11.7 %collective-permute-start.6 = (bf16[256,512]{1,0:T(8,128)(2,1)S(1)}, bf16[256,512]{1,0:T(8,128)(2,1)S(1)}, u32[]{:S(2)}, u32[]{:S(2)}) collective-permute-start(bf16[256,512]{1,0:T(8,128)(2,1)S(1)} %get-tuple-element.46), channel_id=1, source_target_pairs={{0,5},{1,4},{2,7},{3,6},{4,1},{5,0},{6,3},{7,2},{8,13},{9,12},{10,... | collective-permute-start | bytes 786440 | tf_op jit(solution)/shard_map/ppermute | solution.py:35
  42.1 13.4 %collective-permute-start.17 = (bf16[1024,256]{1,0:T(8,128)(2,1)S(1)}, bf16[1024,256]{1,0:T(8,128)(2,1)S(1)}, u32[]{:S(2)}, u32[]{:S(2)}) collective-permute-start(bf16[1024,256]{1,0:T(8,128)(2,1)S(1)} %get-tuple-element.71), channel_id=1, source_target_pairs={{8,0},{9,1},{10,2},{11,3},{12,4},{13,5},{14,6},{15,7},{16,8},{17,9... | collective-permute-start | bytes 1572872 | tf_op jit(solution)/shard_map/ppermute | solution.py:55
  43.6 6.6 %collective-permute-start.11 = (bf16[256,256]{1,0:T(8,128)(2,1)S(1)}, bf16[256,256]{1,0:T(8,128)(2,1)S(1)}, u32[]{:S(2)}, u32[]{:S(2)}) collective-permute-start(bf16[256,256]{1,0:T(8,128)(2,1)S(1)} %get-tuple-element.52), channel_id=1, source_target_pairs={{0,1},{1,0},{2,3},{3,2},{4,5},{5,4},{6,7},{7,6},{8,9},{9,8},{10,11... | collective-permute-start | bytes 393224 | tf_op jit(solution)/shard_map/ppermute | solution.py:35
  44.0 6.2 %collective-permute-start.12 = (bf16[256,256]{1,0:T(8,128)(2,1)S(1)}, bf16[256,256]{1,0:T(8,128)(2,1)S(1)}, u32[]{:S(2)}, u32[]{:S(2)}) collective-permute-start(bf16[256,256]{1,0:T(8,128)(2,1)S(1)} %get-tuple-element.53), channel_id=1, source_target_pairs={{0,4},{1,5},{2,6},{3,7},{4,0},{5,1},{6,2},{7,3},{8,12},{9,13},{10,... | collective-permute-start | bytes 393224 | tf_op jit(solution)/shard_map/ppermute | solution.py:35
  45.4 6.5 %collective-permute-start.13 = (bf16[256,256]{1,0:T(8,128)(2,1)S(1)}, bf16[256,256]{1,0:T(8,128)(2,1)S(1)}, u32[]{:S(2)}, u32[]{:S(2)}) collective-permute-start(bf16[256,256]{1,0:T(8,128)(2,1)S(1)} %get-tuple-element.54), channel_id=1, source_target_pairs={{0,5},{1,4},{2,7},{3,6},{4,1},{5,0},{6,3},{7,2},{8,13},{9,12},{10,... | collective-permute-start | bytes 393224 | tf_op jit(solution)/shard_map/ppermute | solution.py:35
  52.0 6.3 %collective-permute-start.14 = (bf16[256,256]{1,0:T(8,128)(2,1)S(1)}, bf16[256,256]{1,0:T(8,128)(2,1)S(1)}, u32[]{:S(2)}, u32[]{:S(2)}) collective-permute-start(bf16[256,256]{1,0:T(8,128)(2,1)S(1)} %get-tuple-element.67), channel_id=1, source_target_pairs={{0,1},{1,0},{2,3},{3,2},{4,5},{5,4},{6,7},{7,6},{8,9},{9,8},{10,11... | collective-permute-start | bytes 393224 | tf_op jit(solution)/shard_map/ppermute | solution.py:35
  53.0 8.0 %collective-permute-start.15 = (bf16[256,256]{1,0:T(8,128)(2,1)S(1)}, bf16[256,256]{1,0:T(8,128)(2,1)S(1)}, u32[]{:S(2)}, u32[]{:S(2)}) collective-permute-start(bf16[256,256]{1,0:T(8,128)(2,1)S(1)} %get-tuple-element.68), channel_id=1, source_target_pairs={{0,4},{1,5},{2,6},{3,7},{4,0},{5,1},{6,2},{7,3},{8,12},{9,13},{10,... | collective-permute-start | bytes 393224 | tf_op jit(solution)/shard_map/ppermute | solution.py:35
  54.6 6.3 %collective-permute-start.16 = (bf16[256,256]{1,0:T(8,128)(2,1)S(1)}, bf16[256,256]{1,0:T(8,128)(2,1)S(1)}, u32[]{:S(2)}, u32[]{:S(2)}) collective-permute-start(bf16[256,256]{1,0:T(8,128)(2,1)S(1)} %get-tuple-element.69), channel_id=1, source_target_pairs={{0,5},{1,4},{2,7},{3,6},{4,1},{5,0},{6,3},{7,2},{8,13},{9,12},{10,... | collective-permute-start | bytes 393224 | tf_op jit(solution)/shard_map/ppermute | solution.py:35
  55.5 5.6 %collective-permute-start.18 = (bf16[256,256]{1,0:T(8,128)(2,1)S(1)}, bf16[256,256]{1,0:T(8,128)(2,1)S(1)}, u32[]{:S(2)}, u32[]{:S(2)}) collective-permute-start(bf16[256,256]{1,0:T(8,128)(2,1)S(1)} %get-tuple-element.73), channel_id=1, source_target_pairs={{0,1},{1,0},{2,3},{3,2},{4,5},{5,4},{6,7},{7,6},{8,9},{9,8},{10,11... | collective-permute-start | bytes 393224 | tf_op jit(solution)/shard_map/ppermute | solution.py:35
  56.6 6.4 %collective-permute-start.19 = (bf16[256,256]{1,0:T(8,128)(2,1)S(1)}, bf16[256,256]{1,0:T(8,128)(2,1)S(1)}, u32[]{:S(2)}, u32[]{:S(2)}) collective-permute-start(bf16[256,256]{1,0:T(8,128)(2,1)S(1)} %get-tuple-element.74), channel_id=1, source_target_pairs={{0,4},{1,5},{2,6},{3,7},{4,0},{5,1},{6,2},{7,3},{8,12},{9,13},{10,... | collective-permute-start | bytes 393224 | tf_op jit(solution)/shard_map/ppermute | solution.py:35
  58.3 5.9 %collective-permute-start.20 = (bf16[256,256]{1,0:T(8,128)(2,1)S(1)}, bf16[256,256]{1,0:T(8,128)(2,1)S(1)}, u32[]{:S(2)}, u32[]{:S(2)}) collective-permute-start(bf16[256,256]{1,0:T(8,128)(2,1)S(1)} %get-tuple-element.75), channel_id=1, source_target_pairs={{0,5},{1,4},{2,7},{3,6},{4,1},{5,0},{6,3},{7,2},{8,13},{9,12},{10,... | collective-permute-start | bytes 393224 | tf_op jit(solution)/shard_map/ppermute | solution.py:35
  64.2 2.4 %collective-permute-start.21 = (bf16[128,3072]{1,0:T(8,128)(2,1)S(1)}, bf16[128,3072]{1,0:T(8,128)(2,1)S(1)}, u32[]{:S(2)}, u32[]{:S(2)}) collective-permute-start(bf16[128,3072]{1,0:T(8,128)(2,1)S(1)} %bottom.1), channel_id=1, source_target_pairs={{0,2},{1,3},{2,0},{3,1},{4,6},{5,7},{6,4},{7,5},{8,10},{9,11},{10,... | collective-permute-start | bytes 2359304 | tf_op jit(solution)/shard_map/ppermute | solution.py:35

commit v11 on v10

--- a/solution.py
+++ b/solution.py
@@ -267,79 +267,126 @@
     return slice(start, start + (tile + 1) * TILE)
 
 
+def query_columns(qg, seg_q, base, group):
+    mine = jnp.concatenate([seg_q[base : base + TILE, :]] * group, axis=0)
+    return jnp.concatenate([stacked(qg, base, group), mine], axis=1)
+
+
+def fold_rows(rows, op):
+    parts = [fold(rows[at : at + TILE, :], op) for at in range(0, rows.shape[0], TILE)]
+    whole = functools.reduce(op, parts)
+    reduce = jnp.max if op is jnp.maximum else jnp.sum
+    return reduce(whole, axis=0, keepdims=True)
+
+
+def weigh(scores, top, keep):
+    total = None
+    for at in range(0, scores.shape[0], TILE):
+        part = slice(at, at + TILE)
+        e = jnp.exp2(scores[part, :] * exp2_scale - top)
+        keep[part, :] = e.astype(BF16)
+        e = fold(e, jnp.add)
+        total = e if total is None else total + e
+    return jnp.sum(total, axis=0, keepdims=True)
+
+
+def tile_causal(group):
+    row_of = lax.broadcasted_iota(jnp.int32, (TILE, TILE), 0)
+    col_of = lax.broadcasted_iota(jnp.int32, (TILE, TILE), 1)
+    return jnp.concatenate([row_of <= col_of] * group, axis=1)
+
+
+def own_body(size, core, masks, tok, group, *refs):
+    take = taker(refs)
+    (seg_k, seg_q), qg_pieces, (kv,) = take(2), take(len(masks)), take(1)
+    e_own, out_part, stats = take(3)
+    qg, ka, vt, s_scr = take(4)
+    wide, tiles = group * TILE, tok // TILE
+    place_rows(size, core, masks, qg_pieces, qg)
+    ka[:, :HEAD_DIM] = kv[:, :HEAD_DIM]
+    ka[:, HEAD_DIM:] = seg_k[WINDOW:, :]
+    vt[...] = kv[:, HEAD_DIM:].T
+    causal = tile_causal(group)
+
+    def scores(tile):
+        queries = query_columns(qg, seg_q, tile * TILE, group)
+        s_scr[tile % 2, : (tile + 1) * TILE, :] = dot_t(ka[: (tile + 1) * TILE, :], queries)
+
+    scores(0)
+    for tile in range(tiles):
+        base, turn = tile * TILE, tile % 2
+        count = base + TILE
+        s_scr[turn, base:count, :] = jnp.where(causal, s_scr[turn, base:count, :], FAR)
+        rows = s_scr.at[turn, :count, :]
+        top = fold_rows(rows, jnp.maximum) * exp2_scale
+        if tile + 1 < tiles:
+            scores(tile + 1)
+        mine = e_own.at[own_rows(tile), :]
+        stats[tile : tile + 1, :] = top
+        stats[tiles + tile : tiles + tile + 1, :] = weigh(rows, top, mine)
+        out_part[:, tile * wide : (tile + 1) * wide] = dot(vt[:, :count], mine[...])
+
+
 def forward_body(size, core, masks, reach, tok, group, *refs):
     take = taker(refs)
-    (seg_k, seg_q), qg_pieces, kvs = take(2), take(len(masks)), take(1 + reach)
-    out_pieces, sent, (e_own, g_own, dq_part) = take(len(masks)), take(reach), take(3)
+    (seg_k, seg_q), qg_pieces, kvs = take(2), take(len(masks)), take(reach)
+    out_own, stats = take(2)
+    out_pieces, sent, (g_own, dq_part) = take(len(masks)), take(reach), take(2)
     qg, outs, ka, va, kt, vt, dk, dv, s_scr, e_scr, ds_scr = take(11)
-    width = group * HEAD_DIM
-    span, wide = WINDOW + TILE, group * TILE
+    width, wide, tiles = group * HEAD_DIM, group * TILE, tok // TILE
     place_rows(size, core, masks, qg_pieces, qg)
-    ka[:, HEAD_DIM:] = seg_k[...]
-    for lag in range(reach + 1):
+    ka[:, HEAD_DIM:] = seg_k[:WINDOW, :]
+    for lag in range(1, reach + 1):
         there = slice((reach - lag) * tok, (reach - lag + 1) * tok)
-        kv = kvs[lag][...]
+        kv = kvs[lag - 1][...]
         ka[there, :HEAD_DIM] = kv[:, :HEAD_DIM]
+        kt[:, there] = kv[:, :HEAD_DIM].T
         vt[:, there] = kv[:, HEAD_DIM:].T
-        if lag:
-            kt[:, there] = kv[:, :HEAD_DIM].T
-            set_values(va.at[there, :], kv[:, HEAD_DIM:])
+        set_values(va.at[there, :], kv[:, HEAD_DIM:])
     wide_lane = lax.broadcasted_iota(jnp.int32, (wide, HEAD_DIM), 1)
-    row_of = lax.broadcasted_iota(jnp.int32, (TILE, TILE), 0)
-    col_of = lax.broadcasted_iota(jnp.int32, (TILE, TILE), 1)
-    causal = jnp.concatenate([row_of <= col_of] * group, axis=1)
+    beyond = ~tile_causal(group)
 
     def scores(tile):
         base = tile * TILE
-        mine = jnp.concatenate([seg_q[base : base + TILE, :]] * group, axis=0)
-        queries = jnp.concatenate([stacked(qg, base, group), mine], axis=1)
-        s_scr[tile % 2] = dot_t(ka[base : base + span, :], queries)
-
-    tiles = tok // TILE
+        queries = query_columns(qg, seg_q, base, group)
+        s_scr[tile % 2, : WINDOW - base, :] = dot_t(ka[base:, :], queries)
+
+    def with_delta(g2, out):
+        delta = jnp.sum(g2.astype(F32) * out.astype(F32), axis=1, keepdims=True)
+        high = delta.astype(BF16).astype(F32)
+        extra = jnp.where(wide_lane == 0, -high, jnp.where(wide_lane == 1, high - delta, 0.0))
+        return jnp.concatenate([g2, extra.astype(BF16)], axis=1)
+
     scores(0)
     for tile in range(tiles):
         base, turn = tile * TILE, tile % 2
         early = WINDOW - base
-        for at, keep in ((0, ~causal), (WINDOW, causal)):
-            part = slice(at, at + TILE)
-            s_scr[turn, part, :] = jnp.where(keep, s_scr[turn, part, :], FAR)
-        top = None
-        for at in range(0, span, TILE):
-            part = fold(s_scr[turn, at : at + TILE, :], jnp.maximum)
-            top = part if top is None else jnp.maximum(top, part)
-        top = jnp.max(top, axis=0, keepdims=True) * exp2_scale
+        columns = slice(tile * wide, (tile + 1) * wide)
+        s_scr[turn, :TILE, :] = jnp.where(beyond, s_scr[turn, :TILE, :], FAR)
+        rows = s_scr.at[turn, :early, :]
+        top_own = stats[tile : tile + 1, :]
+        top = jnp.maximum(fold_rows(rows, jnp.maximum) * exp2_scale, top_own)
         if tile + 1 < tiles:
             scores(tile + 1)
-        e_mine = e_own.at[own_rows(tile), :]
-        total = None
-        for at in range(0, span, TILE):
-            e = jnp.exp2(s_scr[turn, at : at + TILE, :] * exp2_scale - top)
-            if at < early:
-                e_scr[turn, at : at + TILE, :] = e.astype(BF16)
-            else:
-                e_mine[at - early : at - early + TILE, :] = e.astype(BF16)
-            part = fold(e, jnp.add)
-            total = part if total is None else total + part
-        inv = 1.0 / jnp.sum(total, axis=0, keepdims=True)
-        inv = jnp.broadcast_to(inv, (HEAD_DIM, wide)).T
-        e_early = e_scr[turn, :early, :]
-        out = dot(vt[:, base:WINDOW], e_early)
-        out = out + dot(vt[:, WINDOW : base + span], e_mine[...])
-        out = (out.T * inv).astype(BF16)
+        mine = e_scr.at[turn, :early, :]
+        total = weigh(rows, top, mine)
+        scale = jnp.exp2(top_own - top)
+        inv = 1.0 / (total + stats[tiles + tile : tiles + tile + 1, :] * scale)
+        e = mine[...]
+        out = dot(vt[:, base:], e) + out_own[:, columns] * scale
+        out = (out * inv).T.astype(BF16)
         unstacked(outs, base, group, out)
-        g2 = (stacked(qg, base, group, width).astype(F32) * inv).astype(BF16)
-        delta = jnp.sum(g2.astype(F32) * out.astype(F32), axis=1, keepdims=True)
-        high = delta.astype(BF16).astype(F32)
-        extra = jnp.where(wide_lane == 0, -high, jnp.where(wide_lane == 1, high - delta, 0.0))
-        g_wide = jnp.concatenate([g2, extra.astype(BF16)], axis=1)
-        g_own[tile * wide : (tile + 1) * wide, :] = g_wide
-        dp = dot_t(va[base:WINDOW, :], g_wide)
+        g2 = stacked(qg, base, group, width).astype(F32)
+        g_mine = (g2 * jnp.broadcast_to(inv * scale, (HEAD_DIM, wide)).T).astype(BF16)
+        g_own[columns, :] = with_delta(g_mine, out)
+        g2 = (g2 * jnp.broadcast_to(inv, (HEAD_DIM, wide)).T).astype(BF16)
+        dp = dot_t(va[base:, :], with_delta(g2, out))
         old = early if tile else 0
-        add_rows(dv, base, old, dot(e_early, g2))
-        score_gradients(ds_scr.at[turn, :early, :], e_early, dp)
+        add_rows(dv, base, old, dot(e, g2))
+        score_gradients(ds_scr.at[turn, :early, :], e, dp)
         ds = ds_scr[turn, :early, :]
         add_rows(dk, base, old, dot(ds, stacked(qg, base, group)))
-        dq_part[:, tile * wide : (tile + 1) * wide] = dot(kt[:, base:WINDOW], ds)
+        dq_part[:, columns] = dot(kt[:, base:], ds)
 
     for lag in range(1, reach + 1):
         there = slice((reach - lag) * tok, (reach - lag + 1) * tok)
@@ -389,28 +436,53 @@
     )(*args)
 
 
-def forward(documents, qg, kv, lags, size):
+def forward_own(documents, qg, kv, size):
+    rows, cols = qg[0].shape
+    tok = len(qg) * rows
+    group = cols // (2 * HEAD_DIM)
+    wide, tiles = group * TILE, tok // TILE
+    return attend_call(
+        functools.partial(own_body, size, core_mask(), chip_masks(size), tok, group),
+        [
+            jax.ShapeDtypeStruct((own_rows(tiles - 1).stop, wide), BF16),
+            jax.ShapeDtypeStruct((HEAD_DIM, tiles * wide), F32),
+            jax.ShapeDtypeStruct((2 * tiles, wide), F32),
+        ],
+        [
+            pltpu.VMEM((tok, cols), BF16),
+            pltpu.VMEM((tok, 2 * HEAD_DIM), BF16),
+            pltpu.VMEM((HEAD_DIM, tok), BF16),
+            pltpu.VMEM((2, tok, wide), F32),
+        ],
+        16 * tok * group * (WINDOW + TILE) * HEAD_DIM,
+        "forward_own",
+        *documents,
+        *qg,
+        kv,
+    )
+
+
+def forward(documents, qg, lags, carried, size):
     rows, cols = qg[0].shape
     tok, count, reach = len(qg) * rows, len(qg), len(lags)
     group = cols // (2 * HEAD_DIM)
-    span, wide, keys, tiles = WINDOW + TILE, group * TILE, (reach + 1) * tok, tok // TILE
+    wide, tiles = group * TILE, tok // TILE
     half = jax.ShapeDtypeStruct((tok, 2 * HEAD_DIM), BF16)
     out_shape = [jax.ShapeDtypeStruct((rows, cols // 2), BF16)] * count + [half] * reach
     out_shape += [
-        jax.ShapeDtypeStruct((own_rows(tiles - 1).stop, wide), BF16),
         jax.ShapeDtypeStruct((tiles * wide, 2 * HEAD_DIM), BF16),
         jax.ShapeDtypeStruct((HEAD_DIM, tiles * wide), F32),
     ]
     scratch = [
         pltpu.VMEM((tok, cols), BF16),
         pltpu.VMEM((tok, cols // 2), BF16),
-        pltpu.VMEM((keys, 2 * HEAD_DIM), BF16),
+        pltpu.VMEM((WINDOW, 2 * HEAD_DIM), BF16),
         pltpu.VMEM((WINDOW, 2 * HEAD_DIM), BF16),
         pltpu.VMEM((HEAD_DIM, WINDOW), BF16),
-        pltpu.VMEM((HEAD_DIM, keys), BF16),
+        pltpu.VMEM((HEAD_DIM, WINDOW), BF16),
         pltpu.VMEM((WINDOW, HEAD_DIM), F32),
         pltpu.VMEM((WINDOW, HEAD_DIM), F32),
-        pltpu.VMEM((2, span, wide), F32),
+        pltpu.VMEM((2, WINDOW, wide), F32),
         pltpu.VMEM((2, WINDOW, wide), BF16),
         pltpu.VMEM((2, WINDOW, wide), BF16),
     ]
@@ -420,12 +492,12 @@
         ),
         out_shape,
         scratch,
-        8 * tok * group * span * HEAD_DIM,
+        6 * tok * group * (WINDOW + TILE) * HEAD_DIM,
         "forward",
         *documents,
         *qg,
-        kv,
         *lags,
+        *carried,
     )
     return results[:count], results[count : count + reach], results[count + reach :]
 
@@ -484,10 +556,11 @@
     lags = [shifted(kv, lag * size) for lag in range(1, reach + 1)]
     qg = swap_chips(gather_cores((query, grad_out), got[2:], size), size)
 
-    out, sent, carried = forward(documents, qg, kv, lags, size)
+    e_own, *partial = forward_own(documents, qg, kv, size)
+    out, sent, carried = forward(documents, qg, lags, partial, size)
     backs = [shifted(sent[lag - 1], -lag * size) for lag in range(1, reach + 1)]
     out = swap_chips(out, size)
-    grad_q, dkv = backward(qg, kv, carried, size)
+    grad_q, dkv = backward(qg, kv, [e_own, *carried], size)
     both = after(*out, *grad_q)
     out, grad_q = both[: len(out)], both[len(out) :]
     grad_q = swap_chips(grad_q, size)

time: 68.6 us -> 65 us (0.948)
  waiting for transfers between devices: 23 us -> 17.8 us
  Pallas kernels: 13.8 us -> 15.1 us
    ppermute x20, waiting for transfers between devices: 23 us -> 16.8 us  [swap(): lax.ppermute(value, BOTH, [(i, i ^ mask) for i in range(device_count())])]
    pallas_call x2 -> x3, Pallas kernels: 11.9 us -> 13.2 us  [attend_call(): pl.pallas_call(kernel, out_shape=out_shape, in_specs=[VMEM] * len(args),...]
    ppermute x2, waiting for transfers between devices: 0.01 us -> 0.99 us  [shifted(): return lax.ppermute(value, BOTH, pairs)]
  transfers between devices with their start and end apart: 22 -> 22, of which waited for: 10 -> 9; matrix products, arithmetic and copies ran while one was open for 6% -> 6% of each run, Pallas kernels for 5% -> 9%
where the time goes in v11:
time: 65 us; the launch traced here: 64.7 us
  starting transfers between devices  26.6 us (41%)
  waiting for transfers between devices  17.8 us (27%)
  Pallas kernels  15.1 us (23%)
  local copies, waits for them, and re-layouts  3.39 us (5%)
  between operations  1.04 us (2%)
  other arithmetic  0.74 us (1%)
    ppermute x20, starting transfers between devices, swap(): lax.ppermute(value, BOTH, [(i, i ^ mask) for i in range(device_count())])  21.6 us
    ppermute x20, waiting for transfers between devices, swap(): lax.ppermute(value, BOTH, [(i, i ^ mask) for i in range(device_count())])  16.8 us
    pallas_call x3, Pallas kernels, attend_call(): pl.pallas_call(kernel, out_shape=out_shape, in_specs=[VMEM] * len(args),...  13.2 us
    ppermute x2, starting transfers between devices, shifted(): return lax.ppermute(value, BOTH, pairs)  5 us
    slice x4, local copies, waits for them, and re-layouts, this_core(): shares = [array[:, r * width:(r + 1) * width] for r in range(size)]  1.99 us
    pallas_call x1, Pallas kernels, spread_cores(): pl.pallas_call(functools.partial(spread_body, size, core_mask(), chip_mas...  1.39 us
  transfers between devices with their start and end apart: 22, of which 9 were waited for; matrix products, arithmetic and copies ran while one was open for 6% of the time, Pallas kernels for 9%

profile of v11, /device:TPU:0, one launch (start us, length us, event | category | flops | bytes accessed | tf_op | source)
XLA Modules:
  0.0 64.7 jit_solution(7771748620854876889)
XLA Ops:
  1.7 1.0 %fusion.3 = (bf16[128,256]{1,0:T(8,128)(2,1)S(1)}, bf16[128,256]{1,0:T(8,128)(2,1)S(1)}, bf16[128,256]{1,0:T(8,128)(2,1)S(1)}, bf16[128,256]{1,0:T(8,128)(2,1)S(1)}) fusion(bf16[128,1024]{1,0:T(8,128)(2,1)} %param.6), kind=kLoop, calls=%fused_computation.12 | loop fusion | bytes 524288 | tf_op jit(solution)/shard_map/slice | solution.py:94
  2.7 1.0 %fusion.2 = (bf16[128,256]{1,0:T(8,128)(2,1)S(1)}, bf16[128,256]{1,0:T(8,128)(2,1)S(1)}, bf16[128,256]{1,0:T(8,128)(2,1)S(1)}, bf16[128,256]{1,0:T(8,128)(2,1)S(1)}) fusion(bf16[128,1024]{1,0:T(8,128)(2,1)} %param.7), kind=kLoop, calls=%fused_computation.11 | loop fusion | bytes 524288 | tf_op jit(solution)/shard_map/slice | solution.py:94
  3.7 0.7 %pad_dynamic-slice_fusion = s32[2048]{0:T(1024)S(1)} fusion(s32[]{:T(128)S(6)} %select_n.62, s32[4096]{0:T(1024)} %param.9), kind=kLoop, calls=%fused_computation.8 | loop fusion | bytes 24580 | tf_op jit(solution)/shard_map/dynamic_slice | solution.py:535
  4.6 3.0 %collective-permute-start.7 = (bf16[256,256]{1,0:T(8,128)(2,1)S(1)}, bf16[256,256]{1,0:T(8,128)(2,1)S(1)}, u32[]{:S(2)}, u32[]{:S(2)}) collective-permute-start(bf16[256,256]{1,0:T(8,128)(2,1)S(1)} %get-tuple-element.50), channel_id=1, source_target_pairs={{0,1},{1,0},{2,3},{3,2},{4,5},{5,4},{6,7},{7,6},{8,9},{9,8},{10,11... | collective-permute-start | bytes 393224 | tf_op jit(solution)/shard_map/ppermute | solution.py:35
  7.6 1.5 %collective-permute-start.8 = (bf16[256,256]{1,0:T(8,128)(2,1)S(1)}, bf16[256,256]{1,0:T(8,128)(2,1)S(1)}, u32[]{:S(2)}, u32[]{:S(2)}) collective-permute-start(bf16[256,256]{1,0:T(8,128)(2,1)S(1)} %get-tuple-element.51), channel_id=1, source_target_pairs={{0,4},{1,5},{2,6},{3,7},{4,0},{5,1},{6,2},{7,3},{8,12},{9,13},{10,... | collective-permute-start | bytes 393224 | tf_op jit(solution)/shard_map/ppermute | solution.py:35
  9.6 2.0 %collective-permute-start.4 = (bf16[256,512]{1,0:T(8,128)(2,1)S(1)}, bf16[256,512]{1,0:T(8,128)(2,1)S(1)}, u32[]{:S(2)}, u32[]{:S(2)}) collective-permute-start(bf16[256,512]{1,0:T(8,128)(2,1)S(1)} %get-tuple-element.46), channel_id=1, source_target_pairs={{0,1},{1,0},{2,3},{3,2},{4,5},{5,4},{6,7},{7,6},{8,9},{9,8},{10,11... | collective-permute-start | bytes 786440 | tf_op jit(solution)/shard_map/ppermute | solution.py:35
  11.6 1.5 %collective-permute-start.5 = (bf16[256,512]{1,0:T(8,128)(2,1)S(1)}, bf16[256,512]{1,0:T(8,128)(2,1)S(1)}, u32[]{:S(2)}, u32[]{:S(2)}) collective-permute-start(bf16[256,512]{1,0:T(8,128)(2,1)S(1)} %get-tuple-element.47), channel_id=1, source_target_pairs={{0,4},{1,5},{2,6},{3,7},{4,0},{5,1},{6,2},{7,3},{8,12},{9,13},{10,... | collective-permute-start | bytes 786440 | tf_op jit(solution)/shard_map/ppermute | solution.py:35
  13.1 1.8 %collective-permute-start.6 = (bf16[256,512]{1,0:T(8,128)(2,1)S(1)}, bf16[256,512]{1,0:T(8,128)(2,1)S(1)}, u32[]{:S(2)}, u32[]{:S(2)}) collective-permute-start(bf16[256,512]{1,0:T(8,128)(2,1)S(1)} %get-tuple-element.48), channel_id=1, source_target_pairs={{0,5},{1,4},{2,7},{3,6},{4,1},{5,0},{6,3},{7,2},{8,13},{9,12},{10,... | collective-permute-start | bytes 786440 | tf_op jit(solution)/shard_map/ppermute | solution.py:35
  15.3 0.7 %dynamic_slice.7 = s32[1024]{0:T(1024)S(1)} dynamic-slice(s32[4096]{0:T(1024)} %param.9, s32[]{:T(128)S(6)} %select_n.64), dynamic_slice_sizes={1024} | dynamic-slice | bytes 8196 | tf_op jit(solution)/shard_map/dynamic_slice | solution.py:536
  16.0 0.5 collective-permute-done.9.refs_3_
  16.6 3.5 %collective-permute-start.10 = (bf16[1024,256]{1,0:T(8,128)(2,1)S(1)}, bf16[1024,256]{1,0:T(8,128)(2,1)S(1)}, u32[]{:S(2)}, u32[]{:S(2)}) collective-permute-start(bf16[1024,256]{1,0:T(8,128)(2,1)S(1)} %join.1.refs_6_.refs_4_), channel_id=1, source_target_pairs={{0,8},{1,9},{2,10},{3,11},{4,12},{5,13},{6,14},{7,15},{8,16},{9,17... | collective-permute-start | bytes 1572872 | tf_op jit(solution)/shard_map/ppermute | solution.py:55
  20.3 0.8 %collective-permute-done.4.refs_3_.refs_1_ = bf16[256,512]{1,0:T(8,128)(2,1)S(1)} collective-permute-done((bf16[256,512]{1,0:T(8,128)(2,1)S(1)}, bf16[256,512]{1,0:T(8,128)(2,1)S(1)}, u32[]{:S(2)}, u32[]{:S(2)}) %collective-permute-start.4) | collective-permute-done | bytes 262176 | tf_op jit(solution)/shard_map/ppermute | solution.py:35
  21.1 5.7 %collective-permute-done.5.refs_4_.refs_2_ = bf16[256,512]{1,0:T(8,128)(2,1)S(1)} collective-permute-done((bf16[256,512]{1,0:T(8,128)(2,1)S(1)}, bf16[256,512]{1,0:T(8,128)(2,1)S(1)}, u32[]{:S(2)}, u32[]{:S(2)}) %collective-permute-start.5) | collective-permute-done | bytes 262176 | tf_op jit(solution)/shard_map/ppermute | solution.py:35
  26.9 2.6 %forward_own.1 = (bf16[4608,256]{1,0:T(8,128)(2,1)S(1)}, f32[128,2048]{1,0:T(8,128)S(1)}, f32[16,256]{1,0:T(8,128)S(1)}) custom-call(bf16[2048,128]{1,0:T(8,128)(2,1)S(1)} %select_convert_fusion.refs_0_, bf16[1024,128]{1,0:T(8,128)(2,1)S(1)} %select_convert_fusion.1.refs_1_, bf16[256,512]{1,0:T(8,128)(2,1)S(1)} %get-tuple-element.45.refs_2_.refs_0_, ...), custom_call_target="tpu_custom_call" | custom-call | flops 4831838208 | bytes 8388608 | tf_op jit(solution)/shard_map/forward_own/pallas_call | solution.py:425
  29.5 7.5 %forward.1 = (bf16[256,256]{1,0:T(8,128)(2,1)S(1)}, bf16[256,256]{1,0:T(8,128)(2,1)S(1)}, bf16[256,256]{1,0:T(8,128)(2,1)S(1)}, bf16[256,256]{1,0:T(8,128)(2,1)S...) custom-call(bf16[2048,128]{1,0:T(8,128)(2,1)S(1)} %select_convert_fusion.refs_0_, ...), custom_call_target="tpu_custom_call" | custom-call | flops 1811939328 | bytes 8388608 | tf_op jit(solution)/shard_map/forward/pallas_call | solution.py:425
  37.0 1.5 %collective-permute-start.17 = (bf16[1024,256]{1,0:T(8,128)(2,1)S(1)}, bf16[1024,256]{1,0:T(8,128)(2,1)S(1)}, u32[]{:S(2)}, u32[]{:S(2)}) collective-permute-start(bf16[1024,256]{1,0:T(8,128)(2,1)S(1)} %get-tuple-element.75), channel_id=1, source_target_pairs={{8,0},{9,1},{10,2},{11,3},{12,4},{13,5},{14,6},{15,7},{16,8},{17,9... | collective-permute-start | bytes 1572872 | tf_op jit(solution)/shard_map/ppermute | solution.py:55
  38.5 1.6 %collective-permute-start.11 = (bf16[256,256]{1,0:T(8,128)(2,1)S(1)}, bf16[256,256]{1,0:T(8,128)(2,1)S(1)}, u32[]{:S(2)}, u32[]{:S(2)}) collective-permute-start(bf16[256,256]{1,0:T(8,128)(2,1)S(1)} %get-tuple-element.56), channel_id=1, source_target_pairs={{0,1},{1,0},{2,3},{3,2},{4,5},{5,4},{6,7},{7,6},{8,9},{9,8},{10,11... | collective-permute-start | bytes 393224 | tf_op jit(solution)/shard_map/ppermute | solution.py:35
  40.6 1.4 %collective-permute-start.13 = (bf16[256,256]{1,0:T(8,128)(2,1)S(1)}, bf16[256,256]{1,0:T(8,128)(2,1)S(1)}, u32[]{:S(2)}, u32[]{:S(2)}) collective-permute-start(bf16[256,256]{1,0:T(8,128)(2,1)S(1)} %get-tuple-element.58), channel_id=1, source_target_pairs={{0,5},{1,4},{2,7},{3,6},{4,1},{5,0},{6,3},{7,2},{8,13},{9,12},{10,... | collective-permute-start | bytes 393224 | tf_op jit(solution)/shard_map/ppermute | solution.py:35
  42.1 3.0 %backward.1 = (bf16[256,256]{1,0:T(8,128)(2,1)S(1)}, bf16[256,256]{1,0:T(8,128)(2,1)S(1)}, bf16[256,256]{1,0:T(8,128)(2,1)S(1)}, bf16[256,256]{1,0:T(8,128)(2,1)S(1)}, f32[1024,256]{1,0:T(8,128)S(1)}) custom-call(bf16[256,512]{1,0:T(8,128)(2,1)S(1)} %get-tuple-element.45.refs_2_.refs_0_, bf16[256,512]{1,0:T(8,128)(2,1)S(1)} %collective-permute-done.4.refs_3_.refs_1_, ...), custom_call_target="tpu_custom_call" | custom-call | flops 1207959552 | bytes 8388608 | tf_op jit(solution)/shard_map/backward/pallas_call | solution.py:425
  45.1 2.0 %collective-permute-done.12.refs_2_ = bf16[256,256]{1,0:T(8,128)(2,1)S(1)} collective-permute-done((bf16[256,256]{1,0:T(8,128)(2,1)S(1)}, bf16[256,256]{1,0:T(8,128)(2,1)S(1)}, u32[]{:S(2)}, u32[]{:S(2)}) %collective-permute-start.12) | collective-permute-done | bytes 131104 | tf_op jit(solution)/shard_map/ppermute | solution.py:35
  47.1 1.1 %collective-permute-start.14 = (bf16[256,256]{1,0:T(8,128)(2,1)S(1)}, bf16[256,256]{1,0:T(8,128)(2,1)S(1)}, u32[]{:S(2)}, u32[]{:S(2)}) collective-permute-start(bf16[256,256]{1,0:T(8,128)(2,1)S(1)} %get-tuple-element.71), channel_id=1, source_target_pairs={{0,1},{1,0},{2,3},{3,2},{4,5},{5,4},{6,7},{7,6},{8,9},{9,8},{10,11... | collective-permute-start | bytes 393224 | tf_op jit(solution)/shard_map/ppermute | solution.py:35
  48.2 0.8 %collective-permute-start.15 = (bf16[256,256]{1,0:T(8,128)(2,1)S(1)}, bf16[256,256]{1,0:T(8,128)(2,1)S(1)}, u32[]{:S(2)}, u32[]{:S(2)}) collective-permute-start(bf16[256,256]{1,0:T(8,128)(2,1)S(1)} %get-tuple-element.72), channel_id=1, source_target_pairs={{0,4},{1,5},{2,6},{3,7},{4,0},{5,1},{6,2},{7,3},{8,12},{9,13},{10,... | collective-permute-start | bytes 393224 | tf_op jit(solution)/shard_map/ppermute | solution.py:35
  49.0 1.6 %collective-permute-start.16 = (bf16[256,256]{1,0:T(8,128)(2,1)S(1)}, bf16[256,256]{1,0:T(8,128)(2,1)S(1)}, u32[]{:S(2)}, u32[]{:S(2)}) collective-permute-start(bf16[256,256]{1,0:T(8,128)(2,1)S(1)} %get-tuple-element.73), channel_id=1, source_target_pairs={{0,5},{1,4},{2,7},{3,6},{4,1},{5,0},{6,3},{7,2},{8,13},{9,12},{10,... | collective-permute-start | bytes 393224 | tf_op jit(solution)/shard_map/ppermute | solution.py:35
  50.6 1.0 %collective-permute-done.17.refs_1_ = bf16[1024,256]{1,0:T(8,128)(2,1)S(1)} collective-permute-done((bf16[1024,256]{1,0:T(8,128)(2,1)S(1)}, bf16[1024,256]{1,0:T(8,128)(2,1)S(1)}, u32[]{:S(2)}, u32[]{:S(2)}) %collective-permute-start.17) | collective-permute-done | bytes 524320 | tf_op jit(solution)/shard_map/ppermute | solution.py:55
  51.7 1.7 %collective-permute-start.18 = (bf16[256,256]{1,0:T(8,128)(2,1)S(1)}, bf16[256,256]{1,0:T(8,128)(2,1)S(1)}, u32[]{:S(2)}, u32[]{:S(2)}) collective-permute-start(bf16[256,256]{1,0:T(8,128)(2,1)S(1)} %get-tuple-element.77), channel_id=1, source_target_pairs={{0,1},{1,0},{2,3},{3,2},{4,5},{5,4},{6,7},{7,6},{8,9},{9,8},{10,11... | collective-permute-start | bytes 393224 | tf_op jit(solution)/shard_map/ppermute | solution.py:35
  53.4 0.6 collective-permute-start.19
  54.0 1.3 %collective-permute-start.20 = (bf16[256,256]{1,0:T(8,128)(2,1)S(1)}, bf16[256,256]{1,0:T(8,128)(2,1)S(1)}, u32[]{:S(2)}, u32[]{:S(2)}) collective-permute-start(bf16[256,256]{1,0:T(8,128)(2,1)S(1)} %get-tuple-element.79), channel_id=1, source_target_pairs={{0,5},{1,4},{2,7},{3,6},{4,1},{5,0},{6,3},{7,2},{8,13},{9,12},{10,... | collective-permute-start | bytes 393224 | tf_op jit(solution)/shard_map/ppermute | solution.py:35
  55.3 1.0 %collective-permute-done.16.refs_7_ = bf16[256,256]{1,0:T(8,128)(2,1)S(1)} collective-permute-done((bf16[256,256]{1,0:T(8,128)(2,1)S(1)}, bf16[256,256]{1,0:T(8,128)(2,1)S(1)}, u32[]{:S(2)}, u32[]{:S(2)}) %collective-permute-start.16) | collective-permute-done | bytes 131104 | tf_op jit(solution)/shard_map/ppermute | solution.py:35
  56.3 2.0 %collective-permute-done.18.refs_9_ = bf16[256,256]{1,0:T(8,128)(2,1)S(1)} collective-permute-done((bf16[256,256]{1,0:T(8,128)(2,1)S(1)}, bf16[256,256]{1,0:T(8,128)(2,1)S(1)}, u32[]{:S(2)}, u32[]{:S(2)}) %collective-permute-start.18) | collective-permute-done | bytes 131104 | tf_op jit(solution)/shard_map/ppermute | solution.py:35
  58.3 2.4 %collective-permute-done.19.refs_10_ = bf16[256,256]{1,0:T(8,128)(2,1)S(1)} collective-permute-done((bf16[256,256]{1,0:T(8,128)(2,1)S(1)}, bf16[256,256]{1,0:T(8,128)(2,1)S(1)}, u32[]{:S(2)}, u32[]{:S(2)}) %collective-permute-start.19) | collective-permute-done | bytes 131104 | tf_op jit(solution)/shard_map/ppermute | solution.py:35
  60.9 2.3 %collective-permute-done.21.refs_12_ = bf16[128,3072]{1,0:T(8,128)(2,1)S(1)} collective-permute-done((bf16[128,3072]{1,0:T(8,128)(2,1)S(1)}, bf16[128,3072]{1,0:T(8,128)(2,1)S(1)}, u32[]{:S(2)}, u32[]{:S(2)}) %collective-permute-start.21) | collective-permute-done | bytes 786464 | tf_op jit(solution)/shard_map/ppermute | solution.py:35
  63.1 1.4 %spread.1 = (bf16[128,2048]{1,0:T(8,128)(2,1)}, bf16[128,2048]{1,0:T(8,128)(2,1)}, bf16[128,1024]{1,0:T(8,128)(2,1)}, bf16[128,1024]{1,0:T(8,128)(2,1)}) custom-call(bf16[256,256]{1,0:T(8,128)(2,1)S(1)} %get-tuple-element.66.refs_0_, bf16[256,256]{1,0:T(8,128)(2,1)S(1)} %collective-permute-done.11.refs_1_, ...), custom_call_target="tpu_custom_call" | custom-call | tf_op jit(solution)/shard_map/spread/pallas_call | solution.py:201
  (36 shorter events, 3.1 us)
Async XLA Ops:
  0.6 8.5 %copy-start = (bf16[128,2048]{1,0:T(8,128)(2,1)S(1)}, bf16[128,2048]{1,0:T(8,128)(2,1)}, u32[]{:S(2)}) copy-start(bf16[128,2048]{1,0:T(8,128)(2,1)} %param.5) | copy-start | bytes 1572868
  0.6 3.8 %collective-permute-start = (bf16[128,1024]{1,0:T(8,128)(2,1)}, bf16[128,1024]{1,0:T(8,128)(2,1)S(1)}, u32[]{:S(2)}, u32[]{:S(2)}) collective-permute-start(bf16[128,1024]{1,0:T(8,128)(2,1)} %param.6), channel_id=1, source_target_pairs={{0,2},{1,3},{2,0},{3,1},{4,6},{5,7},{6,4},{7,5},{8,10},{9,11},{10,... | collective-permute-start | bytes 786440 | tf_op jit(solution)/shard_map/ppermute | solution.py:35
  1.2 3.3 %collective-permute-start.1 = (bf16[128,1024]{1,0:T(8,128)(2,1)}, bf16[128,1024]{1,0:T(8,128)(2,1)S(1)}, u32[]{:S(2)}, u32[]{:S(2)}) collective-permute-start(bf16[128,1024]{1,0:T(8,128)(2,1)} %param.7), channel_id=1, source_target_pairs={{0,2},{1,3},{2,0},{3,1},{4,6},{5,7},{6,4},{7,5},{8,10},{9,11},{10,... | collective-permute-start | bytes 786440 | tf_op jit(solution)/shard_map/ppermute | solution.py:35
  1.2 8.2 %collective-permute-start.2 = (bf16[128,2048]{1,0:T(8,128)(2,1)}, bf16[128,2048]{1,0:T(8,128)(2,1)S(1)}, u32[]{:S(2)}, u32[]{:S(2)}) collective-permute-start(bf16[128,2048]{1,0:T(8,128)(2,1)} %param.5), channel_id=1, source_target_pairs={{0,2},{1,3},{2,0},{3,1},{4,6},{5,7},{6,4},{7,5},{8,10},{9,11},{10,... | collective-permute-start | bytes 1572872 | tf_op jit(solution)/shard_map/ppermute | solution.py:35
  1.7 7.8 %collective-permute-start.3 = (bf16[128,2048]{1,0:T(8,128)(2,1)}, bf16[128,2048]{1,0:T(8,128)(2,1)S(1)}, u32[]{:S(2)}, u32[]{:S(2)}) collective-permute-start(bf16[128,2048]{1,0:T(8,128)(2,1)} %param.8), channel_id=1, source_target_pairs={{0,2},{1,3},{2,0},{3,1},{4,6},{5,7},{6,4},{7,5},{8,10},{9,11},{10,... | collective-permute-start | bytes 1572872 | tf_op jit(solution)/shard_map/ppermute | solution.py:35
  4.4 4.8 %copy-start.1 = (bf16[128,2048]{1,0:T(8,128)(2,1)S(1)}, bf16[128,2048]{1,0:T(8,128)(2,1)}, u32[]{:S(2)}) copy-start(bf16[128,2048]{1,0:T(8,128)(2,1)} %param.8) | copy-start | bytes 1572868
  4.6 8.5 %collective-permute-start.7 = (bf16[256,256]{1,0:T(8,128)(2,1)S(1)}, bf16[256,256]{1,0:T(8,128)(2,1)S(1)}, u32[]{:S(2)}, u32[]{:S(2)}) collective-permute-start(bf16[256,256]{1,0:T(8,128)(2,1)S(1)} %get-tuple-element.50), channel_id=1, source_target_pairs={{0,1},{1,0},{2,3},{3,2},{4,5},{5,4},{6,7},{7,6},{8,9},{9,8},{10,11... | collective-permute-start | bytes 393224 | tf_op jit(solution)/shard_map/ppermute | solution.py:35
  7.6 8.4 %collective-permute-start.8 = (bf16[256,256]{1,0:T(8,128)(2,1)S(1)}, bf16[256,256]{1,0:T(8,128)(2,1)S(1)}, u32[]{:S(2)}, u32[]{:S(2)}) collective-permute-start(bf16[256,256]{1,0:T(8,128)(2,1)S(1)} %get-tuple-element.51), channel_id=1, source_target_pairs={{0,4},{1,5},{2,6},{3,7},{4,0},{5,1},{6,2},{7,3},{8,12},{9,13},{10,... | collective-permute-start | bytes 393224 | tf_op jit(solution)/shard_map/ppermute | solution.py:35
  9.1 7.4 %collective-permute-start.9 = (bf16[256,256]{1,0:T(8,128)(2,1)S(1)}, bf16[256,256]{1,0:T(8,128)(2,1)S(1)}, u32[]{:S(2)}, u32[]{:S(2)}) collective-permute-start(bf16[256,256]{1,0:T(8,128)(2,1)S(1)} %get-tuple-element.52), channel_id=1, source_target_pairs={{0,5},{1,4},{2,7},{3,6},{4,1},{5,0},{6,3},{7,2},{8,13},{9,12},{10,... | collective-permute-start | bytes 393224 | tf_op jit(solution)/shard_map/ppermute | solution.py:35
  9.6 11.5 %collective-permute-start.4 = (bf16[256,512]{1,0:T(8,128)(2,1)S(1)}, bf16[256,512]{1,0:T(8,128)(2,1)S(1)}, u32[]{:S(2)}, u32[]{:S(2)}) collective-permute-start(bf16[256,512]{1,0:T(8,128)(2,1)S(1)} %get-tuple-element.46), channel_id=1, source_target_pairs={{0,1},{1,0},{2,3},{3,2},{4,5},{5,4},{6,7},{7,6},{8,9},{9,8},{10,11... | collective-permute-start | bytes 786440 | tf_op jit(solution)/shard_map/ppermute | solution.py:35
  11.6 15.2 %collective-permute-start.5 = (bf16[256,512]{1,0:T(8,128)(2,1)S(1)}, bf16[256,512]{1,0:T(8,128)(2,1)S(1)}, u32[]{:S(2)}, u32[]{:S(2)}) collective-permute-start(bf16[256,512]{1,0:T(8,128)(2,1)S(1)} %get-tuple-element.47), channel_id=1, source_target_pairs={{0,4},{1,5},{2,6},{3,7},{4,0},{5,1},{6,2},{7,3},{8,12},{9,13},{10,... | collective-permute-start | bytes 786440 | tf_op jit(solution)/shard_map/ppermute | solution.py:35
  13.1 13.7 %collective-permute-start.6 = (bf16[256,512]{1,0:T(8,128)(2,1)S(1)}, bf16[256,512]{1,0:T(8,128)(2,1)S(1)}, u32[]{:S(2)}, u32[]{:S(2)}) collective-permute-start(bf16[256,512]{1,0:T(8,128)(2,1)S(1)} %get-tuple-element.48), channel_id=1, source_target_pairs={{0,5},{1,4},{2,7},{3,6},{4,1},{5,0},{6,3},{7,2},{8,13},{9,12},{10,... | collective-permute-start | bytes 786440 | tf_op jit(solution)/shard_map/ppermute | solution.py:35
  16.6 12.9 %collective-permute-start.10 = (bf16[1024,256]{1,0:T(8,128)(2,1)S(1)}, bf16[1024,256]{1,0:T(8,128)(2,1)S(1)}, u32[]{:S(2)}, u32[]{:S(2)}) collective-permute-start(bf16[1024,256]{1,0:T(8,128)(2,1)S(1)} %join.1.refs_6_.refs_4_), channel_id=1, source_target_pairs={{0,8},{1,9},{2,10},{3,11},{4,12},{5,13},{6,14},{7,15},{8,16},{9,17... | collective-permute-start | bytes 1572872 | tf_op jit(solution)/shard_map/ppermute | solution.py:55
  37.0 14.6 %collective-permute-start.17 = (bf16[1024,256]{1,0:T(8,128)(2,1)S(1)}, bf16[1024,256]{1,0:T(8,128)(2,1)S(1)}, u32[]{:S(2)}, u32[]{:S(2)}) collective-permute-start(bf16[1024,256]{1,0:T(8,128)(2,1)S(1)} %get-tuple-element.75), channel_id=1, source_target_pairs={{8,0},{9,1},{10,2},{11,3},{12,4},{13,5},{14,6},{15,7},{16,8},{17,9... | collective-permute-start | bytes 1572872 | tf_op jit(solution)/shard_map/ppermute | solution.py:55
  38.5 6.6 %collective-permute-start.11 = (bf16[256,256]{1,0:T(8,128)(2,1)S(1)}, bf16[256,256]{1,0:T(8,128)(2,1)S(1)}, u32[]{:S(2)}, u32[]{:S(2)}) collective-permute-start(bf16[256,256]{1,0:T(8,128)(2,1)S(1)} %get-tuple-element.56), channel_id=1, source_target_pairs={{0,1},{1,0},{2,3},{3,2},{4,5},{5,4},{6,7},{7,6},{8,9},{9,8},{10,11... | collective-permute-start | bytes 393224 | tf_op jit(solution)/shard_map/ppermute | solution.py:35
  40.1 7.0 %collective-permute-start.12 = (bf16[256,256]{1,0:T(8,128)(2,1)S(1)}, bf16[256,256]{1,0:T(8,128)(2,1)S(1)}, u32[]{:S(2)}, u32[]{:S(2)}) collective-permute-start(bf16[256,256]{1,0:T(8,128)(2,1)S(1)} %get-tuple-element.57), channel_id=1, source_target_pairs={{0,4},{1,5},{2,6},{3,7},{4,0},{5,1},{6,2},{7,3},{8,12},{9,13},{10,... | collective-permute-start | bytes 393224 | tf_op jit(solution)/shard_map/ppermute | solution.py:35
  40.6 6.5 %collective-permute-start.13 = (bf16[256,256]{1,0:T(8,128)(2,1)S(1)}, bf16[256,256]{1,0:T(8,128)(2,1)S(1)}, u32[]{:S(2)}, u32[]{:S(2)}) collective-permute-start(bf16[256,256]{1,0:T(8,128)(2,1)S(1)} %get-tuple-element.58), channel_id=1, source_target_pairs={{0,5},{1,4},{2,7},{3,6},{4,1},{5,0},{6,3},{7,2},{8,13},{9,12},{10,... | collective-permute-start | bytes 393224 | tf_op jit(solution)/shard_map/ppermute | solution.py:35
  47.1 6.9 %collective-permute-start.14 = (bf16[256,256]{1,0:T(8,128)(2,1)S(1)}, bf16[256,256]{1,0:T(8,128)(2,1)S(1)}, u32[]{:S(2)}, u32[]{:S(2)}) collective-permute-start(bf16[256,256]{1,0:T(8,128)(2,1)S(1)} %get-tuple-element.71), channel_id=1, source_target_pairs={{0,1},{1,0},{2,3},{3,2},{4,5},{5,4},{6,7},{7,6},{8,9},{9,8},{10,11... | collective-permute-start | bytes 393224 | tf_op jit(solution)/shard_map/ppermute | solution.py:35
  48.2 7.0 %collective-permute-start.15 = (bf16[256,256]{1,0:T(8,128)(2,1)S(1)}, bf16[256,256]{1,0:T(8,128)(2,1)S(1)}, u32[]{:S(2)}, u32[]{:S(2)}) collective-permute-start(bf16[256,256]{1,0:T(8,128)(2,1)S(1)} %get-tuple-element.72), channel_id=1, source_target_pairs={{0,4},{1,5},{2,6},{3,7},{4,0},{5,1},{6,2},{7,3},{8,12},{9,13},{10,... | collective-permute-start | bytes 393224 | tf_op jit(solution)/shard_map/ppermute | solution.py:35
  49.0 7.3 %collective-permute-start.16 = (bf16[256,256]{1,0:T(8,128)(2,1)S(1)}, bf16[256,256]{1,0:T(8,128)(2,1)S(1)}, u32[]{:S(2)}, u32[]{:S(2)}) collective-permute-start(bf16[256,256]{1,0:T(8,128)(2,1)S(1)} %get-tuple-element.73), channel_id=1, source_target_pairs={{0,5},{1,4},{2,7},{3,6},{4,1},{5,0},{6,3},{7,2},{8,13},{9,12},{10,... | collective-permute-start | bytes 393224 | tf_op jit(solution)/shard_map/ppermute | solution.py:35
  51.7 6.6 %collective-permute-start.18 = (bf16[256,256]{1,0:T(8,128)(2,1)S(1)}, bf16[256,256]{1,0:T(8,128)(2,1)S(1)}, u32[]{:S(2)}, u32[]{:S(2)}) collective-permute-start(bf16[256,256]{1,0:T(8,128)(2,1)S(1)} %get-tuple-element.77), channel_id=1, source_target_pairs={{0,1},{1,0},{2,3},{3,2},{4,5},{5,4},{6,7},{7,6},{8,9},{9,8},{10,11... | collective-permute-start | bytes 393224 | tf_op jit(solution)/shard_map/ppermute | solution.py:35
  53.4 7.3 %collective-permute-start.19 = (bf16[256,256]{1,0:T(8,128)(2,1)S(1)}, bf16[256,256]{1,0:T(8,128)(2,1)S(1)}, u32[]{:S(2)}, u32[]{:S(2)}) collective-permute-start(bf16[256,256]{1,0:T(8,128)(2,1)S(1)} %get-tuple-element.78), channel_id=1, source_target_pairs={{0,4},{1,5},{2,6},{3,7},{4,0},{5,1},{6,2},{7,3},{8,12},{9,13},{10,... | collective-permute-start | bytes 393224 | tf_op jit(solution)/shard_map/ppermute | solution.py:35
  54.0 6.7 %collective-permute-start.20 = (bf16[256,256]{1,0:T(8,128)(2,1)S(1)}, bf16[256,256]{1,0:T(8,128)(2,1)S(1)}, u32[]{:S(2)}, u32[]{:S(2)}) collective-permute-start(bf16[256,256]{1,0:T(8,128)(2,1)S(1)} %get-tuple-element.79), channel_id=1, source_target_pairs={{0,5},{1,4},{2,7},{3,6},{4,1},{5,0},{6,3},{7,2},{8,13},{9,12},{10,... | collective-permute-start | bytes 393224 | tf_op jit(solution)/shard_map/ppermute | solution.py:35
  60.8 2.4 %collective-permute-start.21 = (bf16[128,3072]{1,0:T(8,128)(2,1)S(1)}, bf16[128,3072]{1,0:T(8,128)(2,1)S(1)}, u32[]{:S(2)}, u32[]{:S(2)}) collective-permute-start(bf16[128,3072]{1,0:T(8,128)(2,1)S(1)} %bottom.1), channel_id=1, source_target_pairs={{0,2},{1,3},{2,0},{3,1},{4,6},{5,7},{6,4},{7,5},{8,10},{9,11},{10,... | collective-permute-start | bytes 2359304 | tf_op jit(solution)/shard_map/ppermute | solution.py:35

commit v12 on v11

--- a/solution.py
+++ b/solution.py
@@ -262,6 +262,17 @@
         ds_scr[part, :] = (e[part, :].astype(F32) * dp[part]).astype(BF16)
 
 
+def gradient_rows(qg, base, group, scale, out):
+    first = qg.shape[1] // 2
+    columns = jnp.broadcast_to(scale, (HEAD_DIM, scale.shape[1])).T
+    g2 = (stacked(qg, base, group, first).astype(F32) * columns).astype(BF16)
+    delta = jnp.sum(g2.astype(F32) * out.astype(F32), axis=1, keepdims=True)
+    high = delta.astype(BF16).astype(F32)
+    lane = lax.broadcasted_iota(jnp.int32, g2.shape, 1)
+    extra = jnp.where(lane == 0, -high, jnp.where(lane == 1, high - delta, 0.0))
+    return g2, jnp.concatenate([g2, extra.astype(BF16)], axis=1)
+
+
 def own_rows(tile):
     start = tile * (tile + 1) // 2 * TILE
     return slice(start, start + (tile + 1) * TILE)
@@ -331,9 +342,9 @@
     take = taker(refs)
     (seg_k, seg_q), qg_pieces, kvs = take(2), take(len(masks)), take(reach)
     out_own, stats = take(2)
-    out_pieces, sent, (g_own, dq_part) = take(len(masks)), take(reach), take(2)
-    qg, outs, ka, va, kt, vt, dk, dv, s_scr, e_scr, ds_scr = take(11)
-    width, wide, tiles = group * HEAD_DIM, group * TILE, tok // TILE
+    out_pieces, sent, (outs, own_scale, dq_part) = take(len(masks)), take(reach), take(3)
+    qg, ka, va, kt, vt, dk, dv, s_scr, e_scr, ds_scr = take(10)
+    wide, tiles = group * TILE, tok // TILE
     place_rows(size, core, masks, qg_pieces, qg)
     ka[:, HEAD_DIM:] = seg_k[:WINDOW, :]
     for lag in range(1, reach + 1):
@@ -343,19 +354,12 @@
         kt[:, there] = kv[:, :HEAD_DIM].T
         vt[:, there] = kv[:, HEAD_DIM:].T
         set_values(va.at[there, :], kv[:, HEAD_DIM:])
-    wide_lane = lax.broadcasted_iota(jnp.int32, (wide, HEAD_DIM), 1)
     beyond = ~tile_causal(group)
 
     def scores(tile):
         base = tile * TILE
         queries = query_columns(qg, seg_q, base, group)
         s_scr[tile % 2, : WINDOW - base, :] = dot_t(ka[base:, :], queries)
-
-    def with_delta(g2, out):
-        delta = jnp.sum(g2.astype(F32) * out.astype(F32), axis=1, keepdims=True)
-        high = delta.astype(BF16).astype(F32)
-        extra = jnp.where(wide_lane == 0, -high, jnp.where(wide_lane == 1, high - delta, 0.0))
-        return jnp.concatenate([g2, extra.astype(BF16)], axis=1)
 
     scores(0)
     for tile in range(tiles):
@@ -376,11 +380,9 @@
         out = dot(vt[:, base:], e) + out_own[:, columns] * scale
         out = (out * inv).T.astype(BF16)
         unstacked(outs, base, group, out)
-        g2 = stacked(qg, base, group, width).astype(F32)
-        g_mine = (g2 * jnp.broadcast_to(inv * scale, (HEAD_DIM, wide)).T).astype(BF16)
-        g_own[columns, :] = with_delta(g_mine, out)
-        g2 = (g2 * jnp.broadcast_to(inv, (HEAD_DIM, wide)).T).astype(BF16)
-        dp = dot_t(va[base:, :], with_delta(g2, out))
+        own_scale[tile : tile + 1, :] = inv * scale
+        g2, g_wide = gradient_rows(qg, base, group, inv, out)
+        dp = dot_t(va[base:, :], g_wide)
         old = early if tile else 0
         add_rows(dv, base, old, dot(e, g2))
         score_gradients(ds_scr.at[turn, :early, :], e, dp)
@@ -397,7 +399,7 @@
 
 def backward_body(size, core, masks, tok, group, *refs):
     take = taker(refs)
-    qg_pieces, (kv, e_own, g_own, dq_part) = take(len(masks)), take(4)
+    qg_pieces, (kv, e_own, outs, own_scale, dq_part) = take(len(masks)), take(5)
     dq_pieces, (dkv,) = take(len(masks)), take(1)
     qg, dqs, va, kt, dk, dv, ds_scr = take(7)
     wide = group * TILE
@@ -409,8 +411,10 @@
         count = base + TILE
         columns = slice(tile * wide, (tile + 1) * wide)
         e = e_own[own_rows(tile), :]
-        dp = dot_t(va[:count, :], g_own[columns, :])
-        add_rows(dv, 0, base, dot(e, g_own[columns, :HEAD_DIM]))
+        scale = own_scale[tile : tile + 1, :]
+        g2, g_wide = gradient_rows(qg, base, group, scale, stacked(outs, base, group))
+        dp = dot_t(va[:count, :], g_wide)
+        add_rows(dv, 0, base, dot(e, g2))
         score_gradients(ds_scr.at[turn, :count, :], e, dp)
         ds = ds_scr[turn, :count, :]
         add_rows(dk, 0, base, dot(ds, stacked(qg, base, group)))
@@ -470,12 +474,12 @@
     half = jax.ShapeDtypeStruct((tok, 2 * HEAD_DIM), BF16)
     out_shape = [jax.ShapeDtypeStruct((rows, cols // 2), BF16)] * count + [half] * reach
     out_shape += [
-        jax.ShapeDtypeStruct((tiles * wide, 2 * HEAD_DIM), BF16),
+        jax.ShapeDtypeStruct((tok, cols // 2), BF16),
+        jax.ShapeDtypeStruct((tiles, wide), F32),
         jax.ShapeDtypeStruct((HEAD_DIM, tiles * wide), F32),
     ]
     scratch = [
         pltpu.VMEM((tok, cols), BF16),
-        pltpu.VMEM((tok, cols // 2), BF16),
         pltpu.VMEM((WINDOW, 2 * HEAD_DIM), BF16),
         pltpu.VMEM((WINDOW, 2 * HEAD_DIM), BF16),
         pltpu.VMEM((HEAD_DIM, WINDOW), BF16),
@@ -547,11 +551,11 @@
     tok = size * rows
     reach = WINDOW // tok
     assert reach * tok == WINDOW and device_count() % size == 0
-    documents = document_columns(segment_ids, tok, size)
 
     got = [swap(array, core_mask()) for array in (key, value, query, grad_out)]
     pieces = list(gather_cores((key, value), got[:2], size))
-    pieces[0], query, grad_out = after(pieces[0], query, grad_out)
+    pieces[0], query, grad_out, segment_ids = after(pieces[0], query, grad_out, segment_ids)
+    documents = document_columns(segment_ids, tok, size)
     kv = join(swap_chips(pieces, size), size)
     lags = [shifted(kv, lag * size) for lag in range(1, reach + 1)]
     qg = swap_chips(gather_cores((query, grad_out), got[2:], size), size)

time: 65 us -> 64.3 us (0.989)
  local copies, waits for them, and re-layouts: 3.39 us -> 2.03 us
    dynamic_slice x1, local copies, waits for them, and re-layouts: 0.7 us -> 0.01 us  [document_columns(): keys = lax.dynamic_slice_in_dim(padded, start, WINDOW + tok, 0)]
    dynamic_slice x1 -> x2, local copies, waits for them, and re-layouts: 0.69 us -> 0.01 us  [document_columns(): queries = lax.dynamic_slice_in_dim(segment_ids, start, tok, 0)]
  transfers between devices with their start and end apart: 22 -> 22, of which waited for: 9 -> 10; matrix products, arithmetic and copies ran while one was open for 6% -> 4% of each run, Pallas kernels for 9% -> 10%
where the time goes in v12:
time: 64.3 us; the launch traced here: 64.1 us
  starting transfers between devices  26.6 us (41%)
  waiting for transfers between devices  18 us (28%)
  Pallas kernels  15.7 us (24%)
  local copies, waits for them, and re-layouts  2.03 us (3%)
  between operations  1.1 us (2%)
  other arithmetic  0.74 us (1%)
    ppermute x20, starting transfers between devices, swap(): lax.ppermute(value, BOTH, [(i, i ^ mask) for i in range(device_count())])  21.6 us
    ppermute x20, waiting for transfers between devices, swap(): lax.ppermute(value, BOTH, [(i, i ^ mask) for i in range(device_count())])  16.9 us
    pallas_call x3, Pallas kernels, attend_call(): pl.pallas_call(kernel, out_shape=out_shape, in_specs=[VMEM] * len(args),...  13.7 us
    ppermute x2, starting transfers between devices, shifted(): return lax.ppermute(value, BOTH, pairs)  4.99 us
    slice x4, local copies, waits for them, and re-layouts, this_core(): shares = [array[:, r * width:(r + 1) * width] for r in range(size)]  1.99 us
    pallas_call x1, Pallas kernels, spread_cores(): pl.pallas_call(functools.partial(spread_body, size, core_mask(), chip_mas...  1.39 us
  transfers between devices with their start and end apart: 22, of which 10 were waited for; matrix products, arithmetic and copies ran while one was open for 4% of the time, Pallas kernels for 10%

profile of v12, /device:TPU:0, one launch (start us, length us, event | category | flops | bytes accessed | tf_op | source)
XLA Modules:
  0.0 64.1 jit_solution(14646559829582376522)
XLA Ops:
  1.8 1.0 %fusion.3 = (bf16[128,256]{1,0:T(8,128)(2,1)S(1)}, bf16[128,256]{1,0:T(8,128)(2,1)S(1)}, bf16[128,256]{1,0:T(8,128)(2,1)S(1)}, bf16[128,256]{1,0:T(8,128)(2,1)S(1)}) fusion(bf16[128,1024]{1,0:T(8,128)(2,1)} %param.6), kind=kLoop, calls=%fused_computation.12 | loop fusion | bytes 524288 | tf_op jit(solution)/shard_map/slice | solution.py:94
  2.7 1.0 %fusion.2 = (bf16[128,256]{1,0:T(8,128)(2,1)S(1)}, bf16[128,256]{1,0:T(8,128)(2,1)S(1)}, bf16[128,256]{1,0:T(8,128)(2,1)S(1)}, bf16[128,256]{1,0:T(8,128)(2,1)S(1)}) fusion(bf16[128,1024]{1,0:T(8,128)(2,1)} %param.7), kind=kLoop, calls=%fused_computation.11 | loop fusion | bytes 524288 | tf_op jit(solution)/shard_map/slice | solution.py:94
  4.0 3.0 %collective-permute-start.7 = (bf16[256,256]{1,0:T(8,128)(2,1)S(1)}, bf16[256,256]{1,0:T(8,128)(2,1)S(1)}, u32[]{:S(2)}, u32[]{:S(2)}) collective-permute-start(bf16[256,256]{1,0:T(8,128)(2,1)S(1)} %get-tuple-element.53), channel_id=1, source_target_pairs={{0,1},{1,0},{2,3},{3,2},{4,5},{5,4},{6,7},{7,6},{8,9},{9,8},{10,11... | collective-permute-start | bytes 393224 | tf_op jit(solution)/shard_map/ppermute | solution.py:35
  7.0 1.5 %collective-permute-start.8 = (bf16[256,256]{1,0:T(8,128)(2,1)S(1)}, bf16[256,256]{1,0:T(8,128)(2,1)S(1)}, u32[]{:S(2)}, u32[]{:S(2)}) collective-permute-start(bf16[256,256]{1,0:T(8,128)(2,1)S(1)} %get-tuple-element.54), channel_id=1, source_target_pairs={{0,4},{1,5},{2,6},{3,7},{4,0},{5,1},{6,2},{7,3},{8,12},{9,13},{10,... | collective-permute-start | bytes 393224 | tf_op jit(solution)/shard_map/ppermute | solution.py:35
  9.0 2.0 %collective-permute-start.4 = (bf16[256,512]{1,0:T(8,128)(2,1)S(1)}, bf16[256,512]{1,0:T(8,128)(2,1)S(1)}, u32[]{:S(2)}, u32[]{:S(2)}) collective-permute-start(bf16[256,512]{1,0:T(8,128)(2,1)S(1)} %get-tuple-element.49), channel_id=1, source_target_pairs={{0,1},{1,0},{2,3},{3,2},{4,5},{5,4},{6,7},{7,6},{8,9},{9,8},{10,11... | collective-permute-start | bytes 786440 | tf_op jit(solution)/shard_map/ppermute | solution.py:35
  11.0 1.5 %collective-permute-start.5 = (bf16[256,512]{1,0:T(8,128)(2,1)S(1)}, bf16[256,512]{1,0:T(8,128)(2,1)S(1)}, u32[]{:S(2)}, u32[]{:S(2)}) collective-permute-start(bf16[256,512]{1,0:T(8,128)(2,1)S(1)} %get-tuple-element.50), channel_id=1, source_target_pairs={{0,4},{1,5},{2,6},{3,7},{4,0},{5,1},{6,2},{7,3},{8,12},{9,13},{10,... | collective-permute-start | bytes 786440 | tf_op jit(solution)/shard_map/ppermute | solution.py:35
  12.5 1.7 %collective-permute-start.6 = (bf16[256,512]{1,0:T(8,128)(2,1)S(1)}, bf16[256,512]{1,0:T(8,128)(2,1)S(1)}, u32[]{:S(2)}, u32[]{:S(2)}) collective-permute-start(bf16[256,512]{1,0:T(8,128)(2,1)S(1)} %get-tuple-element.51), channel_id=1, source_target_pairs={{0,5},{1,4},{2,7},{3,6},{4,1},{5,0},{6,3},{7,2},{8,13},{9,12},{10,... | collective-permute-start | bytes 786440 | tf_op jit(solution)/shard_map/ppermute | solution.py:35
  14.6 0.6 collective-permute-done.8.refs_2_
  15.2 0.7 %collective-permute-done.9.refs_3_ = bf16[256,256]{1,0:T(8,128)(2,1)S(1)} collective-permute-done((bf16[256,256]{1,0:T(8,128)(2,1)S(1)}, bf16[256,256]{1,0:T(8,128)(2,1)S(1)}, u32[]{:S(2)}, u32[]{:S(2)}) %collective-permute-start.9) | collective-permute-done | bytes 131104 | tf_op jit(solution)/shard_map/ppermute | solution.py:35
  15.9 3.5 %collective-permute-start.10 = (bf16[1024,256]{1,0:T(8,128)(2,1)S(1)}, bf16[1024,256]{1,0:T(8,128)(2,1)S(1)}, u32[]{:S(2)}, u32[]{:S(2)}) collective-permute-start(bf16[1024,256]{1,0:T(8,128)(2,1)S(1)} %join.1.refs_6_.refs_4_), channel_id=1, source_target_pairs={{0,8},{1,9},{2,10},{3,11},{4,12},{5,13},{6,14},{7,15},{8,16},{9,17... | collective-permute-start | bytes 1572872 | tf_op jit(solution)/shard_map/ppermute | solution.py:55
  19.7 0.8 %collective-permute-done.4.refs_3_.refs_1_ = bf16[256,512]{1,0:T(8,128)(2,1)S(1)} collective-permute-done((bf16[256,512]{1,0:T(8,128)(2,1)S(1)}, bf16[256,512]{1,0:T(8,128)(2,1)S(1)}, u32[]{:S(2)}, u32[]{:S(2)}) %collective-permute-start.4) | collective-permute-done | bytes 262176 | tf_op jit(solution)/shard_map/ppermute | solution.py:35
  20.5 5.7 %collective-permute-done.5.refs_4_.refs_2_ = bf16[256,512]{1,0:T(8,128)(2,1)S(1)} collective-permute-done((bf16[256,512]{1,0:T(8,128)(2,1)S(1)}, bf16[256,512]{1,0:T(8,128)(2,1)S(1)}, u32[]{:S(2)}, u32[]{:S(2)}) %collective-permute-start.5) | collective-permute-done | bytes 262176 | tf_op jit(solution)/shard_map/ppermute | solution.py:35
  26.2 2.7 %forward_own.1 = (bf16[4608,256]{1,0:T(8,128)(2,1)S(1)}, f32[128,2048]{1,0:T(8,128)S(1)}, f32[16,256]{1,0:T(8,128)S(1)}) custom-call(bf16[2048,128]{1,0:T(8,128)(2,1)S(1)} %select_convert_fusion.refs_0_, bf16[1024,128]{1,0:T(8,128)(2,1)S(1)} %select_convert_fusion.1.refs_1_, bf16[256,512]{1,0:T(8,128)(2,1)S(1)} %get-tuple-element.48.refs_2_.refs_0_, ...), custom_call_target="tpu_custom_call" | custom-call | flops 4831838208 | bytes 8388608 | tf_op jit(solution)/shard_map/forward_own/pallas_call | solution.py:429
  28.9 7.5 %forward.1 = (bf16[256,256]{1,0:T(8,128)(2,1)S(1)}, bf16[256,256]{1,0:T(8,128)(2,1)S(1)}, bf16[256,256]{1,0:T(8,128)(2,1)S(1)}, bf16[256,256]{1,0:T(8,128)(2,1)S...) custom-call(bf16[2048,128]{1,0:T(8,128)(2,1)S(1)} %select_convert_fu, ...), custom_call_target="tpu_custom_call" | custom-call | flops 1811939328 | bytes 8388608 | tf_op jit(solution)/shard_map/forward/pallas_call | solution.py:429
  36.4 1.5 %collective-permute-start.17 = (bf16[1024,256]{1,0:T(8,128)(2,1)S(1)}, bf16[1024,256]{1,0:T(8,128)(2,1)S(1)}, u32[]{:S(2)}, u32[]{:S(2)}) collective-permute-start(bf16[1024,256]{1,0:T(8,128)(2,1)S(1)} %get-tuple-element.79), channel_id=1, source_target_pairs={{8,0},{9,1},{10,2},{11,3},{12,4},{13,5},{14,6},{15,7},{16,8},{17,9... | collective-permute-start | bytes 1572872 | tf_op jit(solution)/shard_map/ppermute | solution.py:55
  37.9 1.5 %collective-permute-start.11 = (bf16[256,256]{1,0:T(8,128)(2,1)S(1)}, bf16[256,256]{1,0:T(8,128)(2,1)S(1)}, u32[]{:S(2)}, u32[]{:S(2)}) collective-permute-start(bf16[256,256]{1,0:T(8,128)(2,1)S(1)} %get-tuple-element.59), channel_id=1, source_target_pairs={{0,1},{1,0},{2,3},{3,2},{4,5},{5,4},{6,7},{7,6},{8,9},{9,8},{10,11... | collective-permute-start | bytes 393224 | tf_op jit(solution)/shard_map/ppermute | solution.py:35
  39.4 0.6 collective-permute-start.12
  40.0 1.4 %collective-permute-start.13 = (bf16[256,256]{1,0:T(8,128)(2,1)S(1)}, bf16[256,256]{1,0:T(8,128)(2,1)S(1)}, u32[]{:S(2)}, u32[]{:S(2)}) collective-permute-start(bf16[256,256]{1,0:T(8,128)(2,1)S(1)} %get-tuple-element.61), channel_id=1, source_target_pairs={{0,5},{1,4},{2,7},{3,6},{4,1},{5,0},{6,3},{7,2},{8,13},{9,12},{10,... | collective-permute-start | bytes 393224 | tf_op jit(solution)/shard_map/ppermute | solution.py:35
  41.4 3.6 %backward.1 = (bf16[256,256]{1,0:T(8,128)(2,1)S(1)}, bf16[256,256]{1,0:T(8,128)(2,1)S(1)}, bf16[256,256]{1,0:T(8,128)(2,1)S(1)}, bf16[256,256]{1,0:T(8,128)(2,1)S(1)}, f32[1024,256]{1,0:T(8,128)S(1)}) custom-call(bf16[256,512]{1,0:T(8,128)(2,1)S(1)} %get-tuple-element.48.refs_2_.refs_0_, bf16[256,512]{1,0:T(8,128)(2,1)S(1)} %collective-permute-done.4.refs_3_.refs_1_, ...), custom_call_target="tpu_custom_call" | custom-call | flops 1207959552 | bytes 8388608 | tf_op jit(solution)/shard_map/backward/pallas_call | solution.py:429
  45.0 1.4 %collective-permute-done.12.refs_2_ = bf16[256,256]{1,0:T(8,128)(2,1)S(1)} collective-permute-done((bf16[256,256]{1,0:T(8,128)(2,1)S(1)}, bf16[256,256]{1,0:T(8,128)(2,1)S(1)}, u32[]{:S(2)}, u32[]{:S(2)}) %collective-permute-start.12) | collective-permute-done | bytes 131104 | tf_op jit(solution)/shard_map/ppermute | solution.py:35
  46.5 1.2 %collective-permute-start.14 = (bf16[256,256]{1,0:T(8,128)(2,1)S(1)}, bf16[256,256]{1,0:T(8,128)(2,1)S(1)}, u32[]{:S(2)}, u32[]{:S(2)}) collective-permute-start(bf16[256,256]{1,0:T(8,128)(2,1)S(1)} %get-tuple-element.75), channel_id=1, source_target_pairs={{0,1},{1,0},{2,3},{3,2},{4,5},{5,4},{6,7},{7,6},{8,9},{9,8},{10,11... | collective-permute-start | bytes 393224 | tf_op jit(solution)/shard_map/ppermute | solution.py:35
  47.7 0.8 %collective-permute-start.15 = (bf16[256,256]{1,0:T(8,128)(2,1)S(1)}, bf16[256,256]{1,0:T(8,128)(2,1)S(1)}, u32[]{:S(2)}, u32[]{:S(2)}) collective-permute-start(bf16[256,256]{1,0:T(8,128)(2,1)S(1)} %get-tuple-element.76), channel_id=1, source_target_pairs={{0,4},{1,5},{2,6},{3,7},{4,0},{5,1},{6,2},{7,3},{8,12},{9,13},{10,... | collective-permute-start | bytes 393224 | tf_op jit(solution)/shard_map/ppermute | solution.py:35
  48.4 1.5 %collective-permute-start.16 = (bf16[256,256]{1,0:T(8,128)(2,1)S(1)}, bf16[256,256]{1,0:T(8,128)(2,1)S(1)}, u32[]{:S(2)}, u32[]{:S(2)}) collective-permute-start(bf16[256,256]{1,0:T(8,128)(2,1)S(1)} %get-tuple-element.77), channel_id=1, source_target_pairs={{0,5},{1,4},{2,7},{3,6},{4,1},{5,0},{6,3},{7,2},{8,13},{9,12},{10,... | collective-permute-start | bytes 393224 | tf_op jit(solution)/shard_map/ppermute | solution.py:35
  49.9 1.0 %collective-permute-done.17.refs_1_ = bf16[1024,256]{1,0:T(8,128)(2,1)S(1)} collective-permute-done((bf16[1024,256]{1,0:T(8,128)(2,1)S(1)}, bf16[1024,256]{1,0:T(8,128)(2,1)S(1)}, u32[]{:S(2)}, u32[]{:S(2)}) %collective-permute-start.17) | collective-permute-done | bytes 524320 | tf_op jit(solution)/shard_map/ppermute | solution.py:55
  51.1 1.7 %collective-permute-start.18 = (bf16[256,256]{1,0:T(8,128)(2,1)S(1)}, bf16[256,256]{1,0:T(8,128)(2,1)S(1)}, u32[]{:S(2)}, u32[]{:S(2)}) collective-permute-start(bf16[256,256]{1,0:T(8,128)(2,1)S(1)} %get-tuple-element.81), channel_id=1, source_target_pairs={{0,1},{1,0},{2,3},{3,2},{4,5},{5,4},{6,7},{7,6},{8,9},{9,8},{10,11... | collective-permute-start | bytes 393224 | tf_op jit(solution)/shard_map/ppermute | solution.py:35
  52.8 0.6 collective-permute-start.19
  53.4 1.3 %collective-permute-start.20 = (bf16[256,256]{1,0:T(8,128)(2,1)S(1)}, bf16[256,256]{1,0:T(8,128)(2,1)S(1)}, u32[]{:S(2)}, u32[]{:S(2)}) collective-permute-start(bf16[256,256]{1,0:T(8,128)(2,1)S(1)} %get-tuple-element.83), channel_id=1, source_target_pairs={{0,5},{1,4},{2,7},{3,6},{4,1},{5,0},{6,3},{7,2},{8,13},{9,12},{10,... | collective-permute-start | bytes 393224 | tf_op jit(solution)/shard_map/ppermute | solution.py:35
  54.7 1.0 %collective-permute-done.16.refs_7_ = bf16[256,256]{1,0:T(8,128)(2,1)S(1)} collective-permute-done((bf16[256,256]{1,0:T(8,128)(2,1)S(1)}, bf16[256,256]{1,0:T(8,128)(2,1)S(1)}, u32[]{:S(2)}, u32[]{:S(2)}) %collective-permute-start.16) | collective-permute-done | bytes 131104 | tf_op jit(solution)/shard_map/ppermute | solution.py:35
  55.7 2.0 %collective-permute-done.18.refs_9_ = bf16[256,256]{1,0:T(8,128)(2,1)S(1)} collective-permute-done((bf16[256,256]{1,0:T(8,128)(2,1)S(1)}, bf16[256,256]{1,0:T(8,128)(2,1)S(1)}, u32[]{:S(2)}, u32[]{:S(2)}) %collective-permute-start.18) | collective-permute-done | bytes 131104 | tf_op jit(solution)/shard_map/ppermute | solution.py:35
  57.7 2.4 %collective-permute-done.19.refs_10_ = bf16[256,256]{1,0:T(8,128)(2,1)S(1)} collective-permute-done((bf16[256,256]{1,0:T(8,128)(2,1)S(1)}, bf16[256,256]{1,0:T(8,128)(2,1)S(1)}, u32[]{:S(2)}, u32[]{:S(2)}) %collective-permute-start.19) | collective-permute-done | bytes 131104 | tf_op jit(solution)/shard_map/ppermute | solution.py:35
  60.2 2.3 %collective-permute-done.21.refs_12_ = bf16[128,3072]{1,0:T(8,128)(2,1)S(1)} collective-permute-done((bf16[128,3072]{1,0:T(8,128)(2,1)S(1)}, bf16[128,3072]{1,0:T(8,128)(2,1)S(1)}, u32[]{:S(2)}, u32[]{:S(2)}) %collective-permute-start.21) | collective-permute-done | bytes 786464 | tf_op jit(solution)/shard_map/ppermute | solution.py:35
  62.5 1.4 %spread.1 = (bf16[128,2048]{1,0:T(8,128)(2,1)}, bf16[128,2048]{1,0:T(8,128)(2,1)}, bf16[128,1024]{1,0:T(8,128)(2,1)}, bf16[128,1024]{1,0:T(8,128)(2,1)}) custom-call(bf16[256,256]{1,0:T(8,128)(2,1)S(1)} %get-tuple-element.70.refs_0_, bf16[256,256]{1,0:T(8,128)(2,1)S(1)} %collective-permute-done.11.refs_1_, ...), custom_call_target="tpu_custom_call" | custom-call | tf_op jit(solution)/shard_map/spread/pallas_call | solution.py:201
  (39 shorter events, 2.6 us)
Async XLA Ops:
  0.6 7.9 %copy-start = (bf16[128,2048]{1,0:T(8,128)(2,1)S(1)}, bf16[128,2048]{1,0:T(8,128)(2,1)}, u32[]{:S(2)}) copy-start(bf16[128,2048]{1,0:T(8,128)(2,1)} %param.5) | copy-start | bytes 1572868
  0.6 7.9 %copy-start.1 = (bf16[128,2048]{1,0:T(8,128)(2,1)S(1)}, bf16[128,2048]{1,0:T(8,128)(2,1)}, u32[]{:S(2)}) copy-start(bf16[128,2048]{1,0:T(8,128)(2,1)} %param.8) | copy-start | bytes 1572868
  0.7 8.0 %copy-start.2 = (s32[4096]{0:T(1024)S(1)}, s32[4096]{0:T(1024)}, u32[]{:S(2)}) copy-start(s32[4096]{0:T(1024)} %param.9) | copy-start | bytes 49156
  0.7 3.2 %collective-permute-start = (bf16[128,1024]{1,0:T(8,128)(2,1)}, bf16[128,1024]{1,0:T(8,128)(2,1)S(1)}, u32[]{:S(2)}, u32[]{:S(2)}) collective-permute-start(bf16[128,1024]{1,0:T(8,128)(2,1)} %param.6), channel_id=1, source_target_pairs={{0,2},{1,3},{2,0},{3,1},{4,6},{5,7},{6,4},{7,5},{8,10},{9,11},{10,... | collective-permute-start | bytes 786440 | tf_op jit(solution)/shard_map/ppermute | solution.py:35
  1.2 2.7 %collective-permute-start.1 = (bf16[128,1024]{1,0:T(8,128)(2,1)}, bf16[128,1024]{1,0:T(8,128)(2,1)S(1)}, u32[]{:S(2)}, u32[]{:S(2)}) collective-permute-start(bf16[128,1024]{1,0:T(8,128)(2,1)} %param.7), channel_id=1, source_target_pairs={{0,2},{1,3},{2,0},{3,1},{4,6},{5,7},{6,4},{7,5},{8,10},{9,11},{10,... | collective-permute-start | bytes 786440 | tf_op jit(solution)/shard_map/ppermute | solution.py:35
  1.3 7.5 %collective-permute-start.2 = (bf16[128,2048]{1,0:T(8,128)(2,1)}, bf16[128,2048]{1,0:T(8,128)(2,1)S(1)}, u32[]{:S(2)}, u32[]{:S(2)}) collective-permute-start(bf16[128,2048]{1,0:T(8,128)(2,1)} %param.5), channel_id=1, source_target_pairs={{0,2},{1,3},{2,0},{3,1},{4,6},{5,7},{6,4},{7,5},{8,10},{9,11},{10,... | collective-permute-start | bytes 1572872 | tf_op jit(solution)/shard_map/ppermute | solution.py:35
  1.7 7.1 %collective-permute-start.3 = (bf16[128,2048]{1,0:T(8,128)(2,1)}, bf16[128,2048]{1,0:T(8,128)(2,1)S(1)}, u32[]{:S(2)}, u32[]{:S(2)}) collective-permute-start(bf16[128,2048]{1,0:T(8,128)(2,1)} %param.8), channel_id=1, source_target_pairs={{0,2},{1,3},{2,0},{3,1},{4,6},{5,7},{6,4},{7,5},{8,10},{9,11},{10,... | collective-permute-start | bytes 1572872 | tf_op jit(solution)/shard_map/ppermute | solution.py:35
  4.0 8.5 %collective-permute-start.7 = (bf16[256,256]{1,0:T(8,128)(2,1)S(1)}, bf16[256,256]{1,0:T(8,128)(2,1)S(1)}, u32[]{:S(2)}, u32[]{:S(2)}) collective-permute-start(bf16[256,256]{1,0:T(8,128)(2,1)S(1)} %get-tuple-element.53), channel_id=1, source_target_pairs={{0,1},{1,0},{2,3},{3,2},{4,5},{5,4},{6,7},{7,6},{8,9},{9,8},{10,11... | collective-permute-start | bytes 393224 | tf_op jit(solution)/shard_map/ppermute | solution.py:35
  7.0 8.2 %collective-permute-start.8 = (bf16[256,256]{1,0:T(8,128)(2,1)S(1)}, bf16[256,256]{1,0:T(8,128)(2,1)S(1)}, u32[]{:S(2)}, u32[]{:S(2)}) collective-permute-start(bf16[256,256]{1,0:T(8,128)(2,1)S(1)} %get-tuple-element.54), channel_id=1, source_target_pairs={{0,4},{1,5},{2,6},{3,7},{4,0},{5,1},{6,2},{7,3},{8,12},{9,13},{10,... | collective-permute-start | bytes 393224 | tf_op jit(solution)/shard_map/ppermute | solution.py:35
  8.5 7.4 %collective-permute-start.9 = (bf16[256,256]{1,0:T(8,128)(2,1)S(1)}, bf16[256,256]{1,0:T(8,128)(2,1)S(1)}, u32[]{:S(2)}, u32[]{:S(2)}) collective-permute-start(bf16[256,256]{1,0:T(8,128)(2,1)S(1)} %get-tuple-element.55), channel_id=1, source_target_pairs={{0,5},{1,4},{2,7},{3,6},{4,1},{5,0},{6,3},{7,2},{8,13},{9,12},{10,... | collective-permute-start | bytes 393224 | tf_op jit(solution)/shard_map/ppermute | solution.py:35
  8.6 10.8 %dynamic-slice-start = ((s32[4096]{0:T(1024)}, s32[]{:T(128)}), s32[1024]{0:T(1024)S(1)}, s32[]{:S(2)}) async-start(s32[4096]{0:T(1024)} %param.9, s32[]{:T(128)} %select_n.69), calls=%async_computation | async-start | bytes 8704 | tf_op jit(solution)/shard_map/dynamic_slice | solution.py:540
  9.0 11.5 %collective-permute-start.4 = (bf16[256,512]{1,0:T(8,128)(2,1)S(1)}, bf16[256,512]{1,0:T(8,128)(2,1)S(1)}, u32[]{:S(2)}, u32[]{:S(2)}) collective-permute-start(bf16[256,512]{1,0:T(8,128)(2,1)S(1)} %get-tuple-element.49), channel_id=1, source_target_pairs={{0,1},{1,0},{2,3},{3,2},{4,5},{5,4},{6,7},{7,6},{8,9},{9,8},{10,11... | collective-permute-start | bytes 786440 | tf_op jit(solution)/shard_map/ppermute | solution.py:35
  11.0 15.2 %collective-permute-start.5 = (bf16[256,512]{1,0:T(8,128)(2,1)S(1)}, bf16[256,512]{1,0:T(8,128)(2,1)S(1)}, u32[]{:S(2)}, u32[]{:S(2)}) collective-permute-start(bf16[256,512]{1,0:T(8,128)(2,1)S(1)} %get-tuple-element.50), channel_id=1, source_target_pairs={{0,4},{1,5},{2,6},{3,7},{4,0},{5,1},{6,2},{7,3},{8,12},{9,13},{10,... | collective-permute-start | bytes 786440 | tf_op jit(solution)/shard_map/ppermute | solution.py:35
  12.5 13.7 %collective-permute-start.6 = (bf16[256,512]{1,0:T(8,128)(2,1)S(1)}, bf16[256,512]{1,0:T(8,128)(2,1)S(1)}, u32[]{:S(2)}, u32[]{:S(2)}) collective-permute-start(bf16[256,512]{1,0:T(8,128)(2,1)S(1)} %get-tuple-element.51), channel_id=1, source_target_pairs={{0,5},{1,4},{2,7},{3,6},{4,1},{5,0},{6,3},{7,2},{8,13},{9,12},{10,... | collective-permute-start | bytes 786440 | tf_op jit(solution)/shard_map/ppermute | solution.py:35
  15.9 13.0 %collective-permute-start.10 = (bf16[1024,256]{1,0:T(8,128)(2,1)S(1)}, bf16[1024,256]{1,0:T(8,128)(2,1)S(1)}, u32[]{:S(2)}, u32[]{:S(2)}) collective-permute-start(bf16[1024,256]{1,0:T(8,128)(2,1)S(1)} %join.1.refs_6_.refs_4_), channel_id=1, source_target_pairs={{0,8},{1,9},{2,10},{3,11},{4,12},{5,13},{6,14},{7,15},{8,16},{9,17... | collective-permute-start | bytes 1572872 | tf_op jit(solution)/shard_map/ppermute | solution.py:55
  36.4 14.6 %collective-permute-start.17 = (bf16[1024,256]{1,0:T(8,128)(2,1)S(1)}, bf16[1024,256]{1,0:T(8,128)(2,1)S(1)}, u32[]{:S(2)}, u32[]{:S(2)}) collective-permute-start(bf16[1024,256]{1,0:T(8,128)(2,1)S(1)} %get-tuple-element.79), channel_id=1, source_target_pairs={{8,0},{9,1},{10,2},{11,3},{12,4},{13,5},{14,6},{15,7},{16,8},{17,9... | collective-permute-start | bytes 1572872 | tf_op jit(solution)/shard_map/ppermute | solution.py:55
  37.9 7.1 %collective-permute-start.11 = (bf16[256,256]{1,0:T(8,128)(2,1)S(1)}, bf16[256,256]{1,0:T(8,128)(2,1)S(1)}, u32[]{:S(2)}, u32[]{:S(2)}) collective-permute-start(bf16[256,256]{1,0:T(8,128)(2,1)S(1)} %get-tuple-element.59), channel_id=1, source_target_pairs={{0,1},{1,0},{2,3},{3,2},{4,5},{5,4},{6,7},{7,6},{8,9},{9,8},{10,11... | collective-permute-start | bytes 393224 | tf_op jit(solution)/shard_map/ppermute | solution.py:35
  39.4 7.0 %collective-permute-start.12 = (bf16[256,256]{1,0:T(8,128)(2,1)S(1)}, bf16[256,256]{1,0:T(8,128)(2,1)S(1)}, u32[]{:S(2)}, u32[]{:S(2)}) collective-permute-start(bf16[256,256]{1,0:T(8,128)(2,1)S(1)} %get-tuple-element.60), channel_id=1, source_target_pairs={{0,4},{1,5},{2,6},{3,7},{4,0},{5,1},{6,2},{7,3},{8,12},{9,13},{10,... | collective-permute-start | bytes 393224 | tf_op jit(solution)/shard_map/ppermute | solution.py:35
  40.0 6.5 %collective-permute-start.13 = (bf16[256,256]{1,0:T(8,128)(2,1)S(1)}, bf16[256,256]{1,0:T(8,128)(2,1)S(1)}, u32[]{:S(2)}, u32[]{:S(2)}) collective-permute-start(bf16[256,256]{1,0:T(8,128)(2,1)S(1)} %get-tuple-element.61), channel_id=1, source_target_pairs={{0,5},{1,4},{2,7},{3,6},{4,1},{5,0},{6,3},{7,2},{8,13},{9,12},{10,... | collective-permute-start | bytes 393224 | tf_op jit(solution)/shard_map/ppermute | solution.py:35
  46.5 6.9 %collective-permute-start.14 = (bf16[256,256]{1,0:T(8,128)(2,1)S(1)}, bf16[256,256]{1,0:T(8,128)(2,1)S(1)}, u32[]{:S(2)}, u32[]{:S(2)}) collective-permute-start(bf16[256,256]{1,0:T(8,128)(2,1)S(1)} %get-tuple-element.75), channel_id=1, source_target_pairs={{0,1},{1,0},{2,3},{3,2},{4,5},{5,4},{6,7},{7,6},{8,9},{9,8},{10,11... | collective-permute-start | bytes 393224 | tf_op jit(solution)/shard_map/ppermute | solution.py:35
  47.7 7.0 %collective-permute-start.15 = (bf16[256,256]{1,0:T(8,128)(2,1)S(1)}, bf16[256,256]{1,0:T(8,128)(2,1)S(1)}, u32[]{:S(2)}, u32[]{:S(2)}) collective-permute-start(bf16[256,256]{1,0:T(8,128)(2,1)S(1)} %get-tuple-element.76), channel_id=1, source_target_pairs={{0,4},{1,5},{2,6},{3,7},{4,0},{5,1},{6,2},{7,3},{8,12},{9,13},{10,... | collective-permute-start | bytes 393224 | tf_op jit(solution)/shard_map/ppermute | solution.py:35
  48.4 7.3 %collective-permute-start.16 = (bf16[256,256]{1,0:T(8,128)(2,1)S(1)}, bf16[256,256]{1,0:T(8,128)(2,1)S(1)}, u32[]{:S(2)}, u32[]{:S(2)}) collective-permute-start(bf16[256,256]{1,0:T(8,128)(2,1)S(1)} %get-tuple-element.77), channel_id=1, source_target_pairs={{0,5},{1,4},{2,7},{3,6},{4,1},{5,0},{6,3},{7,2},{8,13},{9,12},{10,... | collective-permute-start | bytes 393224 | tf_op jit(solution)/shard_map/ppermute | solution.py:35
  51.1 6.6 %collective-permute-start.18 = (bf16[256,256]{1,0:T(8,128)(2,1)S(1)}, bf16[256,256]{1,0:T(8,128)(2,1)S(1)}, u32[]{:S(2)}, u32[]{:S(2)}) collective-permute-start(bf16[256,256]{1,0:T(8,128)(2,1)S(1)} %get-tuple-element.81), channel_id=1, source_target_pairs={{0,1},{1,0},{2,3},{3,2},{4,5},{5,4},{6,7},{7,6},{8,9},{9,8},{10,11... | collective-permute-start | bytes 393224 | tf_op jit(solution)/shard_map/ppermute | solution.py:35
  52.8 7.3 %collective-permute-start.19 = (bf16[256,256]{1,0:T(8,128)(2,1)S(1)}, bf16[256,256]{1,0:T(8,128)(2,1)S(1)}, u32[]{:S(2)}, u32[]{:S(2)}) collective-permute-start(bf16[256,256]{1,0:T(8,128)(2,1)S(1)} %get-tuple-element.82), channel_id=1, source_target_pairs={{0,4},{1,5},{2,6},{3,7},{4,0},{5,1},{6,2},{7,3},{8,12},{9,13},{10,... | collective-permute-start | bytes 393224 | tf_op jit(solution)/shard_map/ppermute | solution.py:35
  53.4 6.7 %collective-permute-start.20 = (bf16[256,256]{1,0:T(8,128)(2,1)S(1)}, bf16[256,256]{1,0:T(8,128)(2,1)S(1)}, u32[]{:S(2)}, u32[]{:S(2)}) collective-permute-start(bf16[256,256]{1,0:T(8,128)(2,1)S(1)} %get-tuple-element.83), channel_id=1, source_target_pairs={{0,5},{1,4},{2,7},{3,6},{4,1},{5,0},{6,3},{7,2},{8,13},{9,12},{10,... | collective-permute-start | bytes 393224 | tf_op jit(solution)/shard_map/ppermute | solution.py:35
  60.2 2.4 %collective-permute-start.21 = (bf16[128,3072]{1,0:T(8,128)(2,1)S(1)}, bf16[128,3072]{1,0:T(8,128)(2,1)S(1)}, u32[]{:S(2)}, u32[]{:S(2)}) collective-permute-start(bf16[128,3072]{1,0:T(8,128)(2,1)S(1)} %bottom.1), channel_id=1, source_target_pairs={{0,2},{1,3},{2,0},{3,1},{4,6},{5,7},{6,4},{7,5},{8,10},{9,11},{10,... | collective-permute-start | bytes 2359304 | tf_op jit(solution)/shard_map/ppermute | solution.py:35

commit v13 on v12

--- a/solution.py
+++ b/solution.py
@@ -259,7 +259,14 @@
 def score_gradients(ds_scr, e, dp):
     for at in range(0, e.shape[0], TILE):
         part = slice(at, at + TILE)
-        ds_scr[part, :] = (e[part, :].astype(F32) * dp[part]).astype(BF16)
+        ds_scr[part, :] = (e[part, :].astype(F32) * dp[part, :]).astype(BF16)
+
+
+def pipeline(tiles, *stages):
+    for step in range(tiles + len(stages) - 1):
+        for behind, stage in enumerate(stages):
+            if 0 <= step - behind < tiles:
+                stage(step - behind)
 
 
 def gradient_rows(qg, base, group, scale, out):
@@ -323,19 +330,20 @@
         queries = query_columns(qg, seg_q, tile * TILE, group)
         s_scr[tile % 2, : (tile + 1) * TILE, :] = dot_t(ka[: (tile + 1) * TILE, :], queries)
 
-    scores(0)
-    for tile in range(tiles):
+    def weights(tile):
         base, turn = tile * TILE, tile % 2
-        count = base + TILE
-        s_scr[turn, base:count, :] = jnp.where(causal, s_scr[turn, base:count, :], FAR)
-        rows = s_scr.at[turn, :count, :]
+        last = slice(base, base + TILE)
+        s_scr[turn, last, :] = jnp.where(causal, s_scr[turn, last, :], FAR)
+        rows = s_scr.at[turn, : base + TILE, :]
         top = fold_rows(rows, jnp.maximum) * exp2_scale
-        if tile + 1 < tiles:
-            scores(tile + 1)
-        mine = e_own.at[own_rows(tile), :]
         stats[tile : tile + 1, :] = top
-        stats[tiles + tile : tiles + tile + 1, :] = weigh(rows, top, mine)
-        out_part[:, tile * wide : (tile + 1) * wide] = dot(vt[:, :count], mine[...])
+        stats[tiles + tile : tiles + tile + 1, :] = weigh(rows, top, e_own.at[own_rows(tile), :])
+
+    def outputs(tile):
+        e = e_own[own_rows(tile), :]
+        out_part[:, tile * wide : (tile + 1) * wide] = dot(vt[:, : (tile + 1) * TILE], e)
+
+    pipeline(tiles, scores, weights, outputs)
 
 
 def forward_body(size, core, masks, reach, tok, group, *refs):
@@ -343,7 +351,7 @@
     (seg_k, seg_q), qg_pieces, kvs = take(2), take(len(masks)), take(reach)
     out_own, stats = take(2)
     out_pieces, sent, (outs, own_scale, dq_part) = take(len(masks)), take(reach), take(3)
-    qg, ka, va, kt, vt, dk, dv, s_scr, e_scr, ds_scr = take(10)
+    qg, ka, va, kt, vt, dk, dv, s_scr, e_scr, dp_scr, ds_scr, g_scr = take(12)
     wide, tiles = group * TILE, tok // TILE
     place_rows(size, core, masks, qg_pieces, qg)
     ka[:, HEAD_DIM:] = seg_k[:WINDOW, :]
@@ -361,34 +369,44 @@
         queries = query_columns(qg, seg_q, base, group)
         s_scr[tile % 2, : WINDOW - base, :] = dot_t(ka[base:, :], queries)
 
-    scores(0)
-    for tile in range(tiles):
-        base, turn = tile * TILE, tile % 2
-        early = WINDOW - base
-        columns = slice(tile * wide, (tile + 1) * wide)
+    scales = {}
+
+    def weights(tile):
+        early = WINDOW - tile * TILE
+        turn = tile % 2
         s_scr[turn, :TILE, :] = jnp.where(beyond, s_scr[turn, :TILE, :], FAR)
         rows = s_scr.at[turn, :early, :]
         top_own = stats[tile : tile + 1, :]
         top = jnp.maximum(fold_rows(rows, jnp.maximum) * exp2_scale, top_own)
-        if tile + 1 < tiles:
-            scores(tile + 1)
-        mine = e_scr.at[turn, :early, :]
-        total = weigh(rows, top, mine)
+        total = weigh(rows, top, e_scr.at[tile % 3, :early, :])
         scale = jnp.exp2(top_own - top)
         inv = 1.0 / (total + stats[tiles + tile : tiles + tile + 1, :] * scale)
-        e = mine[...]
-        out = dot(vt[:, base:], e) + out_own[:, columns] * scale
+        own_scale[tile : tile + 1, :] = inv * scale
+        scales[tile] = scale, inv
+
+    def outputs(tile):
+        base, turn = tile * TILE, tile % 2
+        early = WINDOW - base
+        scale, inv = scales.pop(tile)
+        out = dot(vt[:, base:], e_scr[tile % 3, :early, :])
+        out = out + out_own[:, tile * wide : (tile + 1) * wide] * scale
         out = (out * inv).T.astype(BF16)
         unstacked(outs, base, group, out)
-        own_scale[tile : tile + 1, :] = inv * scale
-        g2, g_wide = gradient_rows(qg, base, group, inv, out)
-        dp = dot_t(va[base:, :], g_wide)
+        g_scr[turn], g_wide = gradient_rows(qg, base, group, inv, out)
+        dp_scr[turn, :early, :] = dot_t(va[base:, :], g_wide)
+
+    def gradients(tile):
+        base, turn = tile * TILE, tile % 2
+        early = WINDOW - base
+        e = e_scr[tile % 3, :early, :]
         old = early if tile else 0
-        add_rows(dv, base, old, dot(e, g2))
-        score_gradients(ds_scr.at[turn, :early, :], e, dp)
+        add_rows(dv, base, old, dot(e, g_scr[turn]))
+        score_gradients(ds_scr.at[turn, :early, :], e, dp_scr.at[turn, :early, :])
         ds = ds_scr[turn, :early, :]
         add_rows(dk, base, old, dot(ds, stacked(qg, base, group)))
-        dq_part[:, columns] = dot(kt[:, base:], ds)
+        dq_part[:, tile * wide : (tile + 1) * wide] = dot(kt[:, base:], ds)
+
+    pipeline(tiles, scores, weights, outputs, gradients)
 
     for lag in range(1, reach + 1):
         there = slice((reach - lag) * tok, (reach - lag + 1) * tok)
@@ -401,25 +419,32 @@
     take = taker(refs)
     qg_pieces, (kv, e_own, outs, own_scale, dq_part) = take(len(masks)), take(5)
     dq_pieces, (dkv,) = take(len(masks)), take(1)
-    qg, dqs, va, kt, dk, dv, ds_scr = take(7)
+    qg, dqs, va, kt, dk, dv, dp_scr, ds_scr, g_scr = take(9)
     wide = group * TILE
     place_rows(size, core, masks, qg_pieces, qg)
     kt[...] = kv[:, :HEAD_DIM].T
     set_values(va, kv[:, HEAD_DIM:])
-    for tile in range(tok // TILE):
+
+    def products(tile):
+        base, turn = tile * TILE, tile % 2
+        scale = own_scale[tile : tile + 1, :]
+        out = stacked(outs, base, group)
+        g_scr[turn], g_wide = gradient_rows(qg, base, group, scale, out)
+        dp_scr[turn, : base + TILE, :] = dot_t(va[: base + TILE, :], g_wide)
+
+    def gradients(tile):
         base, turn = tile * TILE, tile % 2
         count = base + TILE
         columns = slice(tile * wide, (tile + 1) * wide)
         e = e_own[own_rows(tile), :]
-        scale = own_scale[tile : tile + 1, :]
-        g2, g_wide = gradient_rows(qg, base, group, scale, stacked(outs, base, group))
-        dp = dot_t(va[:count, :], g_wide)
-        add_rows(dv, 0, base, dot(e, g2))
-        score_gradients(ds_scr.at[turn, :count, :], e, dp)
+        add_rows(dv, 0, base, dot(e, g_scr[turn]))
+        score_gradients(ds_scr.at[turn, :count, :], e, dp_scr.at[turn, :count, :])
         ds = ds_scr[turn, :count, :]
         add_rows(dk, 0, base, dot(ds, stacked(qg, base, group)))
         dq = (dq_part[:, columns] + dot(kt[:, :count], ds)) * logit_scale
         unstacked(dqs, base, group, dq.T.astype(BF16))
+
+    pipeline(tok // TILE, products, gradients)
     dkv[:, :HEAD_DIM] = dk[...] * logit_scale
     dkv[:, HEAD_DIM:] = dv[...]
     take_rows(size, core, masks, lambda there: dqs[there, :], dq_pieces)
@@ -487,8 +512,10 @@
         pltpu.VMEM((WINDOW, HEAD_DIM), F32),
         pltpu.VMEM((WINDOW, HEAD_DIM), F32),
         pltpu.VMEM((2, WINDOW, wide), F32),
+        pltpu.VMEM((3, WINDOW, wide), BF16),
+        pltpu.VMEM((2, WINDOW, wide), F32),
         pltpu.VMEM((2, WINDOW, wide), BF16),
-        pltpu.VMEM((2, WINDOW, wide), BF16),
+        pltpu.VMEM((2, wide, HEAD_DIM), BF16),
     ]
     results = attend_call(
         functools.partial(
@@ -522,7 +549,9 @@
             pltpu.VMEM((HEAD_DIM, tok), BF16),
             pltpu.VMEM((tok, HEAD_DIM), F32),
             pltpu.VMEM((tok, HEAD_DIM), F32),
+            pltpu.VMEM((2, tok, wide), F32),
             pltpu.VMEM((2, tok, wide), BF16),
+            pltpu.VMEM((2, wide, HEAD_DIM), BF16),
         ],
         4 * tok * group * (WINDOW + TILE) * HEAD_DIM,
         "backward",

time: 64.3 us -> 62.8 us (0.977)
  Pallas kernels: 15.7 us -> 13.8 us
    pallas_call x3, Pallas kernels: 13.7 us -> 11.8 us  [attend_call(): pl.pallas_call(kernel, out_shape=out_shape, in_specs=[VMEM] * len(args),...]
  transfers between devices with their start and end apart: 22 -> 22, of which waited for: 10 -> 11; matrix products, arithmetic and copies ran while one was open for 4% -> 4% of each run, Pallas kernels for 10% -> 10%
where the time goes in v13:
time: 62.8 us; the launch traced here: 62.6 us
  starting transfers between devices  26.6 us (42%)
  waiting for transfers between devices  18.4 us (29%)
  Pallas kernels  13.8 us (22%)
  local copies, waits for them, and re-layouts  2.03 us (3%)
  between operations  1.1 us (2%)
  other arithmetic  0.74 us (1%)
    ppermute x20, starting transfers between devices, swap(): lax.ppermute(value, BOTH, [(i, i ^ mask) for i in range(device_count())])  21.6 us
    ppermute x20, waiting for transfers between devices, swap(): lax.ppermute(value, BOTH, [(i, i ^ mask) for i in range(device_count())])  17.4 us
    pallas_call x3, Pallas kernels, attend_call(): pl.pallas_call(kernel, out_shape=out_shape, in_specs=[VMEM] * len(args),...  11.8 us
    ppermute x2, starting transfers between devices, shifted(): return lax.ppermute(value, BOTH, pairs)  4.99 us
    slice x4, local copies, waits for them, and re-layouts, this_core(): shares = [array[:, r * width:(r + 1) * width] for r in range(size)]  1.99 us
    pallas_call x1, Pallas kernels, spread_cores(): pl.pallas_call(functools.partial(spread_body, size, core_mask(), chip_mas...  1.39 us
  transfers between devices with their start and end apart: 22, of which 11 were waited for; matrix products, arithmetic and copies ran while one was open for 4% of the time, Pallas kernels for 10%

profile of v13, /device:TPU:0, one launch (start us, length us, event | category | flops | bytes accessed | tf_op | source)
XLA Modules:
  0.0 62.6 jit_solution(14047204016415216082)
XLA Ops:
  0.7 0.5 collective-permute-start
  1.8 1.0 %fusion.3 = (bf16[128,256]{1,0:T(8,128)(2,1)S(1)}, bf16[128,256]{1,0:T(8,128)(2,1)S(1)}, bf16[128,256]{1,0:T(8,128)(2,1)S(1)}, bf16[128,256]{1,0:T(8,128)(2,1)S(1)}) fusion(bf16[128,1024]{1,0:T(8,128)(2,1)} %param.6), kind=kLoop, calls=%fused_computation.12 | loop fusion | bytes 524288 | tf_op jit(solution)/shard_map/slice | solution.py:94
  2.7 1.0 %fusion.2 = (bf16[128,256]{1,0:T(8,128)(2,1)S(1)}, bf16[128,256]{1,0:T(8,128)(2,1)S(1)}, bf16[128,256]{1,0:T(8,128)(2,1)S(1)}, bf16[128,256]{1,0:T(8,128)(2,1)S(1)}) fusion(bf16[128,1024]{1,0:T(8,128)(2,1)} %param.7), kind=kLoop, calls=%fused_computation.11 | loop fusion | bytes 524288 | tf_op jit(solution)/shard_map/slice | solution.py:94
  4.0 3.0 %collective-permute-start.7 = (bf16[256,256]{1,0:T(8,128)(2,1)S(1)}, bf16[256,256]{1,0:T(8,128)(2,1)S(1)}, u32[]{:S(2)}, u32[]{:S(2)}) collective-permute-start(bf16[256,256]{1,0:T(8,128)(2,1)S(1)} %get-tuple-element.53), channel_id=1, source_target_pairs={{0,1},{1,0},{2,3},{3,2},{4,5},{5,4},{6,7},{7,6},{8,9},{9,8},{10,11... | collective-permute-start | bytes 393224 | tf_op jit(solution)/shard_map/ppermute | solution.py:35
  7.0 1.5 %collective-permute-start.8 = (bf16[256,256]{1,0:T(8,128)(2,1)S(1)}, bf16[256,256]{1,0:T(8,128)(2,1)S(1)}, u32[]{:S(2)}, u32[]{:S(2)}) collective-permute-start(bf16[256,256]{1,0:T(8,128)(2,1)S(1)} %get-tuple-element.54), channel_id=1, source_target_pairs={{0,4},{1,5},{2,6},{3,7},{4,0},{5,1},{6,2},{7,3},{8,12},{9,13},{10,... | collective-permute-start | bytes 393224 | tf_op jit(solution)/shard_map/ppermute | solution.py:35
  9.0 2.0 %collective-permute-start.4 = (bf16[256,512]{1,0:T(8,128)(2,1)S(1)}, bf16[256,512]{1,0:T(8,128)(2,1)S(1)}, u32[]{:S(2)}, u32[]{:S(2)}) collective-permute-start(bf16[256,512]{1,0:T(8,128)(2,1)S(1)} %get-tuple-element.49), channel_id=1, source_target_pairs={{0,1},{1,0},{2,3},{3,2},{4,5},{5,4},{6,7},{7,6},{8,9},{9,8},{10,11... | collective-permute-start | bytes 786440 | tf_op jit(solution)/shard_map/ppermute | solution.py:35
  11.0 1.5 %collective-permute-start.5 = (bf16[256,512]{1,0:T(8,128)(2,1)S(1)}, bf16[256,512]{1,0:T(8,128)(2,1)S(1)}, u32[]{:S(2)}, u32[]{:S(2)}) collective-permute-start(bf16[256,512]{1,0:T(8,128)(2,1)S(1)} %get-tuple-element.50), channel_id=1, source_target_pairs={{0,4},{1,5},{2,6},{3,7},{4,0},{5,1},{6,2},{7,3},{8,12},{9,13},{10,... | collective-permute-start | bytes 786440 | tf_op jit(solution)/shard_map/ppermute | solution.py:35
  12.5 1.7 %collective-permute-start.6 = (bf16[256,512]{1,0:T(8,128)(2,1)S(1)}, bf16[256,512]{1,0:T(8,128)(2,1)S(1)}, u32[]{:S(2)}, u32[]{:S(2)}) collective-permute-start(bf16[256,512]{1,0:T(8,128)(2,1)S(1)} %get-tuple-element.51), channel_id=1, source_target_pairs={{0,5},{1,4},{2,7},{3,6},{4,1},{5,0},{6,3},{7,2},{8,13},{9,12},{10,... | collective-permute-start | bytes 786440 | tf_op jit(solution)/shard_map/ppermute | solution.py:35
  14.6 0.6 collective-permute-done.8.refs_2_
  15.2 0.7 %collective-permute-done.9.refs_3_ = bf16[256,256]{1,0:T(8,128)(2,1)S(1)} collective-permute-done((bf16[256,256]{1,0:T(8,128)(2,1)S(1)}, bf16[256,256]{1,0:T(8,128)(2,1)S(1)}, u32[]{:S(2)}, u32[]{:S(2)}) %collective-permute-start.9) | collective-permute-done | bytes 131104 | tf_op jit(solution)/shard_map/ppermute | solution.py:35
  15.9 3.5 %collective-permute-start.10 = (bf16[1024,256]{1,0:T(8,128)(2,1)S(1)}, bf16[1024,256]{1,0:T(8,128)(2,1)S(1)}, u32[]{:S(2)}, u32[]{:S(2)}) collective-permute-start(bf16[1024,256]{1,0:T(8,128)(2,1)S(1)} %join.1.refs_6_.refs_4_), channel_id=1, source_target_pairs={{0,8},{1,9},{2,10},{3,11},{4,12},{5,13},{6,14},{7,15},{8,16},{9,17... | collective-permute-start | bytes 1572872 | tf_op jit(solution)/shard_map/ppermute | solution.py:55
  19.7 0.8 %collective-permute-done.4.refs_3_.refs_1_ = bf16[256,512]{1,0:T(8,128)(2,1)S(1)} collective-permute-done((bf16[256,512]{1,0:T(8,128)(2,1)S(1)}, bf16[256,512]{1,0:T(8,128)(2,1)S(1)}, u32[]{:S(2)}, u32[]{:S(2)}) %collective-permute-start.4) | collective-permute-done | bytes 262176 | tf_op jit(solution)/shard_map/ppermute | solution.py:35
  20.5 5.7 %collective-permute-done.5.refs_4_.refs_2_ = bf16[256,512]{1,0:T(8,128)(2,1)S(1)} collective-permute-done((bf16[256,512]{1,0:T(8,128)(2,1)S(1)}, bf16[256,512]{1,0:T(8,128)(2,1)S(1)}, u32[]{:S(2)}, u32[]{:S(2)}) %collective-permute-start.5) | collective-permute-done | bytes 262176 | tf_op jit(solution)/shard_map/ppermute | solution.py:35
  26.2 2.4 %forward_own.1 = (bf16[4608,256]{1,0:T(8,128)(2,1)S(1)}, f32[128,2048]{1,0:T(8,128)S(1)}, f32[16,256]{1,0:T(8,128)S(1)}) custom-call(bf16[2048,128]{1,0:T(8,128)(2,1)S(1)} %select_convert_fusion.refs_0_, bf16[1024,128]{1,0:T(8,128)(2,1)S(1)} %select_convert_fusion.1.refs_1_, bf16[256,512]{1,0:T(8,128)(2,1)S(1)} %get-tuple-element.48.refs_2_.refs_0_, ...), custom_call_target="tpu_custom_call" | custom-call | flops 4831838208 | bytes 8388608 | tf_op jit(solution)/shard_map/forward_own/pallas_call | solution.py:454
  28.7 6.3 %forward.1 = (bf16[256,256]{1,0:T(8,128)(2,1)S(1)}, bf16[256,256]{1,0:T(8,128)(2,1)S(1)}, bf16[256,256]{1,0:T(8,128)(2,1)S(1)}, bf16[256,256]{1,0:T(8,128)(2,1)S...) custom-call(bf16[2048,128]{1,0:T(8,128)(2,1)S(1)} %select_convert_fu, ...), custom_call_target="tpu_custom_call" | custom-call | flops 1811939328 | bytes 8388608 | tf_op jit(solution)/shard_map/forward/pallas_call | solution.py:454
  34.9 1.5 %collective-permute-start.17 = (bf16[1024,256]{1,0:T(8,128)(2,1)S(1)}, bf16[1024,256]{1,0:T(8,128)(2,1)S(1)}, u32[]{:S(2)}, u32[]{:S(2)}) collective-permute-start(bf16[1024,256]{1,0:T(8,128)(2,1)S(1)} %get-tuple-element.79), channel_id=1, source_target_pairs={{8,0},{9,1},{10,2},{11,3},{12,4},{13,5},{14,6},{15,7},{16,8},{17,9... | collective-permute-start | bytes 1572872 | tf_op jit(solution)/shard_map/ppermute | solution.py:55
  36.4 1.8 %collective-permute-start.11 = (bf16[256,256]{1,0:T(8,128)(2,1)S(1)}, bf16[256,256]{1,0:T(8,128)(2,1)S(1)}, u32[]{:S(2)}, u32[]{:S(2)}) collective-permute-start(bf16[256,256]{1,0:T(8,128)(2,1)S(1)} %get-tuple-element.59), channel_id=1, source_target_pairs={{0,1},{1,0},{2,3},{3,2},{4,5},{5,4},{6,7},{7,6},{8,9},{9,8},{10,11... | collective-permute-start | bytes 393224 | tf_op jit(solution)/shard_map/ppermute | solution.py:35
  38.7 1.3 %collective-permute-start.13 = (bf16[256,256]{1,0:T(8,128)(2,1)S(1)}, bf16[256,256]{1,0:T(8,128)(2,1)S(1)}, u32[]{:S(2)}, u32[]{:S(2)}) collective-permute-start(bf16[256,256]{1,0:T(8,128)(2,1)S(1)} %get-tuple-element.61), channel_id=1, source_target_pairs={{0,5},{1,4},{2,7},{3,6},{4,1},{5,0},{6,3},{7,2},{8,13},{9,12},{10,... | collective-permute-start | bytes 393224 | tf_op jit(solution)/shard_map/ppermute | solution.py:35
  40.0 3.2 %backward.1 = (bf16[256,256]{1,0:T(8,128)(2,1)S(1)}, bf16[256,256]{1,0:T(8,128)(2,1)S(1)}, bf16[256,256]{1,0:T(8,128)(2,1)S(1)}, bf16[256,256]{1,0:T(8,128)(2,1)S(1)}, f32[1024,256]{1,0:T(8,128)S(1)}) custom-call(bf16[256,512]{1,0:T(8,128)(2,1)S(1)} %get-tuple-element.48.refs_2_.refs_0_, bf16[256,512]{1,0:T(8,128)(2,1)S(1)} %collective-permute-done.4.refs_3_.refs_1_, ...), custom_call_target="tpu_custom_call" | custom-call | flops 1207959552 | bytes 8388608 | tf_op jit(solution)/shard_map/backward/pallas_call | solution.py:454
  43.2 1.9 %collective-permute-done.12.refs_2_ = bf16[256,256]{1,0:T(8,128)(2,1)S(1)} collective-permute-done((bf16[256,256]{1,0:T(8,128)(2,1)S(1)}, bf16[256,256]{1,0:T(8,128)(2,1)S(1)}, u32[]{:S(2)}, u32[]{:S(2)}) %collective-permute-start.12) | collective-permute-done | bytes 131104 | tf_op jit(solution)/shard_map/ppermute | solution.py:35
  45.1 1.1 %collective-permute-start.14 = (bf16[256,256]{1,0:T(8,128)(2,1)S(1)}, bf16[256,256]{1,0:T(8,128)(2,1)S(1)}, u32[]{:S(2)}, u32[]{:S(2)}) collective-permute-start(bf16[256,256]{1,0:T(8,128)(2,1)S(1)} %get-tuple-element.75), channel_id=1, source_target_pairs={{0,1},{1,0},{2,3},{3,2},{4,5},{5,4},{6,7},{7,6},{8,9},{9,8},{10,11... | collective-permute-start | bytes 393224 | tf_op jit(solution)/shard_map/ppermute | solution.py:35
  46.2 0.7 %collective-permute-start.15 = (bf16[256,256]{1,0:T(8,128)(2,1)S(1)}, bf16[256,256]{1,0:T(8,128)(2,1)S(1)}, u32[]{:S(2)}, u32[]{:S(2)}) collective-permute-start(bf16[256,256]{1,0:T(8,128)(2,1)S(1)} %get-tuple-element.76), channel_id=1, source_target_pairs={{0,4},{1,5},{2,6},{3,7},{4,0},{5,1},{6,2},{7,3},{8,12},{9,13},{10,... | collective-permute-start | bytes 393224 | tf_op jit(solution)/shard_map/ppermute | solution.py:35
  46.8 1.7 %collective-permute-start.16 = (bf16[256,256]{1,0:T(8,128)(2,1)S(1)}, bf16[256,256]{1,0:T(8,128)(2,1)S(1)}, u32[]{:S(2)}, u32[]{:S(2)}) collective-permute-start(bf16[256,256]{1,0:T(8,128)(2,1)S(1)} %get-tuple-element.77), channel_id=1, source_target_pairs={{0,5},{1,4},{2,7},{3,6},{4,1},{5,0},{6,3},{7,2},{8,13},{9,12},{10,... | collective-permute-start | bytes 393224 | tf_op jit(solution)/shard_map/ppermute | solution.py:35
  48.6 0.9 %collective-permute-done.17.refs_1_ = bf16[1024,256]{1,0:T(8,128)(2,1)S(1)} collective-permute-done((bf16[1024,256]{1,0:T(8,128)(2,1)S(1)}, bf16[1024,256]{1,0:T(8,128)(2,1)S(1)}, u32[]{:S(2)}, u32[]{:S(2)}) %collective-permute-start.17) | collective-permute-done | bytes 524320 | tf_op jit(solution)/shard_map/ppermute | solution.py:55
  49.6 1.7 %collective-permute-start.18 = (bf16[256,256]{1,0:T(8,128)(2,1)S(1)}, bf16[256,256]{1,0:T(8,128)(2,1)S(1)}, u32[]{:S(2)}, u32[]{:S(2)}) collective-permute-start(bf16[256,256]{1,0:T(8,128)(2,1)S(1)} %get-tuple-element.81), channel_id=1, source_target_pairs={{0,1},{1,0},{2,3},{3,2},{4,5},{5,4},{6,7},{7,6},{8,9},{9,8},{10,11... | collective-permute-start | bytes 393224 | tf_op jit(solution)/shard_map/ppermute | solution.py:35
  51.3 0.6 collective-permute-start.19
  51.9 1.3 %collective-permute-start.20 = (bf16[256,256]{1,0:T(8,128)(2,1)S(1)}, bf16[256,256]{1,0:T(8,128)(2,1)S(1)}, u32[]{:S(2)}, u32[]{:S(2)}) collective-permute-start(bf16[256,256]{1,0:T(8,128)(2,1)S(1)} %get-tuple-element.83), channel_id=1, source_target_pairs={{0,5},{1,4},{2,7},{3,6},{4,1},{5,0},{6,3},{7,2},{8,13},{9,12},{10,... | collective-permute-start | bytes 393224 | tf_op jit(solution)/shard_map/ppermute | solution.py:35
  53.1 1.0 %collective-permute-done.16.refs_7_ = bf16[256,256]{1,0:T(8,128)(2,1)S(1)} collective-permute-done((bf16[256,256]{1,0:T(8,128)(2,1)S(1)}, bf16[256,256]{1,0:T(8,128)(2,1)S(1)}, u32[]{:S(2)}, u32[]{:S(2)}) %collective-permute-start.16) | collective-permute-done | bytes 131104 | tf_op jit(solution)/shard_map/ppermute | solution.py:35
  54.1 2.5 %collective-permute-done.18.refs_9_ = bf16[256,256]{1,0:T(8,128)(2,1)S(1)} collective-permute-done((bf16[256,256]{1,0:T(8,128)(2,1)S(1)}, bf16[256,256]{1,0:T(8,128)(2,1)S(1)}, u32[]{:S(2)}, u32[]{:S(2)}) %collective-permute-start.18) | collective-permute-done | bytes 131104 | tf_op jit(solution)/shard_map/ppermute | solution.py:35
  56.6 2.0 %collective-permute-done.19.refs_10_ = bf16[256,256]{1,0:T(8,128)(2,1)S(1)} collective-permute-done((bf16[256,256]{1,0:T(8,128)(2,1)S(1)}, bf16[256,256]{1,0:T(8,128)(2,1)S(1)}, u32[]{:S(2)}, u32[]{:S(2)}) %collective-permute-start.19) | collective-permute-done | bytes 131104 | tf_op jit(solution)/shard_map/ppermute | solution.py:35
  58.7 2.3 %collective-permute-done.21.refs_12_ = bf16[128,3072]{1,0:T(8,128)(2,1)S(1)} collective-permute-done((bf16[128,3072]{1,0:T(8,128)(2,1)S(1)}, bf16[128,3072]{1,0:T(8,128)(2,1)S(1)}, u32[]{:S(2)}, u32[]{:S(2)}) %collective-permute-start.21) | collective-permute-done | bytes 786464 | tf_op jit(solution)/shard_map/ppermute | solution.py:35
  61.0 1.4 %spread.1 = (bf16[128,2048]{1,0:T(8,128)(2,1)}, bf16[128,2048]{1,0:T(8,128)(2,1)}, bf16[128,1024]{1,0:T(8,128)(2,1)}, bf16[128,1024]{1,0:T(8,128)(2,1)}) custom-call(bf16[256,256]{1,0:T(8,128)(2,1)S(1)} %get-tuple-element.70.refs_0_, bf16[256,256]{1,0:T(8,128)(2,1)S(1)} %collective-permute-done.11.refs_1_, ...), custom_call_target="tpu_custom_call" | custom-call | tf_op jit(solution)/shard_map/spread/pallas_call | solution.py:201
  (39 shorter events, 2.7 us)
Async XLA Ops:
  0.6 7.9 %copy-start = (bf16[128,2048]{1,0:T(8,128)(2,1)S(1)}, bf16[128,2048]{1,0:T(8,128)(2,1)}, u32[]{:S(2)}) copy-start(bf16[128,2048]{1,0:T(8,128)(2,1)} %param.5) | copy-start | bytes 1572868
  0.6 7.9 %copy-start.1 = (bf16[128,2048]{1,0:T(8,128)(2,1)S(1)}, bf16[128,2048]{1,0:T(8,128)(2,1)}, u32[]{:S(2)}) copy-start(bf16[128,2048]{1,0:T(8,128)(2,1)} %param.8) | copy-start | bytes 1572868
  0.7 8.0 %copy-start.2 = (s32[4096]{0:T(1024)S(1)}, s32[4096]{0:T(1024)}, u32[]{:S(2)}) copy-start(s32[4096]{0:T(1024)} %param.9) | copy-start | bytes 49156
  0.7 3.2 %collective-permute-start = (bf16[128,1024]{1,0:T(8,128)(2,1)}, bf16[128,1024]{1,0:T(8,128)(2,1)S(1)}, u32[]{:S(2)}, u32[]{:S(2)}) collective-permute-start(bf16[128,1024]{1,0:T(8,128)(2,1)} %param.6), channel_id=1, source_target_pairs={{0,2},{1,3},{2,0},{3,1},{4,6},{5,7},{6,4},{7,5},{8,10},{9,11},{10,... | collective-permute-start | bytes 786440 | tf_op jit(solution)/shard_map/ppermute | solution.py:35
  1.2 2.7 %collective-permute-start.1 = (bf16[128,1024]{1,0:T(8,128)(2,1)}, bf16[128,1024]{1,0:T(8,128)(2,1)S(1)}, u32[]{:S(2)}, u32[]{:S(2)}) collective-permute-start(bf16[128,1024]{1,0:T(8,128)(2,1)} %param.7), channel_id=1, source_target_pairs={{0,2},{1,3},{2,0},{3,1},{4,6},{5,7},{6,4},{7,5},{8,10},{9,11},{10,... | collective-permute-start | bytes 786440 | tf_op jit(solution)/shard_map/ppermute | solution.py:35
  1.3 7.5 %collective-permute-start.2 = (bf16[128,2048]{1,0:T(8,128)(2,1)}, bf16[128,2048]{1,0:T(8,128)(2,1)S(1)}, u32[]{:S(2)}, u32[]{:S(2)}) collective-permute-start(bf16[128,2048]{1,0:T(8,128)(2,1)} %param.5), channel_id=1, source_target_pairs={{0,2},{1,3},{2,0},{3,1},{4,6},{5,7},{6,4},{7,5},{8,10},{9,11},{10,... | collective-permute-start | bytes 1572872 | tf_op jit(solution)/shard_map/ppermute | solution.py:35
  1.7 7.1 %collective-permute-start.3 = (bf16[128,2048]{1,0:T(8,128)(2,1)}, bf16[128,2048]{1,0:T(8,128)(2,1)S(1)}, u32[]{:S(2)}, u32[]{:S(2)}) collective-permute-start(bf16[128,2048]{1,0:T(8,128)(2,1)} %param.8), channel_id=1, source_target_pairs={{0,2},{1,3},{2,0},{3,1},{4,6},{5,7},{6,4},{7,5},{8,10},{9,11},{10,... | collective-permute-start | bytes 1572872 | tf_op jit(solution)/shard_map/ppermute | solution.py:35
  4.0 8.5 %collective-permute-start.7 = (bf16[256,256]{1,0:T(8,128)(2,1)S(1)}, bf16[256,256]{1,0:T(8,128)(2,1)S(1)}, u32[]{:S(2)}, u32[]{:S(2)}) collective-permute-start(bf16[256,256]{1,0:T(8,128)(2,1)S(1)} %get-tuple-element.53), channel_id=1, source_target_pairs={{0,1},{1,0},{2,3},{3,2},{4,5},{5,4},{6,7},{7,6},{8,9},{9,8},{10,11... | collective-permute-start | bytes 393224 | tf_op jit(solution)/shard_map/ppermute | solution.py:35
  7.0 8.2 %collective-permute-start.8 = (bf16[256,256]{1,0:T(8,128)(2,1)S(1)}, bf16[256,256]{1,0:T(8,128)(2,1)S(1)}, u32[]{:S(2)}, u32[]{:S(2)}) collective-permute-start(bf16[256,256]{1,0:T(8,128)(2,1)S(1)} %get-tuple-element.54), channel_id=1, source_target_pairs={{0,4},{1,5},{2,6},{3,7},{4,0},{5,1},{6,2},{7,3},{8,12},{9,13},{10,... | collective-permute-start | bytes 393224 | tf_op jit(solution)/shard_map/ppermute | solution.py:35
  8.5 7.4 %collective-permute-start.9 = (bf16[256,256]{1,0:T(8,128)(2,1)S(1)}, bf16[256,256]{1,0:T(8,128)(2,1)S(1)}, u32[]{:S(2)}, u32[]{:S(2)}) collective-permute-start(bf16[256,256]{1,0:T(8,128)(2,1)S(1)} %get-tuple-element.55), channel_id=1, source_target_pairs={{0,5},{1,4},{2,7},{3,6},{4,1},{5,0},{6,3},{7,2},{8,13},{9,12},{10,... | collective-permute-start | bytes 393224 | tf_op jit(solution)/shard_map/ppermute | solution.py:35
  8.6 10.8 %dynamic-slice-start = ((s32[4096]{0:T(1024)}, s32[]{:T(128)}), s32[1024]{0:T(1024)S(1)}, s32[]{:S(2)}) async-start(s32[4096]{0:T(1024)} %param.9, s32[]{:T(128)} %select_n.69), calls=%async_computation | async-start | bytes 8704 | tf_op jit(solution)/shard_map/dynamic_slice | solution.py:569
  9.0 11.5 %collective-permute-start.4 = (bf16[256,512]{1,0:T(8,128)(2,1)S(1)}, bf16[256,512]{1,0:T(8,128)(2,1)S(1)}, u32[]{:S(2)}, u32[]{:S(2)}) collective-permute-start(bf16[256,512]{1,0:T(8,128)(2,1)S(1)} %get-tuple-element.49), channel_id=1, source_target_pairs={{0,1},{1,0},{2,3},{3,2},{4,5},{5,4},{6,7},{7,6},{8,9},{9,8},{10,11... | collective-permute-start | bytes 786440 | tf_op jit(solution)/shard_map/ppermute | solution.py:35
  11.0 15.2 %collective-permute-start.5 = (bf16[256,512]{1,0:T(8,128)(2,1)S(1)}, bf16[256,512]{1,0:T(8,128)(2,1)S(1)}, u32[]{:S(2)}, u32[]{:S(2)}) collective-permute-start(bf16[256,512]{1,0:T(8,128)(2,1)S(1)} %get-tuple-element.50), channel_id=1, source_target_pairs={{0,4},{1,5},{2,6},{3,7},{4,0},{5,1},{6,2},{7,3},{8,12},{9,13},{10,... | collective-permute-start | bytes 786440 | tf_op jit(solution)/shard_map/ppermute | solution.py:35
  12.5 13.7 %collective-permute-start.6 = (bf16[256,512]{1,0:T(8,128)(2,1)S(1)}, bf16[256,512]{1,0:T(8,128)(2,1)S(1)}, u32[]{:S(2)}, u32[]{:S(2)}) collective-permute-start(bf16[256,512]{1,0:T(8,128)(2,1)S(1)} %get-tuple-element.51), channel_id=1, source_target_pairs={{0,5},{1,4},{2,7},{3,6},{4,1},{5,0},{6,3},{7,2},{8,13},{9,12},{10,... | collective-permute-start | bytes 786440 | tf_op jit(solution)/shard_map/ppermute | solution.py:35
  15.9 12.7 %collective-permute-start.10 = (bf16[1024,256]{1,0:T(8,128)(2,1)S(1)}, bf16[1024,256]{1,0:T(8,128)(2,1)S(1)}, u32[]{:S(2)}, u32[]{:S(2)}) collective-permute-start(bf16[1024,256]{1,0:T(8,128)(2,1)S(1)} %join.1.refs_6_.refs_4_), channel_id=1, source_target_pairs={{0,8},{1,9},{2,10},{3,11},{4,12},{5,13},{6,14},{7,15},{8,16},{9,17... | collective-permute-start | bytes 1572872 | tf_op jit(solution)/shard_map/ppermute | solution.py:55
  34.9 14.5 %collective-permute-start.17 = (bf16[1024,256]{1,0:T(8,128)(2,1)S(1)}, bf16[1024,256]{1,0:T(8,128)(2,1)S(1)}, u32[]{:S(2)}, u32[]{:S(2)}) collective-permute-start(bf16[1024,256]{1,0:T(8,128)(2,1)S(1)} %get-tuple-element.79), channel_id=1, source_target_pairs={{8,0},{9,1},{10,2},{11,3},{12,4},{13,5},{14,6},{15,7},{16,8},{17,9... | collective-permute-start | bytes 1572872 | tf_op jit(solution)/shard_map/ppermute | solution.py:55
  36.4 6.8 %collective-permute-start.11 = (bf16[256,256]{1,0:T(8,128)(2,1)S(1)}, bf16[256,256]{1,0:T(8,128)(2,1)S(1)}, u32[]{:S(2)}, u32[]{:S(2)}) collective-permute-start(bf16[256,256]{1,0:T(8,128)(2,1)S(1)} %get-tuple-element.59), channel_id=1, source_target_pairs={{0,1},{1,0},{2,3},{3,2},{4,5},{5,4},{6,7},{7,6},{8,9},{9,8},{10,11... | collective-permute-start | bytes 393224 | tf_op jit(solution)/shard_map/ppermute | solution.py:35
  38.2 6.9 %collective-permute-start.12 = (bf16[256,256]{1,0:T(8,128)(2,1)S(1)}, bf16[256,256]{1,0:T(8,128)(2,1)S(1)}, u32[]{:S(2)}, u32[]{:S(2)}) collective-permute-start(bf16[256,256]{1,0:T(8,128)(2,1)S(1)} %get-tuple-element.60), channel_id=1, source_target_pairs={{0,4},{1,5},{2,6},{3,7},{4,0},{5,1},{6,2},{7,3},{8,12},{9,13},{10,... | collective-permute-start | bytes 393224 | tf_op jit(solution)/shard_map/ppermute | solution.py:35
  38.7 6.4 %collective-permute-start.13 = (bf16[256,256]{1,0:T(8,128)(2,1)S(1)}, bf16[256,256]{1,0:T(8,128)(2,1)S(1)}, u32[]{:S(2)}, u32[]{:S(2)}) collective-permute-start(bf16[256,256]{1,0:T(8,128)(2,1)S(1)} %get-tuple-element.61), channel_id=1, source_target_pairs={{0,5},{1,4},{2,7},{3,6},{4,1},{5,0},{6,3},{7,2},{8,13},{9,12},{10,... | collective-permute-start | bytes 393224 | tf_op jit(solution)/shard_map/ppermute | solution.py:35
  45.1 6.8 %collective-permute-start.14 = (bf16[256,256]{1,0:T(8,128)(2,1)S(1)}, bf16[256,256]{1,0:T(8,128)(2,1)S(1)}, u32[]{:S(2)}, u32[]{:S(2)}) collective-permute-start(bf16[256,256]{1,0:T(8,128)(2,1)S(1)} %get-tuple-element.75), channel_id=1, source_target_pairs={{0,1},{1,0},{2,3},{3,2},{4,5},{5,4},{6,7},{7,6},{8,9},{9,8},{10,11... | collective-permute-start | bytes 393224 | tf_op jit(solution)/shard_map/ppermute | solution.py:35
  46.2 7.0 %collective-permute-start.15 = (bf16[256,256]{1,0:T(8,128)(2,1)S(1)}, bf16[256,256]{1,0:T(8,128)(2,1)S(1)}, u32[]{:S(2)}, u32[]{:S(2)}) collective-permute-start(bf16[256,256]{1,0:T(8,128)(2,1)S(1)} %get-tuple-element.76), channel_id=1, source_target_pairs={{0,4},{1,5},{2,6},{3,7},{4,0},{5,1},{6,2},{7,3},{8,12},{9,13},{10,... | collective-permute-start | bytes 393224 | tf_op jit(solution)/shard_map/ppermute | solution.py:35
  46.8 7.3 %collective-permute-start.16 = (bf16[256,256]{1,0:T(8,128)(2,1)S(1)}, bf16[256,256]{1,0:T(8,128)(2,1)S(1)}, u32[]{:S(2)}, u32[]{:S(2)}) collective-permute-start(bf16[256,256]{1,0:T(8,128)(2,1)S(1)} %get-tuple-element.77), channel_id=1, source_target_pairs={{0,5},{1,4},{2,7},{3,6},{4,1},{5,0},{6,3},{7,2},{8,13},{9,12},{10,... | collective-permute-start | bytes 393224 | tf_op jit(solution)/shard_map/ppermute | solution.py:35
  49.6 7.0 %collective-permute-start.18 = (bf16[256,256]{1,0:T(8,128)(2,1)S(1)}, bf16[256,256]{1,0:T(8,128)(2,1)S(1)}, u32[]{:S(2)}, u32[]{:S(2)}) collective-permute-start(bf16[256,256]{1,0:T(8,128)(2,1)S(1)} %get-tuple-element.81), channel_id=1, source_target_pairs={{0,1},{1,0},{2,3},{3,2},{4,5},{5,4},{6,7},{7,6},{8,9},{9,8},{10,11... | collective-permute-start | bytes 393224 | tf_op jit(solution)/shard_map/ppermute | solution.py:35
  51.3 7.3 %collective-permute-start.19 = (bf16[256,256]{1,0:T(8,128)(2,1)S(1)}, bf16[256,256]{1,0:T(8,128)(2,1)S(1)}, u32[]{:S(2)}, u32[]{:S(2)}) collective-permute-start(bf16[256,256]{1,0:T(8,128)(2,1)S(1)} %get-tuple-element.82), channel_id=1, source_target_pairs={{0,4},{1,5},{2,6},{3,7},{4,0},{5,1},{6,2},{7,3},{8,12},{9,13},{10,... | collective-permute-start | bytes 393224 | tf_op jit(solution)/shard_map/ppermute | solution.py:35
  51.9 6.7 %collective-permute-start.20 = (bf16[256,256]{1,0:T(8,128)(2,1)S(1)}, bf16[256,256]{1,0:T(8,128)(2,1)S(1)}, u32[]{:S(2)}, u32[]{:S(2)}) collective-permute-start(bf16[256,256]{1,0:T(8,128)(2,1)S(1)} %get-tuple-element.83), channel_id=1, source_target_pairs={{0,5},{1,4},{2,7},{3,6},{4,1},{5,0},{6,3},{7,2},{8,13},{9,12},{10,... | collective-permute-start | bytes 393224 | tf_op jit(solution)/shard_map/ppermute | solution.py:35
  58.7 2.4 %collective-permute-start.21 = (bf16[128,3072]{1,0:T(8,128)(2,1)S(1)}, bf16[128,3072]{1,0:T(8,128)(2,1)S(1)}, u32[]{:S(2)}, u32[]{:S(2)}) collective-permute-start(bf16[128,3072]{1,0:T(8,128)(2,1)S(1)} %bottom.1), channel_id=1, source_target_pairs={{0,2},{1,3},{2,0},{3,1},{4,6},{5,7},{6,4},{7,5},{8,10},{9,11},{10,... | collective-permute-start | bytes 2359304 | tf_op jit(solution)/shard_map/ppermute | solution.py:35

commit v14 on v13

--- a/solution.py
+++ b/solution.py
@@ -136,6 +136,21 @@
         piece[rows:, :] = source(place(partner(size, mask ^ core), rows))
 
 
+def take_halves(size, core, masks, source, own, give):
+    rows = own.shape[0] // len(masks)
+    for at, mask in enumerate(masks):
+        part = slice(at * rows, (at + 1) * rows)
+        own[part, :] = source(place(partner(size, mask), rows))
+        give[part, :] = source(place(partner(size, mask ^ core), rows))
+
+
+def take_gradients(size, core, masks, dk, dv, halves):
+    def source(there):
+        return jnp.concatenate([dk[there, :] * logit_scale, dv[there, :]], axis=1).astype(BF16)
+
+    take_halves(size, core, masks, source, *halves)
+
+
 def join(pieces, size):
     rows, cols = pieces[0].shape
     core, masks = core_mask(), chip_masks(size)
@@ -147,66 +162,81 @@
     return small_call(kernel, out, "join", *pieces)
 
 
-def combine(terms, size):
-    tok, cols = terms[0].shape
-    core, masks = core_mask(), chip_masks(size)
+def lay(own, got):
+    def kernel(own, got, out):
+        rows = own.shape[0]
+        out[:rows, :] = own[...]
+        out[rows:, :] = got[...]
+
+    both = jax.ShapeDtypeStruct((2 * own.shape[0], own.shape[1]), BF16)
+    return small_call(kernel, both, "lay", own, got)
+
+
+def combine(own, got, backs, size):
+    count = len(chip_masks(size))
+    half = own.shape[0]
+    rows = half // count
 
     def kernel(*refs):
-        added = refs[: len(terms)]
-
-        def source(there):
-            total = added[0][there, :]
-            for term in added[1:]:
-                total = total + term[there, :].astype(F32)
-            return total.astype(BF16)
-
-        take_rows(size, core, masks, source, refs[len(terms) :])
-
-    piece = jax.ShapeDtypeStruct((2 * (tok // size), cols), BF16)
-    return small_call(kernel, [piece] * len(masks), "combine", *terms)
+        terms, pieces = refs[2:-count], refs[-count:]
+        for side in (0, 1):
+            for at, piece in enumerate(pieces):
+                value = refs[side][at * rows : (at + 1) * rows, :].astype(F32)
+                start = side * half + at * rows
+                for term in terms:
+                    value = value + term[start : start + rows, :].astype(F32)
+                piece[side * rows : (side + 1) * rows, :] = value.astype(BF16)
+
+    piece = jax.ShapeDtypeStruct((2 * rows, own.shape[1]), BF16)
+    return small_call(kernel, [piece] * count, "combine", own, got, *backs)
 
 
 def bottom_body(*refs):
-    out, start = refs[-1], 0
-    for piece in refs[:-1]:
+    count = len(refs) // 3
+    for at, piece in enumerate(refs[: 2 * count]):
         rows, width = piece.shape[0] // 2, piece.shape[1]
-        out[:, start : start + width] = piece[rows:, :]
-        start += width
-
-
-def spread_body(size, core, masks, counts, *refs):
-    refs = list(refs)
-    take = lambda count: [refs.pop(0) for _ in range(count)]
-    sets = [take(len(masks)) for _ in counts]
-    (got,), sets_out, (sems,) = take(1), [take(count) for count in counts], take(1)
-    copies, start = [], 0
+        start = at % 2 * width
+        refs[2 * count + at // 2][:, start : start + width] = piece[rows:, :]
+
+
+def spread_body(size, core, masks, *refs):
+    take = taker(refs)
+    sets, got, sems = [take(len(masks)) for _ in range(3)], take(len(masks)), refs[-1]
+    sets_out = [refs[-5:-4], refs[-4:-3], refs[-3:-1]]
+    copies, hopped = [], 0
     for pieces, outs in zip(sets, sets_out):
         for mask, piece in zip(masks, pieces):
             rows, width = piece.shape[0] // 2, piece.shape[1] // len(outs)
             for at, out in enumerate(outs):
+                part = slice(at * width, (at + 1) * width)
+                if len(outs) == 1:
+                    start = hopped % 2 * width
+                    other = got[hopped // 2].at[:, start : start + width]
+                    hopped += 1
+                else:
+                    other = piece.at[rows:, part]
                 mine = out.at[:, place(partner(size, mask), width)]
-                other = out.at[:, place(partner(size, mask ^ core), width)]
-                copies.append((piece.at[:rows, at * width : (at + 1) * width], mine))
-                copies.append((got.at[:, start : start + width], other))
-                start += width
+                copies.append((piece.at[:rows, part], mine))
+                copies.append((other, out.at[:, place(partner(size, mask ^ core), width)]))
     run_copies(copies, sems)
 
 
-def spread_cores(sets, counts, size):
-    pieces = [piece for part in sets for piece in part]
-    rows = pieces[0].shape[0] // 2
-    give = jax.ShapeDtypeStruct((rows, sum(piece.shape[1] for piece in pieces)), BF16)
-    got = swap(small_call(bottom_body, give, "bottom", *pieces), core_mask())
-    widths = [part[0].shape[1] // count for part, count in zip(sets, counts) for _ in range(count)]
+def spread(out, grad_q, grads, size):
+    rows, width = out[0].shape[0] // 2, out[0].shape[1]
+    give = [jax.ShapeDtypeStruct((rows, 2 * width), BF16)] * len(out)
+    give = small_call(bottom_body, give, "bottom", *out, *grad_q)
+    got = [swap(part, core_mask()) for part in give]
+    widths = [width, width, grads[0].shape[1] // 2, grads[0].shape[1] // 2]
+    pieces = [*out, *grad_q, *grads]
     return pl.pallas_call(
-        functools.partial(spread_body, size, core_mask(), chip_masks(size), counts),
+        functools.partial(spread_body, size, core_mask(), chip_masks(size)),
         out_shape=[jax.ShapeDtypeStruct((rows, width * size), BF16) for width in widths],
-        in_specs=[ANY] * (len(pieces) + 1),
-        out_specs=[ANY] * len(widths),
-        scratch_shapes=[pltpu.SemaphoreType.DMA((len(widths) * size,))],
+        in_specs=[ANY] * (len(pieces) + len(got)),
+        out_specs=[ANY] * 4,
+        scratch_shapes=[pltpu.SemaphoreType.DMA((4 * size,))],
         compiler_params=SMALL,
         name="spread",
-    )(*pieces, got)
+    )(*pieces, *got)
 
 
 def dot(a, b):
@@ -350,7 +380,7 @@
     take = taker(refs)
     (seg_k, seg_q), qg_pieces, kvs = take(2), take(len(masks)), take(reach)
     out_own, stats = take(2)
-    out_pieces, sent, (outs, own_scale, dq_part) = take(len(masks)), take(reach), take(3)
+    out_pieces, sent, (outs, own_scale, dq_part) = take(len(masks)), take(2 * reach), take(3)
     qg, ka, va, kt, vt, dk, dv, s_scr, e_scr, dp_scr, ds_scr, g_scr = take(12)
     wide, tiles = group * TILE, tok // TILE
     place_rows(size, core, masks, qg_pieces, qg)
@@ -410,15 +440,15 @@
 
     for lag in range(1, reach + 1):
         there = slice((reach - lag) * tok, (reach - lag + 1) * tok)
-        sent[lag - 1][:, :HEAD_DIM] = (dk[there, :] * logit_scale).astype(BF16)
-        sent[lag - 1][:, HEAD_DIM:] = dv[there, :].astype(BF16)
+        halves = sent[2 * lag - 2 : 2 * lag]
+        take_gradients(size, core, masks, dk.at[there, :], dv.at[there, :], halves)
     take_rows(size, core, masks, lambda there: outs[there, :], out_pieces)
 
 
 def backward_body(size, core, masks, tok, group, *refs):
     take = taker(refs)
     qg_pieces, (kv, e_own, outs, own_scale, dq_part) = take(len(masks)), take(5)
-    dq_pieces, (dkv,) = take(len(masks)), take(1)
+    dq_pieces, dkv_halves = take(len(masks)), take(2)
     qg, dqs, va, kt, dk, dv, dp_scr, ds_scr, g_scr = take(9)
     wide = group * TILE
     place_rows(size, core, masks, qg_pieces, qg)
@@ -445,8 +475,7 @@
         unstacked(dqs, base, group, dq.T.astype(BF16))
 
     pipeline(tok // TILE, products, gradients)
-    dkv[:, :HEAD_DIM] = dk[...] * logit_scale
-    dkv[:, HEAD_DIM:] = dv[...]
+    take_gradients(size, core, masks, dk, dv, dkv_halves)
     take_rows(size, core, masks, lambda there: dqs[there, :], dq_pieces)
 
 
@@ -496,8 +525,8 @@
     tok, count, reach = len(qg) * rows, len(qg), len(lags)
     group = cols // (2 * HEAD_DIM)
     wide, tiles = group * TILE, tok // TILE
-    half = jax.ShapeDtypeStruct((tok, 2 * HEAD_DIM), BF16)
-    out_shape = [jax.ShapeDtypeStruct((rows, cols // 2), BF16)] * count + [half] * reach
+    half = jax.ShapeDtypeStruct((tok // 2, 2 * HEAD_DIM), BF16)
+    out_shape = [jax.ShapeDtypeStruct((rows, cols // 2), BF16)] * count + [half] * 2 * reach
     out_shape += [
         jax.ShapeDtypeStruct((tok, cols // 2), BF16),
         jax.ShapeDtypeStruct((tiles, wide), F32),
@@ -530,7 +559,8 @@
         *lags,
         *carried,
     )
-    return results[:count], results[count : count + reach], results[count + reach :]
+    sent, carried = results[count : count + 2 * reach], results[count + 2 * reach :]
+    return results[:count], sent, carried
 
 
 def backward(qg, kv, carried, size):
@@ -541,7 +571,7 @@
     results = attend_call(
         functools.partial(backward_body, size, core_mask(), chip_masks(size), tok, group),
         [jax.ShapeDtypeStruct((rows, cols // 2), BF16)] * count
-        + [jax.ShapeDtypeStruct((tok, 2 * HEAD_DIM), F32)],
+        + [jax.ShapeDtypeStruct((tok // 2, 2 * HEAD_DIM), BF16)] * 2,
         [
             pltpu.VMEM((tok, cols), BF16),
             pltpu.VMEM((tok, cols // 2), BF16),
@@ -559,7 +589,7 @@
         kv,
         *carried,
     )
-    return results[:count], results[count]
+    return results[:count], results[count:]
 
 
 def document_columns(segment_ids, tok, size):
@@ -591,14 +621,20 @@
 
     e_own, *partial = forward_own(documents, qg, kv, size)
     out, sent, carried = forward(documents, qg, lags, partial, size)
-    backs = [shifted(sent[lag - 1], -lag * size) for lag in range(1, reach + 1)]
+    laid = [
+        lay(sent[2 * lag - 2], swap(sent[2 * lag - 1], core_mask()))
+        for lag in range(1, reach + 1)
+    ]
+    backs = [shifted(rows, -lag * size) for lag, rows in enumerate(laid, 1)]
     out = swap_chips(out, size)
+    kv, *_ = after(kv, *laid)
     grad_q, dkv = backward(qg, kv, [e_own, *carried], size)
-    both = after(*out, *grad_q)
+    grad_q = swap_chips(grad_q, size)
+    give, *out = after(dkv[1], *out)
+    grads = list(combine(dkv[0], swap(give, core_mask()), backs, size))
+    grads[0], *both = after(grads[0], *out, *grad_q)
     out, grad_q = both[: len(out)], both[len(out) :]
-    grad_q = swap_chips(grad_q, size)
-    grads = swap_chips(combine([dkv, *backs], size), size)
-    return tuple(spread_cores([out, grad_q, grads], (1, 1, 2), size))
+    return tuple(spread(out, grad_q, swap_chips(grads, size), size))
 
 
 def solution(mesh):

time: 62.8 us -> 65.3 us (1.040)
  waiting for transfers between devices: 18.4 us -> 19.4 us
  starting transfers between devices: 26.6 us -> 27.4 us
    ppermute x2, waiting for transfers between devices: 0.94 us -> 1.85 us  [shifted(): return lax.ppermute(value, BOTH, pairs)]
    ppermute x20 -> x25, starting transfers between devices: 21.6 us -> 22.4 us  [swap(): lax.ppermute(value, BOTH, [(i, i ^ mask) for i in range(device_count())])]
    ppermute x20 -> x25, waiting for transfers between devices: 17.4 us -> 17.6 us  [swap(): lax.ppermute(value, BOTH, [(i, i ^ mask) for i in range(device_count())])]
  transfers between devices with their start and end apart: 22 -> 27, of which waited for: 11 -> 13; matrix products, arithmetic and copies ran while one was open for 4% -> 4% of each run, Pallas kernels for 10% -> 10%
where the time goes in v14:
time: 65.3 us; the launch traced here: 64.6 us
  starting transfers between devices  27.4 us (42%)
  waiting for transfers between devices  19.4 us (30%)
  Pallas kernels  13.9 us (21%)
  local copies, waits for them, and re-layouts  2.03 us (3%)
  between operations  1.12 us (2%)
  other arithmetic  0.74 us (1%)
    ppermute x25, starting transfers between devices, swap(): lax.ppermute(value, BOTH, [(i, i ^ mask) for i in range(device_count())])  22.4 us
    ppermute x25, waiting for transfers between devices, swap(): lax.ppermute(value, BOTH, [(i, i ^ mask) for i in range(device_count())])  17.6 us
    pallas_call x3, Pallas kernels, attend_call(): pl.pallas_call(kernel, out_shape=out_shape, in_specs=[VMEM] * len(args),...  12 us
    ppermute x2, starting transfers between devices, shifted(): return lax.ppermute(value, BOTH, pairs)  4.99 us
    slice x4, local copies, waits for them, and re-layouts, this_core(): shares = [array[:, r * width:(r + 1) * width] for r in range(size)]  1.99 us
    ppermute x2, waiting for transfers between devices, shifted(): return lax.ppermute(value, BOTH, pairs)  1.85 us
    pallas_call x1, Pallas kernels, spread(): pl.pallas_call(functools.partial(spread_body, size, core_mask(), chip_mas...  1.42 us
  transfers between devices with their start and end apart: 27, of which 13 were waited for; matrix products, arithmetic and copies ran while one was open for 4% of the time, Pallas kernels for 10%

profile of v14, /device:TPU:0, one launch (start us, length us, event | category | flops | bytes accessed | tf_op | source)
XLA Modules:
  0.0 64.6 jit_solution(17724285683705443856)
XLA Ops:
  0.7 0.5 collective-permute-start
  1.8 1.0 %fusion.3 = (bf16[128,256]{1,0:T(8,128)(2,1)S(1)}, bf16[128,256]{1,0:T(8,128)(2,1)S(1)}, bf16[128,256]{1,0:T(8,128)(2,1)S(1)}, bf16[128,256]{1,0:T(8,128)(2,1)S(1)}) fusion(bf16[128,1024]{1,0:T(8,128)(2,1)} %param.6), kind=kLoop, calls=%fused_computation.12 | loop fusion | bytes 524288 | tf_op jit(solution)/shard_map/slice | solution.py:94
  2.7 1.0 %fusion.2 = (bf16[128,256]{1,0:T(8,128)(2,1)S(1)}, bf16[128,256]{1,0:T(8,128)(2,1)S(1)}, bf16[128,256]{1,0:T(8,128)(2,1)S(1)}, bf16[128,256]{1,0:T(8,128)(2,1)S(1)}) fusion(bf16[128,1024]{1,0:T(8,128)(2,1)} %param.7), kind=kLoop, calls=%fused_computation.11 | loop fusion | bytes 524288 | tf_op jit(solution)/shard_map/slice | solution.py:94
  4.0 3.0 %collective-permute-start.7 = (bf16[256,256]{1,0:T(8,128)(2,1)S(1)}, bf16[256,256]{1,0:T(8,128)(2,1)S(1)}, u32[]{:S(2)}, u32[]{:S(2)}) collective-permute-start(bf16[256,256]{1,0:T(8,128)(2,1)S(1)} %get-tuple-element.65), channel_id=1, source_target_pairs={{0,1},{1,0},{2,3},{3,2},{4,5},{5,4},{6,7},{7,6},{8,9},{9,8},{10,11... | collective-permute-start | bytes 393224 | tf_op jit(solution)/shard_map/ppermute | solution.py:35
  7.0 1.5 %collective-permute-start.8 = (bf16[256,256]{1,0:T(8,128)(2,1)S(1)}, bf16[256,256]{1,0:T(8,128)(2,1)S(1)}, u32[]{:S(2)}, u32[]{:S(2)}) collective-permute-start(bf16[256,256]{1,0:T(8,128)(2,1)S(1)} %get-tuple-element.66), channel_id=1, source_target_pairs={{0,4},{1,5},{2,6},{3,7},{4,0},{5,1},{6,2},{7,3},{8,12},{9,13},{10,... | collective-permute-start | bytes 393224 | tf_op jit(solution)/shard_map/ppermute | solution.py:35
  9.0 2.0 %collective-permute-start.4 = (bf16[256,512]{1,0:T(8,128)(2,1)S(1)}, bf16[256,512]{1,0:T(8,128)(2,1)S(1)}, u32[]{:S(2)}, u32[]{:S(2)}) collective-permute-start(bf16[256,512]{1,0:T(8,128)(2,1)S(1)} %get-tuple-element.61), channel_id=1, source_target_pairs={{0,1},{1,0},{2,3},{3,2},{4,5},{5,4},{6,7},{7,6},{8,9},{9,8},{10,11... | collective-permute-start | bytes 786440 | tf_op jit(solution)/shard_map/ppermute | solution.py:35
  11.0 1.5 %collective-permute-start.5 = (bf16[256,512]{1,0:T(8,128)(2,1)S(1)}, bf16[256,512]{1,0:T(8,128)(2,1)S(1)}, u32[]{:S(2)}, u32[]{:S(2)}) collective-permute-start(bf16[256,512]{1,0:T(8,128)(2,1)S(1)} %get-tuple-element.62), channel_id=1, source_target_pairs={{0,4},{1,5},{2,6},{3,7},{4,0},{5,1},{6,2},{7,3},{8,12},{9,13},{10,... | collective-permute-start | bytes 786440 | tf_op jit(solution)/shard_map/ppermute | solution.py:35
  12.5 1.7 %collective-permute-start.6 = (bf16[256,512]{1,0:T(8,128)(2,1)S(1)}, bf16[256,512]{1,0:T(8,128)(2,1)S(1)}, u32[]{:S(2)}, u32[]{:S(2)}) collective-permute-start(bf16[256,512]{1,0:T(8,128)(2,1)S(1)} %get-tuple-element.63), channel_id=1, source_target_pairs={{0,5},{1,4},{2,7},{3,6},{4,1},{5,0},{6,3},{7,2},{8,13},{9,12},{10,... | collective-permute-start | bytes 786440 | tf_op jit(solution)/shard_map/ppermute | solution.py:35
  14.6 0.6 collective-permute-done.8.refs_2_
  15.2 0.7 %collective-permute-done.9.refs_3_ = bf16[256,256]{1,0:T(8,128)(2,1)S(1)} collective-permute-done((bf16[256,256]{1,0:T(8,128)(2,1)S(1)}, bf16[256,256]{1,0:T(8,128)(2,1)S(1)}, u32[]{:S(2)}, u32[]{:S(2)}) %collective-permute-start.9) | collective-permute-done | bytes 131104 | tf_op jit(solution)/shard_map/ppermute | solution.py:35
  15.9 3.5 %collective-permute-start.10 = (bf16[1024,256]{1,0:T(8,128)(2,1)S(1)}, bf16[1024,256]{1,0:T(8,128)(2,1)S(1)}, u32[]{:S(2)}, u32[]{:S(2)}) collective-permute-start(bf16[1024,256]{1,0:T(8,128)(2,1)S(1)} %join.1.refs_6_.refs_4_), channel_id=1, source_target_pairs={{0,8},{1,9},{2,10},{3,11},{4,12},{5,13},{6,14},{7,15},{8,16},{9,17... | collective-permute-start | bytes 1572872 | tf_op jit(solution)/shard_map/ppermute | solution.py:55
  19.7 0.8 %collective-permute-done.4.refs_3_.refs_1_ = bf16[256,512]{1,0:T(8,128)(2,1)S(1)} collective-permute-done((bf16[256,512]{1,0:T(8,128)(2,1)S(1)}, bf16[256,512]{1,0:T(8,128)(2,1)S(1)}, u32[]{:S(2)}, u32[]{:S(2)}) %collective-permute-start.4) | collective-permute-done | bytes 262176 | tf_op jit(solution)/shard_map/ppermute | solution.py:35
  20.5 5.7 %collective-permute-done.5.refs_4_.refs_2_ = bf16[256,512]{1,0:T(8,128)(2,1)S(1)} collective-permute-done((bf16[256,512]{1,0:T(8,128)(2,1)S(1)}, bf16[256,512]{1,0:T(8,128)(2,1)S(1)}, u32[]{:S(2)}, u32[]{:S(2)}) %collective-permute-start.5) | collective-permute-done | bytes 262176 | tf_op jit(solution)/shard_map/ppermute | solution.py:35
  26.2 2.4 %forward_own.1 = (bf16[4608,256]{1,0:T(8,128)(2,1)S(1)}, f32[128,2048]{1,0:T(8,128)S(1)}, f32[16,256]{1,0:T(8,128)S(1)}) custom-call(bf16[2048,128]{1,0:T(8,128)(2,1)S(1)} %select_convert_fusion.refs_0_, bf16[1024,128]{1,0:T(8,128)(2,1)S(1)} %select_convert_fusion.1.refs_1_, bf16[256,512]{1,0:T(8,128)(2,1)S(1)} %get-tuple-element.60.refs_2_.refs_0_, ...), custom_call_target="tpu_custom_call" | custom-call | flops 4831838208 | bytes 8388608 | tf_op jit(solution)/shard_map/forward_own/pallas_call | solution.py:483
  28.7 6.3 %forward.1 = (bf16[256,256]{1,0:T(8,128)(2,1)S(1)}, bf16[256,256]{1,0:T(8,128)(2,1)S(1)}, bf16[256,256]{1,0:T(8,128)(2,1)S(1)}, bf16[256,256]{1,0:T(8,128)(2,1)S...) custom-call(bf16[2048,128]{1,0:T(8,128)(2,1)S(1)} %select_convert_fu, ...), custom_call_target="tpu_custom_call" | custom-call | flops 1811939328 | bytes 8388608 | tf_op jit(solution)/shard_map/forward/pallas_call | solution.py:483
  35.1 1.5 %collective-permute-done.11.got = bf16[512,256]{1,0:T(8,128)(2,1)S(1)} collective-permute-done((bf16[512,256]{1,0:T(8,128)(2,1)S(1)}, bf16[512,256]{1,0:T(8,128)(2,1)S(1)}, u32[]{:S(2)}, u32[]{:S(2)}) %collective-permute-start.11) | collective-permute-done | bytes 262176 | tf_op jit(solution)/shard_map/ppermute | solution.py:35
  36.6 1.5 %collective-permute-start.16 = (bf16[1024,256]{1,0:T(8,128)(2,1)S(1)}, bf16[1024,256]{1,0:T(8,128)(2,1)S(1)}, u32[]{:S(2)}, u32[]{:S(2)}) collective-permute-start(bf16[1024,256]{1,0:T(8,128)(2,1)S(1)} %lay.1), channel_id=1, source_target_pairs={{8,0},{9,1},{10,2},{11,3},{12,4},{13,5},{14,6},{15,7},{16,8},{17,9... | collective-permute-start | bytes 1572872 | tf_op jit(solution)/shard_map/ppermute | solution.py:55
  38.1 1.8 %collective-permute-start.12 = (bf16[256,256]{1,0:T(8,128)(2,1)S(1)}, bf16[256,256]{1,0:T(8,128)(2,1)S(1)}, u32[]{:S(2)}, u32[]{:S(2)}) collective-permute-start(bf16[256,256]{1,0:T(8,128)(2,1)S(1)} %get-tuple-element.81), channel_id=1, source_target_pairs={{0,1},{1,0},{2,3},{3,2},{4,5},{5,4},{6,7},{7,6},{8,9},{9,8},{10,11... | collective-permute-start | bytes 393224 | tf_op jit(solution)/shard_map/ppermute | solution.py:35
  40.4 1.3 %collective-permute-start.14 = (bf16[256,256]{1,0:T(8,128)(2,1)S(1)}, bf16[256,256]{1,0:T(8,128)(2,1)S(1)}, u32[]{:S(2)}, u32[]{:S(2)}) collective-permute-start(bf16[256,256]{1,0:T(8,128)(2,1)S(1)} %get-tuple-element.83), channel_id=1, source_target_pairs={{0,5},{1,4},{2,7},{3,6},{4,1},{5,0},{6,3},{7,2},{8,13},{9,12},{10,... | collective-permute-start | bytes 393224 | tf_op jit(solution)/shard_map/ppermute | solution.py:35
  41.7 3.3 %backward.1 = (bf16[256,256]{1,0:T(8,128)(2,1)S(1)}, bf16[256,256]{1,0:T(8,128)(2,1)S(1)}, bf16[256,256]{1,0:T(8,128)(2,1)S(1)}, bf16[256,256]{1,0:T(8,128)(2,1)...) custom-call(bf16[256,512]{1,0:T(8,128)(2,1)S(1)} %get-tuple-element.60.refs_2_.refs_0_, ...), custom_call_target="tpu_custom_call" | custom-call | flops 1207959552 | bytes 8388608 | tf_op jit(solution)/shard_map/backward/pallas_call | solution.py:483
  45.0 3.0 %collective-permute-done.13.refs_2_ = bf16[256,256]{1,0:T(8,128)(2,1)S(1)} collective-permute-done((bf16[256,256]{1,0:T(8,128)(2,1)S(1)}, bf16[256,256]{1,0:T(8,128)(2,1)S(1)}, u32[]{:S(2)}, u32[]{:S(2)}) %collective-permute-start.13) | collective-permute-done | bytes 131104 | tf_op jit(solution)/shard_map/ppermute | solution.py:35
  48.3 1.4 %collective-permute-start.18 = (bf16[256,256]{1,0:T(8,128)(2,1)S(1)}, bf16[256,256]{1,0:T(8,128)(2,1)S(1)}, u32[]{:S(2)}, u32[]{:S(2)}) collective-permute-start(bf16[256,256]{1,0:T(8,128)(2,1)S(1)} %get-tuple-element.92), channel_id=1, source_target_pairs={{0,4},{1,5},{2,6},{3,7},{4,0},{5,1},{6,2},{7,3},{8,12},{9,13},{10,... | collective-permute-start | bytes 393224 | tf_op jit(solution)/shard_map/ppermute | solution.py:35
  49.7 1.7 %collective-permute-start.19 = (bf16[256,256]{1,0:T(8,128)(2,1)S(1)}, bf16[256,256]{1,0:T(8,128)(2,1)S(1)}, u32[]{:S(2)}, u32[]{:S(2)}) collective-permute-start(bf16[256,256]{1,0:T(8,128)(2,1)S(1)} %get-tuple-element.93), channel_id=1, source_target_pairs={{0,5},{1,4},{2,7},{3,6},{4,1},{5,0},{6,3},{7,2},{8,13},{9,12},{10,... | collective-permute-start | bytes 393224 | tf_op jit(solution)/shard_map/ppermute | solution.py:35
  51.5 1.8 %collective-permute-done.16.refs_2_ = bf16[1024,256]{1,0:T(8,128)(2,1)S(1)} collective-permute-done((bf16[1024,256]{1,0:T(8,128)(2,1)S(1)}, bf16[1024,256]{1,0:T(8,128)(2,1)S(1)}, u32[]{:S(2)}, u32[]{:S(2)}) %collective-permute-start.16) | collective-permute-done | bytes 524320 | tf_op jit(solution)/shard_map/ppermute | solution.py:55
  53.4 1.8 %collective-permute-start.20 = (bf16[256,256]{1,0:T(8,128)(2,1)S(1)}, bf16[256,256]{1,0:T(8,128)(2,1)S(1)}, u32[]{:S(2)}, u32[]{:S(2)}) collective-permute-start(bf16[256,256]{1,0:T(8,128)(2,1)S(1)} %get-tuple-element.103), channel_id=1, source_target_pairs={{0,1},{1,0},{2,3},{3,2},{4,5},{5,4},{6,7},{7,6},{8,9},{9,8},{10,11... | collective-permute-start | bytes 393224 | tf_op jit(solution)/shard_map/ppermute | solution.py:35
  55.1 0.5 collective-permute-start.21
  55.7 0.7 %collective-permute-done.18.refs_6_ = bf16[256,256]{1,0:T(8,128)(2,1)S(1)} collective-permute-done((bf16[256,256]{1,0:T(8,128)(2,1)S(1)}, bf16[256,256]{1,0:T(8,128)(2,1)S(1)}, u32[]{:S(2)}, u32[]{:S(2)}) %collective-permute-start.18) | collective-permute-done | bytes 131104 | tf_op jit(solution)/shard_map/ppermute | solution.py:35
  56.4 0.7 %collective-permute-done.19.refs_7_ = bf16[256,256]{1,0:T(8,128)(2,1)S(1)} collective-permute-done((bf16[256,256]{1,0:T(8,128)(2,1)S(1)}, bf16[256,256]{1,0:T(8,128)(2,1)S(1)}, u32[]{:S(2)}, u32[]{:S(2)}) %collective-permute-start.19) | collective-permute-done | bytes 131104 | tf_op jit(solution)/shard_map/ppermute | solution.py:35
  57.1 1.5 %collective-permute-start.22 = (bf16[256,256]{1,0:T(8,128)(2,1)S(1)}, bf16[256,256]{1,0:T(8,128)(2,1)S(1)}, u32[]{:S(2)}, u32[]{:S(2)}) collective-permute-start(bf16[256,256]{1,0:T(8,128)(2,1)S(1)} %get-tuple-element.105), channel_id=1, source_target_pairs={{0,5},{1,4},{2,7},{3,6},{4,1},{5,0},{6,3},{7,2},{8,13},{9,12},{10,... | collective-permute-start | bytes 393224 | tf_op jit(solution)/shard_map/ppermute | solution.py:35
  59.5 2.0 %collective-permute-done.21.refs_10_ = bf16[256,256]{1,0:T(8,128)(2,1)S(1)} collective-permute-done((bf16[256,256]{1,0:T(8,128)(2,1)S(1)}, bf16[256,256]{1,0:T(8,128)(2,1)S(1)}, u32[]{:S(2)}, u32[]{:S(2)}) %collective-permute-start.21) | collective-permute-done | bytes 131104 | tf_op jit(solution)/shard_map/ppermute | solution.py:35
  61.5 1.5 %collective-permute-done.22.refs_11_ = bf16[256,256]{1,0:T(8,128)(2,1)S(1)} collective-permute-done((bf16[256,256]{1,0:T(8,128)(2,1)S(1)}, bf16[256,256]{1,0:T(8,128)(2,1)S(1)}, u32[]{:S(2)}, u32[]{:S(2)}) %collective-permute-start.22) | collective-permute-done | bytes 131104 | tf_op jit(solution)/shard_map/ppermute | solution.py:35
  63.0 1.4 %spread.1 = (bf16[128,2048]{1,0:T(8,128)(2,1)}, bf16[128,2048]{1,0:T(8,128)(2,1)}, bf16[128,1024]{1,0:T(8,128)(2,1)}, bf16[128,1024]{1,0:T(8,128)(2,1)}) custom-call(bf16[256,256]{1,0:T(8,128)(2,1)S(1)} %get-tuple-element.94.refs_0_, bf16[256,256]{1,0:T(8,128)(2,1)S(1)} %collective-permute-done.12.refs_1_, ...), custom_call_target="tpu_custom_call" | custom-call | tf_op jit(solution)/shard_map/spread/pallas_call | solution.py:231
  (50 shorter events, 3.9 us)
Async XLA Ops:
  0.6 7.9 %copy-start = (bf16[128,2048]{1,0:T(8,128)(2,1)S(1)}, bf16[128,2048]{1,0:T(8,128)(2,1)}, u32[]{:S(2)}) copy-start(bf16[128,2048]{1,0:T(8,128)(2,1)} %param.5) | copy-start | bytes 1572868
  0.6 7.9 %copy-start.1 = (bf16[128,2048]{1,0:T(8,128)(2,1)S(1)}, bf16[128,2048]{1,0:T(8,128)(2,1)}, u32[]{:S(2)}) copy-start(bf16[128,2048]{1,0:T(8,128)(2,1)} %param.8) | copy-start | bytes 1572868
  0.7 8.0 %copy-start.2 = (s32[4096]{0:T(1024)S(1)}, s32[4096]{0:T(1024)}, u32[]{:S(2)}) copy-start(s32[4096]{0:T(1024)} %param.9) | copy-start | bytes 49156
  0.7 3.2 %collective-permute-start = (bf16[128,1024]{1,0:T(8,128)(2,1)}, bf16[128,1024]{1,0:T(8,128)(2,1)S(1)}, u32[]{:S(2)}, u32[]{:S(2)}) collective-permute-start(bf16[128,1024]{1,0:T(8,128)(2,1)} %param.6), channel_id=1, source_target_pairs={{0,2},{1,3},{2,0},{3,1},{4,6},{5,7},{6,4},{7,5},{8,10},{9,11},{10,... | collective-permute-start | bytes 786440 | tf_op jit(solution)/shard_map/ppermute | solution.py:35
  1.2 2.7 %collective-permute-start.1 = (bf16[128,1024]{1,0:T(8,128)(2,1)}, bf16[128,1024]{1,0:T(8,128)(2,1)S(1)}, u32[]{:S(2)}, u32[]{:S(2)}) collective-permute-start(bf16[128,1024]{1,0:T(8,128)(2,1)} %param.7), channel_id=1, source_target_pairs={{0,2},{1,3},{2,0},{3,1},{4,6},{5,7},{6,4},{7,5},{8,10},{9,11},{10,... | collective-permute-start | bytes 786440 | tf_op jit(solution)/shard_map/ppermute | solution.py:35
  1.3 7.5 %collective-permute-start.2 = (bf16[128,2048]{1,0:T(8,128)(2,1)}, bf16[128,2048]{1,0:T(8,128)(2,1)S(1)}, u32[]{:S(2)}, u32[]{:S(2)}) collective-permute-start(bf16[128,2048]{1,0:T(8,128)(2,1)} %param.5), channel_id=1, source_target_pairs={{0,2},{1,3},{2,0},{3,1},{4,6},{5,7},{6,4},{7,5},{8,10},{9,11},{10,... | collective-permute-start | bytes 1572872 | tf_op jit(solution)/shard_map/ppermute | solution.py:35
  1.7 7.1 %collective-permute-start.3 = (bf16[128,2048]{1,0:T(8,128)(2,1)}, bf16[128,2048]{1,0:T(8,128)(2,1)S(1)}, u32[]{:S(2)}, u32[]{:S(2)}) collective-permute-start(bf16[128,2048]{1,0:T(8,128)(2,1)} %param.8), channel_id=1, source_target_pairs={{0,2},{1,3},{2,0},{3,1},{4,6},{5,7},{6,4},{7,5},{8,10},{9,11},{10,... | collective-permute-start | bytes 1572872 | tf_op jit(solution)/shard_map/ppermute | solution.py:35
  4.0 8.5 %collective-permute-start.7 = (bf16[256,256]{1,0:T(8,128)(2,1)S(1)}, bf16[256,256]{1,0:T(8,128)(2,1)S(1)}, u32[]{:S(2)}, u32[]{:S(2)}) collective-permute-start(bf16[256,256]{1,0:T(8,128)(2,1)S(1)} %get-tuple-element.65), channel_id=1, source_target_pairs={{0,1},{1,0},{2,3},{3,2},{4,5},{5,4},{6,7},{7,6},{8,9},{9,8},{10,11... | collective-permute-start | bytes 393224 | tf_op jit(solution)/shard_map/ppermute | solution.py:35
  7.0 8.2 %collective-permute-start.8 = (bf16[256,256]{1,0:T(8,128)(2,1)S(1)}, bf16[256,256]{1,0:T(8,128)(2,1)S(1)}, u32[]{:S(2)}, u32[]{:S(2)}) collective-permute-start(bf16[256,256]{1,0:T(8,128)(2,1)S(1)} %get-tuple-element.66), channel_id=1, source_target_pairs={{0,4},{1,5},{2,6},{3,7},{4,0},{5,1},{6,2},{7,3},{8,12},{9,13},{10,... | collective-permute-start | bytes 393224 | tf_op jit(solution)/shard_map/ppermute | solution.py:35
  8.5 7.4 %collective-permute-start.9 = (bf16[256,256]{1,0:T(8,128)(2,1)S(1)}, bf16[256,256]{1,0:T(8,128)(2,1)S(1)}, u32[]{:S(2)}, u32[]{:S(2)}) collective-permute-start(bf16[256,256]{1,0:T(8,128)(2,1)S(1)} %get-tuple-element.67), channel_id=1, source_target_pairs={{0,5},{1,4},{2,7},{3,6},{4,1},{5,0},{6,3},{7,2},{8,13},{9,12},{10,... | collective-permute-start | bytes 393224 | tf_op jit(solution)/shard_map/ppermute | solution.py:35
  8.6 10.8 %dynamic-slice-start = ((s32[4096]{0:T(1024)}, s32[]{:T(128)}), s32[1024]{0:T(1024)S(1)}, s32[]{:S(2)}) async-start(s32[4096]{0:T(1024)} %param.9, s32[]{:T(128)} %select_n.72), calls=%async_computation | async-start | bytes 8704 | tf_op jit(solution)/shard_map/dynamic_slice | solution.py:599
  9.0 11.5 %collective-permute-start.4 = (bf16[256,512]{1,0:T(8,128)(2,1)S(1)}, bf16[256,512]{1,0:T(8,128)(2,1)S(1)}, u32[]{:S(2)}, u32[]{:S(2)}) collective-permute-start(bf16[256,512]{1,0:T(8,128)(2,1)S(1)} %get-tuple-element.61), channel_id=1, source_target_pairs={{0,1},{1,0},{2,3},{3,2},{4,5},{5,4},{6,7},{7,6},{8,9},{9,8},{10,11... | collective-permute-start | bytes 786440 | tf_op jit(solution)/shard_map/ppermute | solution.py:35
  11.0 15.2 %collective-permute-start.5 = (bf16[256,512]{1,0:T(8,128)(2,1)S(1)}, bf16[256,512]{1,0:T(8,128)(2,1)S(1)}, u32[]{:S(2)}, u32[]{:S(2)}) collective-permute-start(bf16[256,512]{1,0:T(8,128)(2,1)S(1)} %get-tuple-element.62), channel_id=1, source_target_pairs={{0,4},{1,5},{2,6},{3,7},{4,0},{5,1},{6,2},{7,3},{8,12},{9,13},{10,... | collective-permute-start | bytes 786440 | tf_op jit(solution)/shard_map/ppermute | solution.py:35
  12.5 13.7 %collective-permute-start.6 = (bf16[256,512]{1,0:T(8,128)(2,1)S(1)}, bf16[256,512]{1,0:T(8,128)(2,1)S(1)}, u32[]{:S(2)}, u32[]{:S(2)}) collective-permute-start(bf16[256,512]{1,0:T(8,128)(2,1)S(1)} %get-tuple-element.63), channel_id=1, source_target_pairs={{0,5},{1,4},{2,7},{3,6},{4,1},{5,0},{6,3},{7,2},{8,13},{9,12},{10,... | collective-permute-start | bytes 786440 | tf_op jit(solution)/shard_map/ppermute | solution.py:35
  15.9 12.7 %collective-permute-start.10 = (bf16[1024,256]{1,0:T(8,128)(2,1)S(1)}, bf16[1024,256]{1,0:T(8,128)(2,1)S(1)}, u32[]{:S(2)}, u32[]{:S(2)}) collective-permute-start(bf16[1024,256]{1,0:T(8,128)(2,1)S(1)} %join.1.refs_6_.refs_4_), channel_id=1, source_target_pairs={{0,8},{1,9},{2,10},{3,11},{4,12},{5,13},{6,14},{7,15},{8,16},{9,17... | collective-permute-start | bytes 1572872 | tf_op jit(solution)/shard_map/ppermute | solution.py:55
  35.0 1.6 %collective-permute-start.11 = (bf16[512,256]{1,0:T(8,128)(2,1)S(1)}, bf16[512,256]{1,0:T(8,128)(2,1)S(1)}, u32[]{:S(2)}, u32[]{:S(2)}) collective-permute-start(bf16[512,256]{1,0:T(8,128)(2,1)S(1)} %get-tuple-element.72), channel_id=1, source_target_pairs={{0,2},{1,3},{2,0},{3,1},{4,6},{5,7},{6,4},{7,5},{8,10},{9,11},{10,... | collective-permute-start | bytes 786440 | tf_op jit(solution)/shard_map/ppermute | solution.py:35
  36.6 16.6 %collective-permute-start.16 = (bf16[1024,256]{1,0:T(8,128)(2,1)S(1)}, bf16[1024,256]{1,0:T(8,128)(2,1)S(1)}, u32[]{:S(2)}, u32[]{:S(2)}) collective-permute-start(bf16[1024,256]{1,0:T(8,128)(2,1)S(1)} %lay.1), channel_id=1, source_target_pairs={{8,0},{9,1},{10,2},{11,3},{12,4},{13,5},{14,6},{15,7},{16,8},{17,9... | collective-permute-start | bytes 1572872 | tf_op jit(solution)/shard_map/ppermute | solution.py:55
  38.1 6.9 %collective-permute-start.12 = (bf16[256,256]{1,0:T(8,128)(2,1)S(1)}, bf16[256,256]{1,0:T(8,128)(2,1)S(1)}, u32[]{:S(2)}, u32[]{:S(2)}) collective-permute-start(bf16[256,256]{1,0:T(8,128)(2,1)S(1)} %get-tuple-element.81), channel_id=1, source_target_pairs={{0,1},{1,0},{2,3},{3,2},{4,5},{5,4},{6,7},{7,6},{8,9},{9,8},{10,11... | collective-permute-start | bytes 393224 | tf_op jit(solution)/shard_map/ppermute | solution.py:35
  39.9 8.1 %collective-permute-start.13 = (bf16[256,256]{1,0:T(8,128)(2,1)S(1)}, bf16[256,256]{1,0:T(8,128)(2,1)S(1)}, u32[]{:S(2)}, u32[]{:S(2)}) collective-permute-start(bf16[256,256]{1,0:T(8,128)(2,1)S(1)} %get-tuple-element.82), channel_id=1, source_target_pairs={{0,4},{1,5},{2,6},{3,7},{4,0},{5,1},{6,2},{7,3},{8,12},{9,13},{10,... | collective-permute-start | bytes 393224 | tf_op jit(solution)/shard_map/ppermute | solution.py:35
  40.4 7.6 %collective-permute-start.14 = (bf16[256,256]{1,0:T(8,128)(2,1)S(1)}, bf16[256,256]{1,0:T(8,128)(2,1)S(1)}, u32[]{:S(2)}, u32[]{:S(2)}) collective-permute-start(bf16[256,256]{1,0:T(8,128)(2,1)S(1)} %get-tuple-element.83), channel_id=1, source_target_pairs={{0,5},{1,4},{2,7},{3,6},{4,1},{5,0},{6,3},{7,2},{8,13},{9,12},{10,... | collective-permute-start | bytes 393224 | tf_op jit(solution)/shard_map/ppermute | solution.py:35
  48.0 3.5 %collective-permute-start.15 = (bf16[512,256]{1,0:T(8,128)(2,1)S(1)}, bf16[512,256]{1,0:T(8,128)(2,1)S(1)}, u32[]{:S(2)}, u32[]{:S(2)}) collective-permute-start(bf16[512,256]{1,0:T(8,128)(2,1)S(1)} %get-tuple-element.84), channel_id=1, source_target_pairs={{0,2},{1,3},{2,0},{3,1},{4,6},{5,7},{6,4},{7,5},{8,10},{9,11},{10,... | collective-permute-start | bytes 786440 | tf_op jit(solution)/shard_map/ppermute | solution.py:35
  48.0 7.7 %collective-permute-start.17 = (bf16[256,256]{1,0:T(8,128)(2,1)S(1)}, bf16[256,256]{1,0:T(8,128)(2,1)S(1)}, u32[]{:S(2)}, u32[]{:S(2)}) collective-permute-start(bf16[256,256]{1,0:T(8,128)(2,1)S(1)} %get-tuple-element.91), channel_id=1, source_target_pairs={{0,1},{1,0},{2,3},{3,2},{4,5},{5,4},{6,7},{7,6},{8,9},{9,8},{10,11... | collective-permute-start | bytes 393224 | tf_op jit(solution)/shard_map/ppermute | solution.py:35
  48.3 8.1 %collective-permute-start.18 = (bf16[256,256]{1,0:T(8,128)(2,1)S(1)}, bf16[256,256]{1,0:T(8,128)(2,1)S(1)}, u32[]{:S(2)}, u32[]{:S(2)}) collective-permute-start(bf16[256,256]{1,0:T(8,128)(2,1)S(1)} %get-tuple-element.92), channel_id=1, source_target_pairs={{0,4},{1,5},{2,6},{3,7},{4,0},{5,1},{6,2},{7,3},{8,12},{9,13},{10,... | collective-permute-start | bytes 393224 | tf_op jit(solution)/shard_map/ppermute | solution.py:35
  49.7 7.4 %collective-permute-start.19 = (bf16[256,256]{1,0:T(8,128)(2,1)S(1)}, bf16[256,256]{1,0:T(8,128)(2,1)S(1)}, u32[]{:S(2)}, u32[]{:S(2)}) collective-permute-start(bf16[256,256]{1,0:T(8,128)(2,1)S(1)} %get-tuple-element.93), channel_id=1, source_target_pairs={{0,5},{1,4},{2,7},{3,6},{4,1},{5,0},{6,3},{7,2},{8,13},{9,12},{10,... | collective-permute-start | bytes 393224 | tf_op jit(solution)/shard_map/ppermute | solution.py:35
  53.4 6.1 %collective-permute-start.20 = (bf16[256,256]{1,0:T(8,128)(2,1)S(1)}, bf16[256,256]{1,0:T(8,128)(2,1)S(1)}, u32[]{:S(2)}, u32[]{:S(2)}) collective-permute-start(bf16[256,256]{1,0:T(8,128)(2,1)S(1)} %get-tuple-element.103), channel_id=1, source_target_pairs={{0,1},{1,0},{2,3},{3,2},{4,5},{5,4},{6,7},{7,6},{8,9},{9,8},{10,11... | collective-permute-start | bytes 393224 | tf_op jit(solution)/shard_map/ppermute | solution.py:35
  55.1 6.4 %collective-permute-start.21 = (bf16[256,256]{1,0:T(8,128)(2,1)S(1)}, bf16[256,256]{1,0:T(8,128)(2,1)S(1)}, u32[]{:S(2)}, u32[]{:S(2)}) collective-permute-start(bf16[256,256]{1,0:T(8,128)(2,1)S(1)} %get-tuple-element.104), channel_id=1, source_target_pairs={{0,4},{1,5},{2,6},{3,7},{4,0},{5,1},{6,2},{7,3},{8,12},{9,13},{10,... | collective-permute-start | bytes 393224 | tf_op jit(solution)/shard_map/ppermute | solution.py:35
  57.1 5.9 %collective-permute-start.22 = (bf16[256,256]{1,0:T(8,128)(2,1)S(1)}, bf16[256,256]{1,0:T(8,128)(2,1)S(1)}, u32[]{:S(2)}, u32[]{:S(2)}) collective-permute-start(bf16[256,256]{1,0:T(8,128)(2,1)S(1)} %get-tuple-element.105), channel_id=1, source_target_pairs={{0,5},{1,4},{2,7},{3,6},{4,1},{5,0},{6,3},{7,2},{8,13},{9,12},{10,... | collective-permute-start | bytes 393224 | tf_op jit(solution)/shard_map/ppermute | solution.py:35
  58.7 4.3 %collective-permute-start.23 = (bf16[128,512]{1,0:T(8,128)(2,1)S(1)}, bf16[128,512]{1,0:T(8,128)(2,1)S(1)}, u32[]{:S(2)}, u32[]{:S(2)}) collective-permute-start(bf16[128,512]{1,0:T(8,128)(2,1)S(1)} %get-tuple-element.106), channel_id=1, source_target_pairs={{0,2},{1,3},{2,0},{3,1},{4,6},{5,7},{6,4},{7,5},{8,10},{9,11},{10,... | collective-permute-start | bytes 393224 | tf_op jit(solution)/shard_map/ppermute | solution.py:35
  58.8 4.2 %collective-permute-start.24 = (bf16[128,512]{1,0:T(8,128)(2,1)S(1)}, bf16[128,512]{1,0:T(8,128)(2,1)S(1)}, u32[]{:S(2)}, u32[]{:S(2)}) collective-permute-start(bf16[128,512]{1,0:T(8,128)(2,1)S(1)} %get-tuple-element.107), channel_id=1, source_target_pairs={{0,2},{1,3},{2,0},{3,1},{4,6},{5,7},{6,4},{7,5},{8,10},{9,11},{10,... | collective-permute-start | bytes 393224 | tf_op jit(solution)/shard_map/ppermute | solution.py:35
  59.5 3.5 %collective-permute-start.25 = (bf16[128,512]{1,0:T(8,128)(2,1)S(1)}, bf16[128,512]{1,0:T(8,128)(2,1)S(1)}, u32[]{:S(2)}, u32[]{:S(2)}) collective-permute-start(bf16[128,512]{1,0:T(8,128)(2,1)S(1)} %get-tuple-element.108), channel_id=1, source_target_pairs={{0,2},{1,3},{2,0},{3,1},{4,6},{5,7},{6,4},{7,5},{8,10},{9,11},{10,... | collective-permute-start | bytes 393224 | tf_op jit(solution)/shard_map/ppermute | solution.py:35
  61.5 1.5 %collective-permute-start.26 = (bf16[128,512]{1,0:T(8,128)(2,1)S(1)}, bf16[128,512]{1,0:T(8,128)(2,1)S(1)}, u32[]{:S(2)}, u32[]{:S(2)}) collective-permute-start(bf16[128,512]{1,0:T(8,128)(2,1)S(1)} %get-tuple-element.109), channel_id=1, source_target_pairs={{0,2},{1,3},{2,0},{3,1},{4,6},{5,7},{6,4},{7,5},{8,10},{9,11},{10,... | collective-permute-start | bytes 393224 | tf_op jit(solution)/shard_map/ppermute | solution.py:35

commit v15 on v13

--- a/solution.py
+++ b/solution.py
@@ -40,13 +40,17 @@
 
 
 def chip_masks(size):
-    return [mask for mask in range(size) if not mask & core_mask()]
+    masks = [mask for mask in range(size) if not mask & core_mask()]
+    order = masks[:1] + masks[2:0:-1] + masks[3:]
+    return list(zip(masks, order))
 
 
 def swap_chips(pieces, size):
-    return [pieces[0]] + [
-        swap(piece, mask) for piece, mask in zip(pieces[1:], chip_masks(size)[1:])
-    ]
+    core, received = core_mask(), list(pieces)
+    for at, masks in list(enumerate(chip_masks(size)))[1:]:
+        pairs = [(i, i ^ masks[i // core % 2]) for i in range(device_count())]
+        received[at] = lax.ppermute(pieces[at], BOTH, pairs)
+    return received
 
 
 def shifted(value, step):
@@ -55,8 +59,11 @@
     return lax.ppermute(value, BOTH, pairs)
 
 
-def partner(size, j):
-    return lax.bitwise_xor(lax.rem(flat_index(), size), j)
+def partner(size, masks, flip=0, twin=False):
+    core, me = core_mask(), lax.rem(flat_index(), size)
+    odd = lax.rem(lax.div(me, core), 2) == 1
+    mask = jnp.where(odd != twin, masks[1], masks[0])
+    return lax.bitwise_xor(me, lax.bitwise_xor(mask, flip))
 
 
 def place(index, width):
@@ -126,14 +133,14 @@
     for mask, piece in zip(masks, pieces):
         rows = piece.shape[0] // 2
         out[place(partner(size, mask), rows), :] = piece[:rows, :]
-        out[place(partner(size, mask ^ core), rows), :] = piece[rows:, :]
+        out[place(partner(size, mask, core), rows), :] = piece[rows:, :]
 
 
 def take_rows(size, core, masks, source, pieces):
     for mask, piece in zip(masks, pieces):
         rows = piece.shape[0] // 2
         piece[:rows, :] = source(place(partner(size, mask), rows))
-        piece[rows:, :] = source(place(partner(size, mask ^ core), rows))
+        piece[rows:, :] = source(place(partner(size, mask, core), rows))
 
 
 def join(pieces, size):
@@ -185,7 +192,7 @@
             rows, width = piece.shape[0] // 2, piece.shape[1] // len(outs)
             for at, out in enumerate(outs):
                 mine = out.at[:, place(partner(size, mask), width)]
-                other = out.at[:, place(partner(size, mask ^ core), width)]
+                other = out.at[:, place(partner(size, mask, core, True), width)]
                 copies.append((piece.at[:rows, at * width : (at + 1) * width], mine))
                 copies.append((got.at[:, start : start + width], other))
                 start += width

time: 62.8 us -> 66.1 us (1.053); the launches traced: 62.6 us -> 65.1 us
  starting transfers between devices: 26.6 us -> 28 us
  waiting for transfers between devices: 18.4 us -> 19.5 us
    ppermute x0 -> x15, starting transfers between devices: none -> 21.8 us  [swap_chips(): received[at] = lax.ppermute(pieces[at], BOTH, pairs)]
    ppermute x20 -> x5, starting transfers between devices: 21.6 us -> 1.18 us  [swap(): lax.ppermute(value, BOTH, [(i, i ^ mask) for i in range(device_count())])]
    ppermute x0 -> x15, waiting for transfers between devices: none -> 16.5 us  [swap_chips(): received[at] = lax.ppermute(pieces[at], BOTH, pairs)]
    ppermute x20 -> x5, waiting for transfers between devices: 17.4 us -> 2.28 us  [swap(): lax.ppermute(value, BOTH, [(i, i ^ mask) for i in range(device_count())])]
  transfers between devices with their start and end apart: 22 -> 22, of which waited for: 11 -> 13; matrix products, arithmetic and copies ran while one was open for 4% -> 4% of each run, Pallas kernels for 10% -> 9%
where the time goes in v15:
time: 66.1 us; the launch traced here: 65.1 us
  starting transfers between devices  28 us (42%)
  waiting for transfers between devices  19.5 us (30%)
  Pallas kernels  13.8 us (21%)
  local copies, waits for them, and re-layouts  2.03 us (3%)
  between operations  1.1 us (2%)
  other arithmetic  0.74 us (1%)
    ppermute x15, starting transfers between devices, swap_chips(): received[at] = lax.ppermute(pieces[at], BOTH, pairs)  21.8 us
    ppermute x15, waiting for transfers between devices, swap_chips(): received[at] = lax.ppermute(pieces[at], BOTH, pairs)  16.5 us
    pallas_call x3, Pallas kernels, attend_call(): pl.pallas_call(kernel, out_shape=out_shape, in_specs=[VMEM] * len(args),...  11.8 us
    ppermute x2, starting transfers between devices, shifted(): return lax.ppermute(value, BOTH, pairs)  4.99 us
    ppermute x5, waiting for transfers between devices, swap(): lax.ppermute(value, BOTH, [(i, i ^ mask) for i in range(device_count())])  2.28 us
    slice x4, local copies, waits for them, and re-layouts, this_core(): shares = [array[:, r * width:(r + 1) * width] for r in range(size)]  1.99 us
    pallas_call x1, Pallas kernels, spread_cores(): pl.pallas_call(functools.partial(spread_body, size, core_mask(), chip_mas...  1.39 us
  transfers between devices with their start and end apart: 22, of which 13 were waited for; matrix products, arithmetic and copies ran while one was open for 4% of the time, Pallas kernels for 9%

profile of v15, /device:TPU:0, one launch (start us, length us, event | category | flops | bytes accessed | tf_op | source)
XLA Modules:
  0.0 65.1 jit_solution(7314283882043236407)
XLA Ops:
  1.8 1.0 %fusion.3 = (bf16[128,256]{1,0:T(8,128)(2,1)S(1)}, bf16[128,256]{1,0:T(8,128)(2,1)S(1)}, bf16[128,256]{1,0:T(8,128)(2,1)S(1)}, bf16[128,256]{1,0:T(8,128)(2,1)S(1)}) fusion(bf16[128,1024]{1,0:T(8,128)(2,1)} %param.6), kind=kLoop, calls=%fused_computation.12 | loop fusion | bytes 524288 | tf_op jit(solution)/shard_map/slice | solution.py:101
  2.7 1.0 %fusion.2 = (bf16[128,256]{1,0:T(8,128)(2,1)S(1)}, bf16[128,256]{1,0:T(8,128)(2,1)S(1)}, bf16[128,256]{1,0:T(8,128)(2,1)S(1)}, bf16[128,256]{1,0:T(8,128)(2,1)S(1)}) fusion(bf16[128,1024]{1,0:T(8,128)(2,1)} %param.7), kind=kLoop, calls=%fused_computation.11 | loop fusion | bytes 524288 | tf_op jit(solution)/shard_map/slice | solution.py:101
  4.0 3.0 %collective-permute-start.7 = (bf16[256,256]{1,0:T(8,128)(2,1)S(1)}, bf16[256,256]{1,0:T(8,128)(2,1)S(1)}, u32[]{:S(2)}, u32[]{:S(2)}) collective-permute-start(bf16[256,256]{1,0:T(8,128)(2,1)S(1)} %get-tuple-element.53), channel_id=1, source_target_pairs={{0,1},{1,0},{2,6},{3,7},{4,5},{5,4},{6,2},{7,3},{8,9},{9,8},{10,14... | collective-permute-start | bytes 393224 | tf_op jit(solution)/shard_map/ppermute | solution.py:52
  7.0 1.5 %collective-permute-start.8 = (bf16[256,256]{1,0:T(8,128)(2,1)S(1)}, bf16[256,256]{1,0:T(8,128)(2,1)S(1)}, u32[]{:S(2)}, u32[]{:S(2)}) collective-permute-start(bf16[256,256]{1,0:T(8,128)(2,1)S(1)} %get-tuple-element.54), channel_id=1, source_target_pairs={{0,4},{1,5},{2,3},{3,2},{4,0},{5,1},{6,7},{7,6},{8,12},{9,13},{10,... | collective-permute-start | bytes 393224 | tf_op jit(solution)/shard_map/ppermute | solution.py:52
  9.0 2.0 %collective-permute-start.4 = (bf16[256,512]{1,0:T(8,128)(2,1)S(1)}, bf16[256,512]{1,0:T(8,128)(2,1)S(1)}, u32[]{:S(2)}, u32[]{:S(2)}) collective-permute-start(bf16[256,512]{1,0:T(8,128)(2,1)S(1)} %get-tuple-element.49), channel_id=1, source_target_pairs={{0,1},{1,0},{2,6},{3,7},{4,5},{5,4},{6,2},{7,3},{8,9},{9,8},{10,14... | collective-permute-start | bytes 786440 | tf_op jit(solution)/shard_map/ppermute | solution.py:52
  11.0 1.5 %collective-permute-start.5 = (bf16[256,512]{1,0:T(8,128)(2,1)S(1)}, bf16[256,512]{1,0:T(8,128)(2,1)S(1)}, u32[]{:S(2)}, u32[]{:S(2)}) collective-permute-start(bf16[256,512]{1,0:T(8,128)(2,1)S(1)} %get-tuple-element.50), channel_id=1, source_target_pairs={{0,4},{1,5},{2,3},{3,2},{4,0},{5,1},{6,7},{7,6},{8,12},{9,13},{10,... | collective-permute-start | bytes 786440 | tf_op jit(solution)/shard_map/ppermute | solution.py:52
  12.5 1.7 %collective-permute-start.6 = (bf16[256,512]{1,0:T(8,128)(2,1)S(1)}, bf16[256,512]{1,0:T(8,128)(2,1)S(1)}, u32[]{:S(2)}, u32[]{:S(2)}) collective-permute-start(bf16[256,512]{1,0:T(8,128)(2,1)S(1)} %get-tuple-element.51), channel_id=1, source_target_pairs={{0,5},{1,4},{2,7},{3,6},{4,1},{5,0},{6,3},{7,2},{8,13},{9,12},{10,... | collective-permute-start | bytes 786440 | tf_op jit(solution)/shard_map/ppermute | solution.py:52
  14.6 0.6 collective-permute-done.8.refs_2_
  15.2 0.7 %collective-permute-done.9.refs_3_ = bf16[256,256]{1,0:T(8,128)(2,1)S(1)} collective-permute-done((bf16[256,256]{1,0:T(8,128)(2,1)S(1)}, bf16[256,256]{1,0:T(8,128)(2,1)S(1)}, u32[]{:S(2)}, u32[]{:S(2)}) %collective-permute-start.9) | collective-permute-done | bytes 131104 | tf_op jit(solution)/shard_map/ppermute | solution.py:52
  15.9 3.5 %collective-permute-start.10 = (bf16[1024,256]{1,0:T(8,128)(2,1)S(1)}, bf16[1024,256]{1,0:T(8,128)(2,1)S(1)}, u32[]{:S(2)}, u32[]{:S(2)}) collective-permute-start(bf16[1024,256]{1,0:T(8,128)(2,1)S(1)} %join.1.refs_6_.refs_4_), channel_id=1, source_target_pairs={{0,8},{1,9},{2,10},{3,11},{4,12},{5,13},{6,14},{7,15},{8,16},{9,17... | collective-permute-start | bytes 1572872 | tf_op jit(solution)/shard_map/ppermute | solution.py:59
  19.7 0.9 %collective-permute-done.4.refs_3_.refs_1_ = bf16[256,512]{1,0:T(8,128)(2,1)S(1)} collective-permute-done((bf16[256,512]{1,0:T(8,128)(2,1)S(1)}, bf16[256,512]{1,0:T(8,128)(2,1)S(1)}, u32[]{:S(2)}, u32[]{:S(2)}) %collective-permute-start.4) | collective-permute-done | bytes 262176 | tf_op jit(solution)/shard_map/ppermute | solution.py:52
  20.5 4.5 %collective-permute-done.5.refs_4_.refs_2_ = bf16[256,512]{1,0:T(8,128)(2,1)S(1)} collective-permute-done((bf16[256,512]{1,0:T(8,128)(2,1)S(1)}, bf16[256,512]{1,0:T(8,128)(2,1)S(1)}, u32[]{:S(2)}, u32[]{:S(2)}) %collective-permute-start.5) | collective-permute-done | bytes 262176 | tf_op jit(solution)/shard_map/ppermute | solution.py:52
  25.1 1.0 %collective-permute-done.6.refs_5_.refs_3_ = bf16[256,512]{1,0:T(8,128)(2,1)S(1)} collective-permute-done((bf16[256,512]{1,0:T(8,128)(2,1)S(1)}, bf16[256,512]{1,0:T(8,128)(2,1)S(1)}, u32[]{:S(2)}, u32[]{:S(2)}) %collective-permute-start.6) | collective-permute-done | bytes 262176 | tf_op jit(solution)/shard_map/ppermute | solution.py:52
  26.1 2.4 %forward_own.1 = (bf16[4608,256]{1,0:T(8,128)(2,1)S(1)}, f32[128,2048]{1,0:T(8,128)S(1)}, f32[16,256]{1,0:T(8,128)S(1)}) custom-call(bf16[2048,128]{1,0:T(8,128)(2,1)S(1)} %select_convert_fusion.refs_0_, bf16[1024,128]{1,0:T(8,128)(2,1)S(1)} %select_convert_fusion.1.refs_1_, bf16[256,512]{1,0:T(8,128)(2,1)S(1)} %get-tuple-element.48.refs_2_.refs_0_, ...), custom_call_target="tpu_custom_call" | custom-call | flops 4831838208 | bytes 8388608 | tf_op jit(solution)/shard_map/forward_own/pallas_call | solution.py:461
  28.5 0.7 %collective-permute-done.10.refs_6_ = bf16[1024,256]{1,0:T(8,128)(2,1)S(1)} collective-permute-done((bf16[1024,256]{1,0:T(8,128)(2,1)S(1)}, bf16[1024,256]{1,0:T(8,128)(2,1)S(1)}, u32[]{:S(2)}, u32[]{:S(2)}) %collective-permute-start.10) | collective-permute-done | bytes 524320 | tf_op jit(solution)/shard_map/ppermute | solution.py:59
  29.1 6.3 %forward.1 = (bf16[256,256]{1,0:T(8,128)(2,1)S(1)}, bf16[256,256]{1,0:T(8,128)(2,1)S(1)}, bf16[256,256]{1,0:T(8,128)(2,1)S(1)}, bf16[256,256]{1,0:T(8,128)(2,1)S...) custom-call(bf16[2048,128]{1,0:T(8,128)(2,1)S(1)} %select_convert_fu, ...), custom_call_target="tpu_custom_call" | custom-call | flops 1811939328 | bytes 8388608 | tf_op jit(solution)/shard_map/forward/pallas_call | solution.py:461
  35.4 1.5 %collective-permute-start.17 = (bf16[1024,256]{1,0:T(8,128)(2,1)S(1)}, bf16[1024,256]{1,0:T(8,128)(2,1)S(1)}, u32[]{:S(2)}, u32[]{:S(2)}) collective-permute-start(bf16[1024,256]{1,0:T(8,128)(2,1)S(1)} %get-tuple-element.79), channel_id=1, source_target_pairs={{8,0},{9,1},{10,2},{11,3},{12,4},{13,5},{14,6},{15,7},{16,8},{17,9... | collective-permute-start | bytes 1572872 | tf_op jit(solution)/shard_map/ppermute | solution.py:59
  36.9 1.8 %collective-permute-start.11 = (bf16[256,256]{1,0:T(8,128)(2,1)S(1)}, bf16[256,256]{1,0:T(8,128)(2,1)S(1)}, u32[]{:S(2)}, u32[]{:S(2)}) collective-permute-start(bf16[256,256]{1,0:T(8,128)(2,1)S(1)} %get-tuple-element.59), channel_id=1, source_target_pairs={{0,1},{1,0},{2,6},{3,7},{4,5},{5,4},{6,2},{7,3},{8,9},{9,8},{10,14... | collective-permute-start | bytes 393224 | tf_op jit(solution)/shard_map/ppermute | solution.py:52
  38.7 1.7 %collective-permute-start.12 = (bf16[256,256]{1,0:T(8,128)(2,1)S(1)}, bf16[256,256]{1,0:T(8,128)(2,1)S(1)}, u32[]{:S(2)}, u32[]{:S(2)}) collective-permute-start(bf16[256,256]{1,0:T(8,128)(2,1)S(1)} %get-tuple-element.60), channel_id=1, source_target_pairs={{0,4},{1,5},{2,3},{3,2},{4,0},{5,1},{6,7},{7,6},{8,12},{9,13},{10,... | collective-permute-start | bytes 393224 | tf_op jit(solution)/shard_map/ppermute | solution.py:52
  40.4 3.2 %backward.1 = (bf16[256,256]{1,0:T(8,128)(2,1)S(1)}, bf16[256,256]{1,0:T(8,128)(2,1)S(1)}, bf16[256,256]{1,0:T(8,128)(2,1)S(1)}, bf16[256,256]{1,0:T(8,128)(2,1)S(1)}, f32[1024,256]{1,0:T(8,128)S(1)}) custom-call(bf16[256,512]{1,0:T(8,128)(2,1)S(1)} %get-tuple-element.48.refs_2_.refs_0_, bf16[256,512]{1,0:T(8,128)(2,1)S(1)} %collective-permute-done.4.refs_3_.refs_1_, ...), custom_call_target="tpu_custom_call" | custom-call | flops 1207959552 | bytes 8388608 | tf_op jit(solution)/shard_map/backward/pallas_call | solution.py:461
  43.6 2.8 %collective-permute-done.12.refs_2_ = bf16[256,256]{1,0:T(8,128)(2,1)S(1)} collective-permute-done((bf16[256,256]{1,0:T(8,128)(2,1)S(1)}, bf16[256,256]{1,0:T(8,128)(2,1)S(1)}, u32[]{:S(2)}, u32[]{:S(2)}) %collective-permute-start.12) | collective-permute-done | bytes 131104 | tf_op jit(solution)/shard_map/ppermute | solution.py:52
  46.5 1.2 %collective-permute-start.14 = (bf16[256,256]{1,0:T(8,128)(2,1)S(1)}, bf16[256,256]{1,0:T(8,128)(2,1)S(1)}, u32[]{:S(2)}, u32[]{:S(2)}) collective-permute-start(bf16[256,256]{1,0:T(8,128)(2,1)S(1)} %get-tuple-element.75), channel_id=1, source_target_pairs={{0,1},{1,0},{2,6},{3,7},{4,5},{5,4},{6,2},{7,3},{8,9},{9,8},{10,14... | collective-permute-start | bytes 393224 | tf_op jit(solution)/shard_map/ppermute | solution.py:52
  47.6 1.7 %collective-permute-start.15 = (bf16[256,256]{1,0:T(8,128)(2,1)S(1)}, bf16[256,256]{1,0:T(8,128)(2,1)S(1)}, u32[]{:S(2)}, u32[]{:S(2)}) collective-permute-start(bf16[256,256]{1,0:T(8,128)(2,1)S(1)} %get-tuple-element.76), channel_id=1, source_target_pairs={{0,4},{1,5},{2,3},{3,2},{4,0},{5,1},{6,7},{7,6},{8,12},{9,13},{10,... | collective-permute-start | bytes 393224 | tf_op jit(solution)/shard_map/ppermute | solution.py:52
  49.3 0.7 %collective-permute-start.16 = (bf16[256,256]{1,0:T(8,128)(2,1)S(1)}, bf16[256,256]{1,0:T(8,128)(2,1)S(1)}, u32[]{:S(2)}, u32[]{:S(2)}) collective-permute-start(bf16[256,256]{1,0:T(8,128)(2,1)S(1)} %get-tuple-element.77), channel_id=1, source_target_pairs={{0,5},{1,4},{2,7},{3,6},{4,1},{5,0},{6,3},{7,2},{8,13},{9,12},{10,... | collective-permute-start | bytes 393224 | tf_op jit(solution)/shard_map/ppermute | solution.py:52
  50.1 1.7 %collective-permute-start.18 = (bf16[256,256]{1,0:T(8,128)(2,1)S(1)}, bf16[256,256]{1,0:T(8,128)(2,1)S(1)}, u32[]{:S(2)}, u32[]{:S(2)}) collective-permute-start(bf16[256,256]{1,0:T(8,128)(2,1)S(1)} %get-tuple-element.81), channel_id=1, source_target_pairs={{0,1},{1,0},{2,6},{3,7},{4,5},{5,4},{6,2},{7,3},{8,9},{9,8},{10,14... | collective-permute-start | bytes 393224 | tf_op jit(solution)/shard_map/ppermute | solution.py:52
  51.8 3.2 %collective-permute-start.19 = (bf16[256,256]{1,0:T(8,128)(2,1)S(1)}, bf16[256,256]{1,0:T(8,128)(2,1)S(1)}, u32[]{:S(2)}, u32[]{:S(2)}) collective-permute-start(bf16[256,256]{1,0:T(8,128)(2,1)S(1)} %get-tuple-element.82), channel_id=1, source_target_pairs={{0,4},{1,5},{2,3},{3,2},{4,0},{5,1},{6,7},{7,6},{8,12},{9,13},{10,... | collective-permute-start | bytes 393224 | tf_op jit(solution)/shard_map/ppermute | solution.py:52
  55.1 1.2 %collective-permute-done.15.refs_6_ = bf16[256,256]{1,0:T(8,128)(2,1)S(1)} collective-permute-done((bf16[256,256]{1,0:T(8,128)(2,1)S(1)}, bf16[256,256]{1,0:T(8,128)(2,1)S(1)}, u32[]{:S(2)}, u32[]{:S(2)}) %collective-permute-start.15) | collective-permute-done | bytes 131104 | tf_op jit(solution)/shard_map/ppermute | solution.py:52
  56.7 1.8 %collective-permute-done.18.refs_9_ = bf16[256,256]{1,0:T(8,128)(2,1)S(1)} collective-permute-done((bf16[256,256]{1,0:T(8,128)(2,1)S(1)}, bf16[256,256]{1,0:T(8,128)(2,1)S(1)}, u32[]{:S(2)}, u32[]{:S(2)}) %collective-permute-start.18) | collective-permute-done | bytes 131104 | tf_op jit(solution)/shard_map/ppermute | solution.py:52
  58.5 0.8 %collective-permute-done.19.refs_10_ = bf16[256,256]{1,0:T(8,128)(2,1)S(1)} collective-permute-done((bf16[256,256]{1,0:T(8,128)(2,1)S(1)}, bf16[256,256]{1,0:T(8,128)(2,1)S(1)}, u32[]{:S(2)}, u32[]{:S(2)}) %collective-permute-start.19) | collective-permute-done | bytes 131104 | tf_op jit(solution)/shard_map/ppermute | solution.py:52
  59.3 1.8 %collective-permute-done.20.refs_11_ = bf16[256,256]{1,0:T(8,128)(2,1)S(1)} collective-permute-done((bf16[256,256]{1,0:T(8,128)(2,1)S(1)}, bf16[256,256]{1,0:T(8,128)(2,1)S(1)}, u32[]{:S(2)}, u32[]{:S(2)}) %collective-permute-start.20) | collective-permute-done | bytes 131104 | tf_op jit(solution)/shard_map/ppermute | solution.py:52
  61.2 2.3 %collective-permute-done.21.refs_12_ = bf16[128,3072]{1,0:T(8,128)(2,1)S(1)} collective-permute-done((bf16[128,3072]{1,0:T(8,128)(2,1)S(1)}, bf16[128,3072]{1,0:T(8,128)(2,1)S(1)}, u32[]{:S(2)}, u32[]{:S(2)}) %collective-permute-start.21) | collective-permute-done | bytes 786464 | tf_op jit(solution)/shard_map/ppermute | solution.py:35
  63.5 1.4 %spread.1 = (bf16[128,2048]{1,0:T(8,128)(2,1)}, bf16[128,2048]{1,0:T(8,128)(2,1)}, bf16[128,1024]{1,0:T(8,128)(2,1)}, bf16[128,1024]{1,0:T(8,128)(2,1)}) custom-call(bf16[256,256]{1,0:T(8,128)(2,1)S(1)} %get-tuple-element.70.refs_0_, bf16[256,256]{1,0:T(8,128)(2,1)S(1)} %collective-permute-done.11.refs_1_, ...), custom_call_target="tpu_custom_call" | custom-call | tf_op jit(solution)/shard_map/spread/pallas_call | solution.py:208
  (39 shorter events, 3.1 us)
Async XLA Ops:
  0.6 7.9 %copy-start = (bf16[128,2048]{1,0:T(8,128)(2,1)S(1)}, bf16[128,2048]{1,0:T(8,128)(2,1)}, u32[]{:S(2)}) copy-start(bf16[128,2048]{1,0:T(8,128)(2,1)} %param.5) | copy-start | bytes 1572868
  0.6 7.9 %copy-start.1 = (bf16[128,2048]{1,0:T(8,128)(2,1)S(1)}, bf16[128,2048]{1,0:T(8,128)(2,1)}, u32[]{:S(2)}) copy-start(bf16[128,2048]{1,0:T(8,128)(2,1)} %param.8) | copy-start | bytes 1572868
  0.7 8.0 %copy-start.2 = (s32[4096]{0:T(1024)S(1)}, s32[4096]{0:T(1024)}, u32[]{:S(2)}) copy-start(s32[4096]{0:T(1024)} %param.9) | copy-start | bytes 49156
  0.7 3.2 %collective-permute-start = (bf16[128,1024]{1,0:T(8,128)(2,1)}, bf16[128,1024]{1,0:T(8,128)(2,1)S(1)}, u32[]{:S(2)}, u32[]{:S(2)}) collective-permute-start(bf16[128,1024]{1,0:T(8,128)(2,1)} %param.6), channel_id=1, source_target_pairs={{0,2},{1,3},{2,0},{3,1},{4,6},{5,7},{6,4},{7,5},{8,10},{9,11},{10,... | collective-permute-start | bytes 786440 | tf_op jit(solution)/shard_map/ppermute | solution.py:35
  1.2 2.7 %collective-permute-start.1 = (bf16[128,1024]{1,0:T(8,128)(2,1)}, bf16[128,1024]{1,0:T(8,128)(2,1)S(1)}, u32[]{:S(2)}, u32[]{:S(2)}) collective-permute-start(bf16[128,1024]{1,0:T(8,128)(2,1)} %param.7), channel_id=1, source_target_pairs={{0,2},{1,3},{2,0},{3,1},{4,6},{5,7},{6,4},{7,5},{8,10},{9,11},{10,... | collective-permute-start | bytes 786440 | tf_op jit(solution)/shard_map/ppermute | solution.py:35
  1.3 7.6 %collective-permute-start.2 = (bf16[128,2048]{1,0:T(8,128)(2,1)}, bf16[128,2048]{1,0:T(8,128)(2,1)S(1)}, u32[]{:S(2)}, u32[]{:S(2)}) collective-permute-start(bf16[128,2048]{1,0:T(8,128)(2,1)} %param.5), channel_id=1, source_target_pairs={{0,2},{1,3},{2,0},{3,1},{4,6},{5,7},{6,4},{7,5},{8,10},{9,11},{10,... | collective-permute-start | bytes 1572872 | tf_op jit(solution)/shard_map/ppermute | solution.py:35
  1.7 7.1 %collective-permute-start.3 = (bf16[128,2048]{1,0:T(8,128)(2,1)}, bf16[128,2048]{1,0:T(8,128)(2,1)S(1)}, u32[]{:S(2)}, u32[]{:S(2)}) collective-permute-start(bf16[128,2048]{1,0:T(8,128)(2,1)} %param.8), channel_id=1, source_target_pairs={{0,2},{1,3},{2,0},{3,1},{4,6},{5,7},{6,4},{7,5},{8,10},{9,11},{10,... | collective-permute-start | bytes 1572872 | tf_op jit(solution)/shard_map/ppermute | solution.py:35
  4.0 8.5 %collective-permute-start.7 = (bf16[256,256]{1,0:T(8,128)(2,1)S(1)}, bf16[256,256]{1,0:T(8,128)(2,1)S(1)}, u32[]{:S(2)}, u32[]{:S(2)}) collective-permute-start(bf16[256,256]{1,0:T(8,128)(2,1)S(1)} %get-tuple-element.53), channel_id=1, source_target_pairs={{0,1},{1,0},{2,6},{3,7},{4,5},{5,4},{6,2},{7,3},{8,9},{9,8},{10,14... | collective-permute-start | bytes 393224 | tf_op jit(solution)/shard_map/ppermute | solution.py:52
  7.0 8.2 %collective-permute-start.8 = (bf16[256,256]{1,0:T(8,128)(2,1)S(1)}, bf16[256,256]{1,0:T(8,128)(2,1)S(1)}, u32[]{:S(2)}, u32[]{:S(2)}) collective-permute-start(bf16[256,256]{1,0:T(8,128)(2,1)S(1)} %get-tuple-element.54), channel_id=1, source_target_pairs={{0,4},{1,5},{2,3},{3,2},{4,0},{5,1},{6,7},{7,6},{8,12},{9,13},{10,... | collective-permute-start | bytes 393224 | tf_op jit(solution)/shard_map/ppermute | solution.py:52
  8.5 7.4 %collective-permute-start.9 = (bf16[256,256]{1,0:T(8,128)(2,1)S(1)}, bf16[256,256]{1,0:T(8,128)(2,1)S(1)}, u32[]{:S(2)}, u32[]{:S(2)}) collective-permute-start(bf16[256,256]{1,0:T(8,128)(2,1)S(1)} %get-tuple-element.55), channel_id=1, source_target_pairs={{0,5},{1,4},{2,7},{3,6},{4,1},{5,0},{6,3},{7,2},{8,13},{9,12},{10,... | collective-permute-start | bytes 393224 | tf_op jit(solution)/shard_map/ppermute | solution.py:52
  8.6 10.8 %dynamic-slice-start = ((s32[4096]{0:T(1024)}, s32[]{:T(128)}), s32[1024]{0:T(1024)S(1)}, s32[]{:S(2)}) async-start(s32[4096]{0:T(1024)} %param.9, s32[]{:T(128)} %select_n.69), calls=%async_computation | async-start | bytes 8704 | tf_op jit(solution)/shard_map/dynamic_slice | solution.py:576
  9.0 11.5 %collective-permute-start.4 = (bf16[256,512]{1,0:T(8,128)(2,1)S(1)}, bf16[256,512]{1,0:T(8,128)(2,1)S(1)}, u32[]{:S(2)}, u32[]{:S(2)}) collective-permute-start(bf16[256,512]{1,0:T(8,128)(2,1)S(1)} %get-tuple-element.49), channel_id=1, source_target_pairs={{0,1},{1,0},{2,6},{3,7},{4,5},{5,4},{6,2},{7,3},{8,9},{9,8},{10,14... | collective-permute-start | bytes 786440 | tf_op jit(solution)/shard_map/ppermute | solution.py:52
  11.0 14.0 %collective-permute-start.5 = (bf16[256,512]{1,0:T(8,128)(2,1)S(1)}, bf16[256,512]{1,0:T(8,128)(2,1)S(1)}, u32[]{:S(2)}, u32[]{:S(2)}) collective-permute-start(bf16[256,512]{1,0:T(8,128)(2,1)S(1)} %get-tuple-element.50), channel_id=1, source_target_pairs={{0,4},{1,5},{2,3},{3,2},{4,0},{5,1},{6,7},{7,6},{8,12},{9,13},{10,... | collective-permute-start | bytes 786440 | tf_op jit(solution)/shard_map/ppermute | solution.py:52
  12.5 13.6 %collective-permute-start.6 = (bf16[256,512]{1,0:T(8,128)(2,1)S(1)}, bf16[256,512]{1,0:T(8,128)(2,1)S(1)}, u32[]{:S(2)}, u32[]{:S(2)}) collective-permute-start(bf16[256,512]{1,0:T(8,128)(2,1)S(1)} %get-tuple-element.51), channel_id=1, source_target_pairs={{0,5},{1,4},{2,7},{3,6},{4,1},{5,0},{6,3},{7,2},{8,13},{9,12},{10,... | collective-permute-start | bytes 786440 | tf_op jit(solution)/shard_map/ppermute | solution.py:52
  15.9 13.2 %collective-permute-start.10 = (bf16[1024,256]{1,0:T(8,128)(2,1)S(1)}, bf16[1024,256]{1,0:T(8,128)(2,1)S(1)}, u32[]{:S(2)}, u32[]{:S(2)}) collective-permute-start(bf16[1024,256]{1,0:T(8,128)(2,1)S(1)} %join.1.refs_6_.refs_4_), channel_id=1, source_target_pairs={{0,8},{1,9},{2,10},{3,11},{4,12},{5,13},{6,14},{7,15},{8,16},{9,17... | collective-permute-start | bytes 1572872 | tf_op jit(solution)/shard_map/ppermute | solution.py:59
  35.4 14.6 %collective-permute-start.17 = (bf16[1024,256]{1,0:T(8,128)(2,1)S(1)}, bf16[1024,256]{1,0:T(8,128)(2,1)S(1)}, u32[]{:S(2)}, u32[]{:S(2)}) collective-permute-start(bf16[1024,256]{1,0:T(8,128)(2,1)S(1)} %get-tuple-element.79), channel_id=1, source_target_pairs={{8,0},{9,1},{10,2},{11,3},{12,4},{13,5},{14,6},{15,7},{16,8},{17,9... | collective-permute-start | bytes 1572872 | tf_op jit(solution)/shard_map/ppermute | solution.py:59
  36.9 6.8 %collective-permute-start.11 = (bf16[256,256]{1,0:T(8,128)(2,1)S(1)}, bf16[256,256]{1,0:T(8,128)(2,1)S(1)}, u32[]{:S(2)}, u32[]{:S(2)}) collective-permute-start(bf16[256,256]{1,0:T(8,128)(2,1)S(1)} %get-tuple-element.59), channel_id=1, source_target_pairs={{0,1},{1,0},{2,6},{3,7},{4,5},{5,4},{6,2},{7,3},{8,9},{9,8},{10,14... | collective-permute-start | bytes 393224 | tf_op jit(solution)/shard_map/ppermute | solution.py:52
  38.7 7.8 %collective-permute-start.12 = (bf16[256,256]{1,0:T(8,128)(2,1)S(1)}, bf16[256,256]{1,0:T(8,128)(2,1)S(1)}, u32[]{:S(2)}, u32[]{:S(2)}) collective-permute-start(bf16[256,256]{1,0:T(8,128)(2,1)S(1)} %get-tuple-element.60), channel_id=1, source_target_pairs={{0,4},{1,5},{2,3},{3,2},{4,0},{5,1},{6,7},{7,6},{8,12},{9,13},{10,... | collective-permute-start | bytes 393224 | tf_op jit(solution)/shard_map/ppermute | solution.py:52
  40.4 6.0 %collective-permute-start.13 = (bf16[256,256]{1,0:T(8,128)(2,1)S(1)}, bf16[256,256]{1,0:T(8,128)(2,1)S(1)}, u32[]{:S(2)}, u32[]{:S(2)}) collective-permute-start(bf16[256,256]{1,0:T(8,128)(2,1)S(1)} %get-tuple-element.61), channel_id=1, source_target_pairs={{0,5},{1,4},{2,7},{3,6},{4,1},{5,0},{6,3},{7,2},{8,13},{9,12},{10,... | collective-permute-start | bytes 393224 | tf_op jit(solution)/shard_map/ppermute | solution.py:52
  46.5 8.5 %collective-permute-start.14 = (bf16[256,256]{1,0:T(8,128)(2,1)S(1)}, bf16[256,256]{1,0:T(8,128)(2,1)S(1)}, u32[]{:S(2)}, u32[]{:S(2)}) collective-permute-start(bf16[256,256]{1,0:T(8,128)(2,1)S(1)} %get-tuple-element.75), channel_id=1, source_target_pairs={{0,1},{1,0},{2,6},{3,7},{4,5},{5,4},{6,2},{7,3},{8,9},{9,8},{10,14... | collective-permute-start | bytes 393224 | tf_op jit(solution)/shard_map/ppermute | solution.py:52
  47.6 8.6 %collective-permute-start.15 = (bf16[256,256]{1,0:T(8,128)(2,1)S(1)}, bf16[256,256]{1,0:T(8,128)(2,1)S(1)}, u32[]{:S(2)}, u32[]{:S(2)}) collective-permute-start(bf16[256,256]{1,0:T(8,128)(2,1)S(1)} %get-tuple-element.76), channel_id=1, source_target_pairs={{0,4},{1,5},{2,3},{3,2},{4,0},{5,1},{6,7},{7,6},{8,12},{9,13},{10,... | collective-permute-start | bytes 393224 | tf_op jit(solution)/shard_map/ppermute | solution.py:52
  49.3 7.4 %collective-permute-start.16 = (bf16[256,256]{1,0:T(8,128)(2,1)S(1)}, bf16[256,256]{1,0:T(8,128)(2,1)S(1)}, u32[]{:S(2)}, u32[]{:S(2)}) collective-permute-start(bf16[256,256]{1,0:T(8,128)(2,1)S(1)} %get-tuple-element.77), channel_id=1, source_target_pairs={{0,5},{1,4},{2,7},{3,6},{4,1},{5,0},{6,3},{7,2},{8,13},{9,12},{10,... | collective-permute-start | bytes 393224 | tf_op jit(solution)/shard_map/ppermute | solution.py:52
  50.1 8.4 %collective-permute-start.18 = (bf16[256,256]{1,0:T(8,128)(2,1)S(1)}, bf16[256,256]{1,0:T(8,128)(2,1)S(1)}, u32[]{:S(2)}, u32[]{:S(2)}) collective-permute-start(bf16[256,256]{1,0:T(8,128)(2,1)S(1)} %get-tuple-element.81), channel_id=1, source_target_pairs={{0,1},{1,0},{2,6},{3,7},{4,5},{5,4},{6,2},{7,3},{8,9},{9,8},{10,14... | collective-permute-start | bytes 393224 | tf_op jit(solution)/shard_map/ppermute | solution.py:52
  51.8 7.5 %collective-permute-start.19 = (bf16[256,256]{1,0:T(8,128)(2,1)S(1)}, bf16[256,256]{1,0:T(8,128)(2,1)S(1)}, u32[]{:S(2)}, u32[]{:S(2)}) collective-permute-start(bf16[256,256]{1,0:T(8,128)(2,1)S(1)} %get-tuple-element.82), channel_id=1, source_target_pairs={{0,4},{1,5},{2,3},{3,2},{4,0},{5,1},{6,7},{7,6},{8,12},{9,13},{10,... | collective-permute-start | bytes 393224 | tf_op jit(solution)/shard_map/ppermute | solution.py:52
  55.0 6.1 %collective-permute-start.20 = (bf16[256,256]{1,0:T(8,128)(2,1)S(1)}, bf16[256,256]{1,0:T(8,128)(2,1)S(1)}, u32[]{:S(2)}, u32[]{:S(2)}) collective-permute-start(bf16[256,256]{1,0:T(8,128)(2,1)S(1)} %get-tuple-element.83), channel_id=1, source_target_pairs={{0,5},{1,4},{2,7},{3,6},{4,1},{5,0},{6,3},{7,2},{8,13},{9,12},{10,... | collective-permute-start | bytes 393224 | tf_op jit(solution)/shard_map/ppermute | solution.py:52
  61.2 2.4 %collective-permute-start.21 = (bf16[128,3072]{1,0:T(8,128)(2,1)S(1)}, bf16[128,3072]{1,0:T(8,128)(2,1)S(1)}, u32[]{:S(2)}, u32[]{:S(2)}) collective-permute-start(bf16[128,3072]{1,0:T(8,128)(2,1)S(1)} %bottom.1), channel_id=1, source_target_pairs={{0,2},{1,3},{2,0},{3,1},{4,6},{5,7},{6,4},{7,5},{8,10},{9,11},{10,... | collective-permute-start | bytes 2359304 | tf_op jit(solution)/shard_map/ppermute | solution.py:35

commit v16 on v13

--- a/solution.py
+++ b/solution.py
@@ -192,11 +192,14 @@
     run_copies(copies, sems)
 
 
-def spread_cores(sets, counts, size):
+def bottom(pieces):
+    shape = (pieces[0].shape[0] // 2, sum(piece.shape[1] for piece in pieces))
+    return small_call(bottom_body, jax.ShapeDtypeStruct(shape, BF16), "bottom", *pieces)
+
+
+def spread_cores(sets, counts, got, size):
     pieces = [piece for part in sets for piece in part]
     rows = pieces[0].shape[0] // 2
-    give = jax.ShapeDtypeStruct((rows, sum(piece.shape[1] for piece in pieces)), BF16)
-    got = swap(small_call(bottom_body, give, "bottom", *pieces), core_mask())
     widths = [part[0].shape[1] // count for part, count in zip(sets, counts) for _ in range(count)]
     return pl.pallas_call(
         functools.partial(spread_body, size, core_mask(), chip_masks(size), counts),
@@ -594,11 +597,14 @@
     backs = [shifted(sent[lag - 1], -lag * size) for lag in range(1, reach + 1)]
     out = swap_chips(out, size)
     grad_q, dkv = backward(qg, kv, [e_own, *carried], size)
-    both = after(*out, *grad_q)
-    out, grad_q = both[: len(out)], both[len(out) :]
+    give, *grad_q = after(bottom(out), *grad_q)
     grad_q = swap_chips(grad_q, size)
+    dkv, got = after(dkv, swap(give, core_mask()))
     grads = swap_chips(combine([dkv, *backs], size), size)
-    return tuple(spread_cores([out, grad_q, grads], (1, 1, 2), size))
+    (attn_out,) = spread_cores([out], (1,), got, size)
+    attn_out, *grad_q = after(attn_out, *grad_q)
+    got = swap(bottom([*grad_q, *grads]), core_mask())
+    return (attn_out, *spread_cores([grad_q, grads], (1, 2), got, size))
 
 
 def solution(mesh):

time: 62.8 us -> 64.5 us (1.027)
    pallas_call x1 -> x2, Pallas kernels: 1.39 us -> 2 us  [spread_cores(): pl.pallas_call(functools.partial(spread_body, size, core_mask(), chip_mas...]
    ppermute x20 -> x21, waiting for transfers between devices: 17.4 us -> 18 us  [swap(): lax.ppermute(value, BOTH, [(i, i ^ mask) for i in range(device_count())])]
    ppermute x20 -> x21, starting transfers between devices: 21.6 us -> 21.7 us  [swap(): lax.ppermute(value, BOTH, [(i, i ^ mask) for i in range(device_count())])]
  transfers between devices with their start and end apart: 22 -> 23, of which waited for: 11 -> 12; matrix products, arithmetic and copies ran while one was open for 4% -> 4% of each run, Pallas kernels for 10% -> 11%
where the time goes in v16:
time: 64.5 us; the launch traced here: 63.7 us
  starting transfers between devices  26.7 us (41%)
  waiting for transfers between devices  18.7 us (29%)
  Pallas kernels  14.4 us (22%)
  local copies, waits for them, and re-layouts  2.03 us (3%)
  between operations  1.12 us (2%)
  other arithmetic  0.74 us (1%)
    ppermute x21, starting transfers between devices, swap(): lax.ppermute(value, BOTH, [(i, i ^ mask) for i in range(device_count())])  21.7 us
    ppermute x21, waiting for transfers between devices, swap(): lax.ppermute(value, BOTH, [(i, i ^ mask) for i in range(device_count())])  18 us
    pallas_call x3, Pallas kernels, attend_call(): pl.pallas_call(kernel, out_shape=out_shape, in_specs=[VMEM] * len(args),...  11.8 us
    ppermute x2, starting transfers between devices, shifted(): return lax.ppermute(value, BOTH, pairs)  4.99 us
    pallas_call x2, Pallas kernels, spread_cores(): pl.pallas_call(functools.partial(spread_body, size, core_mask(), chip_mas...  2 us
    slice x4, local copies, waits for them, and re-layouts, this_core(): shares = [array[:, r * width:(r + 1) * width] for r in range(size)]  1.99 us
  transfers between devices with their start and end apart: 23, of which 12 were waited for; matrix products, arithmetic and copies ran while one was open for 4% of the time, Pallas kernels for 11%

profile of v16, /device:TPU:0, one launch (start us, length us, event | category | flops | bytes accessed | tf_op | source)
XLA Modules:
  0.0 63.7 jit_solution(96943358320539490)
XLA Ops:
  1.8 1.0 %fusion.3 = (bf16[128,256]{1,0:T(8,128)(2,1)S(1)}, bf16[128,256]{1,0:T(8,128)(2,1)S(1)}, bf16[128,256]{1,0:T(8,128)(2,1)S(1)}, bf16[128,256]{1,0:T(8,128)(2,1)S(1)}) fusion(bf16[128,1024]{1,0:T(8,128)(2,1)} %param.6), kind=kLoop, calls=%fused_computation.12 | loop fusion | bytes 524288 | tf_op jit(solution)/shard_map/slice | solution.py:94
  2.7 1.0 %fusion.2 = (bf16[128,256]{1,0:T(8,128)(2,1)S(1)}, bf16[128,256]{1,0:T(8,128)(2,1)S(1)}, bf16[128,256]{1,0:T(8,128)(2,1)S(1)}, bf16[128,256]{1,0:T(8,128)(2,1)S(1)}) fusion(bf16[128,1024]{1,0:T(8,128)(2,1)} %param.7), kind=kLoop, calls=%fused_computation.11 | loop fusion | bytes 524288 | tf_op jit(solution)/shard_map/slice | solution.py:94
  4.0 3.0 %collective-permute-start.7 = (bf16[256,256]{1,0:T(8,128)(2,1)S(1)}, bf16[256,256]{1,0:T(8,128)(2,1)S(1)}, u32[]{:S(2)}, u32[]{:S(2)}) collective-permute-start(bf16[256,256]{1,0:T(8,128)(2,1)S(1)} %get-tuple-element.60), channel_id=1, source_target_pairs={{0,1},{1,0},{2,3},{3,2},{4,5},{5,4},{6,7},{7,6},{8,9},{9,8},{10,11... | collective-permute-start | bytes 393224 | tf_op jit(solution)/shard_map/ppermute | solution.py:35
  7.0 1.5 %collective-permute-start.8 = (bf16[256,256]{1,0:T(8,128)(2,1)S(1)}, bf16[256,256]{1,0:T(8,128)(2,1)S(1)}, u32[]{:S(2)}, u32[]{:S(2)}) collective-permute-start(bf16[256,256]{1,0:T(8,128)(2,1)S(1)} %get-tuple-element.61), channel_id=1, source_target_pairs={{0,4},{1,5},{2,6},{3,7},{4,0},{5,1},{6,2},{7,3},{8,12},{9,13},{10,... | collective-permute-start | bytes 393224 | tf_op jit(solution)/shard_map/ppermute | solution.py:35
  9.0 2.0 %collective-permute-start.4 = (bf16[256,512]{1,0:T(8,128)(2,1)S(1)}, bf16[256,512]{1,0:T(8,128)(2,1)S(1)}, u32[]{:S(2)}, u32[]{:S(2)}) collective-permute-start(bf16[256,512]{1,0:T(8,128)(2,1)S(1)} %get-tuple-element.56), channel_id=1, source_target_pairs={{0,1},{1,0},{2,3},{3,2},{4,5},{5,4},{6,7},{7,6},{8,9},{9,8},{10,11... | collective-permute-start | bytes 786440 | tf_op jit(solution)/shard_map/ppermute | solution.py:35
  11.0 1.5 %collective-permute-start.5 = (bf16[256,512]{1,0:T(8,128)(2,1)S(1)}, bf16[256,512]{1,0:T(8,128)(2,1)S(1)}, u32[]{:S(2)}, u32[]{:S(2)}) collective-permute-start(bf16[256,512]{1,0:T(8,128)(2,1)S(1)} %get-tuple-element.57), channel_id=1, source_target_pairs={{0,4},{1,5},{2,6},{3,7},{4,0},{5,1},{6,2},{7,3},{8,12},{9,13},{10,... | collective-permute-start | bytes 786440 | tf_op jit(solution)/shard_map/ppermute | solution.py:35
  12.5 1.7 %collective-permute-start.6 = (bf16[256,512]{1,0:T(8,128)(2,1)S(1)}, bf16[256,512]{1,0:T(8,128)(2,1)S(1)}, u32[]{:S(2)}, u32[]{:S(2)}) collective-permute-start(bf16[256,512]{1,0:T(8,128)(2,1)S(1)} %get-tuple-element.58), channel_id=1, source_target_pairs={{0,5},{1,4},{2,7},{3,6},{4,1},{5,0},{6,3},{7,2},{8,13},{9,12},{10,... | collective-permute-start | bytes 786440 | tf_op jit(solution)/shard_map/ppermute | solution.py:35
  14.6 0.6 collective-permute-done.8.refs_2_
  15.2 0.7 %collective-permute-done.9.refs_3_ = bf16[256,256]{1,0:T(8,128)(2,1)S(1)} collective-permute-done((bf16[256,256]{1,0:T(8,128)(2,1)S(1)}, bf16[256,256]{1,0:T(8,128)(2,1)S(1)}, u32[]{:S(2)}, u32[]{:S(2)}) %collective-permute-start.9) | collective-permute-done | bytes 131104 | tf_op jit(solution)/shard_map/ppermute | solution.py:35
  15.9 3.5 %collective-permute-start.10 = (bf16[1024,256]{1,0:T(8,128)(2,1)S(1)}, bf16[1024,256]{1,0:T(8,128)(2,1)S(1)}, u32[]{:S(2)}, u32[]{:S(2)}) collective-permute-start(bf16[1024,256]{1,0:T(8,128)(2,1)S(1)} %join.1.refs_6_.refs_4_), channel_id=1, source_target_pairs={{0,8},{1,9},{2,10},{3,11},{4,12},{5,13},{6,14},{7,15},{8,16},{9,17... | collective-permute-start | bytes 1572872 | tf_op jit(solution)/shard_map/ppermute | solution.py:55
  19.7 0.8 %collective-permute-done.4.refs_3_.refs_1_ = bf16[256,512]{1,0:T(8,128)(2,1)S(1)} collective-permute-done((bf16[256,512]{1,0:T(8,128)(2,1)S(1)}, bf16[256,512]{1,0:T(8,128)(2,1)S(1)}, u32[]{:S(2)}, u32[]{:S(2)}) %collective-permute-start.4) | collective-permute-done | bytes 262176 | tf_op jit(solution)/shard_map/ppermute | solution.py:35
  20.5 5.7 %collective-permute-done.5.refs_4_.refs_2_ = bf16[256,512]{1,0:T(8,128)(2,1)S(1)} collective-permute-done((bf16[256,512]{1,0:T(8,128)(2,1)S(1)}, bf16[256,512]{1,0:T(8,128)(2,1)S(1)}, u32[]{:S(2)}, u32[]{:S(2)}) %collective-permute-start.5) | collective-permute-done | bytes 262176 | tf_op jit(solution)/shard_map/ppermute | solution.py:35
  26.2 2.4 %forward_own.1 = (bf16[4608,256]{1,0:T(8,128)(2,1)S(1)}, f32[128,2048]{1,0:T(8,128)S(1)}, f32[16,256]{1,0:T(8,128)S(1)}) custom-call(bf16[2048,128]{1,0:T(8,128)(2,1)S(1)} %select_convert_fusion.refs_0_, bf16[1024,128]{1,0:T(8,128)(2,1)S(1)} %select_convert_fusion.1.refs_1_, bf16[256,512]{1,0:T(8,128)(2,1)S(1)} %get-tuple-element.55.refs_2_.refs_0_, ...), custom_call_target="tpu_custom_call" | custom-call | flops 4831838208 | bytes 8388608 | tf_op jit(solution)/shard_map/forward_own/pallas_call | solution.py:457
  28.7 6.3 %forward.1 = (bf16[256,256]{1,0:T(8,128)(2,1)S(1)}, bf16[256,256]{1,0:T(8,128)(2,1)S(1)}, bf16[256,256]{1,0:T(8,128)(2,1)S(1)}, bf16[256,256]{1,0:T(8,128)(2,1)S...) custom-call(bf16[2048,128]{1,0:T(8,128)(2,1)S(1)} %select_convert_fu, ...), custom_call_target="tpu_custom_call" | custom-call | flops 1811939328 | bytes 8388608 | tf_op jit(solution)/shard_map/forward/pallas_call | solution.py:457
  34.9 1.5 %collective-permute-start.18 = (bf16[1024,256]{1,0:T(8,128)(2,1)S(1)}, bf16[1024,256]{1,0:T(8,128)(2,1)S(1)}, u32[]{:S(2)}, u32[]{:S(2)}) collective-permute-start(bf16[1024,256]{1,0:T(8,128)(2,1)S(1)} %get-tuple-element.90), channel_id=1, source_target_pairs={{8,0},{9,1},{10,2},{11,3},{12,4},{13,5},{14,6},{15,7},{16,8},{17,9... | collective-permute-start | bytes 1572872 | tf_op jit(solution)/shard_map/ppermute | solution.py:55
  36.4 1.8 %collective-permute-start.11 = (bf16[256,256]{1,0:T(8,128)(2,1)S(1)}, bf16[256,256]{1,0:T(8,128)(2,1)S(1)}, u32[]{:S(2)}, u32[]{:S(2)}) collective-permute-start(bf16[256,256]{1,0:T(8,128)(2,1)S(1)} %get-tuple-element.66), channel_id=1, source_target_pairs={{0,1},{1,0},{2,3},{3,2},{4,5},{5,4},{6,7},{7,6},{8,9},{9,8},{10,11... | collective-permute-start | bytes 393224 | tf_op jit(solution)/shard_map/ppermute | solution.py:35
  38.7 1.3 %collective-permute-start.13 = (bf16[256,256]{1,0:T(8,128)(2,1)S(1)}, bf16[256,256]{1,0:T(8,128)(2,1)S(1)}, u32[]{:S(2)}, u32[]{:S(2)}) collective-permute-start(bf16[256,256]{1,0:T(8,128)(2,1)S(1)} %get-tuple-element.68), channel_id=1, source_target_pairs={{0,5},{1,4},{2,7},{3,6},{4,1},{5,0},{6,3},{7,2},{8,13},{9,12},{10,... | collective-permute-start | bytes 393224 | tf_op jit(solution)/shard_map/ppermute | solution.py:35
  40.0 3.2 %backward.1 = (bf16[256,256]{1,0:T(8,128)(2,1)S(1)}, bf16[256,256]{1,0:T(8,128)(2,1)S(1)}, bf16[256,256]{1,0:T(8,128)(2,1)S(1)}, bf16[256,256]{1,0:T(8,128)(2,1)S(1)}, f32[1024,256]{1,0:T(8,128)S(1)}) custom-call(bf16[256,512]{1,0:T(8,128)(2,1)S(1)} %get-tuple-element.55.refs_2_.refs_0_, bf16[256,512]{1,0:T(8,128)(2,1)S(1)} %collective-permute-done.4.refs_3_.refs_1_, ...), custom_call_target="tpu_custom_call" | custom-call | flops 1207959552 | bytes 8388608 | tf_op jit(solution)/shard_map/backward/pallas_call | solution.py:457
  43.2 1.9 %collective-permute-done.12.refs_2_ = bf16[256,256]{1,0:T(8,128)(2,1)S(1)} collective-permute-done((bf16[256,256]{1,0:T(8,128)(2,1)S(1)}, bf16[256,256]{1,0:T(8,128)(2,1)S(1)}, u32[]{:S(2)}, u32[]{:S(2)}) %collective-permute-start.12) | collective-permute-done | bytes 131104 | tf_op jit(solution)/shard_map/ppermute | solution.py:35
  45.2 1.1 %collective-permute-start.15 = (bf16[256,256]{1,0:T(8,128)(2,1)S(1)}, bf16[256,256]{1,0:T(8,128)(2,1)S(1)}, u32[]{:S(2)}, u32[]{:S(2)}) collective-permute-start(bf16[256,256]{1,0:T(8,128)(2,1)S(1)} %get-tuple-element.81), channel_id=1, source_target_pairs={{0,1},{1,0},{2,3},{3,2},{4,5},{5,4},{6,7},{7,6},{8,9},{9,8},{10,11... | collective-permute-start | bytes 393224 | tf_op jit(solution)/shard_map/ppermute | solution.py:35
  46.3 0.7 %collective-permute-start.16 = (bf16[256,256]{1,0:T(8,128)(2,1)S(1)}, bf16[256,256]{1,0:T(8,128)(2,1)S(1)}, u32[]{:S(2)}, u32[]{:S(2)}) collective-permute-start(bf16[256,256]{1,0:T(8,128)(2,1)S(1)} %get-tuple-element.82), channel_id=1, source_target_pairs={{0,4},{1,5},{2,6},{3,7},{4,0},{5,1},{6,2},{7,3},{8,12},{9,13},{10,... | collective-permute-start | bytes 393224 | tf_op jit(solution)/shard_map/ppermute | solution.py:35
  47.0 1.7 %collective-permute-start.17 = (bf16[256,256]{1,0:T(8,128)(2,1)S(1)}, bf16[256,256]{1,0:T(8,128)(2,1)S(1)}, u32[]{:S(2)}, u32[]{:S(2)}) collective-permute-start(bf16[256,256]{1,0:T(8,128)(2,1)S(1)} %get-tuple-element.83), channel_id=1, source_target_pairs={{0,5},{1,4},{2,7},{3,6},{4,1},{5,0},{6,3},{7,2},{8,13},{9,12},{10,... | collective-permute-start | bytes 393224 | tf_op jit(solution)/shard_map/ppermute | solution.py:35
  48.7 0.7 %collective-permute-done.18.refs_1_ = bf16[1024,256]{1,0:T(8,128)(2,1)S(1)} collective-permute-done((bf16[1024,256]{1,0:T(8,128)(2,1)S(1)}, bf16[1024,256]{1,0:T(8,128)(2,1)S(1)}, u32[]{:S(2)}, u32[]{:S(2)}) %collective-permute-start.18) | collective-permute-done | bytes 524320 | tf_op jit(solution)/shard_map/ppermute | solution.py:55
  49.6 1.7 %collective-permute-start.19 = (bf16[256,256]{1,0:T(8,128)(2,1)S(1)}, bf16[256,256]{1,0:T(8,128)(2,1)S(1)}, u32[]{:S(2)}, u32[]{:S(2)}) collective-permute-start(bf16[256,256]{1,0:T(8,128)(2,1)S(1)} %get-tuple-element.92), channel_id=1, source_target_pairs={{0,1},{1,0},{2,3},{3,2},{4,5},{5,4},{6,7},{7,6},{8,9},{9,8},{10,11... | collective-permute-start | bytes 393224 | tf_op jit(solution)/shard_map/ppermute | solution.py:35
  51.3 0.6 collective-permute-start.20
  51.9 1.3 %collective-permute-start.21 = (bf16[256,256]{1,0:T(8,128)(2,1)S(1)}, bf16[256,256]{1,0:T(8,128)(2,1)S(1)}, u32[]{:S(2)}, u32[]{:S(2)}) collective-permute-start(bf16[256,256]{1,0:T(8,128)(2,1)S(1)} %get-tuple-element.94), channel_id=1, source_target_pairs={{0,5},{1,4},{2,7},{3,6},{4,1},{5,0},{6,3},{7,2},{8,13},{9,12},{10,... | collective-permute-start | bytes 393224 | tf_op jit(solution)/shard_map/ppermute | solution.py:35
  53.1 0.8 %spread.2 = bf16[128,2048]{1,0:T(8,128)(2,1)} custom-call(bf16[256,256]{1,0:T(8,128)(2,1)S(1)} %get-tuple-element.65.refs_0_, bf16[256,256]{1,0:T(8,128)(2,1)S(1)} %collective-permute-done.11.refs_1_, bf16[256,256]{1,0:T(8,128)(2,1)S(1)} %collective-permute-done.12.refs_2_, bf16[256,256]{1,0:T(8,128)(2,1)S(1)} %collective-permute-done.13.refs_3_, ...), custom_call_target="tpu_custom_call" | custom-call | tf_op jit(solution)/shard_map/spread/pallas_call | solution.py:204
  54.0 0.9 %collective-permute-done.16.refs_2_ = bf16[256,256]{1,0:T(8,128)(2,1)S(1)} collective-permute-done((bf16[256,256]{1,0:T(8,128)(2,1)S(1)}, bf16[256,256]{1,0:T(8,128)(2,1)S(1)}, u32[]{:S(2)}, u32[]{:S(2)}) %collective-permute-start.16) | collective-permute-done | bytes 131104 | tf_op jit(solution)/shard_map/ppermute | solution.py:35
  55.0 2.2 %collective-permute-done.19.refs_5_ = bf16[256,256]{1,0:T(8,128)(2,1)S(1)} collective-permute-done((bf16[256,256]{1,0:T(8,128)(2,1)S(1)}, bf16[256,256]{1,0:T(8,128)(2,1)S(1)}, u32[]{:S(2)}, u32[]{:S(2)}) %collective-permute-start.19) | collective-permute-done | bytes 131104 | tf_op jit(solution)/shard_map/ppermute | solution.py:35
  57.2 3.1 %collective-permute-done.20.refs_6_ = bf16[256,256]{1,0:T(8,128)(2,1)S(1)} collective-permute-done((bf16[256,256]{1,0:T(8,128)(2,1)S(1)}, bf16[256,256]{1,0:T(8,128)(2,1)S(1)}, u32[]{:S(2)}, u32[]{:S(2)}) %collective-permute-start.20) | collective-permute-done | bytes 131104 | tf_op jit(solution)/shard_map/ppermute | solution.py:35
  60.5 1.9 %collective-permute-done.22.refs_8_ = bf16[128,2048]{1,0:T(8,128)(2,1)S(1)} collective-permute-done((bf16[128,2048]{1,0:T(8,128)(2,1)S(1)}, bf16[128,2048]{1,0:T(8,128)(2,1)S(1)}, u32[]{:S(2)}, u32[]{:S(2)}) %collective-permute-start.22) | collective-permute-done | bytes 524320 | tf_op jit(solution)/shard_map/ppermute | solution.py:35
  62.4 1.2 %spread.3 = (bf16[128,2048]{1,0:T(8,128)(2,1)}, bf16[128,1024]{1,0:T(8,128)(2,1)}, bf16[128,1024]{1,0:T(8,128)(2,1)}) custom-call(bf16[256,256]{1,0:T(8,128)(2,1)S(1)} %get-tuple-element.85.refs_0_, bf16[256,256]{1,0:T(8,128)(2,1)S(1)} %collective-permute-done.15.refs_1_, bf16[256,256]{1,0:T(8,128)(2,1)S(1)} %collective-permute-done.16.refs_2_, ...), custom_call_target="tpu_custom_call" | custom-call | tf_op jit(solution)/shard_map/spread/pallas_call | solution.py:204
  (43 shorter events, 3.4 us)
Async XLA Ops:
  0.6 7.9 %copy-start = (bf16[128,2048]{1,0:T(8,128)(2,1)S(1)}, bf16[128,2048]{1,0:T(8,128)(2,1)}, u32[]{:S(2)}) copy-start(bf16[128,2048]{1,0:T(8,128)(2,1)} %param.5) | copy-start | bytes 1572868
  0.6 7.9 %copy-start.1 = (bf16[128,2048]{1,0:T(8,128)(2,1)S(1)}, bf16[128,2048]{1,0:T(8,128)(2,1)}, u32[]{:S(2)}) copy-start(bf16[128,2048]{1,0:T(8,128)(2,1)} %param.8) | copy-start | bytes 1572868
  0.7 8.0 %copy-start.2 = (s32[4096]{0:T(1024)S(1)}, s32[4096]{0:T(1024)}, u32[]{:S(2)}) copy-start(s32[4096]{0:T(1024)} %param.9) | copy-start | bytes 49156
  0.7 3.2 %collective-permute-start = (bf16[128,1024]{1,0:T(8,128)(2,1)}, bf16[128,1024]{1,0:T(8,128)(2,1)S(1)}, u32[]{:S(2)}, u32[]{:S(2)}) collective-permute-start(bf16[128,1024]{1,0:T(8,128)(2,1)} %param.6), channel_id=1, source_target_pairs={{0,2},{1,3},{2,0},{3,1},{4,6},{5,7},{6,4},{7,5},{8,10},{9,11},{10,... | collective-permute-start | bytes 786440 | tf_op jit(solution)/shard_map/ppermute | solution.py:35
  1.2 2.7 %collective-permute-start.1 = (bf16[128,1024]{1,0:T(8,128)(2,1)}, bf16[128,1024]{1,0:T(8,128)(2,1)S(1)}, u32[]{:S(2)}, u32[]{:S(2)}) collective-permute-start(bf16[128,1024]{1,0:T(8,128)(2,1)} %param.7), channel_id=1, source_target_pairs={{0,2},{1,3},{2,0},{3,1},{4,6},{5,7},{6,4},{7,5},{8,10},{9,11},{10,... | collective-permute-start | bytes 786440 | tf_op jit(solution)/shard_map/ppermute | solution.py:35
  1.3 7.5 %collective-permute-start.2 = (bf16[128,2048]{1,0:T(8,128)(2,1)}, bf16[128,2048]{1,0:T(8,128)(2,1)S(1)}, u32[]{:S(2)}, u32[]{:S(2)}) collective-permute-start(bf16[128,2048]{1,0:T(8,128)(2,1)} %param.5), channel_id=1, source_target_pairs={{0,2},{1,3},{2,0},{3,1},{4,6},{5,7},{6,4},{7,5},{8,10},{9,11},{10,... | collective-permute-start | bytes 1572872 | tf_op jit(solution)/shard_map/ppermute | solution.py:35
  1.7 7.1 %collective-permute-start.3 = (bf16[128,2048]{1,0:T(8,128)(2,1)}, bf16[128,2048]{1,0:T(8,128)(2,1)S(1)}, u32[]{:S(2)}, u32[]{:S(2)}) collective-permute-start(bf16[128,2048]{1,0:T(8,128)(2,1)} %param.8), channel_id=1, source_target_pairs={{0,2},{1,3},{2,0},{3,1},{4,6},{5,7},{6,4},{7,5},{8,10},{9,11},{10,... | collective-permute-start | bytes 1572872 | tf_op jit(solution)/shard_map/ppermute | solution.py:35
  4.0 8.5 %collective-permute-start.7 = (bf16[256,256]{1,0:T(8,128)(2,1)S(1)}, bf16[256,256]{1,0:T(8,128)(2,1)S(1)}, u32[]{:S(2)}, u32[]{:S(2)}) collective-permute-start(bf16[256,256]{1,0:T(8,128)(2,1)S(1)} %get-tuple-element.60), channel_id=1, source_target_pairs={{0,1},{1,0},{2,3},{3,2},{4,5},{5,4},{6,7},{7,6},{8,9},{9,8},{10,11... | collective-permute-start | bytes 393224 | tf_op jit(solution)/shard_map/ppermute | solution.py:35
  7.0 8.2 %collective-permute-start.8 = (bf16[256,256]{1,0:T(8,128)(2,1)S(1)}, bf16[256,256]{1,0:T(8,128)(2,1)S(1)}, u32[]{:S(2)}, u32[]{:S(2)}) collective-permute-start(bf16[256,256]{1,0:T(8,128)(2,1)S(1)} %get-tuple-element.61), channel_id=1, source_target_pairs={{0,4},{1,5},{2,6},{3,7},{4,0},{5,1},{6,2},{7,3},{8,12},{9,13},{10,... | collective-permute-start | bytes 393224 | tf_op jit(solution)/shard_map/ppermute | solution.py:35
  8.5 7.4 %collective-permute-start.9 = (bf16[256,256]{1,0:T(8,128)(2,1)S(1)}, bf16[256,256]{1,0:T(8,128)(2,1)S(1)}, u32[]{:S(2)}, u32[]{:S(2)}) collective-permute-start(bf16[256,256]{1,0:T(8,128)(2,1)S(1)} %get-tuple-element.62), channel_id=1, source_target_pairs={{0,5},{1,4},{2,7},{3,6},{4,1},{5,0},{6,3},{7,2},{8,13},{9,12},{10,... | collective-permute-start | bytes 393224 | tf_op jit(solution)/shard_map/ppermute | solution.py:35
  8.6 10.8 %dynamic-slice-start = ((s32[4096]{0:T(1024)}, s32[]{:T(128)}), s32[1024]{0:T(1024)S(1)}, s32[]{:S(2)}) async-start(s32[4096]{0:T(1024)} %param.9, s32[]{:T(128)} %select_n.69), calls=%async_computation | async-start | bytes 8704 | tf_op jit(solution)/shard_map/dynamic_slice | solution.py:572
  9.0 11.5 %collective-permute-start.4 = (bf16[256,512]{1,0:T(8,128)(2,1)S(1)}, bf16[256,512]{1,0:T(8,128)(2,1)S(1)}, u32[]{:S(2)}, u32[]{:S(2)}) collective-permute-start(bf16[256,512]{1,0:T(8,128)(2,1)S(1)} %get-tuple-element.56), channel_id=1, source_target_pairs={{0,1},{1,0},{2,3},{3,2},{4,5},{5,4},{6,7},{7,6},{8,9},{9,8},{10,11... | collective-permute-start | bytes 786440 | tf_op jit(solution)/shard_map/ppermute | solution.py:35
  11.0 15.2 %collective-permute-start.5 = (bf16[256,512]{1,0:T(8,128)(2,1)S(1)}, bf16[256,512]{1,0:T(8,128)(2,1)S(1)}, u32[]{:S(2)}, u32[]{:S(2)}) collective-permute-start(bf16[256,512]{1,0:T(8,128)(2,1)S(1)} %get-tuple-element.57), channel_id=1, source_target_pairs={{0,4},{1,5},{2,6},{3,7},{4,0},{5,1},{6,2},{7,3},{8,12},{9,13},{10,... | collective-permute-start | bytes 786440 | tf_op jit(solution)/shard_map/ppermute | solution.py:35
  12.5 13.7 %collective-permute-start.6 = (bf16[256,512]{1,0:T(8,128)(2,1)S(1)}, bf16[256,512]{1,0:T(8,128)(2,1)S(1)}, u32[]{:S(2)}, u32[]{:S(2)}) collective-permute-start(bf16[256,512]{1,0:T(8,128)(2,1)S(1)} %get-tuple-element.58), channel_id=1, source_target_pairs={{0,5},{1,4},{2,7},{3,6},{4,1},{5,0},{6,3},{7,2},{8,13},{9,12},{10,... | collective-permute-start | bytes 786440 | tf_op jit(solution)/shard_map/ppermute | solution.py:35
  15.9 12.7 %collective-permute-start.10 = (bf16[1024,256]{1,0:T(8,128)(2,1)S(1)}, bf16[1024,256]{1,0:T(8,128)(2,1)S(1)}, u32[]{:S(2)}, u32[]{:S(2)}) collective-permute-start(bf16[1024,256]{1,0:T(8,128)(2,1)S(1)} %join.1.refs_6_.refs_4_), channel_id=1, source_target_pairs={{0,8},{1,9},{2,10},{3,11},{4,12},{5,13},{6,14},{7,15},{8,16},{9,17... | collective-permute-start | bytes 1572872 | tf_op jit(solution)/shard_map/ppermute | solution.py:55
  34.9 14.5 %collective-permute-start.18 = (bf16[1024,256]{1,0:T(8,128)(2,1)S(1)}, bf16[1024,256]{1,0:T(8,128)(2,1)S(1)}, u32[]{:S(2)}, u32[]{:S(2)}) collective-permute-start(bf16[1024,256]{1,0:T(8,128)(2,1)S(1)} %get-tuple-element.90), channel_id=1, source_target_pairs={{8,0},{9,1},{10,2},{11,3},{12,4},{13,5},{14,6},{15,7},{16,8},{17,9... | collective-permute-start | bytes 1572872 | tf_op jit(solution)/shard_map/ppermute | solution.py:55
  36.4 6.8 %collective-permute-start.11 = (bf16[256,256]{1,0:T(8,128)(2,1)S(1)}, bf16[256,256]{1,0:T(8,128)(2,1)S(1)}, u32[]{:S(2)}, u32[]{:S(2)}) collective-permute-start(bf16[256,256]{1,0:T(8,128)(2,1)S(1)} %get-tuple-element.66), channel_id=1, source_target_pairs={{0,1},{1,0},{2,3},{3,2},{4,5},{5,4},{6,7},{7,6},{8,9},{9,8},{10,11... | collective-permute-start | bytes 393224 | tf_op jit(solution)/shard_map/ppermute | solution.py:35
  38.2 6.9 %collective-permute-start.12 = (bf16[256,256]{1,0:T(8,128)(2,1)S(1)}, bf16[256,256]{1,0:T(8,128)(2,1)S(1)}, u32[]{:S(2)}, u32[]{:S(2)}) collective-permute-start(bf16[256,256]{1,0:T(8,128)(2,1)S(1)} %get-tuple-element.67), channel_id=1, source_target_pairs={{0,4},{1,5},{2,6},{3,7},{4,0},{5,1},{6,2},{7,3},{8,12},{9,13},{10,... | collective-permute-start | bytes 393224 | tf_op jit(solution)/shard_map/ppermute | solution.py:35
  38.7 6.4 %collective-permute-start.13 = (bf16[256,256]{1,0:T(8,128)(2,1)S(1)}, bf16[256,256]{1,0:T(8,128)(2,1)S(1)}, u32[]{:S(2)}, u32[]{:S(2)}) collective-permute-start(bf16[256,256]{1,0:T(8,128)(2,1)S(1)} %get-tuple-element.68), channel_id=1, source_target_pairs={{0,5},{1,4},{2,7},{3,6},{4,1},{5,0},{6,3},{7,2},{8,13},{9,12},{10,... | collective-permute-start | bytes 393224 | tf_op jit(solution)/shard_map/ppermute | solution.py:35
  45.1 3.6 %collective-permute-start.14 = (bf16[128,1024]{1,0:T(8,128)(2,1)S(1)}, bf16[128,1024]{1,0:T(8,128)(2,1)S(1)}, u32[]{:S(2)}, u32[]{:S(2)}) collective-permute-start(bf16[128,1024]{1,0:T(8,128)(2,1)S(1)} %bottom.2), channel_id=1, source_target_pairs={{0,2},{1,3},{2,0},{3,1},{4,6},{5,7},{6,4},{7,5},{8,10},{9,11},{10,... | collective-permute-start | bytes 786440 | tf_op jit(solution)/shard_map/ppermute | solution.py:35
  45.2 6.7 %collective-permute-start.15 = (bf16[256,256]{1,0:T(8,128)(2,1)S(1)}, bf16[256,256]{1,0:T(8,128)(2,1)S(1)}, u32[]{:S(2)}, u32[]{:S(2)}) collective-permute-start(bf16[256,256]{1,0:T(8,128)(2,1)S(1)} %get-tuple-element.81), channel_id=1, source_target_pairs={{0,1},{1,0},{2,3},{3,2},{4,5},{5,4},{6,7},{7,6},{8,9},{9,8},{10,11... | collective-permute-start | bytes 393224 | tf_op jit(solution)/shard_map/ppermute | solution.py:35
  46.3 8.5 %collective-permute-start.16 = (bf16[256,256]{1,0:T(8,128)(2,1)S(1)}, bf16[256,256]{1,0:T(8,128)(2,1)S(1)}, u32[]{:S(2)}, u32[]{:S(2)}) collective-permute-start(bf16[256,256]{1,0:T(8,128)(2,1)S(1)} %get-tuple-element.82), channel_id=1, source_target_pairs={{0,4},{1,5},{2,6},{3,7},{4,0},{5,1},{6,2},{7,3},{8,12},{9,13},{10,... | collective-permute-start | bytes 393224 | tf_op jit(solution)/shard_map/ppermute | solution.py:35
  47.0 8.0 %collective-permute-start.17 = (bf16[256,256]{1,0:T(8,128)(2,1)S(1)}, bf16[256,256]{1,0:T(8,128)(2,1)S(1)}, u32[]{:S(2)}, u32[]{:S(2)}) collective-permute-start(bf16[256,256]{1,0:T(8,128)(2,1)S(1)} %get-tuple-element.83), channel_id=1, source_target_pairs={{0,5},{1,4},{2,7},{3,6},{4,1},{5,0},{6,3},{7,2},{8,13},{9,12},{10,... | collective-permute-start | bytes 393224 | tf_op jit(solution)/shard_map/ppermute | solution.py:35
  49.6 7.6 %collective-permute-start.19 = (bf16[256,256]{1,0:T(8,128)(2,1)S(1)}, bf16[256,256]{1,0:T(8,128)(2,1)S(1)}, u32[]{:S(2)}, u32[]{:S(2)}) collective-permute-start(bf16[256,256]{1,0:T(8,128)(2,1)S(1)} %get-tuple-element.92), channel_id=1, source_target_pairs={{0,1},{1,0},{2,3},{3,2},{4,5},{5,4},{6,7},{7,6},{8,9},{9,8},{10,11... | collective-permute-start | bytes 393224 | tf_op jit(solution)/shard_map/ppermute | solution.py:35
  51.3 9.0 %collective-permute-start.20 = (bf16[256,256]{1,0:T(8,128)(2,1)S(1)}, bf16[256,256]{1,0:T(8,128)(2,1)S(1)}, u32[]{:S(2)}, u32[]{:S(2)}) collective-permute-start(bf16[256,256]{1,0:T(8,128)(2,1)S(1)} %get-tuple-element.93), channel_id=1, source_target_pairs={{0,4},{1,5},{2,6},{3,7},{4,0},{5,1},{6,2},{7,3},{8,12},{9,13},{10,... | collective-permute-start | bytes 393224 | tf_op jit(solution)/shard_map/ppermute | solution.py:35
  51.9 8.5 %collective-permute-start.21 = (bf16[256,256]{1,0:T(8,128)(2,1)S(1)}, bf16[256,256]{1,0:T(8,128)(2,1)S(1)}, u32[]{:S(2)}, u32[]{:S(2)}) collective-permute-start(bf16[256,256]{1,0:T(8,128)(2,1)S(1)} %get-tuple-element.94), channel_id=1, source_target_pairs={{0,5},{1,4},{2,7},{3,6},{4,1},{5,0},{6,3},{7,2},{8,13},{9,12},{10,... | collective-permute-start | bytes 393224 | tf_op jit(solution)/shard_map/ppermute | solution.py:35
  60.4 2.0 %collective-permute-start.22 = (bf16[128,2048]{1,0:T(8,128)(2,1)S(1)}, bf16[128,2048]{1,0:T(8,128)(2,1)S(1)}, u32[]{:S(2)}, u32[]{:S(2)}) collective-permute-start(bf16[128,2048]{1,0:T(8,128)(2,1)S(1)} %bottom.3), channel_id=1, source_target_pairs={{0,2},{1,3},{2,0},{3,1},{4,6},{5,7},{6,4},{7,5},{8,10},{9,11},{10,... | collective-permute-start | bytes 1572872 | tf_op jit(solution)/shard_map/ppermute | solution.py:35

commit v17 on v13

--- a/solution.py
+++ b/solution.py
@@ -317,8 +317,8 @@
 def own_body(size, core, masks, tok, group, *refs):
     take = taker(refs)
     (seg_k, seg_q), qg_pieces, (kv,) = take(2), take(len(masks)), take(1)
-    e_own, out_part, stats = take(3)
-    qg, ka, vt, s_scr = take(4)
+    e_own, out_part, stats, qg = take(4)
+    ka, vt, s_scr = take(3)
     wide, tiles = group * TILE, tok // TILE
     place_rows(size, core, masks, qg_pieces, qg)
     ka[:, :HEAD_DIM] = kv[:, :HEAD_DIM]
@@ -348,12 +348,10 @@
 
 def forward_body(size, core, masks, reach, tok, group, *refs):
     take = taker(refs)
-    (seg_k, seg_q), qg_pieces, kvs = take(2), take(len(masks)), take(reach)
-    out_own, stats = take(2)
+    (seg_k, seg_q, qg), kvs, (out_own, stats) = take(3), take(reach), take(2)
     out_pieces, sent, (outs, own_scale, dq_part) = take(len(masks)), take(reach), take(3)
-    qg, ka, va, kt, vt, dk, dv, s_scr, e_scr, dp_scr, ds_scr, g_scr = take(12)
+    ka, va, kt, vt, dk, dv, s_scr, e_scr, dp_scr, ds_scr, g_scr = take(11)
     wide, tiles = group * TILE, tok // TILE
-    place_rows(size, core, masks, qg_pieces, qg)
     ka[:, HEAD_DIM:] = seg_k[:WINDOW, :]
     for lag in range(1, reach + 1):
         there = slice((reach - lag) * tok, (reach - lag + 1) * tok)
@@ -417,11 +415,10 @@
 
 def backward_body(size, core, masks, tok, group, *refs):
     take = taker(refs)
-    qg_pieces, (kv, e_own, outs, own_scale, dq_part) = take(len(masks)), take(5)
+    qg, kv, e_own, outs, own_scale, dq_part = take(6)
     dq_pieces, (dkv,) = take(len(masks)), take(1)
-    qg, dqs, va, kt, dk, dv, dp_scr, ds_scr, g_scr = take(9)
+    dqs, va, kt, dk, dv, dp_scr, ds_scr, g_scr = take(8)
     wide = group * TILE
-    place_rows(size, core, masks, qg_pieces, qg)
     kt[...] = kv[:, :HEAD_DIM].T
     set_values(va, kv[:, HEAD_DIM:])
 
@@ -476,9 +473,9 @@
             jax.ShapeDtypeStruct((own_rows(tiles - 1).stop, wide), BF16),
             jax.ShapeDtypeStruct((HEAD_DIM, tiles * wide), F32),
             jax.ShapeDtypeStruct((2 * tiles, wide), F32),
+            jax.ShapeDtypeStruct((tok, cols), BF16),
         ],
         [
-            pltpu.VMEM((tok, cols), BF16),
             pltpu.VMEM((tok, 2 * HEAD_DIM), BF16),
             pltpu.VMEM((HEAD_DIM, tok), BF16),
             pltpu.VMEM((2, tok, wide), F32),
@@ -492,8 +489,8 @@
 
 
 def forward(documents, qg, lags, carried, size):
-    rows, cols = qg[0].shape
-    tok, count, reach = len(qg) * rows, len(qg), len(lags)
+    (tok, cols), count, reach = qg.shape, len(chip_masks(size)), len(lags)
+    rows = tok // count
     group = cols // (2 * HEAD_DIM)
     wide, tiles = group * TILE, tok // TILE
     half = jax.ShapeDtypeStruct((tok, 2 * HEAD_DIM), BF16)
@@ -504,7 +501,6 @@
         jax.ShapeDtypeStruct((HEAD_DIM, tiles * wide), F32),
     ]
     scratch = [
-        pltpu.VMEM((tok, cols), BF16),
         pltpu.VMEM((WINDOW, 2 * HEAD_DIM), BF16),
         pltpu.VMEM((WINDOW, 2 * HEAD_DIM), BF16),
         pltpu.VMEM((HEAD_DIM, WINDOW), BF16),
@@ -526,7 +522,7 @@
         6 * tok * group * (WINDOW + TILE) * HEAD_DIM,
         "forward",
         *documents,
-        *qg,
+        qg,
         *lags,
         *carried,
     )
@@ -534,8 +530,8 @@
 
 
 def backward(qg, kv, carried, size):
-    rows, cols = qg[0].shape
-    tok, count = len(qg) * rows, len(qg)
+    (tok, cols), count = qg.shape, len(chip_masks(size))
+    rows = tok // count
     group = cols // (2 * HEAD_DIM)
     wide = group * TILE
     results = attend_call(
@@ -543,7 +539,6 @@
         [jax.ShapeDtypeStruct((rows, cols // 2), BF16)] * count
         + [jax.ShapeDtypeStruct((tok, 2 * HEAD_DIM), F32)],
         [
-            pltpu.VMEM((tok, cols), BF16),
             pltpu.VMEM((tok, cols // 2), BF16),
             pltpu.VMEM((tok, 2 * HEAD_DIM), BF16),
             pltpu.VMEM((HEAD_DIM, tok), BF16),
@@ -555,7 +550,7 @@
         ],
         4 * tok * group * (WINDOW + TILE) * HEAD_DIM,
         "backward",
-        *qg,
+        qg,
         kv,
         *carried,
     )
@@ -582,6 +577,7 @@
     assert reach * tok == WINDOW and device_count() % size == 0
 
     got = [swap(array, core_mask()) for array in (key, value, query, grad_out)]
+    key, value = after(key, value)
     pieces = list(gather_cores((key, value), got[:2], size))
     pieces[0], query, grad_out, segment_ids = after(pieces[0], query, grad_out, segment_ids)
     documents = document_columns(segment_ids, tok, size)
@@ -589,7 +585,7 @@
     lags = [shifted(kv, lag * size) for lag in range(1, reach + 1)]
     qg = swap_chips(gather_cores((query, grad_out), got[2:], size), size)
 
-    e_own, *partial = forward_own(documents, qg, kv, size)
+    e_own, *partial, qg = forward_own(documents, qg, kv, size)
     out, sent, carried = forward(documents, qg, lags, partial, size)
     backs = [shifted(sent[lag - 1], -lag * size) for lag in range(1, reach + 1)]
     out = swap_chips(out, size)

time: 62.8 us -> 61.9 us (0.986)
  local copies, waits for them, and re-layouts: 2.03 us -> 1.22 us
    slice x4 -> x3, local copies, waits for them, and re-layouts: 1.99 us -> 1.18 us  [this_core(): shares = [array[:, r * width:(r + 1) * width] for r in range(size)]]
  transfers between devices with their start and end apart: 22 -> 22, of which waited for: 11 -> 11; matrix products, arithmetic and copies ran while one was open for 4% -> 3% of each run, Pallas kernels for 10% -> 10%
where the time goes in v17:
time: 61.9 us; the launch traced here: 61.7 us
  starting transfers between devices  26.6 us (43%)
  waiting for transfers between devices  18.4 us (30%)
  Pallas kernels  13.7 us (22%)
  local copies, waits for them, and re-layouts  1.22 us (2%)
  between operations  1.1 us (2%)
  other arithmetic  0.73 us (1%)
    ppermute x20, starting transfers between devices, swap(): lax.ppermute(value, BOTH, [(i, i ^ mask) for i in range(device_count())])  21.6 us
    ppermute x20, waiting for transfers between devices, swap(): lax.ppermute(value, BOTH, [(i, i ^ mask) for i in range(device_count())])  17.4 us
    pallas_call x3, Pallas kernels, attend_call(): pl.pallas_call(kernel, out_shape=out_shape, in_specs=[VMEM] * len(args),...  11.8 us
    ppermute x2, starting transfers between devices, shifted(): return lax.ppermute(value, BOTH, pairs)  4.99 us
    pallas_call x1, Pallas kernels, spread_cores(): pl.pallas_call(functools.partial(spread_body, size, core_mask(), chip_mas...  1.39 us
  transfers between devices with their start and end apart: 22, of which 11 were waited for; matrix products, arithmetic and copies ran while one was open for 3% of the time, Pallas kernels for 10%

profile of v17, /device:TPU:0, one launch (start us, length us, event | category | flops | bytes accessed | tf_op | source)
XLA Modules:
  0.0 61.7 jit_solution(15516387200231228431)
XLA Ops:
  0.7 0.5 collective-permute-start
  1.8 1.1 %fusion.2 = (bf16[128,256]{1,0:T(8,128)(2,1)S(1)}, bf16[128,256]{1,0:T(8,128)(2,1)S(1)}, bf16[128,256]{1,0:T(8,128)(2,1)S(1)}, bf16[128,256]{1,0:T(8,128)(2,1)S(...) fusion(bf16[128,1024]{1,0:T(8,128)(2,1)} %param.7, ...), kind=kLoop, calls=%fused_computation.11 | loop fusion | bytes 1048576 | tf_op jit(solution)/shard_map/slice | solution.py:94
  3.2 3.0 %collective-permute-start.7 = (bf16[256,256]{1,0:T(8,128)(2,1)S(1)}, bf16[256,256]{1,0:T(8,128)(2,1)S(1)}, u32[]{:S(2)}, u32[]{:S(2)}) collective-permute-start(bf16[256,256]{1,0:T(8,128)(2,1)S(1)} %get-tuple-element.58), channel_id=1, source_target_pairs={{0,1},{1,0},{2,3},{3,2},{4,5},{5,4},{6,7},{7,6},{8,9},{9,8},{10,11... | collective-permute-start | bytes 393224 | tf_op jit(solution)/shard_map/ppermute | solution.py:35
  6.2 1.5 %collective-permute-start.8 = (bf16[256,256]{1,0:T(8,128)(2,1)S(1)}, bf16[256,256]{1,0:T(8,128)(2,1)S(1)}, u32[]{:S(2)}, u32[]{:S(2)}) collective-permute-start(bf16[256,256]{1,0:T(8,128)(2,1)S(1)} %get-tuple-element.59), channel_id=1, source_target_pairs={{0,4},{1,5},{2,6},{3,7},{4,0},{5,1},{6,2},{7,3},{8,12},{9,13},{10,... | collective-permute-start | bytes 393224 | tf_op jit(solution)/shard_map/ppermute | solution.py:35
  8.2 2.0 %collective-permute-start.4 = (bf16[256,512]{1,0:T(8,128)(2,1)S(1)}, bf16[256,512]{1,0:T(8,128)(2,1)S(1)}, u32[]{:S(2)}, u32[]{:S(2)}) collective-permute-start(bf16[256,512]{1,0:T(8,128)(2,1)S(1)} %get-tuple-element.54), channel_id=1, source_target_pairs={{0,1},{1,0},{2,3},{3,2},{4,5},{5,4},{6,7},{7,6},{8,9},{9,8},{10,11... | collective-permute-start | bytes 786440 | tf_op jit(solution)/shard_map/ppermute | solution.py:35
  10.2 1.5 %collective-permute-start.5 = (bf16[256,512]{1,0:T(8,128)(2,1)S(1)}, bf16[256,512]{1,0:T(8,128)(2,1)S(1)}, u32[]{:S(2)}, u32[]{:S(2)}) collective-permute-start(bf16[256,512]{1,0:T(8,128)(2,1)S(1)} %get-tuple-element.55), channel_id=1, source_target_pairs={{0,4},{1,5},{2,6},{3,7},{4,0},{5,1},{6,2},{7,3},{8,12},{9,13},{10,... | collective-permute-start | bytes 786440 | tf_op jit(solution)/shard_map/ppermute | solution.py:35
  11.7 1.7 %collective-permute-start.6 = (bf16[256,512]{1,0:T(8,128)(2,1)S(1)}, bf16[256,512]{1,0:T(8,128)(2,1)S(1)}, u32[]{:S(2)}, u32[]{:S(2)}) collective-permute-start(bf16[256,512]{1,0:T(8,128)(2,1)S(1)} %get-tuple-element.56), channel_id=1, source_target_pairs={{0,5},{1,4},{2,7},{3,6},{4,1},{5,0},{6,3},{7,2},{8,13},{9,12},{10,... | collective-permute-start | bytes 786440 | tf_op jit(solution)/shard_map/ppermute | solution.py:35
  13.8 0.6 collective-permute-done.8.refs_2_
  14.4 0.7 %collective-permute-done.9.refs_3_ = bf16[256,256]{1,0:T(8,128)(2,1)S(1)} collective-permute-done((bf16[256,256]{1,0:T(8,128)(2,1)S(1)}, bf16[256,256]{1,0:T(8,128)(2,1)S(1)}, u32[]{:S(2)}, u32[]{:S(2)}) %collective-permute-start.9) | collective-permute-done | bytes 131104 | tf_op jit(solution)/shard_map/ppermute | solution.py:35
  15.1 3.5 %collective-permute-start.10 = (bf16[1024,256]{1,0:T(8,128)(2,1)S(1)}, bf16[1024,256]{1,0:T(8,128)(2,1)S(1)}, u32[]{:S(2)}, u32[]{:S(2)}) collective-permute-start(bf16[1024,256]{1,0:T(8,128)(2,1)S(1)} %join.1.refs_6_.refs_1_), channel_id=1, source_target_pairs={{0,8},{1,9},{2,10},{3,11},{4,12},{5,13},{6,14},{7,15},{8,16},{9,17... | collective-permute-start | bytes 1572872 | tf_op jit(solution)/shard_map/ppermute | solution.py:55
  18.8 0.8 %collective-permute-done.4.refs_3_ = bf16[256,512]{1,0:T(8,128)(2,1)S(1)} collective-permute-done((bf16[256,512]{1,0:T(8,128)(2,1)S(1)}, bf16[256,512]{1,0:T(8,128)(2,1)S(1)}, u32[]{:S(2)}, u32[]{:S(2)}) %collective-permute-start.4) | collective-permute-done | bytes 262176 | tf_op jit(solution)/shard_map/ppermute | solution.py:35
  19.7 5.7 %collective-permute-done.5.refs_4_ = bf16[256,512]{1,0:T(8,128)(2,1)S(1)} collective-permute-done((bf16[256,512]{1,0:T(8,128)(2,1)S(1)}, bf16[256,512]{1,0:T(8,128)(2,1)S(1)}, u32[]{:S(2)}, u32[]{:S(2)}) %collective-permute-start.5) | collective-permute-done | bytes 262176 | tf_op jit(solution)/shard_map/ppermute | solution.py:35
  25.4 2.4 %forward_own.1 = (bf16[4608,256]{1,0:T(8,128)(2,1)S(1)}, f32[128,2048]{1,0:T(8,128)S(1)}, f32[16,256]{1,0:T(8,128)S(1)}, bf16[1024,512]{1,0:T(8,128)(2,1)S(1)}) custom-call(bf16[2048,128]{1,0:T(8,128)(2,1)S(1)} %select_convert_fusion.refs_0_, bf16[1024,128]{1,0:T(8,128)(2,1)S(1)} %select_convert_fusion.1.refs_1_, ...), custom_call_target="tpu_custom_call" | custom-call | flops 4831838208 | bytes 8388608 | tf_op jit(solution)/shard_map/forward_own/pallas_call | solution.py:451
  27.8 6.2 %forward.1 = (bf16[256,256]{1,0:T(8,128)(2,1)S(1)}, bf16[256,256]{1,0:T(8,128)(2,1)S(1)}, bf16[256,256]{1,0:T(8,128)(2,1)S(1)}, bf16[256,256]{1,0:T(8,128)(2,1)S...) custom-call(bf16[2048,128]{1,0:T(8,128)(2,1)S(1)} %select_convert_fu, ...), custom_call_target="tpu_custom_call" | custom-call | flops 1811939328 | bytes 8388608 | tf_op jit(solution)/shard_map/forward/pallas_call | solution.py:451
  34.1 1.5 %collective-permute-start.17 = (bf16[1024,256]{1,0:T(8,128)(2,1)S(1)}, bf16[1024,256]{1,0:T(8,128)(2,1)S(1)}, u32[]{:S(2)}, u32[]{:S(2)}) collective-permute-start(bf16[1024,256]{1,0:T(8,128)(2,1)S(1)} %get-tuple-element.85), channel_id=1, source_target_pairs={{8,0},{9,1},{10,2},{11,3},{12,4},{13,5},{14,6},{15,7},{16,8},{17,9... | collective-permute-start | bytes 1572872 | tf_op jit(solution)/shard_map/ppermute | solution.py:55
  35.5 1.8 %collective-permute-start.11 = (bf16[256,256]{1,0:T(8,128)(2,1)S(1)}, bf16[256,256]{1,0:T(8,128)(2,1)S(1)}, u32[]{:S(2)}, u32[]{:S(2)}) collective-permute-start(bf16[256,256]{1,0:T(8,128)(2,1)S(1)} %get-tuple-element.65), channel_id=1, source_target_pairs={{0,1},{1,0},{2,3},{3,2},{4,5},{5,4},{6,7},{7,6},{8,9},{9,8},{10,11... | collective-permute-start | bytes 393224 | tf_op jit(solution)/shard_map/ppermute | solution.py:35
  37.3 0.5 collective-permute-start.12
  37.8 1.3 %collective-permute-start.13 = (bf16[256,256]{1,0:T(8,128)(2,1)S(1)}, bf16[256,256]{1,0:T(8,128)(2,1)S(1)}, u32[]{:S(2)}, u32[]{:S(2)}) collective-permute-start(bf16[256,256]{1,0:T(8,128)(2,1)S(1)} %get-tuple-element.67), channel_id=1, source_target_pairs={{0,5},{1,4},{2,7},{3,6},{4,1},{5,0},{6,3},{7,2},{8,13},{9,12},{10,... | collective-permute-start | bytes 393224 | tf_op jit(solution)/shard_map/ppermute | solution.py:35
  39.1 3.2 %backward.1 = (bf16[256,256]{1,0:T(8,128)(2,1)S(1)}, bf16[256,256]{1,0:T(8,128)(2,1)S(1)}, bf16[256,256]{1,0:T(8,128)(2,1)S(1)}, bf16[256,256]{1,0:T(8,128)(2,1)S(1)}, f32[1024,256]{1,0:T(8,128)S(1)}) custom-call(bf16[1024,512]{1,0:T(8,128)(2,1)S(1)} %get-tuple-element.61.refs_2_.refs_0_, bf16[1024,256]{1,0:T(8,128)(2,1)S(1)} %join.1.refs_6_.refs_1_, ...), custom_call_target="tpu_custom_call" | custom-call | flops 1207959552 | bytes 8388608 | tf_op jit(solution)/shard_map/backward/pallas_call | solution.py:451
  42.3 1.9 %collective-permute-done.12.refs_2_ = bf16[256,256]{1,0:T(8,128)(2,1)S(1)} collective-permute-done((bf16[256,256]{1,0:T(8,128)(2,1)S(1)}, bf16[256,256]{1,0:T(8,128)(2,1)S(1)}, u32[]{:S(2)}, u32[]{:S(2)}) %collective-permute-start.12) | collective-permute-done | bytes 131104 | tf_op jit(solution)/shard_map/ppermute | solution.py:35
  44.2 1.1 %collective-permute-start.14 = (bf16[256,256]{1,0:T(8,128)(2,1)S(1)}, bf16[256,256]{1,0:T(8,128)(2,1)S(1)}, u32[]{:S(2)}, u32[]{:S(2)}) collective-permute-start(bf16[256,256]{1,0:T(8,128)(2,1)S(1)} %get-tuple-element.81), channel_id=1, source_target_pairs={{0,1},{1,0},{2,3},{3,2},{4,5},{5,4},{6,7},{7,6},{8,9},{9,8},{10,11... | collective-permute-start | bytes 393224 | tf_op jit(solution)/shard_map/ppermute | solution.py:35
  45.3 0.7 %collective-permute-start.15 = (bf16[256,256]{1,0:T(8,128)(2,1)S(1)}, bf16[256,256]{1,0:T(8,128)(2,1)S(1)}, u32[]{:S(2)}, u32[]{:S(2)}) collective-permute-start(bf16[256,256]{1,0:T(8,128)(2,1)S(1)} %get-tuple-element.82), channel_id=1, source_target_pairs={{0,4},{1,5},{2,6},{3,7},{4,0},{5,1},{6,2},{7,3},{8,12},{9,13},{10,... | collective-permute-start | bytes 393224 | tf_op jit(solution)/shard_map/ppermute | solution.py:35
  45.9 1.8 %collective-permute-start.16 = (bf16[256,256]{1,0:T(8,128)(2,1)S(1)}, bf16[256,256]{1,0:T(8,128)(2,1)S(1)}, u32[]{:S(2)}, u32[]{:S(2)}) collective-permute-start(bf16[256,256]{1,0:T(8,128)(2,1)S(1)} %get-tuple-element.83), channel_id=1, source_target_pairs={{0,5},{1,4},{2,7},{3,6},{4,1},{5,0},{6,3},{7,2},{8,13},{9,12},{10,... | collective-permute-start | bytes 393224 | tf_op jit(solution)/shard_map/ppermute | solution.py:35
  47.7 0.9 %collective-permute-done.17.refs_1_ = bf16[1024,256]{1,0:T(8,128)(2,1)S(1)} collective-permute-done((bf16[1024,256]{1,0:T(8,128)(2,1)S(1)}, bf16[1024,256]{1,0:T(8,128)(2,1)S(1)}, u32[]{:S(2)}, u32[]{:S(2)}) %collective-permute-start.17) | collective-permute-done | bytes 524320 | tf_op jit(solution)/shard_map/ppermute | solution.py:55
  48.7 1.7 %collective-permute-start.18 = (bf16[256,256]{1,0:T(8,128)(2,1)S(1)}, bf16[256,256]{1,0:T(8,128)(2,1)S(1)}, u32[]{:S(2)}, u32[]{:S(2)}) collective-permute-start(bf16[256,256]{1,0:T(8,128)(2,1)S(1)} %get-tuple-element.87), channel_id=1, source_target_pairs={{0,1},{1,0},{2,3},{3,2},{4,5},{5,4},{6,7},{7,6},{8,9},{9,8},{10,11... | collective-permute-start | bytes 393224 | tf_op jit(solution)/shard_map/ppermute | solution.py:35
  50.4 0.6 collective-permute-start.19
  51.0 1.3 %collective-permute-start.20 = (bf16[256,256]{1,0:T(8,128)(2,1)S(1)}, bf16[256,256]{1,0:T(8,128)(2,1)S(1)}, u32[]{:S(2)}, u32[]{:S(2)}) collective-permute-start(bf16[256,256]{1,0:T(8,128)(2,1)S(1)} %get-tuple-element.89), channel_id=1, source_target_pairs={{0,5},{1,4},{2,7},{3,6},{4,1},{5,0},{6,3},{7,2},{8,13},{9,12},{10,... | collective-permute-start | bytes 393224 | tf_op jit(solution)/shard_map/ppermute | solution.py:35
  52.2 1.0 %collective-permute-done.16.refs_7_ = bf16[256,256]{1,0:T(8,128)(2,1)S(1)} collective-permute-done((bf16[256,256]{1,0:T(8,128)(2,1)S(1)}, bf16[256,256]{1,0:T(8,128)(2,1)S(1)}, u32[]{:S(2)}, u32[]{:S(2)}) %collective-permute-start.16) | collective-permute-done | bytes 131104 | tf_op jit(solution)/shard_map/ppermute | solution.py:35
  53.2 2.5 %collective-permute-done.18.refs_9_ = bf16[256,256]{1,0:T(8,128)(2,1)S(1)} collective-permute-done((bf16[256,256]{1,0:T(8,128)(2,1)S(1)}, bf16[256,256]{1,0:T(8,128)(2,1)S(1)}, u32[]{:S(2)}, u32[]{:S(2)}) %collective-permute-start.18) | collective-permute-done | bytes 131104 | tf_op jit(solution)/shard_map/ppermute | solution.py:35
  55.7 2.0 %collective-permute-done.19.refs_10_ = bf16[256,256]{1,0:T(8,128)(2,1)S(1)} collective-permute-done((bf16[256,256]{1,0:T(8,128)(2,1)S(1)}, bf16[256,256]{1,0:T(8,128)(2,1)S(1)}, u32[]{:S(2)}, u32[]{:S(2)}) %collective-permute-start.19) | collective-permute-done | bytes 131104 | tf_op jit(solution)/shard_map/ppermute | solution.py:35
  57.8 2.3 %collective-permute-done.21.refs_12_ = bf16[128,3072]{1,0:T(8,128)(2,1)S(1)} collective-permute-done((bf16[128,3072]{1,0:T(8,128)(2,1)S(1)}, bf16[128,3072]{1,0:T(8,128)(2,1)S(1)}, u32[]{:S(2)}, u32[]{:S(2)}) %collective-permute-start.21) | collective-permute-done | bytes 786464 | tf_op jit(solution)/shard_map/ppermute | solution.py:35
  60.1 1.4 %spread.1 = (bf16[128,2048]{1,0:T(8,128)(2,1)}, bf16[128,2048]{1,0:T(8,128)(2,1)}, bf16[128,1024]{1,0:T(8,128)(2,1)}, bf16[128,1024]{1,0:T(8,128)(2,1)}) custom-call(bf16[256,256]{1,0:T(8,128)(2,1)S(1)} %get-tuple-element.76.refs_0_, bf16[256,256]{1,0:T(8,128)(2,1)S(1)} %collective-permute-done.11.refs_1_, ...), custom_call_target="tpu_custom_call" | custom-call | tf_op jit(solution)/shard_map/spread/pallas_call | solution.py:201
  (39 shorter events, 2.2 us)
Async XLA Ops:
  0.6 7.1 %copy-start = (bf16[128,2048]{1,0:T(8,128)(2,1)S(1)}, bf16[128,2048]{1,0:T(8,128)(2,1)}, u32[]{:S(2)}) copy-start(bf16[128,2048]{1,0:T(8,128)(2,1)} %param.5) | copy-start | bytes 1572868
  0.6 7.2 %copy-start.1 = (bf16[128,2048]{1,0:T(8,128)(2,1)S(1)}, bf16[128,2048]{1,0:T(8,128)(2,1)}, u32[]{:S(2)}) copy-start(bf16[128,2048]{1,0:T(8,128)(2,1)} %param.8) | copy-start | bytes 1572868
  0.7 2.4 %collective-permute-start = (bf16[128,1024]{1,0:T(8,128)(2,1)}, bf16[128,1024]{1,0:T(8,128)(2,1)S(1)}, u32[]{:S(2)}, u32[]{:S(2)}) collective-permute-start(bf16[128,1024]{1,0:T(8,128)(2,1)} %param.6), channel_id=1, source_target_pairs={{0,2},{1,3},{2,0},{3,1},{4,6},{5,7},{6,4},{7,5},{8,10},{9,11},{10,... | collective-permute-start | bytes 786440 | tf_op jit(solution)/shard_map/ppermute | solution.py:35
  1.2 1.9 %collective-permute-start.1 = (bf16[128,1024]{1,0:T(8,128)(2,1)}, bf16[128,1024]{1,0:T(8,128)(2,1)S(1)}, u32[]{:S(2)}, u32[]{:S(2)}) collective-permute-start(bf16[128,1024]{1,0:T(8,128)(2,1)} %param.7), channel_id=1, source_target_pairs={{0,2},{1,3},{2,0},{3,1},{4,6},{5,7},{6,4},{7,5},{8,10},{9,11},{10,... | collective-permute-start | bytes 786440 | tf_op jit(solution)/shard_map/ppermute | solution.py:35
  1.2 6.7 %collective-permute-start.2 = (bf16[128,2048]{1,0:T(8,128)(2,1)}, bf16[128,2048]{1,0:T(8,128)(2,1)S(1)}, u32[]{:S(2)}, u32[]{:S(2)}) collective-permute-start(bf16[128,2048]{1,0:T(8,128)(2,1)} %param.5), channel_id=1, source_target_pairs={{0,2},{1,3},{2,0},{3,1},{4,6},{5,7},{6,4},{7,5},{8,10},{9,11},{10,... | collective-permute-start | bytes 1572872 | tf_op jit(solution)/shard_map/ppermute | solution.py:35
  1.7 6.3 %collective-permute-start.3 = (bf16[128,2048]{1,0:T(8,128)(2,1)}, bf16[128,2048]{1,0:T(8,128)(2,1)S(1)}, u32[]{:S(2)}, u32[]{:S(2)}) collective-permute-start(bf16[128,2048]{1,0:T(8,128)(2,1)} %param.8), channel_id=1, source_target_pairs={{0,2},{1,3},{2,0},{3,1},{4,6},{5,7},{6,4},{7,5},{8,10},{9,11},{10,... | collective-permute-start | bytes 1572872 | tf_op jit(solution)/shard_map/ppermute | solution.py:35
  2.9 5.0 %copy-start.2 = (s32[4096]{0:T(1024)S(1)}, s32[4096]{0:T(1024)}, u32[]{:S(2)}) copy-start(s32[4096]{0:T(1024)} %param.9) | copy-start | bytes 49156
  3.2 8.5 %collective-permute-start.7 = (bf16[256,256]{1,0:T(8,128)(2,1)S(1)}, bf16[256,256]{1,0:T(8,128)(2,1)S(1)}, u32[]{:S(2)}, u32[]{:S(2)}) collective-permute-start(bf16[256,256]{1,0:T(8,128)(2,1)S(1)} %get-tuple-element.58), channel_id=1, source_target_pairs={{0,1},{1,0},{2,3},{3,2},{4,5},{5,4},{6,7},{7,6},{8,9},{9,8},{10,11... | collective-permute-start | bytes 393224 | tf_op jit(solution)/shard_map/ppermute | solution.py:35
  6.2 8.2 %collective-permute-start.8 = (bf16[256,256]{1,0:T(8,128)(2,1)S(1)}, bf16[256,256]{1,0:T(8,128)(2,1)S(1)}, u32[]{:S(2)}, u32[]{:S(2)}) collective-permute-start(bf16[256,256]{1,0:T(8,128)(2,1)S(1)} %get-tuple-element.59), channel_id=1, source_target_pairs={{0,4},{1,5},{2,6},{3,7},{4,0},{5,1},{6,2},{7,3},{8,12},{9,13},{10,... | collective-permute-start | bytes 393224 | tf_op jit(solution)/shard_map/ppermute | solution.py:35
  7.7 7.4 %collective-permute-start.9 = (bf16[256,256]{1,0:T(8,128)(2,1)S(1)}, bf16[256,256]{1,0:T(8,128)(2,1)S(1)}, u32[]{:S(2)}, u32[]{:S(2)}) collective-permute-start(bf16[256,256]{1,0:T(8,128)(2,1)S(1)} %get-tuple-element.60), channel_id=1, source_target_pairs={{0,5},{1,4},{2,7},{3,6},{4,1},{5,0},{6,3},{7,2},{8,13},{9,12},{10,... | collective-permute-start | bytes 393224 | tf_op jit(solution)/shard_map/ppermute | solution.py:35
  7.8 10.8 %dynamic-slice-start = ((s32[4096]{0:T(1024)}, s32[]{:T(128)}), s32[1024]{0:T(1024)S(1)}, s32[]{:S(2)}) async-start(s32[4096]{0:T(1024)} %param.9, s32[]{:T(128)} %select_n.69), calls=%async_computation | async-start | bytes 8704 | tf_op jit(solution)/shard_map/dynamic_slice | solution.py:564
  8.2 11.5 %collective-permute-start.4 = (bf16[256,512]{1,0:T(8,128)(2,1)S(1)}, bf16[256,512]{1,0:T(8,128)(2,1)S(1)}, u32[]{:S(2)}, u32[]{:S(2)}) collective-permute-start(bf16[256,512]{1,0:T(8,128)(2,1)S(1)} %get-tuple-element.54), channel_id=1, source_target_pairs={{0,1},{1,0},{2,3},{3,2},{4,5},{5,4},{6,7},{7,6},{8,9},{9,8},{10,11... | collective-permute-start | bytes 786440 | tf_op jit(solution)/shard_map/ppermute | solution.py:35
  10.2 15.2 %collective-permute-start.5 = (bf16[256,512]{1,0:T(8,128)(2,1)S(1)}, bf16[256,512]{1,0:T(8,128)(2,1)S(1)}, u32[]{:S(2)}, u32[]{:S(2)}) collective-permute-start(bf16[256,512]{1,0:T(8,128)(2,1)S(1)} %get-tuple-element.55), channel_id=1, source_target_pairs={{0,4},{1,5},{2,6},{3,7},{4,0},{5,1},{6,2},{7,3},{8,12},{9,13},{10,... | collective-permute-start | bytes 786440 | tf_op jit(solution)/shard_map/ppermute | solution.py:35
  11.7 13.7 %collective-permute-start.6 = (bf16[256,512]{1,0:T(8,128)(2,1)S(1)}, bf16[256,512]{1,0:T(8,128)(2,1)S(1)}, u32[]{:S(2)}, u32[]{:S(2)}) collective-permute-start(bf16[256,512]{1,0:T(8,128)(2,1)S(1)} %get-tuple-element.56), channel_id=1, source_target_pairs={{0,5},{1,4},{2,7},{3,6},{4,1},{5,0},{6,3},{7,2},{8,13},{9,12},{10,... | collective-permute-start | bytes 786440 | tf_op jit(solution)/shard_map/ppermute | solution.py:35
  15.1 12.7 %collective-permute-start.10 = (bf16[1024,256]{1,0:T(8,128)(2,1)S(1)}, bf16[1024,256]{1,0:T(8,128)(2,1)S(1)}, u32[]{:S(2)}, u32[]{:S(2)}) collective-permute-start(bf16[1024,256]{1,0:T(8,128)(2,1)S(1)} %join.1.refs_6_.refs_1_), channel_id=1, source_target_pairs={{0,8},{1,9},{2,10},{3,11},{4,12},{5,13},{6,14},{7,15},{8,16},{9,17... | collective-permute-start | bytes 1572872 | tf_op jit(solution)/shard_map/ppermute | solution.py:55
  34.1 14.5 %collective-permute-start.17 = (bf16[1024,256]{1,0:T(8,128)(2,1)S(1)}, bf16[1024,256]{1,0:T(8,128)(2,1)S(1)}, u32[]{:S(2)}, u32[]{:S(2)}) collective-permute-start(bf16[1024,256]{1,0:T(8,128)(2,1)S(1)} %get-tuple-element.85), channel_id=1, source_target_pairs={{8,0},{9,1},{10,2},{11,3},{12,4},{13,5},{14,6},{15,7},{16,8},{17,9... | collective-permute-start | bytes 1572872 | tf_op jit(solution)/shard_map/ppermute | solution.py:55
  35.5 6.8 %collective-permute-start.11 = (bf16[256,256]{1,0:T(8,128)(2,1)S(1)}, bf16[256,256]{1,0:T(8,128)(2,1)S(1)}, u32[]{:S(2)}, u32[]{:S(2)}) collective-permute-start(bf16[256,256]{1,0:T(8,128)(2,1)S(1)} %get-tuple-element.65), channel_id=1, source_target_pairs={{0,1},{1,0},{2,3},{3,2},{4,5},{5,4},{6,7},{7,6},{8,9},{9,8},{10,11... | collective-permute-start | bytes 393224 | tf_op jit(solution)/shard_map/ppermute | solution.py:35
  37.3 6.9 %collective-permute-start.12 = (bf16[256,256]{1,0:T(8,128)(2,1)S(1)}, bf16[256,256]{1,0:T(8,128)(2,1)S(1)}, u32[]{:S(2)}, u32[]{:S(2)}) collective-permute-start(bf16[256,256]{1,0:T(8,128)(2,1)S(1)} %get-tuple-element.66), channel_id=1, source_target_pairs={{0,4},{1,5},{2,6},{3,7},{4,0},{5,1},{6,2},{7,3},{8,12},{9,13},{10,... | collective-permute-start | bytes 393224 | tf_op jit(solution)/shard_map/ppermute | solution.py:35
  37.8 6.4 %collective-permute-start.13 = (bf16[256,256]{1,0:T(8,128)(2,1)S(1)}, bf16[256,256]{1,0:T(8,128)(2,1)S(1)}, u32[]{:S(2)}, u32[]{:S(2)}) collective-permute-start(bf16[256,256]{1,0:T(8,128)(2,1)S(1)} %get-tuple-element.67), channel_id=1, source_target_pairs={{0,5},{1,4},{2,7},{3,6},{4,1},{5,0},{6,3},{7,2},{8,13},{9,12},{10,... | collective-permute-start | bytes 393224 | tf_op jit(solution)/shard_map/ppermute | solution.py:35
  44.2 6.8 %collective-permute-start.14 = (bf16[256,256]{1,0:T(8,128)(2,1)S(1)}, bf16[256,256]{1,0:T(8,128)(2,1)S(1)}, u32[]{:S(2)}, u32[]{:S(2)}) collective-permute-start(bf16[256,256]{1,0:T(8,128)(2,1)S(1)} %get-tuple-element.81), channel_id=1, source_target_pairs={{0,1},{1,0},{2,3},{3,2},{4,5},{5,4},{6,7},{7,6},{8,9},{9,8},{10,11... | collective-permute-start | bytes 393224 | tf_op jit(solution)/shard_map/ppermute | solution.py:35
  45.3 7.0 %collective-permute-start.15 = (bf16[256,256]{1,0:T(8,128)(2,1)S(1)}, bf16[256,256]{1,0:T(8,128)(2,1)S(1)}, u32[]{:S(2)}, u32[]{:S(2)}) collective-permute-start(bf16[256,256]{1,0:T(8,128)(2,1)S(1)} %get-tuple-element.82), channel_id=1, source_target_pairs={{0,4},{1,5},{2,6},{3,7},{4,0},{5,1},{6,2},{7,3},{8,12},{9,13},{10,... | collective-permute-start | bytes 393224 | tf_op jit(solution)/shard_map/ppermute | solution.py:35
  45.9 7.3 %collective-permute-start.16 = (bf16[256,256]{1,0:T(8,128)(2,1)S(1)}, bf16[256,256]{1,0:T(8,128)(2,1)S(1)}, u32[]{:S(2)}, u32[]{:S(2)}) collective-permute-start(bf16[256,256]{1,0:T(8,128)(2,1)S(1)} %get-tuple-element.83), channel_id=1, source_target_pairs={{0,5},{1,4},{2,7},{3,6},{4,1},{5,0},{6,3},{7,2},{8,13},{9,12},{10,... | collective-permute-start | bytes 393224 | tf_op jit(solution)/shard_map/ppermute | solution.py:35
  48.7 7.0 %collective-permute-start.18 = (bf16[256,256]{1,0:T(8,128)(2,1)S(1)}, bf16[256,256]{1,0:T(8,128)(2,1)S(1)}, u32[]{:S(2)}, u32[]{:S(2)}) collective-permute-start(bf16[256,256]{1,0:T(8,128)(2,1)S(1)} %get-tuple-element.87), channel_id=1, source_target_pairs={{0,1},{1,0},{2,3},{3,2},{4,5},{5,4},{6,7},{7,6},{8,9},{9,8},{10,11... | collective-permute-start | bytes 393224 | tf_op jit(solution)/shard_map/ppermute | solution.py:35
  50.4 7.3 %collective-permute-start.19 = (bf16[256,256]{1,0:T(8,128)(2,1)S(1)}, bf16[256,256]{1,0:T(8,128)(2,1)S(1)}, u32[]{:S(2)}, u32[]{:S(2)}) collective-permute-start(bf16[256,256]{1,0:T(8,128)(2,1)S(1)} %get-tuple-element.88), channel_id=1, source_target_pairs={{0,4},{1,5},{2,6},{3,7},{4,0},{5,1},{6,2},{7,3},{8,12},{9,13},{10,... | collective-permute-start | bytes 393224 | tf_op jit(solution)/shard_map/ppermute | solution.py:35
  51.0 6.7 %collective-permute-start.20 = (bf16[256,256]{1,0:T(8,128)(2,1)S(1)}, bf16[256,256]{1,0:T(8,128)(2,1)S(1)}, u32[]{:S(2)}, u32[]{:S(2)}) collective-permute-start(bf16[256,256]{1,0:T(8,128)(2,1)S(1)} %get-tuple-element.89), channel_id=1, source_target_pairs={{0,5},{1,4},{2,7},{3,6},{4,1},{5,0},{6,3},{7,2},{8,13},{9,12},{10,... | collective-permute-start | bytes 393224 | tf_op jit(solution)/shard_map/ppermute | solution.py:35
  57.8 2.4 %collective-permute-start.21 = (bf16[128,3072]{1,0:T(8,128)(2,1)S(1)}, bf16[128,3072]{1,0:T(8,128)(2,1)S(1)}, u32[]{:S(2)}, u32[]{:S(2)}) collective-permute-start(bf16[128,3072]{1,0:T(8,128)(2,1)S(1)} %bottom.1), channel_id=1, source_target_pairs={{0,2},{1,3},{2,0},{3,1},{4,6},{5,7},{6,4},{7,5},{8,10},{9,11},{10,... | collective-permute-start | bytes 2359304 | tf_op jit(solution)/shard_map/ppermute | solution.py:35

commit v18 on v17

--- a/solution.py
+++ b/solution.py
@@ -269,6 +269,12 @@
                 stage(step - behind)
 
 
+def early_rows(tile):
+    count = WINDOW // TILE
+    start = (tile * count - tile * (tile - 1) // 2) * TILE
+    return slice(start, start + (count - tile) * TILE)
+
+
 def gradient_rows(qg, base, group, scale, out):
     first = qg.shape[1] // 2
     columns = jnp.broadcast_to(scale, (HEAD_DIM, scale.shape[1])).T
@@ -349,8 +355,8 @@
 def forward_body(size, core, masks, reach, tok, group, *refs):
     take = taker(refs)
     (seg_k, seg_q, qg), kvs, (out_own, stats) = take(3), take(reach), take(2)
-    out_pieces, sent, (outs, own_scale, dq_part) = take(len(masks)), take(reach), take(3)
-    ka, va, kt, vt, dk, dv, s_scr, e_scr, dp_scr, ds_scr, g_scr = take(11)
+    out_pieces, sent, (outs, own_scale, ds_early, kt) = take(len(masks)), take(reach), take(4)
+    ka, va, vt, dk, dv, s_scr, e_scr, dp_scr, g_scr = take(9)
     wide, tiles = group * TILE, tok // TILE
     ka[:, HEAD_DIM:] = seg_k[:WINDOW, :]
     for lag in range(1, reach + 1):
@@ -399,10 +405,9 @@
         e = e_scr[tile % 3, :early, :]
         old = early if tile else 0
         add_rows(dv, base, old, dot(e, g_scr[turn]))
-        score_gradients(ds_scr.at[turn, :early, :], e, dp_scr.at[turn, :early, :])
-        ds = ds_scr[turn, :early, :]
-        add_rows(dk, base, old, dot(ds, stacked(qg, base, group)))
-        dq_part[:, tile * wide : (tile + 1) * wide] = dot(kt[:, base:], ds)
+        ds = ds_early.at[early_rows(tile), :]
+        score_gradients(ds, e, dp_scr.at[turn, :early, :])
+        add_rows(dk, base, old, dot(ds[...], stacked(qg, base, group)))
 
     pipeline(tiles, scores, weights, outputs, gradients)
 
@@ -415,7 +420,7 @@
 
 def backward_body(size, core, masks, tok, group, *refs):
     take = taker(refs)
-    qg, kv, e_own, outs, own_scale, dq_part = take(6)
+    qg, kv, e_own, outs, own_scale, ds_early, kt_early = take(7)
     dq_pieces, (dkv,) = take(len(masks)), take(1)
     dqs, va, kt, dk, dv, dp_scr, ds_scr, g_scr = take(8)
     wide = group * TILE
@@ -432,13 +437,13 @@
     def gradients(tile):
         base, turn = tile * TILE, tile % 2
         count = base + TILE
-        columns = slice(tile * wide, (tile + 1) * wide)
         e = e_own[own_rows(tile), :]
         add_rows(dv, 0, base, dot(e, g_scr[turn]))
         score_gradients(ds_scr.at[turn, :count, :], e, dp_scr.at[turn, :count, :])
         ds = ds_scr[turn, :count, :]
         add_rows(dk, 0, base, dot(ds, stacked(qg, base, group)))
-        dq = (dq_part[:, columns] + dot(kt[:, :count], ds)) * logit_scale
+        dq = dot(kt_early[:, base:], ds_early[early_rows(tile), :]) + dot(kt[:, :count], ds)
+        dq = dq * logit_scale
         unstacked(dqs, base, group, dq.T.astype(BF16))
 
     pipeline(tok // TILE, products, gradients)
@@ -498,19 +503,18 @@
     out_shape += [
         jax.ShapeDtypeStruct((tok, cols // 2), BF16),
         jax.ShapeDtypeStruct((tiles, wide), F32),
-        jax.ShapeDtypeStruct((HEAD_DIM, tiles * wide), F32),
+        jax.ShapeDtypeStruct((early_rows(tiles - 1).stop, wide), BF16),
+        jax.ShapeDtypeStruct((HEAD_DIM, WINDOW), BF16),
     ]
     scratch = [
         pltpu.VMEM((WINDOW, 2 * HEAD_DIM), BF16),
         pltpu.VMEM((WINDOW, 2 * HEAD_DIM), BF16),
-        pltpu.VMEM((HEAD_DIM, WINDOW), BF16),
         pltpu.VMEM((HEAD_DIM, WINDOW), BF16),
         pltpu.VMEM((WINDOW, HEAD_DIM), F32),
         pltpu.VMEM((WINDOW, HEAD_DIM), F32),
         pltpu.VMEM((2, WINDOW, wide), F32),
         pltpu.VMEM((3, WINDOW, wide), BF16),
         pltpu.VMEM((2, WINDOW, wide), F32),
-        pltpu.VMEM((2, WINDOW, wide), BF16),
         pltpu.VMEM((2, wide, HEAD_DIM), BF16),
     ]
     results = attend_call(

time: 61.9 us -> 60.5 us (0.977)
  Pallas kernels: 13.7 us -> 12.7 us
    pallas_call x3, Pallas kernels: 11.8 us -> 10.8 us  [attend_call(): pl.pallas_call(kernel, out_shape=out_shape, in_specs=[VMEM] * len(args),...]
  transfers between devices with their start and end apart: 22 -> 22, of which waited for: 11 -> 11; matrix products, arithmetic and copies ran while one was open for 3% -> 3% of each run, Pallas kernels for 10% -> 11%
where the time goes in v18:
time: 60.5 us; the launch traced here: 60.3 us
  starting transfers between devices  26.6 us (44%)
  waiting for transfers between devices  17.9 us (30%)
  Pallas kernels  12.7 us (21%)
  local copies, waits for them, and re-layouts  1.22 us (2%)
  between operations  1.1 us (2%)
  other arithmetic  0.73 us (1%)
    ppermute x20, starting transfers between devices, swap(): lax.ppermute(value, BOTH, [(i, i ^ mask) for i in range(device_count())])  21.6 us
    ppermute x20, waiting for transfers between devices, swap(): lax.ppermute(value, BOTH, [(i, i ^ mask) for i in range(device_count())])  17 us
    pallas_call x3, Pallas kernels, attend_call(): pl.pallas_call(kernel, out_shape=out_shape, in_specs=[VMEM] * len(args),...  10.8 us
    ppermute x2, starting transfers between devices, shifted(): return lax.ppermute(value, BOTH, pairs)  4.99 us
    pallas_call x1, Pallas kernels, spread_cores(): pl.pallas_call(functools.partial(spread_body, size, core_mask(), chip_mas...  1.39 us
  transfers between devices with their start and end apart: 22, of which 11 were waited for; matrix products, arithmetic and copies ran while one was open for 3% of the time, Pallas kernels for 11%

profile of v18, /device:TPU:0, one launch (start us, length us, event | category | flops | bytes accessed | tf_op | source)
XLA Modules:
  0.0 60.3 jit_solution(9976578220164929026)
XLA Ops:
  0.7 0.5 collective-permute-start
  1.8 1.1 %fusion.2 = (bf16[128,256]{1,0:T(8,128)(2,1)S(1)}, bf16[128,256]{1,0:T(8,128)(2,1)S(1)}, bf16[128,256]{1,0:T(8,128)(2,1)S(1)}, bf16[128,256]{1,0:T(8,128)(2,1)S(...) fusion(bf16[128,1024]{1,0:T(8,128)(2,1)} %param.7, ...), kind=kLoop, calls=%fused_computation.11 | loop fusion | bytes 1048576 | tf_op jit(solution)/shard_map/slice | solution.py:94
  3.2 3.0 %collective-permute-start.7 = (bf16[256,256]{1,0:T(8,128)(2,1)S(1)}, bf16[256,256]{1,0:T(8,128)(2,1)S(1)}, u32[]{:S(2)}, u32[]{:S(2)}) collective-permute-start(bf16[256,256]{1,0:T(8,128)(2,1)S(1)} %get-tuple-element.59), channel_id=1, source_target_pairs={{0,1},{1,0},{2,3},{3,2},{4,5},{5,4},{6,7},{7,6},{8,9},{9,8},{10,11... | collective-permute-start | bytes 393224 | tf_op jit(solution)/shard_map/ppermute | solution.py:35
  6.2 1.5 %collective-permute-start.8 = (bf16[256,256]{1,0:T(8,128)(2,1)S(1)}, bf16[256,256]{1,0:T(8,128)(2,1)S(1)}, u32[]{:S(2)}, u32[]{:S(2)}) collective-permute-start(bf16[256,256]{1,0:T(8,128)(2,1)S(1)} %get-tuple-element.60), channel_id=1, source_target_pairs={{0,4},{1,5},{2,6},{3,7},{4,0},{5,1},{6,2},{7,3},{8,12},{9,13},{10,... | collective-permute-start | bytes 393224 | tf_op jit(solution)/shard_map/ppermute | solution.py:35
  8.2 2.0 %collective-permute-start.4 = (bf16[256,512]{1,0:T(8,128)(2,1)S(1)}, bf16[256,512]{1,0:T(8,128)(2,1)S(1)}, u32[]{:S(2)}, u32[]{:S(2)}) collective-permute-start(bf16[256,512]{1,0:T(8,128)(2,1)S(1)} %get-tuple-element.55), channel_id=1, source_target_pairs={{0,1},{1,0},{2,3},{3,2},{4,5},{5,4},{6,7},{7,6},{8,9},{9,8},{10,11... | collective-permute-start | bytes 786440 | tf_op jit(solution)/shard_map/ppermute | solution.py:35
  10.2 1.5 %collective-permute-start.5 = (bf16[256,512]{1,0:T(8,128)(2,1)S(1)}, bf16[256,512]{1,0:T(8,128)(2,1)S(1)}, u32[]{:S(2)}, u32[]{:S(2)}) collective-permute-start(bf16[256,512]{1,0:T(8,128)(2,1)S(1)} %get-tuple-element.56), channel_id=1, source_target_pairs={{0,4},{1,5},{2,6},{3,7},{4,0},{5,1},{6,2},{7,3},{8,12},{9,13},{10,... | collective-permute-start | bytes 786440 | tf_op jit(solution)/shard_map/ppermute | solution.py:35
  11.7 1.7 %collective-permute-start.6 = (bf16[256,512]{1,0:T(8,128)(2,1)S(1)}, bf16[256,512]{1,0:T(8,128)(2,1)S(1)}, u32[]{:S(2)}, u32[]{:S(2)}) collective-permute-start(bf16[256,512]{1,0:T(8,128)(2,1)S(1)} %get-tuple-element.57), channel_id=1, source_target_pairs={{0,5},{1,4},{2,7},{3,6},{4,1},{5,0},{6,3},{7,2},{8,13},{9,12},{10,... | collective-permute-start | bytes 786440 | tf_op jit(solution)/shard_map/ppermute | solution.py:35
  13.8 0.6 collective-permute-done.8.refs_2_
  14.4 0.7 %collective-permute-done.9.refs_3_ = bf16[256,256]{1,0:T(8,128)(2,1)S(1)} collective-permute-done((bf16[256,256]{1,0:T(8,128)(2,1)S(1)}, bf16[256,256]{1,0:T(8,128)(2,1)S(1)}, u32[]{:S(2)}, u32[]{:S(2)}) %collective-permute-start.9) | collective-permute-done | bytes 131104 | tf_op jit(solution)/shard_map/ppermute | solution.py:35
  15.1 3.5 %collective-permute-start.10 = (bf16[1024,256]{1,0:T(8,128)(2,1)S(1)}, bf16[1024,256]{1,0:T(8,128)(2,1)S(1)}, u32[]{:S(2)}, u32[]{:S(2)}) collective-permute-start(bf16[1024,256]{1,0:T(8,128)(2,1)S(1)} %join.1.refs_6_.refs_1_), channel_id=1, source_target_pairs={{0,8},{1,9},{2,10},{3,11},{4,12},{5,13},{6,14},{7,15},{8,16},{9,17... | collective-permute-start | bytes 1572872 | tf_op jit(solution)/shard_map/ppermute | solution.py:55
  18.8 0.8 %collective-permute-done.4.refs_3_ = bf16[256,512]{1,0:T(8,128)(2,1)S(1)} collective-permute-done((bf16[256,512]{1,0:T(8,128)(2,1)S(1)}, bf16[256,512]{1,0:T(8,128)(2,1)S(1)}, u32[]{:S(2)}, u32[]{:S(2)}) %collective-permute-start.4) | collective-permute-done | bytes 262176 | tf_op jit(solution)/shard_map/ppermute | solution.py:35
  19.7 5.7 %collective-permute-done.5.refs_4_ = bf16[256,512]{1,0:T(8,128)(2,1)S(1)} collective-permute-done((bf16[256,512]{1,0:T(8,128)(2,1)S(1)}, bf16[256,512]{1,0:T(8,128)(2,1)S(1)}, u32[]{:S(2)}, u32[]{:S(2)}) %collective-permute-start.5) | collective-permute-done | bytes 262176 | tf_op jit(solution)/shard_map/ppermute | solution.py:35
  25.4 2.4 %forward_own.1 = (bf16[4608,256]{1,0:T(8,128)(2,1)S(1)}, f32[128,2048]{1,0:T(8,128)S(1)}, f32[16,256]{1,0:T(8,128)S(1)}, bf16[1024,512]{1,0:T(8,128)(2,1)S(1)}) custom-call(bf16[2048,128]{1,0:T(8,128)(2,1)S(1)} %select_convert_fusion.refs_0_, bf16[1024,128]{1,0:T(8,128)(2,1)S(1)} %select_convert_fusion.1.refs_1_, ...), custom_call_target="tpu_custom_call" | custom-call | flops 4831838208 | bytes 8388608 | tf_op jit(solution)/shard_map/forward_own/pallas_call | solution.py:456
  27.8 4.8 %forward.1 = (bf16[256,256]{1,0:T(8,128)(2,1)S(1)}, bf16[256,256]{1,0:T(8,128)(2,1)S(1)}, bf16[256,256]{1,0:T(8,128)(2,1)S(1)}, bf16[256,256]{1,0:T(8,128)(2,1)S...) custom-call(bf16[2048,128]{1,0:T(8,128)(2,1)S(1)} %select_convert_fu, ...), custom_call_target="tpu_custom_call" | custom-call | flops 1811939328 | bytes 8388608 | tf_op jit(solution)/shard_map/forward/pallas_call | solution.py:456
  32.7 1.5 %collective-permute-start.17 = (bf16[1024,256]{1,0:T(8,128)(2,1)S(1)}, bf16[1024,256]{1,0:T(8,128)(2,1)S(1)}, u32[]{:S(2)}, u32[]{:S(2)}) collective-permute-start(bf16[1024,256]{1,0:T(8,128)(2,1)S(1)} %get-tuple-element.87), channel_id=1, source_target_pairs={{8,0},{9,1},{10,2},{11,3},{12,4},{13,5},{14,6},{15,7},{16,8},{17,9... | collective-permute-start | bytes 1572872 | tf_op jit(solution)/shard_map/ppermute | solution.py:55
  34.1 1.8 %collective-permute-start.11 = (bf16[256,256]{1,0:T(8,128)(2,1)S(1)}, bf16[256,256]{1,0:T(8,128)(2,1)S(1)}, u32[]{:S(2)}, u32[]{:S(2)}) collective-permute-start(bf16[256,256]{1,0:T(8,128)(2,1)S(1)} %get-tuple-element.66), channel_id=1, source_target_pairs={{0,1},{1,0},{2,3},{3,2},{4,5},{5,4},{6,7},{7,6},{8,9},{9,8},{10,11... | collective-permute-start | bytes 393224 | tf_op jit(solution)/shard_map/ppermute | solution.py:35
  35.9 0.5 collective-permute-start.12
  36.4 1.3 %collective-permute-start.13 = (bf16[256,256]{1,0:T(8,128)(2,1)S(1)}, bf16[256,256]{1,0:T(8,128)(2,1)S(1)}, u32[]{:S(2)}, u32[]{:S(2)}) collective-permute-start(bf16[256,256]{1,0:T(8,128)(2,1)S(1)} %get-tuple-element.68), channel_id=1, source_target_pairs={{0,5},{1,4},{2,7},{3,6},{4,1},{5,0},{6,3},{7,2},{8,13},{9,12},{10,... | collective-permute-start | bytes 393224 | tf_op jit(solution)/shard_map/ppermute | solution.py:35
  37.7 3.6 %backward.1 = (bf16[256,256]{1,0:T(8,128)(2,1)S(1)}, bf16[256,256]{1,0:T(8,128)(2,1)S(1)}, bf16[256,256]{1,0:T(8,128)(2,1)S(1)}, bf16[256,256]{1,0:T(8,128)(2,1)S(1)}, f32[1024,256]{1,0:T(8,128)S(1)}) custom-call(bf16[1024,512]{1,0:T(8,128)(2,1)S(1)} %get-tuple-element.62.refs_2_.refs_0_, bf16[1024,256]{1,0:T(8,128)(2,1)S(1)} %join.1.refs_6_.refs_1_, ...), custom_call_target="tpu_custom_call" | custom-call | flops 1207959552 | bytes 8388608 | tf_op jit(solution)/shard_map/backward/pallas_call | solution.py:456
  41.3 1.5 %collective-permute-done.12.refs_2_ = bf16[256,256]{1,0:T(8,128)(2,1)S(1)} collective-permute-done((bf16[256,256]{1,0:T(8,128)(2,1)S(1)}, bf16[256,256]{1,0:T(8,128)(2,1)S(1)}, u32[]{:S(2)}, u32[]{:S(2)}) %collective-permute-start.12) | collective-permute-done | bytes 131104 | tf_op jit(solution)/shard_map/ppermute | solution.py:35
  42.8 1.1 %collective-permute-start.14 = (bf16[256,256]{1,0:T(8,128)(2,1)S(1)}, bf16[256,256]{1,0:T(8,128)(2,1)S(1)}, u32[]{:S(2)}, u32[]{:S(2)}) collective-permute-start(bf16[256,256]{1,0:T(8,128)(2,1)S(1)} %get-tuple-element.83), channel_id=1, source_target_pairs={{0,1},{1,0},{2,3},{3,2},{4,5},{5,4},{6,7},{7,6},{8,9},{9,8},{10,11... | collective-permute-start | bytes 393224 | tf_op jit(solution)/shard_map/ppermute | solution.py:35
  43.9 0.7 %collective-permute-start.15 = (bf16[256,256]{1,0:T(8,128)(2,1)S(1)}, bf16[256,256]{1,0:T(8,128)(2,1)S(1)}, u32[]{:S(2)}, u32[]{:S(2)}) collective-permute-start(bf16[256,256]{1,0:T(8,128)(2,1)S(1)} %get-tuple-element.84), channel_id=1, source_target_pairs={{0,4},{1,5},{2,6},{3,7},{4,0},{5,1},{6,2},{7,3},{8,12},{9,13},{10,... | collective-permute-start | bytes 393224 | tf_op jit(solution)/shard_map/ppermute | solution.py:35
  44.6 1.8 %collective-permute-start.16 = (bf16[256,256]{1,0:T(8,128)(2,1)S(1)}, bf16[256,256]{1,0:T(8,128)(2,1)S(1)}, u32[]{:S(2)}, u32[]{:S(2)}) collective-permute-start(bf16[256,256]{1,0:T(8,128)(2,1)S(1)} %get-tuple-element.85), channel_id=1, source_target_pairs={{0,5},{1,4},{2,7},{3,6},{4,1},{5,0},{6,3},{7,2},{8,13},{9,12},{10,... | collective-permute-start | bytes 393224 | tf_op jit(solution)/shard_map/ppermute | solution.py:35
  46.3 0.9 %collective-permute-done.17.refs_1_ = bf16[1024,256]{1,0:T(8,128)(2,1)S(1)} collective-permute-done((bf16[1024,256]{1,0:T(8,128)(2,1)S(1)}, bf16[1024,256]{1,0:T(8,128)(2,1)S(1)}, u32[]{:S(2)}, u32[]{:S(2)}) %collective-permute-start.17) | collective-permute-done | bytes 524320 | tf_op jit(solution)/shard_map/ppermute | solution.py:55
  47.3 1.7 %collective-permute-start.18 = (bf16[256,256]{1,0:T(8,128)(2,1)S(1)}, bf16[256,256]{1,0:T(8,128)(2,1)S(1)}, u32[]{:S(2)}, u32[]{:S(2)}) collective-permute-start(bf16[256,256]{1,0:T(8,128)(2,1)S(1)} %get-tuple-element.89), channel_id=1, source_target_pairs={{0,1},{1,0},{2,3},{3,2},{4,5},{5,4},{6,7},{7,6},{8,9},{9,8},{10,11... | collective-permute-start | bytes 393224 | tf_op jit(solution)/shard_map/ppermute | solution.py:35
  49.0 0.6 collective-permute-start.19
  49.6 1.3 %collective-permute-start.20 = (bf16[256,256]{1,0:T(8,128)(2,1)S(1)}, bf16[256,256]{1,0:T(8,128)(2,1)S(1)}, u32[]{:S(2)}, u32[]{:S(2)}) collective-permute-start(bf16[256,256]{1,0:T(8,128)(2,1)S(1)} %get-tuple-element.91), channel_id=1, source_target_pairs={{0,5},{1,4},{2,7},{3,6},{4,1},{5,0},{6,3},{7,2},{8,13},{9,12},{10,... | collective-permute-start | bytes 393224 | tf_op jit(solution)/shard_map/ppermute | solution.py:35
  50.8 1.0 %collective-permute-done.16.refs_7_ = bf16[256,256]{1,0:T(8,128)(2,1)S(1)} collective-permute-done((bf16[256,256]{1,0:T(8,128)(2,1)S(1)}, bf16[256,256]{1,0:T(8,128)(2,1)S(1)}, u32[]{:S(2)}, u32[]{:S(2)}) %collective-permute-start.16) | collective-permute-done | bytes 131104 | tf_op jit(solution)/shard_map/ppermute | solution.py:35
  51.8 2.5 %collective-permute-done.18.refs_9_ = bf16[256,256]{1,0:T(8,128)(2,1)S(1)} collective-permute-done((bf16[256,256]{1,0:T(8,128)(2,1)S(1)}, bf16[256,256]{1,0:T(8,128)(2,1)S(1)}, u32[]{:S(2)}, u32[]{:S(2)}) %collective-permute-start.18) | collective-permute-done | bytes 131104 | tf_op jit(solution)/shard_map/ppermute | solution.py:35
  54.3 2.0 %collective-permute-done.19.refs_10_ = bf16[256,256]{1,0:T(8,128)(2,1)S(1)} collective-permute-done((bf16[256,256]{1,0:T(8,128)(2,1)S(1)}, bf16[256,256]{1,0:T(8,128)(2,1)S(1)}, u32[]{:S(2)}, u32[]{:S(2)}) %collective-permute-start.19) | collective-permute-done | bytes 131104 | tf_op jit(solution)/shard_map/ppermute | solution.py:35
  56.4 2.3 %collective-permute-done.21.refs_12_ = bf16[128,3072]{1,0:T(8,128)(2,1)S(1)} collective-permute-done((bf16[128,3072]{1,0:T(8,128)(2,1)S(1)}, bf16[128,3072]{1,0:T(8,128)(2,1)S(1)}, u32[]{:S(2)}, u32[]{:S(2)}) %collective-permute-start.21) | collective-permute-done | bytes 786464 | tf_op jit(solution)/shard_map/ppermute | solution.py:35
  58.7 1.4 %spread.1 = (bf16[128,2048]{1,0:T(8,128)(2,1)}, bf16[128,2048]{1,0:T(8,128)(2,1)}, bf16[128,1024]{1,0:T(8,128)(2,1)}, bf16[128,1024]{1,0:T(8,128)(2,1)}) custom-call(bf16[256,256]{1,0:T(8,128)(2,1)S(1)} %get-tuple-element.78.refs_0_, bf16[256,256]{1,0:T(8,128)(2,1)S(1)} %collective-permute-done.11.refs_1_, ...), custom_call_target="tpu_custom_call" | custom-call | tf_op jit(solution)/shard_map/spread/pallas_call | solution.py:201
  (39 shorter events, 2.1 us)
Async XLA Ops:
  0.6 7.1 %copy-start = (bf16[128,2048]{1,0:T(8,128)(2,1)S(1)}, bf16[128,2048]{1,0:T(8,128)(2,1)}, u32[]{:S(2)}) copy-start(bf16[128,2048]{1,0:T(8,128)(2,1)} %param.5) | copy-start | bytes 1572868
  0.6 7.2 %copy-start.1 = (bf16[128,2048]{1,0:T(8,128)(2,1)S(1)}, bf16[128,2048]{1,0:T(8,128)(2,1)}, u32[]{:S(2)}) copy-start(bf16[128,2048]{1,0:T(8,128)(2,1)} %param.8) | copy-start | bytes 1572868
  0.7 2.4 %collective-permute-start = (bf16[128,1024]{1,0:T(8,128)(2,1)}, bf16[128,1024]{1,0:T(8,128)(2,1)S(1)}, u32[]{:S(2)}, u32[]{:S(2)}) collective-permute-start(bf16[128,1024]{1,0:T(8,128)(2,1)} %param.6), channel_id=1, source_target_pairs={{0,2},{1,3},{2,0},{3,1},{4,6},{5,7},{6,4},{7,5},{8,10},{9,11},{10,... | collective-permute-start | bytes 786440 | tf_op jit(solution)/shard_map/ppermute | solution.py:35
  1.2 1.9 %collective-permute-start.1 = (bf16[128,1024]{1,0:T(8,128)(2,1)}, bf16[128,1024]{1,0:T(8,128)(2,1)S(1)}, u32[]{:S(2)}, u32[]{:S(2)}) collective-permute-start(bf16[128,1024]{1,0:T(8,128)(2,1)} %param.7), channel_id=1, source_target_pairs={{0,2},{1,3},{2,0},{3,1},{4,6},{5,7},{6,4},{7,5},{8,10},{9,11},{10,... | collective-permute-start | bytes 786440 | tf_op jit(solution)/shard_map/ppermute | solution.py:35
  1.2 6.7 %collective-permute-start.2 = (bf16[128,2048]{1,0:T(8,128)(2,1)}, bf16[128,2048]{1,0:T(8,128)(2,1)S(1)}, u32[]{:S(2)}, u32[]{:S(2)}) collective-permute-start(bf16[128,2048]{1,0:T(8,128)(2,1)} %param.5), channel_id=1, source_target_pairs={{0,2},{1,3},{2,0},{3,1},{4,6},{5,7},{6,4},{7,5},{8,10},{9,11},{10,... | collective-permute-start | bytes 1572872 | tf_op jit(solution)/shard_map/ppermute | solution.py:35
  1.7 6.3 %collective-permute-start.3 = (bf16[128,2048]{1,0:T(8,128)(2,1)}, bf16[128,2048]{1,0:T(8,128)(2,1)S(1)}, u32[]{:S(2)}, u32[]{:S(2)}) collective-permute-start(bf16[128,2048]{1,0:T(8,128)(2,1)} %param.8), channel_id=1, source_target_pairs={{0,2},{1,3},{2,0},{3,1},{4,6},{5,7},{6,4},{7,5},{8,10},{9,11},{10,... | collective-permute-start | bytes 1572872 | tf_op jit(solution)/shard_map/ppermute | solution.py:35
  2.9 5.0 %copy-start.2 = (s32[4096]{0:T(1024)S(1)}, s32[4096]{0:T(1024)}, u32[]{:S(2)}) copy-start(s32[4096]{0:T(1024)} %param.9) | copy-start | bytes 49156
  3.2 8.5 %collective-permute-start.7 = (bf16[256,256]{1,0:T(8,128)(2,1)S(1)}, bf16[256,256]{1,0:T(8,128)(2,1)S(1)}, u32[]{:S(2)}, u32[]{:S(2)}) collective-permute-start(bf16[256,256]{1,0:T(8,128)(2,1)S(1)} %get-tuple-element.59), channel_id=1, source_target_pairs={{0,1},{1,0},{2,3},{3,2},{4,5},{5,4},{6,7},{7,6},{8,9},{9,8},{10,11... | collective-permute-start | bytes 393224 | tf_op jit(solution)/shard_map/ppermute | solution.py:35
  6.2 8.2 %collective-permute-start.8 = (bf16[256,256]{1,0:T(8,128)(2,1)S(1)}, bf16[256,256]{1,0:T(8,128)(2,1)S(1)}, u32[]{:S(2)}, u32[]{:S(2)}) collective-permute-start(bf16[256,256]{1,0:T(8,128)(2,1)S(1)} %get-tuple-element.60), channel_id=1, source_target_pairs={{0,4},{1,5},{2,6},{3,7},{4,0},{5,1},{6,2},{7,3},{8,12},{9,13},{10,... | collective-permute-start | bytes 393224 | tf_op jit(solution)/shard_map/ppermute | solution.py:35
  7.7 7.4 %collective-permute-start.9 = (bf16[256,256]{1,0:T(8,128)(2,1)S(1)}, bf16[256,256]{1,0:T(8,128)(2,1)S(1)}, u32[]{:S(2)}, u32[]{:S(2)}) collective-permute-start(bf16[256,256]{1,0:T(8,128)(2,1)S(1)} %get-tuple-element.61), channel_id=1, source_target_pairs={{0,5},{1,4},{2,7},{3,6},{4,1},{5,0},{6,3},{7,2},{8,13},{9,12},{10,... | collective-permute-start | bytes 393224 | tf_op jit(solution)/shard_map/ppermute | solution.py:35
  7.8 10.8 %dynamic-slice-start = ((s32[4096]{0:T(1024)}, s32[]{:T(128)}), s32[1024]{0:T(1024)S(1)}, s32[]{:S(2)}) async-start(s32[4096]{0:T(1024)} %param.9, s32[]{:T(128)} %select_n.69), calls=%async_computation | async-start | bytes 8704 | tf_op jit(solution)/shard_map/dynamic_slice | solution.py:568
  8.2 11.5 %collective-permute-start.4 = (bf16[256,512]{1,0:T(8,128)(2,1)S(1)}, bf16[256,512]{1,0:T(8,128)(2,1)S(1)}, u32[]{:S(2)}, u32[]{:S(2)}) collective-permute-start(bf16[256,512]{1,0:T(8,128)(2,1)S(1)} %get-tuple-element.55), channel_id=1, source_target_pairs={{0,1},{1,0},{2,3},{3,2},{4,5},{5,4},{6,7},{7,6},{8,9},{9,8},{10,11... | collective-permute-start | bytes 786440 | tf_op jit(solution)/shard_map/ppermute | solution.py:35
  10.2 15.2 %collective-permute-start.5 = (bf16[256,512]{1,0:T(8,128)(2,1)S(1)}, bf16[256,512]{1,0:T(8,128)(2,1)S(1)}, u32[]{:S(2)}, u32[]{:S(2)}) collective-permute-start(bf16[256,512]{1,0:T(8,128)(2,1)S(1)} %get-tuple-element.56), channel_id=1, source_target_pairs={{0,4},{1,5},{2,6},{3,7},{4,0},{5,1},{6,2},{7,3},{8,12},{9,13},{10,... | collective-permute-start | bytes 786440 | tf_op jit(solution)/shard_map/ppermute | solution.py:35
  11.7 13.7 %collective-permute-start.6 = (bf16[256,512]{1,0:T(8,128)(2,1)S(1)}, bf16[256,512]{1,0:T(8,128)(2,1)S(1)}, u32[]{:S(2)}, u32[]{:S(2)}) collective-permute-start(bf16[256,512]{1,0:T(8,128)(2,1)S(1)} %get-tuple-element.57), channel_id=1, source_target_pairs={{0,5},{1,4},{2,7},{3,6},{4,1},{5,0},{6,3},{7,2},{8,13},{9,12},{10,... | collective-permute-start | bytes 786440 | tf_op jit(solution)/shard_map/ppermute | solution.py:35
  15.1 12.7 %collective-permute-start.10 = (bf16[1024,256]{1,0:T(8,128)(2,1)S(1)}, bf16[1024,256]{1,0:T(8,128)(2,1)S(1)}, u32[]{:S(2)}, u32[]{:S(2)}) collective-permute-start(bf16[1024,256]{1,0:T(8,128)(2,1)S(1)} %join.1.refs_6_.refs_1_), channel_id=1, source_target_pairs={{0,8},{1,9},{2,10},{3,11},{4,12},{5,13},{6,14},{7,15},{8,16},{9,17... | collective-permute-start | bytes 1572872 | tf_op jit(solution)/shard_map/ppermute | solution.py:55
  32.7 14.5 %collective-permute-start.17 = (bf16[1024,256]{1,0:T(8,128)(2,1)S(1)}, bf16[1024,256]{1,0:T(8,128)(2,1)S(1)}, u32[]{:S(2)}, u32[]{:S(2)}) collective-permute-start(bf16[1024,256]{1,0:T(8,128)(2,1)S(1)} %get-tuple-element.87), channel_id=1, source_target_pairs={{8,0},{9,1},{10,2},{11,3},{12,4},{13,5},{14,6},{15,7},{16,8},{17,9... | collective-permute-start | bytes 1572872 | tf_op jit(solution)/shard_map/ppermute | solution.py:55
  34.1 7.2 %collective-permute-start.11 = (bf16[256,256]{1,0:T(8,128)(2,1)S(1)}, bf16[256,256]{1,0:T(8,128)(2,1)S(1)}, u32[]{:S(2)}, u32[]{:S(2)}) collective-permute-start(bf16[256,256]{1,0:T(8,128)(2,1)S(1)} %get-tuple-element.66), channel_id=1, source_target_pairs={{0,1},{1,0},{2,3},{3,2},{4,5},{5,4},{6,7},{7,6},{8,9},{9,8},{10,11... | collective-permute-start | bytes 393224 | tf_op jit(solution)/shard_map/ppermute | solution.py:35
  35.9 6.9 %collective-permute-start.12 = (bf16[256,256]{1,0:T(8,128)(2,1)S(1)}, bf16[256,256]{1,0:T(8,128)(2,1)S(1)}, u32[]{:S(2)}, u32[]{:S(2)}) collective-permute-start(bf16[256,256]{1,0:T(8,128)(2,1)S(1)} %get-tuple-element.67), channel_id=1, source_target_pairs={{0,4},{1,5},{2,6},{3,7},{4,0},{5,1},{6,2},{7,3},{8,12},{9,13},{10,... | collective-permute-start | bytes 393224 | tf_op jit(solution)/shard_map/ppermute | solution.py:35
  36.4 6.4 %collective-permute-start.13 = (bf16[256,256]{1,0:T(8,128)(2,1)S(1)}, bf16[256,256]{1,0:T(8,128)(2,1)S(1)}, u32[]{:S(2)}, u32[]{:S(2)}) collective-permute-start(bf16[256,256]{1,0:T(8,128)(2,1)S(1)} %get-tuple-element.68), channel_id=1, source_target_pairs={{0,5},{1,4},{2,7},{3,6},{4,1},{5,0},{6,3},{7,2},{8,13},{9,12},{10,... | collective-permute-start | bytes 393224 | tf_op jit(solution)/shard_map/ppermute | solution.py:35
  42.8 6.7 %collective-permute-start.14 = (bf16[256,256]{1,0:T(8,128)(2,1)S(1)}, bf16[256,256]{1,0:T(8,128)(2,1)S(1)}, u32[]{:S(2)}, u32[]{:S(2)}) collective-permute-start(bf16[256,256]{1,0:T(8,128)(2,1)S(1)} %get-tuple-element.83), channel_id=1, source_target_pairs={{0,1},{1,0},{2,3},{3,2},{4,5},{5,4},{6,7},{7,6},{8,9},{9,8},{10,11... | collective-permute-start | bytes 393224 | tf_op jit(solution)/shard_map/ppermute | solution.py:35
  43.9 6.9 %collective-permute-start.15 = (bf16[256,256]{1,0:T(8,128)(2,1)S(1)}, bf16[256,256]{1,0:T(8,128)(2,1)S(1)}, u32[]{:S(2)}, u32[]{:S(2)}) collective-permute-start(bf16[256,256]{1,0:T(8,128)(2,1)S(1)} %get-tuple-element.84), channel_id=1, source_target_pairs={{0,4},{1,5},{2,6},{3,7},{4,0},{5,1},{6,2},{7,3},{8,12},{9,13},{10,... | collective-permute-start | bytes 393224 | tf_op jit(solution)/shard_map/ppermute | solution.py:35
  44.6 7.3 %collective-permute-start.16 = (bf16[256,256]{1,0:T(8,128)(2,1)S(1)}, bf16[256,256]{1,0:T(8,128)(2,1)S(1)}, u32[]{:S(2)}, u32[]{:S(2)}) collective-permute-start(bf16[256,256]{1,0:T(8,128)(2,1)S(1)} %get-tuple-element.85), channel_id=1, source_target_pairs={{0,5},{1,4},{2,7},{3,6},{4,1},{5,0},{6,3},{7,2},{8,13},{9,12},{10,... | collective-permute-start | bytes 393224 | tf_op jit(solution)/shard_map/ppermute | solution.py:35
  47.3 7.0 %collective-permute-start.18 = (bf16[256,256]{1,0:T(8,128)(2,1)S(1)}, bf16[256,256]{1,0:T(8,128)(2,1)S(1)}, u32[]{:S(2)}, u32[]{:S(2)}) collective-permute-start(bf16[256,256]{1,0:T(8,128)(2,1)S(1)} %get-tuple-element.89), channel_id=1, source_target_pairs={{0,1},{1,0},{2,3},{3,2},{4,5},{5,4},{6,7},{7,6},{8,9},{9,8},{10,11... | collective-permute-start | bytes 393224 | tf_op jit(solution)/shard_map/ppermute | solution.py:35
  49.0 7.3 %collective-permute-start.19 = (bf16[256,256]{1,0:T(8,128)(2,1)S(1)}, bf16[256,256]{1,0:T(8,128)(2,1)S(1)}, u32[]{:S(2)}, u32[]{:S(2)}) collective-permute-start(bf16[256,256]{1,0:T(8,128)(2,1)S(1)} %get-tuple-element.90), channel_id=1, source_target_pairs={{0,4},{1,5},{2,6},{3,7},{4,0},{5,1},{6,2},{7,3},{8,12},{9,13},{10,... | collective-permute-start | bytes 393224 | tf_op jit(solution)/shard_map/ppermute | solution.py:35
  49.6 6.7 %collective-permute-start.20 = (bf16[256,256]{1,0:T(8,128)(2,1)S(1)}, bf16[256,256]{1,0:T(8,128)(2,1)S(1)}, u32[]{:S(2)}, u32[]{:S(2)}) collective-permute-start(bf16[256,256]{1,0:T(8,128)(2,1)S(1)} %get-tuple-element.91), channel_id=1, source_target_pairs={{0,5},{1,4},{2,7},{3,6},{4,1},{5,0},{6,3},{7,2},{8,13},{9,12},{10,... | collective-permute-start | bytes 393224 | tf_op jit(solution)/shard_map/ppermute | solution.py:35
  56.3 2.4 %collective-permute-start.21 = (bf16[128,3072]{1,0:T(8,128)(2,1)S(1)}, bf16[128,3072]{1,0:T(8,128)(2,1)S(1)}, u32[]{:S(2)}, u32[]{:S(2)}) collective-permute-start(bf16[128,3072]{1,0:T(8,128)(2,1)S(1)} %bottom.1), channel_id=1, source_target_pairs={{0,2},{1,3},{2,0},{3,1},{4,6},{5,7},{6,4},{7,5},{8,10},{9,11},{10,... | collective-permute-start | bytes 2359304 | tf_op jit(solution)/shard_map/ppermute | solution.py:35

commit v19 on v18

--- a/solution.py
+++ b/solution.py
@@ -275,10 +275,9 @@
     return slice(start, start + (count - tile) * TILE)
 
 
-def gradient_rows(qg, base, group, scale, out):
-    first = qg.shape[1] // 2
+def gradient_rows(g_rows, base, group, scale, out):
     columns = jnp.broadcast_to(scale, (HEAD_DIM, scale.shape[1])).T
-    g2 = (stacked(qg, base, group, first).astype(F32) * columns).astype(BF16)
+    g2 = (stacked(g_rows, base, group).astype(F32) * columns).astype(BF16)
     delta = jnp.sum(g2.astype(F32) * out.astype(F32), axis=1, keepdims=True)
     high = delta.astype(BF16).astype(F32)
     lane = lax.broadcasted_iota(jnp.int32, g2.shape, 1)
@@ -322,18 +321,18 @@
 
 def own_body(size, core, masks, tok, group, *refs):
     take = taker(refs)
-    (seg_k, seg_q), qg_pieces, (kv,) = take(2), take(len(masks)), take(1)
-    e_own, out_part, stats, qg = take(4)
+    (seg_k, seg_q), q_pieces, (kv,) = take(2), take(len(masks)), take(1)
+    e_own, out_part, stats, q_rows = take(4)
     ka, vt, s_scr = take(3)
     wide, tiles = group * TILE, tok // TILE
-    place_rows(size, core, masks, qg_pieces, qg)
+    place_rows(size, core, masks, q_pieces, q_rows)
     ka[:, :HEAD_DIM] = kv[:, :HEAD_DIM]
     ka[:, HEAD_DIM:] = seg_k[WINDOW:, :]
     vt[...] = kv[:, HEAD_DIM:].T
     causal = tile_causal(group)
 
     def scores(tile):
-        queries = query_columns(qg, seg_q, tile * TILE, group)
+        queries = query_columns(q_rows, seg_q, tile * TILE, group)
         s_scr[tile % 2, : (tile + 1) * TILE, :] = dot_t(ka[: (tile + 1) * TILE, :], queries)
 
     def weights(tile):
@@ -354,10 +353,13 @@
 
 def forward_body(size, core, masks, reach, tok, group, *refs):
     take = taker(refs)
-    (seg_k, seg_q, qg), kvs, (out_own, stats) = take(3), take(reach), take(2)
+    (seg_k, seg_q, q_rows), g_pieces, kvs = take(3), take(len(masks)), take(reach)
+    out_own, stats = take(2)
     out_pieces, sent, (outs, own_scale, ds_early, kt) = take(len(masks)), take(reach), take(4)
+    (g_rows,) = take(1)
     ka, va, vt, dk, dv, s_scr, e_scr, dp_scr, g_scr = take(9)
     wide, tiles = group * TILE, tok // TILE
+    place_rows(size, core, masks, g_pieces, g_rows)
     ka[:, HEAD_DIM:] = seg_k[:WINDOW, :]
     for lag in range(1, reach + 1):
         there = slice((reach - lag) * tok, (reach - lag + 1) * tok)
@@ -370,7 +372,7 @@
 
     def scores(tile):
         base = tile * TILE
-        queries = query_columns(qg, seg_q, base, group)
+        queries = query_columns(q_rows, seg_q, base, group)
         s_scr[tile % 2, : WINDOW - base, :] = dot_t(ka[base:, :], queries)
 
     scales = {}
@@ -396,7 +398,7 @@
         out = out + out_own[:, tile * wide : (tile + 1) * wide] * scale
         out = (out * inv).T.astype(BF16)
         unstacked(outs, base, group, out)
-        g_scr[turn], g_wide = gradient_rows(qg, base, group, inv, out)
+        g_scr[turn], g_wide = gradient_rows(g_rows, base, group, inv, out)
         dp_scr[turn, :early, :] = dot_t(va[base:, :], g_wide)
 
     def gradients(tile):
@@ -407,7 +409,7 @@
         add_rows(dv, base, old, dot(e, g_scr[turn]))
         ds = ds_early.at[early_rows(tile), :]
         score_gradients(ds, e, dp_scr.at[turn, :early, :])
-        add_rows(dk, base, old, dot(ds[...], stacked(qg, base, group)))
+        add_rows(dk, base, old, dot(ds[...], stacked(q_rows, base, group)))
 
     pipeline(tiles, scores, weights, outputs, gradients)
 
@@ -420,7 +422,7 @@
 
 def backward_body(size, core, masks, tok, group, *refs):
     take = taker(refs)
-    qg, kv, e_own, outs, own_scale, ds_early, kt_early = take(7)
+    q_rows, kv, e_own, outs, own_scale, ds_early, kt_early, g_rows = take(8)
     dq_pieces, (dkv,) = take(len(masks)), take(1)
     dqs, va, kt, dk, dv, dp_scr, ds_scr, g_scr = take(8)
     wide = group * TILE
@@ -431,7 +433,7 @@
         base, turn = tile * TILE, tile % 2
         scale = own_scale[tile : tile + 1, :]
         out = stacked(outs, base, group)
-        g_scr[turn], g_wide = gradient_rows(qg, base, group, scale, out)
+        g_scr[turn], g_wide = gradient_rows(g_rows, base, group, scale, out)
         dp_scr[turn, : base + TILE, :] = dot_t(va[: base + TILE, :], g_wide)
 
     def gradients(tile):
@@ -441,7 +443,7 @@
         add_rows(dv, 0, base, dot(e, g_scr[turn]))
         score_gradients(ds_scr.at[turn, :count, :], e, dp_scr.at[turn, :count, :])
         ds = ds_scr[turn, :count, :]
-        add_rows(dk, 0, base, dot(ds, stacked(qg, base, group)))
+        add_rows(dk, 0, base, dot(ds, stacked(q_rows, base, group)))
         dq = dot(kt_early[:, base:], ds_early[early_rows(tile), :]) + dot(kt[:, :count], ds)
         dq = dq * logit_scale
         unstacked(dqs, base, group, dq.T.astype(BF16))
@@ -467,10 +469,10 @@
     )(*args)
 
 
-def forward_own(documents, qg, kv, size):
-    rows, cols = qg[0].shape
-    tok = len(qg) * rows
-    group = cols // (2 * HEAD_DIM)
+def forward_own(documents, q_pieces, kv, size):
+    rows, cols = q_pieces[0].shape
+    tok = len(q_pieces) * rows
+    group = cols // HEAD_DIM
     wide, tiles = group * TILE, tok // TILE
     return attend_call(
         functools.partial(own_body, size, core_mask(), chip_masks(size), tok, group),
@@ -488,23 +490,24 @@
         16 * tok * group * (WINDOW + TILE) * HEAD_DIM,
         "forward_own",
         *documents,
-        *qg,
+        *q_pieces,
         kv,
     )
 
 
-def forward(documents, qg, lags, carried, size):
-    (tok, cols), count, reach = qg.shape, len(chip_masks(size)), len(lags)
+def forward(documents, q_rows, g_pieces, lags, carried, size):
+    (tok, cols), count, reach = q_rows.shape, len(chip_masks(size)), len(lags)
     rows = tok // count
-    group = cols // (2 * HEAD_DIM)
+    group = cols // HEAD_DIM
     wide, tiles = group * TILE, tok // TILE
     half = jax.ShapeDtypeStruct((tok, 2 * HEAD_DIM), BF16)
-    out_shape = [jax.ShapeDtypeStruct((rows, cols // 2), BF16)] * count + [half] * reach
+    out_shape = [jax.ShapeDtypeStruct((rows, cols), BF16)] * count + [half] * reach
     out_shape += [
-        jax.ShapeDtypeStruct((tok, cols // 2), BF16),
+        jax.ShapeDtypeStruct((tok, cols), BF16),
         jax.ShapeDtypeStruct((tiles, wide), F32),
         jax.ShapeDtypeStruct((early_rows(tiles - 1).stop, wide), BF16),
         jax.ShapeDtypeStruct((HEAD_DIM, WINDOW), BF16),
+        jax.ShapeDtypeStruct((tok, cols), BF16),
     ]
     scratch = [
         pltpu.VMEM((WINDOW, 2 * HEAD_DIM), BF16),
@@ -526,24 +529,25 @@
         6 * tok * group * (WINDOW + TILE) * HEAD_DIM,
         "forward",
         *documents,
-        qg,
+        q_rows,
+        *g_pieces,
         *lags,
         *carried,
     )
     return results[:count], results[count : count + reach], results[count + reach :]
 
 
-def backward(qg, kv, carried, size):
-    (tok, cols), count = qg.shape, len(chip_masks(size))
+def backward(q_rows, kv, carried, size):
+    (tok, cols), count = q_rows.shape, len(chip_masks(size))
     rows = tok // count
-    group = cols // (2 * HEAD_DIM)
+    group = cols // HEAD_DIM
     wide = group * TILE
     results = attend_call(
         functools.partial(backward_body, size, core_mask(), chip_masks(size), tok, group),
-        [jax.ShapeDtypeStruct((rows, cols // 2), BF16)] * count
+        [jax.ShapeDtypeStruct((rows, cols), BF16)] * count
         + [jax.ShapeDtypeStruct((tok, 2 * HEAD_DIM), F32)],
         [
-            pltpu.VMEM((tok, cols // 2), BF16),
+            pltpu.VMEM((tok, cols), BF16),
             pltpu.VMEM((tok, 2 * HEAD_DIM), BF16),
             pltpu.VMEM((HEAD_DIM, tok), BF16),
             pltpu.VMEM((tok, HEAD_DIM), F32),
@@ -554,7 +558,7 @@
         ],
         4 * tok * group * (WINDOW + TILE) * HEAD_DIM,
         "backward",
-        qg,
+        q_rows,
         kv,
         *carried,
     )
@@ -587,13 +591,14 @@
     documents = document_columns(segment_ids, tok, size)
     kv = join(swap_chips(pieces, size), size)
     lags = [shifted(kv, lag * size) for lag in range(1, reach + 1)]
-    qg = swap_chips(gather_cores((query, grad_out), got[2:], size), size)
-
-    e_own, *partial, qg = forward_own(documents, qg, kv, size)
-    out, sent, carried = forward(documents, qg, lags, partial, size)
+    q_pieces = swap_chips(gather_cores((query,), got[2:3], size), size)
+    g_pieces = swap_chips(gather_cores((grad_out,), got[3:], size), size)
+
+    e_own, *partial, q_rows = forward_own(documents, q_pieces, kv, size)
+    out, sent, carried = forward(documents, q_rows, g_pieces, lags, partial, size)
     backs = [shifted(sent[lag - 1], -lag * size) for lag in range(1, reach + 1)]
     out = swap_chips(out, size)
-    grad_q, dkv = backward(qg, kv, [e_own, *carried], size)
+    grad_q, dkv = backward(q_rows, kv, [e_own, *carried], size)
     both = after(*out, *grad_q)
     out, grad_q = both[: len(out)], both[len(out) :]
     grad_q = swap_chips(grad_q, size)

time: 60.5 us -> 62.2 us (1.028)
  starting transfers between devices: 26.6 us -> 31.1 us
  waiting for transfers between devices: 17.9 us -> 15 us
    ppermute x20 -> x23, starting transfers between devices: 21.6 us -> 26.2 us  [swap(): lax.ppermute(value, BOTH, [(i, i ^ mask) for i in range(device_count())])]
    ppermute x20 -> x23, waiting for transfers between devices: 17 us -> 15 us  [swap(): lax.ppermute(value, BOTH, [(i, i ^ mask) for i in range(device_count())])]
    ppermute x2, waiting for transfers between devices: 0.93 us -> 0.01 us  [shifted(): return lax.ppermute(value, BOTH, pairs)]
  transfers between devices with their start and end apart: 22 -> 25, of which waited for: 11 -> 8; matrix products, arithmetic and copies ran while one was open for 3% -> 3% of each run, Pallas kernels for 11% -> 10%
where the time goes in v19:
time: 62.2 us; the launch traced here: 62 us
  starting transfers between devices  31.1 us (50%)
  waiting for transfers between devices  15 us (24%)
  Pallas kernels  12.8 us (21%)
  local copies, waits for them, and re-layouts  1.22 us (2%)
  between operations  1.14 us (2%)
  other arithmetic  0.73 us (1%)
    ppermute x23, starting transfers between devices, swap(): lax.ppermute(value, BOTH, [(i, i ^ mask) for i in range(device_count())])  26.2 us
    ppermute x23, waiting for transfers between devices, swap(): lax.ppermute(value, BOTH, [(i, i ^ mask) for i in range(device_count())])  15 us
    pallas_call x3, Pallas kernels, attend_call(): pl.pallas_call(kernel, out_shape=out_shape, in_specs=[VMEM] * len(args),...  10.9 us
    ppermute x2, starting transfers between devices, shifted(): return lax.ppermute(value, BOTH, pairs)  4.99 us
    pallas_call x1, Pallas kernels, spread_cores(): pl.pallas_call(functools.partial(spread_body, size, core_mask(), chip_mas...  1.39 us
  transfers between devices with their start and end apart: 25, of which 8 were waited for; matrix products, arithmetic and copies ran while one was open for 3% of the time, Pallas kernels for 10%

profile of v19, /device:TPU:0, one launch (start us, length us, event | category | flops | bytes accessed | tf_op | source)
XLA Modules:
  0.0 62.0 jit_solution(2771647329814416478)
XLA Ops:
  0.7 0.5 collective-permute-start
  1.3 0.4 collective-permute-start.2
  1.8 1.1 %fusion.2 = (bf16[128,256]{1,0:T(8,128)(2,1)S(1)}, bf16[128,256]{1,0:T(8,128)(2,1)S(1)}, bf16[128,256]{1,0:T(8,128)(2,1)S(1)}, bf16[128,256]{1,0:T(8,128)(2,1)S(...) fusion(bf16[128,1024]{1,0:T(8,128)(2,1)} %param.7, ...), kind=kLoop, calls=%fused_computation.11 | loop fusion | bytes 1048576 | tf_op jit(solution)/shard_map/slice | solution.py:94
  3.2 3.0 %collective-permute-start.6 = (bf16[256,256]{1,0:T(8,128)(2,1)S(1)}, bf16[256,256]{1,0:T(8,128)(2,1)S(1)}, u32[]{:S(2)}, u32[]{:S(2)}) collective-permute-start(bf16[256,256]{1,0:T(8,128)(2,1)S(1)} %get-tuple-element.63), channel_id=1, source_target_pairs={{0,1},{1,0},{2,3},{3,2},{4,5},{5,4},{6,7},{7,6},{8,9},{9,8},{10,11... | collective-permute-start | bytes 393224 | tf_op jit(solution)/shard_map/ppermute | solution.py:35
  6.2 1.5 %collective-permute-start.7 = (bf16[256,256]{1,0:T(8,128)(2,1)S(1)}, bf16[256,256]{1,0:T(8,128)(2,1)S(1)}, u32[]{:S(2)}, u32[]{:S(2)}) collective-permute-start(bf16[256,256]{1,0:T(8,128)(2,1)S(1)} %get-tuple-element.64), channel_id=1, source_target_pairs={{0,4},{1,5},{2,6},{3,7},{4,0},{5,1},{6,2},{7,3},{8,12},{9,13},{10,... | collective-permute-start | bytes 393224 | tf_op jit(solution)/shard_map/ppermute | solution.py:35
  8.4 2.0 %collective-permute-start.3 = (bf16[256,256]{1,0:T(8,128)(2,1)S(1)}, bf16[256,256]{1,0:T(8,128)(2,1)S(1)}, u32[]{:S(2)}, u32[]{:S(2)}) collective-permute-start(bf16[256,256]{1,0:T(8,128)(2,1)S(1)} %get-tuple-element.59), channel_id=1, source_target_pairs={{0,1},{1,0},{2,3},{3,2},{4,5},{5,4},{6,7},{7,6},{8,9},{9,8},{10,11... | collective-permute-start | bytes 393224 | tf_op jit(solution)/shard_map/ppermute | solution.py:35
  10.4 1.7 %collective-permute-start.4 = (bf16[256,256]{1,0:T(8,128)(2,1)S(1)}, bf16[256,256]{1,0:T(8,128)(2,1)S(1)}, u32[]{:S(2)}, u32[]{:S(2)}) collective-permute-start(bf16[256,256]{1,0:T(8,128)(2,1)S(1)} %get-tuple-element.60), channel_id=1, source_target_pairs={{0,4},{1,5},{2,6},{3,7},{4,0},{5,1},{6,2},{7,3},{8,12},{9,13},{10,... | collective-permute-start | bytes 393224 | tf_op jit(solution)/shard_map/ppermute | solution.py:35
  12.1 2.4 %collective-permute-done.7.refs_2_ = bf16[256,256]{1,0:T(8,128)(2,1)S(1)} collective-permute-done((bf16[256,256]{1,0:T(8,128)(2,1)S(1)}, bf16[256,256]{1,0:T(8,128)(2,1)S(1)}, u32[]{:S(2)}, u32[]{:S(2)}) %collective-permute-start.7) | collective-permute-done | bytes 131104 | tf_op jit(solution)/shard_map/ppermute | solution.py:35
  14.4 0.9 %collective-permute-start.5 = (bf16[256,256]{1,0:T(8,128)(2,1)S(1)}, bf16[256,256]{1,0:T(8,128)(2,1)S(1)}, u32[]{:S(2)}, u32[]{:S(2)}) collective-permute-start(bf16[256,256]{1,0:T(8,128)(2,1)S(1)} %get-tuple-element.61), channel_id=1, source_target_pairs={{0,5},{1,4},{2,7},{3,6},{4,1},{5,0},{6,3},{7,2},{8,13},{9,12},{10,... | collective-permute-start | bytes 393224 | tf_op jit(solution)/shard_map/ppermute | solution.py:35
  15.7 3.5 %collective-permute-start.13 = (bf16[1024,256]{1,0:T(8,128)(2,1)S(1)}, bf16[1024,256]{1,0:T(8,128)(2,1)S(1)}, u32[]{:S(2)}, u32[]{:S(2)}) collective-permute-start(bf16[1024,256]{1,0:T(8,128)(2,1)S(1)} %join.1.refs_6_.refs_1_), channel_id=1, source_target_pairs={{0,8},{1,9},{2,10},{3,11},{4,12},{5,13},{6,14},{7,15},{8,16},{9,17... | collective-permute-start | bytes 1572872 | tf_op jit(solution)/shard_map/ppermute | solution.py:55
  19.4 3.7 %collective-permute-start.10 = (bf16[256,256]{1,0:T(8,128)(2,1)S(1)}, bf16[256,256]{1,0:T(8,128)(2,1)S(1)}, u32[]{:S(2)}, u32[]{:S(2)}) collective-permute-start(bf16[256,256]{1,0:T(8,128)(2,1)S(1)} %get-tuple-element.69), channel_id=1, source_target_pairs={{0,1},{1,0},{2,3},{3,2},{4,5},{5,4},{6,7},{7,6},{8,9},{9,8},{10,11... | collective-permute-start | bytes 393224 | tf_op jit(solution)/shard_map/ppermute | solution.py:35
  23.1 1.5 %collective-permute-start.12 = (bf16[256,256]{1,0:T(8,128)(2,1)S(1)}, bf16[256,256]{1,0:T(8,128)(2,1)S(1)}, u32[]{:S(2)}, u32[]{:S(2)}) collective-permute-start(bf16[256,256]{1,0:T(8,128)(2,1)S(1)} %get-tuple-element.71), channel_id=1, source_target_pairs={{0,5},{1,4},{2,7},{3,6},{4,1},{5,0},{6,3},{7,2},{8,13},{9,12},{10,... | collective-permute-start | bytes 393224 | tf_op jit(solution)/shard_map/ppermute | solution.py:35
  24.6 2.3 %forward_own.1 = (bf16[4608,256]{1,0:T(8,128)(2,1)S(1)}, f32[128,2048]{1,0:T(8,128)S(1)}, f32[16,256]{1,0:T(8,128)S(1)}, bf16[1024,256]{1,0:T(8,128)(2,1)S(1)}) custom-call(bf16[2048,128]{1,0:T(8,128)(2,1)S(1)} %select_convert_fusion.refs_0_, bf16[1024,128]{1,0:T(8,128)(2,1)S(1)} %select_convert_fusion.1.refs_1_, ...), custom_call_target="tpu_custom_call" | custom-call | flops 4831838208 | bytes 8388608 | tf_op jit(solution)/shard_map/forward_own/pallas_call | solution.py:458
  27.0 2.5 %collective-permute-done.11.refs_5_ = bf16[256,256]{1,0:T(8,128)(2,1)S(1)} collective-permute-done((bf16[256,256]{1,0:T(8,128)(2,1)S(1)}, bf16[256,256]{1,0:T(8,128)(2,1)S(1)}, u32[]{:S(2)}, u32[]{:S(2)}) %collective-permute-start.11) | collective-permute-done | bytes 131104 | tf_op jit(solution)/shard_map/ppermute | solution.py:35
  29.4 4.9 %forward.1 = (bf16[256,256]{1,0:T(8,128)(2,1)S(1)}, bf16[256,256]{1,0:T(8,128)(2,1)S(1)}, bf16[256,256]{1,0:T(8,128)(2,1)S(1)}, bf16[256,256]{1,0:T(8,128)(2,1)S...) custom-call(bf16[2048,128]{1,0:T(8,128)(2,1)S(1)} %select_convert_fu, ...), custom_call_target="tpu_custom_call" | custom-call | flops 1811939328 | bytes 8388608 | tf_op jit(solution)/shard_map/forward/pallas_call | solution.py:458
  34.3 1.5 %collective-permute-start.20 = (bf16[1024,256]{1,0:T(8,128)(2,1)S(1)}, bf16[1024,256]{1,0:T(8,128)(2,1)S(1)}, u32[]{:S(2)}, u32[]{:S(2)}) collective-permute-start(bf16[1024,256]{1,0:T(8,128)(2,1)S(1)} %get-tuple-element.97), channel_id=1, source_target_pairs={{8,0},{9,1},{10,2},{11,3},{12,4},{13,5},{14,6},{15,7},{16,8},{17,9... | collective-permute-start | bytes 1572872 | tf_op jit(solution)/shard_map/ppermute | solution.py:55
  36.0 1.5 %collective-permute-start.15 = (bf16[256,256]{1,0:T(8,128)(2,1)S(1)}, bf16[256,256]{1,0:T(8,128)(2,1)S(1)}, u32[]{:S(2)}, u32[]{:S(2)}) collective-permute-start(bf16[256,256]{1,0:T(8,128)(2,1)S(1)} %get-tuple-element.76), channel_id=1, source_target_pairs={{0,4},{1,5},{2,6},{3,7},{4,0},{5,1},{6,2},{7,3},{8,12},{9,13},{10,... | collective-permute-start | bytes 393224 | tf_op jit(solution)/shard_map/ppermute | solution.py:35
  37.5 1.9 %collective-permute-start.16 = (bf16[256,256]{1,0:T(8,128)(2,1)S(1)}, bf16[256,256]{1,0:T(8,128)(2,1)S(1)}, u32[]{:S(2)}, u32[]{:S(2)}) collective-permute-start(bf16[256,256]{1,0:T(8,128)(2,1)S(1)} %get-tuple-element.77), channel_id=1, source_target_pairs={{0,5},{1,4},{2,7},{3,6},{4,1},{5,0},{6,3},{7,2},{8,13},{9,12},{10,... | collective-permute-start | bytes 393224 | tf_op jit(solution)/shard_map/ppermute | solution.py:35
  39.4 3.7 %backward.1 = (bf16[256,256]{1,0:T(8,128)(2,1)S(1)}, bf16[256,256]{1,0:T(8,128)(2,1)S(1)}, bf16[256,256]{1,0:T(8,128)(2,1)S(1)}, bf16[256,256]{1,0:T(8,128)(2,1)S(1)}, f32[1024,256]{1,0:T(8,128)S(1)}) custom-call(bf16[1024,256]{1,0:T(8,128)(2,1)S(1)} %get-tuple-element.66.refs_2_.refs_0_, bf16[1024,256]{1,0:T(8,128)(2,1)S(1)} %join.1.refs_6_.refs_1_, ...), custom_call_target="tpu_custom_call" | custom-call | flops 1207959552 | bytes 8388608 | tf_op jit(solution)/shard_map/backward/pallas_call | solution.py:458
  43.1 3.0 %collective-permute-done.16.refs_3_ = bf16[256,256]{1,0:T(8,128)(2,1)S(1)} collective-permute-done((bf16[256,256]{1,0:T(8,128)(2,1)S(1)}, bf16[256,256]{1,0:T(8,128)(2,1)S(1)}, u32[]{:S(2)}, u32[]{:S(2)}) %collective-permute-start.16) | collective-permute-done | bytes 131104 | tf_op jit(solution)/shard_map/ppermute | solution.py:35
  46.1 0.9 %collective-permute-start.17 = (bf16[256,256]{1,0:T(8,128)(2,1)S(1)}, bf16[256,256]{1,0:T(8,128)(2,1)S(1)}, u32[]{:S(2)}, u32[]{:S(2)}) collective-permute-start(bf16[256,256]{1,0:T(8,128)(2,1)S(1)} %get-tuple-element.93), channel_id=1, source_target_pairs={{0,1},{1,0},{2,3},{3,2},{4,5},{5,4},{6,7},{7,6},{8,9},{9,8},{10,11... | collective-permute-start | bytes 393224 | tf_op jit(solution)/shard_map/ppermute | solution.py:35
  47.0 1.5 %collective-permute-start.18 = (bf16[256,256]{1,0:T(8,128)(2,1)S(1)}, bf16[256,256]{1,0:T(8,128)(2,1)S(1)}, u32[]{:S(2)}, u32[]{:S(2)}) collective-permute-start(bf16[256,256]{1,0:T(8,128)(2,1)S(1)} %get-tuple-element.94), channel_id=1, source_target_pairs={{0,4},{1,5},{2,6},{3,7},{4,0},{5,1},{6,2},{7,3},{8,12},{9,13},{10,... | collective-permute-start | bytes 393224 | tf_op jit(solution)/shard_map/ppermute | solution.py:35
  48.5 1.0 %collective-permute-start.19 = (bf16[256,256]{1,0:T(8,128)(2,1)S(1)}, bf16[256,256]{1,0:T(8,128)(2,1)S(1)}, u32[]{:S(2)}, u32[]{:S(2)}) collective-permute-start(bf16[256,256]{1,0:T(8,128)(2,1)S(1)} %get-tuple-element.95), channel_id=1, source_target_pairs={{0,5},{1,4},{2,7},{3,6},{4,1},{5,0},{6,3},{7,2},{8,13},{9,12},{10,... | collective-permute-start | bytes 393224 | tf_op jit(solution)/shard_map/ppermute | solution.py:35
  49.6 1.0 %collective-permute-start.21 = (bf16[256,256]{1,0:T(8,128)(2,1)S(1)}, bf16[256,256]{1,0:T(8,128)(2,1)S(1)}, u32[]{:S(2)}, u32[]{:S(2)}) collective-permute-start(bf16[256,256]{1,0:T(8,128)(2,1)S(1)} %get-tuple-element.99), channel_id=1, source_target_pairs={{0,1},{1,0},{2,3},{3,2},{4,5},{5,4},{6,7},{7,6},{8,9},{9,8},{10,11... | collective-permute-start | bytes 393224 | tf_op jit(solution)/shard_map/ppermute | solution.py:35
  50.6 1.5 %collective-permute-start.22 = (bf16[256,256]{1,0:T(8,128)(2,1)S(1)}, bf16[256,256]{1,0:T(8,128)(2,1)S(1)}, u32[]{:S(2)}, u32[]{:S(2)}) collective-permute-start(bf16[256,256]{1,0:T(8,128)(2,1)S(1)} %get-tuple-element.100), channel_id=1, source_target_pairs={{0,4},{1,5},{2,6},{3,7},{4,0},{5,1},{6,2},{7,3},{8,12},{9,13},{10,... | collective-permute-start | bytes 393224 | tf_op jit(solution)/shard_map/ppermute | solution.py:35
  52.2 1.0 %collective-permute-start.23 = (bf16[256,256]{1,0:T(8,128)(2,1)S(1)}, bf16[256,256]{1,0:T(8,128)(2,1)S(1)}, u32[]{:S(2)}, u32[]{:S(2)}) collective-permute-start(bf16[256,256]{1,0:T(8,128)(2,1)S(1)} %get-tuple-element.101), channel_id=1, source_target_pairs={{0,5},{1,4},{2,7},{3,6},{4,1},{5,0},{6,3},{7,2},{8,13},{9,12},{10,... | collective-permute-start | bytes 393224 | tf_op jit(solution)/shard_map/ppermute | solution.py:35
  53.2 1.2 %collective-permute-done.19.refs_7_ = bf16[256,256]{1,0:T(8,128)(2,1)S(1)} collective-permute-done((bf16[256,256]{1,0:T(8,128)(2,1)S(1)}, bf16[256,256]{1,0:T(8,128)(2,1)S(1)}, u32[]{:S(2)}, u32[]{:S(2)}) %collective-permute-start.19) | collective-permute-done | bytes 131104 | tf_op jit(solution)/shard_map/ppermute | solution.py:35
  54.4 0.4 collective-permute-done.21.refs_9_
  54.8 1.0 %collective-permute-done.22.refs_10_ = bf16[256,256]{1,0:T(8,128)(2,1)S(1)} collective-permute-done((bf16[256,256]{1,0:T(8,128)(2,1)S(1)}, bf16[256,256]{1,0:T(8,128)(2,1)S(1)}, u32[]{:S(2)}, u32[]{:S(2)}) %collective-permute-start.22) | collective-permute-done | bytes 131104 | tf_op jit(solution)/shard_map/ppermute | solution.py:35
  55.8 2.2 %collective-permute-done.23.refs_11_ = bf16[256,256]{1,0:T(8,128)(2,1)S(1)} collective-permute-done((bf16[256,256]{1,0:T(8,128)(2,1)S(1)}, bf16[256,256]{1,0:T(8,128)(2,1)S(1)}, u32[]{:S(2)}, u32[]{:S(2)}) %collective-permute-start.23) | collective-permute-done | bytes 131104 | tf_op jit(solution)/shard_map/ppermute | solution.py:35
  58.2 2.3 %collective-permute-done.24.refs_12_ = bf16[128,3072]{1,0:T(8,128)(2,1)S(1)} collective-permute-done((bf16[128,3072]{1,0:T(8,128)(2,1)S(1)}, bf16[128,3072]{1,0:T(8,128)(2,1)S(1)}, u32[]{:S(2)}, u32[]{:S(2)}) %collective-permute-start.24) | collective-permute-done | bytes 786464 | tf_op jit(solution)/shard_map/ppermute | solution.py:35
  60.5 1.4 %spread.1 = (bf16[128,2048]{1,0:T(8,128)(2,1)}, bf16[128,2048]{1,0:T(8,128)(2,1)}, bf16[128,1024]{1,0:T(8,128)(2,1)}, bf16[128,1024]{1,0:T(8,128)(2,1)}) custom-call(bf16[256,256]{1,0:T(8,128)(2,1)S(1)} %get-tuple-element.88.refs_0_, bf16[256,256]{1,0:T(8,128)(2,1)S(1)} %collective-permute-done.14.refs_1_, ...), custom_call_target="tpu_custom_call" | custom-call | tf_op jit(solution)/shard_map/spread/pallas_call | solution.py:201
  (46 shorter events, 1.8 us)
Async XLA Ops:
  0.6 7.5 %copy-start = (bf16[128,2048]{1,0:T(8,128)(2,1)S(1)}, bf16[128,2048]{1,0:T(8,128)(2,1)}, u32[]{:S(2)}) copy-start(bf16[128,2048]{1,0:T(8,128)(2,1)} %param.5) | copy-start | bytes 1572868
  0.6 7.4 %copy-start.1 = (bf16[128,2048]{1,0:T(8,128)(2,1)S(1)}, bf16[128,2048]{1,0:T(8,128)(2,1)}, u32[]{:S(2)}) copy-start(bf16[128,2048]{1,0:T(8,128)(2,1)} %param.8) | copy-start | bytes 1572868
  0.7 2.5 %copy-start.2 = (s32[4096]{0:T(1024)S(1)}, s32[4096]{0:T(1024)}, u32[]{:S(2)}) copy-start(s32[4096]{0:T(1024)} %param.9) | copy-start | bytes 49156
  0.7 2.4 %collective-permute-start = (bf16[128,1024]{1,0:T(8,128)(2,1)}, bf16[128,1024]{1,0:T(8,128)(2,1)S(1)}, u32[]{:S(2)}, u32[]{:S(2)}) collective-permute-start(bf16[128,1024]{1,0:T(8,128)(2,1)} %param.6), channel_id=1, source_target_pairs={{0,2},{1,3},{2,0},{3,1},{4,6},{5,7},{6,4},{7,5},{8,10},{9,11},{10,... | collective-permute-start | bytes 786440 | tf_op jit(solution)/shard_map/ppermute | solution.py:35
  1.2 1.9 %collective-permute-start.1 = (bf16[128,1024]{1,0:T(8,128)(2,1)}, bf16[128,1024]{1,0:T(8,128)(2,1)S(1)}, u32[]{:S(2)}, u32[]{:S(2)}) collective-permute-start(bf16[128,1024]{1,0:T(8,128)(2,1)} %param.7), channel_id=1, source_target_pairs={{0,2},{1,3},{2,0},{3,1},{4,6},{5,7},{6,4},{7,5},{8,10},{9,11},{10,... | collective-permute-start | bytes 786440 | tf_op jit(solution)/shard_map/ppermute | solution.py:35
  1.3 7.0 %collective-permute-start.2 = (bf16[128,2048]{1,0:T(8,128)(2,1)}, bf16[128,2048]{1,0:T(8,128)(2,1)S(1)}, u32[]{:S(2)}, u32[]{:S(2)}) collective-permute-start(bf16[128,2048]{1,0:T(8,128)(2,1)} %param.5), channel_id=1, source_target_pairs={{0,2},{1,3},{2,0},{3,1},{4,6},{5,7},{6,4},{7,5},{8,10},{9,11},{10,... | collective-permute-start | bytes 1572872 | tf_op jit(solution)/shard_map/ppermute | solution.py:35
  1.7 17.6 %collective-permute-start.9 = (bf16[128,2048]{1,0:T(8,128)(2,1)}, bf16[128,2048]{1,0:T(8,128)(2,1)S(1)}, u32[]{:S(2)}, u32[]{:S(2)}) collective-permute-start(bf16[128,2048]{1,0:T(8,128)(2,1)} %param.8), channel_id=1, source_target_pairs={{0,2},{1,3},{2,0},{3,1},{4,6},{5,7},{6,4},{7,5},{8,10},{9,11},{10,... | collective-permute-start | bytes 1572872 | tf_op jit(solution)/shard_map/ppermute | solution.py:35
  3.0 12.4 %dynamic-slice-start = ((s32[4096]{0:T(1024)}, s32[]{:T(128)}), s32[1024]{0:T(1024)S(1)}, s32[]{:S(2)}) async-start(s32[4096]{0:T(1024)} %param.9, s32[]{:T(128)} %select_n.69), calls=%async_computation | async-start | bytes 8704 | tf_op jit(solution)/shard_map/dynamic_slice | solution.py:572
  3.2 7.2 %collective-permute-start.6 = (bf16[256,256]{1,0:T(8,128)(2,1)S(1)}, bf16[256,256]{1,0:T(8,128)(2,1)S(1)}, u32[]{:S(2)}, u32[]{:S(2)}) collective-permute-start(bf16[256,256]{1,0:T(8,128)(2,1)S(1)} %get-tuple-element.63), channel_id=1, source_target_pairs={{0,1},{1,0},{2,3},{3,2},{4,5},{5,4},{6,7},{7,6},{8,9},{9,8},{10,11... | collective-permute-start | bytes 393224 | tf_op jit(solution)/shard_map/ppermute | solution.py:35
  6.2 8.2 %collective-permute-start.7 = (bf16[256,256]{1,0:T(8,128)(2,1)S(1)}, bf16[256,256]{1,0:T(8,128)(2,1)S(1)}, u32[]{:S(2)}, u32[]{:S(2)}) collective-permute-start(bf16[256,256]{1,0:T(8,128)(2,1)S(1)} %get-tuple-element.64), channel_id=1, source_target_pairs={{0,4},{1,5},{2,6},{3,7},{4,0},{5,1},{6,2},{7,3},{8,12},{9,13},{10,... | collective-permute-start | bytes 393224 | tf_op jit(solution)/shard_map/ppermute | solution.py:35
  7.7 7.9 %collective-permute-start.8 = (bf16[256,256]{1,0:T(8,128)(2,1)S(1)}, bf16[256,256]{1,0:T(8,128)(2,1)S(1)}, u32[]{:S(2)}, u32[]{:S(2)}) collective-permute-start(bf16[256,256]{1,0:T(8,128)(2,1)S(1)} %get-tuple-element.65), channel_id=1, source_target_pairs={{0,5},{1,4},{2,7},{3,6},{4,1},{5,0},{6,3},{7,2},{8,13},{9,12},{10,... | collective-permute-start | bytes 393224 | tf_op jit(solution)/shard_map/ppermute | solution.py:35
  8.4 14.7 %collective-permute-start.3 = (bf16[256,256]{1,0:T(8,128)(2,1)S(1)}, bf16[256,256]{1,0:T(8,128)(2,1)S(1)}, u32[]{:S(2)}, u32[]{:S(2)}) collective-permute-start(bf16[256,256]{1,0:T(8,128)(2,1)S(1)} %get-tuple-element.59), channel_id=1, source_target_pairs={{0,1},{1,0},{2,3},{3,2},{4,5},{5,4},{6,7},{7,6},{8,9},{9,8},{10,11... | collective-permute-start | bytes 393224 | tf_op jit(solution)/shard_map/ppermute | solution.py:35
  10.4 12.7 %collective-permute-start.4 = (bf16[256,256]{1,0:T(8,128)(2,1)S(1)}, bf16[256,256]{1,0:T(8,128)(2,1)S(1)}, u32[]{:S(2)}, u32[]{:S(2)}) collective-permute-start(bf16[256,256]{1,0:T(8,128)(2,1)S(1)} %get-tuple-element.60), channel_id=1, source_target_pairs={{0,4},{1,5},{2,6},{3,7},{4,0},{5,1},{6,2},{7,3},{8,12},{9,13},{10,... | collective-permute-start | bytes 393224 | tf_op jit(solution)/shard_map/ppermute | solution.py:35
  14.4 10.2 %collective-permute-start.5 = (bf16[256,256]{1,0:T(8,128)(2,1)S(1)}, bf16[256,256]{1,0:T(8,128)(2,1)S(1)}, u32[]{:S(2)}, u32[]{:S(2)}) collective-permute-start(bf16[256,256]{1,0:T(8,128)(2,1)S(1)} %get-tuple-element.61), channel_id=1, source_target_pairs={{0,5},{1,4},{2,7},{3,6},{4,1},{5,0},{6,3},{7,2},{8,13},{9,12},{10,... | collective-permute-start | bytes 393224 | tf_op jit(solution)/shard_map/ppermute | solution.py:35
  15.7 13.8 %collective-permute-start.13 = (bf16[1024,256]{1,0:T(8,128)(2,1)S(1)}, bf16[1024,256]{1,0:T(8,128)(2,1)S(1)}, u32[]{:S(2)}, u32[]{:S(2)}) collective-permute-start(bf16[1024,256]{1,0:T(8,128)(2,1)S(1)} %join.1.refs_6_.refs_1_), channel_id=1, source_target_pairs={{0,8},{1,9},{2,10},{3,11},{4,12},{5,13},{6,14},{7,15},{8,16},{9,17... | collective-permute-start | bytes 1572872 | tf_op jit(solution)/shard_map/ppermute | solution.py:55
  19.4 7.6 %collective-permute-start.10 = (bf16[256,256]{1,0:T(8,128)(2,1)S(1)}, bf16[256,256]{1,0:T(8,128)(2,1)S(1)}, u32[]{:S(2)}, u32[]{:S(2)}) collective-permute-start(bf16[256,256]{1,0:T(8,128)(2,1)S(1)} %get-tuple-element.69), channel_id=1, source_target_pairs={{0,1},{1,0},{2,3},{3,2},{4,5},{5,4},{6,7},{7,6},{8,9},{9,8},{10,11... | collective-permute-start | bytes 393224 | tf_op jit(solution)/shard_map/ppermute | solution.py:35
  23.1 6.4 %collective-permute-start.11 = (bf16[256,256]{1,0:T(8,128)(2,1)S(1)}, bf16[256,256]{1,0:T(8,128)(2,1)S(1)}, u32[]{:S(2)}, u32[]{:S(2)}) collective-permute-start(bf16[256,256]{1,0:T(8,128)(2,1)S(1)} %get-tuple-element.70), channel_id=1, source_target_pairs={{0,4},{1,5},{2,6},{3,7},{4,0},{5,1},{6,2},{7,3},{8,12},{9,13},{10,... | collective-permute-start | bytes 393224 | tf_op jit(solution)/shard_map/ppermute | solution.py:35
  23.1 6.4 %collective-permute-start.12 = (bf16[256,256]{1,0:T(8,128)(2,1)S(1)}, bf16[256,256]{1,0:T(8,128)(2,1)S(1)}, u32[]{:S(2)}, u32[]{:S(2)}) collective-permute-start(bf16[256,256]{1,0:T(8,128)(2,1)S(1)} %get-tuple-element.71), channel_id=1, source_target_pairs={{0,5},{1,4},{2,7},{3,6},{4,1},{5,0},{6,3},{7,2},{8,13},{9,12},{10,... | collective-permute-start | bytes 393224 | tf_op jit(solution)/shard_map/ppermute | solution.py:35
  34.3 15.2 %collective-permute-start.20 = (bf16[1024,256]{1,0:T(8,128)(2,1)S(1)}, bf16[1024,256]{1,0:T(8,128)(2,1)S(1)}, u32[]{:S(2)}, u32[]{:S(2)}) collective-permute-start(bf16[1024,256]{1,0:T(8,128)(2,1)S(1)} %get-tuple-element.97), channel_id=1, source_target_pairs={{8,0},{9,1},{10,2},{11,3},{12,4},{13,5},{14,6},{15,7},{16,8},{17,9... | collective-permute-start | bytes 1572872 | tf_op jit(solution)/shard_map/ppermute | solution.py:55
  35.8 7.2 %collective-permute-start.14 = (bf16[256,256]{1,0:T(8,128)(2,1)S(1)}, bf16[256,256]{1,0:T(8,128)(2,1)S(1)}, u32[]{:S(2)}, u32[]{:S(2)}) collective-permute-start(bf16[256,256]{1,0:T(8,128)(2,1)S(1)} %get-tuple-element.75), channel_id=1, source_target_pairs={{0,1},{1,0},{2,3},{3,2},{4,5},{5,4},{6,7},{7,6},{8,9},{9,8},{10,11... | collective-permute-start | bytes 393224 | tf_op jit(solution)/shard_map/ppermute | solution.py:35
  36.0 7.1 %collective-permute-start.15 = (bf16[256,256]{1,0:T(8,128)(2,1)S(1)}, bf16[256,256]{1,0:T(8,128)(2,1)S(1)}, u32[]{:S(2)}, u32[]{:S(2)}) collective-permute-start(bf16[256,256]{1,0:T(8,128)(2,1)S(1)} %get-tuple-element.76), channel_id=1, source_target_pairs={{0,4},{1,5},{2,6},{3,7},{4,0},{5,1},{6,2},{7,3},{8,12},{9,13},{10,... | collective-permute-start | bytes 393224 | tf_op jit(solution)/shard_map/ppermute | solution.py:35
  37.5 8.6 %collective-permute-start.16 = (bf16[256,256]{1,0:T(8,128)(2,1)S(1)}, bf16[256,256]{1,0:T(8,128)(2,1)S(1)}, u32[]{:S(2)}, u32[]{:S(2)}) collective-permute-start(bf16[256,256]{1,0:T(8,128)(2,1)S(1)} %get-tuple-element.77), channel_id=1, source_target_pairs={{0,5},{1,4},{2,7},{3,6},{4,1},{5,0},{6,3},{7,2},{8,13},{9,12},{10,... | collective-permute-start | bytes 393224 | tf_op jit(solution)/shard_map/ppermute | solution.py:35
  46.1 6.1 %collective-permute-start.17 = (bf16[256,256]{1,0:T(8,128)(2,1)S(1)}, bf16[256,256]{1,0:T(8,128)(2,1)S(1)}, u32[]{:S(2)}, u32[]{:S(2)}) collective-permute-start(bf16[256,256]{1,0:T(8,128)(2,1)S(1)} %get-tuple-element.93), channel_id=1, source_target_pairs={{0,1},{1,0},{2,3},{3,2},{4,5},{5,4},{6,7},{7,6},{8,9},{9,8},{10,11... | collective-permute-start | bytes 393224 | tf_op jit(solution)/shard_map/ppermute | solution.py:35
  47.0 6.2 %collective-permute-start.18 = (bf16[256,256]{1,0:T(8,128)(2,1)S(1)}, bf16[256,256]{1,0:T(8,128)(2,1)S(1)}, u32[]{:S(2)}, u32[]{:S(2)}) collective-permute-start(bf16[256,256]{1,0:T(8,128)(2,1)S(1)} %get-tuple-element.94), channel_id=1, source_target_pairs={{0,4},{1,5},{2,6},{3,7},{4,0},{5,1},{6,2},{7,3},{8,12},{9,13},{10,... | collective-permute-start | bytes 393224 | tf_op jit(solution)/shard_map/ppermute | solution.py:35
  48.5 5.9 %collective-permute-start.19 = (bf16[256,256]{1,0:T(8,128)(2,1)S(1)}, bf16[256,256]{1,0:T(8,128)(2,1)S(1)}, u32[]{:S(2)}, u32[]{:S(2)}) collective-permute-start(bf16[256,256]{1,0:T(8,128)(2,1)S(1)} %get-tuple-element.95), channel_id=1, source_target_pairs={{0,5},{1,4},{2,7},{3,6},{4,1},{5,0},{6,3},{7,2},{8,13},{9,12},{10,... | collective-permute-start | bytes 393224 | tf_op jit(solution)/shard_map/ppermute | solution.py:35
  49.6 5.2 %collective-permute-start.21 = (bf16[256,256]{1,0:T(8,128)(2,1)S(1)}, bf16[256,256]{1,0:T(8,128)(2,1)S(1)}, u32[]{:S(2)}, u32[]{:S(2)}) collective-permute-start(bf16[256,256]{1,0:T(8,128)(2,1)S(1)} %get-tuple-element.99), channel_id=1, source_target_pairs={{0,1},{1,0},{2,3},{3,2},{4,5},{5,4},{6,7},{7,6},{8,9},{9,8},{10,11... | collective-permute-start | bytes 393224 | tf_op jit(solution)/shard_map/ppermute | solution.py:35
  50.6 5.2 %collective-permute-start.22 = (bf16[256,256]{1,0:T(8,128)(2,1)S(1)}, bf16[256,256]{1,0:T(8,128)(2,1)S(1)}, u32[]{:S(2)}, u32[]{:S(2)}) collective-permute-start(bf16[256,256]{1,0:T(8,128)(2,1)S(1)} %get-tuple-element.100), channel_id=1, source_target_pairs={{0,4},{1,5},{2,6},{3,7},{4,0},{5,1},{6,2},{7,3},{8,12},{9,13},{10,... | collective-permute-start | bytes 393224 | tf_op jit(solution)/shard_map/ppermute | solution.py:35
  52.2 5.9 %collective-permute-start.23 = (bf16[256,256]{1,0:T(8,128)(2,1)S(1)}, bf16[256,256]{1,0:T(8,128)(2,1)S(1)}, u32[]{:S(2)}, u32[]{:S(2)}) collective-permute-start(bf16[256,256]{1,0:T(8,128)(2,1)S(1)} %get-tuple-element.101), channel_id=1, source_target_pairs={{0,5},{1,4},{2,7},{3,6},{4,1},{5,0},{6,3},{7,2},{8,13},{9,12},{10,... | collective-permute-start | bytes 393224 | tf_op jit(solution)/shard_map/ppermute | solution.py:35
  58.1 2.4 %collective-permute-start.24 = (bf16[128,3072]{1,0:T(8,128)(2,1)S(1)}, bf16[128,3072]{1,0:T(8,128)(2,1)S(1)}, u32[]{:S(2)}, u32[]{:S(2)}) collective-permute-start(bf16[128,3072]{1,0:T(8,128)(2,1)S(1)} %bottom.1), channel_id=1, source_target_pairs={{0,2},{1,3},{2,0},{3,1},{4,6},{5,7},{6,4},{7,5},{8,10},{9,11},{10,... | collective-permute-start | bytes 2359304 | tf_op jit(solution)/shard_map/ppermute | solution.py:35

commit v20 on v18

--- a/solution.py
+++ b/solution.py
@@ -249,11 +249,20 @@
     va[:, HEAD_DIM:] = jnp.where(lane < 2, 1.0, 0.0).astype(BF16)
 
 
-def add_rows(target, start, old, value):
-    if old:
-        target[start : start + old, :] += value[:old]
-    if old < value.shape[0]:
-        target[start + old : start + value.shape[0], :] = value[old:]
+def add_rows(target, start, value, known):
+    ends = range(0, value.shape[0] + TILE, TILE)
+    first = 0
+    for at in ends[1:]:
+        last = at == value.shape[0]
+        old = (start + at - TILE) in known
+        if last or ((start + at) in known) != old:
+            part = slice(start + first, start + at)
+            if old:
+                target[part, :] += value[first:at]
+            else:
+                target[part, :] = value[first:at]
+            first = at
+    known.update(range(start, start + value.shape[0], TILE))
 
 
 def score_gradients(ds_scr, e, dp):
@@ -262,11 +271,12 @@
         ds_scr[part, :] = (e[part, :].astype(F32) * dp[part, :]).astype(BF16)
 
 
-def pipeline(tiles, *stages):
-    for step in range(tiles + len(stages) - 1):
+def pipeline(order, *stages):
+    for step in range(len(order) + len(stages) - 1):
         for behind, stage in enumerate(stages):
-            if 0 <= step - behind < tiles:
-                stage(step - behind)
+            at = step - behind
+            if 0 <= at < len(order):
+                stage(order[at], at)
 
 
 def early_rows(tile):
@@ -332,12 +342,12 @@
     vt[...] = kv[:, HEAD_DIM:].T
     causal = tile_causal(group)
 
-    def scores(tile):
+    def scores(tile, at):
         queries = query_columns(qg, seg_q, tile * TILE, group)
-        s_scr[tile % 2, : (tile + 1) * TILE, :] = dot_t(ka[: (tile + 1) * TILE, :], queries)
-
-    def weights(tile):
-        base, turn = tile * TILE, tile % 2
+        s_scr[at % 2, : (tile + 1) * TILE, :] = dot_t(ka[: (tile + 1) * TILE, :], queries)
+
+    def weights(tile, at):
+        base, turn = tile * TILE, at % 2
         last = slice(base, base + TILE)
         s_scr[turn, last, :] = jnp.where(causal, s_scr[turn, last, :], FAR)
         rows = s_scr.at[turn, : base + TILE, :]
@@ -345,17 +355,17 @@
         stats[tile : tile + 1, :] = top
         stats[tiles + tile : tiles + tile + 1, :] = weigh(rows, top, e_own.at[own_rows(tile), :])
 
-    def outputs(tile):
+    def outputs(tile, at):
         e = e_own[own_rows(tile), :]
         out_part[:, tile * wide : (tile + 1) * wide] = dot(vt[:, : (tile + 1) * TILE], e)
 
-    pipeline(tiles, scores, weights, outputs)
+    pipeline([*range(1, tiles), 0], scores, weights, outputs)
 
 
 def forward_body(size, core, masks, reach, tok, group, *refs):
     take = taker(refs)
     (seg_k, seg_q, qg), kvs, (out_own, stats) = take(3), take(reach), take(2)
-    out_pieces, sent, (outs, own_scale, ds_early, kt) = take(len(masks)), take(reach), take(4)
+    out_pieces, sent, (outs, own_scale, ds_early) = take(len(masks)), take(reach), take(3)
     ka, va, vt, dk, dv, s_scr, e_scr, dp_scr, g_scr = take(9)
     wide, tiles = group * TILE, tok // TILE
     ka[:, HEAD_DIM:] = seg_k[:WINDOW, :]
@@ -363,53 +373,52 @@
         there = slice((reach - lag) * tok, (reach - lag + 1) * tok)
         kv = kvs[lag - 1][...]
         ka[there, :HEAD_DIM] = kv[:, :HEAD_DIM]
-        kt[:, there] = kv[:, :HEAD_DIM].T
         vt[:, there] = kv[:, HEAD_DIM:].T
         set_values(va.at[there, :], kv[:, HEAD_DIM:])
     beyond = ~tile_causal(group)
 
-    def scores(tile):
+    def scores(tile, at):
         base = tile * TILE
         queries = query_columns(qg, seg_q, base, group)
-        s_scr[tile % 2, : WINDOW - base, :] = dot_t(ka[base:, :], queries)
-
-    scales = {}
-
-    def weights(tile):
+        s_scr[at % 2, : WINDOW - base, :] = dot_t(ka[base:, :], queries)
+
+    scales, known = {}, (set(), set())
+
+    def weights(tile, at):
         early = WINDOW - tile * TILE
-        turn = tile % 2
+        turn = at % 2
         s_scr[turn, :TILE, :] = jnp.where(beyond, s_scr[turn, :TILE, :], FAR)
         rows = s_scr.at[turn, :early, :]
         top_own = stats[tile : tile + 1, :]
         top = jnp.maximum(fold_rows(rows, jnp.maximum) * exp2_scale, top_own)
-        total = weigh(rows, top, e_scr.at[tile % 3, :early, :])
+        total = weigh(rows, top, e_scr.at[at % 3, :early, :])
         scale = jnp.exp2(top_own - top)
         inv = 1.0 / (total + stats[tiles + tile : tiles + tile + 1, :] * scale)
         own_scale[tile : tile + 1, :] = inv * scale
         scales[tile] = scale, inv
 
-    def outputs(tile):
-        base, turn = tile * TILE, tile % 2
+    def outputs(tile, at):
+        base, turn = tile * TILE, at % 2
         early = WINDOW - base
         scale, inv = scales.pop(tile)
-        out = dot(vt[:, base:], e_scr[tile % 3, :early, :])
+        out = dot(vt[:, base:], e_scr[at % 3, :early, :])
         out = out + out_own[:, tile * wide : (tile + 1) * wide] * scale
         out = (out * inv).T.astype(BF16)
         unstacked(outs, base, group, out)
         g_scr[turn], g_wide = gradient_rows(qg, base, group, inv, out)
         dp_scr[turn, :early, :] = dot_t(va[base:, :], g_wide)
 
-    def gradients(tile):
-        base, turn = tile * TILE, tile % 2
+    def gradients(tile, at):
+        base, turn = tile * TILE, at % 2
         early = WINDOW - base
-        e = e_scr[tile % 3, :early, :]
-        old = early if tile else 0
-        add_rows(dv, base, old, dot(e, g_scr[turn]))
+        e = e_scr[at % 3, :early, :]
+        add_rows(dv, base, dot(e, g_scr[turn]), known[0])
         ds = ds_early.at[early_rows(tile), :]
         score_gradients(ds, e, dp_scr.at[turn, :early, :])
-        add_rows(dk, base, old, dot(ds[...], stacked(qg, base, group)))
-
-    pipeline(tiles, scores, weights, outputs, gradients)
+        add_rows(dk, base, dot(ds[...], stacked(qg, base, group)), known[1])
+
+    order = [tiles - 1, *range(tiles - 1)]
+    pipeline(order, scores, weights, outputs, gradients)
 
     for lag in range(1, reach + 1):
         there = slice((reach - lag) * tok, (reach - lag + 1) * tok)
@@ -418,35 +427,41 @@
     take_rows(size, core, masks, lambda there: outs[there, :], out_pieces)
 
 
-def backward_body(size, core, masks, tok, group, *refs):
+def backward_body(size, core, masks, reach, tok, group, *refs):
     take = taker(refs)
-    qg, kv, e_own, outs, own_scale, ds_early, kt_early = take(7)
+    qg, kv, e_own, outs, own_scale, ds_early = take(6)
+    lags = take(reach)
     dq_pieces, (dkv,) = take(len(masks)), take(1)
-    dqs, va, kt, dk, dv, dp_scr, ds_scr, g_scr = take(8)
+    dqs, va, kt, kt_early, dk, dv, dp_scr, ds_scr, g_scr = take(9)
     wide = group * TILE
     kt[...] = kv[:, :HEAD_DIM].T
+    for lag in range(1, reach + 1):
+        there = slice((reach - lag) * tok, (reach - lag + 1) * tok)
+        kt_early[:, there] = lags[lag - 1][:, :HEAD_DIM].T
     set_values(va, kv[:, HEAD_DIM:])
 
-    def products(tile):
-        base, turn = tile * TILE, tile % 2
+    known = (set(), set())
+
+    def products(tile, at):
+        base, turn = tile * TILE, at % 2
         scale = own_scale[tile : tile + 1, :]
         out = stacked(outs, base, group)
         g_scr[turn], g_wide = gradient_rows(qg, base, group, scale, out)
         dp_scr[turn, : base + TILE, :] = dot_t(va[: base + TILE, :], g_wide)
 
-    def gradients(tile):
-        base, turn = tile * TILE, tile % 2
+    def gradients(tile, at):
+        base, turn = tile * TILE, at % 2
         count = base + TILE
         e = e_own[own_rows(tile), :]
-        add_rows(dv, 0, base, dot(e, g_scr[turn]))
+        add_rows(dv, 0, dot(e, g_scr[turn]), known[0])
         score_gradients(ds_scr.at[turn, :count, :], e, dp_scr.at[turn, :count, :])
         ds = ds_scr[turn, :count, :]
-        add_rows(dk, 0, base, dot(ds, stacked(qg, base, group)))
+        add_rows(dk, 0, dot(ds, stacked(qg, base, group)), known[1])
         dq = dot(kt_early[:, base:], ds_early[early_rows(tile), :]) + dot(kt[:, :count], ds)
         dq = dq * logit_scale
         unstacked(dqs, base, group, dq.T.astype(BF16))
 
-    pipeline(tok // TILE, products, gradients)
+    pipeline([*range(1, tok // TILE), 0], products, gradients)
     dkv[:, :HEAD_DIM] = dk[...] * logit_scale
     dkv[:, HEAD_DIM:] = dv[...]
     take_rows(size, core, masks, lambda there: dqs[there, :], dq_pieces)
@@ -504,7 +519,6 @@
         jax.ShapeDtypeStruct((tok, cols // 2), BF16),
         jax.ShapeDtypeStruct((tiles, wide), F32),
         jax.ShapeDtypeStruct((early_rows(tiles - 1).stop, wide), BF16),
-        jax.ShapeDtypeStruct((HEAD_DIM, WINDOW), BF16),
     ]
     scratch = [
         pltpu.VMEM((WINDOW, 2 * HEAD_DIM), BF16),
@@ -533,19 +547,22 @@
     return results[:count], results[count : count + reach], results[count + reach :]
 
 
-def backward(qg, kv, carried, size):
+def backward(qg, kv, carried, lags, size):
     (tok, cols), count = qg.shape, len(chip_masks(size))
     rows = tok // count
     group = cols // (2 * HEAD_DIM)
     wide = group * TILE
     results = attend_call(
-        functools.partial(backward_body, size, core_mask(), chip_masks(size), tok, group),
+        functools.partial(
+            backward_body, size, core_mask(), chip_masks(size), len(lags), tok, group
+        ),
         [jax.ShapeDtypeStruct((rows, cols // 2), BF16)] * count
         + [jax.ShapeDtypeStruct((tok, 2 * HEAD_DIM), F32)],
         [
             pltpu.VMEM((tok, cols // 2), BF16),
             pltpu.VMEM((tok, 2 * HEAD_DIM), BF16),
             pltpu.VMEM((HEAD_DIM, tok), BF16),
+            pltpu.VMEM((HEAD_DIM, WINDOW), BF16),
             pltpu.VMEM((tok, HEAD_DIM), F32),
             pltpu.VMEM((tok, HEAD_DIM), F32),
             pltpu.VMEM((2, tok, wide), F32),
@@ -557,6 +574,7 @@
         qg,
         kv,
         *carried,
+        *lags,
     )
     return results[:count], results[count]
 
@@ -593,7 +611,7 @@
     out, sent, carried = forward(documents, qg, lags, partial, size)
     backs = [shifted(sent[lag - 1], -lag * size) for lag in range(1, reach + 1)]
     out = swap_chips(out, size)
-    grad_q, dkv = backward(qg, kv, [e_own, *carried], size)
+    grad_q, dkv = backward(qg, kv, [e_own, *carried], lags, size)
     both = after(*out, *grad_q)
     out, grad_q = both[: len(out)], both[len(out) :]
     grad_q = swap_chips(grad_q, size)

time: 60.5 us -> 60.7 us (level)
  transfers between devices with their start and end apart: 22 -> 22, of which waited for: 11 -> 11; matrix products, arithmetic and copies ran while one was open for 3% -> 3% of each run, Pallas kernels for 11% -> 10%
where the time goes in v20:
time: 60.7 us; the launch traced here: 60.5 us
  starting transfers between devices  26.6 us (44%)
  waiting for transfers between devices  18.1 us (30%)
  Pallas kernels  12.7 us (21%)
  local copies, waits for them, and re-layouts  1.22 us (2%)
  between operations  1.1 us (2%)
  other arithmetic  0.73 us (1%)
    ppermute x20, starting transfers between devices, swap(): lax.ppermute(value, BOTH, [(i, i ^ mask) for i in range(device_count())])  21.6 us
    ppermute x20, waiting for transfers between devices, swap(): lax.ppermute(value, BOTH, [(i, i ^ mask) for i in range(device_count())])  17.2 us
    pallas_call x3, Pallas kernels, attend_call(): pl.pallas_call(kernel, out_shape=out_shape, in_specs=[VMEM] * len(args),...  10.8 us
    ppermute x2, starting transfers between devices, shifted(): return lax.ppermute(value, BOTH, pairs)  4.99 us
    pallas_call x1, Pallas kernels, spread_cores(): pl.pallas_call(functools.partial(spread_body, size, core_mask(), chip_mas...  1.39 us
  transfers between devices with their start and end apart: 22, of which 11 were waited for; matrix products, arithmetic and copies ran while one was open for 3% of the time, Pallas kernels for 10%

profile of v20, /device:TPU:0, one launch (start us, length us, event | category | flops | bytes accessed | tf_op | source)
XLA Modules:
  0.0 60.5 jit_solution(9342773351159214894)
XLA Ops:
  0.7 0.5 collective-permute-start
  1.8 1.1 %fusion.2 = (bf16[128,256]{1,0:T(8,128)(2,1)S(1)}, bf16[128,256]{1,0:T(8,128)(2,1)S(1)}, bf16[128,256]{1,0:T(8,128)(2,1)S(1)}, bf16[128,256]{1,0:T(8,128)(2,1)S(...) fusion(bf16[128,1024]{1,0:T(8,128)(2,1)} %param.7, ...), kind=kLoop, calls=%fused_computation.11 | loop fusion | bytes 1048576 | tf_op jit(solution)/shard_map/slice | solution.py:94
  3.2 3.0 %collective-permute-start.7 = (bf16[256,256]{1,0:T(8,128)(2,1)S(1)}, bf16[256,256]{1,0:T(8,128)(2,1)S(1)}, u32[]{:S(2)}, u32[]{:S(2)}) collective-permute-start(bf16[256,256]{1,0:T(8,128)(2,1)S(1)} %get-tuple-element.58), channel_id=1, source_target_pairs={{0,1},{1,0},{2,3},{3,2},{4,5},{5,4},{6,7},{7,6},{8,9},{9,8},{10,11... | collective-permute-start | bytes 393224 | tf_op jit(solution)/shard_map/ppermute | solution.py:35
  6.2 1.5 %collective-permute-start.8 = (bf16[256,256]{1,0:T(8,128)(2,1)S(1)}, bf16[256,256]{1,0:T(8,128)(2,1)S(1)}, u32[]{:S(2)}, u32[]{:S(2)}) collective-permute-start(bf16[256,256]{1,0:T(8,128)(2,1)S(1)} %get-tuple-element.59), channel_id=1, source_target_pairs={{0,4},{1,5},{2,6},{3,7},{4,0},{5,1},{6,2},{7,3},{8,12},{9,13},{10,... | collective-permute-start | bytes 393224 | tf_op jit(solution)/shard_map/ppermute | solution.py:35
  8.2 2.0 %collective-permute-start.4 = (bf16[256,512]{1,0:T(8,128)(2,1)S(1)}, bf16[256,512]{1,0:T(8,128)(2,1)S(1)}, u32[]{:S(2)}, u32[]{:S(2)}) collective-permute-start(bf16[256,512]{1,0:T(8,128)(2,1)S(1)} %get-tuple-element.54), channel_id=1, source_target_pairs={{0,1},{1,0},{2,3},{3,2},{4,5},{5,4},{6,7},{7,6},{8,9},{9,8},{10,11... | collective-permute-start | bytes 786440 | tf_op jit(solution)/shard_map/ppermute | solution.py:35
  10.2 1.5 %collective-permute-start.5 = (bf16[256,512]{1,0:T(8,128)(2,1)S(1)}, bf16[256,512]{1,0:T(8,128)(2,1)S(1)}, u32[]{:S(2)}, u32[]{:S(2)}) collective-permute-start(bf16[256,512]{1,0:T(8,128)(2,1)S(1)} %get-tuple-element.55), channel_id=1, source_target_pairs={{0,4},{1,5},{2,6},{3,7},{4,0},{5,1},{6,2},{7,3},{8,12},{9,13},{10,... | collective-permute-start | bytes 786440 | tf_op jit(solution)/shard_map/ppermute | solution.py:35
  11.7 1.7 %collective-permute-start.6 = (bf16[256,512]{1,0:T(8,128)(2,1)S(1)}, bf16[256,512]{1,0:T(8,128)(2,1)S(1)}, u32[]{:S(2)}, u32[]{:S(2)}) collective-permute-start(bf16[256,512]{1,0:T(8,128)(2,1)S(1)} %get-tuple-element.56), channel_id=1, source_target_pairs={{0,5},{1,4},{2,7},{3,6},{4,1},{5,0},{6,3},{7,2},{8,13},{9,12},{10,... | collective-permute-start | bytes 786440 | tf_op jit(solution)/shard_map/ppermute | solution.py:35
  13.8 0.6 collective-permute-done.8.refs_2_
  14.4 0.7 %collective-permute-done.9.refs_3_ = bf16[256,256]{1,0:T(8,128)(2,1)S(1)} collective-permute-done((bf16[256,256]{1,0:T(8,128)(2,1)S(1)}, bf16[256,256]{1,0:T(8,128)(2,1)S(1)}, u32[]{:S(2)}, u32[]{:S(2)}) %collective-permute-start.9) | collective-permute-done | bytes 131104 | tf_op jit(solution)/shard_map/ppermute | solution.py:35
  15.1 3.5 %collective-permute-start.10 = (bf16[1024,256]{1,0:T(8,128)(2,1)S(1)}, bf16[1024,256]{1,0:T(8,128)(2,1)S(1)}, u32[]{:S(2)}, u32[]{:S(2)}) collective-permute-start(bf16[1024,256]{1,0:T(8,128)(2,1)S(1)} %join.1.refs_6_.refs_1_), channel_id=1, source_target_pairs={{0,8},{1,9},{2,10},{3,11},{4,12},{5,13},{6,14},{7,15},{8,16},{9,17... | collective-permute-start | bytes 1572872 | tf_op jit(solution)/shard_map/ppermute | solution.py:55
  18.8 0.8 %collective-permute-done.4.refs_3_ = bf16[256,512]{1,0:T(8,128)(2,1)S(1)} collective-permute-done((bf16[256,512]{1,0:T(8,128)(2,1)S(1)}, bf16[256,512]{1,0:T(8,128)(2,1)S(1)}, u32[]{:S(2)}, u32[]{:S(2)}) %collective-permute-start.4) | collective-permute-done | bytes 262176 | tf_op jit(solution)/shard_map/ppermute | solution.py:35
  19.7 5.7 %collective-permute-done.5.refs_4_ = bf16[256,512]{1,0:T(8,128)(2,1)S(1)} collective-permute-done((bf16[256,512]{1,0:T(8,128)(2,1)S(1)}, bf16[256,512]{1,0:T(8,128)(2,1)S(1)}, u32[]{:S(2)}, u32[]{:S(2)}) %collective-permute-start.5) | collective-permute-done | bytes 262176 | tf_op jit(solution)/shard_map/ppermute | solution.py:35
  25.4 2.3 %forward_own.1 = (bf16[4608,256]{1,0:T(8,128)(2,1)S(1)}, f32[128,2048]{1,0:T(8,128)S(1)}, f32[16,256]{1,0:T(8,128)S(1)}, bf16[1024,512]{1,0:T(8,128)(2,1)S(1)}) custom-call(bf16[2048,128]{1,0:T(8,128)(2,1)S(1)} %select_convert_fusion.refs_0_, bf16[1024,128]{1,0:T(8,128)(2,1)S(1)} %select_convert_fusion.1.refs_1_, ...), custom_call_target="tpu_custom_call" | custom-call | flops 4831838208 | bytes 8388608 | tf_op jit(solution)/shard_map/forward_own/pallas_call | solution.py:471
  27.8 5.0 %forward.1 = (bf16[256,256]{1,0:T(8,128)(2,1)S(1)}, bf16[256,256]{1,0:T(8,128)(2,1)S(1)}, bf16[256,256]{1,0:T(8,128)(2,1)S(1)}, bf16[256,256]{1,0:T(8,128)(2,1)S...) custom-call(bf16[2048,128]{1,0:T(8,128)(2,1)S(1)} %select_convert_fu, ...), custom_call_target="tpu_custom_call" | custom-call | flops 1811939328 | bytes 8388608 | tf_op jit(solution)/shard_map/forward/pallas_call | solution.py:471
  32.9 1.5 %collective-permute-start.17 = (bf16[1024,256]{1,0:T(8,128)(2,1)S(1)}, bf16[1024,256]{1,0:T(8,128)(2,1)S(1)}, u32[]{:S(2)}, u32[]{:S(2)}) collective-permute-start(bf16[1024,256]{1,0:T(8,128)(2,1)S(1)} %get-tuple-element.85), channel_id=1, source_target_pairs={{8,0},{9,1},{10,2},{11,3},{12,4},{13,5},{14,6},{15,7},{16,8},{17,9... | collective-permute-start | bytes 1572872 | tf_op jit(solution)/shard_map/ppermute | solution.py:55
  34.4 1.8 %collective-permute-start.11 = (bf16[256,256]{1,0:T(8,128)(2,1)S(1)}, bf16[256,256]{1,0:T(8,128)(2,1)S(1)}, u32[]{:S(2)}, u32[]{:S(2)}) collective-permute-start(bf16[256,256]{1,0:T(8,128)(2,1)S(1)} %get-tuple-element.65), channel_id=1, source_target_pairs={{0,1},{1,0},{2,3},{3,2},{4,5},{5,4},{6,7},{7,6},{8,9},{9,8},{10,11... | collective-permute-start | bytes 393224 | tf_op jit(solution)/shard_map/ppermute | solution.py:35
  36.1 0.5 collective-permute-start.12
  36.6 1.3 %collective-permute-start.13 = (bf16[256,256]{1,0:T(8,128)(2,1)S(1)}, bf16[256,256]{1,0:T(8,128)(2,1)S(1)}, u32[]{:S(2)}, u32[]{:S(2)}) collective-permute-start(bf16[256,256]{1,0:T(8,128)(2,1)S(1)} %get-tuple-element.67), channel_id=1, source_target_pairs={{0,5},{1,4},{2,7},{3,6},{4,1},{5,0},{6,3},{7,2},{8,13},{9,12},{10,... | collective-permute-start | bytes 393224 | tf_op jit(solution)/shard_map/ppermute | solution.py:35
  37.9 3.5 %backward.1 = (bf16[256,256]{1,0:T(8,128)(2,1)S(1)}, bf16[256,256]{1,0:T(8,128)(2,1)S(1)}, bf16[256,256]{1,0:T(8,128)(2,1)S(1)}, bf16[256,256]{1,0:T(8,128)(2,1)S(1)}, f32[1024,256]{1,0:T(8,128)S(1)}) custom-call(bf16[1024,512]{1,0:T(8,128)(2,1)S(1)} %get-tuple-element.61.refs_2_.refs_0_, bf16[1024,256]{1,0:T(8,128)(2,1)S(1)} %join.1.refs_6_.refs_1_, ...), custom_call_target="tpu_custom_call" | custom-call | flops 1207959552 | bytes 8388608 | tf_op jit(solution)/shard_map/backward/pallas_call | solution.py:471
  41.4 1.6 %collective-permute-done.12.refs_2_ = bf16[256,256]{1,0:T(8,128)(2,1)S(1)} collective-permute-done((bf16[256,256]{1,0:T(8,128)(2,1)S(1)}, bf16[256,256]{1,0:T(8,128)(2,1)S(1)}, u32[]{:S(2)}, u32[]{:S(2)}) %collective-permute-start.12) | collective-permute-done | bytes 131104 | tf_op jit(solution)/shard_map/ppermute | solution.py:35
  43.0 1.1 %collective-permute-start.14 = (bf16[256,256]{1,0:T(8,128)(2,1)S(1)}, bf16[256,256]{1,0:T(8,128)(2,1)S(1)}, u32[]{:S(2)}, u32[]{:S(2)}) collective-permute-start(bf16[256,256]{1,0:T(8,128)(2,1)S(1)} %get-tuple-element.81), channel_id=1, source_target_pairs={{0,1},{1,0},{2,3},{3,2},{4,5},{5,4},{6,7},{7,6},{8,9},{9,8},{10,11... | collective-permute-start | bytes 393224 | tf_op jit(solution)/shard_map/ppermute | solution.py:35
  44.1 0.6 %collective-permute-start.15 = (bf16[256,256]{1,0:T(8,128)(2,1)S(1)}, bf16[256,256]{1,0:T(8,128)(2,1)S(1)}, u32[]{:S(2)}, u32[]{:S(2)}) collective-permute-start(bf16[256,256]{1,0:T(8,128)(2,1)S(1)} %get-tuple-element.82), channel_id=1, source_target_pairs={{0,4},{1,5},{2,6},{3,7},{4,0},{5,1},{6,2},{7,3},{8,12},{9,13},{10,... | collective-permute-start | bytes 393224 | tf_op jit(solution)/shard_map/ppermute | solution.py:35
  44.7 1.8 %collective-permute-start.16 = (bf16[256,256]{1,0:T(8,128)(2,1)S(1)}, bf16[256,256]{1,0:T(8,128)(2,1)S(1)}, u32[]{:S(2)}, u32[]{:S(2)}) collective-permute-start(bf16[256,256]{1,0:T(8,128)(2,1)S(1)} %get-tuple-element.83), channel_id=1, source_target_pairs={{0,5},{1,4},{2,7},{3,6},{4,1},{5,0},{6,3},{7,2},{8,13},{9,12},{10,... | collective-permute-start | bytes 393224 | tf_op jit(solution)/shard_map/ppermute | solution.py:35
  46.5 0.9 %collective-permute-done.17.refs_1_ = bf16[1024,256]{1,0:T(8,128)(2,1)S(1)} collective-permute-done((bf16[1024,256]{1,0:T(8,128)(2,1)S(1)}, bf16[1024,256]{1,0:T(8,128)(2,1)S(1)}, u32[]{:S(2)}, u32[]{:S(2)}) %collective-permute-start.17) | collective-permute-done | bytes 524320 | tf_op jit(solution)/shard_map/ppermute | solution.py:55
  47.4 1.7 %collective-permute-start.18 = (bf16[256,256]{1,0:T(8,128)(2,1)S(1)}, bf16[256,256]{1,0:T(8,128)(2,1)S(1)}, u32[]{:S(2)}, u32[]{:S(2)}) collective-permute-start(bf16[256,256]{1,0:T(8,128)(2,1)S(1)} %get-tuple-element.87), channel_id=1, source_target_pairs={{0,1},{1,0},{2,3},{3,2},{4,5},{5,4},{6,7},{7,6},{8,9},{9,8},{10,11... | collective-permute-start | bytes 393224 | tf_op jit(solution)/shard_map/ppermute | solution.py:35
  49.2 0.6 collective-permute-start.19
  49.7 1.3 %collective-permute-start.20 = (bf16[256,256]{1,0:T(8,128)(2,1)S(1)}, bf16[256,256]{1,0:T(8,128)(2,1)S(1)}, u32[]{:S(2)}, u32[]{:S(2)}) collective-permute-start(bf16[256,256]{1,0:T(8,128)(2,1)S(1)} %get-tuple-element.89), channel_id=1, source_target_pairs={{0,5},{1,4},{2,7},{3,6},{4,1},{5,0},{6,3},{7,2},{8,13},{9,12},{10,... | collective-permute-start | bytes 393224 | tf_op jit(solution)/shard_map/ppermute | solution.py:35
  51.0 1.0 %collective-permute-done.16.refs_7_ = bf16[256,256]{1,0:T(8,128)(2,1)S(1)} collective-permute-done((bf16[256,256]{1,0:T(8,128)(2,1)S(1)}, bf16[256,256]{1,0:T(8,128)(2,1)S(1)}, u32[]{:S(2)}, u32[]{:S(2)}) %collective-permute-start.16) | collective-permute-done | bytes 131104 | tf_op jit(solution)/shard_map/ppermute | solution.py:35
  52.0 2.5 %collective-permute-done.18.refs_9_ = bf16[256,256]{1,0:T(8,128)(2,1)S(1)} collective-permute-done((bf16[256,256]{1,0:T(8,128)(2,1)S(1)}, bf16[256,256]{1,0:T(8,128)(2,1)S(1)}, u32[]{:S(2)}, u32[]{:S(2)}) %collective-permute-start.18) | collective-permute-done | bytes 131104 | tf_op jit(solution)/shard_map/ppermute | solution.py:35
  54.6 1.9 %collective-permute-done.19.refs_10_ = bf16[256,256]{1,0:T(8,128)(2,1)S(1)} collective-permute-done((bf16[256,256]{1,0:T(8,128)(2,1)S(1)}, bf16[256,256]{1,0:T(8,128)(2,1)S(1)}, u32[]{:S(2)}, u32[]{:S(2)}) %collective-permute-start.19) | collective-permute-done | bytes 131104 | tf_op jit(solution)/shard_map/ppermute | solution.py:35
  56.6 2.3 %collective-permute-done.21.refs_12_ = bf16[128,3072]{1,0:T(8,128)(2,1)S(1)} collective-permute-done((bf16[128,3072]{1,0:T(8,128)(2,1)S(1)}, bf16[128,3072]{1,0:T(8,128)(2,1)S(1)}, u32[]{:S(2)}, u32[]{:S(2)}) %collective-permute-start.21) | collective-permute-done | bytes 786464 | tf_op jit(solution)/shard_map/ppermute | solution.py:35
  58.9 1.4 %spread.1 = (bf16[128,2048]{1,0:T(8,128)(2,1)}, bf16[128,2048]{1,0:T(8,128)(2,1)}, bf16[128,1024]{1,0:T(8,128)(2,1)}, bf16[128,1024]{1,0:T(8,128)(2,1)}) custom-call(bf16[256,256]{1,0:T(8,128)(2,1)S(1)} %get-tuple-element.76.refs_0_, bf16[256,256]{1,0:T(8,128)(2,1)S(1)} %collective-permute-done.11.refs_1_, ...), custom_call_target="tpu_custom_call" | custom-call | tf_op jit(solution)/shard_map/spread/pallas_call | solution.py:201
  (39 shorter events, 2.2 us)
Async XLA Ops:
  0.6 7.1 %copy-start = (bf16[128,2048]{1,0:T(8,128)(2,1)S(1)}, bf16[128,2048]{1,0:T(8,128)(2,1)}, u32[]{:S(2)}) copy-start(bf16[128,2048]{1,0:T(8,128)(2,1)} %param.5) | copy-start | bytes 1572868
  0.6 7.2 %copy-start.1 = (bf16[128,2048]{1,0:T(8,128)(2,1)S(1)}, bf16[128,2048]{1,0:T(8,128)(2,1)}, u32[]{:S(2)}) copy-start(bf16[128,2048]{1,0:T(8,128)(2,1)} %param.8) | copy-start | bytes 1572868
  0.7 2.4 %collective-permute-start = (bf16[128,1024]{1,0:T(8,128)(2,1)}, bf16[128,1024]{1,0:T(8,128)(2,1)S(1)}, u32[]{:S(2)}, u32[]{:S(2)}) collective-permute-start(bf16[128,1024]{1,0:T(8,128)(2,1)} %param.6), channel_id=1, source_target_pairs={{0,2},{1,3},{2,0},{3,1},{4,6},{5,7},{6,4},{7,5},{8,10},{9,11},{10,... | collective-permute-start | bytes 786440 | tf_op jit(solution)/shard_map/ppermute | solution.py:35
  1.2 1.9 %collective-permute-start.1 = (bf16[128,1024]{1,0:T(8,128)(2,1)}, bf16[128,1024]{1,0:T(8,128)(2,1)S(1)}, u32[]{:S(2)}, u32[]{:S(2)}) collective-permute-start(bf16[128,1024]{1,0:T(8,128)(2,1)} %param.7), channel_id=1, source_target_pairs={{0,2},{1,3},{2,0},{3,1},{4,6},{5,7},{6,4},{7,5},{8,10},{9,11},{10,... | collective-permute-start | bytes 786440 | tf_op jit(solution)/shard_map/ppermute | solution.py:35
  1.2 6.7 %collective-permute-start.2 = (bf16[128,2048]{1,0:T(8,128)(2,1)}, bf16[128,2048]{1,0:T(8,128)(2,1)S(1)}, u32[]{:S(2)}, u32[]{:S(2)}) collective-permute-start(bf16[128,2048]{1,0:T(8,128)(2,1)} %param.5), channel_id=1, source_target_pairs={{0,2},{1,3},{2,0},{3,1},{4,6},{5,7},{6,4},{7,5},{8,10},{9,11},{10,... | collective-permute-start | bytes 1572872 | tf_op jit(solution)/shard_map/ppermute | solution.py:35
  1.7 6.3 %collective-permute-start.3 = (bf16[128,2048]{1,0:T(8,128)(2,1)}, bf16[128,2048]{1,0:T(8,128)(2,1)S(1)}, u32[]{:S(2)}, u32[]{:S(2)}) collective-permute-start(bf16[128,2048]{1,0:T(8,128)(2,1)} %param.8), channel_id=1, source_target_pairs={{0,2},{1,3},{2,0},{3,1},{4,6},{5,7},{6,4},{7,5},{8,10},{9,11},{10,... | collective-permute-start | bytes 1572872 | tf_op jit(solution)/shard_map/ppermute | solution.py:35
  2.9 5.0 %copy-start.2 = (s32[4096]{0:T(1024)S(1)}, s32[4096]{0:T(1024)}, u32[]{:S(2)}) copy-start(s32[4096]{0:T(1024)} %param.9) | copy-start | bytes 49156
  3.2 8.5 %collective-permute-start.7 = (bf16[256,256]{1,0:T(8,128)(2,1)S(1)}, bf16[256,256]{1,0:T(8,128)(2,1)S(1)}, u32[]{:S(2)}, u32[]{:S(2)}) collective-permute-start(bf16[256,256]{1,0:T(8,128)(2,1)S(1)} %get-tuple-element.58), channel_id=1, source_target_pairs={{0,1},{1,0},{2,3},{3,2},{4,5},{5,4},{6,7},{7,6},{8,9},{9,8},{10,11... | collective-permute-start | bytes 393224 | tf_op jit(solution)/shard_map/ppermute | solution.py:35
  6.2 8.2 %collective-permute-start.8 = (bf16[256,256]{1,0:T(8,128)(2,1)S(1)}, bf16[256,256]{1,0:T(8,128)(2,1)S(1)}, u32[]{:S(2)}, u32[]{:S(2)}) collective-permute-start(bf16[256,256]{1,0:T(8,128)(2,1)S(1)} %get-tuple-element.59), channel_id=1, source_target_pairs={{0,4},{1,5},{2,6},{3,7},{4,0},{5,1},{6,2},{7,3},{8,12},{9,13},{10,... | collective-permute-start | bytes 393224 | tf_op jit(solution)/shard_map/ppermute | solution.py:35
  7.7 7.4 %collective-permute-start.9 = (bf16[256,256]{1,0:T(8,128)(2,1)S(1)}, bf16[256,256]{1,0:T(8,128)(2,1)S(1)}, u32[]{:S(2)}, u32[]{:S(2)}) collective-permute-start(bf16[256,256]{1,0:T(8,128)(2,1)S(1)} %get-tuple-element.60), channel_id=1, source_target_pairs={{0,5},{1,4},{2,7},{3,6},{4,1},{5,0},{6,3},{7,2},{8,13},{9,12},{10,... | collective-permute-start | bytes 393224 | tf_op jit(solution)/shard_map/ppermute | solution.py:35
  7.8 10.8 %dynamic-slice-start = ((s32[4096]{0:T(1024)}, s32[]{:T(128)}), s32[1024]{0:T(1024)S(1)}, s32[]{:S(2)}) async-start(s32[4096]{0:T(1024)} %param.9, s32[]{:T(128)} %select_n.69), calls=%async_computation | async-start | bytes 8704 | tf_op jit(solution)/shard_map/dynamic_slice | solution.py:586
  8.2 11.5 %collective-permute-start.4 = (bf16[256,512]{1,0:T(8,128)(2,1)S(1)}, bf16[256,512]{1,0:T(8,128)(2,1)S(1)}, u32[]{:S(2)}, u32[]{:S(2)}) collective-permute-start(bf16[256,512]{1,0:T(8,128)(2,1)S(1)} %get-tuple-element.54), channel_id=1, source_target_pairs={{0,1},{1,0},{2,3},{3,2},{4,5},{5,4},{6,7},{7,6},{8,9},{9,8},{10,11... | collective-permute-start | bytes 786440 | tf_op jit(solution)/shard_map/ppermute | solution.py:35
  10.2 15.2 %collective-permute-start.5 = (bf16[256,512]{1,0:T(8,128)(2,1)S(1)}, bf16[256,512]{1,0:T(8,128)(2,1)S(1)}, u32[]{:S(2)}, u32[]{:S(2)}) collective-permute-start(bf16[256,512]{1,0:T(8,128)(2,1)S(1)} %get-tuple-element.55), channel_id=1, source_target_pairs={{0,4},{1,5},{2,6},{3,7},{4,0},{5,1},{6,2},{7,3},{8,12},{9,13},{10,... | collective-permute-start | bytes 786440 | tf_op jit(solution)/shard_map/ppermute | solution.py:35
  11.7 13.7 %collective-permute-start.6 = (bf16[256,512]{1,0:T(8,128)(2,1)S(1)}, bf16[256,512]{1,0:T(8,128)(2,1)S(1)}, u32[]{:S(2)}, u32[]{:S(2)}) collective-permute-start(bf16[256,512]{1,0:T(8,128)(2,1)S(1)} %get-tuple-element.56), channel_id=1, source_target_pairs={{0,5},{1,4},{2,7},{3,6},{4,1},{5,0},{6,3},{7,2},{8,13},{9,12},{10,... | collective-permute-start | bytes 786440 | tf_op jit(solution)/shard_map/ppermute | solution.py:35
  15.1 12.7 %collective-permute-start.10 = (bf16[1024,256]{1,0:T(8,128)(2,1)S(1)}, bf16[1024,256]{1,0:T(8,128)(2,1)S(1)}, u32[]{:S(2)}, u32[]{:S(2)}) collective-permute-start(bf16[1024,256]{1,0:T(8,128)(2,1)S(1)} %join.1.refs_6_.refs_1_), channel_id=1, source_target_pairs={{0,8},{1,9},{2,10},{3,11},{4,12},{5,13},{6,14},{7,15},{8,16},{9,17... | collective-permute-start | bytes 1572872 | tf_op jit(solution)/shard_map/ppermute | solution.py:55
  32.9 14.5 %collective-permute-start.17 = (bf16[1024,256]{1,0:T(8,128)(2,1)S(1)}, bf16[1024,256]{1,0:T(8,128)(2,1)S(1)}, u32[]{:S(2)}, u32[]{:S(2)}) collective-permute-start(bf16[1024,256]{1,0:T(8,128)(2,1)S(1)} %get-tuple-element.85), channel_id=1, source_target_pairs={{8,0},{9,1},{10,2},{11,3},{12,4},{13,5},{14,6},{15,7},{16,8},{17,9... | collective-permute-start | bytes 1572872 | tf_op jit(solution)/shard_map/ppermute | solution.py:55
  34.4 7.0 %collective-permute-start.11 = (bf16[256,256]{1,0:T(8,128)(2,1)S(1)}, bf16[256,256]{1,0:T(8,128)(2,1)S(1)}, u32[]{:S(2)}, u32[]{:S(2)}) collective-permute-start(bf16[256,256]{1,0:T(8,128)(2,1)S(1)} %get-tuple-element.65), channel_id=1, source_target_pairs={{0,1},{1,0},{2,3},{3,2},{4,5},{5,4},{6,7},{7,6},{8,9},{9,8},{10,11... | collective-permute-start | bytes 393224 | tf_op jit(solution)/shard_map/ppermute | solution.py:35
  36.1 6.9 %collective-permute-start.12 = (bf16[256,256]{1,0:T(8,128)(2,1)S(1)}, bf16[256,256]{1,0:T(8,128)(2,1)S(1)}, u32[]{:S(2)}, u32[]{:S(2)}) collective-permute-start(bf16[256,256]{1,0:T(8,128)(2,1)S(1)} %get-tuple-element.66), channel_id=1, source_target_pairs={{0,4},{1,5},{2,6},{3,7},{4,0},{5,1},{6,2},{7,3},{8,12},{9,13},{10,... | collective-permute-start | bytes 393224 | tf_op jit(solution)/shard_map/ppermute | solution.py:35
  36.6 6.4 %collective-permute-start.13 = (bf16[256,256]{1,0:T(8,128)(2,1)S(1)}, bf16[256,256]{1,0:T(8,128)(2,1)S(1)}, u32[]{:S(2)}, u32[]{:S(2)}) collective-permute-start(bf16[256,256]{1,0:T(8,128)(2,1)S(1)} %get-tuple-element.67), channel_id=1, source_target_pairs={{0,5},{1,4},{2,7},{3,6},{4,1},{5,0},{6,3},{7,2},{8,13},{9,12},{10,... | collective-permute-start | bytes 393224 | tf_op jit(solution)/shard_map/ppermute | solution.py:35
  43.0 6.7 %collective-permute-start.14 = (bf16[256,256]{1,0:T(8,128)(2,1)S(1)}, bf16[256,256]{1,0:T(8,128)(2,1)S(1)}, u32[]{:S(2)}, u32[]{:S(2)}) collective-permute-start(bf16[256,256]{1,0:T(8,128)(2,1)S(1)} %get-tuple-element.81), channel_id=1, source_target_pairs={{0,1},{1,0},{2,3},{3,2},{4,5},{5,4},{6,7},{7,6},{8,9},{9,8},{10,11... | collective-permute-start | bytes 393224 | tf_op jit(solution)/shard_map/ppermute | solution.py:35
  44.1 6.9 %collective-permute-start.15 = (bf16[256,256]{1,0:T(8,128)(2,1)S(1)}, bf16[256,256]{1,0:T(8,128)(2,1)S(1)}, u32[]{:S(2)}, u32[]{:S(2)}) collective-permute-start(bf16[256,256]{1,0:T(8,128)(2,1)S(1)} %get-tuple-element.82), channel_id=1, source_target_pairs={{0,4},{1,5},{2,6},{3,7},{4,0},{5,1},{6,2},{7,3},{8,12},{9,13},{10,... | collective-permute-start | bytes 393224 | tf_op jit(solution)/shard_map/ppermute | solution.py:35
  44.7 7.3 %collective-permute-start.16 = (bf16[256,256]{1,0:T(8,128)(2,1)S(1)}, bf16[256,256]{1,0:T(8,128)(2,1)S(1)}, u32[]{:S(2)}, u32[]{:S(2)}) collective-permute-start(bf16[256,256]{1,0:T(8,128)(2,1)S(1)} %get-tuple-element.83), channel_id=1, source_target_pairs={{0,5},{1,4},{2,7},{3,6},{4,1},{5,0},{6,3},{7,2},{8,13},{9,12},{10,... | collective-permute-start | bytes 393224 | tf_op jit(solution)/shard_map/ppermute | solution.py:35
  47.4 7.1 %collective-permute-start.18 = (bf16[256,256]{1,0:T(8,128)(2,1)S(1)}, bf16[256,256]{1,0:T(8,128)(2,1)S(1)}, u32[]{:S(2)}, u32[]{:S(2)}) collective-permute-start(bf16[256,256]{1,0:T(8,128)(2,1)S(1)} %get-tuple-element.87), channel_id=1, source_target_pairs={{0,1},{1,0},{2,3},{3,2},{4,5},{5,4},{6,7},{7,6},{8,9},{9,8},{10,11... | collective-permute-start | bytes 393224 | tf_op jit(solution)/shard_map/ppermute | solution.py:35
  49.2 7.3 %collective-permute-start.19 = (bf16[256,256]{1,0:T(8,128)(2,1)S(1)}, bf16[256,256]{1,0:T(8,128)(2,1)S(1)}, u32[]{:S(2)}, u32[]{:S(2)}) collective-permute-start(bf16[256,256]{1,0:T(8,128)(2,1)S(1)} %get-tuple-element.88), channel_id=1, source_target_pairs={{0,4},{1,5},{2,6},{3,7},{4,0},{5,1},{6,2},{7,3},{8,12},{9,13},{10,... | collective-permute-start | bytes 393224 | tf_op jit(solution)/shard_map/ppermute | solution.py:35
  49.7 6.7 %collective-permute-start.20 = (bf16[256,256]{1,0:T(8,128)(2,1)S(1)}, bf16[256,256]{1,0:T(8,128)(2,1)S(1)}, u32[]{:S(2)}, u32[]{:S(2)}) collective-permute-start(bf16[256,256]{1,0:T(8,128)(2,1)S(1)} %get-tuple-element.89), channel_id=1, source_target_pairs={{0,5},{1,4},{2,7},{3,6},{4,1},{5,0},{6,3},{7,2},{8,13},{9,12},{10,... | collective-permute-start | bytes 393224 | tf_op jit(solution)/shard_map/ppermute | solution.py:35
  56.5 2.4 %collective-permute-start.21 = (bf16[128,3072]{1,0:T(8,128)(2,1)S(1)}, bf16[128,3072]{1,0:T(8,128)(2,1)S(1)}, u32[]{:S(2)}, u32[]{:S(2)}) collective-permute-start(bf16[128,3072]{1,0:T(8,128)(2,1)S(1)} %bottom.1), channel_id=1, source_target_pairs={{0,2},{1,3},{2,0},{3,1},{4,6},{5,7},{6,4},{7,5},{8,10},{9,11},{10,... | collective-permute-start | bytes 2359304 | tf_op jit(solution)/shard_map/ppermute | solution.py:35

commit v21 on v20

--- a/solution.py
+++ b/solution.py
@@ -417,8 +417,7 @@
         score_gradients(ds, e, dp_scr.at[turn, :early, :])
         add_rows(dk, base, dot(ds[...], stacked(qg, base, group)), known[1])
 
-    order = [tiles - 1, *range(tiles - 1)]
-    pipeline(order, scores, weights, outputs, gradients)
+    pipeline(range(tiles), scores, weights, outputs, gradients)
 
     for lag in range(1, reach + 1):
         there = slice((reach - lag) * tok, (reach - lag + 1) * tok)

time: 60.7 us -> 60.4 us (level)
  no operation moved by 1% of the time
where the time goes in v21:
time: 60.4 us; the launch traced here: 60.2 us
  starting transfers between devices  26.6 us (44%)
  waiting for transfers between devices  18.1 us (30%)
  Pallas kernels  12.4 us (21%)
  local copies, waits for them, and re-layouts  1.22 us (2%)
  between operations  1.1 us (2%)
  other arithmetic  0.73 us (1%)
    ppermute x20, starting transfers between devices, swap(): lax.ppermute(value, BOTH, [(i, i ^ mask) for i in range(device_count())])  21.6 us
    ppermute x20, waiting for transfers between devices, swap(): lax.ppermute(value, BOTH, [(i, i ^ mask) for i in range(device_count())])  17.2 us
    pallas_call x3, Pallas kernels, attend_call(): pl.pallas_call(kernel, out_shape=out_shape, in_specs=[VMEM] * len(args),...  10.5 us
    ppermute x2, starting transfers between devices, shifted(): return lax.ppermute(value, BOTH, pairs)  4.99 us
    pallas_call x1, Pallas kernels, spread_cores(): pl.pallas_call(functools.partial(spread_body, size, core_mask(), chip_mas...  1.39 us
  transfers between devices with their start and end apart: 22, of which 11 were waited for; matrix products, arithmetic and copies ran while one was open for 3% of the time, Pallas kernels for 10%

profile of v21, /device:TPU:0, one launch (start us, length us, event | category | flops | bytes accessed | tf_op | source)
XLA Modules:
  0.0 60.2 jit_solution(14220284258517761268)
XLA Ops:
  0.7 0.5 collective-permute-start
  1.8 1.1 %fusion.2 = (bf16[128,256]{1,0:T(8,128)(2,1)S(1)}, bf16[128,256]{1,0:T(8,128)(2,1)S(1)}, bf16[128,256]{1,0:T(8,128)(2,1)S(1)}, bf16[128,256]{1,0:T(8,128)(2,1)S(...) fusion(bf16[128,1024]{1,0:T(8,128)(2,1)} %param.7, ...), kind=kLoop, calls=%fused_computation.11 | loop fusion | bytes 1048576 | tf_op jit(solution)/shard_map/slice | solution.py:94
  3.2 3.0 %collective-permute-start.7 = (bf16[256,256]{1,0:T(8,128)(2,1)S(1)}, bf16[256,256]{1,0:T(8,128)(2,1)S(1)}, u32[]{:S(2)}, u32[]{:S(2)}) collective-permute-start(bf16[256,256]{1,0:T(8,128)(2,1)S(1)} %get-tuple-element.58), channel_id=1, source_target_pairs={{0,1},{1,0},{2,3},{3,2},{4,5},{5,4},{6,7},{7,6},{8,9},{9,8},{10,11... | collective-permute-start | bytes 393224 | tf_op jit(solution)/shard_map/ppermute | solution.py:35
  6.2 1.5 %collective-permute-start.8 = (bf16[256,256]{1,0:T(8,128)(2,1)S(1)}, bf16[256,256]{1,0:T(8,128)(2,1)S(1)}, u32[]{:S(2)}, u32[]{:S(2)}) collective-permute-start(bf16[256,256]{1,0:T(8,128)(2,1)S(1)} %get-tuple-element.59), channel_id=1, source_target_pairs={{0,4},{1,5},{2,6},{3,7},{4,0},{5,1},{6,2},{7,3},{8,12},{9,13},{10,... | collective-permute-start | bytes 393224 | tf_op jit(solution)/shard_map/ppermute | solution.py:35
  8.2 2.0 %collective-permute-start.4 = (bf16[256,512]{1,0:T(8,128)(2,1)S(1)}, bf16[256,512]{1,0:T(8,128)(2,1)S(1)}, u32[]{:S(2)}, u32[]{:S(2)}) collective-permute-start(bf16[256,512]{1,0:T(8,128)(2,1)S(1)} %get-tuple-element.54), channel_id=1, source_target_pairs={{0,1},{1,0},{2,3},{3,2},{4,5},{5,4},{6,7},{7,6},{8,9},{9,8},{10,11... | collective-permute-start | bytes 786440 | tf_op jit(solution)/shard_map/ppermute | solution.py:35
  10.2 1.5 %collective-permute-start.5 = (bf16[256,512]{1,0:T(8,128)(2,1)S(1)}, bf16[256,512]{1,0:T(8,128)(2,1)S(1)}, u32[]{:S(2)}, u32[]{:S(2)}) collective-permute-start(bf16[256,512]{1,0:T(8,128)(2,1)S(1)} %get-tuple-element.55), channel_id=1, source_target_pairs={{0,4},{1,5},{2,6},{3,7},{4,0},{5,1},{6,2},{7,3},{8,12},{9,13},{10,... | collective-permute-start | bytes 786440 | tf_op jit(solution)/shard_map/ppermute | solution.py:35
  11.7 1.7 %collective-permute-start.6 = (bf16[256,512]{1,0:T(8,128)(2,1)S(1)}, bf16[256,512]{1,0:T(8,128)(2,1)S(1)}, u32[]{:S(2)}, u32[]{:S(2)}) collective-permute-start(bf16[256,512]{1,0:T(8,128)(2,1)S(1)} %get-tuple-element.56), channel_id=1, source_target_pairs={{0,5},{1,4},{2,7},{3,6},{4,1},{5,0},{6,3},{7,2},{8,13},{9,12},{10,... | collective-permute-start | bytes 786440 | tf_op jit(solution)/shard_map/ppermute | solution.py:35
  13.8 0.6 collective-permute-done.8.refs_2_
  14.4 0.7 %collective-permute-done.9.refs_3_ = bf16[256,256]{1,0:T(8,128)(2,1)S(1)} collective-permute-done((bf16[256,256]{1,0:T(8,128)(2,1)S(1)}, bf16[256,256]{1,0:T(8,128)(2,1)S(1)}, u32[]{:S(2)}, u32[]{:S(2)}) %collective-permute-start.9) | collective-permute-done | bytes 131104 | tf_op jit(solution)/shard_map/ppermute | solution.py:35
  15.1 3.5 %collective-permute-start.10 = (bf16[1024,256]{1,0:T(8,128)(2,1)S(1)}, bf16[1024,256]{1,0:T(8,128)(2,1)S(1)}, u32[]{:S(2)}, u32[]{:S(2)}) collective-permute-start(bf16[1024,256]{1,0:T(8,128)(2,1)S(1)} %join.1.refs_6_.refs_1_), channel_id=1, source_target_pairs={{0,8},{1,9},{2,10},{3,11},{4,12},{5,13},{6,14},{7,15},{8,16},{9,17... | collective-permute-start | bytes 1572872 | tf_op jit(solution)/shard_map/ppermute | solution.py:55
  18.8 0.8 %collective-permute-done.4.refs_3_ = bf16[256,512]{1,0:T(8,128)(2,1)S(1)} collective-permute-done((bf16[256,512]{1,0:T(8,128)(2,1)S(1)}, bf16[256,512]{1,0:T(8,128)(2,1)S(1)}, u32[]{:S(2)}, u32[]{:S(2)}) %collective-permute-start.4) | collective-permute-done | bytes 262176 | tf_op jit(solution)/shard_map/ppermute | solution.py:35
  19.7 5.7 %collective-permute-done.5.refs_4_ = bf16[256,512]{1,0:T(8,128)(2,1)S(1)} collective-permute-done((bf16[256,512]{1,0:T(8,128)(2,1)S(1)}, bf16[256,512]{1,0:T(8,128)(2,1)S(1)}, u32[]{:S(2)}, u32[]{:S(2)}) %collective-permute-start.5) | collective-permute-done | bytes 262176 | tf_op jit(solution)/shard_map/ppermute | solution.py:35
  25.4 2.3 %forward_own.1 = (bf16[4608,256]{1,0:T(8,128)(2,1)S(1)}, f32[128,2048]{1,0:T(8,128)S(1)}, f32[16,256]{1,0:T(8,128)S(1)}, bf16[1024,512]{1,0:T(8,128)(2,1)S(1)}) custom-call(bf16[2048,128]{1,0:T(8,128)(2,1)S(1)} %select_convert_fusion.refs_0_, bf16[1024,128]{1,0:T(8,128)(2,1)S(1)} %select_convert_fusion.1.refs_1_, ...), custom_call_target="tpu_custom_call" | custom-call | flops 4831838208 | bytes 8388608 | tf_op jit(solution)/shard_map/forward_own/pallas_call | solution.py:470
  27.8 4.8 %forward.1 = (bf16[256,256]{1,0:T(8,128)(2,1)S(1)}, bf16[256,256]{1,0:T(8,128)(2,1)S(1)}, bf16[256,256]{1,0:T(8,128)(2,1)S(1)}, bf16[256,256]{1,0:T(8,128)(2,1)S...) custom-call(bf16[2048,128]{1,0:T(8,128)(2,1)S(1)} %select_convert_fu, ...), custom_call_target="tpu_custom_call" | custom-call | flops 1811939328 | bytes 8388608 | tf_op jit(solution)/shard_map/forward/pallas_call | solution.py:470
  32.6 1.5 %collective-permute-start.17 = (bf16[1024,256]{1,0:T(8,128)(2,1)S(1)}, bf16[1024,256]{1,0:T(8,128)(2,1)S(1)}, u32[]{:S(2)}, u32[]{:S(2)}) collective-permute-start(bf16[1024,256]{1,0:T(8,128)(2,1)S(1)} %get-tuple-element.85), channel_id=1, source_target_pairs={{8,0},{9,1},{10,2},{11,3},{12,4},{13,5},{14,6},{15,7},{16,8},{17,9... | collective-permute-start | bytes 1572872 | tf_op jit(solution)/shard_map/ppermute | solution.py:55
  34.1 1.8 %collective-permute-start.11 = (bf16[256,256]{1,0:T(8,128)(2,1)S(1)}, bf16[256,256]{1,0:T(8,128)(2,1)S(1)}, u32[]{:S(2)}, u32[]{:S(2)}) collective-permute-start(bf16[256,256]{1,0:T(8,128)(2,1)S(1)} %get-tuple-element.65), channel_id=1, source_target_pairs={{0,1},{1,0},{2,3},{3,2},{4,5},{5,4},{6,7},{7,6},{8,9},{9,8},{10,11... | collective-permute-start | bytes 393224 | tf_op jit(solution)/shard_map/ppermute | solution.py:35
  35.9 0.5 collective-permute-start.12
  36.4 1.3 %collective-permute-start.13 = (bf16[256,256]{1,0:T(8,128)(2,1)S(1)}, bf16[256,256]{1,0:T(8,128)(2,1)S(1)}, u32[]{:S(2)}, u32[]{:S(2)}) collective-permute-start(bf16[256,256]{1,0:T(8,128)(2,1)S(1)} %get-tuple-element.67), channel_id=1, source_target_pairs={{0,5},{1,4},{2,7},{3,6},{4,1},{5,0},{6,3},{7,2},{8,13},{9,12},{10,... | collective-permute-start | bytes 393224 | tf_op jit(solution)/shard_map/ppermute | solution.py:35
  37.6 3.5 %backward.1 = (bf16[256,256]{1,0:T(8,128)(2,1)S(1)}, bf16[256,256]{1,0:T(8,128)(2,1)S(1)}, bf16[256,256]{1,0:T(8,128)(2,1)S(1)}, bf16[256,256]{1,0:T(8,128)(2,1)S(1)}, f32[1024,256]{1,0:T(8,128)S(1)}) custom-call(bf16[1024,512]{1,0:T(8,128)(2,1)S(1)} %get-tuple-element.61.refs_2_.refs_0_, bf16[1024,256]{1,0:T(8,128)(2,1)S(1)} %join.1.refs_6_.refs_1_, ...), custom_call_target="tpu_custom_call" | custom-call | flops 1207959552 | bytes 8388608 | tf_op jit(solution)/shard_map/backward/pallas_call | solution.py:470
  41.1 1.6 %collective-permute-done.12.refs_2_ = bf16[256,256]{1,0:T(8,128)(2,1)S(1)} collective-permute-done((bf16[256,256]{1,0:T(8,128)(2,1)S(1)}, bf16[256,256]{1,0:T(8,128)(2,1)S(1)}, u32[]{:S(2)}, u32[]{:S(2)}) %collective-permute-start.12) | collective-permute-done | bytes 131104 | tf_op jit(solution)/shard_map/ppermute | solution.py:35
  42.7 1.1 %collective-permute-start.14 = (bf16[256,256]{1,0:T(8,128)(2,1)S(1)}, bf16[256,256]{1,0:T(8,128)(2,1)S(1)}, u32[]{:S(2)}, u32[]{:S(2)}) collective-permute-start(bf16[256,256]{1,0:T(8,128)(2,1)S(1)} %get-tuple-element.81), channel_id=1, source_target_pairs={{0,1},{1,0},{2,3},{3,2},{4,5},{5,4},{6,7},{7,6},{8,9},{9,8},{10,11... | collective-permute-start | bytes 393224 | tf_op jit(solution)/shard_map/ppermute | solution.py:35
  43.8 0.6 %collective-permute-start.15 = (bf16[256,256]{1,0:T(8,128)(2,1)S(1)}, bf16[256,256]{1,0:T(8,128)(2,1)S(1)}, u32[]{:S(2)}, u32[]{:S(2)}) collective-permute-start(bf16[256,256]{1,0:T(8,128)(2,1)S(1)} %get-tuple-element.82), channel_id=1, source_target_pairs={{0,4},{1,5},{2,6},{3,7},{4,0},{5,1},{6,2},{7,3},{8,12},{9,13},{10,... | collective-permute-start | bytes 393224 | tf_op jit(solution)/shard_map/ppermute | solution.py:35
  44.5 1.8 %collective-permute-start.16 = (bf16[256,256]{1,0:T(8,128)(2,1)S(1)}, bf16[256,256]{1,0:T(8,128)(2,1)S(1)}, u32[]{:S(2)}, u32[]{:S(2)}) collective-permute-start(bf16[256,256]{1,0:T(8,128)(2,1)S(1)} %get-tuple-element.83), channel_id=1, source_target_pairs={{0,5},{1,4},{2,7},{3,6},{4,1},{5,0},{6,3},{7,2},{8,13},{9,12},{10,... | collective-permute-start | bytes 393224 | tf_op jit(solution)/shard_map/ppermute | solution.py:35
  46.2 0.9 %collective-permute-done.17.refs_1_ = bf16[1024,256]{1,0:T(8,128)(2,1)S(1)} collective-permute-done((bf16[1024,256]{1,0:T(8,128)(2,1)S(1)}, bf16[1024,256]{1,0:T(8,128)(2,1)S(1)}, u32[]{:S(2)}, u32[]{:S(2)}) %collective-permute-start.17) | collective-permute-done | bytes 524320 | tf_op jit(solution)/shard_map/ppermute | solution.py:55
  47.2 1.7 %collective-permute-start.18 = (bf16[256,256]{1,0:T(8,128)(2,1)S(1)}, bf16[256,256]{1,0:T(8,128)(2,1)S(1)}, u32[]{:S(2)}, u32[]{:S(2)}) collective-permute-start(bf16[256,256]{1,0:T(8,128)(2,1)S(1)} %get-tuple-element.87), channel_id=1, source_target_pairs={{0,1},{1,0},{2,3},{3,2},{4,5},{5,4},{6,7},{7,6},{8,9},{9,8},{10,11... | collective-permute-start | bytes 393224 | tf_op jit(solution)/shard_map/ppermute | solution.py:35
  48.9 0.6 collective-permute-start.19
  49.5 1.3 %collective-permute-start.20 = (bf16[256,256]{1,0:T(8,128)(2,1)S(1)}, bf16[256,256]{1,0:T(8,128)(2,1)S(1)}, u32[]{:S(2)}, u32[]{:S(2)}) collective-permute-start(bf16[256,256]{1,0:T(8,128)(2,1)S(1)} %get-tuple-element.89), channel_id=1, source_target_pairs={{0,5},{1,4},{2,7},{3,6},{4,1},{5,0},{6,3},{7,2},{8,13},{9,12},{10,... | collective-permute-start | bytes 393224 | tf_op jit(solution)/shard_map/ppermute | solution.py:35
  50.7 1.0 %collective-permute-done.16.refs_7_ = bf16[256,256]{1,0:T(8,128)(2,1)S(1)} collective-permute-done((bf16[256,256]{1,0:T(8,128)(2,1)S(1)}, bf16[256,256]{1,0:T(8,128)(2,1)S(1)}, u32[]{:S(2)}, u32[]{:S(2)}) %collective-permute-start.16) | collective-permute-done | bytes 131104 | tf_op jit(solution)/shard_map/ppermute | solution.py:35
  51.8 2.5 %collective-permute-done.18.refs_9_ = bf16[256,256]{1,0:T(8,128)(2,1)S(1)} collective-permute-done((bf16[256,256]{1,0:T(8,128)(2,1)S(1)}, bf16[256,256]{1,0:T(8,128)(2,1)S(1)}, u32[]{:S(2)}, u32[]{:S(2)}) %collective-permute-start.18) | collective-permute-done | bytes 131104 | tf_op jit(solution)/shard_map/ppermute | solution.py:35
  54.3 1.9 %collective-permute-done.19.refs_10_ = bf16[256,256]{1,0:T(8,128)(2,1)S(1)} collective-permute-done((bf16[256,256]{1,0:T(8,128)(2,1)S(1)}, bf16[256,256]{1,0:T(8,128)(2,1)S(1)}, u32[]{:S(2)}, u32[]{:S(2)}) %collective-permute-start.19) | collective-permute-done | bytes 131104 | tf_op jit(solution)/shard_map/ppermute | solution.py:35
  56.3 2.3 %collective-permute-done.21.refs_12_ = bf16[128,3072]{1,0:T(8,128)(2,1)S(1)} collective-permute-done((bf16[128,3072]{1,0:T(8,128)(2,1)S(1)}, bf16[128,3072]{1,0:T(8,128)(2,1)S(1)}, u32[]{:S(2)}, u32[]{:S(2)}) %collective-permute-start.21) | collective-permute-done | bytes 786464 | tf_op jit(solution)/shard_map/ppermute | solution.py:35
  58.6 1.4 %spread.1 = (bf16[128,2048]{1,0:T(8,128)(2,1)}, bf16[128,2048]{1,0:T(8,128)(2,1)}, bf16[128,1024]{1,0:T(8,128)(2,1)}, bf16[128,1024]{1,0:T(8,128)(2,1)}) custom-call(bf16[256,256]{1,0:T(8,128)(2,1)S(1)} %get-tuple-element.76.refs_0_, bf16[256,256]{1,0:T(8,128)(2,1)S(1)} %collective-permute-done.11.refs_1_, ...), custom_call_target="tpu_custom_call" | custom-call | tf_op jit(solution)/shard_map/spread/pallas_call | solution.py:201
  (39 shorter events, 2.2 us)
Async XLA Ops:
  0.6 7.1 %copy-start = (bf16[128,2048]{1,0:T(8,128)(2,1)S(1)}, bf16[128,2048]{1,0:T(8,128)(2,1)}, u32[]{:S(2)}) copy-start(bf16[128,2048]{1,0:T(8,128)(2,1)} %param.5) | copy-start | bytes 1572868
  0.6 7.2 %copy-start.1 = (bf16[128,2048]{1,0:T(8,128)(2,1)S(1)}, bf16[128,2048]{1,0:T(8,128)(2,1)}, u32[]{:S(2)}) copy-start(bf16[128,2048]{1,0:T(8,128)(2,1)} %param.8) | copy-start | bytes 1572868
  0.7 2.4 %collective-permute-start = (bf16[128,1024]{1,0:T(8,128)(2,1)}, bf16[128,1024]{1,0:T(8,128)(2,1)S(1)}, u32[]{:S(2)}, u32[]{:S(2)}) collective-permute-start(bf16[128,1024]{1,0:T(8,128)(2,1)} %param.6), channel_id=1, source_target_pairs={{0,2},{1,3},{2,0},{3,1},{4,6},{5,7},{6,4},{7,5},{8,10},{9,11},{10,... | collective-permute-start | bytes 786440 | tf_op jit(solution)/shard_map/ppermute | solution.py:35
  1.2 1.9 %collective-permute-start.1 = (bf16[128,1024]{1,0:T(8,128)(2,1)}, bf16[128,1024]{1,0:T(8,128)(2,1)S(1)}, u32[]{:S(2)}, u32[]{:S(2)}) collective-permute-start(bf16[128,1024]{1,0:T(8,128)(2,1)} %param.7), channel_id=1, source_target_pairs={{0,2},{1,3},{2,0},{3,1},{4,6},{5,7},{6,4},{7,5},{8,10},{9,11},{10,... | collective-permute-start | bytes 786440 | tf_op jit(solution)/shard_map/ppermute | solution.py:35
  1.2 6.7 %collective-permute-start.2 = (bf16[128,2048]{1,0:T(8,128)(2,1)}, bf16[128,2048]{1,0:T(8,128)(2,1)S(1)}, u32[]{:S(2)}, u32[]{:S(2)}) collective-permute-start(bf16[128,2048]{1,0:T(8,128)(2,1)} %param.5), channel_id=1, source_target_pairs={{0,2},{1,3},{2,0},{3,1},{4,6},{5,7},{6,4},{7,5},{8,10},{9,11},{10,... | collective-permute-start | bytes 1572872 | tf_op jit(solution)/shard_map/ppermute | solution.py:35
  1.7 6.3 %collective-permute-start.3 = (bf16[128,2048]{1,0:T(8,128)(2,1)}, bf16[128,2048]{1,0:T(8,128)(2,1)S(1)}, u32[]{:S(2)}, u32[]{:S(2)}) collective-permute-start(bf16[128,2048]{1,0:T(8,128)(2,1)} %param.8), channel_id=1, source_target_pairs={{0,2},{1,3},{2,0},{3,1},{4,6},{5,7},{6,4},{7,5},{8,10},{9,11},{10,... | collective-permute-start | bytes 1572872 | tf_op jit(solution)/shard_map/ppermute | solution.py:35
  2.9 5.0 %copy-start.2 = (s32[4096]{0:T(1024)S(1)}, s32[4096]{0:T(1024)}, u32[]{:S(2)}) copy-start(s32[4096]{0:T(1024)} %param.9) | copy-start | bytes 49156
  3.2 8.5 %collective-permute-start.7 = (bf16[256,256]{1,0:T(8,128)(2,1)S(1)}, bf16[256,256]{1,0:T(8,128)(2,1)S(1)}, u32[]{:S(2)}, u32[]{:S(2)}) collective-permute-start(bf16[256,256]{1,0:T(8,128)(2,1)S(1)} %get-tuple-element.58), channel_id=1, source_target_pairs={{0,1},{1,0},{2,3},{3,2},{4,5},{5,4},{6,7},{7,6},{8,9},{9,8},{10,11... | collective-permute-start | bytes 393224 | tf_op jit(solution)/shard_map/ppermute | solution.py:35
  6.2 8.2 %collective-permute-start.8 = (bf16[256,256]{1,0:T(8,128)(2,1)S(1)}, bf16[256,256]{1,0:T(8,128)(2,1)S(1)}, u32[]{:S(2)}, u32[]{:S(2)}) collective-permute-start(bf16[256,256]{1,0:T(8,128)(2,1)S(1)} %get-tuple-element.59), channel_id=1, source_target_pairs={{0,4},{1,5},{2,6},{3,7},{4,0},{5,1},{6,2},{7,3},{8,12},{9,13},{10,... | collective-permute-start | bytes 393224 | tf_op jit(solution)/shard_map/ppermute | solution.py:35
  7.7 7.4 %collective-permute-start.9 = (bf16[256,256]{1,0:T(8,128)(2,1)S(1)}, bf16[256,256]{1,0:T(8,128)(2,1)S(1)}, u32[]{:S(2)}, u32[]{:S(2)}) collective-permute-start(bf16[256,256]{1,0:T(8,128)(2,1)S(1)} %get-tuple-element.60), channel_id=1, source_target_pairs={{0,5},{1,4},{2,7},{3,6},{4,1},{5,0},{6,3},{7,2},{8,13},{9,12},{10,... | collective-permute-start | bytes 393224 | tf_op jit(solution)/shard_map/ppermute | solution.py:35
  7.8 10.8 %dynamic-slice-start = ((s32[4096]{0:T(1024)}, s32[]{:T(128)}), s32[1024]{0:T(1024)S(1)}, s32[]{:S(2)}) async-start(s32[4096]{0:T(1024)} %param.9, s32[]{:T(128)} %select_n.69), calls=%async_computation | async-start | bytes 8704 | tf_op jit(solution)/shard_map/dynamic_slice | solution.py:585
  8.2 11.5 %collective-permute-start.4 = (bf16[256,512]{1,0:T(8,128)(2,1)S(1)}, bf16[256,512]{1,0:T(8,128)(2,1)S(1)}, u32[]{:S(2)}, u32[]{:S(2)}) collective-permute-start(bf16[256,512]{1,0:T(8,128)(2,1)S(1)} %get-tuple-element.54), channel_id=1, source_target_pairs={{0,1},{1,0},{2,3},{3,2},{4,5},{5,4},{6,7},{7,6},{8,9},{9,8},{10,11... | collective-permute-start | bytes 786440 | tf_op jit(solution)/shard_map/ppermute | solution.py:35
  10.2 15.2 %collective-permute-start.5 = (bf16[256,512]{1,0:T(8,128)(2,1)S(1)}, bf16[256,512]{1,0:T(8,128)(2,1)S(1)}, u32[]{:S(2)}, u32[]{:S(2)}) collective-permute-start(bf16[256,512]{1,0:T(8,128)(2,1)S(1)} %get-tuple-element.55), channel_id=1, source_target_pairs={{0,4},{1,5},{2,6},{3,7},{4,0},{5,1},{6,2},{7,3},{8,12},{9,13},{10,... | collective-permute-start | bytes 786440 | tf_op jit(solution)/shard_map/ppermute | solution.py:35
  11.7 13.7 %collective-permute-start.6 = (bf16[256,512]{1,0:T(8,128)(2,1)S(1)}, bf16[256,512]{1,0:T(8,128)(2,1)S(1)}, u32[]{:S(2)}, u32[]{:S(2)}) collective-permute-start(bf16[256,512]{1,0:T(8,128)(2,1)S(1)} %get-tuple-element.56), channel_id=1, source_target_pairs={{0,5},{1,4},{2,7},{3,6},{4,1},{5,0},{6,3},{7,2},{8,13},{9,12},{10,... | collective-permute-start | bytes 786440 | tf_op jit(solution)/shard_map/ppermute | solution.py:35
  15.1 12.7 %collective-permute-start.10 = (bf16[1024,256]{1,0:T(8,128)(2,1)S(1)}, bf16[1024,256]{1,0:T(8,128)(2,1)S(1)}, u32[]{:S(2)}, u32[]{:S(2)}) collective-permute-start(bf16[1024,256]{1,0:T(8,128)(2,1)S(1)} %join.1.refs_6_.refs_1_), channel_id=1, source_target_pairs={{0,8},{1,9},{2,10},{3,11},{4,12},{5,13},{6,14},{7,15},{8,16},{9,17... | collective-permute-start | bytes 1572872 | tf_op jit(solution)/shard_map/ppermute | solution.py:55
  32.6 14.5 %collective-permute-start.17 = (bf16[1024,256]{1,0:T(8,128)(2,1)S(1)}, bf16[1024,256]{1,0:T(8,128)(2,1)S(1)}, u32[]{:S(2)}, u32[]{:S(2)}) collective-permute-start(bf16[1024,256]{1,0:T(8,128)(2,1)S(1)} %get-tuple-element.85), channel_id=1, source_target_pairs={{8,0},{9,1},{10,2},{11,3},{12,4},{13,5},{14,6},{15,7},{16,8},{17,9... | collective-permute-start | bytes 1572872 | tf_op jit(solution)/shard_map/ppermute | solution.py:55
  34.1 7.0 %collective-permute-start.11 = (bf16[256,256]{1,0:T(8,128)(2,1)S(1)}, bf16[256,256]{1,0:T(8,128)(2,1)S(1)}, u32[]{:S(2)}, u32[]{:S(2)}) collective-permute-start(bf16[256,256]{1,0:T(8,128)(2,1)S(1)} %get-tuple-element.65), channel_id=1, source_target_pairs={{0,1},{1,0},{2,3},{3,2},{4,5},{5,4},{6,7},{7,6},{8,9},{9,8},{10,11... | collective-permute-start | bytes 393224 | tf_op jit(solution)/shard_map/ppermute | solution.py:35
  35.9 6.9 %collective-permute-start.12 = (bf16[256,256]{1,0:T(8,128)(2,1)S(1)}, bf16[256,256]{1,0:T(8,128)(2,1)S(1)}, u32[]{:S(2)}, u32[]{:S(2)}) collective-permute-start(bf16[256,256]{1,0:T(8,128)(2,1)S(1)} %get-tuple-element.66), channel_id=1, source_target_pairs={{0,4},{1,5},{2,6},{3,7},{4,0},{5,1},{6,2},{7,3},{8,12},{9,13},{10,... | collective-permute-start | bytes 393224 | tf_op jit(solution)/shard_map/ppermute | solution.py:35
  36.4 6.4 %collective-permute-start.13 = (bf16[256,256]{1,0:T(8,128)(2,1)S(1)}, bf16[256,256]{1,0:T(8,128)(2,1)S(1)}, u32[]{:S(2)}, u32[]{:S(2)}) collective-permute-start(bf16[256,256]{1,0:T(8,128)(2,1)S(1)} %get-tuple-element.67), channel_id=1, source_target_pairs={{0,5},{1,4},{2,7},{3,6},{4,1},{5,0},{6,3},{7,2},{8,13},{9,12},{10,... | collective-permute-start | bytes 393224 | tf_op jit(solution)/shard_map/ppermute | solution.py:35
  42.7 6.7 %collective-permute-start.14 = (bf16[256,256]{1,0:T(8,128)(2,1)S(1)}, bf16[256,256]{1,0:T(8,128)(2,1)S(1)}, u32[]{:S(2)}, u32[]{:S(2)}) collective-permute-start(bf16[256,256]{1,0:T(8,128)(2,1)S(1)} %get-tuple-element.81), channel_id=1, source_target_pairs={{0,1},{1,0},{2,3},{3,2},{4,5},{5,4},{6,7},{7,6},{8,9},{9,8},{10,11... | collective-permute-start | bytes 393224 | tf_op jit(solution)/shard_map/ppermute | solution.py:35
  43.8 6.9 %collective-permute-start.15 = (bf16[256,256]{1,0:T(8,128)(2,1)S(1)}, bf16[256,256]{1,0:T(8,128)(2,1)S(1)}, u32[]{:S(2)}, u32[]{:S(2)}) collective-permute-start(bf16[256,256]{1,0:T(8,128)(2,1)S(1)} %get-tuple-element.82), channel_id=1, source_target_pairs={{0,4},{1,5},{2,6},{3,7},{4,0},{5,1},{6,2},{7,3},{8,12},{9,13},{10,... | collective-permute-start | bytes 393224 | tf_op jit(solution)/shard_map/ppermute | solution.py:35
  44.5 7.3 %collective-permute-start.16 = (bf16[256,256]{1,0:T(8,128)(2,1)S(1)}, bf16[256,256]{1,0:T(8,128)(2,1)S(1)}, u32[]{:S(2)}, u32[]{:S(2)}) collective-permute-start(bf16[256,256]{1,0:T(8,128)(2,1)S(1)} %get-tuple-element.83), channel_id=1, source_target_pairs={{0,5},{1,4},{2,7},{3,6},{4,1},{5,0},{6,3},{7,2},{8,13},{9,12},{10,... | collective-permute-start | bytes 393224 | tf_op jit(solution)/shard_map/ppermute | solution.py:35
  47.2 7.1 %collective-permute-start.18 = (bf16[256,256]{1,0:T(8,128)(2,1)S(1)}, bf16[256,256]{1,0:T(8,128)(2,1)S(1)}, u32[]{:S(2)}, u32[]{:S(2)}) collective-permute-start(bf16[256,256]{1,0:T(8,128)(2,1)S(1)} %get-tuple-element.87), channel_id=1, source_target_pairs={{0,1},{1,0},{2,3},{3,2},{4,5},{5,4},{6,7},{7,6},{8,9},{9,8},{10,11... | collective-permute-start | bytes 393224 | tf_op jit(solution)/shard_map/ppermute | solution.py:35
  48.9 7.3 %collective-permute-start.19 = (bf16[256,256]{1,0:T(8,128)(2,1)S(1)}, bf16[256,256]{1,0:T(8,128)(2,1)S(1)}, u32[]{:S(2)}, u32[]{:S(2)}) collective-permute-start(bf16[256,256]{1,0:T(8,128)(2,1)S(1)} %get-tuple-element.88), channel_id=1, source_target_pairs={{0,4},{1,5},{2,6},{3,7},{4,0},{5,1},{6,2},{7,3},{8,12},{9,13},{10,... | collective-permute-start | bytes 393224 | tf_op jit(solution)/shard_map/ppermute | solution.py:35
  49.5 6.7 %collective-permute-start.20 = (bf16[256,256]{1,0:T(8,128)(2,1)S(1)}, bf16[256,256]{1,0:T(8,128)(2,1)S(1)}, u32[]{:S(2)}, u32[]{:S(2)}) collective-permute-start(bf16[256,256]{1,0:T(8,128)(2,1)S(1)} %get-tuple-element.89), channel_id=1, source_target_pairs={{0,5},{1,4},{2,7},{3,6},{4,1},{5,0},{6,3},{7,2},{8,13},{9,12},{10,... | collective-permute-start | bytes 393224 | tf_op jit(solution)/shard_map/ppermute | solution.py:35
  56.2 2.4 %collective-permute-start.21 = (bf16[128,3072]{1,0:T(8,128)(2,1)S(1)}, bf16[128,3072]{1,0:T(8,128)(2,1)S(1)}, u32[]{:S(2)}, u32[]{:S(2)}) collective-permute-start(bf16[128,3072]{1,0:T(8,128)(2,1)S(1)} %bottom.1), channel_id=1, source_target_pairs={{0,2},{1,3},{2,0},{3,1},{4,6},{5,7},{6,4},{7,5},{8,10},{9,11},{10,... | collective-permute-start | bytes 2359304 | tf_op jit(solution)/shard_map/ppermute | solution.py:35

commit v22 on v18

--- a/solution.py
+++ b/solution.py
@@ -594,8 +594,8 @@
     backs = [shifted(sent[lag - 1], -lag * size) for lag in range(1, reach + 1)]
     out = swap_chips(out, size)
     grad_q, dkv = backward(qg, kv, [e_own, *carried], size)
-    both = after(*out, *grad_q)
-    out, grad_q = both[: len(out)], both[len(out) :]
+    both = after(*out[:-1], *grad_q)
+    out, grad_q = [*both[: len(out) - 1], out[-1]], both[len(out) - 1 :]
     grad_q = swap_chips(grad_q, size)
     grads = swap_chips(combine([dkv, *backs], size), size)
     return tuple(spread_cores([out, grad_q, grads], (1, 1, 2), size))

time: 60.5 us -> 60.5 us (level)
  no operation moved by 1% of the time
where the time goes in v22:
time: 60.5 us; the launch traced here: 60.3 us
  starting transfers between devices  26.6 us (44%)
  waiting for transfers between devices  17.9 us (30%)
  Pallas kernels  12.7 us (21%)
  local copies, waits for them, and re-layouts  1.22 us (2%)
  between operations  1.1 us (2%)
  other arithmetic  0.73 us (1%)
    ppermute x20, starting transfers between devices, swap(): lax.ppermute(value, BOTH, [(i, i ^ mask) for i in range(device_count())])  21.6 us
    ppermute x20, waiting for transfers between devices, swap(): lax.ppermute(value, BOTH, [(i, i ^ mask) for i in range(device_count())])  17 us
    pallas_call x3, Pallas kernels, attend_call(): pl.pallas_call(kernel, out_shape=out_shape, in_specs=[VMEM] * len(args),...  10.8 us
    ppermute x2, starting transfers between devices, shifted(): return lax.ppermute(value, BOTH, pairs)  4.99 us
    pallas_call x1, Pallas kernels, spread_cores(): pl.pallas_call(functools.partial(spread_body, size, core_mask(), chip_mas...  1.39 us
  transfers between devices with their start and end apart: 22, of which 11 were waited for; matrix products, arithmetic and copies ran while one was open for 3% of the time, Pallas kernels for 11%

profile of v22, /device:TPU:0, one launch (start us, length us, event | category | flops | bytes accessed | tf_op | source)
XLA Modules:
  0.0 60.3 jit_solution(13912522992208209631)
XLA Ops:
  0.7 0.5 collective-permute-start
  1.8 1.1 %fusion.2 = (bf16[128,256]{1,0:T(8,128)(2,1)S(1)}, bf16[128,256]{1,0:T(8,128)(2,1)S(1)}, bf16[128,256]{1,0:T(8,128)(2,1)S(1)}, bf16[128,256]{1,0:T(8,128)(2,1)S(...) fusion(bf16[128,1024]{1,0:T(8,128)(2,1)} %param.7, ...), kind=kLoop, calls=%fused_computation.11 | loop fusion | bytes 1048576 | tf_op jit(solution)/shard_map/slice | solution.py:94
  3.2 3.0 %collective-permute-start.7 = (bf16[256,256]{1,0:T(8,128)(2,1)S(1)}, bf16[256,256]{1,0:T(8,128)(2,1)S(1)}, u32[]{:S(2)}, u32[]{:S(2)}) collective-permute-start(bf16[256,256]{1,0:T(8,128)(2,1)S(1)} %get-tuple-element.58), channel_id=1, source_target_pairs={{0,1},{1,0},{2,3},{3,2},{4,5},{5,4},{6,7},{7,6},{8,9},{9,8},{10,11... | collective-permute-start | bytes 393224 | tf_op jit(solution)/shard_map/ppermute | solution.py:35
  6.2 1.5 %collective-permute-start.8 = (bf16[256,256]{1,0:T(8,128)(2,1)S(1)}, bf16[256,256]{1,0:T(8,128)(2,1)S(1)}, u32[]{:S(2)}, u32[]{:S(2)}) collective-permute-start(bf16[256,256]{1,0:T(8,128)(2,1)S(1)} %get-tuple-element.59), channel_id=1, source_target_pairs={{0,4},{1,5},{2,6},{3,7},{4,0},{5,1},{6,2},{7,3},{8,12},{9,13},{10,... | collective-permute-start | bytes 393224 | tf_op jit(solution)/shard_map/ppermute | solution.py:35
  8.2 2.0 %collective-permute-start.4 = (bf16[256,512]{1,0:T(8,128)(2,1)S(1)}, bf16[256,512]{1,0:T(8,128)(2,1)S(1)}, u32[]{:S(2)}, u32[]{:S(2)}) collective-permute-start(bf16[256,512]{1,0:T(8,128)(2,1)S(1)} %get-tuple-element.54), channel_id=1, source_target_pairs={{0,1},{1,0},{2,3},{3,2},{4,5},{5,4},{6,7},{7,6},{8,9},{9,8},{10,11... | collective-permute-start | bytes 786440 | tf_op jit(solution)/shard_map/ppermute | solution.py:35
  10.2 1.5 %collective-permute-start.5 = (bf16[256,512]{1,0:T(8,128)(2,1)S(1)}, bf16[256,512]{1,0:T(8,128)(2,1)S(1)}, u32[]{:S(2)}, u32[]{:S(2)}) collective-permute-start(bf16[256,512]{1,0:T(8,128)(2,1)S(1)} %get-tuple-element.55), channel_id=1, source_target_pairs={{0,4},{1,5},{2,6},{3,7},{4,0},{5,1},{6,2},{7,3},{8,12},{9,13},{10,... | collective-permute-start | bytes 786440 | tf_op jit(solution)/shard_map/ppermute | solution.py:35
  11.7 1.7 %collective-permute-start.6 = (bf16[256,512]{1,0:T(8,128)(2,1)S(1)}, bf16[256,512]{1,0:T(8,128)(2,1)S(1)}, u32[]{:S(2)}, u32[]{:S(2)}) collective-permute-start(bf16[256,512]{1,0:T(8,128)(2,1)S(1)} %get-tuple-element.56), channel_id=1, source_target_pairs={{0,5},{1,4},{2,7},{3,6},{4,1},{5,0},{6,3},{7,2},{8,13},{9,12},{10,... | collective-permute-start | bytes 786440 | tf_op jit(solution)/shard_map/ppermute | solution.py:35
  13.8 0.6 collective-permute-done.8.refs_2_
  14.4 0.7 %collective-permute-done.9.refs_3_ = bf16[256,256]{1,0:T(8,128)(2,1)S(1)} collective-permute-done((bf16[256,256]{1,0:T(8,128)(2,1)S(1)}, bf16[256,256]{1,0:T(8,128)(2,1)S(1)}, u32[]{:S(2)}, u32[]{:S(2)}) %collective-permute-start.9) | collective-permute-done | bytes 131104 | tf_op jit(solution)/shard_map/ppermute | solution.py:35
  15.1 3.5 %collective-permute-start.10 = (bf16[1024,256]{1,0:T(8,128)(2,1)S(1)}, bf16[1024,256]{1,0:T(8,128)(2,1)S(1)}, u32[]{:S(2)}, u32[]{:S(2)}) collective-permute-start(bf16[1024,256]{1,0:T(8,128)(2,1)S(1)} %join.1.refs_6_.refs_1_), channel_id=1, source_target_pairs={{0,8},{1,9},{2,10},{3,11},{4,12},{5,13},{6,14},{7,15},{8,16},{9,17... | collective-permute-start | bytes 1572872 | tf_op jit(solution)/shard_map/ppermute | solution.py:55
  18.8 0.8 %collective-permute-done.4.refs_3_ = bf16[256,512]{1,0:T(8,128)(2,1)S(1)} collective-permute-done((bf16[256,512]{1,0:T(8,128)(2,1)S(1)}, bf16[256,512]{1,0:T(8,128)(2,1)S(1)}, u32[]{:S(2)}, u32[]{:S(2)}) %collective-permute-start.4) | collective-permute-done | bytes 262176 | tf_op jit(solution)/shard_map/ppermute | solution.py:35
  19.7 5.7 %collective-permute-done.5.refs_4_ = bf16[256,512]{1,0:T(8,128)(2,1)S(1)} collective-permute-done((bf16[256,512]{1,0:T(8,128)(2,1)S(1)}, bf16[256,512]{1,0:T(8,128)(2,1)S(1)}, u32[]{:S(2)}, u32[]{:S(2)}) %collective-permute-start.5) | collective-permute-done | bytes 262176 | tf_op jit(solution)/shard_map/ppermute | solution.py:35
  25.4 2.4 %forward_own.1 = (bf16[4608,256]{1,0:T(8,128)(2,1)S(1)}, f32[128,2048]{1,0:T(8,128)S(1)}, f32[16,256]{1,0:T(8,128)S(1)}, bf16[1024,512]{1,0:T(8,128)(2,1)S(1)}) custom-call(bf16[2048,128]{1,0:T(8,128)(2,1)S(1)} %select_convert_fusion.refs_0_, bf16[1024,128]{1,0:T(8,128)(2,1)S(1)} %select_convert_fusion.1.refs_1_, ...), custom_call_target="tpu_custom_call" | custom-call | flops 4831838208 | bytes 8388608 | tf_op jit(solution)/shard_map/forward_own/pallas_call | solution.py:456
  27.8 4.8 %forward.1 = (bf16[256,256]{1,0:T(8,128)(2,1)S(1)}, bf16[256,256]{1,0:T(8,128)(2,1)S(1)}, bf16[256,256]{1,0:T(8,128)(2,1)S(1)}, bf16[256,256]{1,0:T(8,128)(2,1)S...) custom-call(bf16[2048,128]{1,0:T(8,128)(2,1)S(1)} %select_convert_fu, ...), custom_call_target="tpu_custom_call" | custom-call | flops 1811939328 | bytes 8388608 | tf_op jit(solution)/shard_map/forward/pallas_call | solution.py:456
  32.7 1.5 %collective-permute-start.17 = (bf16[1024,256]{1,0:T(8,128)(2,1)S(1)}, bf16[1024,256]{1,0:T(8,128)(2,1)S(1)}, u32[]{:S(2)}, u32[]{:S(2)}) collective-permute-start(bf16[1024,256]{1,0:T(8,128)(2,1)S(1)} %get-tuple-element.85), channel_id=1, source_target_pairs={{8,0},{9,1},{10,2},{11,3},{12,4},{13,5},{14,6},{15,7},{16,8},{17,9... | collective-permute-start | bytes 1572872 | tf_op jit(solution)/shard_map/ppermute | solution.py:55
  34.1 1.8 %collective-permute-start.11 = (bf16[256,256]{1,0:T(8,128)(2,1)S(1)}, bf16[256,256]{1,0:T(8,128)(2,1)S(1)}, u32[]{:S(2)}, u32[]{:S(2)}) collective-permute-start(bf16[256,256]{1,0:T(8,128)(2,1)S(1)} %get-tuple-element.65), channel_id=1, source_target_pairs={{0,1},{1,0},{2,3},{3,2},{4,5},{5,4},{6,7},{7,6},{8,9},{9,8},{10,11... | collective-permute-start | bytes 393224 | tf_op jit(solution)/shard_map/ppermute | solution.py:35
  35.9 0.5 collective-permute-start.12
  36.4 1.3 %collective-permute-start.13 = (bf16[256,256]{1,0:T(8,128)(2,1)S(1)}, bf16[256,256]{1,0:T(8,128)(2,1)S(1)}, u32[]{:S(2)}, u32[]{:S(2)}) collective-permute-start(bf16[256,256]{1,0:T(8,128)(2,1)S(1)} %get-tuple-element.79), channel_id=1, source_target_pairs={{0,5},{1,4},{2,7},{3,6},{4,1},{5,0},{6,3},{7,2},{8,13},{9,12},{10,... | collective-permute-start | bytes 393224 | tf_op jit(solution)/shard_map/ppermute | solution.py:35
  37.7 3.6 %backward.1 = (bf16[256,256]{1,0:T(8,128)(2,1)S(1)}, bf16[256,256]{1,0:T(8,128)(2,1)S(1)}, bf16[256,256]{1,0:T(8,128)(2,1)S(1)}, bf16[256,256]{1,0:T(8,128)(2,1)S(1)}, f32[1024,256]{1,0:T(8,128)S(1)}) custom-call(bf16[1024,512]{1,0:T(8,128)(2,1)S(1)} %get-tuple-element.61.refs_2_.refs_0_, bf16[1024,256]{1,0:T(8,128)(2,1)S(1)} %join.1.refs_6_.refs_1_, ...), custom_call_target="tpu_custom_call" | custom-call | flops 1207959552 | bytes 8388608 | tf_op jit(solution)/shard_map/backward/pallas_call | solution.py:456
  41.3 1.5 %collective-permute-done.12.refs_2_ = bf16[256,256]{1,0:T(8,128)(2,1)S(1)} collective-permute-done((bf16[256,256]{1,0:T(8,128)(2,1)S(1)}, bf16[256,256]{1,0:T(8,128)(2,1)S(1)}, u32[]{:S(2)}, u32[]{:S(2)}) %collective-permute-start.12) | collective-permute-done | bytes 131104 | tf_op jit(solution)/shard_map/ppermute | solution.py:35
  42.8 1.2 %collective-permute-start.14 = (bf16[256,256]{1,0:T(8,128)(2,1)S(1)}, bf16[256,256]{1,0:T(8,128)(2,1)S(1)}, u32[]{:S(2)}, u32[]{:S(2)}) collective-permute-start(bf16[256,256]{1,0:T(8,128)(2,1)S(1)} %get-tuple-element.81), channel_id=1, source_target_pairs={{0,1},{1,0},{2,3},{3,2},{4,5},{5,4},{6,7},{7,6},{8,9},{9,8},{10,11... | collective-permute-start | bytes 393224 | tf_op jit(solution)/shard_map/ppermute | solution.py:35
  44.0 0.6 collective-permute-start.15
  44.5 1.8 %collective-permute-start.16 = (bf16[256,256]{1,0:T(8,128)(2,1)S(1)}, bf16[256,256]{1,0:T(8,128)(2,1)S(1)}, u32[]{:S(2)}, u32[]{:S(2)}) collective-permute-start(bf16[256,256]{1,0:T(8,128)(2,1)S(1)} %get-tuple-element.83), channel_id=1, source_target_pairs={{0,5},{1,4},{2,7},{3,6},{4,1},{5,0},{6,3},{7,2},{8,13},{9,12},{10,... | collective-permute-start | bytes 393224 | tf_op jit(solution)/shard_map/ppermute | solution.py:35
  46.3 0.9 %collective-permute-done.17.refs_1_ = bf16[1024,256]{1,0:T(8,128)(2,1)S(1)} collective-permute-done((bf16[1024,256]{1,0:T(8,128)(2,1)S(1)}, bf16[1024,256]{1,0:T(8,128)(2,1)S(1)}, u32[]{:S(2)}, u32[]{:S(2)}) %collective-permute-start.17) | collective-permute-done | bytes 524320 | tf_op jit(solution)/shard_map/ppermute | solution.py:55
  47.3 1.7 %collective-permute-start.18 = (bf16[256,256]{1,0:T(8,128)(2,1)S(1)}, bf16[256,256]{1,0:T(8,128)(2,1)S(1)}, u32[]{:S(2)}, u32[]{:S(2)}) collective-permute-start(bf16[256,256]{1,0:T(8,128)(2,1)S(1)} %get-tuple-element.87), channel_id=1, source_target_pairs={{0,1},{1,0},{2,3},{3,2},{4,5},{5,4},{6,7},{7,6},{8,9},{9,8},{10,11... | collective-permute-start | bytes 393224 | tf_op jit(solution)/shard_map/ppermute | solution.py:35
  49.0 0.6 collective-permute-start.19
  49.6 1.3 %collective-permute-start.20 = (bf16[256,256]{1,0:T(8,128)(2,1)S(1)}, bf16[256,256]{1,0:T(8,128)(2,1)S(1)}, u32[]{:S(2)}, u32[]{:S(2)}) collective-permute-start(bf16[256,256]{1,0:T(8,128)(2,1)S(1)} %get-tuple-element.89), channel_id=1, source_target_pairs={{0,5},{1,4},{2,7},{3,6},{4,1},{5,0},{6,3},{7,2},{8,13},{9,12},{10,... | collective-permute-start | bytes 393224 | tf_op jit(solution)/shard_map/ppermute | solution.py:35
  50.8 1.0 %collective-permute-done.16.refs_7_ = bf16[256,256]{1,0:T(8,128)(2,1)S(1)} collective-permute-done((bf16[256,256]{1,0:T(8,128)(2,1)S(1)}, bf16[256,256]{1,0:T(8,128)(2,1)S(1)}, u32[]{:S(2)}, u32[]{:S(2)}) %collective-permute-start.16) | collective-permute-done | bytes 131104 | tf_op jit(solution)/shard_map/ppermute | solution.py:35
  51.8 1.6 %collective-permute-done.18.refs_9_ = bf16[256,256]{1,0:T(8,128)(2,1)S(1)} collective-permute-done((bf16[256,256]{1,0:T(8,128)(2,1)S(1)}, bf16[256,256]{1,0:T(8,128)(2,1)S(1)}, u32[]{:S(2)}, u32[]{:S(2)}) %collective-permute-start.18) | collective-permute-done | bytes 131104 | tf_op jit(solution)/shard_map/ppermute | solution.py:35
  53.4 2.8 %collective-permute-done.19.refs_10_ = bf16[256,256]{1,0:T(8,128)(2,1)S(1)} collective-permute-done((bf16[256,256]{1,0:T(8,128)(2,1)S(1)}, bf16[256,256]{1,0:T(8,128)(2,1)S(1)}, u32[]{:S(2)}, u32[]{:S(2)}) %collective-permute-start.19) | collective-permute-done | bytes 131104 | tf_op jit(solution)/shard_map/ppermute | solution.py:35
  56.4 2.3 %collective-permute-done.21.refs_12_ = bf16[128,3072]{1,0:T(8,128)(2,1)S(1)} collective-permute-done((bf16[128,3072]{1,0:T(8,128)(2,1)S(1)}, bf16[128,3072]{1,0:T(8,128)(2,1)S(1)}, u32[]{:S(2)}, u32[]{:S(2)}) %collective-permute-start.21) | collective-permute-done | bytes 786464 | tf_op jit(solution)/shard_map/ppermute | solution.py:35
  58.7 1.4 %spread.1 = (bf16[128,2048]{1,0:T(8,128)(2,1)}, bf16[128,2048]{1,0:T(8,128)(2,1)}, bf16[128,1024]{1,0:T(8,128)(2,1)}, bf16[128,1024]{1,0:T(8,128)(2,1)}) custom-call(bf16[256,256]{1,0:T(8,128)(2,1)S(1)} %get-tuple-element.76.refs_0_, bf16[256,256]{1,0:T(8,128)(2,1)S(1)} %collective-permute-done.11.refs_1_, ...), custom_call_target="tpu_custom_call" | custom-call | tf_op jit(solution)/shard_map/spread/pallas_call | solution.py:201
  (39 shorter events, 2.1 us)
Async XLA Ops:
  0.6 7.1 %copy-start = (bf16[128,2048]{1,0:T(8,128)(2,1)S(1)}, bf16[128,2048]{1,0:T(8,128)(2,1)}, u32[]{:S(2)}) copy-start(bf16[128,2048]{1,0:T(8,128)(2,1)} %param.5) | copy-start | bytes 1572868
  0.6 7.2 %copy-start.1 = (bf16[128,2048]{1,0:T(8,128)(2,1)S(1)}, bf16[128,2048]{1,0:T(8,128)(2,1)}, u32[]{:S(2)}) copy-start(bf16[128,2048]{1,0:T(8,128)(2,1)} %param.8) | copy-start | bytes 1572868
  0.7 2.4 %collective-permute-start = (bf16[128,1024]{1,0:T(8,128)(2,1)}, bf16[128,1024]{1,0:T(8,128)(2,1)S(1)}, u32[]{:S(2)}, u32[]{:S(2)}) collective-permute-start(bf16[128,1024]{1,0:T(8,128)(2,1)} %param.6), channel_id=1, source_target_pairs={{0,2},{1,3},{2,0},{3,1},{4,6},{5,7},{6,4},{7,5},{8,10},{9,11},{10,... | collective-permute-start | bytes 786440 | tf_op jit(solution)/shard_map/ppermute | solution.py:35
  1.2 1.9 %collective-permute-start.1 = (bf16[128,1024]{1,0:T(8,128)(2,1)}, bf16[128,1024]{1,0:T(8,128)(2,1)S(1)}, u32[]{:S(2)}, u32[]{:S(2)}) collective-permute-start(bf16[128,1024]{1,0:T(8,128)(2,1)} %param.7), channel_id=1, source_target_pairs={{0,2},{1,3},{2,0},{3,1},{4,6},{5,7},{6,4},{7,5},{8,10},{9,11},{10,... | collective-permute-start | bytes 786440 | tf_op jit(solution)/shard_map/ppermute | solution.py:35
  1.2 6.7 %collective-permute-start.2 = (bf16[128,2048]{1,0:T(8,128)(2,1)}, bf16[128,2048]{1,0:T(8,128)(2,1)S(1)}, u32[]{:S(2)}, u32[]{:S(2)}) collective-permute-start(bf16[128,2048]{1,0:T(8,128)(2,1)} %param.5), channel_id=1, source_target_pairs={{0,2},{1,3},{2,0},{3,1},{4,6},{5,7},{6,4},{7,5},{8,10},{9,11},{10,... | collective-permute-start | bytes 1572872 | tf_op jit(solution)/shard_map/ppermute | solution.py:35
  1.7 6.3 %collective-permute-start.3 = (bf16[128,2048]{1,0:T(8,128)(2,1)}, bf16[128,2048]{1,0:T(8,128)(2,1)S(1)}, u32[]{:S(2)}, u32[]{:S(2)}) collective-permute-start(bf16[128,2048]{1,0:T(8,128)(2,1)} %param.8), channel_id=1, source_target_pairs={{0,2},{1,3},{2,0},{3,1},{4,6},{5,7},{6,4},{7,5},{8,10},{9,11},{10,... | collective-permute-start | bytes 1572872 | tf_op jit(solution)/shard_map/ppermute | solution.py:35
  2.9 5.0 %copy-start.2 = (s32[4096]{0:T(1024)S(1)}, s32[4096]{0:T(1024)}, u32[]{:S(2)}) copy-start(s32[4096]{0:T(1024)} %param.9) | copy-start | bytes 49156
  3.2 8.5 %collective-permute-start.7 = (bf16[256,256]{1,0:T(8,128)(2,1)S(1)}, bf16[256,256]{1,0:T(8,128)(2,1)S(1)}, u32[]{:S(2)}, u32[]{:S(2)}) collective-permute-start(bf16[256,256]{1,0:T(8,128)(2,1)S(1)} %get-tuple-element.58), channel_id=1, source_target_pairs={{0,1},{1,0},{2,3},{3,2},{4,5},{5,4},{6,7},{7,6},{8,9},{9,8},{10,11... | collective-permute-start | bytes 393224 | tf_op jit(solution)/shard_map/ppermute | solution.py:35
  6.2 8.2 %collective-permute-start.8 = (bf16[256,256]{1,0:T(8,128)(2,1)S(1)}, bf16[256,256]{1,0:T(8,128)(2,1)S(1)}, u32[]{:S(2)}, u32[]{:S(2)}) collective-permute-start(bf16[256,256]{1,0:T(8,128)(2,1)S(1)} %get-tuple-element.59), channel_id=1, source_target_pairs={{0,4},{1,5},{2,6},{3,7},{4,0},{5,1},{6,2},{7,3},{8,12},{9,13},{10,... | collective-permute-start | bytes 393224 | tf_op jit(solution)/shard_map/ppermute | solution.py:35
  7.7 7.4 %collective-permute-start.9 = (bf16[256,256]{1,0:T(8,128)(2,1)S(1)}, bf16[256,256]{1,0:T(8,128)(2,1)S(1)}, u32[]{:S(2)}, u32[]{:S(2)}) collective-permute-start(bf16[256,256]{1,0:T(8,128)(2,1)S(1)} %get-tuple-element.60), channel_id=1, source_target_pairs={{0,5},{1,4},{2,7},{3,6},{4,1},{5,0},{6,3},{7,2},{8,13},{9,12},{10,... | collective-permute-start | bytes 393224 | tf_op jit(solution)/shard_map/ppermute | solution.py:35
  7.8 10.8 %dynamic-slice-start = ((s32[4096]{0:T(1024)}, s32[]{:T(128)}), s32[1024]{0:T(1024)S(1)}, s32[]{:S(2)}) async-start(s32[4096]{0:T(1024)} %param.9, s32[]{:T(128)} %select_n.69), calls=%async_computation | async-start | bytes 8704 | tf_op jit(solution)/shard_map/dynamic_slice | solution.py:568
  8.2 11.5 %collective-permute-start.4 = (bf16[256,512]{1,0:T(8,128)(2,1)S(1)}, bf16[256,512]{1,0:T(8,128)(2,1)S(1)}, u32[]{:S(2)}, u32[]{:S(2)}) collective-permute-start(bf16[256,512]{1,0:T(8,128)(2,1)S(1)} %get-tuple-element.54), channel_id=1, source_target_pairs={{0,1},{1,0},{2,3},{3,2},{4,5},{5,4},{6,7},{7,6},{8,9},{9,8},{10,11... | collective-permute-start | bytes 786440 | tf_op jit(solution)/shard_map/ppermute | solution.py:35
  10.2 15.2 %collective-permute-start.5 = (bf16[256,512]{1,0:T(8,128)(2,1)S(1)}, bf16[256,512]{1,0:T(8,128)(2,1)S(1)}, u32[]{:S(2)}, u32[]{:S(2)}) collective-permute-start(bf16[256,512]{1,0:T(8,128)(2,1)S(1)} %get-tuple-element.55), channel_id=1, source_target_pairs={{0,4},{1,5},{2,6},{3,7},{4,0},{5,1},{6,2},{7,3},{8,12},{9,13},{10,... | collective-permute-start | bytes 786440 | tf_op jit(solution)/shard_map/ppermute | solution.py:35
  11.7 13.7 %collective-permute-start.6 = (bf16[256,512]{1,0:T(8,128)(2,1)S(1)}, bf16[256,512]{1,0:T(8,128)(2,1)S(1)}, u32[]{:S(2)}, u32[]{:S(2)}) collective-permute-start(bf16[256,512]{1,0:T(8,128)(2,1)S(1)} %get-tuple-element.56), channel_id=1, source_target_pairs={{0,5},{1,4},{2,7},{3,6},{4,1},{5,0},{6,3},{7,2},{8,13},{9,12},{10,... | collective-permute-start | bytes 786440 | tf_op jit(solution)/shard_map/ppermute | solution.py:35
  15.1 12.7 %collective-permute-start.10 = (bf16[1024,256]{1,0:T(8,128)(2,1)S(1)}, bf16[1024,256]{1,0:T(8,128)(2,1)S(1)}, u32[]{:S(2)}, u32[]{:S(2)}) collective-permute-start(bf16[1024,256]{1,0:T(8,128)(2,1)S(1)} %join.1.refs_6_.refs_1_), channel_id=1, source_target_pairs={{0,8},{1,9},{2,10},{3,11},{4,12},{5,13},{6,14},{7,15},{8,16},{9,17... | collective-permute-start | bytes 1572872 | tf_op jit(solution)/shard_map/ppermute | solution.py:55
  32.7 14.5 %collective-permute-start.17 = (bf16[1024,256]{1,0:T(8,128)(2,1)S(1)}, bf16[1024,256]{1,0:T(8,128)(2,1)S(1)}, u32[]{:S(2)}, u32[]{:S(2)}) collective-permute-start(bf16[1024,256]{1,0:T(8,128)(2,1)S(1)} %get-tuple-element.85), channel_id=1, source_target_pairs={{8,0},{9,1},{10,2},{11,3},{12,4},{13,5},{14,6},{15,7},{16,8},{17,9... | collective-permute-start | bytes 1572872 | tf_op jit(solution)/shard_map/ppermute | solution.py:55
  34.1 7.2 %collective-permute-start.11 = (bf16[256,256]{1,0:T(8,128)(2,1)S(1)}, bf16[256,256]{1,0:T(8,128)(2,1)S(1)}, u32[]{:S(2)}, u32[]{:S(2)}) collective-permute-start(bf16[256,256]{1,0:T(8,128)(2,1)S(1)} %get-tuple-element.65), channel_id=1, source_target_pairs={{0,1},{1,0},{2,3},{3,2},{4,5},{5,4},{6,7},{7,6},{8,9},{9,8},{10,11... | collective-permute-start | bytes 393224 | tf_op jit(solution)/shard_map/ppermute | solution.py:35
  35.9 6.9 %collective-permute-start.12 = (bf16[256,256]{1,0:T(8,128)(2,1)S(1)}, bf16[256,256]{1,0:T(8,128)(2,1)S(1)}, u32[]{:S(2)}, u32[]{:S(2)}) collective-permute-start(bf16[256,256]{1,0:T(8,128)(2,1)S(1)} %get-tuple-element.66), channel_id=1, source_target_pairs={{0,4},{1,5},{2,6},{3,7},{4,0},{5,1},{6,2},{7,3},{8,12},{9,13},{10,... | collective-permute-start | bytes 393224 | tf_op jit(solution)/shard_map/ppermute | solution.py:35
  36.4 12.6 %collective-permute-start.13 = (bf16[256,256]{1,0:T(8,128)(2,1)S(1)}, bf16[256,256]{1,0:T(8,128)(2,1)S(1)}, u32[]{:S(2)}, u32[]{:S(2)}) collective-permute-start(bf16[256,256]{1,0:T(8,128)(2,1)S(1)} %get-tuple-element.79), channel_id=1, source_target_pairs={{0,5},{1,4},{2,7},{3,6},{4,1},{5,0},{6,3},{7,2},{8,13},{9,12},{10,... | collective-permute-start | bytes 393224 | tf_op jit(solution)/shard_map/ppermute | solution.py:35
  42.8 6.7 %collective-permute-start.14 = (bf16[256,256]{1,0:T(8,128)(2,1)S(1)}, bf16[256,256]{1,0:T(8,128)(2,1)S(1)}, u32[]{:S(2)}, u32[]{:S(2)}) collective-permute-start(bf16[256,256]{1,0:T(8,128)(2,1)S(1)} %get-tuple-element.81), channel_id=1, source_target_pairs={{0,1},{1,0},{2,3},{3,2},{4,5},{5,4},{6,7},{7,6},{8,9},{9,8},{10,11... | collective-permute-start | bytes 393224 | tf_op jit(solution)/shard_map/ppermute | solution.py:35
  44.0 6.9 %collective-permute-start.15 = (bf16[256,256]{1,0:T(8,128)(2,1)S(1)}, bf16[256,256]{1,0:T(8,128)(2,1)S(1)}, u32[]{:S(2)}, u32[]{:S(2)}) collective-permute-start(bf16[256,256]{1,0:T(8,128)(2,1)S(1)} %get-tuple-element.82), channel_id=1, source_target_pairs={{0,4},{1,5},{2,6},{3,7},{4,0},{5,1},{6,2},{7,3},{8,12},{9,13},{10,... | collective-permute-start | bytes 393224 | tf_op jit(solution)/shard_map/ppermute | solution.py:35
  44.5 7.3 %collective-permute-start.16 = (bf16[256,256]{1,0:T(8,128)(2,1)S(1)}, bf16[256,256]{1,0:T(8,128)(2,1)S(1)}, u32[]{:S(2)}, u32[]{:S(2)}) collective-permute-start(bf16[256,256]{1,0:T(8,128)(2,1)S(1)} %get-tuple-element.83), channel_id=1, source_target_pairs={{0,5},{1,4},{2,7},{3,6},{4,1},{5,0},{6,3},{7,2},{8,13},{9,12},{10,... | collective-permute-start | bytes 393224 | tf_op jit(solution)/shard_map/ppermute | solution.py:35
  47.3 6.2 %collective-permute-start.18 = (bf16[256,256]{1,0:T(8,128)(2,1)S(1)}, bf16[256,256]{1,0:T(8,128)(2,1)S(1)}, u32[]{:S(2)}, u32[]{:S(2)}) collective-permute-start(bf16[256,256]{1,0:T(8,128)(2,1)S(1)} %get-tuple-element.87), channel_id=1, source_target_pairs={{0,1},{1,0},{2,3},{3,2},{4,5},{5,4},{6,7},{7,6},{8,9},{9,8},{10,11... | collective-permute-start | bytes 393224 | tf_op jit(solution)/shard_map/ppermute | solution.py:35
  49.0 7.3 %collective-permute-start.19 = (bf16[256,256]{1,0:T(8,128)(2,1)S(1)}, bf16[256,256]{1,0:T(8,128)(2,1)S(1)}, u32[]{:S(2)}, u32[]{:S(2)}) collective-permute-start(bf16[256,256]{1,0:T(8,128)(2,1)S(1)} %get-tuple-element.88), channel_id=1, source_target_pairs={{0,4},{1,5},{2,6},{3,7},{4,0},{5,1},{6,2},{7,3},{8,12},{9,13},{10,... | collective-permute-start | bytes 393224 | tf_op jit(solution)/shard_map/ppermute | solution.py:35
  49.6 6.7 %collective-permute-start.20 = (bf16[256,256]{1,0:T(8,128)(2,1)S(1)}, bf16[256,256]{1,0:T(8,128)(2,1)S(1)}, u32[]{:S(2)}, u32[]{:S(2)}) collective-permute-start(bf16[256,256]{1,0:T(8,128)(2,1)S(1)} %get-tuple-element.89), channel_id=1, source_target_pairs={{0,5},{1,4},{2,7},{3,6},{4,1},{5,0},{6,3},{7,2},{8,13},{9,12},{10,... | collective-permute-start | bytes 393224 | tf_op jit(solution)/shard_map/ppermute | solution.py:35
  56.4 2.4 %collective-permute-start.21 = (bf16[128,3072]{1,0:T(8,128)(2,1)S(1)}, bf16[128,3072]{1,0:T(8,128)(2,1)S(1)}, u32[]{:S(2)}, u32[]{:S(2)}) collective-permute-start(bf16[128,3072]{1,0:T(8,128)(2,1)S(1)} %bottom.1), channel_id=1, source_target_pairs={{0,2},{1,3},{2,0},{3,1},{4,6},{5,7},{6,4},{7,5},{8,10},{9,11},{10,... | collective-permute-start | bytes 2359304 | tf_op jit(solution)/shard_map/ppermute | solution.py:35
